TPU v7x, 32 devices: a whole 2x2x4 slice. The times are simulated.
32 devices in a mesh: batch: 4 (over x, core), item: 8 (over z, y).
Axes of the slice: x: 2, y: 2, z: 4, core: 2. Of those that a mesh axis runs over, the one named last changes fastest.
Arguments:
- user_vectors: bfloat16 [8192, 512], P(('batch', 'item')), may hold values from -6 to 6
- item_table: bfloat16 [131072, 512], P(('batch', 'item')), may hold values from -0.25 to 0.25
- tower_weight: bfloat16 [512, 512], replicated, may hold values from -3 to 3
- item_owner: int32 [8192, 1], P(('batch', 'item')), may hold values from 0 to 31; in each aligned block of 256 rows (0 to 255, 256 to 511, ...) at most 16 rows name the same one
- item_row: int32 [8192], P(('batch', 'item')), may hold values from 0 to 4095
Outputs:
- table_grad: bfloat16 [131072, 512], P(('batch', 'item'))
- weight_grad: float32 [512, 512], P(('batch', 'item'))
Inputs may be any that keep to these rules, and one draw needn't show every extreme that they name: `item_owner`: within the rows of one device (aligned blocks of 256 rows) no owner is named by more than 16 rows, a bound that some block reaches.
All inputs are finite; a program needn't handle non-finite values.
Results may differ from a plain program's by a relative error of at most 0.0075.
Values may be sent and summed in bfloat16 or wider, within the bound.
No kernel may reach another device: no remote copies, remote signals or barrier semaphores. Data moves between devices by JAX's collectives and lax.ppermute only.
A program may use at most 64 MiB of HBM per device.

v0:
```python
import jax
import jax.numpy as jnp
from jax import lax
from jax.sharding import PartitionSpec as P

epsilon = 1e-06
score_scale = 60.0
cauchy_scale = 4.0


def local(user_vectors, item_table, tower_weight, item_owner, item_row):
    b_dev, width = user_vectors.shape
    n_batch = lax.axis_size("batch")
    n_item = lax.axis_size("item")
    devices = n_batch * n_item
    slots = 2 * b_dev // devices
    owner = item_owner[:, 0]
    onehot = (owner[:, None] == jnp.arange(devices, dtype=jnp.int32)[None, :]).astype(jnp.int32)
    rank = jnp.sum(jnp.cumsum(onehot, axis=0) * onehot, axis=1) - 1
    place = owner * slots + rank
    request = (
        jnp.zeros((devices * slots,), jnp.int32).at[place].set(item_row).reshape(devices, slots)
    )
    asked = lax.all_to_all(request, ("batch", "item"), split_axis=0, concat_axis=0, tiled=True)
    found = item_table[asked]
    back = lax.all_to_all(found, ("batch", "item"), split_axis=0, concat_axis=0, tiled=True)
    fetched, asked = (back, asked)
    embed = fetched.reshape(devices * slots, width)[place]
    hidden = jnp.dot(embed, tower_weight, preferred_element_type=jnp.float32)
    rscale = lax.rsqrt(jnp.mean(hidden * hidden, axis=1, keepdims=True) + epsilon)
    item_vec = (hidden * rscale / jnp.sqrt(jnp.float32(width))).astype(jnp.bfloat16)
    user_f = user_vectors.astype(jnp.float32)
    user_unit = (
        user_f
        * lax.rsqrt(jnp.mean(user_f * user_f, axis=1, keepdims=True) + epsilon)
        / jnp.sqrt(jnp.float32(width))
    ).astype(jnp.bfloat16)
    piece = lax.all_gather(user_unit, "batch", axis=0, tiled=True)
    score = (
        lax.dot_general(
            item_vec, piece, (((1,), (1,)), ((), ())), preferred_element_type=jnp.float32
        )
        * score_scale
    )
    expo = jnp.exp(score)
    partial_mix = jnp.dot(expo.astype(jnp.bfloat16), piece, preferred_element_type=jnp.float32)
    total = jnp.sum(expo, axis=1)
    unit_f = user_unit.astype(jnp.float32)
    positive = jnp.sum(item_vec.astype(jnp.float32) * unit_f, axis=1) * score_scale
    xent = jnp.log(total) - positive
    cweight = 1.0 / (1.0 + xent / cauchy_scale)
    dvec = cweight[:, None] * score_scale * (partial_mix / total[:, None] - unit_f)
    inner = jnp.sum(hidden * dvec, axis=1, keepdims=True)
    dhidden = (
        rscale / jnp.sqrt(jnp.float32(width)) * (dvec - hidden * rscale * rscale * inner / width)
    ).astype(jnp.bfloat16)
    weight_grad = lax.psum_scatter(
        lax.dot_general(
            embed, dhidden, (((0,), (0,)), ((), ())), preferred_element_type=jnp.float32
        ),
        ("batch", "item"),
        scatter_dimension=0,
        tiled=True,
    )
    drow = jnp.dot(dhidden, tower_weight.T, preferred_element_type=jnp.float32)
    outgoing = jnp.zeros((devices * slots, width), jnp.float32).at[place].set(drow)
    incoming = lax.all_to_all(
        outgoing.reshape(devices, slots, width).astype(jnp.bfloat16),
        ("batch", "item"),
        split_axis=0,
        concat_axis=0,
        tiled=True,
    ).astype(jnp.float32)
    arrived = incoming.reshape(devices * slots, width)
    table_grad = (
        jnp.zeros((item_table.shape[0], width), jnp.float32).at[asked.reshape(-1)].add(arrived)
    )
    return (table_grad.astype(jnp.bfloat16), weight_grad)


def solution(mesh):
    return jax.shard_map(
        local,
        mesh=mesh,
        in_specs=(
            P(("batch", "item"), None),
            P(("batch", "item"), None),
            P(),
            P(("batch", "item"), None),
            P(("batch", "item")),
        ),
        out_specs=(P(("batch", "item"), None), P(("batch", "item"), None)),
        check_vma=False,
    )
```

profile of v0, /device:TPU:0, one launch (start us, length us, event | category | flops | bytes accessed | tf_op | source)
XLA Modules:
  0.0 215.5 jit_solution(6221395303976060483)
XLA Ops:
  7.2 0.8 fusion.15
  7.9 0.6 reduce-window.6
  8.5 0.2 slice_reduce_fusion
  8.7 0.8 fusion.14
  9.5 0.7 compare_select_fusion.2
  10.2 1.6 scatter_custom_fusion
  11.8 0.1 all_to_all.14
  11.9 14.2 %all_to_all.22 = s32[32,1,16]{2,1,0:T(1,128)S(1)} all-to-all(s32[32,1,16]{2,1,0:T(1,128)S(1)} %bitcast.43), channel_id=1, replica_groups=mesh['batch'=4,'item'=8] {'batch','item'}, dimensions={0} | all-to-all | bytes 4096 | tf_op jit(solution)/shard_map/all_to_all | solution.py:24
  26.1 0.1 reshape.147
  26.2 5.4 %gather_fusion = bf16[512,512]{1,0:T(8,128)(2,1)} fusion(bf16[4096,512]{1,0:T(8,128)(2,1)} %param.6, s32[1024]{0:T(1024)S(1)} %pad_clamp_fusion.1), kind=kCustom, calls=%fused_computation | custom fusion | bytes 1050624 | tf_op jit(solution)/shard_map/gather | solution.py:25
  31.6 2.6 %all-to-all-start.1 = ((bf16[32,16,512]{2,1,0:T(8,128)(2,1)}), bf16[32,16,512]{2,1,0:T(8,128)(2,1)S(1)}, u32[]{:S(2)}, u32[]{:S(2)}) async-start(bf16[32,16,512]{2,1,0:T(8,128)(2,1)} %bitcast.8), calls=%async_computation.1 | async-start | bytes 1048576 | tf_op jit(solution)/shard_map/all_to_all | solution.py:26
  34.2 1.1 fusion.6
  35.3 15.2 %all-to-all-done.1 = bf16[32,16,512]{2,1,0:T(8,128)(2,1)S(1)} async-done(((bf16[32,16,512]{2,1,0:T(8,128)(2,1)}), bf16[32,16,512]{2,1,0:T(8,128)(2,1)S(1)}, u32[]{:S(2)}, u32[]{:S(2)}) %all-to-all-start.1) | async-done | bytes 524320 | tf_op jit(solution)/shard_map/all_to_all | solution.py:26
  50.5 1.2 gather_fusion.1
  51.7 0.4 multiply_reduce_fusion.1
  52.1 0.9 fusion.9
  53.1 14.4 %all-gather.2.cloned.1.call-done = bf16[1024,512]{1,0:T(8,128)(2,1)} async-done(((bf16[256,512]{1,0:T(8,128)(2,1)}), bf16[1024,512]{1,0:T(8,128)(2,1)}) %all-gather.2.cloned.1.call-update) | async-done | bytes 1048592 | tf_op jit(solution)/shard_map/all_gather | solution.py:38
  67.5 1.8 fusion.19
  69.3 1.8 multiply_reduce_fusion
  71.1 0.2 multiply_convert_fusion
  71.3 1.4 fusion.21
  72.7 0.3 fusion.20
  73.1 1.7 scatter_custom_fusion.1
  74.8 0.9 convert_element_type.44
  75.6 4.6 %all-to-all-start.2 = ((bf16[32,16,512]{2,1,0:T(8,128)(2,1)}), bf16[32,16,512]{2,1,0:T(8,128)(2,1)S(1)}, u32[]{:S(2)}, u32[]{:S(2)}) async-start(bf16[32,16,512]{2,1,0:T(8,128)(2,1)} %bitcast.10), calls=%async_computation.2 | async-start | bytes 1048576 | tf_op jit(solution)/shard_map/all_to_all | solution.py:67
  80.2 0.6 broadcast.186
  80.8 0.7 reduce.5
  81.6 0.1 reshape.139
  81.6 16.0 %all-to-all-done.2 = bf16[32,16,512]{2,1,0:T(8,128)(2,1)S(1)} async-done(((bf16[32,16,512]{2,1,0:T(8,128)(2,1)}), bf16[32,16,512]{2,1,0:T(8,128)(2,1)S(1)}, u32[]{:S(2)}, u32[]{:S(2)}) %all-to-all-start.2) | async-done | bytes 524320 | tf_op jit(solution)/shard_map/all_to_all | solution.py:67
  97.7 7.4 %scatter_custom_fusion.2 = f32[4096,512]{1,0:T(8,128)} fusion(s32[512]{0:T(512)S(1)} %bitcast.50, f32[]{:T(128)} %constant.12.clone.1, bf16[512,512]{1,0:T(8,128)(2,1)S(1)} %bitcast.41), kind=kCustom, calls=%fused_computation.5 | custom fusion | flops 524288 | bytes 8912900 | tf_op jit(solution)/shard_map/scatter-add | solution.py:76
  105.0 5.9 %convert_element_type.46 = bf16[4096,512]{1,0:T(8,128)(2,1)} convert(f32[4096,512]{1,0:T(8,128)} %scatter_custom_fusion.2) | non-fusion elementwise | flops 2097152 | bytes 12582912 | tf_op jit(solution)/shard_map/convert_element_type | solution.py:78
  111.0 97.7 %reduce-scatter.2.cloned.1.call-done = f32[16,512]{1,0:T(8,128)} async-done(((f32[512,512]{1,0:T(8,128)}), f32[16,512]{1,0:T(8,128)}) %reduce-scatter.2.cloned.1.call-update) | async-done | bytes 32784 | tf_op jit(solution)/shard_map/reduce_scatter | solution.py:57
  (17 shorter events, 0.2 us)
Async XLA Ops:
  7.2 44.5 %copy-start = (bf16[512,512]{1,0:T(8,128)(2,1)S(1)}, bf16[512,512]{1,0:T(8,128)(2,1)}, u32[]{:S(2)}) copy-start(bf16[512,512]{1,0:T(8,128)(2,1)} %param.7) | copy-start | bytes 1572868
  7.2 44.9 %copy-start.1 = (bf16[256,512]{1,0:T(8,128)(2,1)S(1)}, bf16[256,512]{1,0:T(8,128)(2,1)}, u32[]{:S(2)}) copy-start(bf16[256,512]{1,0:T(8,128)(2,1)} %param.5) | copy-start | bytes 786436
  31.6 19.0 %all-to-all-start.1 = ((bf16[32,16,512]{2,1,0:T(8,128)(2,1)}), bf16[32,16,512]{2,1,0:T(8,128)(2,1)S(1)}, u32[]{:S(2)}, u32[]{:S(2)}) async-start(bf16[32,16,512]{2,1,0:T(8,128)(2,1)} %bitcast.8), calls=%async_computation.1 | async-start | bytes 1048576 | tf_op jit(solution)/shard_map/all_to_all | solution.py:26
  34.2 33.3 %all-gather.2.cloned.1.call-start = ((), (), s32[]{:S(2)}) async-start(), calls=%async_computation.4 | async-start | bytes 1310720 | tf_op jit(solution)/shard_map/all_gather | solution.py:38
  53.0 155.7 %reduce-scatter.2.cloned.1.call-start = ((), (), s32[]{:S(2)}) async-start(), calls=%async_computation.5 | async-start | bytes 1081344 | tf_op jit(solution)/shard_map/reduce_scatter | solution.py:57
  75.6 22.0 %all-to-all-start.2 = ((bf16[32,16,512]{2,1,0:T(8,128)(2,1)}), bf16[32,16,512]{2,1,0:T(8,128)(2,1)S(1)}, u32[]{:S(2)}, u32[]{:S(2)}) async-start(bf16[32,16,512]{2,1,0:T(8,128)(2,1)} %bitcast.10), calls=%async_computation.2 | async-start | bytes 1048576 | tf_op jit(solution)/shard_map/all_to_all | solution.py:67
Sparse Core Ops, SparseCore 0:
  53.1 14.2 all-gather.1
  72.9 135.7 reduce-scatter.1
where the time goes:
time: 216 us
  waiting for transfers between devices  143 us (66%)
  other arithmetic  20 us (9%)
  blocking collectives  14.2 us (7%)
  between operations  14.2 us (7%)
  local copies, waits for them, and re-layouts  10.8 us (5%)
  starting transfers between devices  7.29 us (3%)
  matrix products  5.75 us (3%)
    reduce_scatter x1, waiting for transfers between devices, local(): lax.psum_scatter(lax.dot_general(embed, dhidden, (((0,), (0,)), ((), ()))...  97.7 us
    all_to_all x1, waiting for transfers between devices, local(): lax.all_to_all(outgoing.reshape(devices, slots, width).astype(jnp.bfloat1...  16 us
    all_to_all x1, waiting for transfers between devices, local(): lax.all_to_all(found, ('batch', 'item'), split_axis=0, concat_axis=0, til...  15.2 us
    all_gather x1, waiting for transfers between devices, local(): piece = lax.all_gather(user_unit, 'batch', axis=0, tiled=True)  14.4 us
    all_to_all x1, blocking collectives, local(): lax.all_to_all(request, ('batch', 'item'), split_axis=0, concat_axis=0, t...  14.2 us
    scatter-add x1, other arithmetic, local(): jnp.zeros((item_table.shape[0], width), jnp.float32).at[asked.reshape(-1)]  7.38 us
    convert_element_type x1, other arithmetic, local(): return (table_grad.astype(jnp.bfloat16), weight_grad)  5.93 us
    gather x1, local copies, waits for them, and re-layouts, local(): found = item_table[asked]  5.38 us
  transfers between devices with their start and end apart: 4, of which 4 were waited for; matrix products, arithmetic and copies ran while one was open for 9% of the time, Pallas kernels for 0%

commit v1 on v0

v1 whole, which is shorter than its diff:
```python
import functools

import jax
import jax.numpy as jnp
from jax import lax
from jax.experimental import pallas as pl
from jax.experimental.pallas import tpu as pltpu
from jax.sharding import PartitionSpec as P

epsilon = 1e-06
score_scale = 60.0
cauchy_scale = 4.0
f32 = jnp.float32
bf16 = jnp.bfloat16
i32 = jnp.int32
VMEM_LIMIT = 32 * 1024 * 1024


def iota(shape, dim):
    return lax.broadcasted_iota(i32, shape, dim)


def hot(mask):
    return jnp.where(mask, 1.0, 0.0).astype(bf16)


def dot(a, b, a_dim=1, b_dim=0):
    return lax.dot_general(a, b, (((a_dim,), (b_dim,)), ((), ())), preferred_element_type=f32)


def halves(value):
    return (value >> 8).astype(f32), (value & 255).astype(f32)


def request_kernel(owner_ref, row_ref, request_ref, place_ref):
    devices, slots = request_ref.shape
    n = owner_ref.shape[1]
    owner = owner_ref[...]
    named = owner == iota((devices, n), 0)
    count = dot(hot(named), hot(iota((n, n), 0) <= iota((n, n), 1)))
    rank = jnp.sum(jnp.where(named, count, 0.0), axis=0, keepdims=True).astype(i32) - 1
    in_slot = hot(rank == iota((slots, n), 0))
    high, low = halves(row_ref[...] + 1)
    high = dot(jnp.where(named, high, 0.0).astype(bf16), in_slot, 1, 1)
    low = dot(jnp.where(named, low, 0.0).astype(bf16), in_slot, 1, 1)
    request_ref[...] = (high * 256.0 + low).astype(i32) - 1
    place_ref[...] = owner * slots + rank


def asked_column(asked):
    devices, slots = asked.shape
    total = devices * slots
    first = iota((total, devices), 1) * slots
    spot = iota((total, devices), 0)
    pick = hot((spot >= first) & (spot < first + slots))
    high, low = halves(asked)
    value = dot(pick, high.astype(bf16)) * 256.0 + dot(pick, low.astype(bf16))
    mine = lax.rem(iota((total, slots), 0), slots) == iota((total, slots), 1)
    return jnp.sum(jnp.where(mine, value, 0.0), axis=1, keepdims=True)


def asked_line(asked):
    devices, slots = asked.shape
    total = devices * slots
    pick = hot(lax.rem(iota((slots, total), 1), slots) == iota((slots, total), 0))
    high, low = halves(asked)
    value = dot(high.astype(bf16), pick) * 256.0 + dot(low.astype(bf16), pick)
    first = iota((devices, total), 0) * slots
    spot = iota((devices, total), 1)
    mine = (spot >= first) & (spot < first + slots)
    return jnp.sum(jnp.where(mine, value, 0.0), axis=0, keepdims=True)


def fetch_kernel(asked_ref, table_ref, found_ref, column, total):
    step = pl.program_id(0)
    chunk = table_ref.shape[0]

    @pl.when(step == 0)
    def _():
        column[...] = asked_column(asked_ref[...]).astype(i32)

    pick = hot(column[...] - step * chunk == iota((column.shape[0], chunk), 1))
    part = dot(pick, table_ref[...])

    @pl.when(step == 0)
    def _():
        total[...] = part

    @pl.when(step > 0)
    def _():
        total[...] += part

    @pl.when(step == pl.num_programs(0) - 1)
    def _():
        found_ref[...] = total[...].astype(bf16)


def unit_of(users):
    width = users.shape[1]
    users = users.astype(f32)
    mean = jnp.mean(users * users, axis=1, keepdims=True)
    return (users * lax.rsqrt(mean + epsilon) * (1.0 / width**0.5)).astype(bf16)


def prepare_kernel(place_ref, asked_ref, own_ref, users_ref, unit_ref, own_unit_ref, take_ref, give_ref, line_ref):
    n, total = take_ref.shape
    unit_ref[...] = unit_of(users_ref[...])
    own_unit_ref[...] = unit_of(own_ref[...])
    place = place_ref[...]
    column = jnp.sum(jnp.where(iota((n, n), 0) == iota((n, n), 1), place, 0), axis=1, keepdims=True)
    take_ref[...] = hot(column == iota((n, total), 1))
    give_ref[...] = hot(place == iota((total, n), 0))
    line_ref[...] = asked_line(asked_ref[...]).astype(i32)


def main_kernel(fetched_ref, weight_ref, unit_ref, own_unit_ref, take_ref, give_ref, outgoing_ref, embed_ref, dhidden_ref):
    width = weight_ref.shape[0]
    root = 1.0 / width**0.5
    embed = dot(take_ref[...], fetched_ref[...]).astype(bf16)
    hidden = dot(embed, weight_ref[...])
    rscale = lax.rsqrt(jnp.mean(hidden * hidden, axis=1, keepdims=True) + epsilon)
    item_vec = (hidden * (rscale * root)).astype(bf16)
    unit = unit_ref[...]
    expo = jnp.exp(dot(item_vec, unit, 1, 1) * score_scale)
    total = jnp.sum(expo, axis=1, keepdims=True)
    mixed = dot(expo.astype(bf16), unit)
    own = own_unit_ref[...].astype(f32)
    positive = jnp.sum(item_vec.astype(f32) * own, axis=1, keepdims=True) * score_scale
    xent = jnp.log(total) - positive
    cweight = 1.0 / (1.0 + xent * (1.0 / cauchy_scale))
    dvec = (cweight * score_scale) * (mixed * (1.0 / total) - own)
    inner = jnp.sum(hidden * dvec, axis=1, keepdims=True)
    dhidden = (rscale * root * (dvec - hidden * (rscale * rscale * inner * (1.0 / width)))).astype(bf16)
    outgoing_ref[...] = dot(give_ref[...], dhidden).astype(bf16)
    embed_ref[...] = embed
    dhidden_ref[...] = dhidden


def share_kernel(embed_ref, dhidden_ref, share_ref):
    share_ref[...] = dot(embed_ref[...], dhidden_ref[...], 0, 0).astype(bf16)


def table_kernel(line_ref, incoming_ref, weight_ref, table_grad_ref, drow):
    step = pl.program_id(0)
    chunk = table_grad_ref.shape[0]

    @pl.when(step == 0)
    def _():
        drow[...] = dot(incoming_ref[...], weight_ref[...], 1, 1).astype(bf16)

    pick = hot(line_ref[...] - step * chunk == iota((chunk, line_ref.shape[1]), 0))
    table_grad_ref[...] = dot(pick, drow[...]).astype(bf16)


def params():
    return pltpu.CompilerParams(vmem_limit_bytes=VMEM_LIMIT)


def call(kernel, outs, *args, flops=0):
    return pl.pallas_call(
        kernel,
        out_shape=[jax.ShapeDtypeStruct(shape, dtype) for shape, dtype in outs],
        compiler_params=params(),
        cost_estimate=pl.CostEstimate(flops=flops, bytes_accessed=1 << 20, transcendentals=0),
    )(*args)


def local(user_vectors, item_table, tower_weight, item_owner, item_row):
    n, width = user_vectors.shape
    rows = item_table.shape[0]
    axes = ("batch", "item")
    devices = lax.axis_size("batch") * lax.axis_size("item")
    slots = 2 * n // devices
    total = devices * slots
    chunk = min(512, rows)

    exchange = functools.partial(lax.all_to_all, axis_name=axes, split_axis=0, concat_axis=0, tiled=True)

    users = lax.all_gather(user_vectors, "batch", axis=0, tiled=True)
    request, place = call(
        request_kernel,
        [((devices, slots), i32), ((1, n), i32)],
        item_owner.reshape(1, n),
        item_row.reshape(1, n),
    )
    asked = exchange(request)
    found = pl.pallas_call(
        fetch_kernel,
        grid=(rows // chunk,),
        in_specs=[
            pl.BlockSpec((devices, slots), lambda k: (0, 0)),
            pl.BlockSpec((chunk, width), lambda k: (k, 0)),
        ],
        out_specs=pl.BlockSpec((total, width), lambda k: (0, 0)),
        out_shape=jax.ShapeDtypeStruct((total, width), bf16),
        scratch_shapes=[pltpu.VMEM((total, 1), i32), pltpu.VMEM((total, width), f32)],
        compiler_params=params(),
        cost_estimate=pl.CostEstimate(flops=2 * total * rows * width, bytes_accessed=2 * rows * width, transcendentals=0),
    )(asked, item_table)
    fetched = exchange(found.reshape(devices, slots, width)).reshape(total, width)
    unit, own_unit, take, give, line = call(
        prepare_kernel,
        [
            (users.shape, bf16),
            ((n, width), bf16),
            ((n, total), bf16),
            ((total, n), bf16),
            ((1, total), i32),
        ],
        place,
        asked,
        user_vectors,
        users,
        flops=1 << 28,
    )
    outgoing, embed, dhidden = call(
        main_kernel,
        [((total, width), bf16), ((n, width), bf16), ((n, width), bf16)],
        fetched,
        tower_weight,
        unit,
        own_unit,
        take,
        give,
        flops=1 << 30,
    )
    incoming = exchange(outgoing.reshape(devices, slots, width)).reshape(total, width)
    (share,) = call(share_kernel, [((width, width), bf16)], embed, dhidden, flops=1 << 27)
    shares = exchange(share.reshape(devices, width // devices, width))
    weight_grad = jnp.sum(shares.astype(f32), axis=0)
    table_grad = pl.pallas_call(
        table_kernel,
        grid=(rows // chunk,),
        in_specs=[
            pl.BlockSpec((1, total), lambda k: (0, 0)),
            pl.BlockSpec((total, width), lambda k: (0, 0)),
            pl.BlockSpec((width, width), lambda k: (0, 0)),
        ],
        out_specs=pl.BlockSpec((chunk, width), lambda k: (k, 0)),
        out_shape=jax.ShapeDtypeStruct((rows, width), bf16),
        scratch_shapes=[pltpu.VMEM((total, width), bf16)],
        compiler_params=params(),
        cost_estimate=pl.CostEstimate(flops=2 * total * rows * width, bytes_accessed=2 * rows * width, transcendentals=0),
    )(line, incoming, tower_weight)
    return (table_grad, weight_grad)


def solution(mesh):
    return jax.shard_map(
        local,
        mesh=mesh,
        in_specs=(
            P(("batch", "item"), None),
            P(("batch", "item"), None),
            P(),
            P(("batch", "item"), None),
            P(("batch", "item")),
        ),
        out_specs=(P(("batch", "item"), None), P(("batch", "item"), None)),
        check_vma=False,
    )
```

time: 216 us -> 100 us (0.46)
  waiting for transfers between devices: 143 us -> 40.1 us
  other arithmetic: 20 us -> 0.7 us
  Pallas kernels: 0 us -> 16.3 us
  matrix products: 5.75 us -> 0 us
  local copies, waits for them, and re-layouts: 10.8 us -> 6.42 us
    reduce_scatter x1 -> x0, waiting for transfers between devices: 97.7 us -> none  [local(): lax.psum_scatter(lax.dot_general(embed, dhidden, (((0,), (0,)), ((), ()))...]
    pallas_call x0 -> x6, Pallas kernels: none -> 16.3 us  [the longest x1 5.87 us: local(): pl.pallas_call(fetch_kernel, grid=(rows // chunk,), in_specs=[pl.BlockSpe...]
    all_gather x1, waiting for transfers between devices: 14.4 us -> 0.02 us  [local(): users = lax.all_gather(user_vectors, 'batch', axis=0, tiled=True)]
    all_to_all x2 -> x3, waiting for transfers between devices: 31.2 us -> 39.4 us  [the longest x1 15.2 us: local(): exchange(outgoing.reshape(devices, slots, width)).reshape(total, width)]
    convert_element_type x4 -> x0, other arithmetic: 7.74 us -> none  [the longest x1 5.93 us: local(): return (table_grad.astype(jnp.bfloat16), weight_grad)]
    scatter-add x1 -> x0, other arithmetic: 7.38 us -> none  [local(): jnp.zeros((item_table.shape[0], width), jnp.float32).at[asked.reshape(-1)]]
    gather x2 -> x0, local copies, waits for them, and re-layouts: 6.53 us -> none  [the longest x1 5.38 us: local(): found = item_table[asked]]
    unnamed x4 -> x16, local copies, waits for them, and re-layouts: 0.02 us -> 6.42 us
  transfers between devices with their start and end apart: 4 -> 4, of which waited for: 4 -> 3; matrix products, arithmetic and copies ran while one was open for 9% -> 0% of each run, Pallas kernels for 0% -> 14%
where the time goes in v1:
time: 100 us; the launch traced here: 99.7 us
  waiting for transfers between devices  40.1 us (40%)
  Pallas kernels  16.3 us (16%)
  blocking collectives  14.2 us (14%)
  between operations  14.1 us (14%)
  starting transfers between devices  7.85 us (8%)
  local copies, waits for them, and re-layouts  6.42 us (6%)
    all_to_all x1, waiting for transfers between devices, local(): exchange(outgoing.reshape(devices, slots, width)).reshape(total, width)  15.2 us
    all_to_all x1, blocking collectives, local(): asked = exchange(request)  14.2 us
    all_to_all x1, waiting for transfers between devices, local(): exchange(found.reshape(devices, slots, width)).reshape(total, width)  13.7 us
    all_to_all x1, waiting for transfers between devices, local(): shares = exchange(share.reshape(devices, width // devices, width))  10.5 us
    unnamed x16, local copies, waits for them, and re-layouts  6.42 us
    pallas_call x1, Pallas kernels, local(): pl.pallas_call(fetch_kernel, grid=(rows // chunk,), in_specs=[pl.BlockSpe...  5.87 us
    pallas_call x1, Pallas kernels, local(): pl.pallas_call(table_kernel, grid=(rows // chunk,), in_specs=[pl.BlockSpe...  5.87 us
    pallas_call x4, Pallas kernels, call(): pl.pallas_call(kernel, out_shape=[jax.ShapeDtypeStruct(shape, dtype) for...  4.61 us
  transfers between devices with their start and end apart: 4, of which 3 were waited for; matrix products, arithmetic and copies ran while one was open for 0% of the time, Pallas kernels for 14%

profile of v1, /device:TPU:0, one launch (start us, length us, event | category | flops | bytes accessed | tf_op | source)
XLA Modules:
  0.0 99.7 jit_solution(4570579934603184)
XLA Ops:
  7.2 0.0 all-gather.2.cloned.1.call-start
  7.2 0.7 all-gather.2.cloned.1.call-update
  7.9 0.0 copy-start.2
  7.9 0.7 copy-done.2
  8.6 0.0 copy-start.3
  8.6 0.7 copy-done.3
  9.3 0.3 shard_map.68
  9.6 14.2 %all_to_all.26 = s32[32,1,16]{2,1,0:T(1,128)S(1)} all-to-all(s32[32,1,16]{2,1,0:T(1,128)S(1)} %bitcast.15), channel_id=1, replica_groups=mesh['batch'=4,'item'=8] {'batch','item'}, dimensions={0} | all-to-all | bytes 4096 | tf_op jit(solution)/shard_map/all_to_all | solution.py:186
  23.8 0.0 copy-start.4
  23.8 2.2 %copy-done.4 = bf16[4096,512]{1,0:T(8,128)(2,1)S(1)} copy-done((bf16[4096,512]{1,0:T(8,128)(2,1)S(1)}, bf16[4096,512]{1,0:T(8,128)(2,1)}, u32[]{:S(2)}) %copy-start.4) | copy-done | bytes 4194328
  26.0 0.0 copy-start.1
  26.0 0.0 copy-start.5
  26.0 5.9 %shard_map.70 = bf16[512,512]{1,0:T(8,128)(2,1)} custom-call(s32[32,16]{1,0:T(8,128)S(1)} %bitcast.13, bf16[4096,512]{1,0:T(8,128)(2,1)S(1)} %copy-done.4), custom_call_target="tpu_custom_call" | custom-call | flops 2147483648 | bytes 4194304 | tf_op jit(solution)/shard_map/pallas_call | solution.py:187
  31.9 2.6 %all-to-all-start.1 = ((bf16[32,16,512]{2,1,0:T(8,128)(2,1)}), bf16[32,16,512]{2,1,0:T(8,128)(2,1)S(1)}, u32[]{:S(2)}, u32[]{:S(2)}) async-start(bf16[32,16,512]{2,1,0:T(8,128)(2,1)} %bitcast.5), calls=%async_computation.1 | async-start | bytes 1048576 | tf_op jit(solution)/shard_map/all_to_all | solution.py:200
  34.5 0.0 all-gather.2.cloned.1.call-done.users_ref
  34.5 0.0 copy-done.1
  34.5 0.0 copy-start
  34.5 1.2 %copy-done = bf16[1024,512]{1,0:T(8,128)(2,1)S(1)} copy-done((bf16[1024,512]{1,0:T(8,128)(2,1)S(1)}, bf16[1024,512]{1,0:T(8,128)(2,1)}, u32[]{:S(2)}) %copy-start) | copy-done | bytes 1048600
  35.7 0.7 shard_map.69
  36.5 0.0 copy-start.6
  36.5 0.7 copy-done.6
  37.2 13.7 %all-to-all-done.1 = bf16[32,16,512]{2,1,0:T(8,128)(2,1)S(1)} async-done(((bf16[32,16,512]{2,1,0:T(8,128)(2,1)}), bf16[32,16,512]{2,1,0:T(8,128)(2,1)S(1)}, u32[]{:S(2)}, u32[]{:S(2)}) %all-to-all-start.1) | async-done | bytes 524320 | tf_op jit(solution)/shard_map/all_to_all | solution.py:200
  50.8 0.0 copy-done.5
  50.8 0.9 copy-done.7
  51.8 2.5 %shard_map.71 = (bf16[512,512]{1,0:T(8,128)(2,1)}, bf16[256,512]{1,0:T(8,128)(2,1)S(1)}, bf16[256,512]{1,0:T(8,128)(2,1)S(1)}) custom-call(bf16[512,512]{1,0:T(8,128)(2,1)S(1)} %bitcast.11, bf16[512,512]{1,0:T(8,128)(2,1)S(1)} %copy-done.5, bf16[1024,512]{1,0:T(8,128)(2,1)S(1)} %get-tuple-element.15.unit_ref, ...), custom_call_target="tpu_custom_call" | custom-call | flops 1073741824 | bytes 1048576 | tf_op jit(solution)/shard_map/pallas_call | solution.py:160
  54.3 2.6 %all-to-all-start.2 = ((bf16[32,16,512]{2,1,0:T(8,128)(2,1)}), bf16[32,16,512]{2,1,0:T(8,128)(2,1)S(1)}, u32[]{:S(2)}, u32[]{:S(2)}) async-start(bf16[32,16,512]{2,1,0:T(8,128)(2,1)} %bitcast.7), calls=%async_computation.2 | async-start | bytes 1048576 | tf_op jit(solution)/shard_map/all_to_all | solution.py:227
  56.9 1.1 %shard_map.73 = bf16[512,512]{1,0:T(8,128)(2,1)} custom-call(bf16[256,512]{1,0:T(8,128)(2,1)S(1)} %get-tuple-element.20.embed_ref, bf16[256,512]{1,0:T(8,128)(2,1)S(1)} %get-tuple-element.21.dhidden_ref), custom_call_target="tpu_custom_call" | custom-call | flops 134217728 | bytes 1048576 | tf_op jit(solution)/shard_map/pallas_call | solution.py:160
  58.0 15.2 %all-to-all-done.2 = bf16[32,16,512]{2,1,0:T(8,128)(2,1)S(1)} async-done(((bf16[32,16,512]{2,1,0:T(8,128)(2,1)}), bf16[32,16,512]{2,1,0:T(8,128)(2,1)S(1)}, u32[]{:S(2)}, u32[]{:S(2)}) %all-to-all-start.2) | async-done | bytes 524320 | tf_op jit(solution)/shard_map/all_to_all | solution.py:227
  73.2 2.6 %all-to-all-start.3 = ((bf16[32,16,512]{2,1,0:T(8,128)(2,1)}), bf16[32,16,512]{2,1,0:T(8,128)(2,1)S(1)}, u32[]{:S(2)}, u32[]{:S(2)}) async-start(bf16[32,16,512]{2,1,0:T(8,128)(2,1)} %bitcast.9), calls=%async_computation.3 | async-start | bytes 1048576 | tf_op jit(solution)/shard_map/all_to_all | solution.py:229
  75.9 5.9 %shard_map.72 = bf16[4096,512]{1,0:T(8,128)(2,1)} custom-call(s32[1,512]{1,0:T(1,128)S(1)} %get-tuple-element.14.line_ref, bf16[512,512]{1,0:T(8,128)(2,1)S(1)} %bitcast.12, bf16[512,512]{1,0:T(8,128)(2,1)S(1)} %copy-done.5), custom_call_target="tpu_custom_call" | custom-call | flops 2147483648 | bytes 4194304 | tf_op jit(solution)/shard_map/pallas_call | solution.py:231
  81.7 10.5 %all-to-all-done.3 = bf16[32,16,512]{2,1,0:T(8,128)(2,1)S(1)} async-done(((bf16[32,16,512]{2,1,0:T(8,128)(2,1)}), bf16[32,16,512]{2,1,0:T(8,128)(2,1)S(1)}, u32[]{:S(2)}, u32[]{:S(2)}) %all-to-all-start.3) | async-done | bytes 524320 | tf_op jit(solution)/shard_map/all_to_all | solution.py:229
  92.2 0.7 convert_reduce_fusion
  (1 shorter events, 0.0 us)
Async XLA Ops:
  7.2 27.3 %all-gather.2.cloned.1.call-start = ((), (), s32[]{:S(2)}) async-start(), calls=%async_computation.4 | async-start | bytes 1310720 | tf_op jit(solution)/shard_map/all_gather | solution.py:179
  7.9 0.7 copy-start.2
  8.6 0.7 copy-start.3
  23.8 2.2 %copy-start.4 = (bf16[4096,512]{1,0:T(8,128)(2,1)S(1)}, bf16[4096,512]{1,0:T(8,128)(2,1)}, u32[]{:S(2)}) copy-start(bf16[4096,512]{1,0:T(8,128)(2,1)} %table_ref.1) | copy-start | bytes 12582916
  26.0 8.5 %copy-start.1 = (bf16[256,512]{1,0:T(8,128)(2,1)S(1)}, bf16[256,512]{1,0:T(8,128)(2,1)}, u32[]{:S(2)}) copy-start(bf16[256,512]{1,0:T(8,128)(2,1)} %own_ref.1) | copy-start | bytes 786436
  26.0 24.8 %copy-start.5 = (bf16[512,512]{1,0:T(8,128)(2,1)S(1)}, bf16[512,512]{1,0:T(8,128)(2,1)}, u32[]{:S(2)}) copy-start(bf16[512,512]{1,0:T(8,128)(2,1)} %weight_ref.3) | copy-start | bytes 1572868
  31.9 19.0 %all-to-all-start.1 = ((bf16[32,16,512]{2,1,0:T(8,128)(2,1)}), bf16[32,16,512]{2,1,0:T(8,128)(2,1)S(1)}, u32[]{:S(2)}, u32[]{:S(2)}) async-start(bf16[32,16,512]{2,1,0:T(8,128)(2,1)} %bitcast.5), calls=%async_computation.1 | async-start | bytes 1048576 | tf_op jit(solution)/shard_map/all_to_all | solution.py:200
  34.5 1.2 %copy-start = (bf16[1024,512]{1,0:T(8,128)(2,1)S(1)}, bf16[1024,512]{1,0:T(8,128)(2,1)}, u32[]{:S(2)}) copy-start(bf16[1024,512]{1,0:T(8,128)(2,1)} %all-gather.2.cloned.1.call-done.users_ref) | copy-start | bytes 3145732
  36.5 0.7 copy-start.6
  50.8 1.0 copy-start.7
  54.3 19.0 %all-to-all-start.2 = ((bf16[32,16,512]{2,1,0:T(8,128)(2,1)}), bf16[32,16,512]{2,1,0:T(8,128)(2,1)S(1)}, u32[]{:S(2)}, u32[]{:S(2)}) async-start(bf16[32,16,512]{2,1,0:T(8,128)(2,1)} %bitcast.7), calls=%async_computation.2 | async-start | bytes 1048576 | tf_op jit(solution)/shard_map/all_to_all | solution.py:227
  73.2 19.0 %all-to-all-start.3 = ((bf16[32,16,512]{2,1,0:T(8,128)(2,1)}), bf16[32,16,512]{2,1,0:T(8,128)(2,1)S(1)}, u32[]{:S(2)}, u32[]{:S(2)}) async-start(bf16[32,16,512]{2,1,0:T(8,128)(2,1)} %bitcast.9), calls=%async_computation.3 | async-start | bytes 1048576 | tf_op jit(solution)/shard_map/all_to_all | solution.py:229
Sparse Core Ops, SparseCore 0:
  9.6 19.4 all-gather.1

commit v2 on v1

v2 whole, which is shorter than its diff:
```python
import functools

import jax
import jax.numpy as jnp
from jax import lax
from jax.experimental import pallas as pl
from jax.experimental.pallas import tpu as pltpu
from jax.sharding import PartitionSpec as P

epsilon = 1e-06
score_scale = 60.0
cauchy_scale = 4.0
f32 = jnp.float32
bf16 = jnp.bfloat16
i32 = jnp.int32
BLOCK = 256


def iota(shape, dim):
    return lax.broadcasted_iota(i32, shape, dim)


def hot(mask):
    return jnp.where(mask, 1.0, 0.0).astype(bf16)


def dot(a, b, a_dim=1, b_dim=0):
    return lax.dot_general(a, b, (((a_dim,), (b_dim,)), ((), ())), preferred_element_type=f32)


def halves(value):
    return (value >> 8).astype(f32), (value & 255).astype(f32)


def request_kernel(owner_ref, row_ref, request_ref, place_ref):
    devices, slots = request_ref.shape
    n = owner_ref.shape[1]
    owner = owner_ref[...]
    named = owner == iota((devices, n), 0)
    count = dot(hot(named), hot(iota((n, n), 0) <= iota((n, n), 1)))
    rank = jnp.sum(jnp.where(named, count, 0.0), axis=0, keepdims=True).astype(i32) - 1
    in_slot = hot(rank == iota((slots, n), 0))
    high, low = halves(row_ref[...] + 1)
    high = dot(jnp.where(named, high, 0.0).astype(bf16), in_slot, 1, 1)
    low = dot(jnp.where(named, low, 0.0).astype(bf16), in_slot, 1, 1)
    request_ref[...] = (high * 256.0 + low).astype(i32) - 1
    place_ref[...] = owner * slots + rank


def asked_column(asked):
    devices, slots = asked.shape
    total = devices * slots
    first = iota((total, devices), 1) * slots
    spot = iota((total, devices), 0)
    pick = hot((spot >= first) & (spot < first + slots))
    high, low = halves(asked)
    value = dot(pick, high.astype(bf16)) * 256.0 + dot(pick, low.astype(bf16))
    mine = lax.rem(iota((total, slots), 0), slots) == iota((total, slots), 1)
    return jnp.sum(jnp.where(mine, value, 0.0), axis=1, keepdims=True)


def asked_line(asked):
    devices, slots = asked.shape
    total = devices * slots
    pick = hot(lax.rem(iota((slots, total), 1), slots) == iota((slots, total), 0))
    high, low = halves(asked)
    value = dot(high.astype(bf16), pick) * 256.0 + dot(low.astype(bf16), pick)
    first = iota((devices, total), 0) * slots
    spot = iota((devices, total), 1)
    mine = (spot >= first) & (spot < first + slots)
    return jnp.sum(jnp.where(mine, value, 0.0), axis=0, keepdims=True)


def parts_of(value):
    return value >> 8, value & 255


def fetch_kernel(asked_ref, table_hbm, found_ref, table, sems):
    groups = sems.shape[0]
    size = table.shape[0] // groups
    copies = [
        pltpu.make_async_copy(table_hbm.at[pl.ds(g * size, size)], table.at[pl.ds(g * size, size)], sems.at[g])
        for g in range(groups)
    ]
    for copy in copies:
        copy.start()
    block, low = parts_of(asked_column(asked_ref[...]).astype(i32))
    total = block.shape[0]
    low_hot = hot(low == iota((total, BLOCK), 1))
    block = jnp.broadcast_to(block.astype(f32), (total, BLOCK)).astype(bf16)
    found = None
    for g, copy in enumerate(copies):
        picks = [
            jnp.where(block == jnp.bfloat16(k), low_hot, jnp.bfloat16(0))
            for k in range(g * size // BLOCK, (g + 1) * size // BLOCK)
        ]
        copy.wait()
        part = dot(jnp.concatenate(picks, axis=1), table[pl.ds(g * size, size)])
        found = part if found is None else found + part
    found_ref[...] = found.astype(bf16)


def unit_of(users):
    width = users.shape[1]
    users = users.astype(f32)
    mean = jnp.mean(users * users, axis=1, keepdims=True)
    return (users * lax.rsqrt(mean + epsilon) * (1.0 / width**0.5)).astype(bf16)


def prepare_kernel(place_ref, asked_ref, *refs):
    *users, unit_ref, column_ref, line_ref = refs
    n = place_ref.shape[1]
    for k, users_ref in enumerate(users):
        unit_ref[pl.ds(k * n, n)] = unit_of(users_ref[...])
    eye = iota((n, n), 0) == iota((n, n), 1)
    column_ref[...] = jnp.sum(jnp.where(eye, place_ref[...], 0), axis=1, keepdims=True)
    line_ref[...] = asked_line(asked_ref[...]).astype(i32)


def main_kernel(fetched_ref, weight_ref, unit_ref, place_ref, column_ref, outgoing_ref, embed_ref, dhidden_ref):
    n = place_ref.shape[1]
    total, width = fetched_ref.shape
    root = 1.0 / width**0.5
    embed = dot(hot(column_ref[...] == iota((n, total), 1)), fetched_ref[...]).astype(bf16)
    hidden = dot(embed, weight_ref[...])
    rscale = lax.rsqrt(jnp.mean(hidden * hidden, axis=1, keepdims=True) + epsilon)
    item_vec = (hidden * (rscale * root)).astype(bf16)
    unit = unit_ref[...]
    expo = jnp.exp(dot(item_vec, unit, 1, 1) * score_scale)
    sums = jnp.sum(expo, axis=1, keepdims=True)
    mixed = dot(expo.astype(bf16), unit)
    own = unit_ref[pl.ds(0, n)].astype(f32)
    positive = jnp.sum(item_vec.astype(f32) * own, axis=1, keepdims=True) * score_scale
    xent = jnp.log(sums) - positive
    cweight = 1.0 / (1.0 + xent * (1.0 / cauchy_scale))
    dvec = (cweight * score_scale) * (mixed * (1.0 / sums) - own)
    inner = jnp.sum(hidden * dvec, axis=1, keepdims=True)
    dhidden = (rscale * root * (dvec - hidden * (rscale * rscale * inner * (1.0 / width)))).astype(bf16)
    outgoing_ref[...] = dot(hot(place_ref[...] == iota((total, n), 0)), dhidden).astype(bf16)
    embed_ref[...] = embed
    dhidden_ref[...] = dhidden


def share_kernel(embed_ref, dhidden_ref, keep_ref, *refs):
    *sends, share = refs
    share[...] = dot(embed_ref[...], dhidden_ref[...], 0, 0)
    count, size = len(sends) + 1, keep_ref.shape[0]
    me = lax.axis_index("batch")
    for step, ref in enumerate([keep_ref, *sends]):
        start = pl.multiple_of(lax.rem(me + step, count) * size, size)
        ref[...] = share[pl.ds(start, size)].astype(ref.dtype)


def combine_kernel(count, *refs):
    (kept, *came), (keep_ref, *sends), total = refs[:count], refs[count:-1], refs[-1]
    total[...] = kept[...] + sum(ref[...].astype(f32) for ref in came)
    me = lax.axis_index("item")
    for step, ref in enumerate([keep_ref, *sends]):
        ref[...] = total[lax.rem(me + step, total.shape[0])]


def table_kernel(line_ref, incoming_ref, weight_ref, table_grad_ref, drow, low_hot, block, pick):
    step = pl.program_id(0)
    chunk, total = pick.shape

    @pl.when(step == 0)
    def _():
        drow[...] = dot(incoming_ref[...], weight_ref[...], 1, 1).astype(bf16)
        high, low = parts_of(line_ref[...])
        low_hot[...] = hot(low == iota((BLOCK, total), 0))
        block[...] = jnp.broadcast_to(high.astype(f32), (BLOCK, total)).astype(bf16)

    for k in range(chunk // BLOCK):
        mine = (step * (chunk // BLOCK) + k).astype(f32).astype(bf16)
        pick[pl.ds(k * BLOCK, BLOCK)] = jnp.where(block[...] == mine, low_hot[...], jnp.bfloat16(0))
    table_grad_ref[...] = dot(pick[...], drow[...]).astype(bf16)


def params(mib=16):
    return pltpu.CompilerParams(vmem_limit_bytes=mib * 1024 * 1024)


def cost(flops, bytes_accessed=1 << 20):
    return pl.CostEstimate(flops=flops, bytes_accessed=bytes_accessed, transcendentals=0)


def call(kernel, outs, *args, flops=0, scratch=()):
    return pl.pallas_call(
        kernel,
        out_shape=[jax.ShapeDtypeStruct(shape, dtype) for shape, dtype in outs],
        scratch_shapes=scratch,
        compiler_params=params(),
        cost_estimate=cost(flops),
    )(*args)


def shift(value, axis, step):
    size = lax.axis_size(axis)
    return lax.ppermute(value, axis, [(k, (k + step) % size) for k in range(size)])


def local(user_vectors, item_table, tower_weight, item_owner, item_row):
    n, width = user_vectors.shape
    rows = item_table.shape[0]
    axes = ("batch", "item")
    n_batch, n_item = lax.axis_size("batch"), lax.axis_size("item")
    devices = n_batch * n_item
    slots = 2 * n // devices
    total = devices * slots
    chunk = min(1024, rows)
    groups = rows // chunk

    exchange = functools.partial(lax.all_to_all, axis_name=axes, split_axis=0, concat_axis=0, tiled=True)

    users = [user_vectors] + [shift(user_vectors, "batch", step) for step in range(1, n_batch)]
    request, place = call(
        request_kernel,
        [((devices, slots), i32), ((1, n), i32)],
        item_owner.reshape(1, n),
        item_row.reshape(1, n),
    )
    asked = exchange(request)
    found = pl.pallas_call(
        fetch_kernel,
        in_specs=[pl.BlockSpec(memory_space=pltpu.VMEM), pl.BlockSpec(memory_space=pltpu.HBM)],
        out_shape=jax.ShapeDtypeStruct((total, width), bf16),
        scratch_shapes=[pltpu.VMEM((rows, width), bf16), pltpu.SemaphoreType.DMA((groups,))],
        compiler_params=params(32),
        cost_estimate=cost(2 * total * rows * width, 2 * rows * width),
    )(asked, item_table)
    fetched = exchange(found.reshape(devices, slots, width)).reshape(total, width)
    unit, column, line = call(
        prepare_kernel,
        [((n_batch * n, width), bf16), ((n, 1), i32), ((1, total), i32)],
        place,
        asked,
        *users,
        flops=1 << 28,
    )
    outgoing, embed, dhidden = call(
        main_kernel,
        [((total, width), bf16), ((n, width), bf16), ((n, width), bf16)],
        fetched,
        tower_weight,
        unit,
        place,
        column,
        flops=1 << 30,
    )
    incoming = exchange(outgoing.reshape(devices, slots, width)).reshape(total, width)

    half = width // n_batch
    kept, *sends = call(
        share_kernel,
        [((half, width), f32)] + [((half, width), bf16)] * (n_batch - 1),
        embed,
        dhidden,
        flops=1 << 27,
        scratch=[pltpu.VMEM((width, width), f32)],
    )
    came = [shift(value, "batch", step + 1) for step, value in enumerate(sends)]
    part = half // n_item
    kept, *sends = call(
        functools.partial(combine_kernel, n_batch),
        [((part, width), f32)] * n_item,
        *[value.reshape(n_item, part, width) for value in [kept, *came]],
        flops=1 << 20,
        scratch=[pltpu.VMEM((n_item, part, width), f32)],
    )
    weight_grad = kept
    for step, value in enumerate(sends):
        weight_grad += shift(value, "item", step + 1)

    table_grad = pl.pallas_call(
        table_kernel,
        grid=(groups,),
        in_specs=[
            pl.BlockSpec((1, total), lambda k: (0, 0)),
            pl.BlockSpec((total, width), lambda k: (0, 0)),
            pl.BlockSpec((width, width), lambda k: (0, 0)),
        ],
        out_specs=pl.BlockSpec((chunk, width), lambda k: (k, 0)),
        out_shape=jax.ShapeDtypeStruct((rows, width), bf16),
        scratch_shapes=[
            pltpu.VMEM((total, width), bf16),
            pltpu.VMEM((BLOCK, total), bf16),
            pltpu.VMEM((BLOCK, total), bf16),
            pltpu.VMEM((chunk, total), bf16),
        ],
        compiler_params=params(32),
        cost_estimate=cost(2 * total * rows * width, 2 * rows * width),
    )(line, incoming, tower_weight)
    return (table_grad, weight_grad)


def solution(mesh):
    return jax.shard_map(
        local,
        mesh=mesh,
        in_specs=(
            P(("batch", "item"), None),
            P(("batch", "item"), None),
            P(),
            P(("batch", "item"), None),
            P(("batch", "item")),
        ),
        out_specs=(P(("batch", "item"), None), P(("batch", "item"), None)),
        check_vma=False,
    )
```

time: 100 us -> 85.1 us (0.85)
  starting transfers between devices: 7.85 us -> 27.2 us
  waiting for transfers between devices: 40.1 us -> 25.8 us
  between operations: 14.1 us -> 0.72 us
  Pallas kernels: 16.3 us -> 12.6 us
  local copies, waits for them, and re-layouts: 6.42 us -> 3.55 us
    ppermute x0 -> x13, waiting for transfers between devices: none -> 25.8 us  [shift(): lax.ppermute(value, axis, [(k, (k + step) % size) for k in range(size)])]
    ppermute x0 -> x13, starting transfers between devices: none -> 19.7 us  [shift(): lax.ppermute(value, axis, [(k, (k + step) % size) for k in range(size)])]
    all_to_all x1, waiting for transfers between devices: 15.2 us -> 0.01 us  [local(): exchange(outgoing.reshape(devices, slots, width)).reshape(total, width)]
    all_to_all x1, waiting for transfers between devices: 13.7 us -> 0.01 us  [local(): exchange(found.reshape(devices, slots, width)).reshape(total, width)]
    all_to_all x1 -> x0, waiting for transfers between devices: 10.5 us -> none  [local(): shares = exchange(share.reshape(devices, width // devices, width))]
    pallas_call x2, Pallas kernels: 11.7 us -> 8.74 us  [the longest x1 4.6 us: local(): pl.pallas_call(table_kernel, grid=(groups,), in_specs=[pl.BlockSpec((1, t...]
    unnamed x16 -> x10, local copies, waits for them, and re-layouts: 6.42 us -> 3.55 us
    all_to_all x1 -> x0, starting transfers between devices: 2.6 us -> none  [local(): shares = exchange(share.reshape(devices, width // devices, width))]
  transfers between devices with their start and end apart: 4 -> 15, of which waited for: 3 -> 8; matrix products, arithmetic and copies ran while one was open for 0% -> 1% of each run, Pallas kernels for 14% -> 1%
where the time goes in v2:
time: 85.1 us; the launch traced here: 84.7 us
  starting transfers between devices  27.2 us (32%)
  waiting for transfers between devices  25.8 us (30%)
  blocking collectives  14.2 us (17%)
  Pallas kernels  12.6 us (15%)
  local copies, waits for them, and re-layouts  3.55 us (4%)
    ppermute x13, waiting for transfers between devices, shift(): lax.ppermute(value, axis, [(k, (k + step) % size) for k in range(size)])  25.8 us
    ppermute x13, starting transfers between devices, shift(): lax.ppermute(value, axis, [(k, (k + step) % size) for k in range(size)])  19.7 us
    all_to_all x1, blocking collectives, local(): asked = exchange(request)  14.2 us
    all_to_all x1, starting transfers between devices, local(): exchange(outgoing.reshape(devices, slots, width)).reshape(total, width)  4.86 us
    pallas_call x1, Pallas kernels, local(): pl.pallas_call(table_kernel, grid=(groups,), in_specs=[pl.BlockSpec((1, t...  4.6 us
    pallas_call x1, Pallas kernels, local(): pl.pallas_call(fetch_kernel, in_specs=[pl.BlockSpec(memory_space=pltpu.VM...  4.13 us
    pallas_call x5, Pallas kernels, call(): pl.pallas_call(kernel, out_shape=[jax.ShapeDtypeStruct(shape, dtype) for...  3.85 us
    unnamed x10, local copies, waits for them, and re-layouts  3.55 us
  transfers between devices with their start and end apart: 15, of which 8 were waited for; matrix products, arithmetic and copies ran while one was open for 1% of the time, Pallas kernels for 1%

profile of v2, /device:TPU:0, one launch (start us, length us, event | category | flops | bytes accessed | tf_op | source)
XLA Modules:
  0.0 84.7 jit_solution(10873367239777800564)
XLA Ops:
  0.6 0.7 copy-done.1
  1.3 0.7 copy-done.2
  2.0 0.3 shard_map.68
  2.3 14.2 %all_to_all.21 = s32[32,1,16]{2,1,0:T(1,128)S(1)} all-to-all(s32[32,1,16]{2,1,0:T(1,128)S(1)} %bitcast.22), channel_id=1, replica_groups=mesh['batch'=4,'item'=8] {'batch','item'}, dimensions={0} | all-to-all | bytes 4096 | tf_op jit(solution)/shard_map/all_to_all | solution.py:222
  16.5 2.2 %copy-done.3 = bf16[4096,512]{1,0:T(8,128)(2,1)S(1)} copy-done((bf16[4096,512]{1,0:T(8,128)(2,1)S(1)}, bf16[4096,512]{1,0:T(8,128)(2,1)}, u32[]{:S(2)}) %copy-start.3) | copy-done | bytes 4194328
  18.7 4.1 %shard_map.70 = bf16[512,512]{1,0:T(8,128)(2,1)} custom-call(s32[32,16]{1,0:T(8,128)S(1)} %bitcast.20, bf16[4096,512]{1,0:T(8,128)(2,1)S(1)} %copy-done.3), custom_call_target="tpu_custom_call" | custom-call | flops 2147483648 | bytes 4194304 | tf_op jit(solution)/shard_map/pallas_call | solution.py:223
  22.8 2.6 %all-to-all-start.1 = ((bf16[32,16,512]{2,1,0:T(8,128)(2,1)}), bf16[32,16,512]{2,1,0:T(8,128)(2,1)S(1)}, u32[]{:S(2)}, u32[]{:S(2)}) async-start(bf16[32,16,512]{2,1,0:T(8,128)(2,1)} %bitcast.5), calls=%async_computation.1 | async-start | bytes 1048576 | tf_op jit(solution)/shard_map/all_to_all | solution.py:231
  25.5 1.7 %collective-permute-start.1 = (bf16[256,512]{1,0:T(8,128)(2,1)S(1)}, bf16[256,512]{1,0:T(8,128)(2,1)S(1)}, u32[]{:S(2)}, u32[]{:S(2)}) collective-permute-start(bf16[256,512]{1,0:T(8,128)(2,1)S(1)} %copy-done), channel_id=1, source_target_pairs={{0,16},{8,24},{16,0},{24,8},{1,17},{9,25},{17,1},{25,9},{2,18},{10... | collective-permute-start | bytes 786440 | tf_op jit(solution)/shard_map/ppermute | solution.py:199
  27.2 1.7 %collective-permute-start.2 = (bf16[256,512]{1,0:T(8,128)(2,1)S(1)}, bf16[256,512]{1,0:T(8,128)(2,1)S(1)}, u32[]{:S(2)}, u32[]{:S(2)}) collective-permute-start(bf16[256,512]{1,0:T(8,128)(2,1)S(1)} %copy-done), channel_id=1, source_target_pairs={{0,24},{8,0},{16,8},{24,16},{1,25},{9,1},{17,9},{25,17},{2,26},{10... | collective-permute-start | bytes 786440 | tf_op jit(solution)/shard_map/ppermute | solution.py:199
  28.9 10.3 %collective-permute-done.1.refs_2_ = bf16[256,512]{1,0:T(8,128)(2,1)S(1)} collective-permute-done((bf16[256,512]{1,0:T(8,128)(2,1)S(1)}, bf16[256,512]{1,0:T(8,128)(2,1)S(1)}, u32[]{:S(2)}, u32[]{:S(2)}) %collective-permute-start.1) | collective-permute-done | bytes 262176 | tf_op jit(solution)/shard_map/ppermute | solution.py:199
  39.2 5.3 %collective-permute-done.refs_1_ = bf16[256,512]{1,0:T(8,128)(2,1)S(1)} collective-permute-done((bf16[256,512]{1,0:T(8,128)(2,1)S(1)}, bf16[256,512]{1,0:T(8,128)(2,1)S(1)}, u32[]{:S(2)}, u32[]{:S(2)}) %collective-permute-start) | collective-permute-done | bytes 262176 | tf_op jit(solution)/shard_map/ppermute | solution.py:199
  44.6 0.5 shard_map.69
  45.1 2.5 %shard_map.71 = (bf16[512,512]{1,0:T(8,128)(2,1)}, bf16[256,512]{1,0:T(8,128)(2,1)S(1)}, bf16[256,512]{1,0:T(8,128)(2,1)S(1)}) custom-call(bf16[512,512]{1,0:T(8,128)(2,1)S(1)} %bitcast.15, bf16[512,512]{1,0:T(8,128)(2,1)S(1)} %copy-done.4, bf16[1024,512]{1,0:T(8,128)(2,1)S(1)} %get-tuple-element.25.unit_ref, s32[1,256]{1,0:T(1,128)S(1)} %get-tuple-element.22.place_ref, ...), custom_call_target="tpu_custom_call" | custom-call | flops 1073741824 | bytes 1048576 | tf_op jit(solution)/shard_map/pallas_call | solution.py:188
  47.7 4.9 %all-to-all-start.2 = ((bf16[32,16,512]{2,1,0:T(8,128)(2,1)}), bf16[32,16,512]{2,1,0:T(8,128)(2,1)S(1)}, u32[]{:S(2)}, u32[]{:S(2)}) async-start(bf16[32,16,512]{2,1,0:T(8,128)(2,1)} %bitcast.7), calls=%async_computation.2 | async-start | bytes 1048576 | tf_op jit(solution)/shard_map/all_to_all | solution.py:250
  52.5 0.4 shard_map.73
  53.0 0.3 collective-permute-start.3
  53.3 1.7 %collective-permute-start.4 = (bf16[128,512]{1,0:T(8,128)(2,1)S(1)}, bf16[128,512]{1,0:T(8,128)(2,1)S(1)}, u32[]{:S(2)}, u32[]{:S(2)}) collective-permute-start(bf16[128,512]{1,0:T(8,128)(2,1)S(1)} %get-tuple-element.32), channel_id=1, source_target_pairs={{0,16},{8,24},{16,0},{24,8},{1,17},{9,25},{17,1},{25,9},{2,18},{10... | collective-permute-start | bytes 393224 | tf_op jit(solution)/shard_map/ppermute | solution.py:199
  54.9 1.3 %collective-permute-start.5 = (bf16[128,512]{1,0:T(8,128)(2,1)S(1)}, bf16[128,512]{1,0:T(8,128)(2,1)S(1)}, u32[]{:S(2)}, u32[]{:S(2)}) collective-permute-start(bf16[128,512]{1,0:T(8,128)(2,1)S(1)} %get-tuple-element.33), channel_id=1, source_target_pairs={{0,24},{8,0},{16,8},{24,16},{1,25},{9,1},{17,9},{25,17},{2,26},{10... | collective-permute-start | bytes 393224 | tf_op jit(solution)/shard_map/ppermute | solution.py:199
  56.3 5.2 %collective-permute-done.3 = bf16[128,512]{1,0:T(8,128)(2,1)S(1)} collective-permute-done((bf16[128,512]{1,0:T(8,128)(2,1)S(1)}, bf16[128,512]{1,0:T(8,128)(2,1)S(1)}, u32[]{:S(2)}, u32[]{:S(2)}) %collective-permute-start.3) | collective-permute-done | bytes 131104 | tf_op jit(solution)/shard_map/ppermute | solution.py:199
  61.4 1.3 %collective-permute-done.4 = bf16[128,512]{1,0:T(8,128)(2,1)S(1)} collective-permute-done((bf16[128,512]{1,0:T(8,128)(2,1)S(1)}, bf16[128,512]{1,0:T(8,128)(2,1)S(1)}, u32[]{:S(2)}, u32[]{:S(2)}) %collective-permute-start.4) | collective-permute-done | bytes 131104 | tf_op jit(solution)/shard_map/ppermute | solution.py:199
  62.7 1.2 %collective-permute-done.5 = bf16[128,512]{1,0:T(8,128)(2,1)S(1)} collective-permute-done((bf16[128,512]{1,0:T(8,128)(2,1)S(1)}, bf16[128,512]{1,0:T(8,128)(2,1)S(1)}, u32[]{:S(2)}, u32[]{:S(2)}) %collective-permute-start.5) | collective-permute-done | bytes 131104 | tf_op jit(solution)/shard_map/ppermute | solution.py:199
  64.0 1.9 %collective-permute-start.6 = (f32[16,512]{1,0:T(8,128)S(1)}, f32[16,512]{1,0:T(8,128)S(1)}, u32[]{:S(2)}, u32[]{:S(2)}) collective-permute-start(f32[16,512]{1,0:T(8,128)S(1)} %get-tuple-element.35), channel_id=1, source_target_pairs={{0,1},{1,2},{2,3},{3,4},{4,5},{5,6},{6,7},{7,0},{8,9},{9,10},{10,1... | collective-permute-start | bytes 98312 | tf_op jit(solution)/shard_map/ppermute | solution.py:199
  65.9 1.8 %collective-permute-start.7 = (f32[16,512]{1,0:T(8,128)S(1)}, f32[16,512]{1,0:T(8,128)S(1)}, u32[]{:S(2)}, u32[]{:S(2)}) collective-permute-start(f32[16,512]{1,0:T(8,128)S(1)} %get-tuple-element.36), channel_id=1, source_target_pairs={{0,2},{1,3},{2,4},{3,5},{4,6},{5,7},{6,0},{7,1},{8,10},{9,11},{10,... | collective-permute-start | bytes 98312 | tf_op jit(solution)/shard_map/ppermute | solution.py:199
  67.7 2.6 %collective-permute-start.8 = (f32[16,512]{1,0:T(8,128)S(1)}, f32[16,512]{1,0:T(8,128)S(1)}, u32[]{:S(2)}, u32[]{:S(2)}) collective-permute-start(f32[16,512]{1,0:T(8,128)S(1)} %get-tuple-element.37), channel_id=1, source_target_pairs={{0,3},{1,4},{2,5},{3,6},{4,7},{5,0},{6,1},{7,2},{8,11},{9,12},{10,... | collective-permute-start | bytes 98312 | tf_op jit(solution)/shard_map/ppermute | solution.py:199
  70.3 1.2 %collective-permute-start.9 = (f32[16,512]{1,0:T(8,128)S(1)}, f32[16,512]{1,0:T(8,128)S(1)}, u32[]{:S(2)}, u32[]{:S(2)}) collective-permute-start(f32[16,512]{1,0:T(8,128)S(1)} %get-tuple-element.38), channel_id=1, source_target_pairs={{0,4},{1,5},{2,6},{3,7},{4,0},{5,1},{6,2},{7,3},{8,12},{9,13},{10,... | collective-permute-start | bytes 98312 | tf_op jit(solution)/shard_map/ppermute | solution.py:199
  71.5 2.6 %collective-permute-start.10 = (f32[16,512]{1,0:T(8,128)S(1)}, f32[16,512]{1,0:T(8,128)S(1)}, u32[]{:S(2)}, u32[]{:S(2)}) collective-permute-start(f32[16,512]{1,0:T(8,128)S(1)} %get-tuple-element.39), channel_id=1, source_target_pairs={{0,5},{1,6},{2,7},{3,0},{4,1},{5,2},{6,3},{7,4},{8,13},{9,14},{10,... | collective-permute-start | bytes 98312 | tf_op jit(solution)/shard_map/ppermute | solution.py:199
  74.1 1.4 %collective-permute-start.11 = (f32[16,512]{1,0:T(8,128)S(1)}, f32[16,512]{1,0:T(8,128)S(1)}, u32[]{:S(2)}, u32[]{:S(2)}) collective-permute-start(f32[16,512]{1,0:T(8,128)S(1)} %get-tuple-element.40), channel_id=1, source_target_pairs={{0,6},{1,7},{2,0},{3,1},{4,2},{5,3},{6,4},{7,5},{8,14},{9,15},{10,... | collective-permute-start | bytes 98312 | tf_op jit(solution)/shard_map/ppermute | solution.py:199
  75.5 1.4 %collective-permute-start.12 = (f32[16,512]{1,0:T(8,128)S(1)}, f32[16,512]{1,0:T(8,128)S(1)}, u32[]{:S(2)}, u32[]{:S(2)}) collective-permute-start(f32[16,512]{1,0:T(8,128)S(1)} %get-tuple-element.41), channel_id=1, source_target_pairs={{0,7},{1,0},{2,1},{3,2},{4,3},{5,4},{6,5},{7,6},{8,15},{9,8},{10,9... | collective-permute-start | bytes 98312 | tf_op jit(solution)/shard_map/ppermute | solution.py:199
  77.2 0.8 collective-permute-done.11
  78.0 1.4 %collective-permute-done.12 = f32[16,512]{1,0:T(8,128)S(1)} collective-permute-done((f32[16,512]{1,0:T(8,128)S(1)}, f32[16,512]{1,0:T(8,128)S(1)}, u32[]{:S(2)}, u32[]{:S(2)}) %collective-permute-start.12) | collective-permute-done | bytes 32800 | tf_op jit(solution)/shard_map/ppermute | solution.py:199
  79.4 0.6 add_add_fusion
  80.1 4.6 %shard_map.72 = bf16[4096,512]{1,0:T(8,128)(2,1)} custom-call(s32[1,512]{1,0:T(1,128)S(1)} %get-tuple-element.24.line_ref, bf16[512,512]{1,0:T(8,128)(2,1)S(1)} %bitcast.14, bf16[512,512]{1,0:T(8,128)(2,1)S(1)} %copy-done.4), custom_call_target="tpu_custom_call" | custom-call | flops 2147483648 | bytes 4194304 | tf_op jit(solution)/shard_map/pallas_call | solution.py:274
  (17 shorter events, 0.4 us)
Async XLA Ops:
  0.6 0.7 copy-start.1
  1.3 0.7 copy-start.2
  16.5 2.2 %copy-start.3 = (bf16[4096,512]{1,0:T(8,128)(2,1)S(1)}, bf16[4096,512]{1,0:T(8,128)(2,1)}, u32[]{:S(2)}) copy-start(bf16[4096,512]{1,0:T(8,128)(2,1)} %table_hbm.1) | copy-start | bytes 12582916
  18.7 6.8 %copy-start = (bf16[256,512]{1,0:T(8,128)(2,1)S(1)}, bf16[256,512]{1,0:T(8,128)(2,1)}, u32[]{:S(2)}) copy-start(bf16[256,512]{1,0:T(8,128)(2,1)} %refs_0_.1) | copy-start | bytes 786436
  18.7 26.4 %copy-start.4 = (bf16[512,512]{1,0:T(8,128)(2,1)S(1)}, bf16[512,512]{1,0:T(8,128)(2,1)}, u32[]{:S(2)}) copy-start(bf16[512,512]{1,0:T(8,128)(2,1)} %weight_ref.3) | copy-start | bytes 1572868
  22.8 22.3 %all-to-all-start.1 = ((bf16[32,16,512]{2,1,0:T(8,128)(2,1)}), bf16[32,16,512]{2,1,0:T(8,128)(2,1)S(1)}, u32[]{:S(2)}, u32[]{:S(2)}) async-start(bf16[32,16,512]{2,1,0:T(8,128)(2,1)} %bitcast.5), calls=%async_computation.1 | async-start | bytes 1048576 | tf_op jit(solution)/shard_map/all_to_all | solution.py:231
  25.5 13.8 %collective-permute-start.1 = (bf16[256,512]{1,0:T(8,128)(2,1)S(1)}, bf16[256,512]{1,0:T(8,128)(2,1)S(1)}, u32[]{:S(2)}, u32[]{:S(2)}) collective-permute-start(bf16[256,512]{1,0:T(8,128)(2,1)S(1)} %copy-done), channel_id=1, source_target_pairs={{0,16},{8,24},{16,0},{24,8},{1,17},{9,25},{17,1},{25,9},{2,18},{10... | collective-permute-start | bytes 786440 | tf_op jit(solution)/shard_map/ppermute | solution.py:199
  27.2 17.4 %collective-permute-start = (bf16[256,512]{1,0:T(8,128)(2,1)S(1)}, bf16[256,512]{1,0:T(8,128)(2,1)S(1)}, u32[]{:S(2)}, u32[]{:S(2)}) collective-permute-start(bf16[256,512]{1,0:T(8,128)(2,1)S(1)} %copy-done), channel_id=1, source_target_pairs={{0,8},{8,16},{16,24},{24,0},{1,9},{9,17},{17,25},{25,1},{2,10},{10... | collective-permute-start | bytes 786440 | tf_op jit(solution)/shard_map/ppermute | solution.py:199
  27.2 17.4 %collective-permute-start.2 = (bf16[256,512]{1,0:T(8,128)(2,1)S(1)}, bf16[256,512]{1,0:T(8,128)(2,1)S(1)}, u32[]{:S(2)}, u32[]{:S(2)}) collective-permute-start(bf16[256,512]{1,0:T(8,128)(2,1)S(1)} %copy-done), channel_id=1, source_target_pairs={{0,24},{8,0},{16,8},{24,16},{1,25},{9,1},{17,9},{25,17},{2,26},{10... | collective-permute-start | bytes 786440 | tf_op jit(solution)/shard_map/ppermute | solution.py:199
  47.7 32.4 %all-to-all-start.2 = ((bf16[32,16,512]{2,1,0:T(8,128)(2,1)}), bf16[32,16,512]{2,1,0:T(8,128)(2,1)S(1)}, u32[]{:S(2)}, u32[]{:S(2)}) async-start(bf16[32,16,512]{2,1,0:T(8,128)(2,1)} %bitcast.7), calls=%async_computation.2 | async-start | bytes 1048576 | tf_op jit(solution)/shard_map/all_to_all | solution.py:250
  53.0 8.5 %collective-permute-start.3 = (bf16[128,512]{1,0:T(8,128)(2,1)S(1)}, bf16[128,512]{1,0:T(8,128)(2,1)S(1)}, u32[]{:S(2)}, u32[]{:S(2)}) collective-permute-start(bf16[128,512]{1,0:T(8,128)(2,1)S(1)} %get-tuple-element.31), channel_id=1, source_target_pairs={{0,8},{8,16},{16,24},{24,0},{1,9},{9,17},{17,25},{25,1},{2,10},{10... | collective-permute-start | bytes 393224 | tf_op jit(solution)/shard_map/ppermute | solution.py:199
  53.3 9.4 %collective-permute-start.4 = (bf16[128,512]{1,0:T(8,128)(2,1)S(1)}, bf16[128,512]{1,0:T(8,128)(2,1)S(1)}, u32[]{:S(2)}, u32[]{:S(2)}) collective-permute-start(bf16[128,512]{1,0:T(8,128)(2,1)S(1)} %get-tuple-element.32), channel_id=1, source_target_pairs={{0,16},{8,24},{16,0},{24,8},{1,17},{9,25},{17,1},{25,9},{2,18},{10... | collective-permute-start | bytes 393224 | tf_op jit(solution)/shard_map/ppermute | solution.py:199
  54.9 9.0 %collective-permute-start.5 = (bf16[128,512]{1,0:T(8,128)(2,1)S(1)}, bf16[128,512]{1,0:T(8,128)(2,1)S(1)}, u32[]{:S(2)}, u32[]{:S(2)}) collective-permute-start(bf16[128,512]{1,0:T(8,128)(2,1)S(1)} %get-tuple-element.33), channel_id=1, source_target_pairs={{0,24},{8,0},{16,8},{24,16},{1,25},{9,1},{17,9},{25,17},{2,26},{10... | collective-permute-start | bytes 393224 | tf_op jit(solution)/shard_map/ppermute | solution.py:199
  64.0 10.1 %collective-permute-start.6 = (f32[16,512]{1,0:T(8,128)S(1)}, f32[16,512]{1,0:T(8,128)S(1)}, u32[]{:S(2)}, u32[]{:S(2)}) collective-permute-start(f32[16,512]{1,0:T(8,128)S(1)} %get-tuple-element.35), channel_id=1, source_target_pairs={{0,1},{1,2},{2,3},{3,4},{4,5},{5,6},{6,7},{7,0},{8,9},{9,10},{10,1... | collective-permute-start | bytes 98312 | tf_op jit(solution)/shard_map/ppermute | solution.py:199
  65.9 9.6 %collective-permute-start.7 = (f32[16,512]{1,0:T(8,128)S(1)}, f32[16,512]{1,0:T(8,128)S(1)}, u32[]{:S(2)}, u32[]{:S(2)}) collective-permute-start(f32[16,512]{1,0:T(8,128)S(1)} %get-tuple-element.36), channel_id=1, source_target_pairs={{0,2},{1,3},{2,4},{3,5},{4,6},{5,7},{6,0},{7,1},{8,10},{9,11},{10,... | collective-permute-start | bytes 98312 | tf_op jit(solution)/shard_map/ppermute | solution.py:199
  67.7 9.3 %collective-permute-start.8 = (f32[16,512]{1,0:T(8,128)S(1)}, f32[16,512]{1,0:T(8,128)S(1)}, u32[]{:S(2)}, u32[]{:S(2)}) collective-permute-start(f32[16,512]{1,0:T(8,128)S(1)} %get-tuple-element.37), channel_id=1, source_target_pairs={{0,3},{1,4},{2,5},{3,6},{4,7},{5,0},{6,1},{7,2},{8,11},{9,12},{10,... | collective-permute-start | bytes 98312 | tf_op jit(solution)/shard_map/ppermute | solution.py:199
  70.3 6.7 %collective-permute-start.9 = (f32[16,512]{1,0:T(8,128)S(1)}, f32[16,512]{1,0:T(8,128)S(1)}, u32[]{:S(2)}, u32[]{:S(2)}) collective-permute-start(f32[16,512]{1,0:T(8,128)S(1)} %get-tuple-element.38), channel_id=1, source_target_pairs={{0,4},{1,5},{2,6},{3,7},{4,0},{5,1},{6,2},{7,3},{8,12},{9,13},{10,... | collective-permute-start | bytes 98312 | tf_op jit(solution)/shard_map/ppermute | solution.py:199
  71.5 5.7 %collective-permute-start.10 = (f32[16,512]{1,0:T(8,128)S(1)}, f32[16,512]{1,0:T(8,128)S(1)}, u32[]{:S(2)}, u32[]{:S(2)}) collective-permute-start(f32[16,512]{1,0:T(8,128)S(1)} %get-tuple-element.39), channel_id=1, source_target_pairs={{0,5},{1,6},{2,7},{3,0},{4,1},{5,2},{6,3},{7,4},{8,13},{9,14},{10,... | collective-permute-start | bytes 98312 | tf_op jit(solution)/shard_map/ppermute | solution.py:199
  74.1 3.9 %collective-permute-start.11 = (f32[16,512]{1,0:T(8,128)S(1)}, f32[16,512]{1,0:T(8,128)S(1)}, u32[]{:S(2)}, u32[]{:S(2)}) collective-permute-start(f32[16,512]{1,0:T(8,128)S(1)} %get-tuple-element.40), channel_id=1, source_target_pairs={{0,6},{1,7},{2,0},{3,1},{4,2},{5,3},{6,4},{7,5},{8,14},{9,15},{10,... | collective-permute-start | bytes 98312 | tf_op jit(solution)/shard_map/ppermute | solution.py:199
  75.5 3.9 %collective-permute-start.12 = (f32[16,512]{1,0:T(8,128)S(1)}, f32[16,512]{1,0:T(8,128)S(1)}, u32[]{:S(2)}, u32[]{:S(2)}) collective-permute-start(f32[16,512]{1,0:T(8,128)S(1)} %get-tuple-element.41), channel_id=1, source_target_pairs={{0,7},{1,0},{2,1},{3,2},{4,3},{5,4},{6,5},{7,6},{8,15},{9,8},{10,9... | collective-permute-start | bytes 98312 | tf_op jit(solution)/shard_map/ppermute | solution.py:199

commit v3 on v2

--- a/solution.py
+++ b/solution.py
@@ -32,15 +32,15 @@
     return (value >> 8).astype(f32), (value & 255).astype(f32)
 
 
-def request_kernel(owner_ref, row_ref, request_ref, place_ref):
+def request_kernel(named_ref, request_ref, place_ref):
     devices, slots = request_ref.shape
-    n = owner_ref.shape[1]
-    owner = owner_ref[...]
+    n = named_ref.shape[1]
+    owner, row = named_ref[0:1], named_ref[1:2]
     named = owner == iota((devices, n), 0)
     count = dot(hot(named), hot(iota((n, n), 0) <= iota((n, n), 1)))
     rank = jnp.sum(jnp.where(named, count, 0.0), axis=0, keepdims=True).astype(i32) - 1
     in_slot = hot(rank == iota((slots, n), 0))
-    high, low = halves(row_ref[...] + 1)
+    high, low = halves(row + 1)
     high = dot(jnp.where(named, high, 0.0).astype(bf16), in_slot, 1, 1)
     low = dot(jnp.where(named, low, 0.0).astype(bf16), in_slot, 1, 1)
     request_ref[...] = (high * 256.0 + low).astype(i32) - 1
@@ -141,22 +141,25 @@
     dhidden_ref[...] = dhidden
 
 
-def share_kernel(embed_ref, dhidden_ref, keep_ref, *refs):
-    *sends, share = refs
-    share[...] = dot(embed_ref[...], dhidden_ref[...], 0, 0)
-    count, size = len(sends) + 1, keep_ref.shape[0]
-    me = lax.axis_index("batch")
-    for step, ref in enumerate([keep_ref, *sends]):
-        start = pl.multiple_of(lax.rem(me + step, count) * size, size)
-        ref[...] = share[pl.ds(start, size)].astype(ref.dtype)
-
-
-def combine_kernel(count, *refs):
-    (kept, *came), (keep_ref, *sends), total = refs[:count], refs[count:-1], refs[-1]
-    total[...] = kept[...] + sum(ref[...].astype(f32) for ref in came)
-    me = lax.axis_index("item")
-    for step, ref in enumerate([keep_ref, *sends]):
-        ref[...] = total[lax.rem(me + step, total.shape[0])]
+def halve(blocks, bit, keep_ref, send_ref):
+    half = keep_ref.shape[0]
+    axis, level = bit
+    mine = (lax.axis_index(axis) >> level) & 1
+    keep_ref[...] = blocks[pl.ds(mine * half, half)]
+    send_ref[...] = blocks[pl.ds((1 - mine) * half, half)].astype(send_ref.dtype)
+
+
+def share_kernel(order, bit, embed_ref, dhidden_ref, keep_ref, send_ref, blocks):
+    share = dot(embed_ref[...], dhidden_ref[...], 0, 0)
+    size = blocks.shape[1]
+    for spot, block in enumerate(order):
+        blocks[spot] = share[block * size : (block + 1) * size]
+    halve(blocks, bit, keep_ref, send_ref)
+
+
+def halve_kernel(bit, kept_ref, came_ref, keep_ref, send_ref, blocks):
+    blocks[...] = kept_ref[...] + came_ref[...].astype(f32)
+    halve(blocks, bit, keep_ref, send_ref)
 
 
 def table_kernel(line_ref, incoming_ref, weight_ref, table_grad_ref, drow, low_hot, block, pick):
@@ -194,9 +197,13 @@
     )(*args)
 
 
-def shift(value, axis, step):
-    size = lax.axis_size(axis)
-    return lax.ppermute(value, axis, [(k, (k + step) % size) for k in range(size)])
+def swap(value, bit):
+    axis, level = bit
+    return lax.ppermute(value, axis, [(k, k ^ (1 << level)) for k in range(lax.axis_size(axis))])
+
+
+def bits_of(axis):
+    return [(axis, level) for level in range(lax.axis_size(axis).bit_length() - 1)]
 
 
 def local(user_vectors, item_table, tower_weight, item_owner, item_row):
@@ -212,20 +219,22 @@
 
     exchange = functools.partial(lax.all_to_all, axis_name=axes, split_axis=0, concat_axis=0, tiled=True)
 
-    users = [user_vectors] + [shift(user_vectors, "batch", step) for step in range(1, n_batch)]
+    users = [user_vectors]
+    for bit in reversed(bits_of("batch")):
+        users += [swap(value, bit) for value in users]
     request, place = call(
         request_kernel,
         [((devices, slots), i32), ((1, n), i32)],
-        item_owner.reshape(1, n),
-        item_row.reshape(1, n),
+        jnp.stack([item_owner.reshape(n), item_row]),
     )
-    asked = exchange(request)
+    early = n_batch // 2 + 1
+    asked, *users[1:early] = lax.optimization_barrier((exchange(request), *users[1:early]))
     found = pl.pallas_call(
         fetch_kernel,
         in_specs=[pl.BlockSpec(memory_space=pltpu.VMEM), pl.BlockSpec(memory_space=pltpu.HBM)],
         out_shape=jax.ShapeDtypeStruct((total, width), bf16),
         scratch_shapes=[pltpu.VMEM((rows, width), bf16), pltpu.SemaphoreType.DMA((groups,))],
-        compiler_params=params(32),
+        compiler_params=params(61),
         cost_estimate=cost(2 * total * rows * width, 2 * rows * width),
     )(asked, item_table)
     fetched = exchange(found.reshape(devices, slots, width)).reshape(total, width)
@@ -249,27 +258,26 @@
     )
     incoming = exchange(outgoing.reshape(devices, slots, width)).reshape(total, width)
 
-    half = width // n_batch
-    kept, *sends = call(
-        share_kernel,
-        [((half, width), f32)] + [((half, width), bf16)] * (n_batch - 1),
-        embed,
-        dhidden,
-        flops=1 << 27,
-        scratch=[pltpu.VMEM((width, width), f32)],
-    )
-    came = [shift(value, "batch", step + 1) for step, value in enumerate(sends)]
-    part = half // n_item
-    kept, *sends = call(
-        functools.partial(combine_kernel, n_batch),
-        [((part, width), f32)] * n_item,
-        *[value.reshape(n_item, part, width) for value in [kept, *came]],
-        flops=1 << 20,
-        scratch=[pltpu.VMEM((n_item, part, width), f32)],
-    )
-    weight_grad = kept
-    for step, value in enumerate(sends):
-        weight_grad += shift(value, "item", step + 1)
+    part = width // devices
+    bits = bits_of("batch") + bits_of("item")
+    order = []
+    for spot in range(devices):
+        at = {"batch": 0, "item": 0}
+        for k, (axis, level) in enumerate(bits):
+            at[axis] |= (spot >> (len(bits) - 1 - k) & 1) << level
+        order.append(at["batch"] * n_item + at["item"])
+    kept, came = None, None
+    for k, bit in enumerate(bits):
+        half = devices >> (k + 1)
+        outs = [((half, part, width), f32), ((half, part, width), bf16 if half >= 4 else f32)]
+        scratch = [pltpu.VMEM((2 * half, part, width), f32)]
+        if k == 0:
+            kernel = functools.partial(share_kernel, order, bit)
+            kept, sent = call(kernel, outs, embed, dhidden, flops=1 << 27, scratch=scratch)
+        else:
+            kept, sent = call(functools.partial(halve_kernel, bit), outs, kept, came, scratch=scratch)
+        came = swap(sent, bit)
+    weight_grad = (kept + came.astype(f32)).reshape(part, width)
 
     table_grad = pl.pallas_call(
         table_kernel,

time: 85.1 us -> 75.9 us (0.89)
  starting transfers between devices: 27.2 us -> 17.5 us
  waiting for transfers between devices: 25.8 us -> 29.7 us
  local copies, waits for them, and re-layouts: 3.55 us -> 0.01 us
  blocking collectives: 14.2 us -> 11.9 us
  Pallas kernels: 12.6 us -> 14.2 us
    all_to_all x1, waiting for transfers between devices: 0.01 us -> 14.2 us  [local(): exchange(found.reshape(devices, slots, width)).reshape(total, width)]
    ppermute x13 -> x8, waiting for transfers between devices: 25.8 us -> 15.5 us  [swap(): lax.ppermute(value, axis, [(k, k ^ 1 << level) for k in range(lax.axis_si...]
    ppermute x13 -> x8, starting transfers between devices: 19.7 us -> 12.2 us  [swap(): lax.ppermute(value, axis, [(k, k ^ 1 << level) for k in range(lax.axis_si...]
    unnamed x10 -> x6, local copies, waits for them, and re-layouts: 3.55 us -> 0.01 us
    all_to_all x1, blocking collectives: 14.2 us -> 11.9 us  [local(): exchange(request)]
    all_to_all x1, starting transfers between devices: 4.86 us -> 2.61 us  [local(): exchange(outgoing.reshape(devices, slots, width)).reshape(total, width)]
    pallas_call x1, Pallas kernels: 4.13 us -> 5.68 us  [local(): pl.pallas_call(fetch_kernel, in_specs=[pl.BlockSpec(memory_space=pltpu.VM...]
    pallas_call x5 -> x8, Pallas kernels: 3.85 us -> 3.96 us  [call(): pl.pallas_call(kernel, out_shape=[jax.ShapeDtypeStruct(shape, dtype) for...]
  transfers between devices with their start and end apart: 15 -> 10, of which waited for: 8 -> 7; matrix products, arithmetic and copies ran while one was open for 1% -> 2% of each run, Pallas kernels for 1% -> 2%
where the time goes in v3:
time: 75.9 us; the launch traced here: 75.4 us
  waiting for transfers between devices  29.7 us (39%)
  starting transfers between devices  17.5 us (23%)
  Pallas kernels  14.2 us (19%)
  blocking collectives  11.9 us (16%)
  other arithmetic  1.32 us (2%)
    ppermute x8, waiting for transfers between devices, swap(): lax.ppermute(value, axis, [(k, k ^ 1 << level) for k in range(lax.axis_si...  15.5 us
    all_to_all x1, waiting for transfers between devices, local(): exchange(found.reshape(devices, slots, width)).reshape(total, width)  14.2 us
    ppermute x8, starting transfers between devices, swap(): lax.ppermute(value, axis, [(k, k ^ 1 << level) for k in range(lax.axis_si...  12.2 us
    all_to_all x1, blocking collectives, local(): exchange(request)  11.9 us
    pallas_call x1, Pallas kernels, local(): pl.pallas_call(fetch_kernel, in_specs=[pl.BlockSpec(memory_space=pltpu.VM...  5.68 us
    pallas_call x1, Pallas kernels, local(): pl.pallas_call(table_kernel, grid=(groups,), in_specs=[pl.BlockSpec((1, t...  4.6 us
    pallas_call x8, Pallas kernels, call(): pl.pallas_call(kernel, out_shape=[jax.ShapeDtypeStruct(shape, dtype) for...  3.96 us
    all_to_all x1, starting transfers between devices, local(): exchange(found.reshape(devices, slots, width)).reshape(total, width)  2.62 us
  transfers between devices with their start and end apart: 10, of which 7 were waited for; matrix products, arithmetic and copies ran while one was open for 2% of the time, Pallas kernels for 2%

profile of v3, /device:TPU:0, one launch (start us, length us, event | category | flops | bytes accessed | tf_op | source)
XLA Modules:
  0.0 75.4 jit_solution(888369845968479500)
XLA Ops:
  0.6 3.0 %collective-permute-start = (bf16[256,512]{1,0:T(8,128)(2,1)}, bf16[256,512]{1,0:T(8,128)(2,1)S(1)}, u32[]{:S(2)}, u32[]{:S(2)}) collective-permute-start(bf16[256,512]{1,0:T(8,128)(2,1)} %refs_0_.1), channel_id=1, source_target_pairs={{0,16},{8,24},{16,0},{24,8},{1,17},{9,25},{17,1},{25,9},{2,18},{10... | collective-permute-start | bytes 786440 | tf_op jit(solution)/shard_map/ppermute | solution.py:202
  3.6 0.0 collective-permute-start.1
  3.6 0.7 pad_add_fusion.named_ref
  4.3 0.3 shard_map.68
  4.6 11.9 %all_to_all.22 = s32[32,1,16]{2,1,0:T(1,128)} all-to-all(s32[32,1,16]{2,1,0:T(1,128)S(1)} %bitcast.16), channel_id=1, replica_groups=mesh['batch'=4,'item'=8] {'batch','item'}, dimensions={0} | all-to-all | bytes 4096 | tf_op jit(solution)/shard_map/all_to_all | solution.py:231
  16.6 0.0 collective-permute-done.refs_1_
  16.6 0.0 collective-permute-done.1.refs_2_
  16.6 0.0 copy-start.1
  16.6 0.0 copy-start.2
  16.6 5.7 %shard_map.70 = bf16[512,512]{1,0:T(8,128)(2,1)} custom-call(s32[32,16]{1,0:T(8,128)} %bitcast.14, bf16[4096,512]{1,0:T(8,128)(2,1)} %table_hbm.1), custom_call_target="tpu_custom_call" | custom-call | flops 2147483648 | bytes 4194304 | tf_op jit(solution)/shard_map/pallas_call | solution.py:232
  22.3 2.6 %all-to-all-start.1 = ((bf16[32,16,512]{2,1,0:T(8,128)(2,1)}), bf16[32,16,512]{2,1,0:T(8,128)(2,1)S(1)}, u32[]{:S(2)}, u32[]{:S(2)}) async-start(bf16[32,16,512]{2,1,0:T(8,128)(2,1)} %bitcast.17), calls=%async_computation.1 | async-start | bytes 1048576 | tf_op jit(solution)/shard_map/all_to_all | solution.py:240
  24.9 0.2 collective-permute-start.2
  25.1 1.4 %collective-permute-done.2.refs_3_ = bf16[256,512]{1,0:T(8,128)(2,1)S(1)} collective-permute-done((bf16[256,512]{1,0:T(8,128)(2,1)S(1)}, bf16[256,512]{1,0:T(8,128)(2,1)S(1)}, u32[]{:S(2)}, u32[]{:S(2)}) %collective-permute-start.2) | collective-permute-done | bytes 262176 | tf_op jit(solution)/shard_map/ppermute | solution.py:202
  26.5 0.5 shard_map.69
  27.0 14.2 %all-to-all-done.1 = bf16[32,16,512]{2,1,0:T(8,128)(2,1)S(1)} async-done(((bf16[32,16,512]{2,1,0:T(8,128)(2,1)}), bf16[32,16,512]{2,1,0:T(8,128)(2,1)S(1)}, u32[]{:S(2)}, u32[]{:S(2)}) %all-to-all-start.1) | async-done | bytes 524320 | tf_op jit(solution)/shard_map/all_to_all | solution.py:240
  41.3 2.5 %shard_map.71 = (bf16[512,512]{1,0:T(8,128)(2,1)}, bf16[256,512]{1,0:T(8,128)(2,1)S(1)}, bf16[256,512]{1,0:T(8,128)(2,1)S(1)}) custom-call(bf16[512,512]{1,0:T(8,128)(2,1)S(1)} %bitcast.13, bf16[512,512]{1,0:T(8,128)(2,1)S(1)} %copy-done.2, bf16[1024,512]{1,0:T(8,128)(2,1)S(1)} %get-tuple-element.29.unit_ref, s32[1,256]{1,0:T(1,128)S(1)} %get-tuple-element.23.place_ref, ...), custom_call_target="tpu_custom_call" | custom-call | flops 1073741824 | bytes 1048576 | tf_op jit(solution)/shard_map/pallas_call | solution.py:191
  43.8 2.6 %all-to-all-start.2 = ((bf16[32,16,512]{2,1,0:T(8,128)(2,1)}), bf16[32,16,512]{2,1,0:T(8,128)(2,1)S(1)}, u32[]{:S(2)}, u32[]{:S(2)}) async-start(bf16[32,16,512]{2,1,0:T(8,128)(2,1)} %bitcast.7), calls=%async_computation.2 | async-start | bytes 1048576 | tf_op jit(solution)/shard_map/all_to_all | solution.py:259
  46.4 0.4 shard_map.73
  46.8 0.2 collective-permute-start.3
  47.0 1.4 %collective-permute-done.3.came_ref = bf16[16,16,512]{2,1,0:T(8,128)(2,1)S(1)} collective-permute-done((bf16[16,16,512]{2,1,0:T(8,128)(2,1)S(1)}, bf16[16,16,512]{2,1,0:T(8,128)(2,1)S(1)}, u32[]{:S(2)}, u32[]{:S(2)}) %collective-permute-start.3) | collective-permute-done | bytes 262176 | tf_op jit(solution)/shard_map/ppermute | solution.py:202
  48.4 0.1 shard_map.74
  48.5 1.7 %collective-permute-start.4 = (bf16[8,16,512]{2,1,0:T(8,128)(2,1)S(1)}, bf16[8,16,512]{2,1,0:T(8,128)(2,1)S(1)}, u32[]{:S(2)}, u32[]{:S(2)}) collective-permute-start(bf16[8,16,512]{2,1,0:T(8,128)(2,1)S(1)} %get-tuple-element.37), channel_id=1, source_target_pairs={{0,16},{8,24},{16,0},{24,8},{1,17},{9,25},{17,1},{25,9},{2,18},{10... | collective-permute-start | bytes 393224 | tf_op jit(solution)/shard_map/ppermute | solution.py:202
  50.2 5.8 %collective-permute-done.4.came_ref = bf16[8,16,512]{2,1,0:T(8,128)(2,1)S(1)} collective-permute-done((bf16[8,16,512]{2,1,0:T(8,128)(2,1)S(1)}, bf16[8,16,512]{2,1,0:T(8,128)(2,1)S(1)}, u32[]{:S(2)}, u32[]{:S(2)}) %collective-permute-start.4) | collective-permute-done | bytes 131104 | tf_op jit(solution)/shard_map/ppermute | solution.py:202
  56.0 2.1 %collective-permute-start.5 = (bf16[4,16,512]{2,1,0:T(8,128)(2,1)S(1)}, bf16[4,16,512]{2,1,0:T(8,128)(2,1)S(1)}, u32[]{:S(2)}, u32[]{:S(2)}) collective-permute-start(bf16[4,16,512]{2,1,0:T(8,128)(2,1)S(1)} %get-tuple-element.39), channel_id=1, source_target_pairs={{0,1},{1,0},{2,3},{3,2},{4,5},{5,4},{6,7},{7,6},{8,9},{9,8},{10,11... | collective-permute-start | bytes 196616 | tf_op jit(solution)/shard_map/ppermute | solution.py:202
  58.2 2.5 %collective-permute-done.5.came_ref = bf16[4,16,512]{2,1,0:T(8,128)(2,1)S(1)} collective-permute-done((bf16[4,16,512]{2,1,0:T(8,128)(2,1)S(1)}, bf16[4,16,512]{2,1,0:T(8,128)(2,1)S(1)}, u32[]{:S(2)}, u32[]{:S(2)}) %collective-permute-start.5) | collective-permute-done | bytes 65568 | tf_op jit(solution)/shard_map/ppermute | solution.py:202
  60.7 2.3 %collective-permute-start.6 = (f32[2,16,512]{2,1,0:T(8,128)S(1)}, f32[2,16,512]{2,1,0:T(8,128)S(1)}, u32[]{:S(2)}, u32[]{:S(2)}) collective-permute-start(f32[2,16,512]{2,1,0:T(8,128)S(1)} %get-tuple-element.41), channel_id=1, source_target_pairs={{0,2},{1,3},{2,0},{3,1},{4,6},{5,7},{6,4},{7,5},{8,10},{9,11},{10,... | collective-permute-start | bytes 196616 | tf_op jit(solution)/shard_map/ppermute | solution.py:202
  63.0 2.2 %collective-permute-done.6.came_ref = f32[2,16,512]{2,1,0:T(8,128)S(1)} collective-permute-done((f32[2,16,512]{2,1,0:T(8,128)S(1)}, f32[2,16,512]{2,1,0:T(8,128)S(1)}, u32[]{:S(2)}, u32[]{:S(2)}) %collective-permute-start.6) | collective-permute-done | bytes 65568 | tf_op jit(solution)/shard_map/ppermute | solution.py:202
  65.3 2.7 %collective-permute-start.7 = (f32[1,16,512]{2,1,0:T(8,128)S(1)}, f32[1,16,512]{2,1,0:T(8,128)S(1)}, u32[]{:S(2)}, u32[]{:S(2)}) collective-permute-start(f32[1,16,512]{2,1,0:T(8,128)S(1)} %get-tuple-element.43), channel_id=1, source_target_pairs={{0,4},{1,5},{2,6},{3,7},{4,0},{5,1},{6,2},{7,3},{8,12},{9,13},{10,... | collective-permute-start | bytes 98312 | tf_op jit(solution)/shard_map/ppermute | solution.py:202
  68.0 2.1 %collective-permute-done.7 = f32[1,16,512]{2,1,0:T(8,128)S(1)} collective-permute-done((f32[1,16,512]{2,1,0:T(8,128)S(1)}, f32[1,16,512]{2,1,0:T(8,128)S(1)}, u32[]{:S(2)}, u32[]{:S(2)}) %collective-permute-start.7) | collective-permute-done | bytes 32800 | tf_op jit(solution)/shard_map/ppermute | solution.py:202
  70.2 0.6 add_bitcast_fusion
  70.8 0.0 all-to-all-done.2
  70.8 4.6 %shard_map.72 = bf16[4096,512]{1,0:T(8,128)(2,1)} custom-call(s32[1,512]{1,0:T(1,128)S(1)} %get-tuple-element.28.line_ref, bf16[512,512]{1,0:T(8,128)(2,1)S(1)} %bitcast.12, bf16[512,512]{1,0:T(8,128)(2,1)S(1)} %copy-done.2), custom_call_target="tpu_custom_call" | custom-call | flops 2147483648 | bytes 4194304 | tf_op jit(solution)/shard_map/pallas_call | solution.py:282
  (7 shorter events, 0.1 us)
Async XLA Ops:
  0.6 15.9 %collective-permute-start = (bf16[256,512]{1,0:T(8,128)(2,1)}, bf16[256,512]{1,0:T(8,128)(2,1)S(1)}, u32[]{:S(2)}, u32[]{:S(2)}) collective-permute-start(bf16[256,512]{1,0:T(8,128)(2,1)} %refs_0_.1), channel_id=1, source_target_pairs={{0,16},{8,24},{16,0},{24,8},{1,17},{9,25},{17,1},{25,9},{2,18},{10... | collective-permute-start | bytes 786440 | tf_op jit(solution)/shard_map/ppermute | solution.py:202
  3.6 12.9 %collective-permute-start.1 = (bf16[256,512]{1,0:T(8,128)(2,1)}, bf16[256,512]{1,0:T(8,128)(2,1)S(1)}, u32[]{:S(2)}, u32[]{:S(2)}) collective-permute-start(bf16[256,512]{1,0:T(8,128)(2,1)} %refs_0_.1), channel_id=1, source_target_pairs={{0,8},{8,0},{16,24},{24,16},{1,9},{9,1},{17,25},{25,17},{2,10},{10... | collective-permute-start | bytes 786440 | tf_op jit(solution)/shard_map/ppermute | solution.py:202
  16.6 9.9 %copy-start = (bf16[256,512]{1,0:T(8,128)(2,1)S(1)}, bf16[256,512]{1,0:T(8,128)(2,1)}, u32[]{:S(2)}) copy-start(bf16[256,512]{1,0:T(8,128)(2,1)} %refs_0_.1) | copy-start | bytes 786436
  16.6 9.9 %copy-start.1 = (s32[32,1,16]{2,1,0:T(1,128)S(1)}, s32[32,1,16]{2,1,0:T(1,128)}, u32[]{:S(2)}) copy-start(s32[32,1,16]{2,1,0:T(1,128)} %all_to_all.22) | copy-start | bytes 6148
  16.6 24.7 %copy-start.2 = (bf16[512,512]{1,0:T(8,128)(2,1)S(1)}, bf16[512,512]{1,0:T(8,128)(2,1)}, u32[]{:S(2)}) copy-start(bf16[512,512]{1,0:T(8,128)(2,1)} %weight_ref.3) | copy-start | bytes 1572868
  22.3 19.0 %all-to-all-start.1 = ((bf16[32,16,512]{2,1,0:T(8,128)(2,1)}), bf16[32,16,512]{2,1,0:T(8,128)(2,1)S(1)}, u32[]{:S(2)}, u32[]{:S(2)}) async-start(bf16[32,16,512]{2,1,0:T(8,128)(2,1)} %bitcast.17), calls=%async_computation.1 | async-start | bytes 1048576 | tf_op jit(solution)/shard_map/all_to_all | solution.py:240
  24.9 1.6 %collective-permute-start.2 = (bf16[256,512]{1,0:T(8,128)(2,1)S(1)}, bf16[256,512]{1,0:T(8,128)(2,1)S(1)}, u32[]{:S(2)}, u32[]{:S(2)}) collective-permute-start(bf16[256,512]{1,0:T(8,128)(2,1)S(1)} %collective-permute-done.refs_1_), channel_id=1, source_target_pairs={{0,8},{8,0},{16,24},{24,16},{1,9},{9,1},{17,25},{25,17},{2,10},{10... | collective-permute-start | bytes 786440 | tf_op jit(solution)/shard_map/ppermute | solution.py:202
  43.8 27.0 %all-to-all-start.2 = ((bf16[32,16,512]{2,1,0:T(8,128)(2,1)}), bf16[32,16,512]{2,1,0:T(8,128)(2,1)S(1)}, u32[]{:S(2)}, u32[]{:S(2)}) async-start(bf16[32,16,512]{2,1,0:T(8,128)(2,1)} %bitcast.7), calls=%async_computation.2 | async-start | bytes 1048576 | tf_op jit(solution)/shard_map/all_to_all | solution.py:259
  46.8 1.6 %collective-permute-start.3 = (bf16[16,16,512]{2,1,0:T(8,128)(2,1)S(1)}, bf16[16,16,512]{2,1,0:T(8,128)(2,1)S(1)}, u32[]{:S(2)}, u32[]{:S(2)}) collective-permute-start(bf16[16,16,512]{2,1,0:T(8,128)(2,1)S(1)} %get-tuple-element.35), channel_id=1, source_target_pairs={{0,8},{8,0},{16,24},{24,16},{1,9},{9,1},{17,25},{25,17},{2,10},{10... | collective-permute-start | bytes 786440 | tf_op jit(solution)/shard_map/ppermute | solution.py:202
  48.5 7.5 %collective-permute-start.4 = (bf16[8,16,512]{2,1,0:T(8,128)(2,1)S(1)}, bf16[8,16,512]{2,1,0:T(8,128)(2,1)S(1)}, u32[]{:S(2)}, u32[]{:S(2)}) collective-permute-start(bf16[8,16,512]{2,1,0:T(8,128)(2,1)S(1)} %get-tuple-element.37), channel_id=1, source_target_pairs={{0,16},{8,24},{16,0},{24,8},{1,17},{9,25},{17,1},{25,9},{2,18},{10... | collective-permute-start | bytes 393224 | tf_op jit(solution)/shard_map/ppermute | solution.py:202
  56.0 4.6 %collective-permute-start.5 = (bf16[4,16,512]{2,1,0:T(8,128)(2,1)S(1)}, bf16[4,16,512]{2,1,0:T(8,128)(2,1)S(1)}, u32[]{:S(2)}, u32[]{:S(2)}) collective-permute-start(bf16[4,16,512]{2,1,0:T(8,128)(2,1)S(1)} %get-tuple-element.39), channel_id=1, source_target_pairs={{0,1},{1,0},{2,3},{3,2},{4,5},{5,4},{6,7},{7,6},{8,9},{9,8},{10,11... | collective-permute-start | bytes 196616 | tf_op jit(solution)/shard_map/ppermute | solution.py:202
  60.7 4.6 %collective-permute-start.6 = (f32[2,16,512]{2,1,0:T(8,128)S(1)}, f32[2,16,512]{2,1,0:T(8,128)S(1)}, u32[]{:S(2)}, u32[]{:S(2)}) collective-permute-start(f32[2,16,512]{2,1,0:T(8,128)S(1)} %get-tuple-element.41), channel_id=1, source_target_pairs={{0,2},{1,3},{2,0},{3,1},{4,6},{5,7},{6,4},{7,5},{8,10},{9,11},{10,... | collective-permute-start | bytes 196616 | tf_op jit(solution)/shard_map/ppermute | solution.py:202
  65.3 4.9 %collective-permute-start.7 = (f32[1,16,512]{2,1,0:T(8,128)S(1)}, f32[1,16,512]{2,1,0:T(8,128)S(1)}, u32[]{:S(2)}, u32[]{:S(2)}) collective-permute-start(f32[1,16,512]{2,1,0:T(8,128)S(1)} %get-tuple-element.43), channel_id=1, source_target_pairs={{0,4},{1,5},{2,6},{3,7},{4,0},{5,1},{6,2},{7,3},{8,12},{9,13},{10,... | collective-permute-start | bytes 98312 | tf_op jit(solution)/shard_map/ppermute | solution.py:202

commit v4 on v3

--- a/solution.py
+++ b/solution.py
@@ -75,29 +75,15 @@
     return value >> 8, value & 255
 
 
-def fetch_kernel(asked_ref, table_hbm, found_ref, table, sems):
-    groups = sems.shape[0]
-    size = table.shape[0] // groups
-    copies = [
-        pltpu.make_async_copy(table_hbm.at[pl.ds(g * size, size)], table.at[pl.ds(g * size, size)], sems.at[g])
-        for g in range(groups)
-    ]
-    for copy in copies:
-        copy.start()
+def fetch_kernel(asked_ref, table_ref, found_ref):
     block, low = parts_of(asked_column(asked_ref[...]).astype(i32))
     total = block.shape[0]
     low_hot = hot(low == iota((total, BLOCK), 1))
     block = jnp.broadcast_to(block.astype(f32), (total, BLOCK)).astype(bf16)
-    found = None
-    for g, copy in enumerate(copies):
-        picks = [
-            jnp.where(block == jnp.bfloat16(k), low_hot, jnp.bfloat16(0))
-            for k in range(g * size // BLOCK, (g + 1) * size // BLOCK)
-        ]
-        copy.wait()
-        part = dot(jnp.concatenate(picks, axis=1), table[pl.ds(g * size, size)])
-        found = part if found is None else found + part
-    found_ref[...] = found.astype(bf16)
+    picks = [
+        jnp.where(block == jnp.bfloat16(k), low_hot, jnp.bfloat16(0)) for k in range(table_ref.shape[0] // BLOCK)
+    ]
+    found_ref[...] = dot(jnp.concatenate(picks, axis=1), table_ref[...]).astype(bf16)
 
 
 def unit_of(users):
@@ -108,13 +94,18 @@
 
 
 def prepare_kernel(place_ref, asked_ref, *refs):
-    *users, unit_ref, column_ref, line_ref = refs
+    *users, unit_ref, column_ref, pick_ref = refs
     n = place_ref.shape[1]
     for k, users_ref in enumerate(users):
         unit_ref[pl.ds(k * n, n)] = unit_of(users_ref[...])
     eye = iota((n, n), 0) == iota((n, n), 1)
     column_ref[...] = jnp.sum(jnp.where(eye, place_ref[...], 0), axis=1, keepdims=True)
-    line_ref[...] = asked_line(asked_ref[...]).astype(i32)
+    block, low = parts_of(asked_line(asked_ref[...]).astype(i32))
+    total = block.shape[1]
+    low_hot = hot(low == iota((BLOCK, total), 0))
+    block = jnp.broadcast_to(block.astype(f32), (BLOCK, total)).astype(bf16)
+    for k in range(pick_ref.shape[0] // BLOCK):
+        pick_ref[pl.ds(k * BLOCK, BLOCK)] = jnp.where(block == jnp.bfloat16(k), low_hot, jnp.bfloat16(0))
 
 
 def main_kernel(fetched_ref, weight_ref, unit_ref, place_ref, column_ref, outgoing_ref, embed_ref, dhidden_ref):
@@ -162,21 +153,23 @@
     halve(blocks, bit, keep_ref, send_ref)
 
 
-def table_kernel(line_ref, incoming_ref, weight_ref, table_grad_ref, drow, low_hot, block, pick):
-    step = pl.program_id(0)
-    chunk, total = pick.shape
-
-    @pl.when(step == 0)
-    def _():
-        drow[...] = dot(incoming_ref[...], weight_ref[...], 1, 1).astype(bf16)
-        high, low = parts_of(line_ref[...])
-        low_hot[...] = hot(low == iota((BLOCK, total), 0))
-        block[...] = jnp.broadcast_to(high.astype(f32), (BLOCK, total)).astype(bf16)
-
-    for k in range(chunk // BLOCK):
-        mine = (step * (chunk // BLOCK) + k).astype(f32).astype(bf16)
-        pick[pl.ds(k * BLOCK, BLOCK)] = jnp.where(block[...] == mine, low_hot[...], jnp.bfloat16(0))
-    table_grad_ref[...] = dot(pick[...], drow[...]).astype(bf16)
+def add_kernel(kept_ref, came_ref, total_ref):
+    total_ref[...] = kept_ref[...] + came_ref[...].astype(f32)
+
+
+def table_kernel(pick_ref, incoming_ref, weight_ref, table_grad_hbm, ready, sems):
+    drow = dot(incoming_ref[...], weight_ref[...], 1, 1).astype(bf16)
+    groups = sems.shape[0]
+    size = ready.shape[0] // groups
+    copies = []
+    for g in range(groups):
+        here = pl.ds(g * size, size)
+        ready[here] = dot(pick_ref[here], drow).astype(bf16)
+        copy = pltpu.make_async_copy(ready.at[here], table_grad_hbm.at[here], sems.at[g])
+        copy.start()
+        copies.append(copy)
+    for copy in copies:
+        copy.wait()
 
 
 def params(mib=16):
@@ -214,33 +207,26 @@
     devices = n_batch * n_item
     slots = 2 * n // devices
     total = devices * slots
-    chunk = min(1024, rows)
-    groups = rows // chunk
+    groups = rows // min(512, rows)
 
     exchange = functools.partial(lax.all_to_all, axis_name=axes, split_axis=0, concat_axis=0, tiled=True)
 
-    users = [user_vectors]
-    for bit in reversed(bits_of("batch")):
-        users += [swap(value, bit) for value in users]
+    far, *near = reversed(bits_of("batch"))
+    users = [user_vectors, swap(user_vectors, far)]
     request, place = call(
         request_kernel,
         [((devices, slots), i32), ((1, n), i32)],
         jnp.stack([item_owner.reshape(n), item_row]),
-    )
-    early = n_batch // 2 + 1
-    asked, *users[1:early] = lax.optimization_barrier((exchange(request), *users[1:early]))
-    found = pl.pallas_call(
-        fetch_kernel,
-        in_specs=[pl.BlockSpec(memory_space=pltpu.VMEM), pl.BlockSpec(memory_space=pltpu.HBM)],
-        out_shape=jax.ShapeDtypeStruct((total, width), bf16),
-        scratch_shapes=[pltpu.VMEM((rows, width), bf16), pltpu.SemaphoreType.DMA((groups,))],
-        compiler_params=params(61),
-        cost_estimate=cost(2 * total * rows * width, 2 * rows * width),
-    )(asked, item_table)
+        flops=1 << 34,
+    )
+    asked, *users = lax.optimization_barrier((exchange(request), *users))
+    (found,) = call(fetch_kernel, [((total, width), bf16)], asked, item_table, flops=2 * total * rows * width)
     fetched = exchange(found.reshape(devices, slots, width)).reshape(total, width)
-    unit, column, line = call(
+    for bit in near:
+        users += [swap(value, bit) for value in users]
+    unit, column, pick = call(
         prepare_kernel,
-        [((n_batch * n, width), bf16), ((n, 1), i32), ((1, total), i32)],
+        [((n_batch * n, width), bf16), ((n, 1), i32), ((rows, total), bf16)],
         place,
         asked,
         *users,
@@ -259,17 +245,15 @@
     incoming = exchange(outgoing.reshape(devices, slots, width)).reshape(total, width)
 
     part = width // devices
-    bits = bits_of("batch") + bits_of("item")
+    bits = bits_of("batch")
     order = []
-    for spot in range(devices):
-        at = {"batch": 0, "item": 0}
-        for k, (axis, level) in enumerate(bits):
-            at[axis] |= (spot >> (len(bits) - 1 - k) & 1) << level
-        order.append(at["batch"] * n_item + at["item"])
+    for spot in range(n_batch):
+        at = sum((spot >> (len(bits) - 1 - k) & 1) << level for k, (_, level) in enumerate(bits))
+        order += [at * n_item + item for item in range(n_item)]
     kept, came = None, None
     for k, bit in enumerate(bits):
         half = devices >> (k + 1)
-        outs = [((half, part, width), f32), ((half, part, width), bf16 if half >= 4 else f32)]
+        outs = [((half, part, width), f32), ((half, part, width), bf16)]
         scratch = [pltpu.VMEM((2 * half, part, width), f32)]
         if k == 0:
             kernel = functools.partial(share_kernel, order, bit)
@@ -277,27 +261,18 @@
         else:
             kept, sent = call(functools.partial(halve_kernel, bit), outs, kept, came, scratch=scratch)
         came = swap(sent, bit)
-    weight_grad = (kept + came.astype(f32)).reshape(part, width)
+    (share,) = call(add_kernel, [((n_item, part, width), f32)], kept, came)
+    shares = lax.all_to_all(share, "item", split_axis=0, concat_axis=0, tiled=True)
+    weight_grad = jnp.sum(shares, axis=0)
 
     table_grad = pl.pallas_call(
         table_kernel,
-        grid=(groups,),
-        in_specs=[
-            pl.BlockSpec((1, total), lambda k: (0, 0)),
-            pl.BlockSpec((total, width), lambda k: (0, 0)),
-            pl.BlockSpec((width, width), lambda k: (0, 0)),
-        ],
-        out_specs=pl.BlockSpec((chunk, width), lambda k: (k, 0)),
+        out_specs=pl.BlockSpec(memory_space=pl.ANY),
         out_shape=jax.ShapeDtypeStruct((rows, width), bf16),
-        scratch_shapes=[
-            pltpu.VMEM((total, width), bf16),
-            pltpu.VMEM((BLOCK, total), bf16),
-            pltpu.VMEM((BLOCK, total), bf16),
-            pltpu.VMEM((chunk, total), bf16),
-        ],
-        compiler_params=params(32),
+        scratch_shapes=[pltpu.VMEM((rows, width), bf16), pltpu.SemaphoreType.DMA((groups,))],
+        compiler_params=params(),
         cost_estimate=cost(2 * total * rows * width, 2 * rows * width),
-    )(line, incoming, tower_weight)
+    )(pick, incoming, tower_weight)
     return (table_grad, weight_grad)
 
 

time: 75.9 us -> 85.8 us (1.13)
  blocking collectives: 11.9 us -> 23 us
  starting transfers between devices: 17.5 us -> 9.77 us
  waiting for transfers between devices: 29.7 us -> 35 us
  local copies, waits for them, and re-layouts: 0.01 us -> 4.21 us
  Pallas kernels: 14.2 us -> 11.3 us
    all_to_all x1, waiting for transfers between devices: 0.01 us -> 15.7 us  [local(): exchange(outgoing.reshape(devices, slots, width)).reshape(total, width)]
    all_to_all x1 -> x2, blocking collectives: 11.9 us -> 23 us  [the longest x1 11.8 us: local(): asked, *users = lax.optimization_barrier((exchange(request), *users))]
    ppermute x8 -> x5, starting transfers between devices: 12.2 us -> 4.26 us  [swap(): lax.ppermute(value, axis, [(k, k ^ 1 << level) for k in range(lax.axis_si...]
    ppermute x8 -> x5, waiting for transfers between devices: 15.5 us -> 7.92 us  [swap(): lax.ppermute(value, axis, [(k, k ^ 1 << level) for k in range(lax.axis_si...]
    pallas_call x2 -> x1, Pallas kernels: 10.3 us -> 3.58 us  [local(): pl.pallas_call(table_kernel, out_specs=pl.BlockSpec(memory_space=pl.ANY),...]
    unnamed x6 -> x10, local copies, waits for them, and re-layouts: 0.01 us -> 4.21 us
    pallas_call x8 -> x7, Pallas kernels: 3.96 us -> 7.73 us  [call(): pl.pallas_call(kernel, out_shape=[jax.ShapeDtypeStruct(shape, dtype) for...]
    all_to_all x1, waiting for transfers between devices: 14.2 us -> 11.3 us  [local(): exchange(found.reshape(devices, slots, width)).reshape(total, width)]
  transfers between devices with their start and end apart: 10 -> 7, of which waited for: 7 -> 6; matrix products, arithmetic and copies ran while one was open for 2% -> 2% of each run, Pallas kernels for 2% -> 2%
where the time goes in v4:
time: 85.8 us; the launch traced here: 85.4 us
  waiting for transfers between devices  35 us (41%)
  blocking collectives  23 us (27%)
  Pallas kernels  11.3 us (13%)
  starting transfers between devices  9.77 us (11%)
  local copies, waits for them, and re-layouts  4.21 us (5%)
  other arithmetic  1.34 us (2%)
    all_to_all x1, waiting for transfers between devices, local(): exchange(outgoing.reshape(devices, slots, width)).reshape(total, width)  15.7 us
    all_to_all x1, blocking collectives, local(): asked, *users = lax.optimization_barrier((exchange(request), *users))  11.8 us
    all_to_all x1, waiting for transfers between devices, local(): exchange(found.reshape(devices, slots, width)).reshape(total, width)  11.3 us
    all_to_all x1, blocking collectives, local(): lax.all_to_all(share, 'item', split_axis=0, concat_axis=0, tiled=True)  11.2 us
    ppermute x5, waiting for transfers between devices, swap(): lax.ppermute(value, axis, [(k, k ^ 1 << level) for k in range(lax.axis_si...  7.92 us
    pallas_call x7, Pallas kernels, call(): pl.pallas_call(kernel, out_shape=[jax.ShapeDtypeStruct(shape, dtype) for...  7.73 us
    ppermute x5, starting transfers between devices, swap(): lax.ppermute(value, axis, [(k, k ^ 1 << level) for k in range(lax.axis_si...  4.26 us
    unnamed x10, local copies, waits for them, and re-layouts  4.21 us
  transfers between devices with their start and end apart: 7, of which 6 were waited for; matrix products, arithmetic and copies ran while one was open for 2% of the time, Pallas kernels for 2%

profile of v4, /device:TPU:0, one launch (start us, length us, event | category | flops | bytes accessed | tf_op | source)
XLA Modules:
  0.0 85.4 jit_solution(11403728873621568206)
XLA Ops:
  0.6 3.0 %collective-permute-start = (bf16[256,512]{1,0:T(8,128)(2,1)}, bf16[256,512]{1,0:T(8,128)(2,1)S(1)}, u32[]{:S(2)}, u32[]{:S(2)}) collective-permute-start(bf16[256,512]{1,0:T(8,128)(2,1)} %refs_0_), channel_id=1, source_target_pairs={{0,16},{8,24},{16,0},{24,8},{1,17},{9,25},{17,1},{25,9},{2,18},{10... | collective-permute-start | bytes 786440 | tf_op jit(solution)/shard_map/ppermute | solution.py:195
  3.6 0.7 pad_add_fusion.named_ref
  4.3 0.3 shard_map.68
  4.6 11.8 %all_to_all.27 = s32[32,1,16]{2,1,0:T(1,128)S(1)} all-to-all(s32[32,1,16]{2,1,0:T(1,128)S(1)} %bitcast.14), channel_id=1, replica_groups=mesh['batch'=4,'item'=8] {'batch','item'}, dimensions={0} | all-to-all | bytes 4096 | tf_op jit(solution)/shard_map/all_to_all | solution.py:222
  16.5 0.0 collective-permute-done.refs_1_
  16.5 0.0 copy-done.4
  16.5 0.0 copy-start.2
  16.5 3.3 %shard_map.70 = bf16[512,512]{1,0:T(8,128)(2,1)} custom-call(s32[32,16]{1,0:T(8,128)S(1)} %bitcast.12, bf16[4096,512]{1,0:T(8,128)(2,1)S(1)} %copy-done.4), custom_call_target="tpu_custom_call" | custom-call | flops 2147483648 | bytes 1048576 | tf_op jit(solution)/shard_map/pallas_call | solution.py:184
  19.8 2.6 %all-to-all-start.1 = ((bf16[32,16,512]{2,1,0:T(8,128)(2,1)}), bf16[32,16,512]{2,1,0:T(8,128)(2,1)S(1)}, u32[]{:S(2)}, u32[]{:S(2)}) async-start(bf16[32,16,512]{2,1,0:T(8,128)(2,1)} %bitcast.5), calls=%async_computation.1 | async-start | bytes 1048576 | tf_op jit(solution)/shard_map/all_to_all | solution.py:224
  22.5 0.0 copy-done.3
  22.5 0.2 collective-permute-start.1
  22.6 0.4 collective-permute-start.2
  23.0 1.0 %collective-permute-done.1.refs_2_ = bf16[256,512]{1,0:T(8,128)(2,1)S(1)} collective-permute-done((bf16[256,512]{1,0:T(8,128)(2,1)S(1)}, bf16[256,512]{1,0:T(8,128)(2,1)S(1)}, u32[]{:S(2)}, u32[]{:S(2)}) %collective-permute-start.1) | collective-permute-done | bytes 262176 | tf_op jit(solution)/shard_map/ppermute | solution.py:195
  24.1 0.4 collective-permute-done.2.refs_3_
  24.4 1.0 %shard_map.69 = (bf16[1024,512]{1,0:T(8,128)(2,1)S(1)}, s32[256,1]{1,0:T(8,128)S(1)}, bf16[4096,512]{1,0:T(8,128)(2,1)S(1)}) custom-call(s32[1,256]{1,0:T(1,128)S(1)} %get-tuple-element.17.place_ref, s32[32,16]{1,0:T(8,128)S(1)} %bitcast.13, bf16[256,512]{1,0:T(8,128)(2,1)S(1)} %copy-done.3, bf16[256,512]{1,0:T(8,128)(2,1)S(1)} %collective-permute-done.refs_1_, ...), custom_call_target="tpu_custom_call" | custom-call | flops 268435456 | bytes 1048576 | tf_op jit(solution)/shard_map/pallas_call | solution.py:184
  25.5 0.0 copy-start
  25.5 2.0 %copy-done = bf16[4096,512]{1,0:T(8,128)(2,1)} copy-done((bf16[4096,512]{1,0:T(8,128)(2,1)}, bf16[4096,512]{1,0:T(8,128)(2,1)S(1)}, u32[]{:S(2)}) %copy-start) | copy-done | bytes 4194328
  27.5 11.3 %all-to-all-done.1 = bf16[32,16,512]{2,1,0:T(8,128)(2,1)S(1)} async-done(((bf16[32,16,512]{2,1,0:T(8,128)(2,1)}), bf16[32,16,512]{2,1,0:T(8,128)(2,1)S(1)}, u32[]{:S(2)}, u32[]{:S(2)}) %all-to-all-start.1) | async-done | bytes 524320 | tf_op jit(solution)/shard_map/all_to_all | solution.py:224
  38.8 0.0 copy-done.2
  38.8 2.5 %shard_map.71 = (bf16[512,512]{1,0:T(8,128)(2,1)}, bf16[256,512]{1,0:T(8,128)(2,1)S(1)}, bf16[256,512]{1,0:T(8,128)(2,1)S(1)}) custom-call(bf16[512,512]{1,0:T(8,128)(2,1)S(1)} %bitcast.11, bf16[512,512]{1,0:T(8,128)(2,1)S(1)} %copy-done.2, bf16[1024,512]{1,0:T(8,128)(2,1)S(1)} %get-tuple-element.23.unit_ref, s32[1,256]{1,0:T(1,128)S(1)} %get-tuple-element.17.place_ref, ...), custom_call_target="tpu_custom_call" | custom-call | flops 1073741824 | bytes 1048576 | tf_op jit(solution)/shard_map/pallas_call | solution.py:184
  41.4 0.4 shard_map.73
  41.8 0.1 collective-permute-start.3
  41.9 1.5 %collective-permute-done.3.came_ref = bf16[16,16,512]{2,1,0:T(8,128)(2,1)S(1)} collective-permute-done((bf16[16,16,512]{2,1,0:T(8,128)(2,1)S(1)}, bf16[16,16,512]{2,1,0:T(8,128)(2,1)S(1)}, u32[]{:S(2)}, u32[]{:S(2)}) %collective-permute-start.3) | collective-permute-done | bytes 262176 | tf_op jit(solution)/shard_map/ppermute | solution.py:195
  43.4 0.1 shard_map.74
  43.5 0.6 collective-permute-start.4
  44.1 5.0 %collective-permute-done.4.came_ref = bf16[8,16,512]{2,1,0:T(8,128)(2,1)S(1)} collective-permute-done((bf16[8,16,512]{2,1,0:T(8,128)(2,1)S(1)}, bf16[8,16,512]{2,1,0:T(8,128)(2,1)S(1)}, u32[]{:S(2)}, u32[]{:S(2)}) %collective-permute-start.4) | collective-permute-done | bytes 131104 | tf_op jit(solution)/shard_map/ppermute | solution.py:195
  49.1 11.2 %all_to_all.28 = f32[8,16,512]{2,1,0:T(8,128)S(1)} all-to-all(f32[8,16,512]{2,1,0:T(8,128)S(1)} %shard_map.75), channel_id=1, replica_groups=mesh['batch'=4,'item'=8] {'item'}, dimensions={0} | all-to-all | bytes 524288 | tf_op jit(solution)/shard_map/all_to_all | solution.py:265
  60.3 2.9 %all-to-all-start.2 = ((bf16[32,16,512]{2,1,0:T(8,128)(2,1)}), bf16[32,16,512]{2,1,0:T(8,128)(2,1)S(1)}, u32[]{:S(2)}, u32[]{:S(2)}) async-start(bf16[32,16,512]{2,1,0:T(8,128)(2,1)} %bitcast.7), calls=%async_computation.2 | async-start | bytes 1048576 | tf_op jit(solution)/shard_map/all_to_all | solution.py:245
  63.2 0.6 reduce_sum.9
  63.9 15.7 %all-to-all-done.2 = bf16[32,16,512]{2,1,0:T(8,128)(2,1)S(1)} async-done(((bf16[32,16,512]{2,1,0:T(8,128)(2,1)}), bf16[32,16,512]{2,1,0:T(8,128)(2,1)S(1)}, u32[]{:S(2)}, u32[]{:S(2)}) %all-to-all-start.2) | async-done | bytes 524320 | tf_op jit(solution)/shard_map/all_to_all | solution.py:245
  79.6 2.2 %copy-done.1 = bf16[4096,512]{1,0:T(8,128)(2,1)S(1)} copy-done((bf16[4096,512]{1,0:T(8,128)(2,1)S(1)}, bf16[4096,512]{1,0:T(8,128)(2,1)}, u32[]{:S(2)}) %copy-start.1) | copy-done | bytes 4194328
  81.8 3.6 %shard_map.72 = bf16[4096,512]{1,0:T(8,128)(2,1)} custom-call(bf16[4096,512]{1,0:T(8,128)(2,1)S(1)} %copy-done.1, bf16[512,512]{1,0:T(8,128)(2,1)S(1)} %bitcast.10, bf16[512,512]{1,0:T(8,128)(2,1)S(1)} %copy-done.2), custom_call_target="tpu_custom_call" | custom-call | flops 2147483648 | bytes 4194304 | tf_op jit(solution)/shard_map/pallas_call | solution.py:268
  (4 shorter events, 0.0 us)
Async XLA Ops:
  0.6 15.9 %collective-permute-start = (bf16[256,512]{1,0:T(8,128)(2,1)}, bf16[256,512]{1,0:T(8,128)(2,1)S(1)}, u32[]{:S(2)}, u32[]{:S(2)}) collective-permute-start(bf16[256,512]{1,0:T(8,128)(2,1)} %refs_0_), channel_id=1, source_target_pairs={{0,16},{8,24},{16,0},{24,8},{1,17},{9,25},{17,1},{25,9},{2,18},{10... | collective-permute-start | bytes 786440 | tf_op jit(solution)/shard_map/ppermute | solution.py:195
  4.3 12.2 %copy-start.4 = (bf16[4096,512]{1,0:T(8,128)(2,1)S(1)}, bf16[4096,512]{1,0:T(8,128)(2,1)}, u32[]{:S(2)}) copy-start(bf16[4096,512]{1,0:T(8,128)(2,1)} %table_ref.1) | copy-start | bytes 12582916
  16.5 6.0 %copy-start.3 = (bf16[256,512]{1,0:T(8,128)(2,1)S(1)}, bf16[256,512]{1,0:T(8,128)(2,1)}, u32[]{:S(2)}) copy-start(bf16[256,512]{1,0:T(8,128)(2,1)} %refs_0_) | copy-start | bytes 786436
  16.5 22.3 %copy-start.2 = (bf16[512,512]{1,0:T(8,128)(2,1)S(1)}, bf16[512,512]{1,0:T(8,128)(2,1)}, u32[]{:S(2)}) copy-start(bf16[512,512]{1,0:T(8,128)(2,1)} %weight_ref.3) | copy-start | bytes 1572868
  19.8 19.0 %all-to-all-start.1 = ((bf16[32,16,512]{2,1,0:T(8,128)(2,1)}), bf16[32,16,512]{2,1,0:T(8,128)(2,1)S(1)}, u32[]{:S(2)}, u32[]{:S(2)}) async-start(bf16[32,16,512]{2,1,0:T(8,128)(2,1)} %bitcast.5), calls=%async_computation.1 | async-start | bytes 1048576 | tf_op jit(solution)/shard_map/all_to_all | solution.py:224
  22.5 1.6 %collective-permute-start.1 = (bf16[256,512]{1,0:T(8,128)(2,1)S(1)}, bf16[256,512]{1,0:T(8,128)(2,1)S(1)}, u32[]{:S(2)}, u32[]{:S(2)}) collective-permute-start(bf16[256,512]{1,0:T(8,128)(2,1)S(1)} %copy-done.3), channel_id=1, source_target_pairs={{0,8},{8,0},{16,24},{24,16},{1,9},{9,1},{17,25},{25,17},{2,10},{10... | collective-permute-start | bytes 786440 | tf_op jit(solution)/shard_map/ppermute | solution.py:195
  22.6 1.8 %collective-permute-start.2 = (bf16[256,512]{1,0:T(8,128)(2,1)S(1)}, bf16[256,512]{1,0:T(8,128)(2,1)S(1)}, u32[]{:S(2)}, u32[]{:S(2)}) collective-permute-start(bf16[256,512]{1,0:T(8,128)(2,1)S(1)} %collective-permute-done.refs_1_), channel_id=1, source_target_pairs={{0,8},{8,0},{16,24},{24,16},{1,9},{9,1},{17,25},{25,17},{2,10},{10... | collective-permute-start | bytes 786440 | tf_op jit(solution)/shard_map/ppermute | solution.py:195
  25.5 2.0 %copy-start = (bf16[4096,512]{1,0:T(8,128)(2,1)}, bf16[4096,512]{1,0:T(8,128)(2,1)S(1)}, u32[]{:S(2)}) copy-start(bf16[4096,512]{1,0:T(8,128)(2,1)S(1)} %get-tuple-element.22.pick_ref) | copy-start | bytes 12582916
  41.8 1.6 %collective-permute-start.3 = (bf16[16,16,512]{2,1,0:T(8,128)(2,1)S(1)}, bf16[16,16,512]{2,1,0:T(8,128)(2,1)S(1)}, u32[]{:S(2)}, u32[]{:S(2)}) collective-permute-start(bf16[16,16,512]{2,1,0:T(8,128)(2,1)S(1)} %get-tuple-element.29), channel_id=1, source_target_pairs={{0,8},{8,0},{16,24},{24,16},{1,9},{9,1},{17,25},{25,17},{2,10},{10... | collective-permute-start | bytes 786440 | tf_op jit(solution)/shard_map/ppermute | solution.py:195
  43.5 5.6 %collective-permute-start.4 = (bf16[8,16,512]{2,1,0:T(8,128)(2,1)S(1)}, bf16[8,16,512]{2,1,0:T(8,128)(2,1)S(1)}, u32[]{:S(2)}, u32[]{:S(2)}) collective-permute-start(bf16[8,16,512]{2,1,0:T(8,128)(2,1)S(1)} %get-tuple-element.31), channel_id=1, source_target_pairs={{0,16},{8,24},{16,0},{24,8},{1,17},{9,25},{17,1},{25,9},{2,18},{10... | collective-permute-start | bytes 393224 | tf_op jit(solution)/shard_map/ppermute | solution.py:195
  60.3 19.3 %all-to-all-start.2 = ((bf16[32,16,512]{2,1,0:T(8,128)(2,1)}), bf16[32,16,512]{2,1,0:T(8,128)(2,1)S(1)}, u32[]{:S(2)}, u32[]{:S(2)}) async-start(bf16[32,16,512]{2,1,0:T(8,128)(2,1)} %bitcast.7), calls=%async_computation.2 | async-start | bytes 1048576 | tf_op jit(solution)/shard_map/all_to_all | solution.py:245
  79.6 2.2 %copy-start.1 = (bf16[4096,512]{1,0:T(8,128)(2,1)S(1)}, bf16[4096,512]{1,0:T(8,128)(2,1)}, u32[]{:S(2)}) copy-start(bf16[4096,512]{1,0:T(8,128)(2,1)} %copy-done) | copy-start | bytes 12582916

commit v5 on v4

--- a/solution.py
+++ b/solution.py
@@ -94,18 +94,15 @@
 
 
 def prepare_kernel(place_ref, asked_ref, *refs):
-    *users, unit_ref, column_ref, pick_ref = refs
+    *users, unit_ref, column_ref, low_hot_ref, block_ref = refs
     n = place_ref.shape[1]
     for k, users_ref in enumerate(users):
         unit_ref[pl.ds(k * n, n)] = unit_of(users_ref[...])
     eye = iota((n, n), 0) == iota((n, n), 1)
     column_ref[...] = jnp.sum(jnp.where(eye, place_ref[...], 0), axis=1, keepdims=True)
     block, low = parts_of(asked_line(asked_ref[...]).astype(i32))
-    total = block.shape[1]
-    low_hot = hot(low == iota((BLOCK, total), 0))
-    block = jnp.broadcast_to(block.astype(f32), (BLOCK, total)).astype(bf16)
-    for k in range(pick_ref.shape[0] // BLOCK):
-        pick_ref[pl.ds(k * BLOCK, BLOCK)] = jnp.where(block == jnp.bfloat16(k), low_hot, jnp.bfloat16(0))
+    low_hot_ref[...] = hot(low == iota(low_hot_ref.shape, 0))
+    block_ref[...] = jnp.broadcast_to(block.astype(f32), block_ref.shape).astype(bf16)
 
 
 def main_kernel(fetched_ref, weight_ref, unit_ref, place_ref, column_ref, outgoing_ref, embed_ref, dhidden_ref):
@@ -132,39 +129,49 @@
     dhidden_ref[...] = dhidden
 
 
-def halve(blocks, bit, keep_ref, send_ref):
-    half = keep_ref.shape[0]
-    axis, level = bit
-    mine = (lax.axis_index(axis) >> level) & 1
-    keep_ref[...] = blocks[pl.ds(mine * half, half)]
-    send_ref[...] = blocks[pl.ds((1 - mine) * half, half)].astype(send_ref.dtype)
-
-
-def share_kernel(order, bit, embed_ref, dhidden_ref, keep_ref, send_ref, blocks):
+def cut(blocks, bits, refs):
+    size = refs[0].shape[0]
+    mine = sum(((lax.axis_index(axis) >> level) & 1) << k for k, (axis, level) in enumerate(reversed(bits)))
+    for step, ref in enumerate(refs):
+        ref[...] = blocks[pl.ds((mine ^ step) * size, size)].astype(ref.dtype)
+
+
+def share_kernel(order, bits, embed_ref, dhidden_ref, *refs):
+    *refs, blocks = refs
     share = dot(embed_ref[...], dhidden_ref[...], 0, 0)
     size = blocks.shape[1]
     for spot, block in enumerate(order):
         blocks[spot] = share[block * size : (block + 1) * size]
-    halve(blocks, bit, keep_ref, send_ref)
-
-
-def halve_kernel(bit, kept_ref, came_ref, keep_ref, send_ref, blocks):
-    blocks[...] = kept_ref[...] + came_ref[...].astype(f32)
-    halve(blocks, bit, keep_ref, send_ref)
-
-
-def add_kernel(kept_ref, came_ref, total_ref):
-    total_ref[...] = kept_ref[...] + came_ref[...].astype(f32)
-
-
-def table_kernel(pick_ref, incoming_ref, weight_ref, table_grad_hbm, ready, sems):
+    cut(blocks, bits, refs)
+
+
+def sum_of(refs):
+    return sum(ref[...].astype(f32) for ref in refs)
+
+
+def stage_kernel(bits, count, *refs):
+    came, (*refs, blocks) = refs[:count], refs[count:]
+    blocks[...] = sum_of(came)
+    cut(blocks, bits, refs)
+
+
+def last_kernel(*refs):
+    *came, total_ref = refs
+    total_ref[...] = sum_of(came)[0]
+
+
+def table_kernel(low_hot_ref, block_ref, incoming_ref, weight_ref, table_grad_hbm, ready, sems):
     drow = dot(incoming_ref[...], weight_ref[...], 1, 1).astype(bf16)
     groups = sems.shape[0]
     size = ready.shape[0] // groups
     copies = []
     for g in range(groups):
         here = pl.ds(g * size, size)
-        ready[here] = dot(pick_ref[here], drow).astype(bf16)
+        picks = [
+            jnp.where(block_ref[...] == jnp.bfloat16(k), low_hot_ref[...], jnp.bfloat16(0))
+            for k in range(g * size // BLOCK, (g + 1) * size // BLOCK)
+        ]
+        ready[here] = dot(jnp.concatenate(picks, axis=0), drow).astype(bf16)
         copy = pltpu.make_async_copy(ready.at[here], table_grad_hbm.at[here], sems.at[g])
         copy.start()
         copies.append(copy)
@@ -190,13 +197,44 @@
     )(*args)
 
 
-def swap(value, bit):
-    axis, level = bit
-    return lax.ppermute(value, axis, [(k, k ^ (1 << level)) for k in range(lax.axis_size(axis))])
+def swap(value, *bits):
+    n_item, devices = lax.axis_size("item"), lax.axis_size("batch") * lax.axis_size("item")
+    mask = sum((n_item if axis == "batch" else 1) << level for axis, level in bits)
+    return lax.ppermute(value, ("batch", "item"), [(k, k ^ mask) for k in range(devices)])
 
 
 def bits_of(axis):
     return [(axis, level) for level in range(lax.axis_size(axis).bit_length() - 1)]
+
+
+def reduce_scatter(embed, dhidden):
+    width = embed.shape[1]
+    n_item, devices = lax.axis_size("item"), lax.axis_size("batch") * lax.axis_size("item")
+    part = width // devices
+    bits = bits_of("batch") + bits_of("item")
+    order = []
+    for spot in range(devices):
+        at = {"batch": 0, "item": 0}
+        for k, (axis, level) in enumerate(bits):
+            at[axis] |= (spot >> (len(bits) - 1 - k) & 1) << level
+        order.append(at["batch"] * n_item + at["item"])
+    odd = len(bits) % 2
+    stages = [bits[:1]] * odd + [bits[k : k + 2] for k in range(odd, len(bits), 2)]
+    left, values = devices, [embed, dhidden]
+    for k, stage in enumerate(stages):
+        whole, left = left, left >> len(stage)
+        sent = f32 if k == len(stages) - 1 else bf16
+        kernel = functools.partial(*((stage_kernel, stage, len(values)) if k else (share_kernel, order, stage)))
+        kept, *sends = call(
+            kernel,
+            [((left, part, width), f32)] + [((left, part, width), sent)] * ((1 << len(stage)) - 1),
+            *values,
+            scratch=[pltpu.VMEM((whole, part, width), f32)],
+        )
+        values = [kept]
+        for step, value in enumerate(sends, 1):
+            values.append(swap(value, *[bit for j, bit in enumerate(reversed(stage)) if step >> j & 1]))
+    return call(last_kernel, [((part, width), f32)], *values)[0]
 
 
 def local(user_vectors, item_table, tower_weight, item_owner, item_row):
@@ -224,9 +262,9 @@
     fetched = exchange(found.reshape(devices, slots, width)).reshape(total, width)
     for bit in near:
         users += [swap(value, bit) for value in users]
-    unit, column, pick = call(
+    unit, column, low_hot, block = call(
         prepare_kernel,
-        [((n_batch * n, width), bf16), ((n, 1), i32), ((rows, total), bf16)],
+        [((n_batch * n, width), bf16), ((n, 1), i32), ((BLOCK, total), bf16), ((BLOCK, total), bf16)],
         place,
         asked,
         *users,
@@ -244,26 +282,7 @@
     )
     incoming = exchange(outgoing.reshape(devices, slots, width)).reshape(total, width)
 
-    part = width // devices
-    bits = bits_of("batch")
-    order = []
-    for spot in range(n_batch):
-        at = sum((spot >> (len(bits) - 1 - k) & 1) << level for k, (_, level) in enumerate(bits))
-        order += [at * n_item + item for item in range(n_item)]
-    kept, came = None, None
-    for k, bit in enumerate(bits):
-        half = devices >> (k + 1)
-        outs = [((half, part, width), f32), ((half, part, width), bf16)]
-        scratch = [pltpu.VMEM((2 * half, part, width), f32)]
-        if k == 0:
-            kernel = functools.partial(share_kernel, order, bit)
-            kept, sent = call(kernel, outs, embed, dhidden, flops=1 << 27, scratch=scratch)
-        else:
-            kept, sent = call(functools.partial(halve_kernel, bit), outs, kept, came, scratch=scratch)
-        came = swap(sent, bit)
-    (share,) = call(add_kernel, [((n_item, part, width), f32)], kept, came)
-    shares = lax.all_to_all(share, "item", split_axis=0, concat_axis=0, tiled=True)
-    weight_grad = jnp.sum(shares, axis=0)
+    weight_grad = reduce_scatter(embed, dhidden)
 
     table_grad = pl.pallas_call(
         table_kernel,
@@ -272,7 +291,7 @@
         scratch_shapes=[pltpu.VMEM((rows, width), bf16), pltpu.SemaphoreType.DMA((groups,))],
         compiler_params=params(),
         cost_estimate=cost(2 * total * rows * width, 2 * rows * width),
-    )(pick, incoming, tower_weight)
+    )(low_hot, block, incoming, tower_weight)
     return (table_grad, weight_grad)
 
 

time: 85.8 us -> 69.9 us (0.81)
  blocking collectives: 23 us -> 11.8 us
  waiting for transfers between devices: 35 us -> 27.7 us
  starting transfers between devices: 9.77 us -> 17 us
  local copies, waits for them, and re-layouts: 4.21 us -> 0.01 us
    all_to_all x1, waiting for transfers between devices: 15.7 us -> 0.01 us  [local(): exchange(outgoing.reshape(devices, slots, width)).reshape(total, width)]
    all_to_all x1 -> x0, blocking collectives: 11.2 us -> none  [local(): lax.all_to_all(share, 'item', split_axis=0, concat_axis=0, tiled=True)]
    ppermute x5 -> x10, starting transfers between devices: 4.26 us -> 11.8 us  [swap(): lax.ppermute(value, ('batch', 'item'), [(k, k ^ mask) for k in range(devi...]
    ppermute x5 -> x10, waiting for transfers between devices: 7.92 us -> 13.9 us  [swap(): lax.ppermute(value, ('batch', 'item'), [(k, k ^ mask) for k in range(devi...]
    unnamed x10 -> x6, local copies, waits for them, and re-layouts: 4.21 us -> 0.01 us
    all_to_all x1, waiting for transfers between devices: 11.3 us -> 13.8 us  [local(): exchange(found.reshape(devices, slots, width)).reshape(total, width)]
    pallas_call x7 -> x8, Pallas kernels: 7.73 us -> 7.89 us  [call(): pl.pallas_call(kernel, out_shape=[jax.ShapeDtypeStruct(shape, dtype) for...]
  transfers between devices with their start and end apart: 7 -> 12, of which waited for: 6 -> 10; matrix products, arithmetic and copies ran while one was open for 2% -> 1% of each run, Pallas kernels for 2% -> 3%
where the time goes in v5:
time: 69.9 us; the launch traced here: 69.4 us
  waiting for transfers between devices  27.7 us (40%)
  starting transfers between devices  17 us (24%)
  blocking collectives  11.8 us (17%)
  Pallas kernels  11.5 us (16%)
  between operations  0.71 us (1%)
  other arithmetic  0.7 us (1%)
    ppermute x10, waiting for transfers between devices, swap(): lax.ppermute(value, ('batch', 'item'), [(k, k ^ mask) for k in range(devi...  13.9 us
    all_to_all x1, waiting for transfers between devices, local(): exchange(found.reshape(devices, slots, width)).reshape(total, width)  13.8 us
    all_to_all x1, blocking collectives, local(): asked, *users = lax.optimization_barrier((exchange(request), *users))  11.8 us
    ppermute x10, starting transfers between devices, swap(): lax.ppermute(value, ('batch', 'item'), [(k, k ^ mask) for k in range(devi...  11.8 us
    pallas_call x8, Pallas kernels, call(): pl.pallas_call(kernel, out_shape=[jax.ShapeDtypeStruct(shape, dtype) for...  7.89 us
    pallas_call x1, Pallas kernels, local(): pl.pallas_call(table_kernel, out_specs=pl.BlockSpec(memory_space=pl.ANY),...  3.6 us
    all_to_all x1, starting transfers between devices, local(): exchange(outgoing.reshape(devices, slots, width)).reshape(total, width)  2.61 us
    all_to_all x1, starting transfers between devices, local(): exchange(found.reshape(devices, slots, width)).reshape(total, width)  2.61 us
  transfers between devices with their start and end apart: 12, of which 10 were waited for; matrix products, arithmetic and copies ran while one was open for 1% of the time, Pallas kernels for 3%

profile of v5, /device:TPU:0, one launch (start us, length us, event | category | flops | bytes accessed | tf_op | source)
XLA Modules:
  0.0 69.4 jit_solution(11574274070635965805)
XLA Ops:
  0.6 3.0 %collective-permute-start = (bf16[256,512]{1,0:T(8,128)(2,1)}, bf16[256,512]{1,0:T(8,128)(2,1)S(1)}, u32[]{:S(2)}, u32[]{:S(2)}) collective-permute-start(bf16[256,512]{1,0:T(8,128)(2,1)} %refs_0_), channel_id=1, source_target_pairs={{0,16},{1,17},{2,18},{3,19},{4,20},{5,21},{6,22},{7,23},{8,24},{9,... | collective-permute-start | bytes 786440 | tf_op jit(solution)/shard_map/ppermute | solution.py:203
  3.6 0.7 %pad_add_fusion.named_ref = s32[2,256]{1,0:T(2,128)S(1)} fusion(s32[1,256]{1,0:T(1,128)} %bitcast.15, s32[1,256]{1,0:T(1,128)} %bitcast.16), kind=kLoop, calls=%fused_computation | loop fusion | flops 512 | bytes 4096 | tf_op jit(solution)/shard_map/stack | solution.py:257
  4.3 0.3 shard_map.68
  4.6 11.8 %all_to_all.22 = s32[32,1,16]{2,1,0:T(1,128)S(1)} all-to-all(s32[32,1,16]{2,1,0:T(1,128)S(1)} %bitcast.14), channel_id=1, replica_groups=mesh['batch'=4,'item'=8] {'batch','item'}, dimensions={0} | all-to-all | bytes 4096 | tf_op jit(solution)/shard_map/all_to_all | solution.py:260
  16.5 3.3 %shard_map.70 = bf16[512,512]{1,0:T(8,128)(2,1)} custom-call(s32[32,16]{1,0:T(8,128)S(1)} %bitcast.12, bf16[4096,512]{1,0:T(8,128)(2,1)S(1)} %copy-done.1), custom_call_target="tpu_custom_call" | custom-call | flops 2147483648 | bytes 1048576 | tf_op jit(solution)/shard_map/pallas_call | solution.py:191
  19.8 2.6 %all-to-all-start.1 = ((bf16[32,16,512]{2,1,0:T(8,128)(2,1)}), bf16[32,16,512]{2,1,0:T(8,128)(2,1)S(1)}, u32[]{:S(2)}, u32[]{:S(2)}) async-start(bf16[32,16,512]{2,1,0:T(8,128)(2,1)} %bitcast.5), calls=%async_computation.1 | async-start | bytes 1048576 | tf_op jit(solution)/shard_map/all_to_all | solution.py:262
  22.5 0.2 collective-permute-start.1
  22.6 0.4 collective-permute-start.2
  23.0 1.0 %collective-permute-done.1.refs_2_ = bf16[256,512]{1,0:T(8,128)(2,1)S(1)} collective-permute-done((bf16[256,512]{1,0:T(8,128)(2,1)S(1)}, bf16[256,512]{1,0:T(8,128)(2,1)S(1)}, u32[]{:S(2)}, u32[]{:S(2)}) %collective-permute-start.1) | collective-permute-done | bytes 262176 | tf_op jit(solution)/shard_map/ppermute | solution.py:203
  24.1 0.4 collective-permute-done.2.refs_3_
  24.4 0.6 shard_map.69
  25.0 13.8 %all-to-all-done.1 = bf16[32,16,512]{2,1,0:T(8,128)(2,1)S(1)} async-done(((bf16[32,16,512]{2,1,0:T(8,128)(2,1)}), bf16[32,16,512]{2,1,0:T(8,128)(2,1)S(1)}, u32[]{:S(2)}, u32[]{:S(2)}) %all-to-all-start.1) | async-done | bytes 524320 | tf_op jit(solution)/shard_map/all_to_all | solution.py:262
  38.8 2.5 %shard_map.71 = (bf16[512,512]{1,0:T(8,128)(2,1)}, bf16[256,512]{1,0:T(8,128)(2,1)S(1)}, bf16[256,512]{1,0:T(8,128)(2,1)S(1)}) custom-call(bf16[512,512]{1,0:T(8,128)(2,1)S(1)} %bitcast.11, bf16[512,512]{1,0:T(8,128)(2,1)S(1)} %copy-done.2, bf16[1024,512]{1,0:T(8,128)(2,1)S(1)} %get-tuple-element.31.unit_ref, s32[1,256]{1,0:T(1,128)S(1)} %get-tuple-element.24.place_ref, ...), custom_call_target="tpu_custom_call" | custom-call | flops 1073741824 | bytes 1048576 | tf_op jit(solution)/shard_map/pallas_call | solution.py:191
  41.4 2.6 %all-to-all-start.2 = ((bf16[32,16,512]{2,1,0:T(8,128)(2,1)}), bf16[32,16,512]{2,1,0:T(8,128)(2,1)S(1)}, u32[]{:S(2)}, u32[]{:S(2)}) async-start(bf16[32,16,512]{2,1,0:T(8,128)(2,1)} %bitcast.7), calls=%async_computation.2 | async-start | bytes 1048576 | tf_op jit(solution)/shard_map/all_to_all | solution.py:283
  44.0 0.4 shard_map.73
  44.4 0.2 collective-permute-start.3
  44.6 1.4 %collective-permute-done.3.refs_1_ = bf16[16,16,512]{2,1,0:T(8,128)(2,1)S(1)} collective-permute-done((bf16[16,16,512]{2,1,0:T(8,128)(2,1)S(1)}, bf16[16,16,512]{2,1,0:T(8,128)(2,1)S(1)}, u32[]{:S(2)}, u32[]{:S(2)}) %collective-permute-start.3) | collective-permute-done | bytes 262176 | tf_op jit(solution)/shard_map/ppermute | solution.py:203
  46.0 0.1 shard_map.74
  46.0 1.7 %collective-permute-start.4 = (bf16[4,16,512]{2,1,0:T(8,128)(2,1)S(1)}, bf16[4,16,512]{2,1,0:T(8,128)(2,1)S(1)}, u32[]{:S(2)}, u32[]{:S(2)}) collective-permute-start(bf16[4,16,512]{2,1,0:T(8,128)(2,1)S(1)} %get-tuple-element.39), channel_id=1, source_target_pairs={{0,1},{1,0},{2,3},{3,2},{4,5},{5,4},{6,7},{7,6},{8,9},{9,8},{10,11... | collective-permute-start | bytes 196616 | tf_op jit(solution)/shard_map/ppermute | solution.py:203
  47.8 1.5 %collective-permute-start.5 = (bf16[4,16,512]{2,1,0:T(8,128)(2,1)S(1)}, bf16[4,16,512]{2,1,0:T(8,128)(2,1)S(1)}, u32[]{:S(2)}, u32[]{:S(2)}) collective-permute-start(bf16[4,16,512]{2,1,0:T(8,128)(2,1)S(1)} %get-tuple-element.40), channel_id=1, source_target_pairs={{0,16},{1,17},{2,18},{3,19},{4,20},{5,21},{6,22},{7,23},{8,24},{9,... | collective-permute-start | bytes 196616 | tf_op jit(solution)/shard_map/ppermute | solution.py:203
  49.2 0.4 collective-permute-start.6
  49.6 3.0 %collective-permute-done.4.refs_1_ = bf16[4,16,512]{2,1,0:T(8,128)(2,1)S(1)} collective-permute-done((bf16[4,16,512]{2,1,0:T(8,128)(2,1)S(1)}, bf16[4,16,512]{2,1,0:T(8,128)(2,1)S(1)}, u32[]{:S(2)}, u32[]{:S(2)}) %collective-permute-start.4) | collective-permute-done | bytes 65568 | tf_op jit(solution)/shard_map/ppermute | solution.py:203
  52.6 0.7 %collective-permute-done.5.refs_2_ = bf16[4,16,512]{2,1,0:T(8,128)(2,1)S(1)} collective-permute-done((bf16[4,16,512]{2,1,0:T(8,128)(2,1)S(1)}, bf16[4,16,512]{2,1,0:T(8,128)(2,1)S(1)}, u32[]{:S(2)}, u32[]{:S(2)}) %collective-permute-start.5) | collective-permute-done | bytes 65568 | tf_op jit(solution)/shard_map/ppermute | solution.py:203
  53.3 2.1 %collective-permute-done.6.refs_3_ = bf16[4,16,512]{2,1,0:T(8,128)(2,1)S(1)} collective-permute-done((bf16[4,16,512]{2,1,0:T(8,128)(2,1)S(1)}, bf16[4,16,512]{2,1,0:T(8,128)(2,1)S(1)}, u32[]{:S(2)}, u32[]{:S(2)}) %collective-permute-start.6) | collective-permute-done | bytes 65568 | tf_op jit(solution)/shard_map/ppermute | solution.py:203
  55.4 2.9 %collective-permute-start.7 = (f32[1,16,512]{2,1,0:T(8,128)S(1)}, f32[1,16,512]{2,1,0:T(8,128)S(1)}, u32[]{:S(2)}, u32[]{:S(2)}) collective-permute-start(f32[1,16,512]{2,1,0:T(8,128)S(1)} %get-tuple-element.43), channel_id=1, source_target_pairs={{0,4},{1,5},{2,6},{3,7},{4,0},{5,1},{6,2},{7,3},{8,12},{9,13},{10,... | collective-permute-start | bytes 98312 | tf_op jit(solution)/shard_map/ppermute | solution.py:203
  58.3 1.2 %collective-permute-start.8 = (f32[1,16,512]{2,1,0:T(8,128)S(1)}, f32[1,16,512]{2,1,0:T(8,128)S(1)}, u32[]{:S(2)}, u32[]{:S(2)}) collective-permute-start(f32[1,16,512]{2,1,0:T(8,128)S(1)} %get-tuple-element.44), channel_id=1, source_target_pairs={{0,2},{1,3},{2,0},{3,1},{4,6},{5,7},{6,4},{7,5},{8,10},{9,11},{10,... | collective-permute-start | bytes 98312 | tf_op jit(solution)/shard_map/ppermute | solution.py:203
  59.5 0.4 collective-permute-start.9
  59.9 0.4 collective-permute-done.7.refs_1_
  60.3 1.9 %collective-permute-done.8.refs_2_ = f32[1,16,512]{2,1,0:T(8,128)S(1)} collective-permute-done((f32[1,16,512]{2,1,0:T(8,128)S(1)}, f32[1,16,512]{2,1,0:T(8,128)S(1)}, u32[]{:S(2)}, u32[]{:S(2)}) %collective-permute-start.8) | collective-permute-done | bytes 32800 | tf_op jit(solution)/shard_map/ppermute | solution.py:203
  62.2 3.0 %collective-permute-done.9.refs_3_ = f32[1,16,512]{2,1,0:T(8,128)S(1)} collective-permute-done((f32[1,16,512]{2,1,0:T(8,128)S(1)}, f32[1,16,512]{2,1,0:T(8,128)S(1)}, u32[]{:S(2)}, u32[]{:S(2)}) %collective-permute-start.9) | collective-permute-done | bytes 32800 | tf_op jit(solution)/shard_map/ppermute | solution.py:203
  65.2 0.6 shard_map.76
  65.8 3.6 %shard_map.72 = bf16[4096,512]{1,0:T(8,128)(2,1)} custom-call(bf16[256,512]{1,0:T(8,128)(2,1)S(1)} %get-tuple-element.29.low_hot_ref, bf16[256,512]{1,0:T(8,128)(2,1)S(1)} %get-tuple-element.30.block_ref, bf16[512,512]{1,0:T(8,128)(2,1)S(1)} %bitcast.10, bf16[512,512]{1,0:T(8,128)(2,1)S(1)} %copy-done.2), custom_call_target="tpu_custom_call" | custom-call | flops 2147483648 | bytes 4194304 | tf_op jit(solution)/shard_map/pallas_call | solution.py:287
  (9 shorter events, 0.1 us)
Async XLA Ops:
  0.6 15.9 %collective-permute-start = (bf16[256,512]{1,0:T(8,128)(2,1)}, bf16[256,512]{1,0:T(8,128)(2,1)S(1)}, u32[]{:S(2)}, u32[]{:S(2)}) collective-permute-start(bf16[256,512]{1,0:T(8,128)(2,1)} %refs_0_), channel_id=1, source_target_pairs={{0,16},{1,17},{2,18},{3,19},{4,20},{5,21},{6,22},{7,23},{8,24},{9,... | collective-permute-start | bytes 786440 | tf_op jit(solution)/shard_map/ppermute | solution.py:203
  4.3 12.2 %copy-start.1 = (bf16[4096,512]{1,0:T(8,128)(2,1)S(1)}, bf16[4096,512]{1,0:T(8,128)(2,1)}, u32[]{:S(2)}) copy-start(bf16[4096,512]{1,0:T(8,128)(2,1)} %table_ref.1) | copy-start | bytes 12582916
  16.5 6.0 %copy-start = (bf16[256,512]{1,0:T(8,128)(2,1)S(1)}, bf16[256,512]{1,0:T(8,128)(2,1)}, u32[]{:S(2)}) copy-start(bf16[256,512]{1,0:T(8,128)(2,1)} %refs_0_) | copy-start | bytes 786436
  16.5 22.3 %copy-start.2 = (bf16[512,512]{1,0:T(8,128)(2,1)S(1)}, bf16[512,512]{1,0:T(8,128)(2,1)}, u32[]{:S(2)}) copy-start(bf16[512,512]{1,0:T(8,128)(2,1)} %weight_ref.3) | copy-start | bytes 1572868
  19.8 19.0 %all-to-all-start.1 = ((bf16[32,16,512]{2,1,0:T(8,128)(2,1)}), bf16[32,16,512]{2,1,0:T(8,128)(2,1)S(1)}, u32[]{:S(2)}, u32[]{:S(2)}) async-start(bf16[32,16,512]{2,1,0:T(8,128)(2,1)} %bitcast.5), calls=%async_computation.1 | async-start | bytes 1048576 | tf_op jit(solution)/shard_map/all_to_all | solution.py:262
  22.5 1.6 %collective-permute-start.1 = (bf16[256,512]{1,0:T(8,128)(2,1)S(1)}, bf16[256,512]{1,0:T(8,128)(2,1)S(1)}, u32[]{:S(2)}, u32[]{:S(2)}) collective-permute-start(bf16[256,512]{1,0:T(8,128)(2,1)S(1)} %copy-done), channel_id=1, source_target_pairs={{0,8},{1,9},{2,10},{3,11},{4,12},{5,13},{6,14},{7,15},{8,0},{9,1},... | collective-permute-start | bytes 786440 | tf_op jit(solution)/shard_map/ppermute | solution.py:203
  22.6 1.8 %collective-permute-start.2 = (bf16[256,512]{1,0:T(8,128)(2,1)S(1)}, bf16[256,512]{1,0:T(8,128)(2,1)S(1)}, u32[]{:S(2)}, u32[]{:S(2)}) collective-permute-start(bf16[256,512]{1,0:T(8,128)(2,1)S(1)} %collective-permute-done.refs_1_), channel_id=1, source_target_pairs={{0,8},{1,9},{2,10},{3,11},{4,12},{5,13},{6,14},{7,15},{8,0},{9,1},... | collective-permute-start | bytes 786440 | tf_op jit(solution)/shard_map/ppermute | solution.py:203
  41.4 24.5 %all-to-all-start.2 = ((bf16[32,16,512]{2,1,0:T(8,128)(2,1)}), bf16[32,16,512]{2,1,0:T(8,128)(2,1)S(1)}, u32[]{:S(2)}, u32[]{:S(2)}) async-start(bf16[32,16,512]{2,1,0:T(8,128)(2,1)} %bitcast.7), calls=%async_computation.2 | async-start | bytes 1048576 | tf_op jit(solution)/shard_map/all_to_all | solution.py:283
  44.4 1.6 %collective-permute-start.3 = (bf16[16,16,512]{2,1,0:T(8,128)(2,1)S(1)}, bf16[16,16,512]{2,1,0:T(8,128)(2,1)S(1)}, u32[]{:S(2)}, u32[]{:S(2)}) collective-permute-start(bf16[16,16,512]{2,1,0:T(8,128)(2,1)S(1)} %get-tuple-element.37), channel_id=1, source_target_pairs={{0,8},{1,9},{2,10},{3,11},{4,12},{5,13},{6,14},{7,15},{8,0},{9,1},... | collective-permute-start | bytes 786440 | tf_op jit(solution)/shard_map/ppermute | solution.py:203
  46.0 6.5 %collective-permute-start.4 = (bf16[4,16,512]{2,1,0:T(8,128)(2,1)S(1)}, bf16[4,16,512]{2,1,0:T(8,128)(2,1)S(1)}, u32[]{:S(2)}, u32[]{:S(2)}) collective-permute-start(bf16[4,16,512]{2,1,0:T(8,128)(2,1)S(1)} %get-tuple-element.39), channel_id=1, source_target_pairs={{0,1},{1,0},{2,3},{3,2},{4,5},{5,4},{6,7},{7,6},{8,9},{9,8},{10,11... | collective-permute-start | bytes 196616 | tf_op jit(solution)/shard_map/ppermute | solution.py:203
  47.8 5.5 %collective-permute-start.5 = (bf16[4,16,512]{2,1,0:T(8,128)(2,1)S(1)}, bf16[4,16,512]{2,1,0:T(8,128)(2,1)S(1)}, u32[]{:S(2)}, u32[]{:S(2)}) collective-permute-start(bf16[4,16,512]{2,1,0:T(8,128)(2,1)S(1)} %get-tuple-element.40), channel_id=1, source_target_pairs={{0,16},{1,17},{2,18},{3,19},{4,20},{5,21},{6,22},{7,23},{8,24},{9,... | collective-permute-start | bytes 196616 | tf_op jit(solution)/shard_map/ppermute | solution.py:203
  49.2 6.1 %collective-permute-start.6 = (bf16[4,16,512]{2,1,0:T(8,128)(2,1)S(1)}, bf16[4,16,512]{2,1,0:T(8,128)(2,1)S(1)}, u32[]{:S(2)}, u32[]{:S(2)}) collective-permute-start(bf16[4,16,512]{2,1,0:T(8,128)(2,1)S(1)} %get-tuple-element.41), channel_id=1, source_target_pairs={{0,17},{1,16},{2,19},{3,18},{4,21},{5,20},{6,23},{7,22},{8,25},{9,... | collective-permute-start | bytes 196616 | tf_op jit(solution)/shard_map/ppermute | solution.py:203
  55.4 4.9 %collective-permute-start.7 = (f32[1,16,512]{2,1,0:T(8,128)S(1)}, f32[1,16,512]{2,1,0:T(8,128)S(1)}, u32[]{:S(2)}, u32[]{:S(2)}) collective-permute-start(f32[1,16,512]{2,1,0:T(8,128)S(1)} %get-tuple-element.43), channel_id=1, source_target_pairs={{0,4},{1,5},{2,6},{3,7},{4,0},{5,1},{6,2},{7,3},{8,12},{9,13},{10,... | collective-permute-start | bytes 98312 | tf_op jit(solution)/shard_map/ppermute | solution.py:203
  58.3 3.9 %collective-permute-start.8 = (f32[1,16,512]{2,1,0:T(8,128)S(1)}, f32[1,16,512]{2,1,0:T(8,128)S(1)}, u32[]{:S(2)}, u32[]{:S(2)}) collective-permute-start(f32[1,16,512]{2,1,0:T(8,128)S(1)} %get-tuple-element.44), channel_id=1, source_target_pairs={{0,2},{1,3},{2,0},{3,1},{4,6},{5,7},{6,4},{7,5},{8,10},{9,11},{10,... | collective-permute-start | bytes 98312 | tf_op jit(solution)/shard_map/ppermute | solution.py:203
  59.5 5.7 %collective-permute-start.9 = (f32[1,16,512]{2,1,0:T(8,128)S(1)}, f32[1,16,512]{2,1,0:T(8,128)S(1)}, u32[]{:S(2)}, u32[]{:S(2)}) collective-permute-start(f32[1,16,512]{2,1,0:T(8,128)S(1)} %get-tuple-element.45), channel_id=1, source_target_pairs={{0,6},{1,7},{2,4},{3,5},{4,2},{5,3},{6,0},{7,1},{8,14},{9,15},{10,... | collective-permute-start | bytes 98312 | tf_op jit(solution)/shard_map/ppermute | solution.py:203

commit v6 on v5

--- a/solution.py
+++ b/solution.py
@@ -234,7 +234,7 @@
         values = [kept]
         for step, value in enumerate(sends, 1):
             values.append(swap(value, *[bit for j, bit in enumerate(reversed(stage)) if step >> j & 1]))
-    return call(last_kernel, [((part, width), f32)], *values)[0]
+    return values
 
 
 def local(user_vectors, item_table, tower_weight, item_owner, item_row):
@@ -282,7 +282,7 @@
     )
     incoming = exchange(outgoing.reshape(devices, slots, width)).reshape(total, width)
 
-    weight_grad = reduce_scatter(embed, dhidden)
+    terms = reduce_scatter(embed, dhidden)
 
     table_grad = pl.pallas_call(
         table_kernel,
@@ -292,6 +292,8 @@
         compiler_params=params(),
         cost_estimate=cost(2 * total * rows * width, 2 * rows * width),
     )(low_hot, block, incoming, tower_weight)
+    table_grad, *terms = lax.optimization_barrier((table_grad, *terms))
+    (weight_grad,) = call(last_kernel, [((width // devices, width), f32)], *terms)
     return (table_grad, weight_grad)
 
 

time: 69.9 us -> 66.3 us (0.948)
  waiting for transfers between devices: 27.7 us -> 24 us
    ppermute x10, waiting for transfers between devices: 13.9 us -> 9.85 us  [swap(): lax.ppermute(value, ('batch', 'item'), [(k, k ^ mask) for k in range(devi...]
  transfers between devices with their start and end apart: 12 -> 12, of which waited for: 10 -> 9; matrix products, arithmetic and copies ran while one was open for 1% -> 1% of each run, Pallas kernels for 3% -> 8%
where the time goes in v6:
time: 66.3 us; the launch traced here: 65.8 us
  waiting for transfers between devices  24 us (36%)
  starting transfers between devices  17 us (26%)
  blocking collectives  11.8 us (18%)
  Pallas kernels  11.5 us (17%)
  between operations  0.73 us (1%)
  other arithmetic  0.7 us (1%)
    all_to_all x1, waiting for transfers between devices, local(): exchange(found.reshape(devices, slots, width)).reshape(total, width)  13.8 us
    all_to_all x1, blocking collectives, local(): asked, *users = lax.optimization_barrier((exchange(request), *users))  11.8 us
    ppermute x10, starting transfers between devices, swap(): lax.ppermute(value, ('batch', 'item'), [(k, k ^ mask) for k in range(devi...  11.8 us
    ppermute x10, waiting for transfers between devices, swap(): lax.ppermute(value, ('batch', 'item'), [(k, k ^ mask) for k in range(devi...  9.85 us
    pallas_call x8, Pallas kernels, call(): pl.pallas_call(kernel, out_shape=[jax.ShapeDtypeStruct(shape, dtype) for...  7.89 us
    pallas_call x1, Pallas kernels, local(): pl.pallas_call(table_kernel, out_specs=pl.BlockSpec(memory_space=pl.ANY),...  3.6 us
    all_to_all x1, starting transfers between devices, local(): exchange(found.reshape(devices, slots, width)).reshape(total, width)  2.61 us
    all_to_all x1, starting transfers between devices, local(): exchange(outgoing.reshape(devices, slots, width)).reshape(total, width)  2.61 us
  transfers between devices with their start and end apart: 12, of which 9 were waited for; matrix products, arithmetic and copies ran while one was open for 1% of the time, Pallas kernels for 8%

profile of v6, /device:TPU:0, one launch (start us, length us, event | category | flops | bytes accessed | tf_op | source)
XLA Modules:
  0.0 65.8 jit_solution(865234228726057390)
XLA Ops:
  0.6 3.0 %collective-permute-start = (bf16[256,512]{1,0:T(8,128)(2,1)}, bf16[256,512]{1,0:T(8,128)(2,1)S(1)}, u32[]{:S(2)}, u32[]{:S(2)}) collective-permute-start(bf16[256,512]{1,0:T(8,128)(2,1)} %refs_0_), channel_id=1, source_target_pairs={{0,16},{1,17},{2,18},{3,19},{4,20},{5,21},{6,22},{7,23},{8,24},{9,... | collective-permute-start | bytes 786440 | tf_op jit(solution)/shard_map/ppermute | solution.py:203
  3.6 0.7 %pad_add_fusion.named_ref = s32[2,256]{1,0:T(2,128)S(1)} fusion(s32[1,256]{1,0:T(1,128)} %bitcast.15, s32[1,256]{1,0:T(1,128)} %bitcast.16), kind=kLoop, calls=%fused_computation | loop fusion | flops 512 | bytes 4096 | tf_op jit(solution)/shard_map/stack | solution.py:257
  4.3 0.3 shard_map.68
  4.6 11.8 %all_to_all.22 = s32[32,1,16]{2,1,0:T(1,128)S(1)} all-to-all(s32[32,1,16]{2,1,0:T(1,128)S(1)} %bitcast.14), channel_id=1, replica_groups=mesh['batch'=4,'item'=8] {'batch','item'}, dimensions={0} | all-to-all | bytes 4096 | tf_op jit(solution)/shard_map/all_to_all | solution.py:260
  16.5 0.0 copy-start.2
  16.5 3.3 %shard_map.70 = bf16[512,512]{1,0:T(8,128)(2,1)} custom-call(s32[32,16]{1,0:T(8,128)S(1)} %bitcast.12, bf16[4096,512]{1,0:T(8,128)(2,1)S(1)} %copy-done.1), custom_call_target="tpu_custom_call" | custom-call | flops 2147483648 | bytes 1048576 | tf_op jit(solution)/shard_map/pallas_call | solution.py:191
  19.8 2.6 %all-to-all-start.1 = ((bf16[32,16,512]{2,1,0:T(8,128)(2,1)}), bf16[32,16,512]{2,1,0:T(8,128)(2,1)S(1)}, u32[]{:S(2)}, u32[]{:S(2)}) async-start(bf16[32,16,512]{2,1,0:T(8,128)(2,1)} %bitcast.5), calls=%async_computation.1 | async-start | bytes 1048576 | tf_op jit(solution)/shard_map/all_to_all | solution.py:262
  22.5 0.2 collective-permute-start.1
  22.6 0.4 collective-permute-start.2
  23.0 1.0 %collective-permute-done.1.refs_2_ = bf16[256,512]{1,0:T(8,128)(2,1)S(1)} collective-permute-done((bf16[256,512]{1,0:T(8,128)(2,1)S(1)}, bf16[256,512]{1,0:T(8,128)(2,1)S(1)}, u32[]{:S(2)}, u32[]{:S(2)}) %collective-permute-start.1) | collective-permute-done | bytes 262176 | tf_op jit(solution)/shard_map/ppermute | solution.py:203
  24.1 0.4 collective-permute-done.2.refs_3_
  24.4 0.6 shard_map.69
  25.0 13.8 %all-to-all-done.1 = bf16[32,16,512]{2,1,0:T(8,128)(2,1)S(1)} async-done(((bf16[32,16,512]{2,1,0:T(8,128)(2,1)}), bf16[32,16,512]{2,1,0:T(8,128)(2,1)S(1)}, u32[]{:S(2)}, u32[]{:S(2)}) %all-to-all-start.1) | async-done | bytes 524320 | tf_op jit(solution)/shard_map/all_to_all | solution.py:262
  38.8 2.5 %shard_map.71 = (bf16[512,512]{1,0:T(8,128)(2,1)}, bf16[256,512]{1,0:T(8,128)(2,1)S(1)}, bf16[256,512]{1,0:T(8,128)(2,1)S(1)}) custom-call(bf16[512,512]{1,0:T(8,128)(2,1)S(1)} %bitcast.11, bf16[512,512]{1,0:T(8,128)(2,1)S(1)} %copy-done.2, bf16[1024,512]{1,0:T(8,128)(2,1)S(1)} %get-tuple-element.36.unit_ref, s32[1,256]{1,0:T(1,128)S(1)} %get-tuple-element.29.place_ref, ...), custom_call_target="tpu_custom_call" | custom-call | flops 1073741824 | bytes 1048576 | tf_op jit(solution)/shard_map/pallas_call | solution.py:191
  41.4 2.6 %all-to-all-start.2 = ((bf16[32,16,512]{2,1,0:T(8,128)(2,1)}), bf16[32,16,512]{2,1,0:T(8,128)(2,1)S(1)}, u32[]{:S(2)}, u32[]{:S(2)}) async-start(bf16[32,16,512]{2,1,0:T(8,128)(2,1)} %bitcast.7), calls=%async_computation.2 | async-start | bytes 1048576 | tf_op jit(solution)/shard_map/all_to_all | solution.py:283
  44.0 0.4 shard_map.73
  44.4 0.2 collective-permute-start.3
  44.6 1.4 %collective-permute-done.3.refs_1_ = bf16[16,16,512]{2,1,0:T(8,128)(2,1)S(1)} collective-permute-done((bf16[16,16,512]{2,1,0:T(8,128)(2,1)S(1)}, bf16[16,16,512]{2,1,0:T(8,128)(2,1)S(1)}, u32[]{:S(2)}, u32[]{:S(2)}) %collective-permute-start.3) | collective-permute-done | bytes 262176 | tf_op jit(solution)/shard_map/ppermute | solution.py:203
  46.0 0.1 shard_map.74
  46.0 1.7 %collective-permute-start.4 = (bf16[4,16,512]{2,1,0:T(8,128)(2,1)S(1)}, bf16[4,16,512]{2,1,0:T(8,128)(2,1)S(1)}, u32[]{:S(2)}, u32[]{:S(2)}) collective-permute-start(bf16[4,16,512]{2,1,0:T(8,128)(2,1)S(1)} %get-tuple-element.44), channel_id=1, source_target_pairs={{0,1},{1,0},{2,3},{3,2},{4,5},{5,4},{6,7},{7,6},{8,9},{9,8},{10,11... | collective-permute-start | bytes 196616 | tf_op jit(solution)/shard_map/ppermute | solution.py:203
  47.8 1.5 %collective-permute-start.5 = (bf16[4,16,512]{2,1,0:T(8,128)(2,1)S(1)}, bf16[4,16,512]{2,1,0:T(8,128)(2,1)S(1)}, u32[]{:S(2)}, u32[]{:S(2)}) collective-permute-start(bf16[4,16,512]{2,1,0:T(8,128)(2,1)S(1)} %get-tuple-element.45), channel_id=1, source_target_pairs={{0,16},{1,17},{2,18},{3,19},{4,20},{5,21},{6,22},{7,23},{8,24},{9,... | collective-permute-start | bytes 196616 | tf_op jit(solution)/shard_map/ppermute | solution.py:203
  49.2 0.4 collective-permute-start.6
  49.6 3.0 %collective-permute-done.4.refs_1_ = bf16[4,16,512]{2,1,0:T(8,128)(2,1)S(1)} collective-permute-done((bf16[4,16,512]{2,1,0:T(8,128)(2,1)S(1)}, bf16[4,16,512]{2,1,0:T(8,128)(2,1)S(1)}, u32[]{:S(2)}, u32[]{:S(2)}) %collective-permute-start.4) | collective-permute-done | bytes 65568 | tf_op jit(solution)/shard_map/ppermute | solution.py:203
  52.6 0.7 %collective-permute-done.5.refs_2_ = bf16[4,16,512]{2,1,0:T(8,128)(2,1)S(1)} collective-permute-done((bf16[4,16,512]{2,1,0:T(8,128)(2,1)S(1)}, bf16[4,16,512]{2,1,0:T(8,128)(2,1)S(1)}, u32[]{:S(2)}, u32[]{:S(2)}) %collective-permute-start.5) | collective-permute-done | bytes 65568 | tf_op jit(solution)/shard_map/ppermute | solution.py:203
  53.3 2.1 %collective-permute-done.6.refs_3_ = bf16[4,16,512]{2,1,0:T(8,128)(2,1)S(1)} collective-permute-done((bf16[4,16,512]{2,1,0:T(8,128)(2,1)S(1)}, bf16[4,16,512]{2,1,0:T(8,128)(2,1)S(1)}, u32[]{:S(2)}, u32[]{:S(2)}) %collective-permute-start.6) | collective-permute-done | bytes 65568 | tf_op jit(solution)/shard_map/ppermute | solution.py:203
  55.4 2.9 %collective-permute-start.7 = (f32[1,16,512]{2,1,0:T(8,128)S(1)}, f32[1,16,512]{2,1,0:T(8,128)S(1)}, u32[]{:S(2)}, u32[]{:S(2)}) collective-permute-start(f32[1,16,512]{2,1,0:T(8,128)S(1)} %get-tuple-element.48), channel_id=1, source_target_pairs={{0,4},{1,5},{2,6},{3,7},{4,0},{5,1},{6,2},{7,3},{8,12},{9,13},{10,... | collective-permute-start | bytes 98312 | tf_op jit(solution)/shard_map/ppermute | solution.py:203
  58.3 1.2 %collective-permute-start.8 = (f32[1,16,512]{2,1,0:T(8,128)S(1)}, f32[1,16,512]{2,1,0:T(8,128)S(1)}, u32[]{:S(2)}, u32[]{:S(2)}) collective-permute-start(f32[1,16,512]{2,1,0:T(8,128)S(1)} %get-tuple-element.49), channel_id=1, source_target_pairs={{0,2},{1,3},{2,0},{3,1},{4,6},{5,7},{6,4},{7,5},{8,10},{9,11},{10,... | collective-permute-start | bytes 98312 | tf_op jit(solution)/shard_map/ppermute | solution.py:203
  59.5 0.4 collective-permute-start.9
  59.9 0.4 all-to-all-done.2
  60.3 3.6 %shard_map.72 = bf16[4096,512]{1,0:T(8,128)(2,1)} custom-call(bf16[256,512]{1,0:T(8,128)(2,1)S(1)} %get-tuple-element.34.low_hot_ref, bf16[256,512]{1,0:T(8,128)(2,1)S(1)} %get-tuple-element.35.block_ref, bf16[512,512]{1,0:T(8,128)(2,1)S(1)} %bitcast.10, bf16[512,512]{1,0:T(8,128)(2,1)S(1)} %copy-done.2), custom_call_target="tpu_custom_call" | custom-call | flops 2147483648 | bytes 4194304 | tf_op jit(solution)/shard_map/pallas_call | solution.py:287
  63.9 1.3 %collective-permute-done.9.refs_3_ = f32[1,16,512]{2,1,0:T(8,128)S(1)} collective-permute-done((f32[1,16,512]{2,1,0:T(8,128)S(1)}, f32[1,16,512]{2,1,0:T(8,128)S(1)}, u32[]{:S(2)}, u32[]{:S(2)}) %collective-permute-start.9) | collective-permute-done | bytes 32800 | tf_op jit(solution)/shard_map/ppermute | solution.py:203
  65.2 0.6 shard_map.76
  (9 shorter events, 0.1 us)
Async XLA Ops:
  0.6 15.9 %collective-permute-start = (bf16[256,512]{1,0:T(8,128)(2,1)}, bf16[256,512]{1,0:T(8,128)(2,1)S(1)}, u32[]{:S(2)}, u32[]{:S(2)}) collective-permute-start(bf16[256,512]{1,0:T(8,128)(2,1)} %refs_0_), channel_id=1, source_target_pairs={{0,16},{1,17},{2,18},{3,19},{4,20},{5,21},{6,22},{7,23},{8,24},{9,... | collective-permute-start | bytes 786440 | tf_op jit(solution)/shard_map/ppermute | solution.py:203
  4.3 12.2 %copy-start.1 = (bf16[4096,512]{1,0:T(8,128)(2,1)S(1)}, bf16[4096,512]{1,0:T(8,128)(2,1)}, u32[]{:S(2)}) copy-start(bf16[4096,512]{1,0:T(8,128)(2,1)} %table_ref.1) | copy-start | bytes 12582916
  16.5 6.0 %copy-start = (bf16[256,512]{1,0:T(8,128)(2,1)S(1)}, bf16[256,512]{1,0:T(8,128)(2,1)}, u32[]{:S(2)}) copy-start(bf16[256,512]{1,0:T(8,128)(2,1)} %refs_0_) | copy-start | bytes 786436
  16.5 22.3 %copy-start.2 = (bf16[512,512]{1,0:T(8,128)(2,1)S(1)}, bf16[512,512]{1,0:T(8,128)(2,1)}, u32[]{:S(2)}) copy-start(bf16[512,512]{1,0:T(8,128)(2,1)} %weight_ref.3) | copy-start | bytes 1572868
  19.8 19.0 %all-to-all-start.1 = ((bf16[32,16,512]{2,1,0:T(8,128)(2,1)}), bf16[32,16,512]{2,1,0:T(8,128)(2,1)S(1)}, u32[]{:S(2)}, u32[]{:S(2)}) async-start(bf16[32,16,512]{2,1,0:T(8,128)(2,1)} %bitcast.5), calls=%async_computation.1 | async-start | bytes 1048576 | tf_op jit(solution)/shard_map/all_to_all | solution.py:262
  22.5 1.6 %collective-permute-start.1 = (bf16[256,512]{1,0:T(8,128)(2,1)S(1)}, bf16[256,512]{1,0:T(8,128)(2,1)S(1)}, u32[]{:S(2)}, u32[]{:S(2)}) collective-permute-start(bf16[256,512]{1,0:T(8,128)(2,1)S(1)} %copy-done), channel_id=1, source_target_pairs={{0,8},{1,9},{2,10},{3,11},{4,12},{5,13},{6,14},{7,15},{8,0},{9,1},... | collective-permute-start | bytes 786440 | tf_op jit(solution)/shard_map/ppermute | solution.py:203
  22.6 1.8 %collective-permute-start.2 = (bf16[256,512]{1,0:T(8,128)(2,1)S(1)}, bf16[256,512]{1,0:T(8,128)(2,1)S(1)}, u32[]{:S(2)}, u32[]{:S(2)}) collective-permute-start(bf16[256,512]{1,0:T(8,128)(2,1)S(1)} %collective-permute-done.refs_1_), channel_id=1, source_target_pairs={{0,8},{1,9},{2,10},{3,11},{4,12},{5,13},{6,14},{7,15},{8,0},{9,1},... | collective-permute-start | bytes 786440 | tf_op jit(solution)/shard_map/ppermute | solution.py:203
  41.4 19.0 %all-to-all-start.2 = ((bf16[32,16,512]{2,1,0:T(8,128)(2,1)}), bf16[32,16,512]{2,1,0:T(8,128)(2,1)S(1)}, u32[]{:S(2)}, u32[]{:S(2)}) async-start(bf16[32,16,512]{2,1,0:T(8,128)(2,1)} %bitcast.7), calls=%async_computation.2 | async-start | bytes 1048576 | tf_op jit(solution)/shard_map/all_to_all | solution.py:283
  44.4 1.6 %collective-permute-start.3 = (bf16[16,16,512]{2,1,0:T(8,128)(2,1)S(1)}, bf16[16,16,512]{2,1,0:T(8,128)(2,1)S(1)}, u32[]{:S(2)}, u32[]{:S(2)}) collective-permute-start(bf16[16,16,512]{2,1,0:T(8,128)(2,1)S(1)} %get-tuple-element.42), channel_id=1, source_target_pairs={{0,8},{1,9},{2,10},{3,11},{4,12},{5,13},{6,14},{7,15},{8,0},{9,1},... | collective-permute-start | bytes 786440 | tf_op jit(solution)/shard_map/ppermute | solution.py:203
  46.0 6.5 %collective-permute-start.4 = (bf16[4,16,512]{2,1,0:T(8,128)(2,1)S(1)}, bf16[4,16,512]{2,1,0:T(8,128)(2,1)S(1)}, u32[]{:S(2)}, u32[]{:S(2)}) collective-permute-start(bf16[4,16,512]{2,1,0:T(8,128)(2,1)S(1)} %get-tuple-element.44), channel_id=1, source_target_pairs={{0,1},{1,0},{2,3},{3,2},{4,5},{5,4},{6,7},{7,6},{8,9},{9,8},{10,11... | collective-permute-start | bytes 196616 | tf_op jit(solution)/shard_map/ppermute | solution.py:203
  47.8 5.5 %collective-permute-start.5 = (bf16[4,16,512]{2,1,0:T(8,128)(2,1)S(1)}, bf16[4,16,512]{2,1,0:T(8,128)(2,1)S(1)}, u32[]{:S(2)}, u32[]{:S(2)}) collective-permute-start(bf16[4,16,512]{2,1,0:T(8,128)(2,1)S(1)} %get-tuple-element.45), channel_id=1, source_target_pairs={{0,16},{1,17},{2,18},{3,19},{4,20},{5,21},{6,22},{7,23},{8,24},{9,... | collective-permute-start | bytes 196616 | tf_op jit(solution)/shard_map/ppermute | solution.py:203
  49.2 6.1 %collective-permute-start.6 = (bf16[4,16,512]{2,1,0:T(8,128)(2,1)S(1)}, bf16[4,16,512]{2,1,0:T(8,128)(2,1)S(1)}, u32[]{:S(2)}, u32[]{:S(2)}) collective-permute-start(bf16[4,16,512]{2,1,0:T(8,128)(2,1)S(1)} %get-tuple-element.46), channel_id=1, source_target_pairs={{0,17},{1,16},{2,19},{3,18},{4,21},{5,20},{6,23},{7,22},{8,25},{9,... | collective-permute-start | bytes 196616 | tf_op jit(solution)/shard_map/ppermute | solution.py:203
  55.4 8.5 %collective-permute-start.7 = (f32[1,16,512]{2,1,0:T(8,128)S(1)}, f32[1,16,512]{2,1,0:T(8,128)S(1)}, u32[]{:S(2)}, u32[]{:S(2)}) collective-permute-start(f32[1,16,512]{2,1,0:T(8,128)S(1)} %get-tuple-element.48), channel_id=1, source_target_pairs={{0,4},{1,5},{2,6},{3,7},{4,0},{5,1},{6,2},{7,3},{8,12},{9,13},{10,... | collective-permute-start | bytes 98312 | tf_op jit(solution)/shard_map/ppermute | solution.py:203
  58.3 5.6 %collective-permute-start.8 = (f32[1,16,512]{2,1,0:T(8,128)S(1)}, f32[1,16,512]{2,1,0:T(8,128)S(1)}, u32[]{:S(2)}, u32[]{:S(2)}) collective-permute-start(f32[1,16,512]{2,1,0:T(8,128)S(1)} %get-tuple-element.49), channel_id=1, source_target_pairs={{0,2},{1,3},{2,0},{3,1},{4,6},{5,7},{6,4},{7,5},{8,10},{9,11},{10,... | collective-permute-start | bytes 98312 | tf_op jit(solution)/shard_map/ppermute | solution.py:203
  59.5 5.7 %collective-permute-start.9 = (f32[1,16,512]{2,1,0:T(8,128)S(1)}, f32[1,16,512]{2,1,0:T(8,128)S(1)}, u32[]{:S(2)}, u32[]{:S(2)}) collective-permute-start(f32[1,16,512]{2,1,0:T(8,128)S(1)} %get-tuple-element.50), channel_id=1, source_target_pairs={{0,6},{1,7},{2,4},{3,5},{4,2},{5,3},{6,0},{7,1},{8,14},{9,15},{10,... | collective-permute-start | bytes 98312 | tf_op jit(solution)/shard_map/ppermute | solution.py:203

commit v7 on v6

v7 whole, which is shorter than its diff:
```python
import functools

import jax
import jax.numpy as jnp
from jax import lax
from jax.experimental import pallas as pl
from jax.experimental.pallas import tpu as pltpu
from jax.sharding import PartitionSpec as P

epsilon = 1e-06
score_scale = 60.0
cauchy_scale = 4.0
f32 = jnp.float32
bf16 = jnp.bfloat16
i32 = jnp.int32
BLOCK = 256


def iota(shape, dim):
    return lax.broadcasted_iota(i32, shape, dim)


def hot(mask):
    return jnp.where(mask, 1.0, 0.0).astype(bf16)


def dot(a, b, a_dim=1, b_dim=0):
    return lax.dot_general(a, b, (((a_dim,), (b_dim,)), ((), ())), preferred_element_type=f32)


def halves(value):
    return (value >> 8).astype(f32), (value & 255).astype(f32)


def position():
    return lax.axis_index("batch") * lax.axis_size("item") + lax.axis_index("item")


def log2(value):
    return value.bit_length() - 1


def unit_kernel(users_ref, unit_ref):
    width = users_ref.shape[1]
    users = users_ref[...].astype(f32)
    mean = jnp.mean(users * users, axis=1, keepdims=True)
    unit_ref[...] = (users * lax.rsqrt(mean + epsilon) * (1.0 / width**0.5)).astype(bf16)


def request_kernel(named_ref, request_ref):
    devices, lanes = request_ref.shape
    slots = lanes // 3
    n = named_ref.shape[1]
    owner, row = named_ref[0:1], named_ref[1:2]
    named = owner == iota((devices, n), 0)
    count = dot(hot(named), hot(iota((n, n), 0) <= iota((n, n), 1)))
    rank = jnp.sum(jnp.where(named, count, 0.0), axis=0, keepdims=True).astype(i32) - 1
    in_slot = hot(rank == iota((slots, n), 0))
    partner = (owner ^ 1) == iota((devices, n), 0)
    which = iota((1, n), 1)
    for k, (mask, value) in enumerate([(named, row), (named, which), (partner, which)]):
        high, low = halves(value + 1)
        high = dot(jnp.where(mask, high, 0.0).astype(bf16), in_slot, 1, 1)
        low = dot(jnp.where(mask, low, 0.0).astype(bf16), in_slot, 1, 1)
        request_ref[:, k * slots : (k + 1) * slots] = (high * 256.0 + low).astype(i32) - 1


def asker_of(spot, part, n_batch, slots):
    n_item = lax.axis_size("item")
    batch = (spot >> log2(slots)) & (n_batch - 1)
    level = spot >> log2(slots * n_batch)
    return position() ^ (batch * n_item + level * 2 + part)


def slot_column(asked, n_batch, part):
    devices, slots = asked.shape
    total = devices * slots // 2
    pick = hot(asker_of(iota((total, devices), 0), part, n_batch, slots) == iota((total, devices), 1))
    high, low = halves(asked)
    value = dot(pick, high.astype(bf16)) * 256.0 + dot(pick, low.astype(bf16))
    mine = (iota((total, slots), 0) & (slots - 1)) == iota((total, slots), 1)
    return jnp.sum(jnp.where(mine, value, 0.0), axis=1, keepdims=True)


def slot_line(asked, n_batch):
    devices, slots = asked.shape
    total = devices * slots
    pick = hot((iota((slots, total), 1) & (slots - 1)) == iota((slots, total), 0))
    high, low = halves(asked)
    value = dot(high.astype(bf16), pick) * 256.0 + dot(low.astype(bf16), pick)
    spot = iota((devices, total), 1)
    part = spot >> log2(total // 2)
    mine = asker_of(spot & (total // 2 - 1), part, n_batch, slots) == iota((devices, total), 0)
    return jnp.sum(jnp.where(mine, value, 0.0), axis=0, keepdims=True)


def parts_of(value):
    return value >> 8, value & 255


def fetch_kernel(n_batch, part, asked_ref, table_ref, found_ref):
    slots = asked_ref.shape[1] // 3
    block, low = parts_of(slot_column(asked_ref[:, :slots], n_batch, part).astype(i32))
    total = block.shape[0]
    low_hot = hot(low == iota((total, BLOCK), 1))
    block = jnp.broadcast_to(block.astype(f32), (total, BLOCK)).astype(bf16)
    picks = [
        jnp.where(block == jnp.bfloat16(k), low_hot, jnp.bfloat16(0)) for k in range(table_ref.shape[0] // BLOCK)
    ]
    found_ref[...] = dot(jnp.concatenate(picks, axis=1), table_ref[...]).astype(bf16)


def prepare_kernel(n_batch, n, asked_ref, own_ref, partner_ref, low_hot_ref, block_ref):
    slots = asked_ref.shape[1] // 3
    total = own_ref.shape[0]
    batch = (iota((total, 1), 0) >> log2(slots)) & (n_batch - 1)
    for k, ref in enumerate([own_ref, partner_ref], 1):
        which = slot_column(asked_ref[:, k * slots : (k + 1) * slots], n_batch, 0).astype(i32)
        ref[...] = jnp.where(which < 0, -1, batch * n + which)
    block, low = parts_of(slot_line(asked_ref[:, :slots], n_batch).astype(i32))
    low_hot_ref[...] = hot(low == iota(low_hot_ref.shape, 0))
    block_ref[...] = jnp.broadcast_to(block.astype(f32), block_ref.shape).astype(bf16)


def main_kernel(first, n_batch, weight_ref, *refs):
    fetched, places, (*units, out_a, out_b) = refs[:2], refs[2:4], refs[4:]
    width = weight_ref.shape[0]
    groups = len(units) // n_batch
    size = out_a.shape[0] // groups
    n = units[0].shape[0]
    root = 1.0 / width**0.5
    for group in range(groups):
        here = pl.ds((first + group) * size, size)
        embed = jnp.concatenate([ref[here] for ref in fetched], axis=0)
        place = jnp.concatenate([ref[here] for ref in places], axis=0)
        hidden = dot(embed, weight_ref[...])
        rscale = lax.rsqrt(jnp.mean(hidden * hidden, axis=1, keepdims=True) + epsilon)
        item_vec = (hidden * (rscale * root)).astype(bf16)
        sums, both = 0.0, 0.0
        for k in range(n_batch):
            unit = units[group * n_batch + k][...]
            expo = jnp.exp(dot(item_vec, unit, 1, 1) * score_scale)
            sums += jnp.sum(expo, axis=1, keepdims=True)
            mine = hot(place - k * n == iota((2 * size, n), 1))
            both += dot(jnp.concatenate([expo.astype(bf16), mine], axis=0), unit)
        mixed, own = both[: 2 * size], both[2 * size :]
        positive = jnp.sum(item_vec.astype(f32) * own, axis=1, keepdims=True) * score_scale
        xent = jnp.log(sums) - positive
        cweight = 1.0 / (1.0 + xent * (1.0 / cauchy_scale))
        dvec = (cweight * score_scale) * (mixed * (1.0 / sums) - own)
        inner = jnp.sum(hidden * dvec, axis=1, keepdims=True)
        dhidden = (rscale * root * (dvec - hidden * (rscale * rscale * inner * (1.0 / width)))).astype(bf16)
        out_a[pl.ds(group * size, size)] = dhidden[:size]
        out_b[pl.ds(group * size, size)] = dhidden[size:]


def cut(blocks, bits, refs):
    size = refs[0].shape[0]
    mine = sum(((lax.axis_index(axis) >> level) & 1) << k for k, (axis, level) in enumerate(reversed(bits)))
    for step, ref in enumerate(refs):
        ref[...] = blocks[pl.ds((mine ^ step) * size, size)].astype(ref.dtype)


def share_kernel(order, bits, count, *refs):
    fetched, dhidden, (*refs, blocks) = refs[:2], refs[2:count], refs[count:]
    half = len(dhidden) // 2
    share = 0.0
    for k, ref in enumerate(fetched):
        share += dot(ref[...], jnp.concatenate([d[...] for d in dhidden[k * half : (k + 1) * half]], axis=0), 0, 0)
    size = blocks.shape[1]
    for spot, block in enumerate(order):
        blocks[spot] = share[block * size : (block + 1) * size]
    cut(blocks, bits, refs)


def sum_of(refs):
    return sum(ref[...].astype(f32) for ref in refs)


def stage_kernel(bits, count, *refs):
    came, (*refs, blocks) = refs[:count], refs[count:]
    blocks[...] = sum_of(came)
    cut(blocks, bits, refs)


def last_kernel(*refs):
    *came, total_ref = refs
    total_ref[...] = sum_of(came)[0]


def table_kernel(low_hot_ref, block_ref, weight_ref, *refs):
    *incoming, table_grad_hbm, ready, sems = refs
    drow = jnp.concatenate([dot(ref[...], weight_ref[...], 1, 1).astype(bf16) for ref in incoming], axis=0)
    groups = sems.shape[0]
    size = ready.shape[0] // groups
    copies = []
    for g in range(groups):
        here = pl.ds(g * size, size)
        picks = [
            jnp.where(block_ref[...] == jnp.bfloat16(k), low_hot_ref[...], jnp.bfloat16(0))
            for k in range(g * size // BLOCK, (g + 1) * size // BLOCK)
        ]
        ready[here] = dot(jnp.concatenate(picks, axis=0), drow).astype(bf16)
        copy = pltpu.make_async_copy(ready.at[here], table_grad_hbm.at[here], sems.at[g])
        copy.start()
        copies.append(copy)
    for copy in copies:
        copy.wait()


def params(mib):
    return pltpu.CompilerParams(vmem_limit_bytes=mib * 1024 * 1024)


def cost(flops, bytes_accessed=1 << 20):
    return pl.CostEstimate(flops=flops, bytes_accessed=bytes_accessed, transcendentals=0)


def call(kernel, outs, *args, flops=0, scratch=(), mib=16):
    return pl.pallas_call(
        kernel,
        out_shape=[jax.ShapeDtypeStruct(shape, dtype) for shape, dtype in outs],
        scratch_shapes=scratch,
        compiler_params=params(mib),
        cost_estimate=cost(flops),
    )(*args)


def swap(value, mask):
    devices = lax.axis_size("batch") * lax.axis_size("item")
    return lax.ppermute(value, ("batch", "item"), [(k, k ^ mask) for k in range(devices)])


def bits_of(axis):
    return [(axis, level) for level in range(log2(lax.axis_size(axis)))]


def mask_of(bits):
    return sum((lax.axis_size("item") if axis == "batch" else 1) << level for axis, level in bits)


def reduce_scatter(values, width):
    n_item, devices = lax.axis_size("item"), lax.axis_size("batch") * lax.axis_size("item")
    part = width // devices
    bits = bits_of("batch") + bits_of("item")
    order = []
    for spot in range(devices):
        at = {"batch": 0, "item": 0}
        for k, (axis, level) in enumerate(bits):
            at[axis] |= (spot >> (len(bits) - 1 - k) & 1) << level
        order.append(at["batch"] * n_item + at["item"])
    odd = len(bits) % 2
    stages = [bits[:1]] * odd + [bits[k : k + 2] for k in range(odd, len(bits), 2)]
    left = devices
    for k, stage in enumerate(stages):
        whole, left = left, left >> len(stage)
        sent = f32 if k == len(stages) - 1 else bf16
        kernel = functools.partial(*((stage_kernel, stage) if k else (share_kernel, order, stage)), len(values))
        kept, *sends = call(
            kernel,
            [((left, part, width), f32)] + [((left, part, width), sent)] * ((1 << len(stage)) - 1),
            *values,
            scratch=[pltpu.VMEM((whole, part, width), f32)],
        )
        values = [kept]
        for step, value in enumerate(sends, 1):
            values.append(swap(value, mask_of([bit for j, bit in enumerate(reversed(stage)) if step >> j & 1])))
    return values


def local(user_vectors, item_table, tower_weight, item_owner, item_row):
    n, width = user_vectors.shape
    rows = item_table.shape[0]
    n_batch, n_item = lax.axis_size("batch"), lax.axis_size("item")
    devices = n_batch * n_item
    levels = n_item // 2
    slots = 2 * n // devices
    total = devices * slots
    half = total // 2
    groups = rows // min(512, rows)

    (unit,) = call(unit_kernel, [((n, width), bf16)], user_vectors)
    far = [batch * n_item for batch in range(2, n_batch, 2)]
    units = {0: unit}
    for mask in far + [2 << k for k in range(log2(levels))]:
        units[mask] = swap(unit, mask)

    (request,) = call(
        request_kernel,
        [((devices, 3 * slots), i32)],
        jnp.stack([item_owner.reshape(n), item_row]),
        flops=1 << 34,
    )
    asked = lax.all_to_all(request, ("batch", "item"), split_axis=0, concat_axis=0, tiled=True)
    early = list(units)
    asked, *values = lax.optimization_barrier((asked, *units.values()))
    units = dict(zip(early, values))

    def fetch(part):
        kernel = functools.partial(fetch_kernel, n_batch, part)
        return call(kernel, [((half, width), bf16)], asked, item_table, flops=2 * half * rows * width)[0]

    fetched = [None, swap(fetch(1), 1)]
    fetched[0] = fetch(0)

    for level in range(1, levels):
        if 2 * level not in units:
            top = 1 << log2(level)
            units[2 * level] = swap(units[2 * (level - top)], 2 * top)
        for mask in far:
            units[mask + 2 * level] = swap(units[2 * level], mask)
    for mask in list(units):
        units[mask + n_item] = swap(units[mask], n_item)

    *places, low_hot, block = call(
        functools.partial(prepare_kernel, n_batch, n),
        [((half, 1), i32)] * 2 + [((BLOCK, total), bf16)] * 2,
        asked,
    )
    dhidden = [[], []]
    size = half // levels
    for first, count in [(0, levels - 1), (levels - 1, 1)]:
        outs = call(
            functools.partial(main_kernel, first, n_batch),
            [((count * size, width), bf16)] * 2,
            tower_weight,
            *fetched,
            *places,
            *[units[2 * level + batch * n_item] for level in range(first, first + count) for batch in range(n_batch)],
            flops=count << 29,
            mib=40,
        )
        for part, value in zip(dhidden, outs):
            part.append(value)
    incoming = dhidden[0] + [swap(value, 1) for value in dhidden[1]]
    terms = reduce_scatter([*fetched, *dhidden[0], *dhidden[1]], width)
    table_grad = pl.pallas_call(
        table_kernel,
        out_specs=pl.BlockSpec(memory_space=pl.ANY),
        out_shape=jax.ShapeDtypeStruct((rows, width), bf16),
        scratch_shapes=[pltpu.VMEM((rows, width), bf16), pltpu.SemaphoreType.DMA((groups,))],
        compiler_params=params(16),
        cost_estimate=cost(2 * total * rows * width, 2 * rows * width),
    )(low_hot, block, tower_weight, *incoming)
    table_grad, *terms = lax.optimization_barrier((table_grad, *terms))
    (weight_grad,) = call(last_kernel, [((width // devices, width), f32)], *terms)
    return (table_grad, weight_grad)


def solution(mesh):
    return jax.shard_map(
        local,
        mesh=mesh,
        in_specs=(
            P(("batch", "item"), None),
            P(("batch", "item"), None),
            P(),
            P(("batch", "item"), None),
            P(("batch", "item")),
        ),
        out_specs=(P(("batch", "item"), None), P(("batch", "item"), None)),
        check_vma=False,
    )
```

time: 66.3 us -> 73.8 us (1.11)
  starting transfers between devices: 17 us -> 24.6 us
  waiting for transfers between devices: 24 us -> 20.4 us
  Pallas kernels: 11.5 us -> 14.6 us
  local copies, waits for them, and re-layouts: 0.01 us -> 0.95 us
    all_to_all x2 -> x0, waiting for transfers between devices: 14.2 us -> none  [the longest x1 13.8 us: local(): exchange(found.reshape(devices, slots, width)).reshape(total, width)]
    ppermute x10 -> x25, starting transfers between devices: 11.8 us -> 24.6 us  [swap(): lax.ppermute(value, ('batch', 'item'), [(k, k ^ mask) for k in range(devi...]
    ppermute x10 -> x25, waiting for transfers between devices: 9.85 us -> 20.4 us  [swap(): lax.ppermute(value, ('batch', 'item'), [(k, k ^ mask) for k in range(devi...]
    all_to_all x2 -> x0, starting transfers between devices: 5.21 us -> none  [the longest x1 2.61 us: local(): exchange(found.reshape(devices, slots, width)).reshape(total, width)]
    pallas_call x8 -> x11, Pallas kernels: 7.89 us -> 10.7 us  [call(): pl.pallas_call(kernel, out_shape=[jax.ShapeDtypeStruct(shape, dtype) for...]
    unnamed x6, local copies, waits for them, and re-layouts: 0.01 us -> 0.95 us
  transfers between devices with their start and end apart: 12 -> 25, of which waited for: 9 -> 6; matrix products, arithmetic and copies ran while one was open for 1% -> 1% of each run, Pallas kernels for 8% -> 16%
where the time goes in v7:
time: 73.8 us; the launch traced here: 73.6 us
  starting transfers between devices  24.6 us (33%)
  waiting for transfers between devices  20.4 us (28%)
  Pallas kernels  14.6 us (20%)
  blocking collectives  11.6 us (16%)
  local copies, waits for them, and re-layouts  0.95 us (1%)
  between operations  0.8 us (1%)
    ppermute x25, starting transfers between devices, swap(): lax.ppermute(value, ('batch', 'item'), [(k, k ^ mask) for k in range(devi...  24.6 us
    ppermute x25, waiting for transfers between devices, swap(): lax.ppermute(value, ('batch', 'item'), [(k, k ^ mask) for k in range(devi...  20.4 us
    all_to_all x1, blocking collectives, local(): lax.all_to_all(request, ('batch', 'item'), split_axis=0, concat_axis=0, t...  11.6 us
    pallas_call x11, Pallas kernels, call(): pl.pallas_call(kernel, out_shape=[jax.ShapeDtypeStruct(shape, dtype) for...  10.7 us
    pallas_call x1, Pallas kernels, local(): pl.pallas_call(table_kernel, out_specs=pl.BlockSpec(memory_space=pl.ANY),...  3.86 us
  transfers between devices with their start and end apart: 25, of which 6 were waited for; matrix products, arithmetic and copies ran while one was open for 1% of the time, Pallas kernels for 16%

profile of v7, /device:TPU:0, one launch (start us, length us, event | category | flops | bytes accessed | tf_op | source)
XLA Modules:
  0.0 73.6 jit_solution(22631832021621456)
XLA Ops:
  0.6 0.9 %copy-done.2 = bf16[256,512]{1,0:T(8,128)(2,1)S(1)} copy-done((bf16[256,512]{1,0:T(8,128)(2,1)S(1)}, bf16[256,512]{1,0:T(8,128)(2,1)}, u32[]{:S(2)}) %copy-start.2) | copy-done | bytes 262168
  1.7 3.0 %collective-permute-start = (bf16[256,512]{1,0:T(8,128)(2,1)S(1)}, bf16[256,512]{1,0:T(8,128)(2,1)S(1)}, u32[]{:S(2)}, u32[]{:S(2)}) collective-permute-start(bf16[256,512]{1,0:T(8,128)(2,1)S(1)} %shard_map.69.refs_4_), channel_id=1, source_target_pairs={{0,16},{1,17},{2,18},{3,19},{4,20},{5,21},{6,22},{7,23},{8,24},{9,... | collective-permute-start | bytes 786440 | tf_op jit(solution)/shard_map/ppermute | solution.py:231
  4.7 1.6 %collective-permute-start.1 = (bf16[256,512]{1,0:T(8,128)(2,1)S(1)}, bf16[256,512]{1,0:T(8,128)(2,1)S(1)}, u32[]{:S(2)}, u32[]{:S(2)}) collective-permute-start(bf16[256,512]{1,0:T(8,128)(2,1)S(1)} %shard_map.69.refs_4_), channel_id=1, source_target_pairs={{0,2},{1,3},{2,0},{3,1},{4,6},{5,7},{6,4},{7,5},{8,10},{9,11},{10,... | collective-permute-start | bytes 786440 | tf_op jit(solution)/shard_map/ppermute | solution.py:231
  6.3 2.6 %collective-permute-start.2 = (bf16[256,512]{1,0:T(8,128)(2,1)S(1)}, bf16[256,512]{1,0:T(8,128)(2,1)S(1)}, u32[]{:S(2)}, u32[]{:S(2)}) collective-permute-start(bf16[256,512]{1,0:T(8,128)(2,1)S(1)} %shard_map.69.refs_4_), channel_id=1, source_target_pairs={{0,4},{1,5},{2,6},{3,7},{4,0},{5,1},{6,2},{7,3},{8,12},{9,13},{10,... | collective-permute-start | bytes 786440 | tf_op jit(solution)/shard_map/ppermute | solution.py:231
  8.9 0.7 pad_add_fusion.named_ref
  10.0 11.6 %all_to_all.12 = s32[32,1,48]{2,1,0:T(1,128)S(1)} all-to-all(s32[32,1,48]{2,1,0:T(1,128)S(1)} %bitcast.9), channel_id=1, replica_groups=mesh['batch'=4,'item'=8] {'batch','item'}, dimensions={0} | all-to-all | bytes 12288 | tf_op jit(solution)/shard_map/all_to_all | solution.py:294
  21.6 1.6 %collective-permute-start.12 = (bf16[256,512]{1,0:T(8,128)(2,1)S(1)}, bf16[256,512]{1,0:T(8,128)(2,1)S(1)}, u32[]{:S(2)}, u32[]{:S(2)}) collective-permute-start(bf16[256,512]{1,0:T(8,128)(2,1)S(1)} %collective-permute-done.1.refs_8_), channel_id=1, source_target_pairs={{0,4},{1,5},{2,6},{3,7},{4,0},{5,1},{6,2},{7,3},{8,12},{9,13},{10,... | collective-permute-start | bytes 786440 | tf_op jit(solution)/shard_map/ppermute | solution.py:231
  23.2 1.4 %shard_map.72 = bf16[256,512]{1,0:T(8,128)(2,1)S(1)} custom-call(s32[32,48]{1,0:T(8,128)S(1)} %bitcast.6, bf16[4096,512]{1,0:T(8,128)(2,1)S(1)} %copy-done), custom_call_target="tpu_custom_call" | custom-call | flops 1073741824 | bytes 1048576 | tf_op jit(solution)/shard_map/pallas_call | solution.py:220
  24.7 0.7 collective-permute-start.3
  25.4 1.5 %collective-permute-start.7 = (bf16[256,512]{1,0:T(8,128)(2,1)S(1)}, bf16[256,512]{1,0:T(8,128)(2,1)S(1)}, u32[]{:S(2)}, u32[]{:S(2)}) collective-permute-start(bf16[256,512]{1,0:T(8,128)(2,1)S(1)} %collective-permute-done.1.refs_8_), channel_id=1, source_target_pairs={{0,16},{1,17},{2,18},{3,19},{4,20},{5,21},{6,22},{7,23},{8,24},{9,... | collective-permute-start | bytes 786440 | tf_op jit(solution)/shard_map/ppermute | solution.py:231
  26.8 0.5 collective-permute-start.10
  27.4 8.9 %collective-permute-done.12.refs_4_ = bf16[256,512]{1,0:T(8,128)(2,1)S(1)} collective-permute-done((bf16[256,512]{1,0:T(8,128)(2,1)S(1)}, bf16[256,512]{1,0:T(8,128)(2,1)S(1)}, u32[]{:S(2)}, u32[]{:S(2)}) %collective-permute-start.12) | collective-permute-done | bytes 262176 | tf_op jit(solution)/shard_map/ppermute | solution.py:231
  36.8 1.4 %collective-permute-start.14 = (bf16[256,512]{1,0:T(8,128)(2,1)S(1)}, bf16[256,512]{1,0:T(8,128)(2,1)S(1)}, u32[]{:S(2)}, u32[]{:S(2)}) collective-permute-start(bf16[256,512]{1,0:T(8,128)(2,1)S(1)} %collective-permute-done.12.refs_4_), channel_id=1, source_target_pairs={{0,16},{1,17},{2,18},{3,19},{4,20},{5,21},{6,22},{7,23},{8,24},{9,... | collective-permute-start | bytes 786440 | tf_op jit(solution)/shard_map/ppermute | solution.py:231
  38.5 0.5 collective-permute-start.8
  39.5 5.6 %collective-permute-done.14.refs_6_ = bf16[256,512]{1,0:T(8,128)(2,1)S(1)} collective-permute-done((bf16[256,512]{1,0:T(8,128)(2,1)S(1)}, bf16[256,512]{1,0:T(8,128)(2,1)S(1)}, u32[]{:S(2)}, u32[]{:S(2)}) %collective-permute-start.14) | collective-permute-done | bytes 262176 | tf_op jit(solution)/shard_map/ppermute | solution.py:231
  45.5 1.4 %shard_map.71.refs_0_ = bf16[256,512]{1,0:T(8,128)(2,1)S(1)} custom-call(s32[32,48]{1,0:T(8,128)S(1)} %bitcast.8, bf16[4096,512]{1,0:T(8,128)(2,1)S(1)} %copy-done), custom_call_target="tpu_custom_call" | custom-call | flops 1073741824 | bytes 1048576 | tf_op jit(solution)/shard_map/pallas_call | solution.py:220
  47.0 4.0 %shard_map.73 = (bf16[192,512]{1,0:T(8,128)(2,1)S(1)}, bf16[192,512]{1,0:T(8,128)(2,1)S(1)}) custom-call(bf16[512,512]{1,0:T(8,128)(2,1)S(1)} %copy-done.1, bf16[256,512]{1,0:T(8,128)(2,1)S(1)} %shard_map.71.refs_0_, bf16[256,512]{1,0:T(8,128)(2,1)S(1)} %collective-permute-done.3.refs_1_, s32[256,1]{1,0:T(8,128)S(1)} %get-tuple-element.33.refs_2_, ...), custom_call_target="tpu_custom_call" | custom-call | flops 1610612736 | bytes 1048576 | tf_op jit(solution)/shard_map/pallas_call | solution.py:220
  51.0 1.5 %shard_map.74 = (bf16[64,512]{1,0:T(8,128)(2,1)S(1)}, bf16[64,512]{1,0:T(8,128)(2,1)S(1)}) custom-call(bf16[512,512]{1,0:T(8,128)(2,1)S(1)} %copy-done.1, bf16[256,512]{1,0:T(8,128)(2,1)S(1)} %shard_map.71.refs_0_, bf16[256,512]{1,0:T(8,128)(2,1)S(1)} %collective-permute-done.3.refs_1_, s32[256,1]{1,0:T(8,128)S(1)} %get-tuple-element.33.refs_2_, ...), custom_call_target="tpu_custom_call" | custom-call | flops 536870912 | bytes 1048576 | tf_op jit(solution)/shard_map/pallas_call | solution.py:220
  52.6 0.5 shard_map.76
  53.1 0.6 collective-permute-start.18
  53.7 0.6 collective-permute-start.16
  54.4 0.5 collective-permute-done.18.refs_1_
  55.0 0.9 %collective-permute-start.19 = (bf16[4,16,512]{2,1,0:T(8,128)(2,1)S(1)}, bf16[4,16,512]{2,1,0:T(8,128)(2,1)S(1)}, u32[]{:S(2)}, u32[]{:S(2)}) collective-permute-start(bf16[4,16,512]{2,1,0:T(8,128)(2,1)S(1)} %get-tuple-element.46), channel_id=1, source_target_pairs={{0,1},{1,0},{2,3},{3,2},{4,5},{5,4},{6,7},{7,6},{8,9},{9,8},{10,11... | collective-permute-start | bytes 196616 | tf_op jit(solution)/shard_map/ppermute | solution.py:231
  55.9 1.4 %collective-permute-start.20 = (bf16[4,16,512]{2,1,0:T(8,128)(2,1)S(1)}, bf16[4,16,512]{2,1,0:T(8,128)(2,1)S(1)}, u32[]{:S(2)}, u32[]{:S(2)}) collective-permute-start(bf16[4,16,512]{2,1,0:T(8,128)(2,1)S(1)} %get-tuple-element.47), channel_id=1, source_target_pairs={{0,16},{1,17},{2,18},{3,19},{4,20},{5,21},{6,22},{7,23},{8,24},{9,... | collective-permute-start | bytes 196616 | tf_op jit(solution)/shard_map/ppermute | solution.py:231
  57.3 1.2 %collective-permute-start.21 = (bf16[4,16,512]{2,1,0:T(8,128)(2,1)S(1)}, bf16[4,16,512]{2,1,0:T(8,128)(2,1)S(1)}, u32[]{:S(2)}, u32[]{:S(2)}) collective-permute-start(bf16[4,16,512]{2,1,0:T(8,128)(2,1)S(1)} %get-tuple-element.48), channel_id=1, source_target_pairs={{0,17},{1,16},{2,19},{3,18},{4,21},{5,20},{6,23},{7,22},{8,25},{9,... | collective-permute-start | bytes 196616 | tf_op jit(solution)/shard_map/ppermute | solution.py:231
  58.6 0.9 %collective-permute-start.17 = (bf16[64,512]{1,0:T(8,128)(2,1)S(1)}, bf16[64,512]{1,0:T(8,128)(2,1)S(1)}, u32[]{:S(2)}, u32[]{:S(2)}) collective-permute-start(bf16[64,512]{1,0:T(8,128)(2,1)S(1)} %get-tuple-element.42.refs_5_), channel_id=1, source_target_pairs={{0,1},{1,0},{2,3},{3,2},{4,5},{5,4},{6,7},{7,6},{8,9},{9,8},{10,11... | collective-permute-start | bytes 196616 | tf_op jit(solution)/shard_map/ppermute | solution.py:231
  59.4 4.7 %collective-permute-done.19.refs_1_ = bf16[4,16,512]{2,1,0:T(8,128)(2,1)S(1)} collective-permute-done((bf16[4,16,512]{2,1,0:T(8,128)(2,1)S(1)}, bf16[4,16,512]{2,1,0:T(8,128)(2,1)S(1)}, u32[]{:S(2)}, u32[]{:S(2)}) %collective-permute-start.19) | collective-permute-done | bytes 65568 | tf_op jit(solution)/shard_map/ppermute | solution.py:231
  64.2 0.7 collective-permute-start.22
  64.9 2.4 %collective-permute-start.23 = (f32[1,16,512]{2,1,0:T(8,128)S(1)}, f32[1,16,512]{2,1,0:T(8,128)S(1)}, u32[]{:S(2)}, u32[]{:S(2)}) collective-permute-start(f32[1,16,512]{2,1,0:T(8,128)S(1)} %get-tuple-element.51), channel_id=1, source_target_pairs={{0,2},{1,3},{2,0},{3,1},{4,6},{5,7},{6,4},{7,5},{8,10},{9,11},{10,... | collective-permute-start | bytes 98312 | tf_op jit(solution)/shard_map/ppermute | solution.py:231
  67.2 1.4 %collective-permute-start.24 = (f32[1,16,512]{2,1,0:T(8,128)S(1)}, f32[1,16,512]{2,1,0:T(8,128)S(1)}, u32[]{:S(2)}, u32[]{:S(2)}) collective-permute-start(f32[1,16,512]{2,1,0:T(8,128)S(1)} %get-tuple-element.52), channel_id=1, source_target_pairs={{0,6},{1,7},{2,4},{3,5},{4,2},{5,3},{6,0},{7,1},{8,14},{9,15},{10,... | collective-permute-start | bytes 98312 | tf_op jit(solution)/shard_map/ppermute | solution.py:231
  68.7 3.9 %shard_map.75 = bf16[4096,512]{1,0:T(8,128)(2,1)} custom-call(bf16[256,512]{1,0:T(8,128)(2,1)S(1)} %get-tuple-element.31.low_hot_ref, bf16[256,512]{1,0:T(8,128)(2,1)S(1)} %get-tuple-element.32.block_ref, bf16[512,512]{1,0:T(8,128)(2,1)S(1)} %copy-done.1, bf16[192,512]{1,0:T(8,128)(2,1)S(1)} %get-tuple-element.39.refs_0_.refs_2_, ...), custom_call_target="tpu_custom_call" | custom-call | flops 2147483648 | bytes 4194304 | tf_op jit(solution)/shard_map/pallas_call | solution.py:337
  72.9 0.6 shard_map.79
  (38 shorter events, 2.9 us)
Async XLA Ops:
  0.6 1.0 %copy-start.2 = (bf16[256,512]{1,0:T(8,128)(2,1)S(1)}, bf16[256,512]{1,0:T(8,128)(2,1)}, u32[]{:S(2)}) copy-start(bf16[256,512]{1,0:T(8,128)(2,1)} %users_ref.1) | copy-start | bytes 786436
  1.7 19.9 %collective-permute-start = (bf16[256,512]{1,0:T(8,128)(2,1)S(1)}, bf16[256,512]{1,0:T(8,128)(2,1)S(1)}, u32[]{:S(2)}, u32[]{:S(2)}) collective-permute-start(bf16[256,512]{1,0:T(8,128)(2,1)S(1)} %shard_map.69.refs_4_), channel_id=1, source_target_pairs={{0,16},{1,17},{2,18},{3,19},{4,20},{5,21},{6,22},{7,23},{8,24},{9,... | collective-permute-start | bytes 786440 | tf_op jit(solution)/shard_map/ppermute | solution.py:231
  4.7 16.9 %collective-permute-start.1 = (bf16[256,512]{1,0:T(8,128)(2,1)S(1)}, bf16[256,512]{1,0:T(8,128)(2,1)S(1)}, u32[]{:S(2)}, u32[]{:S(2)}) collective-permute-start(bf16[256,512]{1,0:T(8,128)(2,1)S(1)} %shard_map.69.refs_4_), channel_id=1, source_target_pairs={{0,2},{1,3},{2,0},{3,1},{4,6},{5,7},{6,4},{7,5},{8,10},{9,11},{10,... | collective-permute-start | bytes 786440 | tf_op jit(solution)/shard_map/ppermute | solution.py:231
  6.3 15.3 %collective-permute-start.2 = (bf16[256,512]{1,0:T(8,128)(2,1)S(1)}, bf16[256,512]{1,0:T(8,128)(2,1)S(1)}, u32[]{:S(2)}, u32[]{:S(2)}) collective-permute-start(bf16[256,512]{1,0:T(8,128)(2,1)S(1)} %shard_map.69.refs_4_), channel_id=1, source_target_pairs={{0,4},{1,5},{2,6},{3,7},{4,0},{5,1},{6,2},{7,3},{8,12},{9,13},{10,... | collective-permute-start | bytes 786440 | tf_op jit(solution)/shard_map/ppermute | solution.py:231
  9.6 13.6 %copy-start = (bf16[4096,512]{1,0:T(8,128)(2,1)S(1)}, bf16[4096,512]{1,0:T(8,128)(2,1)}, u32[]{:S(2)}) copy-start(bf16[4096,512]{1,0:T(8,128)(2,1)} %table_ref.3) | copy-start | bytes 12582916
  21.6 25.4 %copy-start.1 = (bf16[512,512]{1,0:T(8,128)(2,1)S(1)}, bf16[512,512]{1,0:T(8,128)(2,1)}, u32[]{:S(2)}) copy-start(bf16[512,512]{1,0:T(8,128)(2,1)} %weight_ref.5) | copy-start | bytes 1572868
  21.6 14.7 %collective-permute-start.12 = (bf16[256,512]{1,0:T(8,128)(2,1)S(1)}, bf16[256,512]{1,0:T(8,128)(2,1)S(1)}, u32[]{:S(2)}, u32[]{:S(2)}) collective-permute-start(bf16[256,512]{1,0:T(8,128)(2,1)S(1)} %collective-permute-done.1.refs_8_), channel_id=1, source_target_pairs={{0,4},{1,5},{2,6},{3,7},{4,0},{5,1},{6,2},{7,3},{8,12},{9,13},{10,... | collective-permute-start | bytes 786440 | tf_op jit(solution)/shard_map/ppermute | solution.py:231
  24.7 11.6 %collective-permute-start.3 = (bf16[256,512]{1,0:T(8,128)(2,1)S(1)}, bf16[256,512]{1,0:T(8,128)(2,1)S(1)}, u32[]{:S(2)}, u32[]{:S(2)}) collective-permute-start(bf16[256,512]{1,0:T(8,128)(2,1)S(1)} %shard_map.72), channel_id=1, source_target_pairs={{0,1},{1,0},{2,3},{3,2},{4,5},{5,4},{6,7},{7,6},{8,9},{9,8},{10,11... | collective-permute-start | bytes 786440 | tf_op jit(solution)/shard_map/ppermute | solution.py:231
  25.4 11.4 %collective-permute-start.7 = (bf16[256,512]{1,0:T(8,128)(2,1)S(1)}, bf16[256,512]{1,0:T(8,128)(2,1)S(1)}, u32[]{:S(2)}, u32[]{:S(2)}) collective-permute-start(bf16[256,512]{1,0:T(8,128)(2,1)S(1)} %collective-permute-done.1.refs_8_), channel_id=1, source_target_pairs={{0,16},{1,17},{2,18},{3,19},{4,20},{5,21},{6,22},{7,23},{8,24},{9,... | collective-permute-start | bytes 786440 | tf_op jit(solution)/shard_map/ppermute | solution.py:231
  26.8 11.6 %collective-permute-start.10 = (bf16[256,512]{1,0:T(8,128)(2,1)S(1)}, bf16[256,512]{1,0:T(8,128)(2,1)S(1)}, u32[]{:S(2)}, u32[]{:S(2)}) collective-permute-start(bf16[256,512]{1,0:T(8,128)(2,1)S(1)} %collective-permute-done.2.refs_12_), channel_id=1, source_target_pairs={{0,16},{1,17},{2,18},{3,19},{4,20},{5,21},{6,22},{7,23},{8,24},{9,... | collective-permute-start | bytes 786440 | tf_op jit(solution)/shard_map/ppermute | solution.py:231
  27.4 11.1 %collective-permute-start.6 = (bf16[256,512]{1,0:T(8,128)(2,1)S(1)}, bf16[256,512]{1,0:T(8,128)(2,1)S(1)}, u32[]{:S(2)}, u32[]{:S(2)}) collective-permute-start(bf16[256,512]{1,0:T(8,128)(2,1)S(1)} %collective-permute-done.1.refs_8_), channel_id=1, source_target_pairs={{0,8},{1,9},{2,10},{3,11},{4,12},{5,13},{6,14},{7,15},{8,0},{9,1},... | collective-permute-start | bytes 786440 | tf_op jit(solution)/shard_map/ppermute | solution.py:231
  36.3 2.7 %collective-permute-start.9 = (bf16[256,512]{1,0:T(8,128)(2,1)S(1)}, bf16[256,512]{1,0:T(8,128)(2,1)S(1)}, u32[]{:S(2)}, u32[]{:S(2)}) collective-permute-start(bf16[256,512]{1,0:T(8,128)(2,1)S(1)} %collective-permute-done.2.refs_12_), channel_id=1, source_target_pairs={{0,8},{1,9},{2,10},{3,11},{4,12},{5,13},{6,14},{7,15},{8,0},{9,1},... | collective-permute-start | bytes 786440 | tf_op jit(solution)/shard_map/ppermute | solution.py:231
  36.3 2.8 %collective-permute-start.4 = (bf16[256,512]{1,0:T(8,128)(2,1)S(1)}, bf16[256,512]{1,0:T(8,128)(2,1)S(1)}, u32[]{:S(2)}, u32[]{:S(2)}) collective-permute-start(bf16[256,512]{1,0:T(8,128)(2,1)S(1)} %shard_map.69.refs_4_), channel_id=1, source_target_pairs={{0,8},{1,9},{2,10},{3,11},{4,12},{5,13},{6,14},{7,15},{8,0},{9,1},... | collective-permute-start | bytes 786440 | tf_op jit(solution)/shard_map/ppermute | solution.py:231
  36.8 8.3 %collective-permute-start.14 = (bf16[256,512]{1,0:T(8,128)(2,1)S(1)}, bf16[256,512]{1,0:T(8,128)(2,1)S(1)}, u32[]{:S(2)}, u32[]{:S(2)}) collective-permute-start(bf16[256,512]{1,0:T(8,128)(2,1)S(1)} %collective-permute-done.12.refs_4_), channel_id=1, source_target_pairs={{0,16},{1,17},{2,18},{3,19},{4,20},{5,21},{6,22},{7,23},{8,24},{9,... | collective-permute-start | bytes 786440 | tf_op jit(solution)/shard_map/ppermute | solution.py:231
  38.5 8.5 %collective-permute-start.5 = (bf16[256,512]{1,0:T(8,128)(2,1)S(1)}, bf16[256,512]{1,0:T(8,128)(2,1)S(1)}, u32[]{:S(2)}, u32[]{:S(2)}) collective-permute-start(bf16[256,512]{1,0:T(8,128)(2,1)S(1)} %collective-permute-done.refs_6_), channel_id=1, source_target_pairs={{0,8},{1,9},{2,10},{3,11},{4,12},{5,13},{6,14},{7,15},{8,0},{9,1},... | collective-permute-start | bytes 786440 | tf_op jit(solution)/shard_map/ppermute | solution.py:231
  38.5 8.5 %collective-permute-start.8 = (bf16[256,512]{1,0:T(8,128)(2,1)S(1)}, bf16[256,512]{1,0:T(8,128)(2,1)S(1)}, u32[]{:S(2)}, u32[]{:S(2)}) collective-permute-start(bf16[256,512]{1,0:T(8,128)(2,1)S(1)} %collective-permute-done.7.refs_10_), channel_id=1, source_target_pairs={{0,8},{1,9},{2,10},{3,11},{4,12},{5,13},{6,14},{7,15},{8,0},{9,1},... | collective-permute-start | bytes 786440 | tf_op jit(solution)/shard_map/ppermute | solution.py:231
  39.0 8.0 %collective-permute-start.11 = (bf16[256,512]{1,0:T(8,128)(2,1)S(1)}, bf16[256,512]{1,0:T(8,128)(2,1)S(1)}, u32[]{:S(2)}, u32[]{:S(2)}) collective-permute-start(bf16[256,512]{1,0:T(8,128)(2,1)S(1)} %collective-permute-done.10.refs_14_), channel_id=1, source_target_pairs={{0,8},{1,9},{2,10},{3,11},{4,12},{5,13},{6,14},{7,15},{8,0},{9,1},... | collective-permute-start | bytes 786440 | tf_op jit(solution)/shard_map/ppermute | solution.py:231
  39.0 12.0 %collective-permute-start.13 = (bf16[256,512]{1,0:T(8,128)(2,1)S(1)}, bf16[256,512]{1,0:T(8,128)(2,1)S(1)}, u32[]{:S(2)}, u32[]{:S(2)}) collective-permute-start(bf16[256,512]{1,0:T(8,128)(2,1)S(1)} %collective-permute-done.12.refs_4_), channel_id=1, source_target_pairs={{0,8},{1,9},{2,10},{3,11},{4,12},{5,13},{6,14},{7,15},{8,0},{9,1},... | collective-permute-start | bytes 786440 | tf_op jit(solution)/shard_map/ppermute | solution.py:231
  45.1 6.0 %collective-permute-start.15 = (bf16[256,512]{1,0:T(8,128)(2,1)S(1)}, bf16[256,512]{1,0:T(8,128)(2,1)S(1)}, u32[]{:S(2)}, u32[]{:S(2)}) collective-permute-start(bf16[256,512]{1,0:T(8,128)(2,1)S(1)} %collective-permute-done.14.refs_6_), channel_id=1, source_target_pairs={{0,8},{1,9},{2,10},{3,11},{4,12},{5,13},{6,14},{7,15},{8,0},{9,1},... | collective-permute-start | bytes 786440 | tf_op jit(solution)/shard_map/ppermute | solution.py:231
  53.1 1.8 %collective-permute-start.18 = (bf16[16,16,512]{2,1,0:T(8,128)(2,1)S(1)}, bf16[16,16,512]{2,1,0:T(8,128)(2,1)S(1)}, u32[]{:S(2)}, u32[]{:S(2)}) collective-permute-start(bf16[16,16,512]{2,1,0:T(8,128)(2,1)S(1)} %get-tuple-element.44), channel_id=1, source_target_pairs={{0,8},{1,9},{2,10},{3,11},{4,12},{5,13},{6,14},{7,15},{8,0},{9,1},... | collective-permute-start | bytes 786440 | tf_op jit(solution)/shard_map/ppermute | solution.py:231
  53.7 14.9 %collective-permute-start.16 = (bf16[192,512]{1,0:T(8,128)(2,1)S(1)}, bf16[192,512]{1,0:T(8,128)(2,1)S(1)}, u32[]{:S(2)}, u32[]{:S(2)}) collective-permute-start(bf16[192,512]{1,0:T(8,128)(2,1)S(1)} %get-tuple-element.41.refs_4_), channel_id=1, source_target_pairs={{0,1},{1,0},{2,3},{3,2},{4,5},{5,4},{6,7},{7,6},{8,9},{9,8},{10,11... | collective-permute-start | bytes 589832 | tf_op jit(solution)/shard_map/ppermute | solution.py:231
  55.0 9.1 %collective-permute-start.19 = (bf16[4,16,512]{2,1,0:T(8,128)(2,1)S(1)}, bf16[4,16,512]{2,1,0:T(8,128)(2,1)S(1)}, u32[]{:S(2)}, u32[]{:S(2)}) collective-permute-start(bf16[4,16,512]{2,1,0:T(8,128)(2,1)S(1)} %get-tuple-element.46), channel_id=1, source_target_pairs={{0,1},{1,0},{2,3},{3,2},{4,5},{5,4},{6,7},{7,6},{8,9},{9,8},{10,11... | collective-permute-start | bytes 196616 | tf_op jit(solution)/shard_map/ppermute | solution.py:231
  55.9 8.2 %collective-permute-start.20 = (bf16[4,16,512]{2,1,0:T(8,128)(2,1)S(1)}, bf16[4,16,512]{2,1,0:T(8,128)(2,1)S(1)}, u32[]{:S(2)}, u32[]{:S(2)}) collective-permute-start(bf16[4,16,512]{2,1,0:T(8,128)(2,1)S(1)} %get-tuple-element.47), channel_id=1, source_target_pairs={{0,16},{1,17},{2,18},{3,19},{4,20},{5,21},{6,22},{7,23},{8,24},{9,... | collective-permute-start | bytes 196616 | tf_op jit(solution)/shard_map/ppermute | solution.py:231
  57.3 6.8 %collective-permute-start.21 = (bf16[4,16,512]{2,1,0:T(8,128)(2,1)S(1)}, bf16[4,16,512]{2,1,0:T(8,128)(2,1)S(1)}, u32[]{:S(2)}, u32[]{:S(2)}) collective-permute-start(bf16[4,16,512]{2,1,0:T(8,128)(2,1)S(1)} %get-tuple-element.48), channel_id=1, source_target_pairs={{0,17},{1,16},{2,19},{3,18},{4,21},{5,20},{6,23},{7,22},{8,25},{9,... | collective-permute-start | bytes 196616 | tf_op jit(solution)/shard_map/ppermute | solution.py:231
  58.6 10.1 %collective-permute-start.17 = (bf16[64,512]{1,0:T(8,128)(2,1)S(1)}, bf16[64,512]{1,0:T(8,128)(2,1)S(1)}, u32[]{:S(2)}, u32[]{:S(2)}) collective-permute-start(bf16[64,512]{1,0:T(8,128)(2,1)S(1)} %get-tuple-element.42.refs_5_), channel_id=1, source_target_pairs={{0,1},{1,0},{2,3},{3,2},{4,5},{5,4},{6,7},{7,6},{8,9},{9,8},{10,11... | collective-permute-start | bytes 196616 | tf_op jit(solution)/shard_map/ppermute | solution.py:231
  64.2 8.3 %collective-permute-start.22 = (f32[1,16,512]{2,1,0:T(8,128)S(1)}, f32[1,16,512]{2,1,0:T(8,128)S(1)}, u32[]{:S(2)}, u32[]{:S(2)}) collective-permute-start(f32[1,16,512]{2,1,0:T(8,128)S(1)} %get-tuple-element.50), channel_id=1, source_target_pairs={{0,4},{1,5},{2,6},{3,7},{4,0},{5,1},{6,2},{7,3},{8,12},{9,13},{10,... | collective-permute-start | bytes 98312 | tf_op jit(solution)/shard_map/ppermute | solution.py:231
  64.9 7.7 %collective-permute-start.23 = (f32[1,16,512]{2,1,0:T(8,128)S(1)}, f32[1,16,512]{2,1,0:T(8,128)S(1)}, u32[]{:S(2)}, u32[]{:S(2)}) collective-permute-start(f32[1,16,512]{2,1,0:T(8,128)S(1)} %get-tuple-element.51), channel_id=1, source_target_pairs={{0,2},{1,3},{2,0},{3,1},{4,6},{5,7},{6,4},{7,5},{8,10},{9,11},{10,... | collective-permute-start | bytes 98312 | tf_op jit(solution)/shard_map/ppermute | solution.py:231
  67.2 5.7 %collective-permute-start.24 = (f32[1,16,512]{2,1,0:T(8,128)S(1)}, f32[1,16,512]{2,1,0:T(8,128)S(1)}, u32[]{:S(2)}, u32[]{:S(2)}) collective-permute-start(f32[1,16,512]{2,1,0:T(8,128)S(1)} %get-tuple-element.52), channel_id=1, source_target_pairs={{0,6},{1,7},{2,4},{3,5},{4,2},{5,3},{6,0},{7,1},{8,14},{9,15},{10,... | collective-permute-start | bytes 98312 | tf_op jit(solution)/shard_map/ppermute | solution.py:231

commit v8 on v7

v8 whole, which is shorter than its diff:
```python
import functools

import jax
import jax.numpy as jnp
from jax import lax
from jax.experimental import pallas as pl
from jax.experimental.pallas import tpu as pltpu
from jax.sharding import PartitionSpec as P

epsilon = 1e-06
score_scale = 60.0
cauchy_scale = 4.0
f32 = jnp.float32
bf16 = jnp.bfloat16
i32 = jnp.int32
BLOCK = 256


def iota(shape, dim):
    return lax.broadcasted_iota(i32, shape, dim)


def hot(mask):
    return jnp.where(mask, 1.0, 0.0).astype(bf16)


def dot(a, b, a_dim=1, b_dim=0):
    return lax.dot_general(a, b, (((a_dim,), (b_dim,)), ((), ())), preferred_element_type=f32)


def halves(value):
    return (value >> 8).astype(f32), (value & 255).astype(f32)


def position():
    return lax.axis_index("batch") * lax.axis_size("item") + lax.axis_index("item")


def log2(value):
    return value.bit_length() - 1


def request_kernel(near, named_ref, request_ref):
    devices, lanes = request_ref.shape
    slots = lanes // (1 + near)
    n = named_ref.shape[1]
    owner, row = named_ref[0:1], named_ref[1:2]
    device = iota((devices, n), 0)
    named = owner == device
    count = dot(hot(named), hot(iota((n, n), 0) <= iota((n, n), 1)))
    rank = jnp.sum(jnp.where(named, count, 0.0), axis=0, keepdims=True).astype(i32) - 1
    in_slot = hot(rank == iota((slots, n), 0))
    which = iota((1, n), 1)
    for k, (value, mask) in enumerate([(row, 0)] + [(which, mask) for mask in range(near)]):
        high, low = halves(value + 1)
        here = (owner ^ mask) == device
        high = dot(jnp.where(here, high, 0.0).astype(bf16), in_slot, 1, 1)
        low = dot(jnp.where(here, low, 0.0).astype(bf16), in_slot, 1, 1)
        request_ref[:, k * slots : (k + 1) * slots] = (high * 256.0 + low).astype(i32) - 1


def asker_of(spot, part, near, n_batch, slots):
    batch = (spot >> log2(slots)) & (n_batch - 1)
    level = spot >> log2(slots * n_batch)
    return position() ^ (batch * lax.axis_size("item") + level * near + part)


def slot_column(asked, part, near, n_batch):
    devices, slots = asked.shape
    total = devices * slots // near
    asker = asker_of(iota((total, devices), 0), part, near, n_batch, slots)
    pick = hot(asker == iota((total, devices), 1))
    high, low = halves(asked)
    value = dot(pick, high.astype(bf16)) * 256.0 + dot(pick, low.astype(bf16))
    mine = (iota((total, slots), 0) & (slots - 1)) == iota((total, slots), 1)
    return jnp.sum(jnp.where(mine, value, 0.0), axis=1, keepdims=True)


def slot_line(asked, near, n_batch):
    devices, slots = asked.shape
    total = devices * slots
    pick = hot((iota((slots, total), 1) & (slots - 1)) == iota((slots, total), 0))
    high, low = halves(asked)
    value = dot(high.astype(bf16), pick) * 256.0 + dot(low.astype(bf16), pick)
    spot = iota((devices, total), 1)
    asker = asker_of(spot & (total // near - 1), spot >> log2(total // near), near, n_batch, slots)
    return jnp.sum(jnp.where(asker == iota((devices, total), 0), value, 0.0), axis=0, keepdims=True)


def parts_of(value):
    return value >> 8, value & 255


def fetch_kernel(parts, near, n_batch, asked_ref, table_ref, *found):
    slots = asked_ref.shape[1] // (1 + near)
    asked = asked_ref[:, :slots]
    column = jnp.concatenate([slot_column(asked, part, near, n_batch) for part in parts], axis=0)
    block, low = parts_of(column.astype(i32))
    total = block.shape[0]
    low_hot = hot(low == iota((total, BLOCK), 1))
    block = jnp.broadcast_to(block.astype(f32), (total, BLOCK)).astype(bf16)
    picks = [
        jnp.where(block == jnp.bfloat16(k), low_hot, jnp.bfloat16(0)) for k in range(table_ref.shape[0] // BLOCK)
    ]
    rows = dot(jnp.concatenate(picks, axis=1), table_ref[...]).astype(bf16)
    size = total // len(found)
    for k, ref in enumerate(found):
        ref[...] = rows[k * size : (k + 1) * size]


def prepare_kernel(near, n_batch, n, asked_ref, place_ref, low_hot_ref, block_ref):
    slots = asked_ref.shape[1] // (1 + near)
    size = place_ref.shape[0] // near
    batch = (iota((size, 1), 0) >> log2(slots)) & (n_batch - 1)
    for part in range(near):
        asked = asked_ref[:, (1 + part) * slots : (2 + part) * slots]
        which = slot_column(asked, 0, near, n_batch).astype(i32)
        place_ref[pl.ds(part * size, size)] = jnp.where(which < 0, -1, batch * n + which)
    block, low = parts_of(slot_line(asked_ref[:, :slots], near, n_batch).astype(i32))
    low_hot_ref[...] = hot(low == iota(low_hot_ref.shape, 0))
    block_ref[...] = jnp.broadcast_to(block.astype(f32), block_ref.shape).astype(bf16)


def users_kernel(level, near, place_ref, *refs):
    *users, unit_ref, own_ref = refs
    n, width = users[0].shape
    for k, ref in enumerate(users):
        value = ref[...].astype(f32)
        mean = jnp.mean(value * value, axis=1, keepdims=True)
        unit_ref[pl.ds(k * n, n)] = (value * lax.rsqrt(mean + epsilon) * (1.0 / width**0.5)).astype(bf16)
    step = place_ref.shape[0] // near
    size = own_ref.shape[0] // near
    place = jnp.concatenate([place_ref[pl.ds(k * step + level * size, size)] for k in range(near)], axis=0)
    own_ref[...] = dot(hot(place == iota((place.shape[0], unit_ref.shape[0]), 1)), unit_ref[...]).astype(bf16)


def main_kernel(levels, weight_ref, *refs):
    parts = (len(refs) - 2 * levels) // 2
    fetched, units, owns, outs = refs[:parts], refs[parts : parts + levels], refs[parts + levels : parts + 2 * levels], refs[-parts:]
    width = weight_ref.shape[0]
    size = outs[0].shape[0] // levels
    root = 1.0 / width**0.5
    for level in range(levels):
        here = pl.ds(level * size, size)
        embed = jnp.concatenate([ref[here] for ref in fetched], axis=0)
        hidden = dot(embed, weight_ref[...])
        rscale = lax.rsqrt(jnp.mean(hidden * hidden, axis=1, keepdims=True) + epsilon)
        item_vec = (hidden * (rscale * root)).astype(bf16)
        unit = units[level][...]
        expo = jnp.exp(dot(item_vec, unit, 1, 1) * score_scale)
        sums = jnp.sum(expo, axis=1, keepdims=True)
        mixed = dot(expo.astype(bf16), unit)
        own = owns[level][...].astype(f32)
        positive = jnp.sum(item_vec.astype(f32) * own, axis=1, keepdims=True) * score_scale
        xent = jnp.log(sums) - positive
        cweight = 1.0 / (1.0 + xent * (1.0 / cauchy_scale))
        dvec = (cweight * score_scale) * (mixed * (1.0 / sums) - own)
        inner = jnp.sum(hidden * dvec, axis=1, keepdims=True)
        dhidden = (rscale * root * (dvec - hidden * (rscale * rscale * inner * (1.0 / width)))).astype(bf16)
        for part, ref in enumerate(outs):
            ref[here] = dhidden[part * size : (part + 1) * size]


def cut(blocks, bits, refs):
    size = refs[0].shape[0]
    mine = sum(((lax.axis_index(axis) >> level) & 1) << k for k, (axis, level) in enumerate(reversed(bits)))
    for step, ref in enumerate(refs):
        ref[...] = blocks[pl.ds((mine ^ step) * size, size)].astype(ref.dtype)


def share_kernel(order, bits, count, *refs):
    values, (*refs, blocks) = refs[:count], refs[count:]
    embed, dhidden = (jnp.concatenate([ref[...] for ref in half], axis=0) for half in (values[: count // 2], values[count // 2 :]))
    share = dot(embed, dhidden, 0, 0)
    size = blocks.shape[1]
    for spot, block in enumerate(order):
        blocks[spot] = share[block * size : (block + 1) * size]
    cut(blocks, bits, refs)


def sum_of(refs):
    return sum(ref[...].astype(f32) for ref in refs)


def stage_kernel(bits, count, *refs):
    came, (*refs, blocks) = refs[:count], refs[count:]
    blocks[...] = sum_of(came)
    cut(blocks, bits, refs)


def last_kernel(*refs):
    *came, total_ref = refs
    total_ref[...] = sum_of(came)[0]


def table_kernel(low_hot_ref, block_ref, weight_ref, *refs):
    *incoming, table_grad_hbm, ready, sems = refs
    drow = jnp.concatenate([dot(ref[...], weight_ref[...], 1, 1).astype(bf16) for ref in incoming], axis=0)
    groups = sems.shape[0]
    size = ready.shape[0] // groups
    copies = []
    for g in range(groups):
        here = pl.ds(g * size, size)
        picks = [
            jnp.where(block_ref[...] == jnp.bfloat16(k), low_hot_ref[...], jnp.bfloat16(0))
            for k in range(g * size // BLOCK, (g + 1) * size // BLOCK)
        ]
        ready[here] = dot(jnp.concatenate(picks, axis=0), drow).astype(bf16)
        copy = pltpu.make_async_copy(ready.at[here], table_grad_hbm.at[here], sems.at[g])
        copy.start()
        copies.append(copy)
    for copy in copies:
        copy.wait()


def params(mib):
    return pltpu.CompilerParams(vmem_limit_bytes=mib * 1024 * 1024)


def cost(flops, bytes_accessed=1 << 20):
    return pl.CostEstimate(flops=flops, bytes_accessed=bytes_accessed, transcendentals=0)


def call(kernel, outs, *args, flops=0, scratch=(), mib=16):
    return pl.pallas_call(
        kernel,
        out_shape=[jax.ShapeDtypeStruct(shape, dtype) for shape, dtype in outs],
        scratch_shapes=scratch,
        compiler_params=params(mib),
        cost_estimate=cost(flops),
    )(*args)


def swap(value, mask):
    devices = lax.axis_size("batch") * lax.axis_size("item")
    return lax.ppermute(value, ("batch", "item"), [(k, k ^ mask) for k in range(devices)])


def bits_of(axis):
    return [(axis, level) for level in range(log2(lax.axis_size(axis)))]


def mask_of(bits):
    return sum((lax.axis_size("item") if axis == "batch" else 1) << level for axis, level in bits)


def reduce_scatter(values, width):
    n_item, devices = lax.axis_size("item"), lax.axis_size("batch") * lax.axis_size("item")
    part = width // devices
    bits = bits_of("batch") + bits_of("item")
    order = []
    for spot in range(devices):
        at = {"batch": 0, "item": 0}
        for k, (axis, level) in enumerate(bits):
            at[axis] |= (spot >> (len(bits) - 1 - k) & 1) << level
        order.append(at["batch"] * n_item + at["item"])
    odd = len(bits) % 2
    stages = [bits[:1]] * odd + [bits[k : k + 2] for k in range(odd, len(bits), 2)]
    left = devices
    for k, stage in enumerate(stages):
        whole, left = left, left >> len(stage)
        sent = f32 if k == len(stages) - 1 else bf16
        kernel = functools.partial(*((stage_kernel, stage) if k else (share_kernel, order, stage)), len(values))
        kept, *sends = call(
            kernel,
            [((left, part, width), f32)] + [((left, part, width), sent)] * ((1 << len(stage)) - 1),
            *values,
            scratch=[pltpu.VMEM((whole, part, width), f32)],
        )
        values = [kept]
        for step, value in enumerate(sends, 1):
            values.append(swap(value, mask_of([bit for j, bit in enumerate(reversed(stage)) if step >> j & 1])))
    return values


def local(user_vectors, item_table, tower_weight, item_owner, item_row):
    n, width = user_vectors.shape
    rows = item_table.shape[0]
    n_batch, n_item = lax.axis_size("batch"), lax.axis_size("item")
    devices = n_batch * n_item
    near = min(4, n_item)
    levels = n_item // near
    slots = 2 * n // devices
    total = devices * slots
    size = total // near
    groups = rows // min(512, rows)

    far = [batch * n_item for batch in range(2, n_batch, 2)]
    users = {0: user_vectors}
    for mask in [near << k for k in range(log2(levels))] + far:
        users[mask] = swap(user_vectors, mask)

    (request,) = call(
        functools.partial(request_kernel, near),
        [((devices, (1 + near) * slots), i32)],
        jnp.stack([item_owner.reshape(n), item_row]),
        flops=1 << 34,
    )
    asked = lax.all_to_all(request, ("batch", "item"), split_axis=0, concat_axis=0, tiled=True)
    early = list(users)
    asked, *values = lax.optimization_barrier((asked, *users.values()))
    users = dict(zip(early, values))

    for level in range(1, levels):
        if near * level not in users:
            top = 1 << log2(level)
            users[near * level] = swap(users[near * (level - top)], near * top)
        for mask in far:
            users[mask + near * level] = swap(users[near * level], mask)

    def fetch(parts):
        return call(
            functools.partial(fetch_kernel, parts, near, n_batch),
            [((size, width), bf16)] * len(parts),
            asked,
            item_table,
            flops=2 * size * len(parts) * rows * width,
        )

    others = list(range(1, near))
    fetched = [swap(value, part) for part, value in zip(others, fetch(others))]
    fetched = [*fetch([0]), *fetched]

    for mask in list(users):
        users[mask + n_item] = swap(users[mask], n_item)

    place, low_hot, block = call(
        functools.partial(prepare_kernel, near, n_batch, n),
        [((total, 1), i32)] + [((BLOCK, total), bf16)] * 2,
        asked,
    )
    units, owns = zip(
        *[
            call(
                functools.partial(users_kernel, level, near),
                [((n_batch * n, width), bf16), ((total // levels, width), bf16)],
                place,
                *[users[near * level + batch * n_item] for batch in range(n_batch)],
                flops=1 << 29,
            )
            for level in range(levels)
        ]
    )
    dhidden = call(
        functools.partial(main_kernel, levels),
        [((size, width), bf16)] * near,
        tower_weight,
        *fetched,
        *units,
        *owns,
        flops=1 << 31,
        mib=40,
    )
    incoming = [dhidden[0]] + [swap(dhidden[part], part) for part in others]
    terms = reduce_scatter([*fetched, *dhidden], width)
    table_grad = pl.pallas_call(
        table_kernel,
        out_specs=pl.BlockSpec(memory_space=pl.ANY),
        out_shape=jax.ShapeDtypeStruct((rows, width), bf16),
        scratch_shapes=[pltpu.VMEM((rows, width), bf16), pltpu.SemaphoreType.DMA((groups,))],
        compiler_params=params(16),
        cost_estimate=cost(2 * total * rows * width, 2 * rows * width),
    )(low_hot, block, tower_weight, *incoming)
    table_grad, *terms = lax.optimization_barrier((table_grad, *terms))
    (weight_grad,) = call(last_kernel, [((width // devices, width), f32)], *terms)
    return (table_grad, weight_grad)


def solution(mesh):
    return jax.shard_map(
        local,
        mesh=mesh,
        in_specs=(
            P(("batch", "item"), None),
            P(("batch", "item"), None),
            P(),
            P(("batch", "item"), None),
            P(("batch", "item")),
        ),
        out_specs=(P(("batch", "item"), None), P(("batch", "item"), None)),
        check_vma=False,
    )
```

time: 73.8 us -> 65.6 us (0.89)
  starting transfers between devices: 24.6 us -> 21.8 us
  waiting for transfers between devices: 20.4 us -> 17.6 us
  Pallas kernels: 14.6 us -> 12.7 us
  local copies, waits for them, and re-layouts: 0.95 us -> 0.01 us
    ppermute x25 -> x20, waiting for transfers between devices: 20.4 us -> 17.6 us  [swap(): lax.ppermute(value, ('batch', 'item'), [(k, k ^ mask) for k in range(devi...]
    ppermute x25 -> x20, starting transfers between devices: 24.6 us -> 21.8 us  [swap(): lax.ppermute(value, ('batch', 'item'), [(k, k ^ mask) for k in range(devi...]
    pallas_call x11, Pallas kernels: 10.7 us -> 8.87 us  [call(): pl.pallas_call(kernel, out_shape=[jax.ShapeDtypeStruct(shape, dtype) for...]
    unnamed x6, local copies, waits for them, and re-layouts: 0.95 us -> 0.01 us
  transfers between devices with their start and end apart: 25 -> 20, of which waited for: 6 -> 7; matrix products, arithmetic and copies ran while one was open for 1% -> 1% of each run, Pallas kernels for 16% -> 14%
where the time goes in v8:
time: 65.6 us; the launch traced here: 65.4 us
  starting transfers between devices  21.8 us (33%)
  waiting for transfers between devices  17.6 us (27%)
  Pallas kernels  12.7 us (19%)
  blocking collectives  11.7 us (18%)
  between operations  0.78 us (1%)
  other arithmetic  0.7 us (1%)
    ppermute x20, starting transfers between devices, swap(): lax.ppermute(value, ('batch', 'item'), [(k, k ^ mask) for k in range(devi...  21.8 us
    ppermute x20, waiting for transfers between devices, swap(): lax.ppermute(value, ('batch', 'item'), [(k, k ^ mask) for k in range(devi...  17.6 us
    all_to_all x1, blocking collectives, local(): lax.all_to_all(request, ('batch', 'item'), split_axis=0, concat_axis=0, t...  11.7 us
    pallas_call x11, Pallas kernels, call(): pl.pallas_call(kernel, out_shape=[jax.ShapeDtypeStruct(shape, dtype) for...  8.87 us
    pallas_call x1, Pallas kernels, local(): pl.pallas_call(table_kernel, out_specs=pl.BlockSpec(memory_space=pl.ANY),...  3.87 us
  transfers between devices with their start and end apart: 20, of which 7 were waited for; matrix products, arithmetic and copies ran while one was open for 1% of the time, Pallas kernels for 14%

profile of v8, /device:TPU:0, one launch (start us, length us, event | category | flops | bytes accessed | tf_op | source)
XLA Modules:
  0.0 65.4 jit_solution(11530201263894959032)
XLA Ops:
  0.6 4.1 %collective-permute-start = (bf16[256,512]{1,0:T(8,128)(2,1)}, bf16[256,512]{1,0:T(8,128)(2,1)S(1)}, u32[]{:S(2)}, u32[]{:S(2)}) collective-permute-start(bf16[256,512]{1,0:T(8,128)(2,1)} %refs_0_), channel_id=1, source_target_pairs={{0,4},{1,5},{2,6},{3,7},{4,0},{5,1},{6,2},{7,3},{8,12},{9,13},{10,... | collective-permute-start | bytes 786440 | tf_op jit(solution)/shard_map/ppermute | solution.py:236
  4.7 1.5 %collective-permute-start.1 = (bf16[256,512]{1,0:T(8,128)(2,1)}, bf16[256,512]{1,0:T(8,128)(2,1)S(1)}, u32[]{:S(2)}, u32[]{:S(2)}) collective-permute-start(bf16[256,512]{1,0:T(8,128)(2,1)} %refs_0_), channel_id=1, source_target_pairs={{0,16},{1,17},{2,18},{3,19},{4,20},{5,21},{6,22},{7,23},{8,24},{9,... | collective-permute-start | bytes 786440 | tf_op jit(solution)/shard_map/ppermute | solution.py:236
  6.2 0.7 %pad_add_fusion.named_ref = s32[2,256]{1,0:T(2,128)S(1)} fusion(s32[1,256]{1,0:T(1,128)} %bitcast.10, s32[1,256]{1,0:T(1,128)} %bitcast.11), kind=kLoop, calls=%fused_computation | loop fusion | flops 512 | bytes 4096 | tf_op jit(solution)/shard_map/stack | solution.py:296
  7.4 11.7 %all_to_all.12 = s32[32,1,80]{2,1,0:T(1,128)S(1)} all-to-all(s32[32,1,80]{2,1,0:T(1,128)S(1)} %bitcast.9), channel_id=1, replica_groups=mesh['batch'=4,'item'=8] {'batch','item'}, dimensions={0} | all-to-all | bytes 20480 | tf_op jit(solution)/shard_map/all_to_all | solution.py:299
  19.1 0.6 collective-permute-start.8
  19.7 0.5 collective-permute-start.6
  20.2 6.9 %collective-permute-done.8.refs_2_ = bf16[256,512]{1,0:T(8,128)(2,1)S(1)} collective-permute-done((bf16[256,512]{1,0:T(8,128)(2,1)S(1)}, bf16[256,512]{1,0:T(8,128)(2,1)S(1)}, u32[]{:S(2)}, u32[]{:S(2)}) %collective-permute-start.8) | collective-permute-done | bytes 262176 | tf_op jit(solution)/shard_map/ppermute | solution.py:236
  27.6 2.1 %shard_map.71 = (bf16[128,512]{1,0:T(8,128)(2,1)S(1)}, bf16[128,512]{1,0:T(8,128)(2,1)S(1)}, bf16[128,512]{1,0:T(8,128)(2,1)S(1)}) custom-call(s32[32,80]{1,0:T(8,128)S(1)} %bitcast.7, bf16[4096,512]{1,0:T(8,128)(2,1)S(1)} %copy-done), custom_call_target="tpu_custom_call" | custom-call | flops 1610612736 | bytes 1048576 | tf_op jit(solution)/shard_map/pallas_call | solution.py:225
  29.7 0.7 %collective-permute-start.2 = (bf16[128,512]{1,0:T(8,128)(2,1)S(1)}, bf16[128,512]{1,0:T(8,128)(2,1)S(1)}, u32[]{:S(2)}, u32[]{:S(2)}) collective-permute-start(bf16[128,512]{1,0:T(8,128)(2,1)S(1)} %get-tuple-element.38), channel_id=1, source_target_pairs={{0,1},{1,0},{2,3},{3,2},{4,5},{5,4},{6,7},{7,6},{8,9},{9,8},{10,11... | collective-permute-start | bytes 393224 | tf_op jit(solution)/shard_map/ppermute | solution.py:236
  30.4 0.5 collective-permute-start.3
  30.9 2.3 %collective-permute-start.4 = (bf16[128,512]{1,0:T(8,128)(2,1)S(1)}, bf16[128,512]{1,0:T(8,128)(2,1)S(1)}, u32[]{:S(2)}, u32[]{:S(2)}) collective-permute-start(bf16[128,512]{1,0:T(8,128)(2,1)S(1)} %get-tuple-element.40), channel_id=1, source_target_pairs={{0,3},{1,2},{2,1},{3,0},{4,7},{5,6},{6,5},{7,4},{8,11},{9,10},{10,... | collective-permute-start | bytes 393224 | tf_op jit(solution)/shard_map/ppermute | solution.py:236
  33.3 0.9 %shard_map.70.refs_0_ = bf16[128,512]{1,0:T(8,128)(2,1)S(1)} custom-call(s32[32,80]{1,0:T(8,128)S(1)} %bitcast.8, bf16[4096,512]{1,0:T(8,128)(2,1)S(1)} %copy-done), custom_call_target="tpu_custom_call" | custom-call | flops 536870912 | bytes 1048576 | tf_op jit(solution)/shard_map/pallas_call | solution.py:225
  34.2 0.7 %shard_map.72 = (bf16[1024,512]{1,0:T(8,128)(2,1)S(1)}, bf16[256,512]{1,0:T(8,128)(2,1)S(1)}) custom-call(s32[512,1]{1,0:T(8,128)S(1)} %get-tuple-element.41.place_ref, bf16[256,512]{1,0:T(8,128)(2,1)S(1)} %copy-done.2, bf16[256,512]{1,0:T(8,128)(2,1)S(1)} %collective-permute-done.5.refs_1_, bf16[256,512]{1,0:T(8,128)(2,1)S(1)} %collective-permute-done.1.refs_2_, ...), custom_call_target="tpu_custom_call" | custom-call | flops 536870912 | bytes 1048576 | tf_op jit(solution)/shard_map/pallas_call | solution.py:225
  34.9 0.7 %shard_map.73 = (bf16[1024,512]{1,0:T(8,128)(2,1)S(1)}, bf16[256,512]{1,0:T(8,128)(2,1)S(1)}) custom-call(s32[512,1]{1,0:T(8,128)S(1)} %get-tuple-element.41.place_ref, bf16[256,512]{1,0:T(8,128)(2,1)S(1)} %collective-permute-done.refs_0_, bf16[256,512]{1,0:T(8,128)(2,1)S(1)} %collective-permute-done.7.refs_1_, ...), custom_call_target="tpu_custom_call" | custom-call | flops 536870912 | bytes 1048576 | tf_op jit(solution)/shard_map/pallas_call | solution.py:225
  35.7 1.0 %collective-permute-done.3.refs_2_ = bf16[128,512]{1,0:T(8,128)(2,1)S(1)} collective-permute-done((bf16[128,512]{1,0:T(8,128)(2,1)S(1)}, bf16[128,512]{1,0:T(8,128)(2,1)S(1)}, u32[]{:S(2)}, u32[]{:S(2)}) %collective-permute-start.3) | collective-permute-done | bytes 131104 | tf_op jit(solution)/shard_map/ppermute | solution.py:236
  36.7 3.0 %collective-permute-done.4.refs_3_ = bf16[128,512]{1,0:T(8,128)(2,1)S(1)} collective-permute-done((bf16[128,512]{1,0:T(8,128)(2,1)S(1)}, bf16[128,512]{1,0:T(8,128)(2,1)S(1)}, u32[]{:S(2)}, u32[]{:S(2)}) %collective-permute-start.4) | collective-permute-done | bytes 131104 | tf_op jit(solution)/shard_map/ppermute | solution.py:236
  39.7 2.3 %shard_map.74 = (bf16[128,512]{1,0:T(8,128)(2,1)S(1)}, bf16[128,512]{1,0:T(8,128)(2,1)S(1)}, bf16[128,512]{1,0:T(8,128)(2,1)S(1)}, bf16[128,512]{1,0:T(8,128)(2,1)S(1)}) custom-call(bf16[512,512]{1,0:T(8,128)(2,1)S(1)} %copy-done.1, bf16[128,512]{1,0:T(8,128)(2,1)S(1)} %shard_map.70.refs_0_, bf16[128,512]{1,0:T(8,128)(2,1)S(1)} %collective-permute-done.2.refs_1_, ...), custom_call_target="tpu_custom_call" | custom-call | flops 2147483648 | bytes 1048576 | tf_op jit(solution)/shard_map/pallas_call | solution.py:225
  42.0 0.5 shard_map.76
  42.6 1.5 %collective-permute-done.13.refs_1_ = bf16[16,16,512]{2,1,0:T(8,128)(2,1)S(1)} collective-permute-done((bf16[16,16,512]{2,1,0:T(8,128)(2,1)S(1)}, bf16[16,16,512]{2,1,0:T(8,128)(2,1)S(1)}, u32[]{:S(2)}, u32[]{:S(2)}) %collective-permute-start.13) | collective-permute-done | bytes 262176 | tf_op jit(solution)/shard_map/ppermute | solution.py:236
  44.2 0.7 %collective-permute-start.14 = (bf16[4,16,512]{2,1,0:T(8,128)(2,1)S(1)}, bf16[4,16,512]{2,1,0:T(8,128)(2,1)S(1)}, u32[]{:S(2)}, u32[]{:S(2)}) collective-permute-start(bf16[4,16,512]{2,1,0:T(8,128)(2,1)S(1)} %get-tuple-element.56), channel_id=1, source_target_pairs={{0,1},{1,0},{2,3},{3,2},{4,5},{5,4},{6,7},{7,6},{8,9},{9,8},{10,11... | collective-permute-start | bytes 196616 | tf_op jit(solution)/shard_map/ppermute | solution.py:236
  44.9 1.4 %collective-permute-start.10 = (bf16[128,512]{1,0:T(8,128)(2,1)S(1)}, bf16[128,512]{1,0:T(8,128)(2,1)S(1)}, u32[]{:S(2)}, u32[]{:S(2)}) collective-permute-start(bf16[128,512]{1,0:T(8,128)(2,1)S(1)} %get-tuple-element.50.refs_5_), channel_id=1, source_target_pairs={{0,1},{1,0},{2,3},{3,2},{4,5},{5,4},{6,7},{7,6},{8,9},{9,8},{10,11... | collective-permute-start | bytes 393224 | tf_op jit(solution)/shard_map/ppermute | solution.py:236
  46.3 0.6 collective-permute-start.11
  46.9 1.4 %collective-permute-start.12 = (bf16[128,512]{1,0:T(8,128)(2,1)S(1)}, bf16[128,512]{1,0:T(8,128)(2,1)S(1)}, u32[]{:S(2)}, u32[]{:S(2)}) collective-permute-start(bf16[128,512]{1,0:T(8,128)(2,1)S(1)} %get-tuple-element.52.refs_7_), channel_id=1, source_target_pairs={{0,3},{1,2},{2,1},{3,0},{4,7},{5,6},{6,5},{7,4},{8,11},{9,10},{10,... | collective-permute-start | bytes 393224 | tf_op jit(solution)/shard_map/ppermute | solution.py:236
  48.3 0.8 %collective-permute-start.15 = (bf16[4,16,512]{2,1,0:T(8,128)(2,1)S(1)}, bf16[4,16,512]{2,1,0:T(8,128)(2,1)S(1)}, u32[]{:S(2)}, u32[]{:S(2)}) collective-permute-start(bf16[4,16,512]{2,1,0:T(8,128)(2,1)S(1)} %get-tuple-element.57), channel_id=1, source_target_pairs={{0,16},{1,17},{2,18},{3,19},{4,20},{5,21},{6,22},{7,23},{8,24},{9,... | collective-permute-start | bytes 196616 | tf_op jit(solution)/shard_map/ppermute | solution.py:236
  49.2 2.0 %collective-permute-start.16 = (bf16[4,16,512]{2,1,0:T(8,128)(2,1)S(1)}, bf16[4,16,512]{2,1,0:T(8,128)(2,1)S(1)}, u32[]{:S(2)}, u32[]{:S(2)}) collective-permute-start(bf16[4,16,512]{2,1,0:T(8,128)(2,1)S(1)} %get-tuple-element.58), channel_id=1, source_target_pairs={{0,17},{1,16},{2,19},{3,18},{4,21},{5,20},{6,23},{7,22},{8,25},{9,... | collective-permute-start | bytes 196616 | tf_op jit(solution)/shard_map/ppermute | solution.py:236
  51.2 1.4 %collective-permute-done.15.refs_2_ = bf16[4,16,512]{2,1,0:T(8,128)(2,1)S(1)} collective-permute-done((bf16[4,16,512]{2,1,0:T(8,128)(2,1)S(1)}, bf16[4,16,512]{2,1,0:T(8,128)(2,1)S(1)}, u32[]{:S(2)}, u32[]{:S(2)}) %collective-permute-start.15) | collective-permute-done | bytes 65568 | tf_op jit(solution)/shard_map/ppermute | solution.py:236
  52.6 2.3 %collective-permute-done.16.refs_3_ = bf16[4,16,512]{2,1,0:T(8,128)(2,1)S(1)} collective-permute-done((bf16[4,16,512]{2,1,0:T(8,128)(2,1)S(1)}, bf16[4,16,512]{2,1,0:T(8,128)(2,1)S(1)}, u32[]{:S(2)}, u32[]{:S(2)}) %collective-permute-start.16) | collective-permute-done | bytes 65568 | tf_op jit(solution)/shard_map/ppermute | solution.py:236
  55.0 2.8 %collective-permute-start.17 = (f32[1,16,512]{2,1,0:T(8,128)S(1)}, f32[1,16,512]{2,1,0:T(8,128)S(1)}, u32[]{:S(2)}, u32[]{:S(2)}) collective-permute-start(f32[1,16,512]{2,1,0:T(8,128)S(1)} %get-tuple-element.60), channel_id=1, source_target_pairs={{0,4},{1,5},{2,6},{3,7},{4,0},{5,1},{6,2},{7,3},{8,12},{9,13},{10,... | collective-permute-start | bytes 98312 | tf_op jit(solution)/shard_map/ppermute | solution.py:236
  57.8 1.2 %collective-permute-start.18 = (f32[1,16,512]{2,1,0:T(8,128)S(1)}, f32[1,16,512]{2,1,0:T(8,128)S(1)}, u32[]{:S(2)}, u32[]{:S(2)}) collective-permute-start(f32[1,16,512]{2,1,0:T(8,128)S(1)} %get-tuple-element.61), channel_id=1, source_target_pairs={{0,2},{1,3},{2,0},{3,1},{4,6},{5,7},{6,4},{7,5},{8,10},{9,11},{10,... | collective-permute-start | bytes 98312 | tf_op jit(solution)/shard_map/ppermute | solution.py:236
  59.4 3.9 %shard_map.75 = bf16[4096,512]{1,0:T(8,128)(2,1)} custom-call(bf16[256,512]{1,0:T(8,128)(2,1)S(1)} %get-tuple-element.36.low_hot_ref, bf16[256,512]{1,0:T(8,128)(2,1)S(1)} %get-tuple-element.37.block_ref, bf16[512,512]{1,0:T(8,128)(2,1)S(1)} %copy-done.1, bf16[128,512]{1,0:T(8,128)(2,1)S(1)} %get-tuple-element.49.refs_0_.refs_4_, ...), custom_call_target="tpu_custom_call" | custom-call | flops 2147483648 | bytes 4194304 | tf_op jit(solution)/shard_map/pallas_call | solution.py:356
  63.3 1.4 %collective-permute-done.19.refs_3_ = f32[1,16,512]{2,1,0:T(8,128)S(1)} collective-permute-done((f32[1,16,512]{2,1,0:T(8,128)S(1)}, f32[1,16,512]{2,1,0:T(8,128)S(1)}, u32[]{:S(2)}, u32[]{:S(2)}) %collective-permute-start.19) | collective-permute-done | bytes 32800 | tf_op jit(solution)/shard_map/ppermute | solution.py:236
  64.8 0.6 shard_map.79
  (28 shorter events, 1.5 us)
Async XLA Ops:
  0.6 18.4 %collective-permute-start = (bf16[256,512]{1,0:T(8,128)(2,1)}, bf16[256,512]{1,0:T(8,128)(2,1)S(1)}, u32[]{:S(2)}, u32[]{:S(2)}) collective-permute-start(bf16[256,512]{1,0:T(8,128)(2,1)} %refs_0_), channel_id=1, source_target_pairs={{0,4},{1,5},{2,6},{3,7},{4,0},{5,1},{6,2},{7,3},{8,12},{9,13},{10,... | collective-permute-start | bytes 786440 | tf_op jit(solution)/shard_map/ppermute | solution.py:236
  4.7 14.4 %collective-permute-start.1 = (bf16[256,512]{1,0:T(8,128)(2,1)}, bf16[256,512]{1,0:T(8,128)(2,1)S(1)}, u32[]{:S(2)}, u32[]{:S(2)}) collective-permute-start(bf16[256,512]{1,0:T(8,128)(2,1)} %refs_0_), channel_id=1, source_target_pairs={{0,16},{1,17},{2,18},{3,19},{4,20},{5,21},{6,22},{7,23},{8,24},{9,... | collective-permute-start | bytes 786440 | tf_op jit(solution)/shard_map/ppermute | solution.py:236
  6.9 12.7 %copy-start.2 = (bf16[256,512]{1,0:T(8,128)(2,1)S(1)}, bf16[256,512]{1,0:T(8,128)(2,1)}, u32[]{:S(2)}) copy-start(bf16[256,512]{1,0:T(8,128)(2,1)} %refs_0_) | copy-start | bytes 786436
  6.9 20.7 %copy-start = (bf16[4096,512]{1,0:T(8,128)(2,1)S(1)}, bf16[4096,512]{1,0:T(8,128)(2,1)}, u32[]{:S(2)}) copy-start(bf16[4096,512]{1,0:T(8,128)(2,1)} %table_ref.3) | copy-start | bytes 12582916
  19.1 8.0 %collective-permute-start.8 = (bf16[256,512]{1,0:T(8,128)(2,1)S(1)}, bf16[256,512]{1,0:T(8,128)(2,1)S(1)}, u32[]{:S(2)}, u32[]{:S(2)}) collective-permute-start(bf16[256,512]{1,0:T(8,128)(2,1)S(1)} %collective-permute-done.refs_0_), channel_id=1, source_target_pairs={{0,16},{1,17},{2,18},{3,19},{4,20},{5,21},{6,22},{7,23},{8,24},{9,... | collective-permute-start | bytes 786440 | tf_op jit(solution)/shard_map/ppermute | solution.py:236
  19.7 10.7 %collective-permute-start.5 = (bf16[256,512]{1,0:T(8,128)(2,1)S(1)}, bf16[256,512]{1,0:T(8,128)(2,1)S(1)}, u32[]{:S(2)}, u32[]{:S(2)}) collective-permute-start(bf16[256,512]{1,0:T(8,128)(2,1)S(1)} %copy-done.2), channel_id=1, source_target_pairs={{0,8},{1,9},{2,10},{3,11},{4,12},{5,13},{6,14},{7,15},{8,0},{9,1},... | collective-permute-start | bytes 786440 | tf_op jit(solution)/shard_map/ppermute | solution.py:236
  19.7 11.2 %collective-permute-start.6 = (bf16[256,512]{1,0:T(8,128)(2,1)S(1)}, bf16[256,512]{1,0:T(8,128)(2,1)S(1)}, u32[]{:S(2)}, u32[]{:S(2)}) collective-permute-start(bf16[256,512]{1,0:T(8,128)(2,1)S(1)} %collective-permute-done.1.refs_2_), channel_id=1, source_target_pairs={{0,8},{1,9},{2,10},{3,11},{4,12},{5,13},{6,14},{7,15},{8,0},{9,1},... | collective-permute-start | bytes 786440 | tf_op jit(solution)/shard_map/ppermute | solution.py:236
  20.2 14.7 %collective-permute-start.7 = (bf16[256,512]{1,0:T(8,128)(2,1)S(1)}, bf16[256,512]{1,0:T(8,128)(2,1)S(1)}, u32[]{:S(2)}, u32[]{:S(2)}) collective-permute-start(bf16[256,512]{1,0:T(8,128)(2,1)S(1)} %collective-permute-done.refs_0_), channel_id=1, source_target_pairs={{0,8},{1,9},{2,10},{3,11},{4,12},{5,13},{6,14},{7,15},{8,0},{9,1},... | collective-permute-start | bytes 786440 | tf_op jit(solution)/shard_map/ppermute | solution.py:236
  27.1 7.8 %collective-permute-start.9 = (bf16[256,512]{1,0:T(8,128)(2,1)S(1)}, bf16[256,512]{1,0:T(8,128)(2,1)S(1)}, u32[]{:S(2)}, u32[]{:S(2)}) collective-permute-start(bf16[256,512]{1,0:T(8,128)(2,1)S(1)} %collective-permute-done.8.refs_2_), channel_id=1, source_target_pairs={{0,8},{1,9},{2,10},{3,11},{4,12},{5,13},{6,14},{7,15},{8,0},{9,1},... | collective-permute-start | bytes 786440 | tf_op jit(solution)/shard_map/ppermute | solution.py:236
  29.7 10.0 %copy-start.1 = (bf16[512,512]{1,0:T(8,128)(2,1)S(1)}, bf16[512,512]{1,0:T(8,128)(2,1)}, u32[]{:S(2)}) copy-start(bf16[512,512]{1,0:T(8,128)(2,1)} %weight_ref.3) | copy-start | bytes 1572868
  29.7 6.0 %collective-permute-start.2 = (bf16[128,512]{1,0:T(8,128)(2,1)S(1)}, bf16[128,512]{1,0:T(8,128)(2,1)S(1)}, u32[]{:S(2)}, u32[]{:S(2)}) collective-permute-start(bf16[128,512]{1,0:T(8,128)(2,1)S(1)} %get-tuple-element.38), channel_id=1, source_target_pairs={{0,1},{1,0},{2,3},{3,2},{4,5},{5,4},{6,7},{7,6},{8,9},{9,8},{10,11... | collective-permute-start | bytes 393224 | tf_op jit(solution)/shard_map/ppermute | solution.py:236
  30.4 6.3 %collective-permute-start.3 = (bf16[128,512]{1,0:T(8,128)(2,1)S(1)}, bf16[128,512]{1,0:T(8,128)(2,1)S(1)}, u32[]{:S(2)}, u32[]{:S(2)}) collective-permute-start(bf16[128,512]{1,0:T(8,128)(2,1)S(1)} %get-tuple-element.39), channel_id=1, source_target_pairs={{0,2},{1,3},{2,0},{3,1},{4,6},{5,7},{6,4},{7,5},{8,10},{9,11},{10,... | collective-permute-start | bytes 393224 | tf_op jit(solution)/shard_map/ppermute | solution.py:236
  30.9 8.7 %collective-permute-start.4 = (bf16[128,512]{1,0:T(8,128)(2,1)S(1)}, bf16[128,512]{1,0:T(8,128)(2,1)S(1)}, u32[]{:S(2)}, u32[]{:S(2)}) collective-permute-start(bf16[128,512]{1,0:T(8,128)(2,1)S(1)} %get-tuple-element.40), channel_id=1, source_target_pairs={{0,3},{1,2},{2,1},{3,0},{4,7},{5,6},{6,5},{7,4},{8,11},{9,10},{10,... | collective-permute-start | bytes 393224 | tf_op jit(solution)/shard_map/ppermute | solution.py:236
  42.5 1.6 %collective-permute-start.13 = (bf16[16,16,512]{2,1,0:T(8,128)(2,1)S(1)}, bf16[16,16,512]{2,1,0:T(8,128)(2,1)S(1)}, u32[]{:S(2)}, u32[]{:S(2)}) collective-permute-start(bf16[16,16,512]{2,1,0:T(8,128)(2,1)S(1)} %get-tuple-element.54), channel_id=1, source_target_pairs={{0,8},{1,9},{2,10},{3,11},{4,12},{5,13},{6,14},{7,15},{8,0},{9,1},... | collective-permute-start | bytes 786440 | tf_op jit(solution)/shard_map/ppermute | solution.py:236
  44.2 5.0 %collective-permute-start.14 = (bf16[4,16,512]{2,1,0:T(8,128)(2,1)S(1)}, bf16[4,16,512]{2,1,0:T(8,128)(2,1)S(1)}, u32[]{:S(2)}, u32[]{:S(2)}) collective-permute-start(bf16[4,16,512]{2,1,0:T(8,128)(2,1)S(1)} %get-tuple-element.56), channel_id=1, source_target_pairs={{0,1},{1,0},{2,3},{3,2},{4,5},{5,4},{6,7},{7,6},{8,9},{9,8},{10,11... | collective-permute-start | bytes 196616 | tf_op jit(solution)/shard_map/ppermute | solution.py:236
  44.9 14.2 %collective-permute-start.10 = (bf16[128,512]{1,0:T(8,128)(2,1)S(1)}, bf16[128,512]{1,0:T(8,128)(2,1)S(1)}, u32[]{:S(2)}, u32[]{:S(2)}) collective-permute-start(bf16[128,512]{1,0:T(8,128)(2,1)S(1)} %get-tuple-element.50.refs_5_), channel_id=1, source_target_pairs={{0,1},{1,0},{2,3},{3,2},{4,5},{5,4},{6,7},{7,6},{8,9},{9,8},{10,11... | collective-permute-start | bytes 393224 | tf_op jit(solution)/shard_map/ppermute | solution.py:236
  46.3 13.1 %collective-permute-start.11 = (bf16[128,512]{1,0:T(8,128)(2,1)S(1)}, bf16[128,512]{1,0:T(8,128)(2,1)S(1)}, u32[]{:S(2)}, u32[]{:S(2)}) collective-permute-start(bf16[128,512]{1,0:T(8,128)(2,1)S(1)} %get-tuple-element.51.refs_6_), channel_id=1, source_target_pairs={{0,2},{1,3},{2,0},{3,1},{4,6},{5,7},{6,4},{7,5},{8,10},{9,11},{10,... | collective-permute-start | bytes 393224 | tf_op jit(solution)/shard_map/ppermute | solution.py:236
  46.9 12.5 %collective-permute-start.12 = (bf16[128,512]{1,0:T(8,128)(2,1)S(1)}, bf16[128,512]{1,0:T(8,128)(2,1)S(1)}, u32[]{:S(2)}, u32[]{:S(2)}) collective-permute-start(bf16[128,512]{1,0:T(8,128)(2,1)S(1)} %get-tuple-element.52.refs_7_), channel_id=1, source_target_pairs={{0,3},{1,2},{2,1},{3,0},{4,7},{5,6},{6,5},{7,4},{8,11},{9,10},{10,... | collective-permute-start | bytes 393224 | tf_op jit(solution)/shard_map/ppermute | solution.py:236
  48.3 4.3 %collective-permute-start.15 = (bf16[4,16,512]{2,1,0:T(8,128)(2,1)S(1)}, bf16[4,16,512]{2,1,0:T(8,128)(2,1)S(1)}, u32[]{:S(2)}, u32[]{:S(2)}) collective-permute-start(bf16[4,16,512]{2,1,0:T(8,128)(2,1)S(1)} %get-tuple-element.57), channel_id=1, source_target_pairs={{0,16},{1,17},{2,18},{3,19},{4,20},{5,21},{6,22},{7,23},{8,24},{9,... | collective-permute-start | bytes 196616 | tf_op jit(solution)/shard_map/ppermute | solution.py:236
  49.2 5.7 %collective-permute-start.16 = (bf16[4,16,512]{2,1,0:T(8,128)(2,1)S(1)}, bf16[4,16,512]{2,1,0:T(8,128)(2,1)S(1)}, u32[]{:S(2)}, u32[]{:S(2)}) collective-permute-start(bf16[4,16,512]{2,1,0:T(8,128)(2,1)S(1)} %get-tuple-element.58), channel_id=1, source_target_pairs={{0,17},{1,16},{2,19},{3,18},{4,21},{5,20},{6,23},{7,22},{8,25},{9,... | collective-permute-start | bytes 196616 | tf_op jit(solution)/shard_map/ppermute | solution.py:236
  55.0 8.3 %collective-permute-start.17 = (f32[1,16,512]{2,1,0:T(8,128)S(1)}, f32[1,16,512]{2,1,0:T(8,128)S(1)}, u32[]{:S(2)}, u32[]{:S(2)}) collective-permute-start(f32[1,16,512]{2,1,0:T(8,128)S(1)} %get-tuple-element.60), channel_id=1, source_target_pairs={{0,4},{1,5},{2,6},{3,7},{4,0},{5,1},{6,2},{7,3},{8,12},{9,13},{10,... | collective-permute-start | bytes 98312 | tf_op jit(solution)/shard_map/ppermute | solution.py:236
  57.8 5.5 %collective-permute-start.18 = (f32[1,16,512]{2,1,0:T(8,128)S(1)}, f32[1,16,512]{2,1,0:T(8,128)S(1)}, u32[]{:S(2)}, u32[]{:S(2)}) collective-permute-start(f32[1,16,512]{2,1,0:T(8,128)S(1)} %get-tuple-element.61), channel_id=1, source_target_pairs={{0,2},{1,3},{2,0},{3,1},{4,6},{5,7},{6,4},{7,5},{8,10},{9,11},{10,... | collective-permute-start | bytes 98312 | tf_op jit(solution)/shard_map/ppermute | solution.py:236
  59.1 5.7 %collective-permute-start.19 = (f32[1,16,512]{2,1,0:T(8,128)S(1)}, f32[1,16,512]{2,1,0:T(8,128)S(1)}, u32[]{:S(2)}, u32[]{:S(2)}) collective-permute-start(f32[1,16,512]{2,1,0:T(8,128)S(1)} %get-tuple-element.62), channel_id=1, source_target_pairs={{0,6},{1,7},{2,4},{3,5},{4,2},{5,3},{6,0},{7,1},{8,14},{9,15},{10,... | collective-permute-start | bytes 98312 | tf_op jit(solution)/shard_map/ppermute | solution.py:236

commit v9 on v8

--- a/solution.py
+++ b/solution.py
@@ -244,7 +244,7 @@
     return sum((lax.axis_size("item") if axis == "batch" else 1) << level for axis, level in bits)
 
 
-def reduce_scatter(values, width):
+def reduce_scatter(values, width, between):
     n_item, devices = lax.axis_size("item"), lax.axis_size("batch") * lax.axis_size("item")
     part = width // devices
     bits = bits_of("batch") + bits_of("item")
@@ -270,6 +270,8 @@
         values = [kept]
         for step, value in enumerate(sends, 1):
             values.append(swap(value, mask_of([bit for j, bit in enumerate(reversed(stage)) if step >> j & 1])))
+        if k == 1:
+            values[1] = between(values[1])
     return values
 
 
@@ -317,9 +319,15 @@
             flops=2 * size * len(parts) * rows * width,
         )
 
-    others = list(range(1, near))
-    fetched = [swap(value, part) for part, value in zip(others, fetch(others))]
-    fetched = [*fetch([0]), *fetched]
+    fetched = {}
+    for parts in [[near - 1], list(range(1, near - 1)), [0]]:
+        asked, *values = lax.optimization_barrier((asked, *fetch(parts)))
+        for part, value in zip(parts, values):
+            fetched[part] = swap(value, part) if part else value
+    late = [mask for mask in users if mask not in early]
+    fetched[0], *values = lax.optimization_barrier((fetched[0], *[users[mask] for mask in late]))
+    users.update(zip(late, values))
+    fetched = [fetched[part] for part in range(near)]
 
     for mask in list(users):
         users[mask + n_item] = swap(users[mask], n_item)
@@ -351,8 +359,14 @@
         flops=1 << 31,
         mib=40,
     )
-    incoming = [dhidden[0]] + [swap(dhidden[part], part) for part in others]
-    terms = reduce_scatter([*fetched, *dhidden], width)
+    incoming = [dhidden[0]]
+
+    def give_back(value):
+        value, *given = lax.optimization_barrier((value, *dhidden[1:]))
+        incoming.extend(swap(rows, part) for part, rows in enumerate(given, 1))
+        return value
+
+    terms = reduce_scatter([*fetched, *dhidden], width, give_back)
     table_grad = pl.pallas_call(
         table_kernel,
         out_specs=pl.BlockSpec(memory_space=pl.ANY),

time: 65.6 us -> 64.9 us (0.989)
  waiting for transfers between devices: 17.6 us -> 16.1 us
    ppermute x20, waiting for transfers between devices: 17.6 us -> 16.1 us  [swap(): lax.ppermute(value, ('batch', 'item'), [(k, k ^ mask) for k in range(devi...]
    pallas_call x11 -> x12, Pallas kernels: 8.87 us -> 9.24 us  [call(): pl.pallas_call(kernel, out_shape=[jax.ShapeDtypeStruct(shape, dtype) for...]
  transfers between devices with their start and end apart: 20 -> 20, of which waited for: 7 -> 8; matrix products, arithmetic and copies ran while one was open for 1% -> 1% of each run, Pallas kernels for 14% -> 15%
where the time goes in v9:
time: 64.9 us; the launch traced here: 64.7 us
  starting transfers between devices  22.3 us (34%)
  waiting for transfers between devices  16.1 us (25%)
  Pallas kernels  13.1 us (20%)
  blocking collectives  11.7 us (18%)
  between operations  0.79 us (1%)
  other arithmetic  0.7 us (1%)
    ppermute x20, starting transfers between devices, swap(): lax.ppermute(value, ('batch', 'item'), [(k, k ^ mask) for k in range(devi...  22.3 us
    ppermute x20, waiting for transfers between devices, swap(): lax.ppermute(value, ('batch', 'item'), [(k, k ^ mask) for k in range(devi...  16.1 us
    all_to_all x1, blocking collectives, local(): lax.all_to_all(request, ('batch', 'item'), split_axis=0, concat_axis=0, t...  11.7 us
    pallas_call x12, Pallas kernels, call(): pl.pallas_call(kernel, out_shape=[jax.ShapeDtypeStruct(shape, dtype) for...  9.24 us
    pallas_call x1, Pallas kernels, local(): pl.pallas_call(table_kernel, out_specs=pl.BlockSpec(memory_space=pl.ANY),...  3.87 us
  transfers between devices with their start and end apart: 20, of which 8 were waited for; matrix products, arithmetic and copies ran while one was open for 1% of the time, Pallas kernels for 15%

profile of v9, /device:TPU:0, one launch (start us, length us, event | category | flops | bytes accessed | tf_op | source)
XLA Modules:
  0.0 64.7 jit_solution(15913976884531656079)
XLA Ops:
  0.6 4.1 %collective-permute-start = (bf16[256,512]{1,0:T(8,128)(2,1)}, bf16[256,512]{1,0:T(8,128)(2,1)S(1)}, u32[]{:S(2)}, u32[]{:S(2)}) collective-permute-start(bf16[256,512]{1,0:T(8,128)(2,1)} %refs_0_), channel_id=1, source_target_pairs={{0,4},{1,5},{2,6},{3,7},{4,0},{5,1},{6,2},{7,3},{8,12},{9,13},{10,... | collective-permute-start | bytes 786440 | tf_op jit(solution)/shard_map/ppermute | solution.py:236
  4.7 1.5 %collective-permute-start.1 = (bf16[256,512]{1,0:T(8,128)(2,1)}, bf16[256,512]{1,0:T(8,128)(2,1)S(1)}, u32[]{:S(2)}, u32[]{:S(2)}) collective-permute-start(bf16[256,512]{1,0:T(8,128)(2,1)} %refs_0_), channel_id=1, source_target_pairs={{0,16},{1,17},{2,18},{3,19},{4,20},{5,21},{6,22},{7,23},{8,24},{9,... | collective-permute-start | bytes 786440 | tf_op jit(solution)/shard_map/ppermute | solution.py:236
  6.2 0.7 %pad_add_fusion.named_ref = s32[2,256]{1,0:T(2,128)S(1)} fusion(s32[1,256]{1,0:T(1,128)} %bitcast.11, s32[1,256]{1,0:T(1,128)} %bitcast.12), kind=kLoop, calls=%fused_computation | loop fusion | flops 512 | bytes 4096 | tf_op jit(solution)/shard_map/stack | solution.py:298
  7.4 11.7 %all_to_all.12 = s32[32,1,80]{2,1,0:T(1,128)S(1)} all-to-all(s32[32,1,80]{2,1,0:T(1,128)S(1)} %bitcast.10), channel_id=1, replica_groups=mesh['batch'=4,'item'=8] {'batch','item'}, dimensions={0} | all-to-all | bytes 20480 | tf_op jit(solution)/shard_map/all_to_all | solution.py:301
  19.1 0.6 collective-permute-start.2
  19.7 0.9 %shard_map.69 = bf16[128,512]{1,0:T(8,128)(2,1)S(1)} custom-call(s32[32,80]{1,0:T(8,128)S(1)} %bitcast.6, bf16[4096,512]{1,0:T(8,128)(2,1)S(1)} %copy-done), custom_call_target="tpu_custom_call" | custom-call | flops 536870912 | bytes 1048576 | tf_op jit(solution)/shard_map/pallas_call | solution.py:225
  21.3 1.6 %shard_map.70 = (bf16[128,512]{1,0:T(8,128)(2,1)S(1)}, bf16[128,512]{1,0:T(8,128)(2,1)S(1)}) custom-call(s32[32,80]{1,0:T(8,128)S(1)} %bitcast.7, bf16[4096,512]{1,0:T(8,128)(2,1)S(1)} %copy-done), custom_call_target="tpu_custom_call" | custom-call | flops 1073741824 | bytes 1048576 | tf_op jit(solution)/shard_map/pallas_call | solution.py:225
  22.8 0.9 %shard_map.71.refs_0_ = bf16[128,512]{1,0:T(8,128)(2,1)S(1)} custom-call(s32[32,80]{1,0:T(8,128)S(1)} %bitcast.8, bf16[4096,512]{1,0:T(8,128)(2,1)S(1)} %copy-done), custom_call_target="tpu_custom_call" | custom-call | flops 536870912 | bytes 1048576 | tf_op jit(solution)/shard_map/pallas_call | solution.py:225
  23.8 3.4 %collective-permute-done.2.refs_2_ = bf16[256,512]{1,0:T(8,128)(2,1)S(1)} collective-permute-done((bf16[256,512]{1,0:T(8,128)(2,1)S(1)}, bf16[256,512]{1,0:T(8,128)(2,1)S(1)}, u32[]{:S(2)}, u32[]{:S(2)}) %collective-permute-start.2) | collective-permute-done | bytes 262176 | tf_op jit(solution)/shard_map/ppermute | solution.py:236
  27.7 1.5 %collective-permute-start.3 = (bf16[128,512]{1,0:T(8,128)(2,1)S(1)}, bf16[128,512]{1,0:T(8,128)(2,1)S(1)}, u32[]{:S(2)}, u32[]{:S(2)}) collective-permute-start(bf16[128,512]{1,0:T(8,128)(2,1)S(1)} %get-tuple-element.58), channel_id=1, source_target_pairs={{0,1},{1,0},{2,3},{3,2},{4,5},{5,4},{6,7},{7,6},{8,9},{9,8},{10,11... | collective-permute-start | bytes 393224 | tf_op jit(solution)/shard_map/ppermute | solution.py:236
  29.2 1.4 %collective-permute-start.4 = (bf16[128,512]{1,0:T(8,128)(2,1)S(1)}, bf16[128,512]{1,0:T(8,128)(2,1)S(1)}, u32[]{:S(2)}, u32[]{:S(2)}) collective-permute-start(bf16[128,512]{1,0:T(8,128)(2,1)S(1)} %get-tuple-element.59), channel_id=1, source_target_pairs={{0,2},{1,3},{2,0},{3,1},{4,6},{5,7},{6,4},{7,5},{8,10},{9,11},{10,... | collective-permute-start | bytes 393224 | tf_op jit(solution)/shard_map/ppermute | solution.py:236
  31.1 0.7 %shard_map.73 = (bf16[1024,512]{1,0:T(8,128)(2,1)S(1)}, bf16[256,512]{1,0:T(8,128)(2,1)S(1)}) custom-call(s32[512,1]{1,0:T(8,128)S(1)} %get-tuple-element.61.place_ref, bf16[256,512]{1,0:T(8,128)(2,1)S(1)} %copy-done.2, bf16[256,512]{1,0:T(8,128)(2,1)S(1)} %collective-permute-done.6.refs_1_, bf16[256,512]{1,0:T(8,128)(2,1)S(1)} %collective-permute-done.1.refs_2_, ...), custom_call_target="tpu_custom_call" | custom-call | flops 536870912 | bytes 1048576 | tf_op jit(solution)/shard_map/pallas_call | solution.py:225
  31.8 0.7 %shard_map.74 = (bf16[1024,512]{1,0:T(8,128)(2,1)S(1)}, bf16[256,512]{1,0:T(8,128)(2,1)S(1)}) custom-call(s32[512,1]{1,0:T(8,128)S(1)} %get-tuple-element.61.place_ref, bf16[256,512]{1,0:T(8,128)(2,1)S(1)} %collective-permute-done.refs_0_, bf16[256,512]{1,0:T(8,128)(2,1)S(1)} %collective-permute-done.8.refs_1_, ...), custom_call_target="tpu_custom_call" | custom-call | flops 536870912 | bytes 1048576 | tf_op jit(solution)/shard_map/pallas_call | solution.py:225
  32.6 1.8 %collective-permute-done.5.refs_3_ = bf16[128,512]{1,0:T(8,128)(2,1)S(1)} collective-permute-done((bf16[128,512]{1,0:T(8,128)(2,1)S(1)}, bf16[128,512]{1,0:T(8,128)(2,1)S(1)}, u32[]{:S(2)}, u32[]{:S(2)}) %collective-permute-start.5) | collective-permute-done | bytes 131104 | tf_op jit(solution)/shard_map/ppermute | solution.py:236
  34.4 1.8 %collective-permute-done.3.refs_1_ = bf16[128,512]{1,0:T(8,128)(2,1)S(1)} collective-permute-done((bf16[128,512]{1,0:T(8,128)(2,1)S(1)}, bf16[128,512]{1,0:T(8,128)(2,1)S(1)}, u32[]{:S(2)}, u32[]{:S(2)}) %collective-permute-start.3) | collective-permute-done | bytes 131104 | tf_op jit(solution)/shard_map/ppermute | solution.py:236
  36.2 2.3 %shard_map.75 = (bf16[128,512]{1,0:T(8,128)(2,1)S(1)}, bf16[128,512]{1,0:T(8,128)(2,1)S(1)}, bf16[128,512]{1,0:T(8,128)(2,1)S(1)}, bf16[128,512]{1,0:T(8,128)(2,1)S(1)}) custom-call(bf16[512,512]{1,0:T(8,128)(2,1)S(1)} %copy-done.1, bf16[128,512]{1,0:T(8,128)(2,1)S(1)} %shard_map.71.refs_0_, bf16[128,512]{1,0:T(8,128)(2,1)S(1)} %collective-permute-done.3.refs_1_, ...), custom_call_target="tpu_custom_call" | custom-call | flops 2147483648 | bytes 1048576 | tf_op jit(solution)/shard_map/pallas_call | solution.py:225
  39.1 1.5 %collective-permute-done.10.refs_1_ = bf16[16,16,512]{2,1,0:T(8,128)(2,1)S(1)} collective-permute-done((bf16[16,16,512]{2,1,0:T(8,128)(2,1)S(1)}, bf16[16,16,512]{2,1,0:T(8,128)(2,1)S(1)}, u32[]{:S(2)}, u32[]{:S(2)}) %collective-permute-start.10) | collective-permute-done | bytes 262176 | tf_op jit(solution)/shard_map/ppermute | solution.py:236
  40.7 1.3 %collective-permute-start.11 = (bf16[4,16,512]{2,1,0:T(8,128)(2,1)S(1)}, bf16[4,16,512]{2,1,0:T(8,128)(2,1)S(1)}, u32[]{:S(2)}, u32[]{:S(2)}) collective-permute-start(bf16[4,16,512]{2,1,0:T(8,128)(2,1)S(1)} %get-tuple-element.75), channel_id=1, source_target_pairs={{0,1},{1,0},{2,3},{3,2},{4,5},{5,4},{6,7},{7,6},{8,9},{9,8},{10,11... | collective-permute-start | bytes 196616 | tf_op jit(solution)/shard_map/ppermute | solution.py:236
  41.9 3.1 %collective-permute-done.11.refs_1_ = bf16[4,16,512]{2,1,0:T(8,128)(2,1)S(1)} collective-permute-done((bf16[4,16,512]{2,1,0:T(8,128)(2,1)S(1)}, bf16[4,16,512]{2,1,0:T(8,128)(2,1)S(1)}, u32[]{:S(2)}, u32[]{:S(2)}) %collective-permute-start.11) | collective-permute-done | bytes 65568 | tf_op jit(solution)/shard_map/ppermute | solution.py:236
  45.0 1.2 %collective-permute-start.12 = (bf16[128,512]{1,0:T(8,128)(2,1)S(1)}, bf16[128,512]{1,0:T(8,128)(2,1)S(1)}, u32[]{:S(2)}, u32[]{:S(2)}) collective-permute-start(bf16[128,512]{1,0:T(8,128)(2,1)S(1)} %get-tuple-element.76.refs_5_), channel_id=1, source_target_pairs={{0,1},{1,0},{2,3},{3,2},{4,5},{5,4},{6,7},{7,6},{8,9},{9,8},{10,11... | collective-permute-start | bytes 393224 | tf_op jit(solution)/shard_map/ppermute | solution.py:236
  46.2 0.6 collective-permute-start.13
  46.8 1.7 %collective-permute-start.14 = (bf16[128,512]{1,0:T(8,128)(2,1)S(1)}, bf16[128,512]{1,0:T(8,128)(2,1)S(1)}, u32[]{:S(2)}, u32[]{:S(2)}) collective-permute-start(bf16[128,512]{1,0:T(8,128)(2,1)S(1)} %get-tuple-element.78.refs_7_), channel_id=1, source_target_pairs={{0,3},{1,2},{2,1},{3,0},{4,7},{5,6},{6,5},{7,4},{8,11},{9,10},{10,... | collective-permute-start | bytes 393224 | tf_op jit(solution)/shard_map/ppermute | solution.py:236
  48.5 0.9 %collective-permute-start.15 = (bf16[4,16,512]{2,1,0:T(8,128)(2,1)S(1)}, bf16[4,16,512]{2,1,0:T(8,128)(2,1)S(1)}, u32[]{:S(2)}, u32[]{:S(2)}) collective-permute-start(bf16[4,16,512]{2,1,0:T(8,128)(2,1)S(1)} %get-tuple-element.81), channel_id=1, source_target_pairs={{0,16},{1,17},{2,18},{3,19},{4,20},{5,21},{6,22},{7,23},{8,24},{9,... | collective-permute-start | bytes 196616 | tf_op jit(solution)/shard_map/ppermute | solution.py:236
  49.4 1.7 %collective-permute-start.16 = (bf16[4,16,512]{2,1,0:T(8,128)(2,1)S(1)}, bf16[4,16,512]{2,1,0:T(8,128)(2,1)S(1)}, u32[]{:S(2)}, u32[]{:S(2)}) collective-permute-start(bf16[4,16,512]{2,1,0:T(8,128)(2,1)S(1)} %get-tuple-element.82), channel_id=1, source_target_pairs={{0,17},{1,16},{2,19},{3,18},{4,21},{5,20},{6,23},{7,22},{8,25},{9,... | collective-permute-start | bytes 196616 | tf_op jit(solution)/shard_map/ppermute | solution.py:236
  51.2 1.6 %collective-permute-done.15.refs_2_ = bf16[4,16,512]{2,1,0:T(8,128)(2,1)S(1)} collective-permute-done((bf16[4,16,512]{2,1,0:T(8,128)(2,1)S(1)}, bf16[4,16,512]{2,1,0:T(8,128)(2,1)S(1)}, u32[]{:S(2)}, u32[]{:S(2)}) %collective-permute-start.15) | collective-permute-done | bytes 65568 | tf_op jit(solution)/shard_map/ppermute | solution.py:236
  52.8 1.8 %collective-permute-done.16.refs_3_ = bf16[4,16,512]{2,1,0:T(8,128)(2,1)S(1)} collective-permute-done((bf16[4,16,512]{2,1,0:T(8,128)(2,1)S(1)}, bf16[4,16,512]{2,1,0:T(8,128)(2,1)S(1)}, u32[]{:S(2)}, u32[]{:S(2)}) %collective-permute-start.16) | collective-permute-done | bytes 65568 | tf_op jit(solution)/shard_map/ppermute | solution.py:236
  54.7 2.8 %collective-permute-start.17 = (f32[1,16,512]{2,1,0:T(8,128)S(1)}, f32[1,16,512]{2,1,0:T(8,128)S(1)}, u32[]{:S(2)}, u32[]{:S(2)}) collective-permute-start(f32[1,16,512]{2,1,0:T(8,128)S(1)} %get-tuple-element.84), channel_id=1, source_target_pairs={{0,4},{1,5},{2,6},{3,7},{4,0},{5,1},{6,2},{7,3},{8,12},{9,13},{10,... | collective-permute-start | bytes 98312 | tf_op jit(solution)/shard_map/ppermute | solution.py:236
  57.5 0.9 %collective-permute-start.18 = (f32[1,16,512]{2,1,0:T(8,128)S(1)}, f32[1,16,512]{2,1,0:T(8,128)S(1)}, u32[]{:S(2)}, u32[]{:S(2)}) collective-permute-start(f32[1,16,512]{2,1,0:T(8,128)S(1)} %get-tuple-element.85), channel_id=1, source_target_pairs={{0,2},{1,3},{2,0},{3,1},{4,6},{5,7},{6,4},{7,5},{8,10},{9,11},{10,... | collective-permute-start | bytes 98312 | tf_op jit(solution)/shard_map/ppermute | solution.py:236
  58.4 0.7 %collective-permute-start.19 = (f32[1,16,512]{2,1,0:T(8,128)S(1)}, f32[1,16,512]{2,1,0:T(8,128)S(1)}, u32[]{:S(2)}, u32[]{:S(2)}) collective-permute-start(f32[1,16,512]{2,1,0:T(8,128)S(1)} %get-tuple-element.86), channel_id=1, source_target_pairs={{0,6},{1,7},{2,4},{3,5},{4,2},{5,3},{6,0},{7,1},{8,14},{9,15},{10,... | collective-permute-start | bytes 98312 | tf_op jit(solution)/shard_map/ppermute | solution.py:236
  59.1 3.9 %shard_map.78 = bf16[4096,512]{1,0:T(8,128)(2,1)} custom-call(bf16[256,512]{1,0:T(8,128)(2,1)S(1)} %get-tuple-element.53.low_hot_ref, bf16[256,512]{1,0:T(8,128)(2,1)S(1)} %get-tuple-element.54.block_ref, bf16[512,512]{1,0:T(8,128)(2,1)S(1)} %copy-done.1, bf16[128,512]{1,0:T(8,128)(2,1)S(1)} %get-tuple-element.69.refs_4_.refs_0_, ...), custom_call_target="tpu_custom_call" | custom-call | flops 2147483648 | bytes 4194304 | tf_op jit(solution)/shard_map/pallas_call | solution.py:370
  63.0 1.1 %collective-permute-done.19.refs_3_ = f32[1,16,512]{2,1,0:T(8,128)S(1)} collective-permute-done((f32[1,16,512]{2,1,0:T(8,128)S(1)}, f32[1,16,512]{2,1,0:T(8,128)S(1)}, u32[]{:S(2)}, u32[]{:S(2)}) %collective-permute-start.19) | collective-permute-done | bytes 32800 | tf_op jit(solution)/shard_map/ppermute | solution.py:236
  64.1 0.6 shard_map.80
  (29 shorter events, 2.9 us)
Async XLA Ops:
  0.6 18.4 %collective-permute-start = (bf16[256,512]{1,0:T(8,128)(2,1)}, bf16[256,512]{1,0:T(8,128)(2,1)S(1)}, u32[]{:S(2)}, u32[]{:S(2)}) collective-permute-start(bf16[256,512]{1,0:T(8,128)(2,1)} %refs_0_), channel_id=1, source_target_pairs={{0,4},{1,5},{2,6},{3,7},{4,0},{5,1},{6,2},{7,3},{8,12},{9,13},{10,... | collective-permute-start | bytes 786440 | tf_op jit(solution)/shard_map/ppermute | solution.py:236
  4.7 14.4 %collective-permute-start.1 = (bf16[256,512]{1,0:T(8,128)(2,1)}, bf16[256,512]{1,0:T(8,128)(2,1)S(1)}, u32[]{:S(2)}, u32[]{:S(2)}) collective-permute-start(bf16[256,512]{1,0:T(8,128)(2,1)} %refs_0_), channel_id=1, source_target_pairs={{0,16},{1,17},{2,18},{3,19},{4,20},{5,21},{6,22},{7,23},{8,24},{9,... | collective-permute-start | bytes 786440 | tf_op jit(solution)/shard_map/ppermute | solution.py:236
  6.9 12.8 %copy-start = (bf16[4096,512]{1,0:T(8,128)(2,1)S(1)}, bf16[4096,512]{1,0:T(8,128)(2,1)}, u32[]{:S(2)}) copy-start(bf16[4096,512]{1,0:T(8,128)(2,1)} %table_ref.5) | copy-start | bytes 12582916
  7.4 13.2 %copy-start.2 = (bf16[256,512]{1,0:T(8,128)(2,1)S(1)}, bf16[256,512]{1,0:T(8,128)(2,1)}, u32[]{:S(2)}) copy-start(bf16[256,512]{1,0:T(8,128)(2,1)} %refs_0_) | copy-start | bytes 786436
  19.1 8.0 %collective-permute-start.2 = (bf16[256,512]{1,0:T(8,128)(2,1)S(1)}, bf16[256,512]{1,0:T(8,128)(2,1)S(1)}, u32[]{:S(2)}, u32[]{:S(2)}) collective-permute-start(bf16[256,512]{1,0:T(8,128)(2,1)S(1)} %collective-permute-done.refs_0_), channel_id=1, source_target_pairs={{0,16},{1,17},{2,18},{3,19},{4,20},{5,21},{6,22},{7,23},{8,24},{9,... | collective-permute-start | bytes 786440 | tf_op jit(solution)/shard_map/ppermute | solution.py:236
  19.7 12.1 %collective-permute-start.8 = (bf16[256,512]{1,0:T(8,128)(2,1)S(1)}, bf16[256,512]{1,0:T(8,128)(2,1)S(1)}, u32[]{:S(2)}, u32[]{:S(2)}) collective-permute-start(bf16[256,512]{1,0:T(8,128)(2,1)S(1)} %collective-permute-done.refs_0_), channel_id=1, source_target_pairs={{0,8},{1,9},{2,10},{3,11},{4,12},{5,13},{6,14},{7,15},{8,0},{9,1},... | collective-permute-start | bytes 786440 | tf_op jit(solution)/shard_map/ppermute | solution.py:236
  20.6 7.1 %collective-permute-start.6 = (bf16[256,512]{1,0:T(8,128)(2,1)S(1)}, bf16[256,512]{1,0:T(8,128)(2,1)S(1)}, u32[]{:S(2)}, u32[]{:S(2)}) collective-permute-start(bf16[256,512]{1,0:T(8,128)(2,1)S(1)} %copy-done.2), channel_id=1, source_target_pairs={{0,8},{1,9},{2,10},{3,11},{4,12},{5,13},{6,14},{7,15},{8,0},{9,1},... | collective-permute-start | bytes 786440 | tf_op jit(solution)/shard_map/ppermute | solution.py:236
  21.2 8.1 %collective-permute-start.7 = (bf16[256,512]{1,0:T(8,128)(2,1)S(1)}, bf16[256,512]{1,0:T(8,128)(2,1)S(1)}, u32[]{:S(2)}, u32[]{:S(2)}) collective-permute-start(bf16[256,512]{1,0:T(8,128)(2,1)S(1)} %collective-permute-done.1.refs_2_), channel_id=1, source_target_pairs={{0,8},{1,9},{2,10},{3,11},{4,12},{5,13},{6,14},{7,15},{8,0},{9,1},... | collective-permute-start | bytes 786440 | tf_op jit(solution)/shard_map/ppermute | solution.py:236
  22.8 13.3 %copy-start.1 = (bf16[512,512]{1,0:T(8,128)(2,1)S(1)}, bf16[512,512]{1,0:T(8,128)(2,1)}, u32[]{:S(2)}) copy-start(bf16[512,512]{1,0:T(8,128)(2,1)} %weight_ref.3) | copy-start | bytes 1572868
  27.1 4.7 %collective-permute-start.9 = (bf16[256,512]{1,0:T(8,128)(2,1)S(1)}, bf16[256,512]{1,0:T(8,128)(2,1)S(1)}, u32[]{:S(2)}, u32[]{:S(2)}) collective-permute-start(bf16[256,512]{1,0:T(8,128)(2,1)S(1)} %collective-permute-done.2.refs_2_), channel_id=1, source_target_pairs={{0,8},{1,9},{2,10},{3,11},{4,12},{5,13},{6,14},{7,15},{8,0},{9,1},... | collective-permute-start | bytes 786440 | tf_op jit(solution)/shard_map/ppermute | solution.py:236
  27.1 7.2 %collective-permute-start.5 = (bf16[128,512]{1,0:T(8,128)(2,1)S(1)}, bf16[128,512]{1,0:T(8,128)(2,1)S(1)}, u32[]{:S(2)}, u32[]{:S(2)}) collective-permute-start(bf16[128,512]{1,0:T(8,128)(2,1)S(1)} %shard_map.69), channel_id=1, source_target_pairs={{0,3},{1,2},{2,1},{3,0},{4,7},{5,6},{6,5},{7,4},{8,11},{9,10},{10,... | collective-permute-start | bytes 393224 | tf_op jit(solution)/shard_map/ppermute | solution.py:236
  27.7 8.4 %collective-permute-start.3 = (bf16[128,512]{1,0:T(8,128)(2,1)S(1)}, bf16[128,512]{1,0:T(8,128)(2,1)S(1)}, u32[]{:S(2)}, u32[]{:S(2)}) collective-permute-start(bf16[128,512]{1,0:T(8,128)(2,1)S(1)} %get-tuple-element.58), channel_id=1, source_target_pairs={{0,1},{1,0},{2,3},{3,2},{4,5},{5,4},{6,7},{7,6},{8,9},{9,8},{10,11... | collective-permute-start | bytes 393224 | tf_op jit(solution)/shard_map/ppermute | solution.py:236
  29.2 6.9 %collective-permute-start.4 = (bf16[128,512]{1,0:T(8,128)(2,1)S(1)}, bf16[128,512]{1,0:T(8,128)(2,1)S(1)}, u32[]{:S(2)}, u32[]{:S(2)}) collective-permute-start(bf16[128,512]{1,0:T(8,128)(2,1)S(1)} %get-tuple-element.59), channel_id=1, source_target_pairs={{0,2},{1,3},{2,0},{3,1},{4,6},{5,7},{6,4},{7,5},{8,10},{9,11},{10,... | collective-permute-start | bytes 393224 | tf_op jit(solution)/shard_map/ppermute | solution.py:236
  39.0 1.6 %collective-permute-start.10 = (bf16[16,16,512]{2,1,0:T(8,128)(2,1)S(1)}, bf16[16,16,512]{2,1,0:T(8,128)(2,1)S(1)}, u32[]{:S(2)}, u32[]{:S(2)}) collective-permute-start(bf16[16,16,512]{2,1,0:T(8,128)(2,1)S(1)} %get-tuple-element.74), channel_id=1, source_target_pairs={{0,8},{1,9},{2,10},{3,11},{4,12},{5,13},{6,14},{7,15},{8,0},{9,1},... | collective-permute-start | bytes 786440 | tf_op jit(solution)/shard_map/ppermute | solution.py:236
  40.7 4.3 %collective-permute-start.11 = (bf16[4,16,512]{2,1,0:T(8,128)(2,1)S(1)}, bf16[4,16,512]{2,1,0:T(8,128)(2,1)S(1)}, u32[]{:S(2)}, u32[]{:S(2)}) collective-permute-start(bf16[4,16,512]{2,1,0:T(8,128)(2,1)S(1)} %get-tuple-element.75), channel_id=1, source_target_pairs={{0,1},{1,0},{2,3},{3,2},{4,5},{5,4},{6,7},{7,6},{8,9},{9,8},{10,11... | collective-permute-start | bytes 196616 | tf_op jit(solution)/shard_map/ppermute | solution.py:236
  45.0 13.4 %collective-permute-start.12 = (bf16[128,512]{1,0:T(8,128)(2,1)S(1)}, bf16[128,512]{1,0:T(8,128)(2,1)S(1)}, u32[]{:S(2)}, u32[]{:S(2)}) collective-permute-start(bf16[128,512]{1,0:T(8,128)(2,1)S(1)} %get-tuple-element.76.refs_5_), channel_id=1, source_target_pairs={{0,1},{1,0},{2,3},{3,2},{4,5},{5,4},{6,7},{7,6},{8,9},{9,8},{10,11... | collective-permute-start | bytes 393224 | tf_op jit(solution)/shard_map/ppermute | solution.py:236
  46.2 12.9 %collective-permute-start.13 = (bf16[128,512]{1,0:T(8,128)(2,1)S(1)}, bf16[128,512]{1,0:T(8,128)(2,1)S(1)}, u32[]{:S(2)}, u32[]{:S(2)}) collective-permute-start(bf16[128,512]{1,0:T(8,128)(2,1)S(1)} %get-tuple-element.77.refs_6_), channel_id=1, source_target_pairs={{0,2},{1,3},{2,0},{3,1},{4,6},{5,7},{6,4},{7,5},{8,10},{9,11},{10,... | collective-permute-start | bytes 393224 | tf_op jit(solution)/shard_map/ppermute | solution.py:236
  46.8 12.3 %collective-permute-start.14 = (bf16[128,512]{1,0:T(8,128)(2,1)S(1)}, bf16[128,512]{1,0:T(8,128)(2,1)S(1)}, u32[]{:S(2)}, u32[]{:S(2)}) collective-permute-start(bf16[128,512]{1,0:T(8,128)(2,1)S(1)} %get-tuple-element.78.refs_7_), channel_id=1, source_target_pairs={{0,3},{1,2},{2,1},{3,0},{4,7},{5,6},{6,5},{7,4},{8,11},{9,10},{10,... | collective-permute-start | bytes 393224 | tf_op jit(solution)/shard_map/ppermute | solution.py:236
  48.5 4.3 %collective-permute-start.15 = (bf16[4,16,512]{2,1,0:T(8,128)(2,1)S(1)}, bf16[4,16,512]{2,1,0:T(8,128)(2,1)S(1)}, u32[]{:S(2)}, u32[]{:S(2)}) collective-permute-start(bf16[4,16,512]{2,1,0:T(8,128)(2,1)S(1)} %get-tuple-element.81), channel_id=1, source_target_pairs={{0,16},{1,17},{2,18},{3,19},{4,20},{5,21},{6,22},{7,23},{8,24},{9,... | collective-permute-start | bytes 196616 | tf_op jit(solution)/shard_map/ppermute | solution.py:236
  49.4 5.2 %collective-permute-start.16 = (bf16[4,16,512]{2,1,0:T(8,128)(2,1)S(1)}, bf16[4,16,512]{2,1,0:T(8,128)(2,1)S(1)}, u32[]{:S(2)}, u32[]{:S(2)}) collective-permute-start(bf16[4,16,512]{2,1,0:T(8,128)(2,1)S(1)} %get-tuple-element.82), channel_id=1, source_target_pairs={{0,17},{1,16},{2,19},{3,18},{4,21},{5,20},{6,23},{7,22},{8,25},{9,... | collective-permute-start | bytes 196616 | tf_op jit(solution)/shard_map/ppermute | solution.py:236
  54.7 8.3 %collective-permute-start.17 = (f32[1,16,512]{2,1,0:T(8,128)S(1)}, f32[1,16,512]{2,1,0:T(8,128)S(1)}, u32[]{:S(2)}, u32[]{:S(2)}) collective-permute-start(f32[1,16,512]{2,1,0:T(8,128)S(1)} %get-tuple-element.84), channel_id=1, source_target_pairs={{0,4},{1,5},{2,6},{3,7},{4,0},{5,1},{6,2},{7,3},{8,12},{9,13},{10,... | collective-permute-start | bytes 98312 | tf_op jit(solution)/shard_map/ppermute | solution.py:236
  57.5 5.5 %collective-permute-start.18 = (f32[1,16,512]{2,1,0:T(8,128)S(1)}, f32[1,16,512]{2,1,0:T(8,128)S(1)}, u32[]{:S(2)}, u32[]{:S(2)}) collective-permute-start(f32[1,16,512]{2,1,0:T(8,128)S(1)} %get-tuple-element.85), channel_id=1, source_target_pairs={{0,2},{1,3},{2,0},{3,1},{4,6},{5,7},{6,4},{7,5},{8,10},{9,11},{10,... | collective-permute-start | bytes 98312 | tf_op jit(solution)/shard_map/ppermute | solution.py:236
  58.4 5.7 %collective-permute-start.19 = (f32[1,16,512]{2,1,0:T(8,128)S(1)}, f32[1,16,512]{2,1,0:T(8,128)S(1)}, u32[]{:S(2)}, u32[]{:S(2)}) collective-permute-start(f32[1,16,512]{2,1,0:T(8,128)S(1)} %get-tuple-element.86), channel_id=1, source_target_pairs={{0,6},{1,7},{2,4},{3,5},{4,2},{5,3},{6,0},{7,1},{8,14},{9,15},{10,... | collective-permute-start | bytes 98312 | tf_op jit(solution)/shard_map/ppermute | solution.py:236

commit v10 on v9

--- a/solution.py
+++ b/solution.py
@@ -161,11 +161,14 @@
             ref[here] = dhidden[part * size : (part + 1) * size]
 
 
+def coordinate(bits):
+    return sum(((lax.axis_index(axis) >> level) & 1) << k for k, (axis, level) in enumerate(reversed(bits)))
+
+
 def cut(blocks, bits, refs):
     size = refs[0].shape[0]
-    mine = sum(((lax.axis_index(axis) >> level) & 1) << k for k, (axis, level) in enumerate(reversed(bits)))
     for step, ref in enumerate(refs):
-        ref[...] = blocks[pl.ds((mine ^ step) * size, size)].astype(ref.dtype)
+        ref[...] = blocks[pl.ds((coordinate(bits) ^ step) * size, size)].astype(ref.dtype)
 
 
 def share_kernel(order, bits, count, *refs):
@@ -178,24 +181,34 @@
     cut(blocks, bits, refs)
 
 
-def sum_of(refs):
-    return sum(ref[...].astype(f32) for ref in refs)
-
-
-def stage_kernel(bits, count, *refs):
-    came, (*refs, blocks) = refs[:count], refs[count:]
-    blocks[...] = sum_of(came)
-    cut(blocks, bits, refs)
+def stage_kernel(bits, count, extra, *refs):
+    came, extras, (keep_ref, *sends, blocks) = refs[:count], refs[count : count + extra], refs[count + extra :]
+    shape = blocks.shape
+    total = came[0][...]
+    for ref in came[1:]:
+        total += ref[...][: shape[0] * shape[1]].reshape(shape).astype(f32)
+    blocks[...] = total
+    if not extra:
+        cut(blocks, bits, [keep_ref, *sends])
+        return
+    size = keep_ref.shape[0]
+    cut(blocks, bits, [keep_ref])
+    for step, (ref, rows) in enumerate(zip(sends, extras), 1):
+        part = blocks[pl.ds((coordinate(bits) ^ step) * size, size)]
+        ref[pl.ds(0, size * shape[1])] = part.reshape(size * shape[1], shape[2]).astype(ref.dtype)
+        ref[pl.ds(size * shape[1], rows.shape[0])] = rows[...]
 
 
 def last_kernel(*refs):
     *came, total_ref = refs
-    total_ref[...] = sum_of(came)[0]
+    total_ref[...] = sum(ref[...].astype(f32) for ref in came)[0]
 
 
 def table_kernel(low_hot_ref, block_ref, weight_ref, *refs):
     *incoming, table_grad_hbm, ready, sems = refs
-    drow = jnp.concatenate([dot(ref[...], weight_ref[...], 1, 1).astype(bf16) for ref in incoming], axis=0)
+    size = incoming[0].shape[0]
+    dhidden = jnp.concatenate([ref[pl.ds(ref.shape[0] - size, size)] for ref in incoming], axis=0)
+    drow = dot(dhidden, weight_ref[...], 1, 1).astype(bf16)
     groups = sems.shape[0]
     size = ready.shape[0] // groups
     copies = []
@@ -221,13 +234,13 @@
     return pl.CostEstimate(flops=flops, bytes_accessed=bytes_accessed, transcendentals=0)
 
 
-def call(kernel, outs, *args, flops=0, scratch=(), mib=16):
+def call(kernel, outs, *args, flops=0, scratch=(), mib=16, free=False):
     return pl.pallas_call(
         kernel,
         out_shape=[jax.ShapeDtypeStruct(shape, dtype) for shape, dtype in outs],
         scratch_shapes=scratch,
         compiler_params=params(mib),
-        cost_estimate=cost(flops),
+        cost_estimate=cost(flops, 0 if free else 1 << 20),
     )(*args)
 
 
@@ -244,35 +257,46 @@
     return sum((lax.axis_size("item") if axis == "batch" else 1) << level for axis, level in bits)
 
 
-def reduce_scatter(values, width, between):
+def reduce_scatter(fetched, dhidden):
+    width = dhidden[0].shape[1]
     n_item, devices = lax.axis_size("item"), lax.axis_size("batch") * lax.axis_size("item")
     part = width // devices
-    bits = bits_of("batch") + bits_of("item")
+    close = log2(len(dhidden))
+    batch_bits, item_bits = bits_of("batch"), bits_of("item")
+    stages = [batch_bits[:1], item_bits[:close]]
+    rest = batch_bits[1:] + item_bits[close:]
+    stages += [rest[k : k + 2] for k in range(0, len(rest), 2)]
+    bits = sum(stages, [])
     order = []
     for spot in range(devices):
         at = {"batch": 0, "item": 0}
         for k, (axis, level) in enumerate(bits):
             at[axis] |= (spot >> (len(bits) - 1 - k) & 1) << level
         order.append(at["batch"] * n_item + at["item"])
-    odd = len(bits) % 2
-    stages = [bits[:1]] * odd + [bits[k : k + 2] for k in range(odd, len(bits), 2)]
-    left = devices
+    left, values, back = devices, [*fetched, *dhidden], {}
     for k, stage in enumerate(stages):
         whole, left = left, left >> len(stage)
-        sent = f32 if k == len(stages) - 1 else bf16
-        kernel = functools.partial(*((stage_kernel, stage) if k else (share_kernel, order, stage)), len(values))
+        masks = [
+            mask_of([bit for j, bit in enumerate(reversed(stage)) if step >> j & 1]) for step in range(1, 1 << len(stage))
+        ]
+        extras = [dhidden[mask] for mask in masks] if k == 1 else []
+        if k == 1:
+            sent = ((left * part + dhidden[0].shape[0], width), bf16)
+        else:
+            sent = ((left, part, width), f32 if k == len(stages) - 1 else bf16)
+        count = len(values)
+        kernel = functools.partial(stage_kernel, stage, count, len(extras)) if k else functools.partial(share_kernel, order, stage, count)
         kept, *sends = call(
             kernel,
-            [((left, part, width), f32)] + [((left, part, width), sent)] * ((1 << len(stage)) - 1),
+            [((left, part, width), f32)] + [sent] * len(masks),
             *values,
+            *extras,
             scratch=[pltpu.VMEM((whole, part, width), f32)],
         )
-        values = [kept]
-        for step, value in enumerate(sends, 1):
-            values.append(swap(value, mask_of([bit for j, bit in enumerate(reversed(stage)) if step >> j & 1])))
+        values = [kept] + [swap(value, mask) for mask, value in zip(masks, sends)]
         if k == 1:
-            values[1] = between(values[1])
-    return values
+            back = dict(zip(masks, values[1:]))
+    return values, [back[mask] for mask in range(1, len(dhidden))]
 
 
 def local(user_vectors, item_table, tower_weight, item_owner, item_row):
@@ -325,7 +349,9 @@
         for part, value in zip(parts, values):
             fetched[part] = swap(value, part) if part else value
     late = [mask for mask in users if mask not in early]
-    fetched[0], *values = lax.optimization_barrier((fetched[0], *[users[mask] for mask in late]))
+    fetched[0], fetched[near - 1], *values = lax.optimization_barrier(
+        (fetched[0], fetched[near - 1], *[users[mask] for mask in late])
+    )
     users.update(zip(late, values))
     fetched = [fetched[part] for part in range(near)]
 
@@ -336,6 +362,7 @@
         functools.partial(prepare_kernel, near, n_batch, n),
         [((total, 1), i32)] + [((BLOCK, total), bf16)] * 2,
         asked,
+        free=True,
     )
     units, owns = zip(
         *[
@@ -344,7 +371,7 @@
                 [((n_batch * n, width), bf16), ((total // levels, width), bf16)],
                 place,
                 *[users[near * level + batch * n_item] for batch in range(n_batch)],
-                flops=1 << 29,
+                free=True,
             )
             for level in range(levels)
         ]
@@ -359,14 +386,7 @@
         flops=1 << 31,
         mib=40,
     )
-    incoming = [dhidden[0]]
-
-    def give_back(value):
-        value, *given = lax.optimization_barrier((value, *dhidden[1:]))
-        incoming.extend(swap(rows, part) for part, rows in enumerate(given, 1))
-        return value
-
-    terms = reduce_scatter([*fetched, *dhidden], width, give_back)
+    terms, incoming = reduce_scatter(fetched, dhidden)
     table_grad = pl.pallas_call(
         table_kernel,
         out_specs=pl.BlockSpec(memory_space=pl.ANY),
@@ -374,7 +394,7 @@
         scratch_shapes=[pltpu.VMEM((rows, width), bf16), pltpu.SemaphoreType.DMA((groups,))],
         compiler_params=params(16),
         cost_estimate=cost(2 * total * rows * width, 2 * rows * width),
-    )(low_hot, block, tower_weight, *incoming)
+    )(low_hot, block, tower_weight, dhidden[0], *incoming)
     table_grad, *terms = lax.optimization_barrier((table_grad, *terms))
     (weight_grad,) = call(last_kernel, [((width // devices, width), f32)], *terms)
     return (table_grad, weight_grad)

time: 64.9 us -> 61.3 us (0.945)
  starting transfers between devices: 22.3 us -> 17 us
  waiting for transfers between devices: 16.1 us -> 18.1 us
    ppermute x20 -> x17, starting transfers between devices: 22.3 us -> 17 us  [swap(): lax.ppermute(value, ('batch', 'item'), [(k, k ^ mask) for k in range(devi...]
    ppermute x20 -> x17, waiting for transfers between devices: 16.1 us -> 18.1 us  [swap(): lax.ppermute(value, ('batch', 'item'), [(k, k ^ mask) for k in range(devi...]
  transfers between devices with their start and end apart: 20 -> 17, of which waited for: 8 -> 8; matrix products, arithmetic and copies ran while one was open for 1% -> 1% of each run, Pallas kernels for 15% -> 15%
where the time goes in v10:
time: 61.3 us; the launch traced here: 61.1 us
  waiting for transfers between devices  18.1 us (30%)
  starting transfers between devices  17 us (28%)
  Pallas kernels  12.8 us (21%)
  blocking collectives  11.7 us (19%)
  between operations  0.79 us (1%)
  other arithmetic  0.7 us (1%)
    ppermute x17, waiting for transfers between devices, swap(): lax.ppermute(value, ('batch', 'item'), [(k, k ^ mask) for k in range(devi...  18.1 us
    ppermute x17, starting transfers between devices, swap(): lax.ppermute(value, ('batch', 'item'), [(k, k ^ mask) for k in range(devi...  17 us
    all_to_all x1, blocking collectives, local(): lax.all_to_all(request, ('batch', 'item'), split_axis=0, concat_axis=0, t...  11.7 us
    pallas_call x12, Pallas kernels, call(): pl.pallas_call(kernel, out_shape=[jax.ShapeDtypeStruct(shape, dtype) for...  9.26 us
    pallas_call x1, Pallas kernels, local(): pl.pallas_call(table_kernel, out_specs=pl.BlockSpec(memory_space=pl.ANY),...  3.59 us
  transfers between devices with their start and end apart: 17, of which 8 were waited for; matrix products, arithmetic and copies ran while one was open for 1% of the time, Pallas kernels for 15%

profile of v10, /device:TPU:0, one launch (start us, length us, event | category | flops | bytes accessed | tf_op | source)
XLA Modules:
  0.0 61.1 jit_solution(12618483931487858181)
XLA Ops:
  0.6 4.1 %collective-permute-start = (bf16[256,512]{1,0:T(8,128)(2,1)}, bf16[256,512]{1,0:T(8,128)(2,1)S(1)}, u32[]{:S(2)}, u32[]{:S(2)}) collective-permute-start(bf16[256,512]{1,0:T(8,128)(2,1)} %refs_0_), channel_id=1, source_target_pairs={{0,4},{1,5},{2,6},{3,7},{4,0},{5,1},{6,2},{7,3},{8,12},{9,13},{10,... | collective-permute-start | bytes 786440 | tf_op jit(solution)/shard_map/ppermute | solution.py:249
  4.7 1.5 %collective-permute-start.1 = (bf16[256,512]{1,0:T(8,128)(2,1)}, bf16[256,512]{1,0:T(8,128)(2,1)S(1)}, u32[]{:S(2)}, u32[]{:S(2)}) collective-permute-start(bf16[256,512]{1,0:T(8,128)(2,1)} %refs_0_), channel_id=1, source_target_pairs={{0,16},{1,17},{2,18},{3,19},{4,20},{5,21},{6,22},{7,23},{8,24},{9,... | collective-permute-start | bytes 786440 | tf_op jit(solution)/shard_map/ppermute | solution.py:249
  6.2 0.7 %pad_add_fusion.named_ref = s32[2,256]{1,0:T(2,128)S(1)} fusion(s32[1,256]{1,0:T(1,128)} %bitcast.11, s32[1,256]{1,0:T(1,128)} %bitcast.12), kind=kLoop, calls=%fused_computation | loop fusion | flops 512 | bytes 4096 | tf_op jit(solution)/shard_map/stack | solution.py:322
  6.9 0.4 shard_map.68
  7.4 11.7 %all_to_all.12 = s32[32,1,80]{2,1,0:T(1,128)S(1)} all-to-all(s32[32,1,80]{2,1,0:T(1,128)S(1)} %bitcast.10), channel_id=1, replica_groups=mesh['batch'=4,'item'=8] {'batch','item'}, dimensions={0} | all-to-all | bytes 20480 | tf_op jit(solution)/shard_map/all_to_all | solution.py:325
  19.1 0.6 collective-permute-start.3
  19.7 0.9 %shard_map.69 = bf16[128,512]{1,0:T(8,128)(2,1)S(1)} custom-call(s32[32,80]{1,0:T(8,128)S(1)} %bitcast.6, bf16[4096,512]{1,0:T(8,128)(2,1)S(1)} %copy-done), custom_call_target="tpu_custom_call" | custom-call | flops 536870912 | bytes 1048576 | tf_op jit(solution)/shard_map/pallas_call | solution.py:238
  20.6 0.8 %collective-permute-start.2 = (bf16[128,512]{1,0:T(8,128)(2,1)S(1)}, bf16[128,512]{1,0:T(8,128)(2,1)S(1)}, u32[]{:S(2)}, u32[]{:S(2)}) collective-permute-start(bf16[128,512]{1,0:T(8,128)(2,1)S(1)} %shard_map.69), channel_id=1, source_target_pairs={{0,3},{1,2},{2,1},{3,0},{4,7},{5,6},{6,5},{7,4},{8,11},{9,10},{10,... | collective-permute-start | bytes 393224 | tf_op jit(solution)/shard_map/ppermute | solution.py:249
  21.6 1.6 %shard_map.70 = (bf16[128,512]{1,0:T(8,128)(2,1)S(1)}, bf16[128,512]{1,0:T(8,128)(2,1)S(1)}) custom-call(s32[32,80]{1,0:T(8,128)S(1)} %bitcast.7, bf16[4096,512]{1,0:T(8,128)(2,1)S(1)} %copy-done), custom_call_target="tpu_custom_call" | custom-call | flops 1073741824 | bytes 1048576 | tf_op jit(solution)/shard_map/pallas_call | solution.py:238
  23.2 0.9 %shard_map.71.refs_0_ = bf16[128,512]{1,0:T(8,128)(2,1)S(1)} custom-call(s32[32,80]{1,0:T(8,128)S(1)} %bitcast.8, bf16[4096,512]{1,0:T(8,128)(2,1)S(1)} %copy-done), custom_call_target="tpu_custom_call" | custom-call | flops 536870912 | bytes 1048576 | tf_op jit(solution)/shard_map/pallas_call | solution.py:238
  24.5 3.0 %collective-permute-done.2.refs_3_ = bf16[128,512]{1,0:T(8,128)(2,1)S(1)} collective-permute-done((bf16[128,512]{1,0:T(8,128)(2,1)S(1)}, bf16[128,512]{1,0:T(8,128)(2,1)S(1)}, u32[]{:S(2)}, u32[]{:S(2)}) %collective-permute-start.2) | collective-permute-done | bytes 131104 | tf_op jit(solution)/shard_map/ppermute | solution.py:249
  27.5 0.7 %collective-permute-start.4 = (bf16[128,512]{1,0:T(8,128)(2,1)S(1)}, bf16[128,512]{1,0:T(8,128)(2,1)S(1)}, u32[]{:S(2)}, u32[]{:S(2)}) collective-permute-start(bf16[128,512]{1,0:T(8,128)(2,1)S(1)} %get-tuple-element.56), channel_id=1, source_target_pairs={{0,1},{1,0},{2,3},{3,2},{4,5},{5,4},{6,7},{7,6},{8,9},{9,8},{10,11... | collective-permute-start | bytes 393224 | tf_op jit(solution)/shard_map/ppermute | solution.py:249
  28.2 0.6 %collective-permute-start.5 = (bf16[128,512]{1,0:T(8,128)(2,1)S(1)}, bf16[128,512]{1,0:T(8,128)(2,1)S(1)}, u32[]{:S(2)}, u32[]{:S(2)}) collective-permute-start(bf16[128,512]{1,0:T(8,128)(2,1)S(1)} %get-tuple-element.57), channel_id=1, source_target_pairs={{0,2},{1,3},{2,0},{3,1},{4,6},{5,7},{6,4},{7,5},{8,10},{9,11},{10,... | collective-permute-start | bytes 393224 | tf_op jit(solution)/shard_map/ppermute | solution.py:249
  28.8 0.4 shard_map.72
  29.2 0.7 %shard_map.73 = (bf16[1024,512]{1,0:T(8,128)(2,1)S(1)}, bf16[256,512]{1,0:T(8,128)(2,1)S(1)}) custom-call(s32[512,1]{1,0:T(8,128)S(1)} %get-tuple-element.59.place_ref, bf16[256,512]{1,0:T(8,128)(2,1)S(1)} %copy-done.1, bf16[256,512]{1,0:T(8,128)(2,1)S(1)} %collective-permute-done.6.refs_1_, bf16[256,512]{1,0:T(8,128)(2,1)S(1)} %collective-permute-done.1.refs_2_, ...), custom_call_target="tpu_custom_call" | custom-call | tf_op jit(solution)/shard_map/pallas_call | solution.py:238
  30.0 0.7 %shard_map.74 = (bf16[1024,512]{1,0:T(8,128)(2,1)S(1)}, bf16[256,512]{1,0:T(8,128)(2,1)S(1)}) custom-call(s32[512,1]{1,0:T(8,128)S(1)} %get-tuple-element.59.place_ref, bf16[256,512]{1,0:T(8,128)(2,1)S(1)} %collective-permute-done.refs_0_, bf16[256,512]{1,0:T(8,128)(2,1)S(1)} %collective-permute-done.8.refs_1_, ...), custom_call_target="tpu_custom_call" | custom-call | tf_op jit(solution)/shard_map/pallas_call | solution.py:238
  30.7 2.6 %collective-permute-done.4.refs_1_ = bf16[128,512]{1,0:T(8,128)(2,1)S(1)} collective-permute-done((bf16[128,512]{1,0:T(8,128)(2,1)S(1)}, bf16[128,512]{1,0:T(8,128)(2,1)S(1)}, u32[]{:S(2)}, u32[]{:S(2)}) %collective-permute-start.4) | collective-permute-done | bytes 131104 | tf_op jit(solution)/shard_map/ppermute | solution.py:249
  33.8 2.3 %shard_map.75 = (bf16[128,512]{1,0:T(8,128)(2,1)S(1)}, bf16[128,512]{1,0:T(8,128)(2,1)S(1)}, bf16[128,512]{1,0:T(8,128)(2,1)S(1)}, bf16[128,512]{1,0:T(8,128)(2,1)S(1)}) custom-call(bf16[512,512]{1,0:T(8,128)(2,1)S(1)} %copy-done.2, bf16[128,512]{1,0:T(8,128)(2,1)S(1)} %shard_map.71.refs_0_, bf16[128,512]{1,0:T(8,128)(2,1)S(1)} %collective-permute-done.4.refs_1_, ...), custom_call_target="tpu_custom_call" | custom-call | flops 2147483648 | bytes 1048576 | tf_op jit(solution)/shard_map/pallas_call | solution.py:238
  36.1 0.5 shard_map.76
  36.7 1.5 %collective-permute-done.10.refs_1_ = bf16[16,16,512]{2,1,0:T(8,128)(2,1)S(1)} collective-permute-done((bf16[16,16,512]{2,1,0:T(8,128)(2,1)S(1)}, bf16[16,16,512]{2,1,0:T(8,128)(2,1)S(1)}, u32[]{:S(2)}, u32[]{:S(2)}) %collective-permute-start.10) | collective-permute-done | bytes 262176 | tf_op jit(solution)/shard_map/ppermute | solution.py:249
  38.3 1.4 %collective-permute-start.11 = (bf16[192,512]{1,0:T(8,128)(2,1)S(1)}, bf16[192,512]{1,0:T(8,128)(2,1)S(1)}, u32[]{:S(2)}, u32[]{:S(2)}) collective-permute-start(bf16[192,512]{1,0:T(8,128)(2,1)S(1)} %get-tuple-element.73), channel_id=1, source_target_pairs={{0,1},{1,0},{2,3},{3,2},{4,5},{5,4},{6,7},{7,6},{8,9},{9,8},{10,11... | collective-permute-start | bytes 589832 | tf_op jit(solution)/shard_map/ppermute | solution.py:249
  39.7 0.6 collective-permute-start.12
  40.3 1.6 %collective-permute-start.13 = (bf16[192,512]{1,0:T(8,128)(2,1)S(1)}, bf16[192,512]{1,0:T(8,128)(2,1)S(1)}, u32[]{:S(2)}, u32[]{:S(2)}) collective-permute-start(bf16[192,512]{1,0:T(8,128)(2,1)S(1)} %get-tuple-element.75), channel_id=1, source_target_pairs={{0,3},{1,2},{2,1},{3,0},{4,7},{5,6},{6,5},{7,4},{8,11},{9,10},{10,... | collective-permute-start | bytes 589832 | tf_op jit(solution)/shard_map/ppermute | solution.py:249
  41.9 3.5 %collective-permute-done.11.refs_1_.refs_2_ = bf16[192,512]{1,0:T(8,128)(2,1)S(1)} collective-permute-done((bf16[192,512]{1,0:T(8,128)(2,1)S(1)}, bf16[192,512]{1,0:T(8,128)(2,1)S(1)}, u32[]{:S(2)}, u32[]{:S(2)}) %collective-permute-start.11) | collective-permute-done | bytes 196640 | tf_op jit(solution)/shard_map/ppermute | solution.py:249
  45.3 2.2 %collective-permute-done.12.refs_2_.refs_1_ = bf16[192,512]{1,0:T(8,128)(2,1)S(1)} collective-permute-done((bf16[192,512]{1,0:T(8,128)(2,1)S(1)}, bf16[192,512]{1,0:T(8,128)(2,1)S(1)}, u32[]{:S(2)}, u32[]{:S(2)}) %collective-permute-start.12) | collective-permute-done | bytes 196640 | tf_op jit(solution)/shard_map/ppermute | solution.py:249
  47.5 3.2 %collective-permute-done.13.refs_3_ = bf16[192,512]{1,0:T(8,128)(2,1)S(1)} collective-permute-done((bf16[192,512]{1,0:T(8,128)(2,1)S(1)}, bf16[192,512]{1,0:T(8,128)(2,1)S(1)}, u32[]{:S(2)}, u32[]{:S(2)}) %collective-permute-start.13) | collective-permute-done | bytes 196640 | tf_op jit(solution)/shard_map/ppermute | solution.py:249
  50.8 2.5 %collective-permute-start.14 = (f32[1,16,512]{2,1,0:T(8,128)S(1)}, f32[1,16,512]{2,1,0:T(8,128)S(1)}, u32[]{:S(2)}, u32[]{:S(2)}) collective-permute-start(f32[1,16,512]{2,1,0:T(8,128)S(1)} %get-tuple-element.78), channel_id=1, source_target_pairs={{0,4},{1,5},{2,6},{3,7},{4,0},{5,1},{6,2},{7,3},{8,12},{9,13},{10,... | collective-permute-start | bytes 98312 | tf_op jit(solution)/shard_map/ppermute | solution.py:249
  53.3 1.5 %collective-permute-start.15 = (f32[1,16,512]{2,1,0:T(8,128)S(1)}, f32[1,16,512]{2,1,0:T(8,128)S(1)}, u32[]{:S(2)}, u32[]{:S(2)}) collective-permute-start(f32[1,16,512]{2,1,0:T(8,128)S(1)} %get-tuple-element.79), channel_id=1, source_target_pairs={{0,16},{1,17},{2,18},{3,19},{4,20},{5,21},{6,22},{7,23},{8,24},{9,... | collective-permute-start | bytes 98312 | tf_op jit(solution)/shard_map/ppermute | solution.py:249
  54.8 0.4 collective-permute-start.16
  55.2 3.6 %shard_map.78 = bf16[4096,512]{1,0:T(8,128)(2,1)} custom-call(bf16[256,512]{1,0:T(8,128)(2,1)S(1)} %get-tuple-element.50.low_hot_ref, bf16[256,512]{1,0:T(8,128)(2,1)S(1)} %get-tuple-element.51.block_ref, bf16[512,512]{1,0:T(8,128)(2,1)S(1)} %copy-done.2, bf16[128,512]{1,0:T(8,128)(2,1)S(1)} %get-tuple-element.67.refs_4_.refs_0_, ...), custom_call_target="tpu_custom_call" | custom-call | flops 2147483648 | bytes 4194304 | tf_op jit(solution)/shard_map/pallas_call | solution.py:390
  58.8 1.7 %collective-permute-done.16.refs_3_ = f32[1,16,512]{2,1,0:T(8,128)S(1)} collective-permute-done((f32[1,16,512]{2,1,0:T(8,128)S(1)}, f32[1,16,512]{2,1,0:T(8,128)S(1)}, u32[]{:S(2)}, u32[]{:S(2)}) %collective-permute-start.16) | collective-permute-done | bytes 32800 | tf_op jit(solution)/shard_map/ppermute | solution.py:249
  60.5 0.6 %shard_map.80 = f32[16,512]{1,0:T(8,128)} custom-call(f32[1,16,512]{2,1,0:T(8,128)S(1)} %get-tuple-element.82.refs_0_, f32[1,16,512]{2,1,0:T(8,128)S(1)} %collective-permute-done.14.refs_1_, f32[1,16,512]{2,1,0:T(8,128)S(1)} %collective-permute-done.15.refs_2_, f32[1,16,512]{2,1,0:T(8,128)S(1)} %collective-permute-done.16.refs_3_), custom_call_target="tpu_custom_call" | custom-call | bytes 1048576 | tf_op jit(solution)/shard_map/pallas_call | solution.py:238
  (23 shorter events, 1.3 us)
Async XLA Ops:
  0.6 18.4 %collective-permute-start = (bf16[256,512]{1,0:T(8,128)(2,1)}, bf16[256,512]{1,0:T(8,128)(2,1)S(1)}, u32[]{:S(2)}, u32[]{:S(2)}) collective-permute-start(bf16[256,512]{1,0:T(8,128)(2,1)} %refs_0_), channel_id=1, source_target_pairs={{0,4},{1,5},{2,6},{3,7},{4,0},{5,1},{6,2},{7,3},{8,12},{9,13},{10,... | collective-permute-start | bytes 786440 | tf_op jit(solution)/shard_map/ppermute | solution.py:249
  4.7 14.4 %collective-permute-start.1 = (bf16[256,512]{1,0:T(8,128)(2,1)}, bf16[256,512]{1,0:T(8,128)(2,1)S(1)}, u32[]{:S(2)}, u32[]{:S(2)}) collective-permute-start(bf16[256,512]{1,0:T(8,128)(2,1)} %refs_0_), channel_id=1, source_target_pairs={{0,16},{1,17},{2,18},{3,19},{4,20},{5,21},{6,22},{7,23},{8,24},{9,... | collective-permute-start | bytes 786440 | tf_op jit(solution)/shard_map/ppermute | solution.py:249
  6.9 12.8 %copy-start = (bf16[4096,512]{1,0:T(8,128)(2,1)S(1)}, bf16[4096,512]{1,0:T(8,128)(2,1)}, u32[]{:S(2)}) copy-start(bf16[4096,512]{1,0:T(8,128)(2,1)} %table_ref.5) | copy-start | bytes 12582916
  7.4 14.1 %copy-start.1 = (bf16[256,512]{1,0:T(8,128)(2,1)S(1)}, bf16[256,512]{1,0:T(8,128)(2,1)}, u32[]{:S(2)}) copy-start(bf16[256,512]{1,0:T(8,128)(2,1)} %refs_0_) | copy-start | bytes 786436
  19.1 8.4 %collective-permute-start.3 = (bf16[256,512]{1,0:T(8,128)(2,1)S(1)}, bf16[256,512]{1,0:T(8,128)(2,1)S(1)}, u32[]{:S(2)}, u32[]{:S(2)}) collective-permute-start(bf16[256,512]{1,0:T(8,128)(2,1)S(1)} %collective-permute-done.refs_0_), channel_id=1, source_target_pairs={{0,16},{1,17},{2,18},{3,19},{4,20},{5,21},{6,22},{7,23},{8,24},{9,... | collective-permute-start | bytes 786440 | tf_op jit(solution)/shard_map/ppermute | solution.py:249
  19.7 10.3 %collective-permute-start.8 = (bf16[256,512]{1,0:T(8,128)(2,1)S(1)}, bf16[256,512]{1,0:T(8,128)(2,1)S(1)}, u32[]{:S(2)}, u32[]{:S(2)}) collective-permute-start(bf16[256,512]{1,0:T(8,128)(2,1)S(1)} %collective-permute-done.refs_0_), channel_id=1, source_target_pairs={{0,8},{1,9},{2,10},{3,11},{4,12},{5,13},{6,14},{7,15},{8,0},{9,1},... | collective-permute-start | bytes 786440 | tf_op jit(solution)/shard_map/ppermute | solution.py:249
  20.6 6.9 %collective-permute-start.2 = (bf16[128,512]{1,0:T(8,128)(2,1)S(1)}, bf16[128,512]{1,0:T(8,128)(2,1)S(1)}, u32[]{:S(2)}, u32[]{:S(2)}) collective-permute-start(bf16[128,512]{1,0:T(8,128)(2,1)S(1)} %shard_map.69), channel_id=1, source_target_pairs={{0,3},{1,2},{2,1},{3,0},{4,7},{5,6},{6,5},{7,4},{8,11},{9,10},{10,... | collective-permute-start | bytes 393224 | tf_op jit(solution)/shard_map/ppermute | solution.py:249
  21.4 6.7 %collective-permute-start.6 = (bf16[256,512]{1,0:T(8,128)(2,1)S(1)}, bf16[256,512]{1,0:T(8,128)(2,1)S(1)}, u32[]{:S(2)}, u32[]{:S(2)}) collective-permute-start(bf16[256,512]{1,0:T(8,128)(2,1)S(1)} %copy-done.1), channel_id=1, source_target_pairs={{0,8},{1,9},{2,10},{3,11},{4,12},{5,13},{6,14},{7,15},{8,0},{9,1},... | collective-permute-start | bytes 786440 | tf_op jit(solution)/shard_map/ppermute | solution.py:249
  23.2 10.6 %copy-start.2 = (bf16[512,512]{1,0:T(8,128)(2,1)S(1)}, bf16[512,512]{1,0:T(8,128)(2,1)}, u32[]{:S(2)}) copy-start(bf16[512,512]{1,0:T(8,128)(2,1)} %weight_ref.3) | copy-start | bytes 1572868
  24.1 5.1 %collective-permute-start.7 = (bf16[256,512]{1,0:T(8,128)(2,1)S(1)}, bf16[256,512]{1,0:T(8,128)(2,1)S(1)}, u32[]{:S(2)}, u32[]{:S(2)}) collective-permute-start(bf16[256,512]{1,0:T(8,128)(2,1)S(1)} %collective-permute-done.1.refs_2_), channel_id=1, source_target_pairs={{0,8},{1,9},{2,10},{3,11},{4,12},{5,13},{6,14},{7,15},{8,0},{9,1},... | collective-permute-start | bytes 786440 | tf_op jit(solution)/shard_map/ppermute | solution.py:249
  27.5 2.5 %collective-permute-start.9 = (bf16[256,512]{1,0:T(8,128)(2,1)S(1)}, bf16[256,512]{1,0:T(8,128)(2,1)S(1)}, u32[]{:S(2)}, u32[]{:S(2)}) collective-permute-start(bf16[256,512]{1,0:T(8,128)(2,1)S(1)} %collective-permute-done.3.refs_2_), channel_id=1, source_target_pairs={{0,8},{1,9},{2,10},{3,11},{4,12},{5,13},{6,14},{7,15},{8,0},{9,1},... | collective-permute-start | bytes 786440 | tf_op jit(solution)/shard_map/ppermute | solution.py:249
  27.5 5.9 %collective-permute-start.4 = (bf16[128,512]{1,0:T(8,128)(2,1)S(1)}, bf16[128,512]{1,0:T(8,128)(2,1)S(1)}, u32[]{:S(2)}, u32[]{:S(2)}) collective-permute-start(bf16[128,512]{1,0:T(8,128)(2,1)S(1)} %get-tuple-element.56), channel_id=1, source_target_pairs={{0,1},{1,0},{2,3},{3,2},{4,5},{5,4},{6,7},{7,6},{8,9},{9,8},{10,11... | collective-permute-start | bytes 393224 | tf_op jit(solution)/shard_map/ppermute | solution.py:249
  28.2 5.6 %collective-permute-start.5 = (bf16[128,512]{1,0:T(8,128)(2,1)S(1)}, bf16[128,512]{1,0:T(8,128)(2,1)S(1)}, u32[]{:S(2)}, u32[]{:S(2)}) collective-permute-start(bf16[128,512]{1,0:T(8,128)(2,1)S(1)} %get-tuple-element.57), channel_id=1, source_target_pairs={{0,2},{1,3},{2,0},{3,1},{4,6},{5,7},{6,4},{7,5},{8,10},{9,11},{10,... | collective-permute-start | bytes 393224 | tf_op jit(solution)/shard_map/ppermute | solution.py:249
  36.6 1.6 %collective-permute-start.10 = (bf16[16,16,512]{2,1,0:T(8,128)(2,1)S(1)}, bf16[16,16,512]{2,1,0:T(8,128)(2,1)S(1)}, u32[]{:S(2)}, u32[]{:S(2)}) collective-permute-start(bf16[16,16,512]{2,1,0:T(8,128)(2,1)S(1)} %get-tuple-element.72), channel_id=1, source_target_pairs={{0,8},{1,9},{2,10},{3,11},{4,12},{5,13},{6,14},{7,15},{8,0},{9,1},... | collective-permute-start | bytes 786440 | tf_op jit(solution)/shard_map/ppermute | solution.py:249
  38.3 7.0 %collective-permute-start.11 = (bf16[192,512]{1,0:T(8,128)(2,1)S(1)}, bf16[192,512]{1,0:T(8,128)(2,1)S(1)}, u32[]{:S(2)}, u32[]{:S(2)}) collective-permute-start(bf16[192,512]{1,0:T(8,128)(2,1)S(1)} %get-tuple-element.73), channel_id=1, source_target_pairs={{0,1},{1,0},{2,3},{3,2},{4,5},{5,4},{6,7},{7,6},{8,9},{9,8},{10,11... | collective-permute-start | bytes 589832 | tf_op jit(solution)/shard_map/ppermute | solution.py:249
  39.7 7.8 %collective-permute-start.12 = (bf16[192,512]{1,0:T(8,128)(2,1)S(1)}, bf16[192,512]{1,0:T(8,128)(2,1)S(1)}, u32[]{:S(2)}, u32[]{:S(2)}) collective-permute-start(bf16[192,512]{1,0:T(8,128)(2,1)S(1)} %get-tuple-element.74), channel_id=1, source_target_pairs={{0,2},{1,3},{2,0},{3,1},{4,6},{5,7},{6,4},{7,5},{8,10},{9,11},{10,... | collective-permute-start | bytes 589832 | tf_op jit(solution)/shard_map/ppermute | solution.py:249
  40.3 10.4 %collective-permute-start.13 = (bf16[192,512]{1,0:T(8,128)(2,1)S(1)}, bf16[192,512]{1,0:T(8,128)(2,1)S(1)}, u32[]{:S(2)}, u32[]{:S(2)}) collective-permute-start(bf16[192,512]{1,0:T(8,128)(2,1)S(1)} %get-tuple-element.75), channel_id=1, source_target_pairs={{0,3},{1,2},{2,1},{3,0},{4,7},{5,6},{6,5},{7,4},{8,11},{9,10},{10,... | collective-permute-start | bytes 589832 | tf_op jit(solution)/shard_map/ppermute | solution.py:249
  50.8 8.1 %collective-permute-start.14 = (f32[1,16,512]{2,1,0:T(8,128)S(1)}, f32[1,16,512]{2,1,0:T(8,128)S(1)}, u32[]{:S(2)}, u32[]{:S(2)}) collective-permute-start(f32[1,16,512]{2,1,0:T(8,128)S(1)} %get-tuple-element.78), channel_id=1, source_target_pairs={{0,4},{1,5},{2,6},{3,7},{4,0},{5,1},{6,2},{7,3},{8,12},{9,13},{10,... | collective-permute-start | bytes 98312 | tf_op jit(solution)/shard_map/ppermute | solution.py:249
  53.3 5.5 %collective-permute-start.15 = (f32[1,16,512]{2,1,0:T(8,128)S(1)}, f32[1,16,512]{2,1,0:T(8,128)S(1)}, u32[]{:S(2)}, u32[]{:S(2)}) collective-permute-start(f32[1,16,512]{2,1,0:T(8,128)S(1)} %get-tuple-element.79), channel_id=1, source_target_pairs={{0,16},{1,17},{2,18},{3,19},{4,20},{5,21},{6,22},{7,23},{8,24},{9,... | collective-permute-start | bytes 98312 | tf_op jit(solution)/shard_map/ppermute | solution.py:249
  54.8 5.7 %collective-permute-start.16 = (f32[1,16,512]{2,1,0:T(8,128)S(1)}, f32[1,16,512]{2,1,0:T(8,128)S(1)}, u32[]{:S(2)}, u32[]{:S(2)}) collective-permute-start(f32[1,16,512]{2,1,0:T(8,128)S(1)} %get-tuple-element.80), channel_id=1, source_target_pairs={{0,20},{1,21},{2,22},{3,23},{4,16},{5,17},{6,18},{7,19},{8,28},{9,... | collective-permute-start | bytes 98312 | tf_op jit(solution)/shard_map/ppermute | solution.py:249

commit v11 on v10

--- a/solution.py
+++ b/solution.py
@@ -181,22 +181,10 @@
     cut(blocks, bits, refs)
 
 
-def stage_kernel(bits, count, extra, *refs):
-    came, extras, (keep_ref, *sends, blocks) = refs[:count], refs[count : count + extra], refs[count + extra :]
-    shape = blocks.shape
-    total = came[0][...]
-    for ref in came[1:]:
-        total += ref[...][: shape[0] * shape[1]].reshape(shape).astype(f32)
-    blocks[...] = total
-    if not extra:
-        cut(blocks, bits, [keep_ref, *sends])
-        return
-    size = keep_ref.shape[0]
-    cut(blocks, bits, [keep_ref])
-    for step, (ref, rows) in enumerate(zip(sends, extras), 1):
-        part = blocks[pl.ds((coordinate(bits) ^ step) * size, size)]
-        ref[pl.ds(0, size * shape[1])] = part.reshape(size * shape[1], shape[2]).astype(ref.dtype)
-        ref[pl.ds(size * shape[1], rows.shape[0])] = rows[...]
+def stage_kernel(bits, count, *refs):
+    came, (*refs, blocks) = refs[:count], refs[count:]
+    blocks[...] = sum(ref[...].astype(f32) for ref in came)
+    cut(blocks, bits, refs)
 
 
 def last_kernel(*refs):
@@ -206,8 +194,7 @@
 
 def table_kernel(low_hot_ref, block_ref, weight_ref, *refs):
     *incoming, table_grad_hbm, ready, sems = refs
-    size = incoming[0].shape[0]
-    dhidden = jnp.concatenate([ref[pl.ds(ref.shape[0] - size, size)] for ref in incoming], axis=0)
+    dhidden = jnp.concatenate([ref[...] for ref in incoming], axis=0)
     drow = dot(dhidden, weight_ref[...], 1, 1).astype(bf16)
     groups = sems.shape[0]
     size = ready.shape[0] // groups
@@ -257,15 +244,14 @@
     return sum((lax.axis_size("item") if axis == "batch" else 1) << level for axis, level in bits)
 
 
-def reduce_scatter(fetched, dhidden):
+def reduce_scatter(fetched, dhidden, incoming):
     width = dhidden[0].shape[1]
     n_item, devices = lax.axis_size("item"), lax.axis_size("batch") * lax.axis_size("item")
     part = width // devices
     close = log2(len(dhidden))
     batch_bits, item_bits = bits_of("batch"), bits_of("item")
-    stages = [batch_bits[:1], item_bits[:close]]
     rest = batch_bits[1:] + item_bits[close:]
-    stages += [rest[k : k + 2] for k in range(0, len(rest), 2)]
+    stages = [batch_bits[:1]] + [rest[k : k + 2] for k in range(0, len(rest), 2)] + [item_bits[:close]]
     bits = sum(stages, [])
     order = []
     for spot in range(devices):
@@ -273,30 +259,26 @@
         for k, (axis, level) in enumerate(bits):
             at[axis] |= (spot >> (len(bits) - 1 - k) & 1) << level
         order.append(at["batch"] * n_item + at["item"])
-    left, values, back = devices, [*fetched, *dhidden], {}
+    left, values = devices, [*fetched, *dhidden]
     for k, stage in enumerate(stages):
         whole, left = left, left >> len(stage)
         masks = [
             mask_of([bit for j, bit in enumerate(reversed(stage)) if step >> j & 1]) for step in range(1, 1 << len(stage))
         ]
-        extras = [dhidden[mask] for mask in masks] if k == 1 else []
-        if k == 1:
-            sent = ((left * part + dhidden[0].shape[0], width), bf16)
-        else:
-            sent = ((left, part, width), f32 if k == len(stages) - 1 else bf16)
+        sent = f32 if k == len(stages) - 1 else bf16
         count = len(values)
-        kernel = functools.partial(stage_kernel, stage, count, len(extras)) if k else functools.partial(share_kernel, order, stage, count)
+        kernel = functools.partial(stage_kernel, stage, count) if k else functools.partial(share_kernel, order, stage, count)
         kept, *sends = call(
             kernel,
-            [((left, part, width), f32)] + [sent] * len(masks),
+            [((left, part, width), f32)] + [((left, part, width), sent)] * len(masks),
             *values,
-            *extras,
             scratch=[pltpu.VMEM((whole, part, width), f32)],
+            free=True,
         )
         values = [kept] + [swap(value, mask) for mask, value in zip(masks, sends)]
         if k == 1:
-            back = dict(zip(masks, values[1:]))
-    return values, [back[mask] for mask in range(1, len(dhidden))]
+            values, incoming = lax.optimization_barrier((values, incoming))
+    return values, incoming
 
 
 def local(user_vectors, item_table, tower_weight, item_owner, item_row):
@@ -349,11 +331,9 @@
         for part, value in zip(parts, values):
             fetched[part] = swap(value, part) if part else value
     late = [mask for mask in users if mask not in early]
-    fetched[0], fetched[near - 1], *values = lax.optimization_barrier(
-        (fetched[0], fetched[near - 1], *[users[mask] for mask in late])
-    )
-    users.update(zip(late, values))
-    fetched = [fetched[part] for part in range(near)]
+    values = [fetched[part] for part in range(near)] + [users[mask] for mask in late]
+    values = lax.optimization_barrier(tuple(values))
+    fetched, users = list(values[:near]), users | dict(zip(late, values[near:]))
 
     for mask in list(users):
         users[mask + n_item] = swap(users[mask], n_item)
@@ -386,7 +366,8 @@
         flops=1 << 31,
         mib=40,
     )
-    terms, incoming = reduce_scatter(fetched, dhidden)
+    incoming = [swap(dhidden[part], part) for part in range(1, near)]
+    terms, incoming = reduce_scatter(fetched, dhidden, incoming)
     table_grad = pl.pallas_call(
         table_kernel,
         out_specs=pl.BlockSpec(memory_space=pl.ANY),

time: 61.3 us -> 59 us (0.962)
  waiting for transfers between devices: 18.1 us -> 8.95 us
  starting transfers between devices: 17 us -> 23.8 us
    ppermute x17 -> x20, waiting for transfers between devices: 18.1 us -> 8.95 us  [swap(): lax.ppermute(value, ('batch', 'item'), [(k, k ^ mask) for k in range(devi...]
    ppermute x17 -> x20, starting transfers between devices: 17 us -> 23.8 us  [swap(): lax.ppermute(value, ('batch', 'item'), [(k, k ^ mask) for k in range(devi...]
  transfers between devices with their start and end apart: 17 -> 20, of which waited for: 8 -> 5; matrix products, arithmetic and copies ran while one was open for 1% -> 1% of each run, Pallas kernels for 15% -> 15%
where the time goes in v11:
time: 59 us; the launch traced here: 58.8 us
  starting transfers between devices  23.8 us (40%)
  Pallas kernels  12.8 us (22%)
  blocking collectives  11.7 us (20%)
  waiting for transfers between devices  8.95 us (15%)
  between operations  0.81 us (1%)
  other arithmetic  0.7 us (1%)
    ppermute x20, starting transfers between devices, swap(): lax.ppermute(value, ('batch', 'item'), [(k, k ^ mask) for k in range(devi...  23.8 us
    all_to_all x1, blocking collectives, local(): lax.all_to_all(request, ('batch', 'item'), split_axis=0, concat_axis=0, t...  11.7 us
    pallas_call x12, Pallas kernels, call(): pl.pallas_call(kernel, out_shape=[jax.ShapeDtypeStruct(shape, dtype) for...  9.24 us
    ppermute x20, waiting for transfers between devices, swap(): lax.ppermute(value, ('batch', 'item'), [(k, k ^ mask) for k in range(devi...  8.95 us
    pallas_call x1, Pallas kernels, local(): pl.pallas_call(table_kernel, out_specs=pl.BlockSpec(memory_space=pl.ANY),...  3.58 us
  transfers between devices with their start and end apart: 20, of which 5 were waited for; matrix products, arithmetic and copies ran while one was open for 1% of the time, Pallas kernels for 15%

profile of v11, /device:TPU:0, one launch (start us, length us, event | category | flops | bytes accessed | tf_op | source)
XLA Modules:
  0.0 58.8 jit_solution(13629337743772381396)
XLA Ops:
  0.6 4.1 %collective-permute-start = (bf16[256,512]{1,0:T(8,128)(2,1)}, bf16[256,512]{1,0:T(8,128)(2,1)S(1)}, u32[]{:S(2)}, u32[]{:S(2)}) collective-permute-start(bf16[256,512]{1,0:T(8,128)(2,1)} %refs_0_), channel_id=1, source_target_pairs={{0,4},{1,5},{2,6},{3,7},{4,0},{5,1},{6,2},{7,3},{8,12},{9,13},{10,... | collective-permute-start | bytes 786440 | tf_op jit(solution)/shard_map/ppermute | solution.py:236
  4.7 1.5 %collective-permute-start.1 = (bf16[256,512]{1,0:T(8,128)(2,1)}, bf16[256,512]{1,0:T(8,128)(2,1)S(1)}, u32[]{:S(2)}, u32[]{:S(2)}) collective-permute-start(bf16[256,512]{1,0:T(8,128)(2,1)} %refs_0_), channel_id=1, source_target_pairs={{0,16},{1,17},{2,18},{3,19},{4,20},{5,21},{6,22},{7,23},{8,24},{9,... | collective-permute-start | bytes 786440 | tf_op jit(solution)/shard_map/ppermute | solution.py:236
  6.2 0.7 %pad_add_fusion.named_ref = s32[2,256]{1,0:T(2,128)S(1)} fusion(s32[1,256]{1,0:T(1,128)} %bitcast.11, s32[1,256]{1,0:T(1,128)} %bitcast.12), kind=kLoop, calls=%fused_computation | loop fusion | flops 512 | bytes 4096 | tf_op jit(solution)/shard_map/stack | solution.py:304
  7.4 11.7 %all_to_all.12 = s32[32,1,80]{2,1,0:T(1,128)S(1)} all-to-all(s32[32,1,80]{2,1,0:T(1,128)S(1)} %bitcast.10), channel_id=1, replica_groups=mesh['batch'=4,'item'=8] {'batch','item'}, dimensions={0} | all-to-all | bytes 20480 | tf_op jit(solution)/shard_map/all_to_all | solution.py:307
  19.1 0.6 collective-permute-start.5
  19.7 0.9 %shard_map.69 = bf16[128,512]{1,0:T(8,128)(2,1)S(1)} custom-call(s32[32,80]{1,0:T(8,128)S(1)} %bitcast.6, bf16[4096,512]{1,0:T(8,128)(2,1)S(1)} %copy-done), custom_call_target="tpu_custom_call" | custom-call | flops 536870912 | bytes 1048576 | tf_op jit(solution)/shard_map/pallas_call | solution.py:225
  20.6 0.8 %collective-permute-start.4 = (bf16[128,512]{1,0:T(8,128)(2,1)S(1)}, bf16[128,512]{1,0:T(8,128)(2,1)S(1)}, u32[]{:S(2)}, u32[]{:S(2)}) collective-permute-start(bf16[128,512]{1,0:T(8,128)(2,1)S(1)} %shard_map.69), channel_id=1, source_target_pairs={{0,3},{1,2},{2,1},{3,0},{4,7},{5,6},{6,5},{7,4},{8,11},{9,10},{10,... | collective-permute-start | bytes 393224 | tf_op jit(solution)/shard_map/ppermute | solution.py:236
  21.4 1.6 %shard_map.70 = (bf16[128,512]{1,0:T(8,128)(2,1)S(1)}, bf16[128,512]{1,0:T(8,128)(2,1)S(1)}) custom-call(s32[32,80]{1,0:T(8,128)S(1)} %bitcast.7, bf16[4096,512]{1,0:T(8,128)(2,1)S(1)} %copy-done), custom_call_target="tpu_custom_call" | custom-call | flops 1073741824 | bytes 1048576 | tf_op jit(solution)/shard_map/pallas_call | solution.py:225
  23.0 1.3 %collective-permute-start.2 = (bf16[128,512]{1,0:T(8,128)(2,1)S(1)}, bf16[128,512]{1,0:T(8,128)(2,1)S(1)}, u32[]{:S(2)}, u32[]{:S(2)}) collective-permute-start(bf16[128,512]{1,0:T(8,128)(2,1)S(1)} %get-tuple-element.62), channel_id=1, source_target_pairs={{0,1},{1,0},{2,3},{3,2},{4,5},{5,4},{6,7},{7,6},{8,9},{9,8},{10,11... | collective-permute-start | bytes 393224 | tf_op jit(solution)/shard_map/ppermute | solution.py:236
  24.4 1.5 %collective-permute-start.3 = (bf16[128,512]{1,0:T(8,128)(2,1)S(1)}, bf16[128,512]{1,0:T(8,128)(2,1)S(1)}, u32[]{:S(2)}, u32[]{:S(2)}) collective-permute-start(bf16[128,512]{1,0:T(8,128)(2,1)S(1)} %get-tuple-element.63), channel_id=1, source_target_pairs={{0,2},{1,3},{2,0},{3,1},{4,6},{5,7},{6,4},{7,5},{8,10},{9,11},{10,... | collective-permute-start | bytes 393224 | tf_op jit(solution)/shard_map/ppermute | solution.py:236
  25.8 0.9 %shard_map.71.refs_0_ = bf16[128,512]{1,0:T(8,128)(2,1)S(1)} custom-call(s32[32,80]{1,0:T(8,128)S(1)} %bitcast.8, bf16[4096,512]{1,0:T(8,128)(2,1)S(1)} %copy-done), custom_call_target="tpu_custom_call" | custom-call | flops 536870912 | bytes 1048576 | tf_op jit(solution)/shard_map/pallas_call | solution.py:225
  26.8 0.5 collective-permute-start.6
  27.3 2.1 %collective-permute-done.2.refs_1_ = bf16[128,512]{1,0:T(8,128)(2,1)S(1)} collective-permute-done((bf16[128,512]{1,0:T(8,128)(2,1)S(1)}, bf16[128,512]{1,0:T(8,128)(2,1)S(1)}, u32[]{:S(2)}, u32[]{:S(2)}) %collective-permute-start.2) | collective-permute-done | bytes 131104 | tf_op jit(solution)/shard_map/ppermute | solution.py:236
  29.4 0.5 collective-permute-start.9
  29.9 0.4 shard_map.72
  30.3 0.6 collective-permute-done.7.refs_3_
  30.9 0.7 %shard_map.73 = (bf16[1024,512]{1,0:T(8,128)(2,1)S(1)}, bf16[256,512]{1,0:T(8,128)(2,1)S(1)}) custom-call(s32[512,1]{1,0:T(8,128)S(1)} %get-tuple-element.70.place_ref, bf16[256,512]{1,0:T(8,128)(2,1)S(1)} %copy-done.1, bf16[256,512]{1,0:T(8,128)(2,1)S(1)} %collective-permute-done.6.refs_1_, bf16[256,512]{1,0:T(8,128)(2,1)S(1)} %collective-permute-done.1.refs_2_, ...), custom_call_target="tpu_custom_call" | custom-call | tf_op jit(solution)/shard_map/pallas_call | solution.py:225
  31.7 0.7 %shard_map.74 = (bf16[1024,512]{1,0:T(8,128)(2,1)S(1)}, bf16[256,512]{1,0:T(8,128)(2,1)S(1)}) custom-call(s32[512,1]{1,0:T(8,128)S(1)} %get-tuple-element.70.place_ref, bf16[256,512]{1,0:T(8,128)(2,1)S(1)} %collective-permute-done.refs_0_, bf16[256,512]{1,0:T(8,128)(2,1)S(1)} %collective-permute-done.8.refs_1_, ...), custom_call_target="tpu_custom_call" | custom-call | tf_op jit(solution)/shard_map/pallas_call | solution.py:225
  32.4 2.3 %shard_map.75 = (bf16[128,512]{1,0:T(8,128)(2,1)S(1)}, bf16[128,512]{1,0:T(8,128)(2,1)S(1)}, bf16[128,512]{1,0:T(8,128)(2,1)S(1)}, bf16[128,512]{1,0:T(8,128)(2,1)S(1)}) custom-call(bf16[512,512]{1,0:T(8,128)(2,1)S(1)} %copy-done.2, bf16[128,512]{1,0:T(8,128)(2,1)S(1)} %shard_map.71.refs_0_, bf16[128,512]{1,0:T(8,128)(2,1)S(1)} %collective-permute-done.2.refs_1_, ...), custom_call_target="tpu_custom_call" | custom-call | flops 2147483648 | bytes 1048576 | tf_op jit(solution)/shard_map/pallas_call | solution.py:225
  34.7 0.5 shard_map.76
  35.4 0.8 %collective-permute-start.14 = (bf16[128,512]{1,0:T(8,128)(2,1)S(1)}, bf16[128,512]{1,0:T(8,128)(2,1)S(1)}, u32[]{:S(2)}, u32[]{:S(2)}) collective-permute-start(bf16[128,512]{1,0:T(8,128)(2,1)S(1)} %get-tuple-element.79.refs_5_), channel_id=1, source_target_pairs={{0,1},{1,0},{2,3},{3,2},{4,5},{5,4},{6,7},{7,6},{8,9},{9,8},{10,11... | collective-permute-start | bytes 393224 | tf_op jit(solution)/shard_map/ppermute | solution.py:236
  36.2 0.7 %collective-permute-start.15 = (bf16[128,512]{1,0:T(8,128)(2,1)S(1)}, bf16[128,512]{1,0:T(8,128)(2,1)S(1)}, u32[]{:S(2)}, u32[]{:S(2)}) collective-permute-start(bf16[128,512]{1,0:T(8,128)(2,1)S(1)} %get-tuple-element.80.refs_6_), channel_id=1, source_target_pairs={{0,2},{1,3},{2,0},{3,1},{4,6},{5,7},{6,4},{7,5},{8,10},{9,11},{10,... | collective-permute-start | bytes 393224 | tf_op jit(solution)/shard_map/ppermute | solution.py:236
  36.9 2.0 %collective-permute-start.16 = (bf16[128,512]{1,0:T(8,128)(2,1)S(1)}, bf16[128,512]{1,0:T(8,128)(2,1)S(1)}, u32[]{:S(2)}, u32[]{:S(2)}) collective-permute-start(bf16[128,512]{1,0:T(8,128)(2,1)S(1)} %get-tuple-element.81.refs_7_), channel_id=1, source_target_pairs={{0,3},{1,2},{2,1},{3,0},{4,7},{5,6},{6,5},{7,4},{8,11},{9,10},{10,... | collective-permute-start | bytes 393224 | tf_op jit(solution)/shard_map/ppermute | solution.py:236
  39.0 2.9 %collective-permute-start.11 = (bf16[4,16,512]{2,1,0:T(8,128)(2,1)S(1)}, bf16[4,16,512]{2,1,0:T(8,128)(2,1)S(1)}, u32[]{:S(2)}, u32[]{:S(2)}) collective-permute-start(bf16[4,16,512]{2,1,0:T(8,128)(2,1)S(1)} %get-tuple-element.85), channel_id=1, source_target_pairs={{0,4},{1,5},{2,6},{3,7},{4,0},{5,1},{6,2},{7,3},{8,12},{9,13},{10,... | collective-permute-start | bytes 196616 | tf_op jit(solution)/shard_map/ppermute | solution.py:236
  41.9 1.4 %collective-permute-start.12 = (bf16[4,16,512]{2,1,0:T(8,128)(2,1)S(1)}, bf16[4,16,512]{2,1,0:T(8,128)(2,1)S(1)}, u32[]{:S(2)}, u32[]{:S(2)}) collective-permute-start(bf16[4,16,512]{2,1,0:T(8,128)(2,1)S(1)} %get-tuple-element.86), channel_id=1, source_target_pairs={{0,16},{1,17},{2,18},{3,19},{4,20},{5,21},{6,22},{7,23},{8,24},{9,... | collective-permute-start | bytes 196616 | tf_op jit(solution)/shard_map/ppermute | solution.py:236
  43.3 1.5 %collective-permute-start.13 = (bf16[4,16,512]{2,1,0:T(8,128)(2,1)S(1)}, bf16[4,16,512]{2,1,0:T(8,128)(2,1)S(1)}, u32[]{:S(2)}, u32[]{:S(2)}) collective-permute-start(bf16[4,16,512]{2,1,0:T(8,128)(2,1)S(1)} %get-tuple-element.87), channel_id=1, source_target_pairs={{0,20},{1,21},{2,22},{3,23},{4,16},{5,17},{6,18},{7,19},{8,28},{9,... | collective-permute-start | bytes 196616 | tf_op jit(solution)/shard_map/ppermute | solution.py:236
  44.7 2.6 %collective-permute-done.16.refs_3_ = bf16[128,512]{1,0:T(8,128)(2,1)S(1)} collective-permute-done((bf16[128,512]{1,0:T(8,128)(2,1)S(1)}, bf16[128,512]{1,0:T(8,128)(2,1)S(1)}, u32[]{:S(2)}, u32[]{:S(2)}) %collective-permute-start.16) | collective-permute-done | bytes 131104 | tf_op jit(solution)/shard_map/ppermute | solution.py:236
  47.3 3.7 %collective-permute-done.13.refs_3_ = bf16[4,16,512]{2,1,0:T(8,128)(2,1)S(1)} collective-permute-done((bf16[4,16,512]{2,1,0:T(8,128)(2,1)S(1)}, bf16[4,16,512]{2,1,0:T(8,128)(2,1)S(1)}, u32[]{:S(2)}, u32[]{:S(2)}) %collective-permute-start.13) | collective-permute-done | bytes 65568 | tf_op jit(solution)/shard_map/ppermute | solution.py:236
  51.1 1.2 %collective-permute-start.18 = (f32[1,16,512]{2,1,0:T(8,128)S(1)}, f32[1,16,512]{2,1,0:T(8,128)S(1)}, u32[]{:S(2)}, u32[]{:S(2)}) collective-permute-start(f32[1,16,512]{2,1,0:T(8,128)S(1)} %get-tuple-element.97), channel_id=1, source_target_pairs={{0,1},{1,0},{2,3},{3,2},{4,5},{5,4},{6,7},{7,6},{8,9},{9,8},{10,11... | collective-permute-start | bytes 98312 | tf_op jit(solution)/shard_map/ppermute | solution.py:236
  52.3 2.3 %collective-permute-start.19 = (f32[1,16,512]{2,1,0:T(8,128)S(1)}, f32[1,16,512]{2,1,0:T(8,128)S(1)}, u32[]{:S(2)}, u32[]{:S(2)}) collective-permute-start(f32[1,16,512]{2,1,0:T(8,128)S(1)} %get-tuple-element.98), channel_id=1, source_target_pairs={{0,3},{1,2},{2,1},{3,0},{4,7},{5,6},{6,5},{7,4},{8,11},{9,10},{10,... | collective-permute-start | bytes 98312 | tf_op jit(solution)/shard_map/ppermute | solution.py:236
  54.6 3.6 %shard_map.78 = bf16[4096,512]{1,0:T(8,128)(2,1)} custom-call(bf16[256,512]{1,0:T(8,128)(2,1)S(1)} %get-tuple-element.59.low_hot_ref, bf16[256,512]{1,0:T(8,128)(2,1)S(1)} %get-tuple-element.60.block_ref, bf16[512,512]{1,0:T(8,128)(2,1)S(1)} %copy-done.2, bf16[128,512]{1,0:T(8,128)(2,1)S(1)} %get-tuple-element.78.refs_4_.refs_0_, ...), custom_call_target="tpu_custom_call" | custom-call | flops 2147483648 | bytes 4194304 | tf_op jit(solution)/shard_map/pallas_call | solution.py:371
  58.2 0.6 %shard_map.80 = f32[16,512]{1,0:T(8,128)} custom-call(f32[1,16,512]{2,1,0:T(8,128)S(1)} %get-tuple-element.100.refs_0_, f32[1,16,512]{2,1,0:T(8,128)S(1)} %collective-permute-done.17.refs_1_, f32[1,16,512]{2,1,0:T(8,128)S(1)} %collective-permute-done.18.refs_2_, f32[1,16,512]{2,1,0:T(8,128)S(1)} %collective-permute-done.19.refs_3_), custom_call_target="tpu_custom_call" | custom-call | bytes 1048576 | tf_op jit(solution)/shard_map/pallas_call | solution.py:225
  (29 shorter events, 1.0 us)
Async XLA Ops:
  0.6 18.4 %collective-permute-start = (bf16[256,512]{1,0:T(8,128)(2,1)}, bf16[256,512]{1,0:T(8,128)(2,1)S(1)}, u32[]{:S(2)}, u32[]{:S(2)}) collective-permute-start(bf16[256,512]{1,0:T(8,128)(2,1)} %refs_0_), channel_id=1, source_target_pairs={{0,4},{1,5},{2,6},{3,7},{4,0},{5,1},{6,2},{7,3},{8,12},{9,13},{10,... | collective-permute-start | bytes 786440 | tf_op jit(solution)/shard_map/ppermute | solution.py:236
  4.7 14.4 %collective-permute-start.1 = (bf16[256,512]{1,0:T(8,128)(2,1)}, bf16[256,512]{1,0:T(8,128)(2,1)S(1)}, u32[]{:S(2)}, u32[]{:S(2)}) collective-permute-start(bf16[256,512]{1,0:T(8,128)(2,1)} %refs_0_), channel_id=1, source_target_pairs={{0,16},{1,17},{2,18},{3,19},{4,20},{5,21},{6,22},{7,23},{8,24},{9,... | collective-permute-start | bytes 786440 | tf_op jit(solution)/shard_map/ppermute | solution.py:236
  6.9 12.7 %copy-start = (bf16[4096,512]{1,0:T(8,128)(2,1)S(1)}, bf16[4096,512]{1,0:T(8,128)(2,1)}, u32[]{:S(2)}) copy-start(bf16[4096,512]{1,0:T(8,128)(2,1)} %table_ref.5) | copy-start | bytes 12582916
  19.1 10.3 %collective-permute-start.5 = (bf16[256,512]{1,0:T(8,128)(2,1)S(1)}, bf16[256,512]{1,0:T(8,128)(2,1)S(1)}, u32[]{:S(2)}, u32[]{:S(2)}) collective-permute-start(bf16[256,512]{1,0:T(8,128)(2,1)S(1)} %collective-permute-done.refs_0_), channel_id=1, source_target_pairs={{0,16},{1,17},{2,18},{3,19},{4,20},{5,21},{6,22},{7,23},{8,24},{9,... | collective-permute-start | bytes 786440 | tf_op jit(solution)/shard_map/ppermute | solution.py:236
  20.6 6.2 %copy-start.1 = (bf16[256,512]{1,0:T(8,128)(2,1)S(1)}, bf16[256,512]{1,0:T(8,128)(2,1)}, u32[]{:S(2)}) copy-start(bf16[256,512]{1,0:T(8,128)(2,1)} %refs_0_) | copy-start | bytes 786436
  20.6 6.2 %collective-permute-start.4 = (bf16[128,512]{1,0:T(8,128)(2,1)S(1)}, bf16[128,512]{1,0:T(8,128)(2,1)S(1)}, u32[]{:S(2)}, u32[]{:S(2)}) collective-permute-start(bf16[128,512]{1,0:T(8,128)(2,1)S(1)} %shard_map.69), channel_id=1, source_target_pairs={{0,3},{1,2},{2,1},{3,0},{4,7},{5,6},{6,5},{7,4},{8,11},{9,10},{10,... | collective-permute-start | bytes 393224 | tf_op jit(solution)/shard_map/ppermute | solution.py:236
  23.0 9.4 %copy-start.2 = (bf16[512,512]{1,0:T(8,128)(2,1)S(1)}, bf16[512,512]{1,0:T(8,128)(2,1)}, u32[]{:S(2)}) copy-start(bf16[512,512]{1,0:T(8,128)(2,1)} %weight_ref.3) | copy-start | bytes 1572868
  23.0 6.4 %collective-permute-start.2 = (bf16[128,512]{1,0:T(8,128)(2,1)S(1)}, bf16[128,512]{1,0:T(8,128)(2,1)S(1)}, u32[]{:S(2)}, u32[]{:S(2)}) collective-permute-start(bf16[128,512]{1,0:T(8,128)(2,1)S(1)} %get-tuple-element.62), channel_id=1, source_target_pairs={{0,1},{1,0},{2,3},{3,2},{4,5},{5,4},{6,7},{7,6},{8,9},{9,8},{10,11... | collective-permute-start | bytes 393224 | tf_op jit(solution)/shard_map/ppermute | solution.py:236
  24.4 5.0 %collective-permute-start.3 = (bf16[128,512]{1,0:T(8,128)(2,1)S(1)}, bf16[128,512]{1,0:T(8,128)(2,1)S(1)}, u32[]{:S(2)}, u32[]{:S(2)}) collective-permute-start(bf16[128,512]{1,0:T(8,128)(2,1)S(1)} %get-tuple-element.63), channel_id=1, source_target_pairs={{0,2},{1,3},{2,0},{3,1},{4,6},{5,7},{6,4},{7,5},{8,10},{9,11},{10,... | collective-permute-start | bytes 393224 | tf_op jit(solution)/shard_map/ppermute | solution.py:236
  25.8 5.8 %collective-permute-start.8 = (bf16[256,512]{1,0:T(8,128)(2,1)S(1)}, bf16[256,512]{1,0:T(8,128)(2,1)S(1)}, u32[]{:S(2)}, u32[]{:S(2)}) collective-permute-start(bf16[256,512]{1,0:T(8,128)(2,1)S(1)} %collective-permute-done.refs_0_), channel_id=1, source_target_pairs={{0,8},{1,9},{2,10},{3,11},{4,12},{5,13},{6,14},{7,15},{8,0},{9,1},... | collective-permute-start | bytes 786440 | tf_op jit(solution)/shard_map/ppermute | solution.py:236
  26.8 3.5 %collective-permute-start.6 = (bf16[256,512]{1,0:T(8,128)(2,1)S(1)}, bf16[256,512]{1,0:T(8,128)(2,1)S(1)}, u32[]{:S(2)}, u32[]{:S(2)}) collective-permute-start(bf16[256,512]{1,0:T(8,128)(2,1)S(1)} %copy-done.1), channel_id=1, source_target_pairs={{0,8},{1,9},{2,10},{3,11},{4,12},{5,13},{6,14},{7,15},{8,0},{9,1},... | collective-permute-start | bytes 786440 | tf_op jit(solution)/shard_map/ppermute | solution.py:236
  29.4 1.5 %collective-permute-start.7 = (bf16[256,512]{1,0:T(8,128)(2,1)S(1)}, bf16[256,512]{1,0:T(8,128)(2,1)S(1)}, u32[]{:S(2)}, u32[]{:S(2)}) collective-permute-start(bf16[256,512]{1,0:T(8,128)(2,1)S(1)} %collective-permute-done.1.refs_2_), channel_id=1, source_target_pairs={{0,8},{1,9},{2,10},{3,11},{4,12},{5,13},{6,14},{7,15},{8,0},{9,1},... | collective-permute-start | bytes 786440 | tf_op jit(solution)/shard_map/ppermute | solution.py:236
  29.4 2.3 %collective-permute-start.9 = (bf16[256,512]{1,0:T(8,128)(2,1)S(1)}, bf16[256,512]{1,0:T(8,128)(2,1)S(1)}, u32[]{:S(2)}, u32[]{:S(2)}) collective-permute-start(bf16[256,512]{1,0:T(8,128)(2,1)S(1)} %collective-permute-done.5.refs_2_), channel_id=1, source_target_pairs={{0,8},{1,9},{2,10},{3,11},{4,12},{5,13},{6,14},{7,15},{8,0},{9,1},... | collective-permute-start | bytes 786440 | tf_op jit(solution)/shard_map/ppermute | solution.py:236
  35.2 3.7 %collective-permute-start.10 = (bf16[16,16,512]{2,1,0:T(8,128)(2,1)S(1)}, bf16[16,16,512]{2,1,0:T(8,128)(2,1)S(1)}, u32[]{:S(2)}, u32[]{:S(2)}) collective-permute-start(bf16[16,16,512]{2,1,0:T(8,128)(2,1)S(1)} %get-tuple-element.83), channel_id=1, source_target_pairs={{0,8},{1,9},{2,10},{3,11},{4,12},{5,13},{6,14},{7,15},{8,0},{9,1},... | collective-permute-start | bytes 786440 | tf_op jit(solution)/shard_map/ppermute | solution.py:236
  35.4 7.8 %collective-permute-start.14 = (bf16[128,512]{1,0:T(8,128)(2,1)S(1)}, bf16[128,512]{1,0:T(8,128)(2,1)S(1)}, u32[]{:S(2)}, u32[]{:S(2)}) collective-permute-start(bf16[128,512]{1,0:T(8,128)(2,1)S(1)} %get-tuple-element.79.refs_5_), channel_id=1, source_target_pairs={{0,1},{1,0},{2,3},{3,2},{4,5},{5,4},{6,7},{7,6},{8,9},{9,8},{10,11... | collective-permute-start | bytes 393224 | tf_op jit(solution)/shard_map/ppermute | solution.py:236
  36.2 8.5 %collective-permute-start.15 = (bf16[128,512]{1,0:T(8,128)(2,1)S(1)}, bf16[128,512]{1,0:T(8,128)(2,1)S(1)}, u32[]{:S(2)}, u32[]{:S(2)}) collective-permute-start(bf16[128,512]{1,0:T(8,128)(2,1)S(1)} %get-tuple-element.80.refs_6_), channel_id=1, source_target_pairs={{0,2},{1,3},{2,0},{3,1},{4,6},{5,7},{6,4},{7,5},{8,10},{9,11},{10,... | collective-permute-start | bytes 393224 | tf_op jit(solution)/shard_map/ppermute | solution.py:236
  36.9 10.4 %collective-permute-start.16 = (bf16[128,512]{1,0:T(8,128)(2,1)S(1)}, bf16[128,512]{1,0:T(8,128)(2,1)S(1)}, u32[]{:S(2)}, u32[]{:S(2)}) collective-permute-start(bf16[128,512]{1,0:T(8,128)(2,1)S(1)} %get-tuple-element.81.refs_7_), channel_id=1, source_target_pairs={{0,3},{1,2},{2,1},{3,0},{4,7},{5,6},{6,5},{7,4},{8,11},{9,10},{10,... | collective-permute-start | bytes 393224 | tf_op jit(solution)/shard_map/ppermute | solution.py:236
  39.0 8.3 %collective-permute-start.11 = (bf16[4,16,512]{2,1,0:T(8,128)(2,1)S(1)}, bf16[4,16,512]{2,1,0:T(8,128)(2,1)S(1)}, u32[]{:S(2)}, u32[]{:S(2)}) collective-permute-start(bf16[4,16,512]{2,1,0:T(8,128)(2,1)S(1)} %get-tuple-element.85), channel_id=1, source_target_pairs={{0,4},{1,5},{2,6},{3,7},{4,0},{5,1},{6,2},{7,3},{8,12},{9,13},{10,... | collective-permute-start | bytes 196616 | tf_op jit(solution)/shard_map/ppermute | solution.py:236
  41.9 5.4 %collective-permute-start.12 = (bf16[4,16,512]{2,1,0:T(8,128)(2,1)S(1)}, bf16[4,16,512]{2,1,0:T(8,128)(2,1)S(1)}, u32[]{:S(2)}, u32[]{:S(2)}) collective-permute-start(bf16[4,16,512]{2,1,0:T(8,128)(2,1)S(1)} %get-tuple-element.86), channel_id=1, source_target_pairs={{0,16},{1,17},{2,18},{3,19},{4,20},{5,21},{6,22},{7,23},{8,24},{9,... | collective-permute-start | bytes 196616 | tf_op jit(solution)/shard_map/ppermute | solution.py:236
  43.3 7.7 %collective-permute-start.13 = (bf16[4,16,512]{2,1,0:T(8,128)(2,1)S(1)}, bf16[4,16,512]{2,1,0:T(8,128)(2,1)S(1)}, u32[]{:S(2)}, u32[]{:S(2)}) collective-permute-start(bf16[4,16,512]{2,1,0:T(8,128)(2,1)S(1)} %get-tuple-element.87), channel_id=1, source_target_pairs={{0,20},{1,21},{2,22},{3,23},{4,16},{5,17},{6,18},{7,19},{8,28},{9,... | collective-permute-start | bytes 196616 | tf_op jit(solution)/shard_map/ppermute | solution.py:236
  51.0 7.2 %collective-permute-start.17 = (f32[1,16,512]{2,1,0:T(8,128)S(1)}, f32[1,16,512]{2,1,0:T(8,128)S(1)}, u32[]{:S(2)}, u32[]{:S(2)}) collective-permute-start(f32[1,16,512]{2,1,0:T(8,128)S(1)} %get-tuple-element.96), channel_id=1, source_target_pairs={{0,2},{1,3},{2,0},{3,1},{4,6},{5,7},{6,4},{7,5},{8,10},{9,11},{10,... | collective-permute-start | bytes 98312 | tf_op jit(solution)/shard_map/ppermute | solution.py:236
  51.1 7.1 %collective-permute-start.18 = (f32[1,16,512]{2,1,0:T(8,128)S(1)}, f32[1,16,512]{2,1,0:T(8,128)S(1)}, u32[]{:S(2)}, u32[]{:S(2)}) collective-permute-start(f32[1,16,512]{2,1,0:T(8,128)S(1)} %get-tuple-element.97), channel_id=1, source_target_pairs={{0,1},{1,0},{2,3},{3,2},{4,5},{5,4},{6,7},{7,6},{8,9},{9,8},{10,11... | collective-permute-start | bytes 98312 | tf_op jit(solution)/shard_map/ppermute | solution.py:236
  52.3 5.9 %collective-permute-start.19 = (f32[1,16,512]{2,1,0:T(8,128)S(1)}, f32[1,16,512]{2,1,0:T(8,128)S(1)}, u32[]{:S(2)}, u32[]{:S(2)}) collective-permute-start(f32[1,16,512]{2,1,0:T(8,128)S(1)} %get-tuple-element.98), channel_id=1, source_target_pairs={{0,3},{1,2},{2,1},{3,0},{4,7},{5,6},{6,5},{7,4},{8,11},{9,10},{10,... | collective-permute-start | bytes 98312 | tf_op jit(solution)/shard_map/ppermute | solution.py:236

commit v12 on v11

--- a/solution.py
+++ b/solution.py
@@ -134,18 +134,28 @@
     own_ref[...] = dot(hot(place == iota((place.shape[0], unit_ref.shape[0]), 1)), unit_ref[...]).astype(bf16)
 
 
-def main_kernel(levels, weight_ref, *refs):
-    parts = (len(refs) - 2 * levels) // 2
-    fetched, units, owns, outs = refs[:parts], refs[parts : parts + levels], refs[parts + levels : parts + 2 * levels], refs[-parts:]
+def hidden_kernel(levels, weight_ref, *refs):
+    *fetched, hidden_ref, rscale_ref, item_ref = refs
     width = weight_ref.shape[0]
+    size = fetched[0].shape[0] // levels
+    for level in range(levels):
+        embed = jnp.concatenate([ref[pl.ds(level * size, size)] for ref in fetched], axis=0)
+        here = pl.ds(level * embed.shape[0], embed.shape[0])
+        hidden = dot(embed, weight_ref[...])
+        rscale = lax.rsqrt(jnp.mean(hidden * hidden, axis=1, keepdims=True) + epsilon)
+        hidden_ref[here] = hidden
+        rscale_ref[here] = rscale
+        item_ref[here] = (hidden * (rscale * (1.0 / width**0.5))).astype(bf16)
+
+
+def main_kernel(levels, hidden_ref, rscale_ref, item_ref, *refs):
+    units, owns, outs = refs[:levels], refs[levels : 2 * levels], refs[2 * levels :]
+    total, width = hidden_ref.shape
     size = outs[0].shape[0] // levels
     root = 1.0 / width**0.5
     for level in range(levels):
-        here = pl.ds(level * size, size)
-        embed = jnp.concatenate([ref[here] for ref in fetched], axis=0)
-        hidden = dot(embed, weight_ref[...])
-        rscale = lax.rsqrt(jnp.mean(hidden * hidden, axis=1, keepdims=True) + epsilon)
-        item_vec = (hidden * (rscale * root)).astype(bf16)
+        here = pl.ds(level * (total // levels), total // levels)
+        hidden, rscale, item_vec = hidden_ref[here], rscale_ref[here], item_ref[here]
         unit = units[level][...]
         expo = jnp.exp(dot(item_vec, unit, 1, 1) * score_scale)
         sums = jnp.sum(expo, axis=1, keepdims=True)
@@ -158,7 +168,7 @@
         inner = jnp.sum(hidden * dvec, axis=1, keepdims=True)
         dhidden = (rscale * root * (dvec - hidden * (rscale * rscale * inner * (1.0 / width)))).astype(bf16)
         for part, ref in enumerate(outs):
-            ref[here] = dhidden[part * size : (part + 1) * size]
+            ref[pl.ds(level * size, size)] = dhidden[part * size : (part + 1) * size]
 
 
 def coordinate(bits):
@@ -248,11 +258,9 @@
     width = dhidden[0].shape[1]
     n_item, devices = lax.axis_size("item"), lax.axis_size("batch") * lax.axis_size("item")
     part = width // devices
-    close = log2(len(dhidden))
-    batch_bits, item_bits = bits_of("batch"), bits_of("item")
-    rest = batch_bits[1:] + item_bits[close:]
-    stages = [batch_bits[:1]] + [rest[k : k + 2] for k in range(0, len(rest), 2)] + [item_bits[:close]]
-    bits = sum(stages, [])
+    bits = bits_of("batch") + bits_of("item")
+    odd = len(bits) % 2
+    stages = [bits[:1]] * odd + [bits[k : k + 2] for k in range(odd, len(bits), 2)]
     order = []
     for spot in range(devices):
         at = {"batch": 0, "item": 0}
@@ -331,9 +339,9 @@
         for part, value in zip(parts, values):
             fetched[part] = swap(value, part) if part else value
     late = [mask for mask in users if mask not in early]
-    values = [fetched[part] for part in range(near)] + [users[mask] for mask in late]
-    values = lax.optimization_barrier(tuple(values))
-    fetched, users = list(values[:near]), users | dict(zip(late, values[near:]))
+    fetched[0], *values = lax.optimization_barrier((fetched[0], *[users[mask] for mask in late]))
+    users.update(zip(late, values))
+    fetched = [fetched[part] for part in range(near)]
 
     for mask in list(users):
         users[mask + n_item] = swap(users[mask], n_item)
@@ -356,11 +364,17 @@
             for level in range(levels)
         ]
     )
+    hidden = call(
+        functools.partial(hidden_kernel, levels),
+        [((total, width), f32), ((total, 1), f32), ((total, width), bf16)],
+        tower_weight,
+        *fetched,
+        flops=1 << 32,
+    )
     dhidden = call(
         functools.partial(main_kernel, levels),
         [((size, width), bf16)] * near,
-        tower_weight,
-        *fetched,
+        *hidden,
         *units,
         *owns,
         flops=1 << 31,

time: 59 us -> 58.1 us (0.985)
  starting transfers between devices: 23.8 us -> 20.9 us
  waiting for transfers between devices: 8.95 us -> 11 us
    ppermute x20, starting transfers between devices: 23.8 us -> 20.9 us  [swap(): lax.ppermute(value, ('batch', 'item'), [(k, k ^ mask) for k in range(devi...]
    ppermute x20, waiting for transfers between devices: 8.95 us -> 11 us  [swap(): lax.ppermute(value, ('batch', 'item'), [(k, k ^ mask) for k in range(devi...]
    pallas_call x12 -> x13, Pallas kernels: 9.24 us -> 9.18 us  [call(): pl.pallas_call(kernel, out_shape=[jax.ShapeDtypeStruct(shape, dtype) for...]
  transfers between devices with their start and end apart: 20 -> 20, of which waited for: 5 -> 6; matrix products, arithmetic and copies ran while one was open for 1% -> 1% of each run, Pallas kernels for 15% -> 16%
where the time goes in v12:
time: 58.1 us; the launch traced here: 57.9 us
  starting transfers between devices  20.9 us (36%)
  Pallas kernels  12.8 us (22%)
  blocking collectives  11.7 us (20%)
  waiting for transfers between devices  11 us (19%)
  between operations  0.83 us (1%)
  other arithmetic  0.7 us (1%)
    ppermute x20, starting transfers between devices, swap(): lax.ppermute(value, ('batch', 'item'), [(k, k ^ mask) for k in range(devi...  20.9 us
    all_to_all x1, blocking collectives, local(): lax.all_to_all(request, ('batch', 'item'), split_axis=0, concat_axis=0, t...  11.7 us
    ppermute x20, waiting for transfers between devices, swap(): lax.ppermute(value, ('batch', 'item'), [(k, k ^ mask) for k in range(devi...  11 us
    pallas_call x13, Pallas kernels, call(): pl.pallas_call(kernel, out_shape=[jax.ShapeDtypeStruct(shape, dtype) for...  9.18 us
    pallas_call x1, Pallas kernels, local(): pl.pallas_call(table_kernel, out_specs=pl.BlockSpec(memory_space=pl.ANY),...  3.59 us
  transfers between devices with their start and end apart: 20, of which 6 were waited for; matrix products, arithmetic and copies ran while one was open for 1% of the time, Pallas kernels for 16%

profile of v12, /device:TPU:0, one launch (start us, length us, event | category | flops | bytes accessed | tf_op | source)
XLA Modules:
  0.0 57.9 jit_solution(15398859640508621606)
XLA Ops:
  0.6 4.1 %collective-permute-start = (bf16[256,512]{1,0:T(8,128)(2,1)}, bf16[256,512]{1,0:T(8,128)(2,1)S(1)}, u32[]{:S(2)}, u32[]{:S(2)}) collective-permute-start(bf16[256,512]{1,0:T(8,128)(2,1)} %refs_0_), channel_id=1, source_target_pairs={{0,4},{1,5},{2,6},{3,7},{4,0},{5,1},{6,2},{7,3},{8,12},{9,13},{10,... | collective-permute-start | bytes 786440 | tf_op jit(solution)/shard_map/ppermute | solution.py:246
  4.7 1.5 %collective-permute-start.1 = (bf16[256,512]{1,0:T(8,128)(2,1)}, bf16[256,512]{1,0:T(8,128)(2,1)S(1)}, u32[]{:S(2)}, u32[]{:S(2)}) collective-permute-start(bf16[256,512]{1,0:T(8,128)(2,1)} %refs_0_), channel_id=1, source_target_pairs={{0,16},{1,17},{2,18},{3,19},{4,20},{5,21},{6,22},{7,23},{8,24},{9,... | collective-permute-start | bytes 786440 | tf_op jit(solution)/shard_map/ppermute | solution.py:246
  6.2 0.7 %pad_add_fusion.named_ref = s32[2,256]{1,0:T(2,128)S(1)} fusion(s32[1,256]{1,0:T(1,128)} %bitcast.11, s32[1,256]{1,0:T(1,128)} %bitcast.12), kind=kLoop, calls=%fused_computation | loop fusion | flops 512 | bytes 4096 | tf_op jit(solution)/shard_map/stack | solution.py:312
  7.4 11.7 %all_to_all.12 = s32[32,1,80]{2,1,0:T(1,128)S(1)} all-to-all(s32[32,1,80]{2,1,0:T(1,128)S(1)} %bitcast.10), channel_id=1, replica_groups=mesh['batch'=4,'item'=8] {'batch','item'}, dimensions={0} | all-to-all | bytes 20480 | tf_op jit(solution)/shard_map/all_to_all | solution.py:315
  19.1 0.6 %collective-permute-start.2 = (bf16[256,512]{1,0:T(8,128)(2,1)S(1)}, bf16[256,512]{1,0:T(8,128)(2,1)S(1)}, u32[]{:S(2)}, u32[]{:S(2)}) collective-permute-start(bf16[256,512]{1,0:T(8,128)(2,1)S(1)} %collective-permute-done.refs_0_), channel_id=1, source_target_pairs={{0,16},{1,17},{2,18},{3,19},{4,20},{5,21},{6,22},{7,23},{8,24},{9,... | collective-permute-start | bytes 786440 | tf_op jit(solution)/shard_map/ppermute | solution.py:246
  20.2 0.9 %shard_map.69 = bf16[128,512]{1,0:T(8,128)(2,1)S(1)} custom-call(s32[32,80]{1,0:T(8,128)S(1)} %bitcast.6, bf16[4096,512]{1,0:T(8,128)(2,1)S(1)} %copy-done), custom_call_target="tpu_custom_call" | custom-call | flops 536870912 | bytes 1048576 | tf_op jit(solution)/shard_map/pallas_call | solution.py:235
  21.1 0.8 %collective-permute-start.5 = (bf16[128,512]{1,0:T(8,128)(2,1)S(1)}, bf16[128,512]{1,0:T(8,128)(2,1)S(1)}, u32[]{:S(2)}, u32[]{:S(2)}) collective-permute-start(bf16[128,512]{1,0:T(8,128)(2,1)S(1)} %shard_map.69), channel_id=1, source_target_pairs={{0,3},{1,2},{2,1},{3,0},{4,7},{5,6},{6,5},{7,4},{8,11},{9,10},{10,... | collective-permute-start | bytes 393224 | tf_op jit(solution)/shard_map/ppermute | solution.py:246
  21.9 1.6 %shard_map.70 = (bf16[128,512]{1,0:T(8,128)(2,1)S(1)}, bf16[128,512]{1,0:T(8,128)(2,1)S(1)}) custom-call(s32[32,80]{1,0:T(8,128)S(1)} %bitcast.7, bf16[4096,512]{1,0:T(8,128)(2,1)S(1)} %copy-done), custom_call_target="tpu_custom_call" | custom-call | flops 1073741824 | bytes 1048576 | tf_op jit(solution)/shard_map/pallas_call | solution.py:235
  23.5 1.3 %collective-permute-start.3 = (bf16[128,512]{1,0:T(8,128)(2,1)S(1)}, bf16[128,512]{1,0:T(8,128)(2,1)S(1)}, u32[]{:S(2)}, u32[]{:S(2)}) collective-permute-start(bf16[128,512]{1,0:T(8,128)(2,1)S(1)} %get-tuple-element.64), channel_id=1, source_target_pairs={{0,1},{1,0},{2,3},{3,2},{4,5},{5,4},{6,7},{7,6},{8,9},{9,8},{10,11... | collective-permute-start | bytes 393224 | tf_op jit(solution)/shard_map/ppermute | solution.py:246
  24.9 2.3 %collective-permute-done.2.refs_2_ = bf16[256,512]{1,0:T(8,128)(2,1)S(1)} collective-permute-done((bf16[256,512]{1,0:T(8,128)(2,1)S(1)}, bf16[256,512]{1,0:T(8,128)(2,1)S(1)}, u32[]{:S(2)}, u32[]{:S(2)}) %collective-permute-start.2) | collective-permute-done | bytes 262176 | tf_op jit(solution)/shard_map/ppermute | solution.py:246
  27.1 0.6 %collective-permute-start.4 = (bf16[128,512]{1,0:T(8,128)(2,1)S(1)}, bf16[128,512]{1,0:T(8,128)(2,1)S(1)}, u32[]{:S(2)}, u32[]{:S(2)}) collective-permute-start(bf16[128,512]{1,0:T(8,128)(2,1)S(1)} %get-tuple-element.65), channel_id=1, source_target_pairs={{0,2},{1,3},{2,0},{3,1},{4,6},{5,7},{6,4},{7,5},{8,10},{9,11},{10,... | collective-permute-start | bytes 393224 | tf_op jit(solution)/shard_map/ppermute | solution.py:246
  27.8 0.9 %shard_map.71.refs_0_ = bf16[128,512]{1,0:T(8,128)(2,1)S(1)} custom-call(s32[32,80]{1,0:T(8,128)S(1)} %bitcast.8, bf16[4096,512]{1,0:T(8,128)(2,1)S(1)} %copy-done), custom_call_target="tpu_custom_call" | custom-call | flops 536870912 | bytes 1048576 | tf_op jit(solution)/shard_map/pallas_call | solution.py:235
  29.7 0.7 %shard_map.74 = (bf16[1024,512]{1,0:T(8,128)(2,1)S(1)}, bf16[256,512]{1,0:T(8,128)(2,1)S(1)}) custom-call(s32[512,1]{1,0:T(8,128)S(1)} %get-tuple-element.70.place_ref, bf16[256,512]{1,0:T(8,128)(2,1)S(1)} %copy-done.1, bf16[256,512]{1,0:T(8,128)(2,1)S(1)} %collective-permute-done.6.refs_1_, bf16[256,512]{1,0:T(8,128)(2,1)S(1)} %collective-permute-done.1.refs_2_, ...), custom_call_target="tpu_custom_call" | custom-call | tf_op jit(solution)/shard_map/pallas_call | solution.py:235
  30.4 1.7 %collective-permute-done.4.refs_2_ = bf16[128,512]{1,0:T(8,128)(2,1)S(1)} collective-permute-done((bf16[128,512]{1,0:T(8,128)(2,1)S(1)}, bf16[128,512]{1,0:T(8,128)(2,1)S(1)}, u32[]{:S(2)}, u32[]{:S(2)}) %collective-permute-start.4) | collective-permute-done | bytes 131104 | tf_op jit(solution)/shard_map/ppermute | solution.py:246
  32.1 0.5 shard_map.73
  32.7 0.7 %shard_map.75 = (bf16[1024,512]{1,0:T(8,128)(2,1)S(1)}, bf16[256,512]{1,0:T(8,128)(2,1)S(1)}) custom-call(s32[512,1]{1,0:T(8,128)S(1)} %get-tuple-element.70.place_ref, bf16[256,512]{1,0:T(8,128)(2,1)S(1)} %collective-permute-done.refs_0_, bf16[256,512]{1,0:T(8,128)(2,1)S(1)} %collective-permute-done.8.refs_1_, ...), custom_call_target="tpu_custom_call" | custom-call | tf_op jit(solution)/shard_map/pallas_call | solution.py:235
  33.4 1.7 %shard_map.76 = (bf16[128,512]{1,0:T(8,128)(2,1)S(1)}, bf16[128,512]{1,0:T(8,128)(2,1)S(1)}, bf16[128,512]{1,0:T(8,128)(2,1)S(1)}, bf16[128,512]{1,0:T(8,128)(2,1)S(1)}) custom-call(f32[512,512]{1,0:T(8,128)S(1)} %get-tuple-element.67.hidden_ref, f32[512,1]{1,0:T(8,128)S(1)} %get-tuple-element.68.rscale_ref, ...), custom_call_target="tpu_custom_call" | custom-call | flops 2147483648 | bytes 1048576 | tf_op jit(solution)/shard_map/pallas_call | solution.py:235
  35.1 0.5 shard_map.77
  35.7 0.7 %collective-permute-start.14 = (bf16[128,512]{1,0:T(8,128)(2,1)S(1)}, bf16[128,512]{1,0:T(8,128)(2,1)S(1)}, u32[]{:S(2)}, u32[]{:S(2)}) collective-permute-start(bf16[128,512]{1,0:T(8,128)(2,1)S(1)} %get-tuple-element.79.refs_5_), channel_id=1, source_target_pairs={{0,1},{1,0},{2,3},{3,2},{4,5},{5,4},{6,7},{7,6},{8,9},{9,8},{10,11... | collective-permute-start | bytes 393224 | tf_op jit(solution)/shard_map/ppermute | solution.py:246
  36.4 0.5 collective-permute-start.15
  36.9 2.4 %collective-permute-start.16 = (bf16[128,512]{1,0:T(8,128)(2,1)S(1)}, bf16[128,512]{1,0:T(8,128)(2,1)S(1)}, u32[]{:S(2)}, u32[]{:S(2)}) collective-permute-start(bf16[128,512]{1,0:T(8,128)(2,1)S(1)} %get-tuple-element.81.refs_7_), channel_id=1, source_target_pairs={{0,3},{1,2},{2,1},{3,0},{4,7},{5,6},{6,5},{7,4},{8,11},{9,10},{10,... | collective-permute-start | bytes 393224 | tf_op jit(solution)/shard_map/ppermute | solution.py:246
  39.4 0.7 %collective-permute-start.11 = (bf16[4,16,512]{2,1,0:T(8,128)(2,1)S(1)}, bf16[4,16,512]{2,1,0:T(8,128)(2,1)S(1)}, u32[]{:S(2)}, u32[]{:S(2)}) collective-permute-start(bf16[4,16,512]{2,1,0:T(8,128)(2,1)S(1)} %get-tuple-element.85), channel_id=1, source_target_pairs={{0,1},{1,0},{2,3},{3,2},{4,5},{5,4},{6,7},{7,6},{8,9},{9,8},{10,11... | collective-permute-start | bytes 196616 | tf_op jit(solution)/shard_map/ppermute | solution.py:246
  40.0 0.8 %collective-permute-start.12 = (bf16[4,16,512]{2,1,0:T(8,128)(2,1)S(1)}, bf16[4,16,512]{2,1,0:T(8,128)(2,1)S(1)}, u32[]{:S(2)}, u32[]{:S(2)}) collective-permute-start(bf16[4,16,512]{2,1,0:T(8,128)(2,1)S(1)} %get-tuple-element.86), channel_id=1, source_target_pairs={{0,16},{1,17},{2,18},{3,19},{4,20},{5,21},{6,22},{7,23},{8,24},{9,... | collective-permute-start | bytes 196616 | tf_op jit(solution)/shard_map/ppermute | solution.py:246
  40.8 0.8 %collective-permute-done.14.refs_1_ = bf16[128,512]{1,0:T(8,128)(2,1)S(1)} collective-permute-done((bf16[128,512]{1,0:T(8,128)(2,1)S(1)}, bf16[128,512]{1,0:T(8,128)(2,1)S(1)}, u32[]{:S(2)}, u32[]{:S(2)}) %collective-permute-start.14) | collective-permute-done | bytes 131104 | tf_op jit(solution)/shard_map/ppermute | solution.py:246
  41.6 1.3 %collective-permute-start.13 = (bf16[4,16,512]{2,1,0:T(8,128)(2,1)S(1)}, bf16[4,16,512]{2,1,0:T(8,128)(2,1)S(1)}, u32[]{:S(2)}, u32[]{:S(2)}) collective-permute-start(bf16[4,16,512]{2,1,0:T(8,128)(2,1)S(1)} %get-tuple-element.87), channel_id=1, source_target_pairs={{0,17},{1,16},{2,19},{3,18},{4,21},{5,20},{6,23},{7,22},{8,25},{9,... | collective-permute-start | bytes 196616 | tf_op jit(solution)/shard_map/ppermute | solution.py:246
  42.9 3.3 %collective-permute-done.16.refs_3_ = bf16[128,512]{1,0:T(8,128)(2,1)S(1)} collective-permute-done((bf16[128,512]{1,0:T(8,128)(2,1)S(1)}, bf16[128,512]{1,0:T(8,128)(2,1)S(1)}, u32[]{:S(2)}, u32[]{:S(2)}) %collective-permute-start.16) | collective-permute-done | bytes 131104 | tf_op jit(solution)/shard_map/ppermute | solution.py:246
  46.2 1.2 %collective-permute-done.11.refs_1_ = bf16[4,16,512]{2,1,0:T(8,128)(2,1)S(1)} collective-permute-done((bf16[4,16,512]{2,1,0:T(8,128)(2,1)S(1)}, bf16[4,16,512]{2,1,0:T(8,128)(2,1)S(1)}, u32[]{:S(2)}, u32[]{:S(2)}) %collective-permute-start.11) | collective-permute-done | bytes 65568 | tf_op jit(solution)/shard_map/ppermute | solution.py:246
  47.5 2.6 %collective-permute-start.17 = (f32[1,16,512]{2,1,0:T(8,128)S(1)}, f32[1,16,512]{2,1,0:T(8,128)S(1)}, u32[]{:S(2)}, u32[]{:S(2)}) collective-permute-start(f32[1,16,512]{2,1,0:T(8,128)S(1)} %get-tuple-element.96), channel_id=1, source_target_pairs={{0,4},{1,5},{2,6},{3,7},{4,0},{5,1},{6,2},{7,3},{8,12},{9,13},{10,... | collective-permute-start | bytes 98312 | tf_op jit(solution)/shard_map/ppermute | solution.py:246
  50.1 1.5 %collective-permute-start.18 = (f32[1,16,512]{2,1,0:T(8,128)S(1)}, f32[1,16,512]{2,1,0:T(8,128)S(1)}, u32[]{:S(2)}, u32[]{:S(2)}) collective-permute-start(f32[1,16,512]{2,1,0:T(8,128)S(1)} %get-tuple-element.97), channel_id=1, source_target_pairs={{0,2},{1,3},{2,0},{3,1},{4,6},{5,7},{6,4},{7,5},{8,10},{9,11},{10,... | collective-permute-start | bytes 98312 | tf_op jit(solution)/shard_map/ppermute | solution.py:246
  51.9 3.6 %shard_map.79 = bf16[4096,512]{1,0:T(8,128)(2,1)} custom-call(bf16[256,512]{1,0:T(8,128)(2,1)S(1)} %get-tuple-element.59.low_hot_ref, bf16[256,512]{1,0:T(8,128)(2,1)S(1)} %get-tuple-element.60.block_ref, bf16[512,512]{1,0:T(8,128)(2,1)S(1)} %copy-done.2, bf16[128,512]{1,0:T(8,128)(2,1)S(1)} %get-tuple-element.78.refs_4_.refs_0_, ...), custom_call_target="tpu_custom_call" | custom-call | flops 2147483648 | bytes 4194304 | tf_op jit(solution)/shard_map/pallas_call | solution.py:385
  55.6 1.7 %collective-permute-done.19.refs_3_ = f32[1,16,512]{2,1,0:T(8,128)S(1)} collective-permute-done((f32[1,16,512]{2,1,0:T(8,128)S(1)}, f32[1,16,512]{2,1,0:T(8,128)S(1)}, u32[]{:S(2)}, u32[]{:S(2)}) %collective-permute-start.19) | collective-permute-done | bytes 32800 | tf_op jit(solution)/shard_map/ppermute | solution.py:246
  57.3 0.6 %shard_map.81 = f32[16,512]{1,0:T(8,128)} custom-call(f32[1,16,512]{2,1,0:T(8,128)S(1)} %get-tuple-element.100.refs_0_, f32[1,16,512]{2,1,0:T(8,128)S(1)} %collective-permute-done.17.refs_1_, f32[1,16,512]{2,1,0:T(8,128)S(1)} %collective-permute-done.18.refs_2_, f32[1,16,512]{2,1,0:T(8,128)S(1)} %collective-permute-done.19.refs_3_), custom_call_target="tpu_custom_call" | custom-call | bytes 1048576 | tf_op jit(solution)/shard_map/pallas_call | solution.py:235
  (30 shorter events, 2.5 us)
Async XLA Ops:
  0.6 18.4 %collective-permute-start = (bf16[256,512]{1,0:T(8,128)(2,1)}, bf16[256,512]{1,0:T(8,128)(2,1)S(1)}, u32[]{:S(2)}, u32[]{:S(2)}) collective-permute-start(bf16[256,512]{1,0:T(8,128)(2,1)} %refs_0_), channel_id=1, source_target_pairs={{0,4},{1,5},{2,6},{3,7},{4,0},{5,1},{6,2},{7,3},{8,12},{9,13},{10,... | collective-permute-start | bytes 786440 | tf_op jit(solution)/shard_map/ppermute | solution.py:246
  4.7 14.4 %collective-permute-start.1 = (bf16[256,512]{1,0:T(8,128)(2,1)}, bf16[256,512]{1,0:T(8,128)(2,1)S(1)}, u32[]{:S(2)}, u32[]{:S(2)}) collective-permute-start(bf16[256,512]{1,0:T(8,128)(2,1)} %refs_0_), channel_id=1, source_target_pairs={{0,16},{1,17},{2,18},{3,19},{4,20},{5,21},{6,22},{7,23},{8,24},{9,... | collective-permute-start | bytes 786440 | tf_op jit(solution)/shard_map/ppermute | solution.py:246
  6.9 12.7 %copy-start.1 = (bf16[256,512]{1,0:T(8,128)(2,1)S(1)}, bf16[256,512]{1,0:T(8,128)(2,1)}, u32[]{:S(2)}) copy-start(bf16[256,512]{1,0:T(8,128)(2,1)} %refs_0_) | copy-start | bytes 786436
  6.9 13.3 %copy-start = (bf16[4096,512]{1,0:T(8,128)(2,1)S(1)}, bf16[4096,512]{1,0:T(8,128)(2,1)}, u32[]{:S(2)}) copy-start(bf16[4096,512]{1,0:T(8,128)(2,1)} %table_ref.5) | copy-start | bytes 12582916
  19.1 8.0 %collective-permute-start.2 = (bf16[256,512]{1,0:T(8,128)(2,1)S(1)}, bf16[256,512]{1,0:T(8,128)(2,1)S(1)}, u32[]{:S(2)}, u32[]{:S(2)}) collective-permute-start(bf16[256,512]{1,0:T(8,128)(2,1)S(1)} %collective-permute-done.refs_0_), channel_id=1, source_target_pairs={{0,16},{1,17},{2,18},{3,19},{4,20},{5,21},{6,22},{7,23},{8,24},{9,... | collective-permute-start | bytes 786440 | tf_op jit(solution)/shard_map/ppermute | solution.py:246
  19.7 9.4 %collective-permute-start.6 = (bf16[256,512]{1,0:T(8,128)(2,1)S(1)}, bf16[256,512]{1,0:T(8,128)(2,1)S(1)}, u32[]{:S(2)}, u32[]{:S(2)}) collective-permute-start(bf16[256,512]{1,0:T(8,128)(2,1)S(1)} %copy-done.1), channel_id=1, source_target_pairs={{0,8},{1,9},{2,10},{3,11},{4,12},{5,13},{6,14},{7,15},{8,0},{9,1},... | collective-permute-start | bytes 786440 | tf_op jit(solution)/shard_map/ppermute | solution.py:246
  19.7 9.5 %collective-permute-start.7 = (bf16[256,512]{1,0:T(8,128)(2,1)S(1)}, bf16[256,512]{1,0:T(8,128)(2,1)S(1)}, u32[]{:S(2)}, u32[]{:S(2)}) collective-permute-start(bf16[256,512]{1,0:T(8,128)(2,1)S(1)} %collective-permute-done.1.refs_2_), channel_id=1, source_target_pairs={{0,8},{1,9},{2,10},{3,11},{4,12},{5,13},{6,14},{7,15},{8,0},{9,1},... | collective-permute-start | bytes 786440 | tf_op jit(solution)/shard_map/ppermute | solution.py:246
  21.1 11.0 %copy-start.2 = (bf16[512,512]{1,0:T(8,128)(2,1)S(1)}, bf16[512,512]{1,0:T(8,128)(2,1)}, u32[]{:S(2)}) copy-start(bf16[512,512]{1,0:T(8,128)(2,1)} %weight_ref.3) | copy-start | bytes 1572868
  21.1 9.3 %collective-permute-start.5 = (bf16[128,512]{1,0:T(8,128)(2,1)S(1)}, bf16[128,512]{1,0:T(8,128)(2,1)S(1)}, u32[]{:S(2)}, u32[]{:S(2)}) collective-permute-start(bf16[128,512]{1,0:T(8,128)(2,1)S(1)} %shard_map.69), channel_id=1, source_target_pairs={{0,3},{1,2},{2,1},{3,0},{4,7},{5,6},{6,5},{7,4},{8,11},{9,10},{10,... | collective-permute-start | bytes 393224 | tf_op jit(solution)/shard_map/ppermute | solution.py:246
  23.5 6.9 %collective-permute-start.3 = (bf16[128,512]{1,0:T(8,128)(2,1)S(1)}, bf16[128,512]{1,0:T(8,128)(2,1)S(1)}, u32[]{:S(2)}, u32[]{:S(2)}) collective-permute-start(bf16[128,512]{1,0:T(8,128)(2,1)S(1)} %get-tuple-element.64), channel_id=1, source_target_pairs={{0,1},{1,0},{2,3},{3,2},{4,5},{5,4},{6,7},{7,6},{8,9},{9,8},{10,11... | collective-permute-start | bytes 393224 | tf_op jit(solution)/shard_map/ppermute | solution.py:246
  27.1 5.0 %collective-permute-start.4 = (bf16[128,512]{1,0:T(8,128)(2,1)S(1)}, bf16[128,512]{1,0:T(8,128)(2,1)S(1)}, u32[]{:S(2)}, u32[]{:S(2)}) collective-permute-start(bf16[128,512]{1,0:T(8,128)(2,1)S(1)} %get-tuple-element.65), channel_id=1, source_target_pairs={{0,2},{1,3},{2,0},{3,1},{4,6},{5,7},{6,4},{7,5},{8,10},{9,11},{10,... | collective-permute-start | bytes 393224 | tf_op jit(solution)/shard_map/ppermute | solution.py:246
  29.1 3.5 %collective-permute-start.8 = (bf16[256,512]{1,0:T(8,128)(2,1)S(1)}, bf16[256,512]{1,0:T(8,128)(2,1)S(1)}, u32[]{:S(2)}, u32[]{:S(2)}) collective-permute-start(bf16[256,512]{1,0:T(8,128)(2,1)S(1)} %collective-permute-done.refs_0_), channel_id=1, source_target_pairs={{0,8},{1,9},{2,10},{3,11},{4,12},{5,13},{6,14},{7,15},{8,0},{9,1},... | collective-permute-start | bytes 786440 | tf_op jit(solution)/shard_map/ppermute | solution.py:246
  29.2 3.4 %collective-permute-start.9 = (bf16[256,512]{1,0:T(8,128)(2,1)S(1)}, bf16[256,512]{1,0:T(8,128)(2,1)S(1)}, u32[]{:S(2)}, u32[]{:S(2)}) collective-permute-start(bf16[256,512]{1,0:T(8,128)(2,1)S(1)} %collective-permute-done.2.refs_2_), channel_id=1, source_target_pairs={{0,8},{1,9},{2,10},{3,11},{4,12},{5,13},{6,14},{7,15},{8,0},{9,1},... | collective-permute-start | bytes 786440 | tf_op jit(solution)/shard_map/ppermute | solution.py:246
  35.6 3.6 %collective-permute-start.10 = (bf16[16,16,512]{2,1,0:T(8,128)(2,1)S(1)}, bf16[16,16,512]{2,1,0:T(8,128)(2,1)S(1)}, u32[]{:S(2)}, u32[]{:S(2)}) collective-permute-start(bf16[16,16,512]{2,1,0:T(8,128)(2,1)S(1)} %get-tuple-element.83), channel_id=1, source_target_pairs={{0,8},{1,9},{2,10},{3,11},{4,12},{5,13},{6,14},{7,15},{8,0},{9,1},... | collective-permute-start | bytes 786440 | tf_op jit(solution)/shard_map/ppermute | solution.py:246
  35.7 5.9 %collective-permute-start.14 = (bf16[128,512]{1,0:T(8,128)(2,1)S(1)}, bf16[128,512]{1,0:T(8,128)(2,1)S(1)}, u32[]{:S(2)}, u32[]{:S(2)}) collective-permute-start(bf16[128,512]{1,0:T(8,128)(2,1)S(1)} %get-tuple-element.79.refs_5_), channel_id=1, source_target_pairs={{0,1},{1,0},{2,3},{3,2},{4,5},{5,4},{6,7},{7,6},{8,9},{9,8},{10,11... | collective-permute-start | bytes 393224 | tf_op jit(solution)/shard_map/ppermute | solution.py:246
  36.4 6.6 %collective-permute-start.15 = (bf16[128,512]{1,0:T(8,128)(2,1)S(1)}, bf16[128,512]{1,0:T(8,128)(2,1)S(1)}, u32[]{:S(2)}, u32[]{:S(2)}) collective-permute-start(bf16[128,512]{1,0:T(8,128)(2,1)S(1)} %get-tuple-element.80.refs_6_), channel_id=1, source_target_pairs={{0,2},{1,3},{2,0},{3,1},{4,6},{5,7},{6,4},{7,5},{8,10},{9,11},{10,... | collective-permute-start | bytes 393224 | tf_op jit(solution)/shard_map/ppermute | solution.py:246
  36.9 9.3 %collective-permute-start.16 = (bf16[128,512]{1,0:T(8,128)(2,1)S(1)}, bf16[128,512]{1,0:T(8,128)(2,1)S(1)}, u32[]{:S(2)}, u32[]{:S(2)}) collective-permute-start(bf16[128,512]{1,0:T(8,128)(2,1)S(1)} %get-tuple-element.81.refs_7_), channel_id=1, source_target_pairs={{0,3},{1,2},{2,1},{3,0},{4,7},{5,6},{6,5},{7,4},{8,11},{9,10},{10,... | collective-permute-start | bytes 393224 | tf_op jit(solution)/shard_map/ppermute | solution.py:246
  39.4 8.1 %collective-permute-start.11 = (bf16[4,16,512]{2,1,0:T(8,128)(2,1)S(1)}, bf16[4,16,512]{2,1,0:T(8,128)(2,1)S(1)}, u32[]{:S(2)}, u32[]{:S(2)}) collective-permute-start(bf16[4,16,512]{2,1,0:T(8,128)(2,1)S(1)} %get-tuple-element.85), channel_id=1, source_target_pairs={{0,1},{1,0},{2,3},{3,2},{4,5},{5,4},{6,7},{7,6},{8,9},{9,8},{10,11... | collective-permute-start | bytes 196616 | tf_op jit(solution)/shard_map/ppermute | solution.py:246
  40.0 7.4 %collective-permute-start.12 = (bf16[4,16,512]{2,1,0:T(8,128)(2,1)S(1)}, bf16[4,16,512]{2,1,0:T(8,128)(2,1)S(1)}, u32[]{:S(2)}, u32[]{:S(2)}) collective-permute-start(bf16[4,16,512]{2,1,0:T(8,128)(2,1)S(1)} %get-tuple-element.86), channel_id=1, source_target_pairs={{0,16},{1,17},{2,18},{3,19},{4,20},{5,21},{6,22},{7,23},{8,24},{9,... | collective-permute-start | bytes 196616 | tf_op jit(solution)/shard_map/ppermute | solution.py:246
  41.6 5.8 %collective-permute-start.13 = (bf16[4,16,512]{2,1,0:T(8,128)(2,1)S(1)}, bf16[4,16,512]{2,1,0:T(8,128)(2,1)S(1)}, u32[]{:S(2)}, u32[]{:S(2)}) collective-permute-start(bf16[4,16,512]{2,1,0:T(8,128)(2,1)S(1)} %get-tuple-element.87), channel_id=1, source_target_pairs={{0,17},{1,16},{2,19},{3,18},{4,21},{5,20},{6,23},{7,22},{8,25},{9,... | collective-permute-start | bytes 196616 | tf_op jit(solution)/shard_map/ppermute | solution.py:246
  47.5 8.1 %collective-permute-start.17 = (f32[1,16,512]{2,1,0:T(8,128)S(1)}, f32[1,16,512]{2,1,0:T(8,128)S(1)}, u32[]{:S(2)}, u32[]{:S(2)}) collective-permute-start(f32[1,16,512]{2,1,0:T(8,128)S(1)} %get-tuple-element.96), channel_id=1, source_target_pairs={{0,4},{1,5},{2,6},{3,7},{4,0},{5,1},{6,2},{7,3},{8,12},{9,13},{10,... | collective-permute-start | bytes 98312 | tf_op jit(solution)/shard_map/ppermute | solution.py:246
  50.1 5.4 %collective-permute-start.18 = (f32[1,16,512]{2,1,0:T(8,128)S(1)}, f32[1,16,512]{2,1,0:T(8,128)S(1)}, u32[]{:S(2)}, u32[]{:S(2)}) collective-permute-start(f32[1,16,512]{2,1,0:T(8,128)S(1)} %get-tuple-element.97), channel_id=1, source_target_pairs={{0,2},{1,3},{2,0},{3,1},{4,6},{5,7},{6,4},{7,5},{8,10},{9,11},{10,... | collective-permute-start | bytes 98312 | tf_op jit(solution)/shard_map/ppermute | solution.py:246
  51.6 5.7 %collective-permute-start.19 = (f32[1,16,512]{2,1,0:T(8,128)S(1)}, f32[1,16,512]{2,1,0:T(8,128)S(1)}, u32[]{:S(2)}, u32[]{:S(2)}) collective-permute-start(f32[1,16,512]{2,1,0:T(8,128)S(1)} %get-tuple-element.98), channel_id=1, source_target_pairs={{0,6},{1,7},{2,4},{3,5},{4,2},{5,3},{6,0},{7,1},{8,14},{9,15},{10,... | collective-permute-start | bytes 98312 | tf_op jit(solution)/shard_map/ppermute | solution.py:246

commit v13 on v12

--- a/solution.py
+++ b/solution.py
@@ -258,9 +258,10 @@
     width = dhidden[0].shape[1]
     n_item, devices = lax.axis_size("item"), lax.axis_size("batch") * lax.axis_size("item")
     part = width // devices
-    bits = bits_of("batch") + bits_of("item")
-    odd = len(bits) % 2
-    stages = [bits[:1]] * odd + [bits[k : k + 2] for k in range(odd, len(bits), 2)]
+    close = log2(len(dhidden))
+    batch_bits, item_bits = bits_of("batch"), bits_of("item")
+    stages = [batch_bits[:1], batch_bits[1:], item_bits[:close], item_bits[close:]]
+    bits = sum(stages, [])
     order = []
     for spot in range(devices):
         at = {"batch": 0, "item": 0}
@@ -284,7 +285,7 @@
             free=True,
         )
         values = [kept] + [swap(value, mask) for mask, value in zip(masks, sends)]
-        if k == 1:
+        if k == 2:
             values, incoming = lax.optimization_barrier((values, incoming))
     return values, incoming
 
@@ -364,12 +365,14 @@
             for level in range(levels)
         ]
     )
+    fetched[0], first = lax.optimization_barrier((fetched[0], (units[0], owns[0])))
+    units, owns = (first[0], *units[1:]), (first[1], *owns[1:])
     hidden = call(
         functools.partial(hidden_kernel, levels),
         [((total, width), f32), ((total, 1), f32), ((total, width), bf16)],
         tower_weight,
         *fetched,
-        flops=1 << 32,
+        flops=1 << 34,
     )
     dhidden = call(
         functools.partial(main_kernel, levels),

time: 58.1 us -> 57 us (0.981)
  waiting for transfers between devices: 11 us -> 9.35 us
    ppermute x20 -> x19, waiting for transfers between devices: 11 us -> 9.35 us  [swap(): lax.ppermute(value, ('batch', 'item'), [(k, k ^ mask) for k in range(devi...]
    ppermute x20 -> x19, starting transfers between devices: 20.9 us -> 21.4 us  [swap(): lax.ppermute(value, ('batch', 'item'), [(k, k ^ mask) for k in range(devi...]
    pallas_call x13 -> x14, Pallas kernels: 9.18 us -> 9.22 us  [call(): pl.pallas_call(kernel, out_shape=[jax.ShapeDtypeStruct(shape, dtype) for...]
  transfers between devices with their start and end apart: 20 -> 19, of which waited for: 6 -> 7; matrix products, arithmetic and copies ran while one was open for 1% -> 1% of each run, Pallas kernels for 16% -> 16%
where the time goes in v13:
time: 57 us; the launch traced here: 56.8 us
  starting transfers between devices  21.4 us (38%)
  Pallas kernels  12.8 us (22%)
  blocking collectives  11.7 us (21%)
  waiting for transfers between devices  9.35 us (16%)
  between operations  0.82 us (1%)
  other arithmetic  0.7 us (1%)
    ppermute x19, starting transfers between devices, swap(): lax.ppermute(value, ('batch', 'item'), [(k, k ^ mask) for k in range(devi...  21.4 us
    all_to_all x1, blocking collectives, local(): lax.all_to_all(request, ('batch', 'item'), split_axis=0, concat_axis=0, t...  11.7 us
    ppermute x19, waiting for transfers between devices, swap(): lax.ppermute(value, ('batch', 'item'), [(k, k ^ mask) for k in range(devi...  9.35 us
    pallas_call x14, Pallas kernels, call(): pl.pallas_call(kernel, out_shape=[jax.ShapeDtypeStruct(shape, dtype) for...  9.22 us
    pallas_call x1, Pallas kernels, local(): pl.pallas_call(table_kernel, out_specs=pl.BlockSpec(memory_space=pl.ANY),...  3.58 us
  transfers between devices with their start and end apart: 19, of which 7 were waited for; matrix products, arithmetic and copies ran while one was open for 1% of the time, Pallas kernels for 16%

profile of v13, /device:TPU:0, one launch (start us, length us, event | category | flops | bytes accessed | tf_op | source)
XLA Modules:
  0.0 56.8 jit_solution(16657000099802279959)
XLA Ops:
  0.6 4.1 %collective-permute-start = (bf16[256,512]{1,0:T(8,128)(2,1)}, bf16[256,512]{1,0:T(8,128)(2,1)S(1)}, u32[]{:S(2)}, u32[]{:S(2)}) collective-permute-start(bf16[256,512]{1,0:T(8,128)(2,1)} %refs_0_), channel_id=1, source_target_pairs={{0,4},{1,5},{2,6},{3,7},{4,0},{5,1},{6,2},{7,3},{8,12},{9,13},{10,... | collective-permute-start | bytes 786440 | tf_op jit(solution)/shard_map/ppermute | solution.py:246
  4.7 1.5 %collective-permute-start.1 = (bf16[256,512]{1,0:T(8,128)(2,1)}, bf16[256,512]{1,0:T(8,128)(2,1)S(1)}, u32[]{:S(2)}, u32[]{:S(2)}) collective-permute-start(bf16[256,512]{1,0:T(8,128)(2,1)} %refs_0_), channel_id=1, source_target_pairs={{0,16},{1,17},{2,18},{3,19},{4,20},{5,21},{6,22},{7,23},{8,24},{9,... | collective-permute-start | bytes 786440 | tf_op jit(solution)/shard_map/ppermute | solution.py:246
  6.2 0.7 %pad_add_fusion.named_ref = s32[2,256]{1,0:T(2,128)S(1)} fusion(s32[1,256]{1,0:T(1,128)} %bitcast.11, s32[1,256]{1,0:T(1,128)} %bitcast.12), kind=kLoop, calls=%fused_computation | loop fusion | flops 512 | bytes 4096 | tf_op jit(solution)/shard_map/stack | solution.py:313
  7.4 11.7 %all_to_all.12 = s32[32,1,80]{2,1,0:T(1,128)S(1)} all-to-all(s32[32,1,80]{2,1,0:T(1,128)S(1)} %bitcast.10), channel_id=1, replica_groups=mesh['batch'=4,'item'=8] {'batch','item'}, dimensions={0} | all-to-all | bytes 20480 | tf_op jit(solution)/shard_map/all_to_all | solution.py:316
  19.1 0.6 %collective-permute-start.2 = (bf16[256,512]{1,0:T(8,128)(2,1)S(1)}, bf16[256,512]{1,0:T(8,128)(2,1)S(1)}, u32[]{:S(2)}, u32[]{:S(2)}) collective-permute-start(bf16[256,512]{1,0:T(8,128)(2,1)S(1)} %collective-permute-done.refs_0_), channel_id=1, source_target_pairs={{0,16},{1,17},{2,18},{3,19},{4,20},{5,21},{6,22},{7,23},{8,24},{9,... | collective-permute-start | bytes 786440 | tf_op jit(solution)/shard_map/ppermute | solution.py:246
  20.2 0.9 %shard_map.69 = bf16[128,512]{1,0:T(8,128)(2,1)S(1)} custom-call(s32[32,80]{1,0:T(8,128)S(1)} %bitcast.6, bf16[4096,512]{1,0:T(8,128)(2,1)S(1)} %copy-done), custom_call_target="tpu_custom_call" | custom-call | flops 536870912 | bytes 1048576 | tf_op jit(solution)/shard_map/pallas_call | solution.py:235
  21.1 0.8 %collective-permute-start.7 = (bf16[128,512]{1,0:T(8,128)(2,1)S(1)}, bf16[128,512]{1,0:T(8,128)(2,1)S(1)}, u32[]{:S(2)}, u32[]{:S(2)}) collective-permute-start(bf16[128,512]{1,0:T(8,128)(2,1)S(1)} %shard_map.69), channel_id=1, source_target_pairs={{0,3},{1,2},{2,1},{3,0},{4,7},{5,6},{6,5},{7,4},{8,11},{9,10},{10,... | collective-permute-start | bytes 393224 | tf_op jit(solution)/shard_map/ppermute | solution.py:246
  21.9 1.6 %shard_map.70 = (bf16[128,512]{1,0:T(8,128)(2,1)S(1)}, bf16[128,512]{1,0:T(8,128)(2,1)S(1)}) custom-call(s32[32,80]{1,0:T(8,128)S(1)} %bitcast.7, bf16[4096,512]{1,0:T(8,128)(2,1)S(1)} %copy-done), custom_call_target="tpu_custom_call" | custom-call | flops 1073741824 | bytes 1048576 | tf_op jit(solution)/shard_map/pallas_call | solution.py:235
  23.5 1.3 %collective-permute-start.5 = (bf16[128,512]{1,0:T(8,128)(2,1)S(1)}, bf16[128,512]{1,0:T(8,128)(2,1)S(1)}, u32[]{:S(2)}, u32[]{:S(2)}) collective-permute-start(bf16[128,512]{1,0:T(8,128)(2,1)S(1)} %get-tuple-element.71), channel_id=1, source_target_pairs={{0,1},{1,0},{2,3},{3,2},{4,5},{5,4},{6,7},{7,6},{8,9},{9,8},{10,11... | collective-permute-start | bytes 393224 | tf_op jit(solution)/shard_map/ppermute | solution.py:246
  24.9 2.3 %collective-permute-done.2.refs_2_ = bf16[256,512]{1,0:T(8,128)(2,1)S(1)} collective-permute-done((bf16[256,512]{1,0:T(8,128)(2,1)S(1)}, bf16[256,512]{1,0:T(8,128)(2,1)S(1)}, u32[]{:S(2)}, u32[]{:S(2)}) %collective-permute-start.2) | collective-permute-done | bytes 262176 | tf_op jit(solution)/shard_map/ppermute | solution.py:246
  27.1 0.6 %collective-permute-start.6 = (bf16[128,512]{1,0:T(8,128)(2,1)S(1)}, bf16[128,512]{1,0:T(8,128)(2,1)S(1)}, u32[]{:S(2)}, u32[]{:S(2)}) collective-permute-start(bf16[128,512]{1,0:T(8,128)(2,1)S(1)} %get-tuple-element.72), channel_id=1, source_target_pairs={{0,2},{1,3},{2,0},{3,1},{4,6},{5,7},{6,4},{7,5},{8,10},{9,11},{10,... | collective-permute-start | bytes 393224 | tf_op jit(solution)/shard_map/ppermute | solution.py:246
  27.8 0.9 %shard_map.71.refs_0_ = bf16[128,512]{1,0:T(8,128)(2,1)S(1)} custom-call(s32[32,80]{1,0:T(8,128)S(1)} %bitcast.8, bf16[4096,512]{1,0:T(8,128)(2,1)S(1)} %copy-done), custom_call_target="tpu_custom_call" | custom-call | flops 536870912 | bytes 1048576 | tf_op jit(solution)/shard_map/pallas_call | solution.py:235
  29.7 0.7 %shard_map.73 = (bf16[1024,512]{1,0:T(8,128)(2,1)S(1)}, bf16[256,512]{1,0:T(8,128)(2,1)S(1)}) custom-call(s32[512,1]{1,0:T(8,128)S(1)} %get-tuple-element.65.place_ref, bf16[256,512]{1,0:T(8,128)(2,1)S(1)} %copy-done.1, bf16[256,512]{1,0:T(8,128)(2,1)S(1)} %collective-permute-done.3.refs_1_, bf16[256,512]{1,0:T(8,128)(2,1)S(1)} %collective-permute-done.1.refs_2_, ...), custom_call_target="tpu_custom_call" | custom-call | tf_op jit(solution)/shard_map/pallas_call | solution.py:235
  30.4 1.7 %collective-permute-done.6.refs_2_ = bf16[128,512]{1,0:T(8,128)(2,1)S(1)} collective-permute-done((bf16[128,512]{1,0:T(8,128)(2,1)S(1)}, bf16[128,512]{1,0:T(8,128)(2,1)S(1)}, u32[]{:S(2)}, u32[]{:S(2)}) %collective-permute-start.6) | collective-permute-done | bytes 131104 | tf_op jit(solution)/shard_map/ppermute | solution.py:246
  32.1 0.5 shard_map.74
  32.7 0.7 %shard_map.75 = (bf16[1024,512]{1,0:T(8,128)(2,1)S(1)}, bf16[256,512]{1,0:T(8,128)(2,1)S(1)}) custom-call(s32[512,1]{1,0:T(8,128)S(1)} %get-tuple-element.65.place_ref, bf16[256,512]{1,0:T(8,128)(2,1)S(1)} %collective-permute-done.refs_0_, bf16[256,512]{1,0:T(8,128)(2,1)S(1)} %collective-permute-done.8.refs_1_, ...), custom_call_target="tpu_custom_call" | custom-call | tf_op jit(solution)/shard_map/pallas_call | solution.py:235
  33.4 1.7 %shard_map.76 = (bf16[128,512]{1,0:T(8,128)(2,1)S(1)}, bf16[128,512]{1,0:T(8,128)(2,1)S(1)}, bf16[128,512]{1,0:T(8,128)(2,1)S(1)}, bf16[128,512]{1,0:T(8,128)(2,1)S(1)}) custom-call(f32[512,512]{1,0:T(8,128)S(1)} %get-tuple-element.74.hidden_ref, f32[512,1]{1,0:T(8,128)S(1)} %get-tuple-element.75.rscale_ref, ...), custom_call_target="tpu_custom_call" | custom-call | flops 2147483648 | bytes 1048576 | tf_op jit(solution)/shard_map/pallas_call | solution.py:235
  35.1 0.5 shard_map.77
  35.7 1.5 %collective-permute-done.10.refs_1_ = bf16[16,16,512]{2,1,0:T(8,128)(2,1)S(1)} collective-permute-done((bf16[16,16,512]{2,1,0:T(8,128)(2,1)S(1)}, bf16[16,16,512]{2,1,0:T(8,128)(2,1)S(1)}, u32[]{:S(2)}, u32[]{:S(2)}) %collective-permute-start.10) | collective-permute-done | bytes 262176 | tf_op jit(solution)/shard_map/ppermute | solution.py:246
  37.3 0.7 %collective-permute-start.11 = (bf16[8,16,512]{2,1,0:T(8,128)(2,1)S(1)}, bf16[8,16,512]{2,1,0:T(8,128)(2,1)S(1)}, u32[]{:S(2)}, u32[]{:S(2)}) collective-permute-start(bf16[8,16,512]{2,1,0:T(8,128)(2,1)S(1)} %get-tuple-element.89), channel_id=1, source_target_pairs={{0,16},{1,17},{2,18},{3,19},{4,20},{5,21},{6,22},{7,23},{8,24},{9,... | collective-permute-start | bytes 393224 | tf_op jit(solution)/shard_map/ppermute | solution.py:246
  38.0 0.8 %collective-permute-start.15 = (bf16[128,512]{1,0:T(8,128)(2,1)S(1)}, bf16[128,512]{1,0:T(8,128)(2,1)S(1)}, u32[]{:S(2)}, u32[]{:S(2)}) collective-permute-start(bf16[128,512]{1,0:T(8,128)(2,1)S(1)} %get-tuple-element.83.refs_5_), channel_id=1, source_target_pairs={{0,1},{1,0},{2,3},{3,2},{4,5},{5,4},{6,7},{7,6},{8,9},{9,8},{10,11... | collective-permute-start | bytes 393224 | tf_op jit(solution)/shard_map/ppermute | solution.py:246
  38.8 0.7 %collective-permute-start.16 = (bf16[128,512]{1,0:T(8,128)(2,1)S(1)}, bf16[128,512]{1,0:T(8,128)(2,1)S(1)}, u32[]{:S(2)}, u32[]{:S(2)}) collective-permute-start(bf16[128,512]{1,0:T(8,128)(2,1)S(1)} %get-tuple-element.84.refs_6_), channel_id=1, source_target_pairs={{0,2},{1,3},{2,0},{3,1},{4,6},{5,7},{6,4},{7,5},{8,10},{9,11},{10,... | collective-permute-start | bytes 393224 | tf_op jit(solution)/shard_map/ppermute | solution.py:246
  39.5 2.0 %collective-permute-start.17 = (bf16[128,512]{1,0:T(8,128)(2,1)S(1)}, bf16[128,512]{1,0:T(8,128)(2,1)S(1)}, u32[]{:S(2)}, u32[]{:S(2)}) collective-permute-start(bf16[128,512]{1,0:T(8,128)(2,1)S(1)} %get-tuple-element.85.refs_7_), channel_id=1, source_target_pairs={{0,3},{1,2},{2,1},{3,0},{4,7},{5,6},{6,5},{7,4},{8,11},{9,10},{10,... | collective-permute-start | bytes 393224 | tf_op jit(solution)/shard_map/ppermute | solution.py:246
  41.5 1.4 %collective-permute-done.11.refs_1_ = bf16[8,16,512]{2,1,0:T(8,128)(2,1)S(1)} collective-permute-done((bf16[8,16,512]{2,1,0:T(8,128)(2,1)S(1)}, bf16[8,16,512]{2,1,0:T(8,128)(2,1)S(1)}, u32[]{:S(2)}, u32[]{:S(2)}) %collective-permute-start.11) | collective-permute-done | bytes 131104 | tf_op jit(solution)/shard_map/ppermute | solution.py:246
  43.0 0.7 %collective-permute-start.12 = (bf16[2,16,512]{2,1,0:T(8,128)(2,1)S(1)}, bf16[2,16,512]{2,1,0:T(8,128)(2,1)S(1)}, u32[]{:S(2)}, u32[]{:S(2)}) collective-permute-start(bf16[2,16,512]{2,1,0:T(8,128)(2,1)S(1)} %get-tuple-element.91), channel_id=1, source_target_pairs={{0,2},{1,3},{2,0},{3,1},{4,6},{5,7},{6,4},{7,5},{8,10},{9,11},{10,... | collective-permute-start | bytes 98312 | tf_op jit(solution)/shard_map/ppermute | solution.py:246
  43.7 0.5 collective-permute-start.13
  44.2 2.4 %collective-permute-start.14 = (bf16[2,16,512]{2,1,0:T(8,128)(2,1)S(1)}, bf16[2,16,512]{2,1,0:T(8,128)(2,1)S(1)}, u32[]{:S(2)}, u32[]{:S(2)}) collective-permute-start(bf16[2,16,512]{2,1,0:T(8,128)(2,1)S(1)} %get-tuple-element.93), channel_id=1, source_target_pairs={{0,3},{1,2},{2,1},{3,0},{4,7},{5,6},{6,5},{7,4},{8,11},{9,10},{10,... | collective-permute-start | bytes 98312 | tf_op jit(solution)/shard_map/ppermute | solution.py:246
  46.6 1.5 %collective-permute-done.17.refs_3_ = bf16[128,512]{1,0:T(8,128)(2,1)S(1)} collective-permute-done((bf16[128,512]{1,0:T(8,128)(2,1)S(1)}, bf16[128,512]{1,0:T(8,128)(2,1)S(1)}, u32[]{:S(2)}, u32[]{:S(2)}) %collective-permute-start.17) | collective-permute-done | bytes 131104 | tf_op jit(solution)/shard_map/ppermute | solution.py:246
  48.3 0.7 %collective-permute-done.14.refs_3_ = bf16[2,16,512]{2,1,0:T(8,128)(2,1)S(1)} collective-permute-done((bf16[2,16,512]{2,1,0:T(8,128)(2,1)S(1)}, bf16[2,16,512]{2,1,0:T(8,128)(2,1)S(1)}, u32[]{:S(2)}, u32[]{:S(2)}) %collective-permute-start.14) | collective-permute-done | bytes 32800 | tf_op jit(solution)/shard_map/ppermute | solution.py:246
  49.0 3.5 %collective-permute-start.18 = (f32[1,16,512]{2,1,0:T(8,128)S(1)}, f32[1,16,512]{2,1,0:T(8,128)S(1)}, u32[]{:S(2)}, u32[]{:S(2)}) collective-permute-start(f32[1,16,512]{2,1,0:T(8,128)S(1)} %get-tuple-element.102), channel_id=1, source_target_pairs={{0,4},{1,5},{2,6},{3,7},{4,0},{5,1},{6,2},{7,3},{8,12},{9,13},{10,... | collective-permute-start | bytes 98312 | tf_op jit(solution)/shard_map/ppermute | solution.py:246
  52.6 3.6 %shard_map.80 = bf16[4096,512]{1,0:T(8,128)(2,1)} custom-call(bf16[256,512]{1,0:T(8,128)(2,1)S(1)} %get-tuple-element.60.low_hot_ref, bf16[256,512]{1,0:T(8,128)(2,1)S(1)} %get-tuple-element.61.block_ref, bf16[512,512]{1,0:T(8,128)(2,1)S(1)} %copy-done.2, bf16[128,512]{1,0:T(8,128)(2,1)S(1)} %get-tuple-element.82.refs_4_.refs_0_, ...), custom_call_target="tpu_custom_call" | custom-call | flops 2147483648 | bytes 4194304 | tf_op jit(solution)/shard_map/pallas_call | solution.py:388
  56.2 0.6 %shard_map.82 = f32[16,512]{1,0:T(8,128)} custom-call(f32[1,16,512]{2,1,0:T(8,128)S(1)} %get-tuple-element.104.refs_0_, f32[1,16,512]{2,1,0:T(8,128)S(1)} %collective-permute-done.18.refs_1_), custom_call_target="tpu_custom_call" | custom-call | bytes 1048576 | tf_op jit(solution)/shard_map/pallas_call | solution.py:235
  (29 shorter events, 2.5 us)
Async XLA Ops:
  0.6 18.4 %collective-permute-start = (bf16[256,512]{1,0:T(8,128)(2,1)}, bf16[256,512]{1,0:T(8,128)(2,1)S(1)}, u32[]{:S(2)}, u32[]{:S(2)}) collective-permute-start(bf16[256,512]{1,0:T(8,128)(2,1)} %refs_0_), channel_id=1, source_target_pairs={{0,4},{1,5},{2,6},{3,7},{4,0},{5,1},{6,2},{7,3},{8,12},{9,13},{10,... | collective-permute-start | bytes 786440 | tf_op jit(solution)/shard_map/ppermute | solution.py:246
  4.7 14.4 %collective-permute-start.1 = (bf16[256,512]{1,0:T(8,128)(2,1)}, bf16[256,512]{1,0:T(8,128)(2,1)S(1)}, u32[]{:S(2)}, u32[]{:S(2)}) collective-permute-start(bf16[256,512]{1,0:T(8,128)(2,1)} %refs_0_), channel_id=1, source_target_pairs={{0,16},{1,17},{2,18},{3,19},{4,20},{5,21},{6,22},{7,23},{8,24},{9,... | collective-permute-start | bytes 786440 | tf_op jit(solution)/shard_map/ppermute | solution.py:246
  6.9 12.7 %copy-start.1 = (bf16[256,512]{1,0:T(8,128)(2,1)S(1)}, bf16[256,512]{1,0:T(8,128)(2,1)}, u32[]{:S(2)}) copy-start(bf16[256,512]{1,0:T(8,128)(2,1)} %refs_0_) | copy-start | bytes 786436
  6.9 13.3 %copy-start = (bf16[4096,512]{1,0:T(8,128)(2,1)S(1)}, bf16[4096,512]{1,0:T(8,128)(2,1)}, u32[]{:S(2)}) copy-start(bf16[4096,512]{1,0:T(8,128)(2,1)} %table_ref.5) | copy-start | bytes 12582916
  19.1 8.0 %collective-permute-start.2 = (bf16[256,512]{1,0:T(8,128)(2,1)S(1)}, bf16[256,512]{1,0:T(8,128)(2,1)S(1)}, u32[]{:S(2)}, u32[]{:S(2)}) collective-permute-start(bf16[256,512]{1,0:T(8,128)(2,1)S(1)} %collective-permute-done.refs_0_), channel_id=1, source_target_pairs={{0,16},{1,17},{2,18},{3,19},{4,20},{5,21},{6,22},{7,23},{8,24},{9,... | collective-permute-start | bytes 786440 | tf_op jit(solution)/shard_map/ppermute | solution.py:246
  19.7 9.4 %collective-permute-start.3 = (bf16[256,512]{1,0:T(8,128)(2,1)S(1)}, bf16[256,512]{1,0:T(8,128)(2,1)S(1)}, u32[]{:S(2)}, u32[]{:S(2)}) collective-permute-start(bf16[256,512]{1,0:T(8,128)(2,1)S(1)} %copy-done.1), channel_id=1, source_target_pairs={{0,8},{1,9},{2,10},{3,11},{4,12},{5,13},{6,14},{7,15},{8,0},{9,1},... | collective-permute-start | bytes 786440 | tf_op jit(solution)/shard_map/ppermute | solution.py:246
  19.7 9.5 %collective-permute-start.4 = (bf16[256,512]{1,0:T(8,128)(2,1)S(1)}, bf16[256,512]{1,0:T(8,128)(2,1)S(1)}, u32[]{:S(2)}, u32[]{:S(2)}) collective-permute-start(bf16[256,512]{1,0:T(8,128)(2,1)S(1)} %collective-permute-done.1.refs_2_), channel_id=1, source_target_pairs={{0,8},{1,9},{2,10},{3,11},{4,12},{5,13},{6,14},{7,15},{8,0},{9,1},... | collective-permute-start | bytes 786440 | tf_op jit(solution)/shard_map/ppermute | solution.py:246
  21.1 11.0 %copy-start.2 = (bf16[512,512]{1,0:T(8,128)(2,1)S(1)}, bf16[512,512]{1,0:T(8,128)(2,1)}, u32[]{:S(2)}) copy-start(bf16[512,512]{1,0:T(8,128)(2,1)} %weight_ref.3) | copy-start | bytes 1572868
  21.1 9.3 %collective-permute-start.7 = (bf16[128,512]{1,0:T(8,128)(2,1)S(1)}, bf16[128,512]{1,0:T(8,128)(2,1)S(1)}, u32[]{:S(2)}, u32[]{:S(2)}) collective-permute-start(bf16[128,512]{1,0:T(8,128)(2,1)S(1)} %shard_map.69), channel_id=1, source_target_pairs={{0,3},{1,2},{2,1},{3,0},{4,7},{5,6},{6,5},{7,4},{8,11},{9,10},{10,... | collective-permute-start | bytes 393224 | tf_op jit(solution)/shard_map/ppermute | solution.py:246
  23.5 6.9 %collective-permute-start.5 = (bf16[128,512]{1,0:T(8,128)(2,1)S(1)}, bf16[128,512]{1,0:T(8,128)(2,1)S(1)}, u32[]{:S(2)}, u32[]{:S(2)}) collective-permute-start(bf16[128,512]{1,0:T(8,128)(2,1)S(1)} %get-tuple-element.71), channel_id=1, source_target_pairs={{0,1},{1,0},{2,3},{3,2},{4,5},{5,4},{6,7},{7,6},{8,9},{9,8},{10,11... | collective-permute-start | bytes 393224 | tf_op jit(solution)/shard_map/ppermute | solution.py:246
  27.1 5.0 %collective-permute-start.6 = (bf16[128,512]{1,0:T(8,128)(2,1)S(1)}, bf16[128,512]{1,0:T(8,128)(2,1)S(1)}, u32[]{:S(2)}, u32[]{:S(2)}) collective-permute-start(bf16[128,512]{1,0:T(8,128)(2,1)S(1)} %get-tuple-element.72), channel_id=1, source_target_pairs={{0,2},{1,3},{2,0},{3,1},{4,6},{5,7},{6,4},{7,5},{8,10},{9,11},{10,... | collective-permute-start | bytes 393224 | tf_op jit(solution)/shard_map/ppermute | solution.py:246
  29.1 3.5 %collective-permute-start.8 = (bf16[256,512]{1,0:T(8,128)(2,1)S(1)}, bf16[256,512]{1,0:T(8,128)(2,1)S(1)}, u32[]{:S(2)}, u32[]{:S(2)}) collective-permute-start(bf16[256,512]{1,0:T(8,128)(2,1)S(1)} %collective-permute-done.refs_0_), channel_id=1, source_target_pairs={{0,8},{1,9},{2,10},{3,11},{4,12},{5,13},{6,14},{7,15},{8,0},{9,1},... | collective-permute-start | bytes 786440 | tf_op jit(solution)/shard_map/ppermute | solution.py:246
  29.2 3.4 %collective-permute-start.9 = (bf16[256,512]{1,0:T(8,128)(2,1)S(1)}, bf16[256,512]{1,0:T(8,128)(2,1)S(1)}, u32[]{:S(2)}, u32[]{:S(2)}) collective-permute-start(bf16[256,512]{1,0:T(8,128)(2,1)S(1)} %collective-permute-done.2.refs_2_), channel_id=1, source_target_pairs={{0,8},{1,9},{2,10},{3,11},{4,12},{5,13},{6,14},{7,15},{8,0},{9,1},... | collective-permute-start | bytes 786440 | tf_op jit(solution)/shard_map/ppermute | solution.py:246
  35.6 1.6 %collective-permute-start.10 = (bf16[16,16,512]{2,1,0:T(8,128)(2,1)S(1)}, bf16[16,16,512]{2,1,0:T(8,128)(2,1)S(1)}, u32[]{:S(2)}, u32[]{:S(2)}) collective-permute-start(bf16[16,16,512]{2,1,0:T(8,128)(2,1)S(1)} %get-tuple-element.87), channel_id=1, source_target_pairs={{0,8},{1,9},{2,10},{3,11},{4,12},{5,13},{6,14},{7,15},{8,0},{9,1},... | collective-permute-start | bytes 786440 | tf_op jit(solution)/shard_map/ppermute | solution.py:246
  37.3 5.6 %collective-permute-start.11 = (bf16[8,16,512]{2,1,0:T(8,128)(2,1)S(1)}, bf16[8,16,512]{2,1,0:T(8,128)(2,1)S(1)}, u32[]{:S(2)}, u32[]{:S(2)}) collective-permute-start(bf16[8,16,512]{2,1,0:T(8,128)(2,1)S(1)} %get-tuple-element.89), channel_id=1, source_target_pairs={{0,16},{1,17},{2,18},{3,19},{4,20},{5,21},{6,22},{7,23},{8,24},{9,... | collective-permute-start | bytes 393224 | tf_op jit(solution)/shard_map/ppermute | solution.py:246
  38.0 6.2 %collective-permute-start.15 = (bf16[128,512]{1,0:T(8,128)(2,1)S(1)}, bf16[128,512]{1,0:T(8,128)(2,1)S(1)}, u32[]{:S(2)}, u32[]{:S(2)}) collective-permute-start(bf16[128,512]{1,0:T(8,128)(2,1)S(1)} %get-tuple-element.83.refs_5_), channel_id=1, source_target_pairs={{0,1},{1,0},{2,3},{3,2},{4,5},{5,4},{6,7},{7,6},{8,9},{9,8},{10,11... | collective-permute-start | bytes 393224 | tf_op jit(solution)/shard_map/ppermute | solution.py:246
  38.8 7.7 %collective-permute-start.16 = (bf16[128,512]{1,0:T(8,128)(2,1)S(1)}, bf16[128,512]{1,0:T(8,128)(2,1)S(1)}, u32[]{:S(2)}, u32[]{:S(2)}) collective-permute-start(bf16[128,512]{1,0:T(8,128)(2,1)S(1)} %get-tuple-element.84.refs_6_), channel_id=1, source_target_pairs={{0,2},{1,3},{2,0},{3,1},{4,6},{5,7},{6,4},{7,5},{8,10},{9,11},{10,... | collective-permute-start | bytes 393224 | tf_op jit(solution)/shard_map/ppermute | solution.py:246
  39.5 8.5 %collective-permute-start.17 = (bf16[128,512]{1,0:T(8,128)(2,1)S(1)}, bf16[128,512]{1,0:T(8,128)(2,1)S(1)}, u32[]{:S(2)}, u32[]{:S(2)}) collective-permute-start(bf16[128,512]{1,0:T(8,128)(2,1)S(1)} %get-tuple-element.85.refs_7_), channel_id=1, source_target_pairs={{0,3},{1,2},{2,1},{3,0},{4,7},{5,6},{6,5},{7,4},{8,11},{9,10},{10,... | collective-permute-start | bytes 393224 | tf_op jit(solution)/shard_map/ppermute | solution.py:246
  43.0 5.1 %collective-permute-start.12 = (bf16[2,16,512]{2,1,0:T(8,128)(2,1)S(1)}, bf16[2,16,512]{2,1,0:T(8,128)(2,1)S(1)}, u32[]{:S(2)}, u32[]{:S(2)}) collective-permute-start(bf16[2,16,512]{2,1,0:T(8,128)(2,1)S(1)} %get-tuple-element.91), channel_id=1, source_target_pairs={{0,2},{1,3},{2,0},{3,1},{4,6},{5,7},{6,4},{7,5},{8,10},{9,11},{10,... | collective-permute-start | bytes 98312 | tf_op jit(solution)/shard_map/ppermute | solution.py:246
  43.7 4.7 %collective-permute-start.13 = (bf16[2,16,512]{2,1,0:T(8,128)(2,1)S(1)}, bf16[2,16,512]{2,1,0:T(8,128)(2,1)S(1)}, u32[]{:S(2)}, u32[]{:S(2)}) collective-permute-start(bf16[2,16,512]{2,1,0:T(8,128)(2,1)S(1)} %get-tuple-element.92), channel_id=1, source_target_pairs={{0,1},{1,0},{2,3},{3,2},{4,5},{5,4},{6,7},{7,6},{8,9},{9,8},{10,11... | collective-permute-start | bytes 98312 | tf_op jit(solution)/shard_map/ppermute | solution.py:246
  44.2 4.8 %collective-permute-start.14 = (bf16[2,16,512]{2,1,0:T(8,128)(2,1)S(1)}, bf16[2,16,512]{2,1,0:T(8,128)(2,1)S(1)}, u32[]{:S(2)}, u32[]{:S(2)}) collective-permute-start(bf16[2,16,512]{2,1,0:T(8,128)(2,1)S(1)} %get-tuple-element.93), channel_id=1, source_target_pairs={{0,3},{1,2},{2,1},{3,0},{4,7},{5,6},{6,5},{7,4},{8,11},{9,10},{10,... | collective-permute-start | bytes 98312 | tf_op jit(solution)/shard_map/ppermute | solution.py:246
  49.0 7.1 %collective-permute-start.18 = (f32[1,16,512]{2,1,0:T(8,128)S(1)}, f32[1,16,512]{2,1,0:T(8,128)S(1)}, u32[]{:S(2)}, u32[]{:S(2)}) collective-permute-start(f32[1,16,512]{2,1,0:T(8,128)S(1)} %get-tuple-element.102), channel_id=1, source_target_pairs={{0,4},{1,5},{2,6},{3,7},{4,0},{5,1},{6,2},{7,3},{8,12},{9,13},{10,... | collective-permute-start | bytes 98312 | tf_op jit(solution)/shard_map/ppermute | solution.py:246

commit v14 on v13

--- a/solution.py
+++ b/solution.py
@@ -108,7 +108,9 @@
         ref[...] = rows[k * size : (k + 1) * size]
 
 
-def prepare_kernel(near, n_batch, n, asked_ref, place_ref, low_hot_ref, block_ref):
+def prepare_kernel(near, n_batch, asked_ref, *refs):
+    *users, place_ref, low_hot_ref, block_ref, unit_ref, own_ref = refs
+    n = users[0].shape[0]
     slots = asked_ref.shape[1] // (1 + near)
     size = place_ref.shape[0] // near
     batch = (iota((size, 1), 0) >> log2(slots)) & (n_batch - 1)
@@ -119,6 +121,7 @@
     block, low = parts_of(slot_line(asked_ref[:, :slots], near, n_batch).astype(i32))
     low_hot_ref[...] = hot(low == iota(low_hot_ref.shape, 0))
     block_ref[...] = jnp.broadcast_to(block.astype(f32), block_ref.shape).astype(bf16)
+    users_kernel(0, near, place_ref, *users, unit_ref, own_ref)
 
 
 def users_kernel(level, near, place_ref, *refs):
@@ -347,26 +350,24 @@
     for mask in list(users):
         users[mask + n_item] = swap(users[mask], n_item)
 
-    place, low_hot, block = call(
-        functools.partial(prepare_kernel, near, n_batch, n),
-        [((total, 1), i32)] + [((BLOCK, total), bf16)] * 2,
+    def group(level):
+        return [users[near * level + batch * n_item] for batch in range(n_batch)]
+
+    group_outs = [((n_batch * n, width), bf16), ((total // levels, width), bf16)]
+    place, low_hot, block, *first = call(
+        functools.partial(prepare_kernel, near, n_batch),
+        [((total, 1), i32)] + [((BLOCK, total), bf16)] * 2 + group_outs,
         asked,
+        *group(0),
         free=True,
     )
     units, owns = zip(
+        first,
         *[
-            call(
-                functools.partial(users_kernel, level, near),
-                [((n_batch * n, width), bf16), ((total // levels, width), bf16)],
-                place,
-                *[users[near * level + batch * n_item] for batch in range(n_batch)],
-                free=True,
-            )
-            for level in range(levels)
-        ]
-    )
-    fetched[0], first = lax.optimization_barrier((fetched[0], (units[0], owns[0])))
-    units, owns = (first[0], *units[1:]), (first[1], *owns[1:])
+            call(functools.partial(users_kernel, level, near), group_outs, place, *group(level), free=True)
+            for level in range(1, levels)
+        ],
+    )
     hidden = call(
         functools.partial(hidden_kernel, levels),
         [((total, width), f32), ((total, 1), f32), ((total, width), bf16)],

time: 57 us -> 55.9 us (0.981)
  waiting for transfers between devices: 9.35 us -> 7.2 us
  starting transfers between devices: 21.4 us -> 22.6 us
    ppermute x19, waiting for transfers between devices: 9.35 us -> 7.2 us  [swap(): lax.ppermute(value, ('batch', 'item'), [(k, k ^ mask) for k in range(devi...]
    ppermute x19, starting transfers between devices: 21.4 us -> 22.6 us  [swap(): lax.ppermute(value, ('batch', 'item'), [(k, k ^ mask) for k in range(devi...]
    pallas_call x14 -> x13, Pallas kernels: 9.22 us -> 9.1 us  [call(): pl.pallas_call(kernel, out_shape=[jax.ShapeDtypeStruct(shape, dtype) for...]
where the time goes in v14:
time: 55.9 us; the launch traced here: 55.8 us
  starting transfers between devices  22.6 us (40%)
  Pallas kernels  12.7 us (23%)
  blocking collectives  11.7 us (21%)
  waiting for transfers between devices  7.2 us (13%)
  between operations  0.79 us (1%)
  other arithmetic  0.7 us (1%)
    ppermute x19, starting transfers between devices, swap(): lax.ppermute(value, ('batch', 'item'), [(k, k ^ mask) for k in range(devi...  22.6 us
    all_to_all x1, blocking collectives, local(): lax.all_to_all(request, ('batch', 'item'), split_axis=0, concat_axis=0, t...  11.7 us
    pallas_call x13, Pallas kernels, call(): pl.pallas_call(kernel, out_shape=[jax.ShapeDtypeStruct(shape, dtype) for...  9.1 us
    ppermute x19, waiting for transfers between devices, swap(): lax.ppermute(value, ('batch', 'item'), [(k, k ^ mask) for k in range(devi...  7.2 us
    pallas_call x1, Pallas kernels, local(): pl.pallas_call(table_kernel, out_specs=pl.BlockSpec(memory_space=pl.ANY),...  3.58 us
  transfers between devices with their start and end apart: 19, of which 7 were waited for; matrix products, arithmetic and copies ran while one was open for 1% of the time, Pallas kernels for 16%

profile of v14, /device:TPU:0, one launch (start us, length us, event | category | flops | bytes accessed | tf_op | source)
XLA Modules:
  0.0 55.8 jit_solution(7177254284627798755)
XLA Ops:
  0.6 4.1 %collective-permute-start = (bf16[256,512]{1,0:T(8,128)(2,1)}, bf16[256,512]{1,0:T(8,128)(2,1)S(1)}, u32[]{:S(2)}, u32[]{:S(2)}) collective-permute-start(bf16[256,512]{1,0:T(8,128)(2,1)} %refs_0_), channel_id=1, source_target_pairs={{0,4},{1,5},{2,6},{3,7},{4,0},{5,1},{6,2},{7,3},{8,12},{9,13},{10,... | collective-permute-start | bytes 786440 | tf_op jit(solution)/shard_map/ppermute | solution.py:249
  4.7 1.5 %collective-permute-start.1 = (bf16[256,512]{1,0:T(8,128)(2,1)}, bf16[256,512]{1,0:T(8,128)(2,1)S(1)}, u32[]{:S(2)}, u32[]{:S(2)}) collective-permute-start(bf16[256,512]{1,0:T(8,128)(2,1)} %refs_0_), channel_id=1, source_target_pairs={{0,16},{1,17},{2,18},{3,19},{4,20},{5,21},{6,22},{7,23},{8,24},{9,... | collective-permute-start | bytes 786440 | tf_op jit(solution)/shard_map/ppermute | solution.py:249
  6.2 0.7 %pad_add_fusion.named_ref = s32[2,256]{1,0:T(2,128)S(1)} fusion(s32[1,256]{1,0:T(1,128)} %bitcast.11, s32[1,256]{1,0:T(1,128)} %bitcast.12), kind=kLoop, calls=%fused_computation | loop fusion | flops 512 | bytes 4096 | tf_op jit(solution)/shard_map/stack | solution.py:316
  7.4 11.7 %all_to_all.12 = s32[32,1,80]{2,1,0:T(1,128)S(1)} all-to-all(s32[32,1,80]{2,1,0:T(1,128)S(1)} %bitcast.10), channel_id=1, replica_groups=mesh['batch'=4,'item'=8] {'batch','item'}, dimensions={0} | all-to-all | bytes 20480 | tf_op jit(solution)/shard_map/all_to_all | solution.py:319
  19.1 0.6 %collective-permute-start.4 = (bf16[256,512]{1,0:T(8,128)(2,1)S(1)}, bf16[256,512]{1,0:T(8,128)(2,1)S(1)}, u32[]{:S(2)}, u32[]{:S(2)}) collective-permute-start(bf16[256,512]{1,0:T(8,128)(2,1)S(1)} %collective-permute-done.refs_0_), channel_id=1, source_target_pairs={{0,16},{1,17},{2,18},{3,19},{4,20},{5,21},{6,22},{7,23},{8,24},{9,... | collective-permute-start | bytes 786440 | tf_op jit(solution)/shard_map/ppermute | solution.py:249
  19.7 0.9 %shard_map.69 = bf16[128,512]{1,0:T(8,128)(2,1)S(1)} custom-call(s32[32,80]{1,0:T(8,128)S(1)} %bitcast.6, bf16[4096,512]{1,0:T(8,128)(2,1)S(1)} %copy-done), custom_call_target="tpu_custom_call" | custom-call | flops 536870912 | bytes 1048576 | tf_op jit(solution)/shard_map/pallas_call | solution.py:238
  20.6 0.8 %collective-permute-start.7 = (bf16[128,512]{1,0:T(8,128)(2,1)S(1)}, bf16[128,512]{1,0:T(8,128)(2,1)S(1)}, u32[]{:S(2)}, u32[]{:S(2)}) collective-permute-start(bf16[128,512]{1,0:T(8,128)(2,1)S(1)} %shard_map.69), channel_id=1, source_target_pairs={{0,3},{1,2},{2,1},{3,0},{4,7},{5,6},{6,5},{7,4},{8,11},{9,10},{10,... | collective-permute-start | bytes 393224 | tf_op jit(solution)/shard_map/ppermute | solution.py:249
  21.4 1.6 %shard_map.70 = (bf16[128,512]{1,0:T(8,128)(2,1)S(1)}, bf16[128,512]{1,0:T(8,128)(2,1)S(1)}) custom-call(s32[32,80]{1,0:T(8,128)S(1)} %bitcast.7, bf16[4096,512]{1,0:T(8,128)(2,1)S(1)} %copy-done), custom_call_target="tpu_custom_call" | custom-call | flops 1073741824 | bytes 1048576 | tf_op jit(solution)/shard_map/pallas_call | solution.py:238
  23.0 1.3 %collective-permute-start.5 = (bf16[128,512]{1,0:T(8,128)(2,1)S(1)}, bf16[128,512]{1,0:T(8,128)(2,1)S(1)}, u32[]{:S(2)}, u32[]{:S(2)}) collective-permute-start(bf16[128,512]{1,0:T(8,128)(2,1)S(1)} %get-tuple-element.64), channel_id=1, source_target_pairs={{0,1},{1,0},{2,3},{3,2},{4,5},{5,4},{6,7},{7,6},{8,9},{9,8},{10,11... | collective-permute-start | bytes 393224 | tf_op jit(solution)/shard_map/ppermute | solution.py:249
  24.4 1.4 %collective-permute-start.6 = (bf16[128,512]{1,0:T(8,128)(2,1)S(1)}, bf16[128,512]{1,0:T(8,128)(2,1)S(1)}, u32[]{:S(2)}, u32[]{:S(2)}) collective-permute-start(bf16[128,512]{1,0:T(8,128)(2,1)S(1)} %get-tuple-element.65), channel_id=1, source_target_pairs={{0,2},{1,3},{2,0},{3,1},{4,6},{5,7},{6,4},{7,5},{8,10},{9,11},{10,... | collective-permute-start | bytes 393224 | tf_op jit(solution)/shard_map/ppermute | solution.py:249
  25.8 0.9 %shard_map.71.refs_0_ = bf16[128,512]{1,0:T(8,128)(2,1)S(1)} custom-call(s32[32,80]{1,0:T(8,128)S(1)} %bitcast.8, bf16[4096,512]{1,0:T(8,128)(2,1)S(1)} %copy-done), custom_call_target="tpu_custom_call" | custom-call | flops 536870912 | bytes 1048576 | tf_op jit(solution)/shard_map/pallas_call | solution.py:238
  27.6 1.7 %collective-permute-done.5.refs_1_ = bf16[128,512]{1,0:T(8,128)(2,1)S(1)} collective-permute-done((bf16[128,512]{1,0:T(8,128)(2,1)S(1)}, bf16[128,512]{1,0:T(8,128)(2,1)S(1)}, u32[]{:S(2)}, u32[]{:S(2)}) %collective-permute-start.5) | collective-permute-done | bytes 131104 | tf_op jit(solution)/shard_map/ppermute | solution.py:249
  29.4 0.5 shard_map.73
  29.9 1.0 %shard_map.72 = (s32[512,1]{1,0:T(8,128)S(1)}, bf16[256,512]{1,0:T(8,128)(2,1)S(1)}, bf16[256,512]{1,0:T(8,128)(2,1)S(1)}, bf16[1024,512]{1,0:T(8,128)(2,1)S(1)}, bf16[256,512]{1,0:T(8,128)(2,1)S(1)}) custom-call(s32[32,80]{1,0:T(8,128)S(1)} %bitcast.9, bf16[256,512]{1,0:T(8,128)(2,1)S(1)} %copy-done.1, bf16[256,512]{1,0:T(8,128)(2,1)S(1)} %collective-permute-done.2.refs_1_, ...), custom_call_target="tpu_custom_call" | custom-call | tf_op jit(solution)/shard_map/pallas_call | solution.py:238
  31.0 0.7 %shard_map.74 = (bf16[1024,512]{1,0:T(8,128)(2,1)S(1)}, bf16[256,512]{1,0:T(8,128)(2,1)S(1)}) custom-call(s32[512,1]{1,0:T(8,128)S(1)} %get-tuple-element.71.place_ref, bf16[256,512]{1,0:T(8,128)(2,1)S(1)} %collective-permute-done.refs_0_, bf16[256,512]{1,0:T(8,128)(2,1)S(1)} %collective-permute-done.8.refs_1_, ...), custom_call_target="tpu_custom_call" | custom-call | tf_op jit(solution)/shard_map/pallas_call | solution.py:238
  31.7 1.7 %shard_map.75 = (bf16[128,512]{1,0:T(8,128)(2,1)S(1)}, bf16[128,512]{1,0:T(8,128)(2,1)S(1)}, bf16[128,512]{1,0:T(8,128)(2,1)S(1)}, bf16[128,512]{1,0:T(8,128)(2,1)S(1)}) custom-call(f32[512,512]{1,0:T(8,128)S(1)} %get-tuple-element.67.hidden_ref, f32[512,1]{1,0:T(8,128)S(1)} %get-tuple-element.68.rscale_ref, ...), custom_call_target="tpu_custom_call" | custom-call | flops 2147483648 | bytes 1048576 | tf_op jit(solution)/shard_map/pallas_call | solution.py:238
  33.5 0.5 shard_map.76
  34.0 0.6 %collective-permute-start.10 = (bf16[16,16,512]{2,1,0:T(8,128)(2,1)S(1)}, bf16[16,16,512]{2,1,0:T(8,128)(2,1)S(1)}, u32[]{:S(2)}, u32[]{:S(2)}) collective-permute-start(bf16[16,16,512]{2,1,0:T(8,128)(2,1)S(1)} %get-tuple-element.81), channel_id=1, source_target_pairs={{0,8},{1,9},{2,10},{3,11},{4,12},{5,13},{6,14},{7,15},{8,0},{9,1},... | collective-permute-start | bytes 786440 | tf_op jit(solution)/shard_map/ppermute | solution.py:249
  34.6 1.2 %collective-permute-done.10.refs_1_ = bf16[16,16,512]{2,1,0:T(8,128)(2,1)S(1)} collective-permute-done((bf16[16,16,512]{2,1,0:T(8,128)(2,1)S(1)}, bf16[16,16,512]{2,1,0:T(8,128)(2,1)S(1)}, u32[]{:S(2)}, u32[]{:S(2)}) %collective-permute-start.10) | collective-permute-done | bytes 262176 | tf_op jit(solution)/shard_map/ppermute | solution.py:249
  35.8 1.5 %collective-permute-start.11 = (bf16[8,16,512]{2,1,0:T(8,128)(2,1)S(1)}, bf16[8,16,512]{2,1,0:T(8,128)(2,1)S(1)}, u32[]{:S(2)}, u32[]{:S(2)}) collective-permute-start(bf16[8,16,512]{2,1,0:T(8,128)(2,1)S(1)} %get-tuple-element.83), channel_id=1, source_target_pairs={{0,16},{1,17},{2,18},{3,19},{4,20},{5,21},{6,22},{7,23},{8,24},{9,... | collective-permute-start | bytes 393224 | tf_op jit(solution)/shard_map/ppermute | solution.py:249
  37.3 0.6 %collective-permute-start.15 = (bf16[128,512]{1,0:T(8,128)(2,1)S(1)}, bf16[128,512]{1,0:T(8,128)(2,1)S(1)}, u32[]{:S(2)}, u32[]{:S(2)}) collective-permute-start(bf16[128,512]{1,0:T(8,128)(2,1)S(1)} %get-tuple-element.77.refs_5_), channel_id=1, source_target_pairs={{0,1},{1,0},{2,3},{3,2},{4,5},{5,4},{6,7},{7,6},{8,9},{9,8},{10,11... | collective-permute-start | bytes 393224 | tf_op jit(solution)/shard_map/ppermute | solution.py:249
  37.9 1.2 %collective-permute-start.16 = (bf16[128,512]{1,0:T(8,128)(2,1)S(1)}, bf16[128,512]{1,0:T(8,128)(2,1)S(1)}, u32[]{:S(2)}, u32[]{:S(2)}) collective-permute-start(bf16[128,512]{1,0:T(8,128)(2,1)S(1)} %get-tuple-element.78.refs_6_), channel_id=1, source_target_pairs={{0,2},{1,3},{2,0},{3,1},{4,6},{5,7},{6,4},{7,5},{8,10},{9,11},{10,... | collective-permute-start | bytes 393224 | tf_op jit(solution)/shard_map/ppermute | solution.py:249
  39.2 1.6 %collective-permute-start.17 = (bf16[128,512]{1,0:T(8,128)(2,1)S(1)}, bf16[128,512]{1,0:T(8,128)(2,1)S(1)}, u32[]{:S(2)}, u32[]{:S(2)}) collective-permute-start(bf16[128,512]{1,0:T(8,128)(2,1)S(1)} %get-tuple-element.79.refs_7_), channel_id=1, source_target_pairs={{0,3},{1,2},{2,1},{3,0},{4,7},{5,6},{6,5},{7,4},{8,11},{9,10},{10,... | collective-permute-start | bytes 393224 | tf_op jit(solution)/shard_map/ppermute | solution.py:249
  40.8 0.9 %collective-permute-done.11.refs_1_ = bf16[8,16,512]{2,1,0:T(8,128)(2,1)S(1)} collective-permute-done((bf16[8,16,512]{2,1,0:T(8,128)(2,1)S(1)}, bf16[8,16,512]{2,1,0:T(8,128)(2,1)S(1)}, u32[]{:S(2)}, u32[]{:S(2)}) %collective-permute-start.11) | collective-permute-done | bytes 131104 | tf_op jit(solution)/shard_map/ppermute | solution.py:249
  41.7 1.1 %collective-permute-start.12 = (bf16[2,16,512]{2,1,0:T(8,128)(2,1)S(1)}, bf16[2,16,512]{2,1,0:T(8,128)(2,1)S(1)}, u32[]{:S(2)}, u32[]{:S(2)}) collective-permute-start(bf16[2,16,512]{2,1,0:T(8,128)(2,1)S(1)} %get-tuple-element.85), channel_id=1, source_target_pairs={{0,2},{1,3},{2,0},{3,1},{4,6},{5,7},{6,4},{7,5},{8,10},{9,11},{10,... | collective-permute-start | bytes 98312 | tf_op jit(solution)/shard_map/ppermute | solution.py:249
  42.8 0.7 %collective-permute-start.13 = (bf16[2,16,512]{2,1,0:T(8,128)(2,1)S(1)}, bf16[2,16,512]{2,1,0:T(8,128)(2,1)S(1)}, u32[]{:S(2)}, u32[]{:S(2)}) collective-permute-start(bf16[2,16,512]{2,1,0:T(8,128)(2,1)S(1)} %get-tuple-element.86), channel_id=1, source_target_pairs={{0,1},{1,0},{2,3},{3,2},{4,5},{5,4},{6,7},{7,6},{8,9},{9,8},{10,11... | collective-permute-start | bytes 98312 | tf_op jit(solution)/shard_map/ppermute | solution.py:249
  43.5 1.8 %collective-permute-start.14 = (bf16[2,16,512]{2,1,0:T(8,128)(2,1)S(1)}, bf16[2,16,512]{2,1,0:T(8,128)(2,1)S(1)}, u32[]{:S(2)}, u32[]{:S(2)}) collective-permute-start(bf16[2,16,512]{2,1,0:T(8,128)(2,1)S(1)} %get-tuple-element.87), channel_id=1, source_target_pairs={{0,3},{1,2},{2,1},{3,0},{4,7},{5,6},{6,5},{7,4},{8,11},{9,10},{10,... | collective-permute-start | bytes 98312 | tf_op jit(solution)/shard_map/ppermute | solution.py:249
  45.3 2.3 %collective-permute-done.17.refs_3_ = bf16[128,512]{1,0:T(8,128)(2,1)S(1)} collective-permute-done((bf16[128,512]{1,0:T(8,128)(2,1)S(1)}, bf16[128,512]{1,0:T(8,128)(2,1)S(1)}, u32[]{:S(2)}, u32[]{:S(2)}) %collective-permute-start.17) | collective-permute-done | bytes 131104 | tf_op jit(solution)/shard_map/ppermute | solution.py:249
  47.8 0.4 collective-permute-done.14.refs_3_
  48.3 3.2 %collective-permute-start.18 = (f32[1,16,512]{2,1,0:T(8,128)S(1)}, f32[1,16,512]{2,1,0:T(8,128)S(1)}, u32[]{:S(2)}, u32[]{:S(2)}) collective-permute-start(f32[1,16,512]{2,1,0:T(8,128)S(1)} %get-tuple-element.96), channel_id=1, source_target_pairs={{0,4},{1,5},{2,6},{3,7},{4,0},{5,1},{6,2},{7,3},{8,12},{9,13},{10,... | collective-permute-start | bytes 98312 | tf_op jit(solution)/shard_map/ppermute | solution.py:249
  51.5 3.6 %shard_map.79 = bf16[4096,512]{1,0:T(8,128)(2,1)} custom-call(bf16[256,512]{1,0:T(8,128)(2,1)S(1)} %get-tuple-element.59.low_hot_ref, bf16[256,512]{1,0:T(8,128)(2,1)S(1)} %get-tuple-element.60.block_ref, bf16[512,512]{1,0:T(8,128)(2,1)S(1)} %copy-done.2, bf16[128,512]{1,0:T(8,128)(2,1)S(1)} %get-tuple-element.76.refs_4_.refs_0_, ...), custom_call_target="tpu_custom_call" | custom-call | flops 2147483648 | bytes 4194304 | tf_op jit(solution)/shard_map/pallas_call | solution.py:389
  55.1 0.6 %shard_map.81 = f32[16,512]{1,0:T(8,128)} custom-call(f32[1,16,512]{2,1,0:T(8,128)S(1)} %get-tuple-element.98.refs_0_, f32[1,16,512]{2,1,0:T(8,128)S(1)} %collective-permute-done.18.refs_1_), custom_call_target="tpu_custom_call" | custom-call | bytes 1048576 | tf_op jit(solution)/shard_map/pallas_call | solution.py:238
  (28 shorter events, 1.8 us)
Async XLA Ops:
  0.6 18.4 %collective-permute-start = (bf16[256,512]{1,0:T(8,128)(2,1)}, bf16[256,512]{1,0:T(8,128)(2,1)S(1)}, u32[]{:S(2)}, u32[]{:S(2)}) collective-permute-start(bf16[256,512]{1,0:T(8,128)(2,1)} %refs_0_), channel_id=1, source_target_pairs={{0,4},{1,5},{2,6},{3,7},{4,0},{5,1},{6,2},{7,3},{8,12},{9,13},{10,... | collective-permute-start | bytes 786440 | tf_op jit(solution)/shard_map/ppermute | solution.py:249
  4.7 14.4 %collective-permute-start.1 = (bf16[256,512]{1,0:T(8,128)(2,1)}, bf16[256,512]{1,0:T(8,128)(2,1)S(1)}, u32[]{:S(2)}, u32[]{:S(2)}) collective-permute-start(bf16[256,512]{1,0:T(8,128)(2,1)} %refs_0_), channel_id=1, source_target_pairs={{0,16},{1,17},{2,18},{3,19},{4,20},{5,21},{6,22},{7,23},{8,24},{9,... | collective-permute-start | bytes 786440 | tf_op jit(solution)/shard_map/ppermute | solution.py:249
  6.9 12.7 %copy-start = (bf16[4096,512]{1,0:T(8,128)(2,1)S(1)}, bf16[4096,512]{1,0:T(8,128)(2,1)}, u32[]{:S(2)}) copy-start(bf16[4096,512]{1,0:T(8,128)(2,1)} %table_ref.5) | copy-start | bytes 12582916
  19.1 8.0 %collective-permute-start.4 = (bf16[256,512]{1,0:T(8,128)(2,1)S(1)}, bf16[256,512]{1,0:T(8,128)(2,1)S(1)}, u32[]{:S(2)}, u32[]{:S(2)}) collective-permute-start(bf16[256,512]{1,0:T(8,128)(2,1)S(1)} %collective-permute-done.refs_0_), channel_id=1, source_target_pairs={{0,16},{1,17},{2,18},{3,19},{4,20},{5,21},{6,22},{7,23},{8,24},{9,... | collective-permute-start | bytes 786440 | tf_op jit(solution)/shard_map/ppermute | solution.py:249
  20.6 6.5 %copy-start.1 = (bf16[256,512]{1,0:T(8,128)(2,1)S(1)}, bf16[256,512]{1,0:T(8,128)(2,1)}, u32[]{:S(2)}) copy-start(bf16[256,512]{1,0:T(8,128)(2,1)} %refs_0_) | copy-start | bytes 786436
  20.6 8.8 %copy-start.2 = (bf16[512,512]{1,0:T(8,128)(2,1)S(1)}, bf16[512,512]{1,0:T(8,128)(2,1)}, u32[]{:S(2)}) copy-start(bf16[512,512]{1,0:T(8,128)(2,1)} %weight_ref.3) | copy-start | bytes 1572868
  20.6 6.7 %collective-permute-start.7 = (bf16[128,512]{1,0:T(8,128)(2,1)S(1)}, bf16[128,512]{1,0:T(8,128)(2,1)S(1)}, u32[]{:S(2)}, u32[]{:S(2)}) collective-permute-start(bf16[128,512]{1,0:T(8,128)(2,1)S(1)} %shard_map.69), channel_id=1, source_target_pairs={{0,3},{1,2},{2,1},{3,0},{4,7},{5,6},{6,5},{7,4},{8,11},{9,10},{10,... | collective-permute-start | bytes 393224 | tf_op jit(solution)/shard_map/ppermute | solution.py:249
  23.0 6.4 %collective-permute-start.5 = (bf16[128,512]{1,0:T(8,128)(2,1)S(1)}, bf16[128,512]{1,0:T(8,128)(2,1)S(1)}, u32[]{:S(2)}, u32[]{:S(2)}) collective-permute-start(bf16[128,512]{1,0:T(8,128)(2,1)S(1)} %get-tuple-element.64), channel_id=1, source_target_pairs={{0,1},{1,0},{2,3},{3,2},{4,5},{5,4},{6,7},{7,6},{8,9},{9,8},{10,11... | collective-permute-start | bytes 393224 | tf_op jit(solution)/shard_map/ppermute | solution.py:249
  24.4 5.0 %collective-permute-start.6 = (bf16[128,512]{1,0:T(8,128)(2,1)S(1)}, bf16[128,512]{1,0:T(8,128)(2,1)S(1)}, u32[]{:S(2)}, u32[]{:S(2)}) collective-permute-start(bf16[128,512]{1,0:T(8,128)(2,1)S(1)} %get-tuple-element.65), channel_id=1, source_target_pairs={{0,2},{1,3},{2,0},{3,1},{4,6},{5,7},{6,4},{7,5},{8,10},{9,11},{10,... | collective-permute-start | bytes 393224 | tf_op jit(solution)/shard_map/ppermute | solution.py:249
  25.8 5.2 %collective-permute-start.8 = (bf16[256,512]{1,0:T(8,128)(2,1)S(1)}, bf16[256,512]{1,0:T(8,128)(2,1)S(1)}, u32[]{:S(2)}, u32[]{:S(2)}) collective-permute-start(bf16[256,512]{1,0:T(8,128)(2,1)S(1)} %collective-permute-done.refs_0_), channel_id=1, source_target_pairs={{0,8},{1,9},{2,10},{3,11},{4,12},{5,13},{6,14},{7,15},{8,0},{9,1},... | collective-permute-start | bytes 786440 | tf_op jit(solution)/shard_map/ppermute | solution.py:249
  27.1 2.8 %collective-permute-start.2 = (bf16[256,512]{1,0:T(8,128)(2,1)S(1)}, bf16[256,512]{1,0:T(8,128)(2,1)S(1)}, u32[]{:S(2)}, u32[]{:S(2)}) collective-permute-start(bf16[256,512]{1,0:T(8,128)(2,1)S(1)} %copy-done.1), channel_id=1, source_target_pairs={{0,8},{1,9},{2,10},{3,11},{4,12},{5,13},{6,14},{7,15},{8,0},{9,1},... | collective-permute-start | bytes 786440 | tf_op jit(solution)/shard_map/ppermute | solution.py:249
  27.3 2.6 %collective-permute-start.3 = (bf16[256,512]{1,0:T(8,128)(2,1)S(1)}, bf16[256,512]{1,0:T(8,128)(2,1)S(1)}, u32[]{:S(2)}, u32[]{:S(2)}) collective-permute-start(bf16[256,512]{1,0:T(8,128)(2,1)S(1)} %collective-permute-done.1.refs_2_), channel_id=1, source_target_pairs={{0,8},{1,9},{2,10},{3,11},{4,12},{5,13},{6,14},{7,15},{8,0},{9,1},... | collective-permute-start | bytes 786440 | tf_op jit(solution)/shard_map/ppermute | solution.py:249
  29.4 1.6 %collective-permute-start.9 = (bf16[256,512]{1,0:T(8,128)(2,1)S(1)}, bf16[256,512]{1,0:T(8,128)(2,1)S(1)}, u32[]{:S(2)}, u32[]{:S(2)}) collective-permute-start(bf16[256,512]{1,0:T(8,128)(2,1)S(1)} %collective-permute-done.4.refs_2_), channel_id=1, source_target_pairs={{0,8},{1,9},{2,10},{3,11},{4,12},{5,13},{6,14},{7,15},{8,0},{9,1},... | collective-permute-start | bytes 786440 | tf_op jit(solution)/shard_map/ppermute | solution.py:249
  34.0 1.8 %collective-permute-start.10 = (bf16[16,16,512]{2,1,0:T(8,128)(2,1)S(1)}, bf16[16,16,512]{2,1,0:T(8,128)(2,1)S(1)}, u32[]{:S(2)}, u32[]{:S(2)}) collective-permute-start(bf16[16,16,512]{2,1,0:T(8,128)(2,1)S(1)} %get-tuple-element.81), channel_id=1, source_target_pairs={{0,8},{1,9},{2,10},{3,11},{4,12},{5,13},{6,14},{7,15},{8,0},{9,1},... | collective-permute-start | bytes 786440 | tf_op jit(solution)/shard_map/ppermute | solution.py:249
  35.8 5.8 %collective-permute-start.11 = (bf16[8,16,512]{2,1,0:T(8,128)(2,1)S(1)}, bf16[8,16,512]{2,1,0:T(8,128)(2,1)S(1)}, u32[]{:S(2)}, u32[]{:S(2)}) collective-permute-start(bf16[8,16,512]{2,1,0:T(8,128)(2,1)S(1)} %get-tuple-element.83), channel_id=1, source_target_pairs={{0,16},{1,17},{2,18},{3,19},{4,20},{5,21},{6,22},{7,23},{8,24},{9,... | collective-permute-start | bytes 393224 | tf_op jit(solution)/shard_map/ppermute | solution.py:249
  37.3 6.2 %collective-permute-start.15 = (bf16[128,512]{1,0:T(8,128)(2,1)S(1)}, bf16[128,512]{1,0:T(8,128)(2,1)S(1)}, u32[]{:S(2)}, u32[]{:S(2)}) collective-permute-start(bf16[128,512]{1,0:T(8,128)(2,1)S(1)} %get-tuple-element.77.refs_5_), channel_id=1, source_target_pairs={{0,1},{1,0},{2,3},{3,2},{4,5},{5,4},{6,7},{7,6},{8,9},{9,8},{10,11... | collective-permute-start | bytes 393224 | tf_op jit(solution)/shard_map/ppermute | solution.py:249
  37.9 7.3 %collective-permute-start.16 = (bf16[128,512]{1,0:T(8,128)(2,1)S(1)}, bf16[128,512]{1,0:T(8,128)(2,1)S(1)}, u32[]{:S(2)}, u32[]{:S(2)}) collective-permute-start(bf16[128,512]{1,0:T(8,128)(2,1)S(1)} %get-tuple-element.78.refs_6_), channel_id=1, source_target_pairs={{0,2},{1,3},{2,0},{3,1},{4,6},{5,7},{6,4},{7,5},{8,10},{9,11},{10,... | collective-permute-start | bytes 393224 | tf_op jit(solution)/shard_map/ppermute | solution.py:249
  39.2 8.4 %collective-permute-start.17 = (bf16[128,512]{1,0:T(8,128)(2,1)S(1)}, bf16[128,512]{1,0:T(8,128)(2,1)S(1)}, u32[]{:S(2)}, u32[]{:S(2)}) collective-permute-start(bf16[128,512]{1,0:T(8,128)(2,1)S(1)} %get-tuple-element.79.refs_7_), channel_id=1, source_target_pairs={{0,3},{1,2},{2,1},{3,0},{4,7},{5,6},{6,5},{7,4},{8,11},{9,10},{10,... | collective-permute-start | bytes 393224 | tf_op jit(solution)/shard_map/ppermute | solution.py:249
  41.7 5.9 %collective-permute-start.12 = (bf16[2,16,512]{2,1,0:T(8,128)(2,1)S(1)}, bf16[2,16,512]{2,1,0:T(8,128)(2,1)S(1)}, u32[]{:S(2)}, u32[]{:S(2)}) collective-permute-start(bf16[2,16,512]{2,1,0:T(8,128)(2,1)S(1)} %get-tuple-element.85), channel_id=1, source_target_pairs={{0,2},{1,3},{2,0},{3,1},{4,6},{5,7},{6,4},{7,5},{8,10},{9,11},{10,... | collective-permute-start | bytes 98312 | tf_op jit(solution)/shard_map/ppermute | solution.py:249
  42.8 5.1 %collective-permute-start.13 = (bf16[2,16,512]{2,1,0:T(8,128)(2,1)S(1)}, bf16[2,16,512]{2,1,0:T(8,128)(2,1)S(1)}, u32[]{:S(2)}, u32[]{:S(2)}) collective-permute-start(bf16[2,16,512]{2,1,0:T(8,128)(2,1)S(1)} %get-tuple-element.86), channel_id=1, source_target_pairs={{0,1},{1,0},{2,3},{3,2},{4,5},{5,4},{6,7},{7,6},{8,9},{9,8},{10,11... | collective-permute-start | bytes 98312 | tf_op jit(solution)/shard_map/ppermute | solution.py:249
  43.5 4.8 %collective-permute-start.14 = (bf16[2,16,512]{2,1,0:T(8,128)(2,1)S(1)}, bf16[2,16,512]{2,1,0:T(8,128)(2,1)S(1)}, u32[]{:S(2)}, u32[]{:S(2)}) collective-permute-start(bf16[2,16,512]{2,1,0:T(8,128)(2,1)S(1)} %get-tuple-element.87), channel_id=1, source_target_pairs={{0,3},{1,2},{2,1},{3,0},{4,7},{5,6},{6,5},{7,4},{8,11},{9,10},{10,... | collective-permute-start | bytes 98312 | tf_op jit(solution)/shard_map/ppermute | solution.py:249
  48.3 6.8 %collective-permute-start.18 = (f32[1,16,512]{2,1,0:T(8,128)S(1)}, f32[1,16,512]{2,1,0:T(8,128)S(1)}, u32[]{:S(2)}, u32[]{:S(2)}) collective-permute-start(f32[1,16,512]{2,1,0:T(8,128)S(1)} %get-tuple-element.96), channel_id=1, source_target_pairs={{0,4},{1,5},{2,6},{3,7},{4,0},{5,1},{6,2},{7,3},{8,12},{9,13},{10,... | collective-permute-start | bytes 98312 | tf_op jit(solution)/shard_map/ppermute | solution.py:249

commit v15 on v14

--- a/solution.py
+++ b/solution.py
@@ -342,12 +342,9 @@
         asked, *values = lax.optimization_barrier((asked, *fetch(parts)))
         for part, value in zip(parts, values):
             fetched[part] = swap(value, part) if part else value
-    late = [mask for mask in users if mask not in early]
-    fetched[0], *values = lax.optimization_barrier((fetched[0], *[users[mask] for mask in late]))
-    users.update(zip(late, values))
     fetched = [fetched[part] for part in range(near)]
 
-    for mask in list(users):
+    for mask in [0, *far]:
         users[mask + n_item] = swap(users[mask], n_item)
 
     def group(level):
@@ -361,6 +358,9 @@
         *group(0),
         free=True,
     )
+    late = {mask: users[mask] for mask in users if mask & (n_item - near)}
+    place, late = lax.optimization_barrier((place, late))
+    users |= late | {mask + n_item: swap(late[mask], n_item) for mask in late}
     units, owns = zip(
         first,
         *[

time: 55.9 us -> 55.2 us (0.987)
  waiting for transfers between devices: 7.2 us -> 6.57 us
    ppermute x19, waiting for transfers between devices: 7.2 us -> 6.57 us  [swap(): lax.ppermute(value, ('batch', 'item'), [(k, k ^ mask) for k in range(devi...]
  transfers between devices with their start and end apart: 19 -> 19, of which waited for: 7 -> 6; matrix products, arithmetic and copies ran while one was open for 1% -> 1% of each run, Pallas kernels for 16% -> 16%
where the time goes in v15:
time: 55.2 us; the launch traced here: 55 us
  starting transfers between devices  22.6 us (41%)
  Pallas kernels  12.7 us (23%)
  blocking collectives  11.7 us (21%)
  waiting for transfers between devices  6.57 us (12%)
  between operations  0.8 us (1%)
  other arithmetic  0.7 us (1%)
    ppermute x19, starting transfers between devices, swap(): lax.ppermute(value, ('batch', 'item'), [(k, k ^ mask) for k in range(devi...  22.6 us
    all_to_all x1, blocking collectives, local(): lax.all_to_all(request, ('batch', 'item'), split_axis=0, concat_axis=0, t...  11.7 us
    pallas_call x13, Pallas kernels, call(): pl.pallas_call(kernel, out_shape=[jax.ShapeDtypeStruct(shape, dtype) for...  9.08 us
    ppermute x19, waiting for transfers between devices, swap(): lax.ppermute(value, ('batch', 'item'), [(k, k ^ mask) for k in range(devi...  6.57 us
    pallas_call x1, Pallas kernels, local(): pl.pallas_call(table_kernel, out_specs=pl.BlockSpec(memory_space=pl.ANY),...  3.58 us
  transfers between devices with their start and end apart: 19, of which 6 were waited for; matrix products, arithmetic and copies ran while one was open for 1% of the time, Pallas kernels for 16%

profile of v15, /device:TPU:0, one launch (start us, length us, event | category | flops | bytes accessed | tf_op | source)
XLA Modules:
  0.0 55.0 jit_solution(799323283396901459)
XLA Ops:
  0.6 4.1 %collective-permute-start = (bf16[256,512]{1,0:T(8,128)(2,1)}, bf16[256,512]{1,0:T(8,128)(2,1)S(1)}, u32[]{:S(2)}, u32[]{:S(2)}) collective-permute-start(bf16[256,512]{1,0:T(8,128)(2,1)} %refs_0_), channel_id=1, source_target_pairs={{0,4},{1,5},{2,6},{3,7},{4,0},{5,1},{6,2},{7,3},{8,12},{9,13},{10,... | collective-permute-start | bytes 786440 | tf_op jit(solution)/shard_map/ppermute | solution.py:249
  4.7 1.5 %collective-permute-start.1 = (bf16[256,512]{1,0:T(8,128)(2,1)}, bf16[256,512]{1,0:T(8,128)(2,1)S(1)}, u32[]{:S(2)}, u32[]{:S(2)}) collective-permute-start(bf16[256,512]{1,0:T(8,128)(2,1)} %refs_0_), channel_id=1, source_target_pairs={{0,16},{1,17},{2,18},{3,19},{4,20},{5,21},{6,22},{7,23},{8,24},{9,... | collective-permute-start | bytes 786440 | tf_op jit(solution)/shard_map/ppermute | solution.py:249
  6.2 0.7 %pad_add_fusion.named_ref = s32[2,256]{1,0:T(2,128)S(1)} fusion(s32[1,256]{1,0:T(1,128)} %bitcast.11, s32[1,256]{1,0:T(1,128)} %bitcast.12), kind=kLoop, calls=%fused_computation | loop fusion | flops 512 | bytes 4096 | tf_op jit(solution)/shard_map/stack | solution.py:316
  7.4 11.7 %all_to_all.12 = s32[32,1,80]{2,1,0:T(1,128)S(1)} all-to-all(s32[32,1,80]{2,1,0:T(1,128)S(1)} %bitcast.10), channel_id=1, replica_groups=mesh['batch'=4,'item'=8] {'batch','item'}, dimensions={0} | all-to-all | bytes 20480 | tf_op jit(solution)/shard_map/all_to_all | solution.py:319
  19.7 0.6 %collective-permute-start.7 = (bf16[256,512]{1,0:T(8,128)(2,1)S(1)}, bf16[256,512]{1,0:T(8,128)(2,1)S(1)}, u32[]{:S(2)}, u32[]{:S(2)}) collective-permute-start(bf16[256,512]{1,0:T(8,128)(2,1)S(1)} %collective-permute-done.refs_0_), channel_id=1, source_target_pairs={{0,16},{1,17},{2,18},{3,19},{4,20},{5,21},{6,22},{7,23},{8,24},{9,... | collective-permute-start | bytes 786440 | tf_op jit(solution)/shard_map/ppermute | solution.py:249
  20.3 0.9 %shard_map.69 = bf16[128,512]{1,0:T(8,128)(2,1)S(1)} custom-call(s32[32,80]{1,0:T(8,128)S(1)} %bitcast.6, bf16[4096,512]{1,0:T(8,128)(2,1)S(1)} %copy-done), custom_call_target="tpu_custom_call" | custom-call | flops 536870912 | bytes 1048576 | tf_op jit(solution)/shard_map/pallas_call | solution.py:238
  21.2 0.8 %collective-permute-start.6 = (bf16[128,512]{1,0:T(8,128)(2,1)S(1)}, bf16[128,512]{1,0:T(8,128)(2,1)S(1)}, u32[]{:S(2)}, u32[]{:S(2)}) collective-permute-start(bf16[128,512]{1,0:T(8,128)(2,1)S(1)} %shard_map.69), channel_id=1, source_target_pairs={{0,3},{1,2},{2,1},{3,0},{4,7},{5,6},{6,5},{7,4},{8,11},{9,10},{10,... | collective-permute-start | bytes 393224 | tf_op jit(solution)/shard_map/ppermute | solution.py:249
  22.0 1.6 %shard_map.70 = (bf16[128,512]{1,0:T(8,128)(2,1)S(1)}, bf16[128,512]{1,0:T(8,128)(2,1)S(1)}) custom-call(s32[32,80]{1,0:T(8,128)S(1)} %bitcast.7, bf16[4096,512]{1,0:T(8,128)(2,1)S(1)} %copy-done), custom_call_target="tpu_custom_call" | custom-call | flops 1073741824 | bytes 1048576 | tf_op jit(solution)/shard_map/pallas_call | solution.py:238
  23.6 1.3 %collective-permute-start.4 = (bf16[128,512]{1,0:T(8,128)(2,1)S(1)}, bf16[128,512]{1,0:T(8,128)(2,1)S(1)}, u32[]{:S(2)}, u32[]{:S(2)}) collective-permute-start(bf16[128,512]{1,0:T(8,128)(2,1)S(1)} %get-tuple-element.63), channel_id=1, source_target_pairs={{0,1},{1,0},{2,3},{3,2},{4,5},{5,4},{6,7},{7,6},{8,9},{9,8},{10,11... | collective-permute-start | bytes 393224 | tf_op jit(solution)/shard_map/ppermute | solution.py:249
  24.9 1.5 %collective-permute-start.5 = (bf16[128,512]{1,0:T(8,128)(2,1)S(1)}, bf16[128,512]{1,0:T(8,128)(2,1)S(1)}, u32[]{:S(2)}, u32[]{:S(2)}) collective-permute-start(bf16[128,512]{1,0:T(8,128)(2,1)S(1)} %get-tuple-element.64), channel_id=1, source_target_pairs={{0,2},{1,3},{2,0},{3,1},{4,6},{5,7},{6,4},{7,5},{8,10},{9,11},{10,... | collective-permute-start | bytes 393224 | tf_op jit(solution)/shard_map/ppermute | solution.py:249
  26.4 0.9 %shard_map.71.refs_0_ = bf16[128,512]{1,0:T(8,128)(2,1)S(1)} custom-call(s32[32,80]{1,0:T(8,128)S(1)} %bitcast.8, bf16[4096,512]{1,0:T(8,128)(2,1)S(1)} %copy-done), custom_call_target="tpu_custom_call" | custom-call | flops 536870912 | bytes 1048576 | tf_op jit(solution)/shard_map/pallas_call | solution.py:238
  27.3 1.0 %shard_map.72 = (s32[512,1]{1,0:T(8,128)S(1)}, bf16[256,512]{1,0:T(8,128)(2,1)S(1)}, bf16[256,512]{1,0:T(8,128)(2,1)S(1)}, bf16[1024,512]{1,0:T(8,128)(2,1)S(1)}, bf16[256,512]{1,0:T(8,128)(2,1)S(1)}) custom-call(s32[32,80]{1,0:T(8,128)S(1)} %bitcast.9, bf16[256,512]{1,0:T(8,128)(2,1)S(1)} %copy-done.1, bf16[256,512]{1,0:T(8,128)(2,1)S(1)} %collective-permute-done.2.refs_1_, ...), custom_call_target="tpu_custom_call" | custom-call | tf_op jit(solution)/shard_map/pallas_call | solution.py:238
  28.4 0.5 collective-permute-start.9
  28.9 1.2 %collective-permute-done.4.refs_1_ = bf16[128,512]{1,0:T(8,128)(2,1)S(1)} collective-permute-done((bf16[128,512]{1,0:T(8,128)(2,1)S(1)}, bf16[128,512]{1,0:T(8,128)(2,1)S(1)}, u32[]{:S(2)}, u32[]{:S(2)}) %collective-permute-start.4) | collective-permute-done | bytes 131104 | tf_op jit(solution)/shard_map/ppermute | solution.py:249
  30.2 0.5 shard_map.73
  30.7 0.7 %shard_map.74 = (bf16[1024,512]{1,0:T(8,128)(2,1)S(1)}, bf16[256,512]{1,0:T(8,128)(2,1)S(1)}) custom-call(s32[512,1]{1,0:T(8,128)S(1)} %get-tuple-element.72.place_ref, bf16[256,512]{1,0:T(8,128)(2,1)S(1)} %collective-permute-done.refs_0_, bf16[256,512]{1,0:T(8,128)(2,1)S(1)} %collective-permute-done.8.refs_1_, ...), custom_call_target="tpu_custom_call" | custom-call | tf_op jit(solution)/shard_map/pallas_call | solution.py:238
  31.4 1.7 %shard_map.75 = (bf16[128,512]{1,0:T(8,128)(2,1)S(1)}, bf16[128,512]{1,0:T(8,128)(2,1)S(1)}, bf16[128,512]{1,0:T(8,128)(2,1)S(1)}, bf16[128,512]{1,0:T(8,128)(2,1)S(1)}) custom-call(f32[512,512]{1,0:T(8,128)S(1)} %get-tuple-element.66.hidden_ref, f32[512,1]{1,0:T(8,128)S(1)} %get-tuple-element.67.rscale_ref, ...), custom_call_target="tpu_custom_call" | custom-call | flops 2147483648 | bytes 1048576 | tf_op jit(solution)/shard_map/pallas_call | solution.py:238
  33.1 0.5 shard_map.76
  33.8 1.5 %collective-permute-done.10.refs_1_ = bf16[16,16,512]{2,1,0:T(8,128)(2,1)S(1)} collective-permute-done((bf16[16,16,512]{2,1,0:T(8,128)(2,1)S(1)}, bf16[16,16,512]{2,1,0:T(8,128)(2,1)S(1)}, u32[]{:S(2)}, u32[]{:S(2)}) %collective-permute-start.10) | collective-permute-done | bytes 262176 | tf_op jit(solution)/shard_map/ppermute | solution.py:249
  35.4 1.5 %collective-permute-start.11 = (bf16[8,16,512]{2,1,0:T(8,128)(2,1)S(1)}, bf16[8,16,512]{2,1,0:T(8,128)(2,1)S(1)}, u32[]{:S(2)}, u32[]{:S(2)}) collective-permute-start(bf16[8,16,512]{2,1,0:T(8,128)(2,1)S(1)} %get-tuple-element.85), channel_id=1, source_target_pairs={{0,16},{1,17},{2,18},{3,19},{4,20},{5,21},{6,22},{7,23},{8,24},{9,... | collective-permute-start | bytes 393224 | tf_op jit(solution)/shard_map/ppermute | solution.py:249
  36.9 0.6 %collective-permute-start.15 = (bf16[128,512]{1,0:T(8,128)(2,1)S(1)}, bf16[128,512]{1,0:T(8,128)(2,1)S(1)}, u32[]{:S(2)}, u32[]{:S(2)}) collective-permute-start(bf16[128,512]{1,0:T(8,128)(2,1)S(1)} %get-tuple-element.79.refs_5_), channel_id=1, source_target_pairs={{0,1},{1,0},{2,3},{3,2},{4,5},{5,4},{6,7},{7,6},{8,9},{9,8},{10,11... | collective-permute-start | bytes 393224 | tf_op jit(solution)/shard_map/ppermute | solution.py:249
  37.5 1.2 %collective-permute-start.16 = (bf16[128,512]{1,0:T(8,128)(2,1)S(1)}, bf16[128,512]{1,0:T(8,128)(2,1)S(1)}, u32[]{:S(2)}, u32[]{:S(2)}) collective-permute-start(bf16[128,512]{1,0:T(8,128)(2,1)S(1)} %get-tuple-element.80.refs_6_), channel_id=1, source_target_pairs={{0,2},{1,3},{2,0},{3,1},{4,6},{5,7},{6,4},{7,5},{8,10},{9,11},{10,... | collective-permute-start | bytes 393224 | tf_op jit(solution)/shard_map/ppermute | solution.py:249
  38.7 1.7 %collective-permute-start.17 = (bf16[128,512]{1,0:T(8,128)(2,1)S(1)}, bf16[128,512]{1,0:T(8,128)(2,1)S(1)}, u32[]{:S(2)}, u32[]{:S(2)}) collective-permute-start(bf16[128,512]{1,0:T(8,128)(2,1)S(1)} %get-tuple-element.81.refs_7_), channel_id=1, source_target_pairs={{0,3},{1,2},{2,1},{3,0},{4,7},{5,6},{6,5},{7,4},{8,11},{9,10},{10,... | collective-permute-start | bytes 393224 | tf_op jit(solution)/shard_map/ppermute | solution.py:249
  40.4 0.6 %collective-permute-done.11.refs_1_ = bf16[8,16,512]{2,1,0:T(8,128)(2,1)S(1)} collective-permute-done((bf16[8,16,512]{2,1,0:T(8,128)(2,1)S(1)}, bf16[8,16,512]{2,1,0:T(8,128)(2,1)S(1)}, u32[]{:S(2)}, u32[]{:S(2)}) %collective-permute-start.11) | collective-permute-done | bytes 131104 | tf_op jit(solution)/shard_map/ppermute | solution.py:249
  41.0 1.3 %collective-permute-start.12 = (bf16[2,16,512]{2,1,0:T(8,128)(2,1)S(1)}, bf16[2,16,512]{2,1,0:T(8,128)(2,1)S(1)}, u32[]{:S(2)}, u32[]{:S(2)}) collective-permute-start(bf16[2,16,512]{2,1,0:T(8,128)(2,1)S(1)} %get-tuple-element.87), channel_id=1, source_target_pairs={{0,2},{1,3},{2,0},{3,1},{4,6},{5,7},{6,4},{7,5},{8,10},{9,11},{10,... | collective-permute-start | bytes 98312 | tf_op jit(solution)/shard_map/ppermute | solution.py:249
  42.3 0.7 %collective-permute-start.13 = (bf16[2,16,512]{2,1,0:T(8,128)(2,1)S(1)}, bf16[2,16,512]{2,1,0:T(8,128)(2,1)S(1)}, u32[]{:S(2)}, u32[]{:S(2)}) collective-permute-start(bf16[2,16,512]{2,1,0:T(8,128)(2,1)S(1)} %get-tuple-element.88), channel_id=1, source_target_pairs={{0,1},{1,0},{2,3},{3,2},{4,5},{5,4},{6,7},{7,6},{8,9},{9,8},{10,11... | collective-permute-start | bytes 98312 | tf_op jit(solution)/shard_map/ppermute | solution.py:249
  43.0 1.6 %collective-permute-start.14 = (bf16[2,16,512]{2,1,0:T(8,128)(2,1)S(1)}, bf16[2,16,512]{2,1,0:T(8,128)(2,1)S(1)}, u32[]{:S(2)}, u32[]{:S(2)}) collective-permute-start(bf16[2,16,512]{2,1,0:T(8,128)(2,1)S(1)} %get-tuple-element.89), channel_id=1, source_target_pairs={{0,3},{1,2},{2,1},{3,0},{4,7},{5,6},{6,5},{7,4},{8,11},{9,10},{10,... | collective-permute-start | bytes 98312 | tf_op jit(solution)/shard_map/ppermute | solution.py:249
  44.6 2.3 %collective-permute-done.17.refs_3_ = bf16[128,512]{1,0:T(8,128)(2,1)S(1)} collective-permute-done((bf16[128,512]{1,0:T(8,128)(2,1)S(1)}, bf16[128,512]{1,0:T(8,128)(2,1)S(1)}, u32[]{:S(2)}, u32[]{:S(2)}) %collective-permute-start.17) | collective-permute-done | bytes 131104 | tf_op jit(solution)/shard_map/ppermute | solution.py:249
  47.2 0.6 %collective-permute-done.14.refs_3_ = bf16[2,16,512]{2,1,0:T(8,128)(2,1)S(1)} collective-permute-done((bf16[2,16,512]{2,1,0:T(8,128)(2,1)S(1)}, bf16[2,16,512]{2,1,0:T(8,128)(2,1)S(1)}, u32[]{:S(2)}, u32[]{:S(2)}) %collective-permute-start.14) | collective-permute-done | bytes 32800 | tf_op jit(solution)/shard_map/ppermute | solution.py:249
  47.8 3.0 %collective-permute-start.18 = (f32[1,16,512]{2,1,0:T(8,128)S(1)}, f32[1,16,512]{2,1,0:T(8,128)S(1)}, u32[]{:S(2)}, u32[]{:S(2)}) collective-permute-start(f32[1,16,512]{2,1,0:T(8,128)S(1)} %get-tuple-element.98), channel_id=1, source_target_pairs={{0,4},{1,5},{2,6},{3,7},{4,0},{5,1},{6,2},{7,3},{8,12},{9,13},{10,... | collective-permute-start | bytes 98312 | tf_op jit(solution)/shard_map/ppermute | solution.py:249
  50.8 3.6 %shard_map.79 = bf16[4096,512]{1,0:T(8,128)(2,1)} custom-call(bf16[256,512]{1,0:T(8,128)(2,1)S(1)} %get-tuple-element.60.low_hot_ref, bf16[256,512]{1,0:T(8,128)(2,1)S(1)} %get-tuple-element.61.block_ref, bf16[512,512]{1,0:T(8,128)(2,1)S(1)} %copy-done.2, bf16[128,512]{1,0:T(8,128)(2,1)S(1)} %get-tuple-element.78.refs_4_.refs_0_, ...), custom_call_target="tpu_custom_call" | custom-call | flops 2147483648 | bytes 4194304 | tf_op jit(solution)/shard_map/pallas_call | solution.py:389
  54.4 0.6 %shard_map.81 = f32[16,512]{1,0:T(8,128)} custom-call(f32[1,16,512]{2,1,0:T(8,128)S(1)} %get-tuple-element.100.refs_0_, f32[1,16,512]{2,1,0:T(8,128)S(1)} %collective-permute-done.18.refs_1_), custom_call_target="tpu_custom_call" | custom-call | bytes 1048576 | tf_op jit(solution)/shard_map/pallas_call | solution.py:238
  (28 shorter events, 1.7 us)
Async XLA Ops:
  0.6 18.4 %collective-permute-start = (bf16[256,512]{1,0:T(8,128)(2,1)}, bf16[256,512]{1,0:T(8,128)(2,1)S(1)}, u32[]{:S(2)}, u32[]{:S(2)}) collective-permute-start(bf16[256,512]{1,0:T(8,128)(2,1)} %refs_0_), channel_id=1, source_target_pairs={{0,4},{1,5},{2,6},{3,7},{4,0},{5,1},{6,2},{7,3},{8,12},{9,13},{10,... | collective-permute-start | bytes 786440 | tf_op jit(solution)/shard_map/ppermute | solution.py:249
  4.7 14.4 %collective-permute-start.1 = (bf16[256,512]{1,0:T(8,128)(2,1)}, bf16[256,512]{1,0:T(8,128)(2,1)S(1)}, u32[]{:S(2)}, u32[]{:S(2)}) collective-permute-start(bf16[256,512]{1,0:T(8,128)(2,1)} %refs_0_), channel_id=1, source_target_pairs={{0,16},{1,17},{2,18},{3,19},{4,20},{5,21},{6,22},{7,23},{8,24},{9,... | collective-permute-start | bytes 786440 | tf_op jit(solution)/shard_map/ppermute | solution.py:249
  6.9 12.2 %copy-start.1 = (bf16[256,512]{1,0:T(8,128)(2,1)S(1)}, bf16[256,512]{1,0:T(8,128)(2,1)}, u32[]{:S(2)}) copy-start(bf16[256,512]{1,0:T(8,128)(2,1)} %refs_0_) | copy-start | bytes 786436
  6.9 13.3 %copy-start = (bf16[4096,512]{1,0:T(8,128)(2,1)S(1)}, bf16[4096,512]{1,0:T(8,128)(2,1)}, u32[]{:S(2)}) copy-start(bf16[4096,512]{1,0:T(8,128)(2,1)} %table_ref.5) | copy-start | bytes 12582916
  19.1 5.8 %collective-permute-start.2 = (bf16[256,512]{1,0:T(8,128)(2,1)S(1)}, bf16[256,512]{1,0:T(8,128)(2,1)S(1)}, u32[]{:S(2)}, u32[]{:S(2)}) collective-permute-start(bf16[256,512]{1,0:T(8,128)(2,1)S(1)} %copy-done.1), channel_id=1, source_target_pairs={{0,8},{1,9},{2,10},{3,11},{4,12},{5,13},{6,14},{7,15},{8,0},{9,1},... | collective-permute-start | bytes 786440 | tf_op jit(solution)/shard_map/ppermute | solution.py:249
  19.2 8.1 %collective-permute-start.3 = (bf16[256,512]{1,0:T(8,128)(2,1)S(1)}, bf16[256,512]{1,0:T(8,128)(2,1)S(1)}, u32[]{:S(2)}, u32[]{:S(2)}) collective-permute-start(bf16[256,512]{1,0:T(8,128)(2,1)S(1)} %collective-permute-done.1.refs_2_), channel_id=1, source_target_pairs={{0,8},{1,9},{2,10},{3,11},{4,12},{5,13},{6,14},{7,15},{8,0},{9,1},... | collective-permute-start | bytes 786440 | tf_op jit(solution)/shard_map/ppermute | solution.py:249
  19.7 8.7 %collective-permute-start.7 = (bf16[256,512]{1,0:T(8,128)(2,1)S(1)}, bf16[256,512]{1,0:T(8,128)(2,1)S(1)}, u32[]{:S(2)}, u32[]{:S(2)}) collective-permute-start(bf16[256,512]{1,0:T(8,128)(2,1)S(1)} %collective-permute-done.refs_0_), channel_id=1, source_target_pairs={{0,16},{1,17},{2,18},{3,19},{4,20},{5,21},{6,22},{7,23},{8,24},{9,... | collective-permute-start | bytes 786440 | tf_op jit(solution)/shard_map/ppermute | solution.py:249
  21.2 9.0 %copy-start.2 = (bf16[512,512]{1,0:T(8,128)(2,1)S(1)}, bf16[512,512]{1,0:T(8,128)(2,1)}, u32[]{:S(2)}) copy-start(bf16[512,512]{1,0:T(8,128)(2,1)} %weight_ref.3) | copy-start | bytes 1572868
  21.2 7.7 %collective-permute-start.6 = (bf16[128,512]{1,0:T(8,128)(2,1)S(1)}, bf16[128,512]{1,0:T(8,128)(2,1)S(1)}, u32[]{:S(2)}, u32[]{:S(2)}) collective-permute-start(bf16[128,512]{1,0:T(8,128)(2,1)S(1)} %shard_map.69), channel_id=1, source_target_pairs={{0,3},{1,2},{2,1},{3,0},{4,7},{5,6},{6,5},{7,4},{8,11},{9,10},{10,... | collective-permute-start | bytes 393224 | tf_op jit(solution)/shard_map/ppermute | solution.py:249
  23.6 6.6 %collective-permute-start.4 = (bf16[128,512]{1,0:T(8,128)(2,1)S(1)}, bf16[128,512]{1,0:T(8,128)(2,1)S(1)}, u32[]{:S(2)}, u32[]{:S(2)}) collective-permute-start(bf16[128,512]{1,0:T(8,128)(2,1)S(1)} %get-tuple-element.63), channel_id=1, source_target_pairs={{0,1},{1,0},{2,3},{3,2},{4,5},{5,4},{6,7},{7,6},{8,9},{9,8},{10,11... | collective-permute-start | bytes 393224 | tf_op jit(solution)/shard_map/ppermute | solution.py:249
  24.9 5.2 %collective-permute-start.5 = (bf16[128,512]{1,0:T(8,128)(2,1)S(1)}, bf16[128,512]{1,0:T(8,128)(2,1)S(1)}, u32[]{:S(2)}, u32[]{:S(2)}) collective-permute-start(bf16[128,512]{1,0:T(8,128)(2,1)S(1)} %get-tuple-element.64), channel_id=1, source_target_pairs={{0,2},{1,3},{2,0},{3,1},{4,6},{5,7},{6,4},{7,5},{8,10},{9,11},{10,... | collective-permute-start | bytes 393224 | tf_op jit(solution)/shard_map/ppermute | solution.py:249
  28.3 2.3 %collective-permute-start.8 = (bf16[256,512]{1,0:T(8,128)(2,1)S(1)}, bf16[256,512]{1,0:T(8,128)(2,1)S(1)}, u32[]{:S(2)}, u32[]{:S(2)}) collective-permute-start(bf16[256,512]{1,0:T(8,128)(2,1)S(1)} %collective-permute-done.refs_0_), channel_id=1, source_target_pairs={{0,8},{1,9},{2,10},{3,11},{4,12},{5,13},{6,14},{7,15},{8,0},{9,1},... | collective-permute-start | bytes 786440 | tf_op jit(solution)/shard_map/ppermute | solution.py:249
  28.4 2.3 %collective-permute-start.9 = (bf16[256,512]{1,0:T(8,128)(2,1)S(1)}, bf16[256,512]{1,0:T(8,128)(2,1)S(1)}, u32[]{:S(2)}, u32[]{:S(2)}) collective-permute-start(bf16[256,512]{1,0:T(8,128)(2,1)S(1)} %collective-permute-done.7.refs_2_), channel_id=1, source_target_pairs={{0,8},{1,9},{2,10},{3,11},{4,12},{5,13},{6,14},{7,15},{8,0},{9,1},... | collective-permute-start | bytes 786440 | tf_op jit(solution)/shard_map/ppermute | solution.py:249
  33.7 1.6 %collective-permute-start.10 = (bf16[16,16,512]{2,1,0:T(8,128)(2,1)S(1)}, bf16[16,16,512]{2,1,0:T(8,128)(2,1)S(1)}, u32[]{:S(2)}, u32[]{:S(2)}) collective-permute-start(bf16[16,16,512]{2,1,0:T(8,128)(2,1)S(1)} %get-tuple-element.83), channel_id=1, source_target_pairs={{0,8},{1,9},{2,10},{3,11},{4,12},{5,13},{6,14},{7,15},{8,0},{9,1},... | collective-permute-start | bytes 786440 | tf_op jit(solution)/shard_map/ppermute | solution.py:249
  35.4 5.6 %collective-permute-start.11 = (bf16[8,16,512]{2,1,0:T(8,128)(2,1)S(1)}, bf16[8,16,512]{2,1,0:T(8,128)(2,1)S(1)}, u32[]{:S(2)}, u32[]{:S(2)}) collective-permute-start(bf16[8,16,512]{2,1,0:T(8,128)(2,1)S(1)} %get-tuple-element.85), channel_id=1, source_target_pairs={{0,16},{1,17},{2,18},{3,19},{4,20},{5,21},{6,22},{7,23},{8,24},{9,... | collective-permute-start | bytes 393224 | tf_op jit(solution)/shard_map/ppermute | solution.py:249
  36.9 6.1 %collective-permute-start.15 = (bf16[128,512]{1,0:T(8,128)(2,1)S(1)}, bf16[128,512]{1,0:T(8,128)(2,1)S(1)}, u32[]{:S(2)}, u32[]{:S(2)}) collective-permute-start(bf16[128,512]{1,0:T(8,128)(2,1)S(1)} %get-tuple-element.79.refs_5_), channel_id=1, source_target_pairs={{0,1},{1,0},{2,3},{3,2},{4,5},{5,4},{6,7},{7,6},{8,9},{9,8},{10,11... | collective-permute-start | bytes 393224 | tf_op jit(solution)/shard_map/ppermute | solution.py:249
  37.5 7.1 %collective-permute-start.16 = (bf16[128,512]{1,0:T(8,128)(2,1)S(1)}, bf16[128,512]{1,0:T(8,128)(2,1)S(1)}, u32[]{:S(2)}, u32[]{:S(2)}) collective-permute-start(bf16[128,512]{1,0:T(8,128)(2,1)S(1)} %get-tuple-element.80.refs_6_), channel_id=1, source_target_pairs={{0,2},{1,3},{2,0},{3,1},{4,6},{5,7},{6,4},{7,5},{8,10},{9,11},{10,... | collective-permute-start | bytes 393224 | tf_op jit(solution)/shard_map/ppermute | solution.py:249
  38.7 8.2 %collective-permute-start.17 = (bf16[128,512]{1,0:T(8,128)(2,1)S(1)}, bf16[128,512]{1,0:T(8,128)(2,1)S(1)}, u32[]{:S(2)}, u32[]{:S(2)}) collective-permute-start(bf16[128,512]{1,0:T(8,128)(2,1)S(1)} %get-tuple-element.81.refs_7_), channel_id=1, source_target_pairs={{0,3},{1,2},{2,1},{3,0},{4,7},{5,6},{6,5},{7,4},{8,11},{9,10},{10,... | collective-permute-start | bytes 393224 | tf_op jit(solution)/shard_map/ppermute | solution.py:249
  41.0 5.9 %collective-permute-start.12 = (bf16[2,16,512]{2,1,0:T(8,128)(2,1)S(1)}, bf16[2,16,512]{2,1,0:T(8,128)(2,1)S(1)}, u32[]{:S(2)}, u32[]{:S(2)}) collective-permute-start(bf16[2,16,512]{2,1,0:T(8,128)(2,1)S(1)} %get-tuple-element.87), channel_id=1, source_target_pairs={{0,2},{1,3},{2,0},{3,1},{4,6},{5,7},{6,4},{7,5},{8,10},{9,11},{10,... | collective-permute-start | bytes 98312 | tf_op jit(solution)/shard_map/ppermute | solution.py:249
  42.3 4.9 %collective-permute-start.13 = (bf16[2,16,512]{2,1,0:T(8,128)(2,1)S(1)}, bf16[2,16,512]{2,1,0:T(8,128)(2,1)S(1)}, u32[]{:S(2)}, u32[]{:S(2)}) collective-permute-start(bf16[2,16,512]{2,1,0:T(8,128)(2,1)S(1)} %get-tuple-element.88), channel_id=1, source_target_pairs={{0,1},{1,0},{2,3},{3,2},{4,5},{5,4},{6,7},{7,6},{8,9},{9,8},{10,11... | collective-permute-start | bytes 98312 | tf_op jit(solution)/shard_map/ppermute | solution.py:249
  43.0 4.8 %collective-permute-start.14 = (bf16[2,16,512]{2,1,0:T(8,128)(2,1)S(1)}, bf16[2,16,512]{2,1,0:T(8,128)(2,1)S(1)}, u32[]{:S(2)}, u32[]{:S(2)}) collective-permute-start(bf16[2,16,512]{2,1,0:T(8,128)(2,1)S(1)} %get-tuple-element.89), channel_id=1, source_target_pairs={{0,3},{1,2},{2,1},{3,0},{4,7},{5,6},{6,5},{7,4},{8,11},{9,10},{10,... | collective-permute-start | bytes 98312 | tf_op jit(solution)/shard_map/ppermute | solution.py:249
  47.8 6.6 %collective-permute-start.18 = (f32[1,16,512]{2,1,0:T(8,128)S(1)}, f32[1,16,512]{2,1,0:T(8,128)S(1)}, u32[]{:S(2)}, u32[]{:S(2)}) collective-permute-start(f32[1,16,512]{2,1,0:T(8,128)S(1)} %get-tuple-element.98), channel_id=1, source_target_pairs={{0,4},{1,5},{2,6},{3,7},{4,0},{5,1},{6,2},{7,3},{8,12},{9,13},{10,... | collective-permute-start | bytes 98312 | tf_op jit(solution)/shard_map/ppermute | solution.py:249

commit v16 on v15

--- a/solution.py
+++ b/solution.py
@@ -261,10 +261,8 @@
     width = dhidden[0].shape[1]
     n_item, devices = lax.axis_size("item"), lax.axis_size("batch") * lax.axis_size("item")
     part = width // devices
-    close = log2(len(dhidden))
-    batch_bits, item_bits = bits_of("batch"), bits_of("item")
-    stages = [batch_bits[:1], batch_bits[1:], item_bits[:close], item_bits[close:]]
-    bits = sum(stages, [])
+    bits = bits_of("batch") + bits_of("item")
+    stages = [[bit] for bit in bits]
     order = []
     for spot in range(devices):
         at = {"batch": 0, "item": 0}
@@ -277,7 +275,7 @@
         masks = [
             mask_of([bit for j, bit in enumerate(reversed(stage)) if step >> j & 1]) for step in range(1, 1 << len(stage))
         ]
-        sent = f32 if k == len(stages) - 1 else bf16
+        sent = bf16 if left > 2 else f32
         count = len(values)
         kernel = functools.partial(stage_kernel, stage, count) if k else functools.partial(share_kernel, order, stage, count)
         kept, *sends = call(
@@ -384,7 +382,7 @@
         flops=1 << 31,
         mib=40,
     )
-    incoming = [swap(dhidden[part], part) for part in range(1, near)]
+    incoming = [swap(dhidden[part], part) for part in reversed(range(1, near))][::-1]
     terms, incoming = reduce_scatter(fetched, dhidden, incoming)
     table_grad = pl.pallas_call(
         table_kernel,

time: 55.2 us -> 58.9 us (1.067)
  waiting for transfers between devices: 6.57 us -> 11.4 us
  starting transfers between devices: 22.6 us -> 21.4 us
    ppermute x19 -> x18, waiting for transfers between devices: 6.57 us -> 11.4 us  [swap(): lax.ppermute(value, ('batch', 'item'), [(k, k ^ mask) for k in range(devi...]
    ppermute x19 -> x18, starting transfers between devices: 22.6 us -> 21.4 us  [swap(): lax.ppermute(value, ('batch', 'item'), [(k, k ^ mask) for k in range(devi...]
    pallas_call x13 -> x14, Pallas kernels: 9.08 us -> 9.1 us  [call(): pl.pallas_call(kernel, out_shape=[jax.ShapeDtypeStruct(shape, dtype) for...]
  transfers between devices with their start and end apart: 19 -> 18, of which waited for: 6 -> 8; matrix products, arithmetic and copies ran while one was open for 1% -> 1% of each run, Pallas kernels for 16% -> 15%
where the time goes in v16:
time: 58.9 us; the launch traced here: 58.7 us
  starting transfers between devices  21.4 us (36%)
  Pallas kernels  12.7 us (22%)
  blocking collectives  11.7 us (20%)
  waiting for transfers between devices  11.4 us (19%)
  between operations  0.8 us (1%)
  other arithmetic  0.7 us (1%)
    ppermute x18, starting transfers between devices, swap(): lax.ppermute(value, ('batch', 'item'), [(k, k ^ mask) for k in range(devi...  21.4 us
    all_to_all x1, blocking collectives, local(): lax.all_to_all(request, ('batch', 'item'), split_axis=0, concat_axis=0, t...  11.7 us
    ppermute x18, waiting for transfers between devices, swap(): lax.ppermute(value, ('batch', 'item'), [(k, k ^ mask) for k in range(devi...  11.4 us
    pallas_call x14, Pallas kernels, call(): pl.pallas_call(kernel, out_shape=[jax.ShapeDtypeStruct(shape, dtype) for...  9.1 us
    pallas_call x1, Pallas kernels, local(): pl.pallas_call(table_kernel, out_specs=pl.BlockSpec(memory_space=pl.ANY),...  3.59 us
  transfers between devices with their start and end apart: 18, of which 8 were waited for; matrix products, arithmetic and copies ran while one was open for 1% of the time, Pallas kernels for 15%

profile of v16, /device:TPU:0, one launch (start us, length us, event | category | flops | bytes accessed | tf_op | source)
XLA Modules:
  0.0 58.7 jit_solution(6995655602537676433)
XLA Ops:
  0.6 4.1 %collective-permute-start = (bf16[256,512]{1,0:T(8,128)(2,1)}, bf16[256,512]{1,0:T(8,128)(2,1)S(1)}, u32[]{:S(2)}, u32[]{:S(2)}) collective-permute-start(bf16[256,512]{1,0:T(8,128)(2,1)} %refs_0_), channel_id=1, source_target_pairs={{0,4},{1,5},{2,6},{3,7},{4,0},{5,1},{6,2},{7,3},{8,12},{9,13},{10,... | collective-permute-start | bytes 786440 | tf_op jit(solution)/shard_map/ppermute | solution.py:249
  4.7 1.5 %collective-permute-start.1 = (bf16[256,512]{1,0:T(8,128)(2,1)}, bf16[256,512]{1,0:T(8,128)(2,1)S(1)}, u32[]{:S(2)}, u32[]{:S(2)}) collective-permute-start(bf16[256,512]{1,0:T(8,128)(2,1)} %refs_0_), channel_id=1, source_target_pairs={{0,16},{1,17},{2,18},{3,19},{4,20},{5,21},{6,22},{7,23},{8,24},{9,... | collective-permute-start | bytes 786440 | tf_op jit(solution)/shard_map/ppermute | solution.py:249
  6.2 0.7 %pad_add_fusion.named_ref = s32[2,256]{1,0:T(2,128)S(1)} fusion(s32[1,256]{1,0:T(1,128)} %bitcast.11, s32[1,256]{1,0:T(1,128)} %bitcast.12), kind=kLoop, calls=%fused_computation | loop fusion | flops 512 | bytes 4096 | tf_op jit(solution)/shard_map/stack | solution.py:314
  7.4 11.7 %all_to_all.12 = s32[32,1,80]{2,1,0:T(1,128)S(1)} all-to-all(s32[32,1,80]{2,1,0:T(1,128)S(1)} %bitcast.10), channel_id=1, replica_groups=mesh['batch'=4,'item'=8] {'batch','item'}, dimensions={0} | all-to-all | bytes 20480 | tf_op jit(solution)/shard_map/all_to_all | solution.py:317
  19.7 0.6 collective-permute-start.7
  20.3 0.9 %shard_map.69 = bf16[128,512]{1,0:T(8,128)(2,1)S(1)} custom-call(s32[32,80]{1,0:T(8,128)S(1)} %bitcast.6, bf16[4096,512]{1,0:T(8,128)(2,1)S(1)} %copy-done), custom_call_target="tpu_custom_call" | custom-call | flops 536870912 | bytes 1048576 | tf_op jit(solution)/shard_map/pallas_call | solution.py:238
  21.2 0.8 %collective-permute-start.6 = (bf16[128,512]{1,0:T(8,128)(2,1)S(1)}, bf16[128,512]{1,0:T(8,128)(2,1)S(1)}, u32[]{:S(2)}, u32[]{:S(2)}) collective-permute-start(bf16[128,512]{1,0:T(8,128)(2,1)S(1)} %shard_map.69), channel_id=1, source_target_pairs={{0,3},{1,2},{2,1},{3,0},{4,7},{5,6},{6,5},{7,4},{8,11},{9,10},{10,... | collective-permute-start | bytes 393224 | tf_op jit(solution)/shard_map/ppermute | solution.py:249
  22.0 1.6 %shard_map.70 = (bf16[128,512]{1,0:T(8,128)(2,1)S(1)}, bf16[128,512]{1,0:T(8,128)(2,1)S(1)}) custom-call(s32[32,80]{1,0:T(8,128)S(1)} %bitcast.7, bf16[4096,512]{1,0:T(8,128)(2,1)S(1)} %copy-done), custom_call_target="tpu_custom_call" | custom-call | flops 1073741824 | bytes 1048576 | tf_op jit(solution)/shard_map/pallas_call | solution.py:238
  23.6 1.3 %collective-permute-start.4 = (bf16[128,512]{1,0:T(8,128)(2,1)S(1)}, bf16[128,512]{1,0:T(8,128)(2,1)S(1)}, u32[]{:S(2)}, u32[]{:S(2)}) collective-permute-start(bf16[128,512]{1,0:T(8,128)(2,1)S(1)} %get-tuple-element.61), channel_id=1, source_target_pairs={{0,1},{1,0},{2,3},{3,2},{4,5},{5,4},{6,7},{7,6},{8,9},{9,8},{10,11... | collective-permute-start | bytes 393224 | tf_op jit(solution)/shard_map/ppermute | solution.py:249
  24.9 1.5 %collective-permute-start.5 = (bf16[128,512]{1,0:T(8,128)(2,1)S(1)}, bf16[128,512]{1,0:T(8,128)(2,1)S(1)}, u32[]{:S(2)}, u32[]{:S(2)}) collective-permute-start(bf16[128,512]{1,0:T(8,128)(2,1)S(1)} %get-tuple-element.62), channel_id=1, source_target_pairs={{0,2},{1,3},{2,0},{3,1},{4,6},{5,7},{6,4},{7,5},{8,10},{9,11},{10,... | collective-permute-start | bytes 393224 | tf_op jit(solution)/shard_map/ppermute | solution.py:249
  26.4 0.9 %shard_map.71.refs_0_ = bf16[128,512]{1,0:T(8,128)(2,1)S(1)} custom-call(s32[32,80]{1,0:T(8,128)S(1)} %bitcast.8, bf16[4096,512]{1,0:T(8,128)(2,1)S(1)} %copy-done), custom_call_target="tpu_custom_call" | custom-call | flops 536870912 | bytes 1048576 | tf_op jit(solution)/shard_map/pallas_call | solution.py:238
  27.3 1.0 %shard_map.72 = (s32[512,1]{1,0:T(8,128)S(1)}, bf16[256,512]{1,0:T(8,128)(2,1)S(1)}, bf16[256,512]{1,0:T(8,128)(2,1)S(1)}, bf16[1024,512]{1,0:T(8,128)(2,1)S(1)}, bf16[256,512]{1,0:T(8,128)(2,1)S(1)}) custom-call(s32[32,80]{1,0:T(8,128)S(1)} %bitcast.9, bf16[256,512]{1,0:T(8,128)(2,1)S(1)} %copy-done.1, bf16[256,512]{1,0:T(8,128)(2,1)S(1)} %collective-permute-done.2.refs_1_, ...), custom_call_target="tpu_custom_call" | custom-call | tf_op jit(solution)/shard_map/pallas_call | solution.py:238
  28.9 1.2 %collective-permute-done.4.refs_1_ = bf16[128,512]{1,0:T(8,128)(2,1)S(1)} collective-permute-done((bf16[128,512]{1,0:T(8,128)(2,1)S(1)}, bf16[128,512]{1,0:T(8,128)(2,1)S(1)}, u32[]{:S(2)}, u32[]{:S(2)}) %collective-permute-start.4) | collective-permute-done | bytes 131104 | tf_op jit(solution)/shard_map/ppermute | solution.py:249
  30.2 0.5 shard_map.73
  30.7 0.7 %shard_map.74 = (bf16[1024,512]{1,0:T(8,128)(2,1)S(1)}, bf16[256,512]{1,0:T(8,128)(2,1)S(1)}) custom-call(s32[512,1]{1,0:T(8,128)S(1)} %get-tuple-element.70.place_ref, bf16[256,512]{1,0:T(8,128)(2,1)S(1)} %collective-permute-done.refs_0_, bf16[256,512]{1,0:T(8,128)(2,1)S(1)} %collective-permute-done.8.refs_1_, ...), custom_call_target="tpu_custom_call" | custom-call | tf_op jit(solution)/shard_map/pallas_call | solution.py:238
  31.4 1.7 %shard_map.75 = (bf16[128,512]{1,0:T(8,128)(2,1)S(1)}, bf16[128,512]{1,0:T(8,128)(2,1)S(1)}, bf16[128,512]{1,0:T(8,128)(2,1)S(1)}, bf16[128,512]{1,0:T(8,128)(2,1)S(1)}) custom-call(f32[512,512]{1,0:T(8,128)S(1)} %get-tuple-element.64.hidden_ref, f32[512,1]{1,0:T(8,128)S(1)} %get-tuple-element.65.rscale_ref, ...), custom_call_target="tpu_custom_call" | custom-call | flops 2147483648 | bytes 1048576 | tf_op jit(solution)/shard_map/pallas_call | solution.py:238
  33.8 1.5 %collective-permute-done.10.refs_1_ = bf16[16,16,512]{2,1,0:T(8,128)(2,1)S(1)} collective-permute-done((bf16[16,16,512]{2,1,0:T(8,128)(2,1)S(1)}, bf16[16,16,512]{2,1,0:T(8,128)(2,1)S(1)}, u32[]{:S(2)}, u32[]{:S(2)}) %collective-permute-start.10) | collective-permute-done | bytes 262176 | tf_op jit(solution)/shard_map/ppermute | solution.py:249
  35.4 1.5 %collective-permute-start.11 = (bf16[8,16,512]{2,1,0:T(8,128)(2,1)S(1)}, bf16[8,16,512]{2,1,0:T(8,128)(2,1)S(1)}, u32[]{:S(2)}, u32[]{:S(2)}) collective-permute-start(bf16[8,16,512]{2,1,0:T(8,128)(2,1)S(1)} %get-tuple-element.83), channel_id=1, source_target_pairs={{0,16},{1,17},{2,18},{3,19},{4,20},{5,21},{6,22},{7,23},{8,24},{9,... | collective-permute-start | bytes 393224 | tf_op jit(solution)/shard_map/ppermute | solution.py:249
  36.9 0.6 %collective-permute-start.13 = (bf16[128,512]{1,0:T(8,128)(2,1)S(1)}, bf16[128,512]{1,0:T(8,128)(2,1)S(1)}, u32[]{:S(2)}, u32[]{:S(2)}) collective-permute-start(bf16[128,512]{1,0:T(8,128)(2,1)S(1)} %get-tuple-element.77.refs_5_), channel_id=1, source_target_pairs={{0,1},{1,0},{2,3},{3,2},{4,5},{5,4},{6,7},{7,6},{8,9},{9,8},{10,11... | collective-permute-start | bytes 393224 | tf_op jit(solution)/shard_map/ppermute | solution.py:249
  37.5 1.2 %collective-permute-start.14 = (bf16[128,512]{1,0:T(8,128)(2,1)S(1)}, bf16[128,512]{1,0:T(8,128)(2,1)S(1)}, u32[]{:S(2)}, u32[]{:S(2)}) collective-permute-start(bf16[128,512]{1,0:T(8,128)(2,1)S(1)} %get-tuple-element.78.refs_6_), channel_id=1, source_target_pairs={{0,2},{1,3},{2,0},{3,1},{4,6},{5,7},{6,4},{7,5},{8,10},{9,11},{10,... | collective-permute-start | bytes 393224 | tf_op jit(solution)/shard_map/ppermute | solution.py:249
  38.7 1.7 %collective-permute-start.15 = (bf16[128,512]{1,0:T(8,128)(2,1)S(1)}, bf16[128,512]{1,0:T(8,128)(2,1)S(1)}, u32[]{:S(2)}, u32[]{:S(2)}) collective-permute-start(bf16[128,512]{1,0:T(8,128)(2,1)S(1)} %get-tuple-element.79.refs_7_), channel_id=1, source_target_pairs={{0,3},{1,2},{2,1},{3,0},{4,7},{5,6},{6,5},{7,4},{8,11},{9,10},{10,... | collective-permute-start | bytes 393224 | tf_op jit(solution)/shard_map/ppermute | solution.py:249
  40.4 0.6 %collective-permute-done.11.refs_1_ = bf16[8,16,512]{2,1,0:T(8,128)(2,1)S(1)} collective-permute-done((bf16[8,16,512]{2,1,0:T(8,128)(2,1)S(1)}, bf16[8,16,512]{2,1,0:T(8,128)(2,1)S(1)}, u32[]{:S(2)}, u32[]{:S(2)}) %collective-permute-start.11) | collective-permute-done | bytes 131104 | tf_op jit(solution)/shard_map/ppermute | solution.py:249
  41.0 0.8 %collective-permute-start.12 = (bf16[4,16,512]{2,1,0:T(8,128)(2,1)S(1)}, bf16[4,16,512]{2,1,0:T(8,128)(2,1)S(1)}, u32[]{:S(2)}, u32[]{:S(2)}) collective-permute-start(bf16[4,16,512]{2,1,0:T(8,128)(2,1)S(1)} %get-tuple-element.85), channel_id=1, source_target_pairs={{0,1},{1,0},{2,3},{3,2},{4,5},{5,4},{6,7},{7,6},{8,9},{9,8},{10,11... | collective-permute-start | bytes 196616 | tf_op jit(solution)/shard_map/ppermute | solution.py:249
  41.8 0.6 %collective-permute-done.13.refs_1_ = bf16[128,512]{1,0:T(8,128)(2,1)S(1)} collective-permute-done((bf16[128,512]{1,0:T(8,128)(2,1)S(1)}, bf16[128,512]{1,0:T(8,128)(2,1)S(1)}, u32[]{:S(2)}, u32[]{:S(2)}) %collective-permute-start.13) | collective-permute-done | bytes 131104 | tf_op jit(solution)/shard_map/ppermute | solution.py:249
  42.4 1.2 %collective-permute-done.14.refs_2_ = bf16[128,512]{1,0:T(8,128)(2,1)S(1)} collective-permute-done((bf16[128,512]{1,0:T(8,128)(2,1)S(1)}, bf16[128,512]{1,0:T(8,128)(2,1)S(1)}, u32[]{:S(2)}, u32[]{:S(2)}) %collective-permute-start.14) | collective-permute-done | bytes 131104 | tf_op jit(solution)/shard_map/ppermute | solution.py:249
  43.6 2.6 %collective-permute-done.15.refs_3_ = bf16[128,512]{1,0:T(8,128)(2,1)S(1)} collective-permute-done((bf16[128,512]{1,0:T(8,128)(2,1)S(1)}, bf16[128,512]{1,0:T(8,128)(2,1)S(1)}, u32[]{:S(2)}, u32[]{:S(2)}) %collective-permute-start.15) | collective-permute-done | bytes 131104 | tf_op jit(solution)/shard_map/ppermute | solution.py:249
  46.2 0.6 collective-permute-done.12.refs_1_
  46.8 1.3 %collective-permute-start.16 = (f32[2,16,512]{2,1,0:T(8,128)S(1)}, f32[2,16,512]{2,1,0:T(8,128)S(1)}, u32[]{:S(2)}, u32[]{:S(2)}) collective-permute-start(f32[2,16,512]{2,1,0:T(8,128)S(1)} %get-tuple-element.92), channel_id=1, source_target_pairs={{0,2},{1,3},{2,0},{3,1},{4,6},{5,7},{6,4},{7,5},{8,10},{9,11},{10,... | collective-permute-start | bytes 196616 | tf_op jit(solution)/shard_map/ppermute | solution.py:249
  48.1 3.1 %collective-permute-done.16.refs_1_ = f32[2,16,512]{2,1,0:T(8,128)S(1)} collective-permute-done((f32[2,16,512]{2,1,0:T(8,128)S(1)}, f32[2,16,512]{2,1,0:T(8,128)S(1)}, u32[]{:S(2)}, u32[]{:S(2)}) %collective-permute-start.16) | collective-permute-done | bytes 65568 | tf_op jit(solution)/shard_map/ppermute | solution.py:249
  51.2 3.3 %collective-permute-start.17 = (f32[1,16,512]{2,1,0:T(8,128)S(1)}, f32[1,16,512]{2,1,0:T(8,128)S(1)}, u32[]{:S(2)}, u32[]{:S(2)}) collective-permute-start(f32[1,16,512]{2,1,0:T(8,128)S(1)} %get-tuple-element.94), channel_id=1, source_target_pairs={{0,4},{1,5},{2,6},{3,7},{4,0},{5,1},{6,2},{7,3},{8,12},{9,13},{10,... | collective-permute-start | bytes 98312 | tf_op jit(solution)/shard_map/ppermute | solution.py:249
  54.5 3.6 %shard_map.79 = bf16[4096,512]{1,0:T(8,128)(2,1)} custom-call(bf16[256,512]{1,0:T(8,128)(2,1)S(1)} %get-tuple-element.58.low_hot_ref, bf16[256,512]{1,0:T(8,128)(2,1)S(1)} %get-tuple-element.59.block_ref, bf16[512,512]{1,0:T(8,128)(2,1)S(1)} %copy-done.2, bf16[128,512]{1,0:T(8,128)(2,1)S(1)} %get-tuple-element.76.refs_4_.refs_0_, ...), custom_call_target="tpu_custom_call" | custom-call | flops 2147483648 | bytes 4194304 | tf_op jit(solution)/shard_map/pallas_call | solution.py:387
  58.1 0.6 %shard_map.82 = f32[16,512]{1,0:T(8,128)} custom-call(f32[1,16,512]{2,1,0:T(8,128)S(1)} %get-tuple-element.96.refs_0_, f32[1,16,512]{2,1,0:T(8,128)S(1)} %collective-permute-done.17.refs_1_), custom_call_target="tpu_custom_call" | custom-call | bytes 1048576 | tf_op jit(solution)/shard_map/pallas_call | solution.py:238
  (27 shorter events, 2.4 us)
Async XLA Ops:
  0.6 18.4 %collective-permute-start = (bf16[256,512]{1,0:T(8,128)(2,1)}, bf16[256,512]{1,0:T(8,128)(2,1)S(1)}, u32[]{:S(2)}, u32[]{:S(2)}) collective-permute-start(bf16[256,512]{1,0:T(8,128)(2,1)} %refs_0_), channel_id=1, source_target_pairs={{0,4},{1,5},{2,6},{3,7},{4,0},{5,1},{6,2},{7,3},{8,12},{9,13},{10,... | collective-permute-start | bytes 786440 | tf_op jit(solution)/shard_map/ppermute | solution.py:249
  4.7 14.4 %collective-permute-start.1 = (bf16[256,512]{1,0:T(8,128)(2,1)}, bf16[256,512]{1,0:T(8,128)(2,1)S(1)}, u32[]{:S(2)}, u32[]{:S(2)}) collective-permute-start(bf16[256,512]{1,0:T(8,128)(2,1)} %refs_0_), channel_id=1, source_target_pairs={{0,16},{1,17},{2,18},{3,19},{4,20},{5,21},{6,22},{7,23},{8,24},{9,... | collective-permute-start | bytes 786440 | tf_op jit(solution)/shard_map/ppermute | solution.py:249
  6.9 12.2 %copy-start.1 = (bf16[256,512]{1,0:T(8,128)(2,1)S(1)}, bf16[256,512]{1,0:T(8,128)(2,1)}, u32[]{:S(2)}) copy-start(bf16[256,512]{1,0:T(8,128)(2,1)} %refs_0_) | copy-start | bytes 786436
  6.9 13.3 %copy-start = (bf16[4096,512]{1,0:T(8,128)(2,1)S(1)}, bf16[4096,512]{1,0:T(8,128)(2,1)}, u32[]{:S(2)}) copy-start(bf16[4096,512]{1,0:T(8,128)(2,1)} %table_ref.5) | copy-start | bytes 12582916
  19.1 5.8 %collective-permute-start.2 = (bf16[256,512]{1,0:T(8,128)(2,1)S(1)}, bf16[256,512]{1,0:T(8,128)(2,1)S(1)}, u32[]{:S(2)}, u32[]{:S(2)}) collective-permute-start(bf16[256,512]{1,0:T(8,128)(2,1)S(1)} %copy-done.1), channel_id=1, source_target_pairs={{0,8},{1,9},{2,10},{3,11},{4,12},{5,13},{6,14},{7,15},{8,0},{9,1},... | collective-permute-start | bytes 786440 | tf_op jit(solution)/shard_map/ppermute | solution.py:249
  19.2 8.1 %collective-permute-start.3 = (bf16[256,512]{1,0:T(8,128)(2,1)S(1)}, bf16[256,512]{1,0:T(8,128)(2,1)S(1)}, u32[]{:S(2)}, u32[]{:S(2)}) collective-permute-start(bf16[256,512]{1,0:T(8,128)(2,1)S(1)} %collective-permute-done.1.refs_2_), channel_id=1, source_target_pairs={{0,8},{1,9},{2,10},{3,11},{4,12},{5,13},{6,14},{7,15},{8,0},{9,1},... | collective-permute-start | bytes 786440 | tf_op jit(solution)/shard_map/ppermute | solution.py:249
  19.7 8.7 %collective-permute-start.7 = (bf16[256,512]{1,0:T(8,128)(2,1)S(1)}, bf16[256,512]{1,0:T(8,128)(2,1)S(1)}, u32[]{:S(2)}, u32[]{:S(2)}) collective-permute-start(bf16[256,512]{1,0:T(8,128)(2,1)S(1)} %collective-permute-done.refs_0_), channel_id=1, source_target_pairs={{0,16},{1,17},{2,18},{3,19},{4,20},{5,21},{6,22},{7,23},{8,24},{9,... | collective-permute-start | bytes 786440 | tf_op jit(solution)/shard_map/ppermute | solution.py:249
  21.2 9.0 %copy-start.2 = (bf16[512,512]{1,0:T(8,128)(2,1)S(1)}, bf16[512,512]{1,0:T(8,128)(2,1)}, u32[]{:S(2)}) copy-start(bf16[512,512]{1,0:T(8,128)(2,1)} %weight_ref.3) | copy-start | bytes 1572868
  21.2 7.7 %collective-permute-start.6 = (bf16[128,512]{1,0:T(8,128)(2,1)S(1)}, bf16[128,512]{1,0:T(8,128)(2,1)S(1)}, u32[]{:S(2)}, u32[]{:S(2)}) collective-permute-start(bf16[128,512]{1,0:T(8,128)(2,1)S(1)} %shard_map.69), channel_id=1, source_target_pairs={{0,3},{1,2},{2,1},{3,0},{4,7},{5,6},{6,5},{7,4},{8,11},{9,10},{10,... | collective-permute-start | bytes 393224 | tf_op jit(solution)/shard_map/ppermute | solution.py:249
  23.6 6.6 %collective-permute-start.4 = (bf16[128,512]{1,0:T(8,128)(2,1)S(1)}, bf16[128,512]{1,0:T(8,128)(2,1)S(1)}, u32[]{:S(2)}, u32[]{:S(2)}) collective-permute-start(bf16[128,512]{1,0:T(8,128)(2,1)S(1)} %get-tuple-element.61), channel_id=1, source_target_pairs={{0,1},{1,0},{2,3},{3,2},{4,5},{5,4},{6,7},{7,6},{8,9},{9,8},{10,11... | collective-permute-start | bytes 393224 | tf_op jit(solution)/shard_map/ppermute | solution.py:249
  24.9 5.2 %collective-permute-start.5 = (bf16[128,512]{1,0:T(8,128)(2,1)S(1)}, bf16[128,512]{1,0:T(8,128)(2,1)S(1)}, u32[]{:S(2)}, u32[]{:S(2)}) collective-permute-start(bf16[128,512]{1,0:T(8,128)(2,1)S(1)} %get-tuple-element.62), channel_id=1, source_target_pairs={{0,2},{1,3},{2,0},{3,1},{4,6},{5,7},{6,4},{7,5},{8,10},{9,11},{10,... | collective-permute-start | bytes 393224 | tf_op jit(solution)/shard_map/ppermute | solution.py:249
  28.3 2.3 %collective-permute-start.8 = (bf16[256,512]{1,0:T(8,128)(2,1)S(1)}, bf16[256,512]{1,0:T(8,128)(2,1)S(1)}, u32[]{:S(2)}, u32[]{:S(2)}) collective-permute-start(bf16[256,512]{1,0:T(8,128)(2,1)S(1)} %collective-permute-done.refs_0_), channel_id=1, source_target_pairs={{0,8},{1,9},{2,10},{3,11},{4,12},{5,13},{6,14},{7,15},{8,0},{9,1},... | collective-permute-start | bytes 786440 | tf_op jit(solution)/shard_map/ppermute | solution.py:249
  28.4 2.3 %collective-permute-start.9 = (bf16[256,512]{1,0:T(8,128)(2,1)S(1)}, bf16[256,512]{1,0:T(8,128)(2,1)S(1)}, u32[]{:S(2)}, u32[]{:S(2)}) collective-permute-start(bf16[256,512]{1,0:T(8,128)(2,1)S(1)} %collective-permute-done.7.refs_2_), channel_id=1, source_target_pairs={{0,8},{1,9},{2,10},{3,11},{4,12},{5,13},{6,14},{7,15},{8,0},{9,1},... | collective-permute-start | bytes 786440 | tf_op jit(solution)/shard_map/ppermute | solution.py:249
  33.7 1.6 %collective-permute-start.10 = (bf16[16,16,512]{2,1,0:T(8,128)(2,1)S(1)}, bf16[16,16,512]{2,1,0:T(8,128)(2,1)S(1)}, u32[]{:S(2)}, u32[]{:S(2)}) collective-permute-start(bf16[16,16,512]{2,1,0:T(8,128)(2,1)S(1)} %get-tuple-element.81), channel_id=1, source_target_pairs={{0,8},{1,9},{2,10},{3,11},{4,12},{5,13},{6,14},{7,15},{8,0},{9,1},... | collective-permute-start | bytes 786440 | tf_op jit(solution)/shard_map/ppermute | solution.py:249
  35.4 5.6 %collective-permute-start.11 = (bf16[8,16,512]{2,1,0:T(8,128)(2,1)S(1)}, bf16[8,16,512]{2,1,0:T(8,128)(2,1)S(1)}, u32[]{:S(2)}, u32[]{:S(2)}) collective-permute-start(bf16[8,16,512]{2,1,0:T(8,128)(2,1)S(1)} %get-tuple-element.83), channel_id=1, source_target_pairs={{0,16},{1,17},{2,18},{3,19},{4,20},{5,21},{6,22},{7,23},{8,24},{9,... | collective-permute-start | bytes 393224 | tf_op jit(solution)/shard_map/ppermute | solution.py:249
  36.9 5.5 %collective-permute-start.13 = (bf16[128,512]{1,0:T(8,128)(2,1)S(1)}, bf16[128,512]{1,0:T(8,128)(2,1)S(1)}, u32[]{:S(2)}, u32[]{:S(2)}) collective-permute-start(bf16[128,512]{1,0:T(8,128)(2,1)S(1)} %get-tuple-element.77.refs_5_), channel_id=1, source_target_pairs={{0,1},{1,0},{2,3},{3,2},{4,5},{5,4},{6,7},{7,6},{8,9},{9,8},{10,11... | collective-permute-start | bytes 393224 | tf_op jit(solution)/shard_map/ppermute | solution.py:249
  37.5 6.1 %collective-permute-start.14 = (bf16[128,512]{1,0:T(8,128)(2,1)S(1)}, bf16[128,512]{1,0:T(8,128)(2,1)S(1)}, u32[]{:S(2)}, u32[]{:S(2)}) collective-permute-start(bf16[128,512]{1,0:T(8,128)(2,1)S(1)} %get-tuple-element.78.refs_6_), channel_id=1, source_target_pairs={{0,2},{1,3},{2,0},{3,1},{4,6},{5,7},{6,4},{7,5},{8,10},{9,11},{10,... | collective-permute-start | bytes 393224 | tf_op jit(solution)/shard_map/ppermute | solution.py:249
  38.7 7.5 %collective-permute-start.15 = (bf16[128,512]{1,0:T(8,128)(2,1)S(1)}, bf16[128,512]{1,0:T(8,128)(2,1)S(1)}, u32[]{:S(2)}, u32[]{:S(2)}) collective-permute-start(bf16[128,512]{1,0:T(8,128)(2,1)S(1)} %get-tuple-element.79.refs_7_), channel_id=1, source_target_pairs={{0,3},{1,2},{2,1},{3,0},{4,7},{5,6},{6,5},{7,4},{8,11},{9,10},{10,... | collective-permute-start | bytes 393224 | tf_op jit(solution)/shard_map/ppermute | solution.py:249
  41.0 5.7 %collective-permute-start.12 = (bf16[4,16,512]{2,1,0:T(8,128)(2,1)S(1)}, bf16[4,16,512]{2,1,0:T(8,128)(2,1)S(1)}, u32[]{:S(2)}, u32[]{:S(2)}) collective-permute-start(bf16[4,16,512]{2,1,0:T(8,128)(2,1)S(1)} %get-tuple-element.85), channel_id=1, source_target_pairs={{0,1},{1,0},{2,3},{3,2},{4,5},{5,4},{6,7},{7,6},{8,9},{9,8},{10,11... | collective-permute-start | bytes 196616 | tf_op jit(solution)/shard_map/ppermute | solution.py:249
  46.8 4.3 %collective-permute-start.16 = (f32[2,16,512]{2,1,0:T(8,128)S(1)}, f32[2,16,512]{2,1,0:T(8,128)S(1)}, u32[]{:S(2)}, u32[]{:S(2)}) collective-permute-start(f32[2,16,512]{2,1,0:T(8,128)S(1)} %get-tuple-element.92), channel_id=1, source_target_pairs={{0,2},{1,3},{2,0},{3,1},{4,6},{5,7},{6,4},{7,5},{8,10},{9,11},{10,... | collective-permute-start | bytes 196616 | tf_op jit(solution)/shard_map/ppermute | solution.py:249
  51.2 6.9 %collective-permute-start.17 = (f32[1,16,512]{2,1,0:T(8,128)S(1)}, f32[1,16,512]{2,1,0:T(8,128)S(1)}, u32[]{:S(2)}, u32[]{:S(2)}) collective-permute-start(f32[1,16,512]{2,1,0:T(8,128)S(1)} %get-tuple-element.94), channel_id=1, source_target_pairs={{0,4},{1,5},{2,6},{3,7},{4,0},{5,1},{6,2},{7,3},{8,12},{9,13},{10,... | collective-permute-start | bytes 98312 | tf_op jit(solution)/shard_map/ppermute | solution.py:249

commit v17 on v15

--- a/solution.py
+++ b/solution.py
@@ -257,13 +257,13 @@
     return sum((lax.axis_size("item") if axis == "batch" else 1) << level for axis, level in bits)
 
 
-def reduce_scatter(fetched, dhidden, incoming):
+def reduce_scatter(fetched, dhidden):
     width = dhidden[0].shape[1]
     n_item, devices = lax.axis_size("item"), lax.axis_size("batch") * lax.axis_size("item")
     part = width // devices
     close = log2(len(dhidden))
     batch_bits, item_bits = bits_of("batch"), bits_of("item")
-    stages = [batch_bits[:1], batch_bits[1:], item_bits[:close], item_bits[close:]]
+    stages = [batch_bits[:1], batch_bits[1:], item_bits[close:], item_bits[:close]]
     bits = sum(stages, [])
     order = []
     for spot in range(devices):
@@ -288,9 +288,7 @@
             free=True,
         )
         values = [kept] + [swap(value, mask) for mask, value in zip(masks, sends)]
-        if k == 2:
-            values, incoming = lax.optimization_barrier((values, incoming))
-    return values, incoming
+    return values
 
 
 def local(user_vectors, item_table, tower_weight, item_owner, item_row):
@@ -385,7 +383,7 @@
         mib=40,
     )
     incoming = [swap(dhidden[part], part) for part in range(1, near)]
-    terms, incoming = reduce_scatter(fetched, dhidden, incoming)
+    terms = reduce_scatter(fetched, dhidden)
     table_grad = pl.pallas_call(
         table_kernel,
         out_specs=pl.BlockSpec(memory_space=pl.ANY),

time: 55.2 us -> 57 us (1.033)
  starting transfers between devices: 22.6 us -> 24.1 us
    ppermute x19, starting transfers between devices: 22.6 us -> 24.1 us  [swap(): lax.ppermute(value, ('batch', 'item'), [(k, k ^ mask) for k in range(devi...]
  transfers between devices with their start and end apart: 19 -> 19, of which waited for: 6 -> 5; matrix products, arithmetic and copies ran while one was open for 1% -> 1% of each run, Pallas kernels for 16% -> 16%
where the time goes in v17:
time: 57 us; the launch traced here: 56.8 us
  starting transfers between devices  24.1 us (42%)
  Pallas kernels  12.7 us (22%)
  blocking collectives  11.7 us (21%)
  waiting for transfers between devices  6.78 us (12%)
  between operations  0.81 us (1%)
  other arithmetic  0.7 us (1%)
    ppermute x19, starting transfers between devices, swap(): lax.ppermute(value, ('batch', 'item'), [(k, k ^ mask) for k in range(devi...  24.1 us
    all_to_all x1, blocking collectives, local(): lax.all_to_all(request, ('batch', 'item'), split_axis=0, concat_axis=0, t...  11.7 us
    pallas_call x13, Pallas kernels, call(): pl.pallas_call(kernel, out_shape=[jax.ShapeDtypeStruct(shape, dtype) for...  9.09 us
    ppermute x19, waiting for transfers between devices, swap(): lax.ppermute(value, ('batch', 'item'), [(k, k ^ mask) for k in range(devi...  6.78 us
    pallas_call x1, Pallas kernels, local(): pl.pallas_call(table_kernel, out_specs=pl.BlockSpec(memory_space=pl.ANY),...  3.59 us
  transfers between devices with their start and end apart: 19, of which 5 were waited for; matrix products, arithmetic and copies ran while one was open for 1% of the time, Pallas kernels for 16%

profile of v17, /device:TPU:0, one launch (start us, length us, event | category | flops | bytes accessed | tf_op | source)
XLA Modules:
  0.0 56.8 jit_solution(4082322422761616387)
XLA Ops:
  0.6 4.1 %collective-permute-start = (bf16[256,512]{1,0:T(8,128)(2,1)}, bf16[256,512]{1,0:T(8,128)(2,1)S(1)}, u32[]{:S(2)}, u32[]{:S(2)}) collective-permute-start(bf16[256,512]{1,0:T(8,128)(2,1)} %refs_0_), channel_id=1, source_target_pairs={{0,4},{1,5},{2,6},{3,7},{4,0},{5,1},{6,2},{7,3},{8,12},{9,13},{10,... | collective-permute-start | bytes 786440 | tf_op jit(solution)/shard_map/ppermute | solution.py:249
  4.7 1.5 %collective-permute-start.1 = (bf16[256,512]{1,0:T(8,128)(2,1)}, bf16[256,512]{1,0:T(8,128)(2,1)S(1)}, u32[]{:S(2)}, u32[]{:S(2)}) collective-permute-start(bf16[256,512]{1,0:T(8,128)(2,1)} %refs_0_), channel_id=1, source_target_pairs={{0,16},{1,17},{2,18},{3,19},{4,20},{5,21},{6,22},{7,23},{8,24},{9,... | collective-permute-start | bytes 786440 | tf_op jit(solution)/shard_map/ppermute | solution.py:249
  6.2 0.7 %pad_add_fusion.named_ref = s32[2,256]{1,0:T(2,128)S(1)} fusion(s32[1,256]{1,0:T(1,128)} %bitcast.11, s32[1,256]{1,0:T(1,128)} %bitcast.12), kind=kLoop, calls=%fused_computation | loop fusion | flops 512 | bytes 4096 | tf_op jit(solution)/shard_map/stack | solution.py:314
  7.4 11.7 %all_to_all.12 = s32[32,1,80]{2,1,0:T(1,128)S(1)} all-to-all(s32[32,1,80]{2,1,0:T(1,128)S(1)} %bitcast.10), channel_id=1, replica_groups=mesh['batch'=4,'item'=8] {'batch','item'}, dimensions={0} | all-to-all | bytes 20480 | tf_op jit(solution)/shard_map/all_to_all | solution.py:317
  19.2 0.5 collective-permute-start.3
  19.7 0.6 %collective-permute-start.7 = (bf16[256,512]{1,0:T(8,128)(2,1)S(1)}, bf16[256,512]{1,0:T(8,128)(2,1)S(1)}, u32[]{:S(2)}, u32[]{:S(2)}) collective-permute-start(bf16[256,512]{1,0:T(8,128)(2,1)S(1)} %collective-permute-done.refs_0_), channel_id=1, source_target_pairs={{0,16},{1,17},{2,18},{3,19},{4,20},{5,21},{6,22},{7,23},{8,24},{9,... | collective-permute-start | bytes 786440 | tf_op jit(solution)/shard_map/ppermute | solution.py:249
  20.3 0.9 %shard_map.69 = bf16[128,512]{1,0:T(8,128)(2,1)S(1)} custom-call(s32[32,80]{1,0:T(8,128)S(1)} %bitcast.6, bf16[4096,512]{1,0:T(8,128)(2,1)S(1)} %copy-done), custom_call_target="tpu_custom_call" | custom-call | flops 536870912 | bytes 1048576 | tf_op jit(solution)/shard_map/pallas_call | solution.py:238
  21.2 0.8 %collective-permute-start.6 = (bf16[128,512]{1,0:T(8,128)(2,1)S(1)}, bf16[128,512]{1,0:T(8,128)(2,1)S(1)}, u32[]{:S(2)}, u32[]{:S(2)}) collective-permute-start(bf16[128,512]{1,0:T(8,128)(2,1)S(1)} %shard_map.69), channel_id=1, source_target_pairs={{0,3},{1,2},{2,1},{3,0},{4,7},{5,6},{6,5},{7,4},{8,11},{9,10},{10,... | collective-permute-start | bytes 393224 | tf_op jit(solution)/shard_map/ppermute | solution.py:249
  22.0 1.6 %shard_map.70 = (bf16[128,512]{1,0:T(8,128)(2,1)S(1)}, bf16[128,512]{1,0:T(8,128)(2,1)S(1)}) custom-call(s32[32,80]{1,0:T(8,128)S(1)} %bitcast.7, bf16[4096,512]{1,0:T(8,128)(2,1)S(1)} %copy-done), custom_call_target="tpu_custom_call" | custom-call | flops 1073741824 | bytes 1048576 | tf_op jit(solution)/shard_map/pallas_call | solution.py:238
  23.6 1.3 %collective-permute-start.4 = (bf16[128,512]{1,0:T(8,128)(2,1)S(1)}, bf16[128,512]{1,0:T(8,128)(2,1)S(1)}, u32[]{:S(2)}, u32[]{:S(2)}) collective-permute-start(bf16[128,512]{1,0:T(8,128)(2,1)S(1)} %get-tuple-element.58), channel_id=1, source_target_pairs={{0,1},{1,0},{2,3},{3,2},{4,5},{5,4},{6,7},{7,6},{8,9},{9,8},{10,11... | collective-permute-start | bytes 393224 | tf_op jit(solution)/shard_map/ppermute | solution.py:249
  24.9 1.5 %collective-permute-start.5 = (bf16[128,512]{1,0:T(8,128)(2,1)S(1)}, bf16[128,512]{1,0:T(8,128)(2,1)S(1)}, u32[]{:S(2)}, u32[]{:S(2)}) collective-permute-start(bf16[128,512]{1,0:T(8,128)(2,1)S(1)} %get-tuple-element.59), channel_id=1, source_target_pairs={{0,2},{1,3},{2,0},{3,1},{4,6},{5,7},{6,4},{7,5},{8,10},{9,11},{10,... | collective-permute-start | bytes 393224 | tf_op jit(solution)/shard_map/ppermute | solution.py:249
  26.4 0.9 %shard_map.71.refs_0_ = bf16[128,512]{1,0:T(8,128)(2,1)S(1)} custom-call(s32[32,80]{1,0:T(8,128)S(1)} %bitcast.8, bf16[4096,512]{1,0:T(8,128)(2,1)S(1)} %copy-done), custom_call_target="tpu_custom_call" | custom-call | flops 536870912 | bytes 1048576 | tf_op jit(solution)/shard_map/pallas_call | solution.py:238
  27.3 1.0 %shard_map.72 = (s32[512,1]{1,0:T(8,128)S(1)}, bf16[256,512]{1,0:T(8,128)(2,1)S(1)}, bf16[256,512]{1,0:T(8,128)(2,1)S(1)}, bf16[1024,512]{1,0:T(8,128)(2,1)S(1)}, bf16[256,512]{1,0:T(8,128)(2,1)S(1)}) custom-call(s32[32,80]{1,0:T(8,128)S(1)} %bitcast.9, bf16[256,512]{1,0:T(8,128)(2,1)S(1)} %copy-done.1, bf16[256,512]{1,0:T(8,128)(2,1)S(1)} %collective-permute-done.2.refs_1_, ...), custom_call_target="tpu_custom_call" | custom-call | tf_op jit(solution)/shard_map/pallas_call | solution.py:238
  28.4 0.5 collective-permute-start.9
  28.9 1.2 %collective-permute-done.4.refs_1_ = bf16[128,512]{1,0:T(8,128)(2,1)S(1)} collective-permute-done((bf16[128,512]{1,0:T(8,128)(2,1)S(1)}, bf16[128,512]{1,0:T(8,128)(2,1)S(1)}, u32[]{:S(2)}, u32[]{:S(2)}) %collective-permute-start.4) | collective-permute-done | bytes 131104 | tf_op jit(solution)/shard_map/ppermute | solution.py:249
  30.2 0.5 shard_map.73
  30.7 0.7 %shard_map.74 = (bf16[1024,512]{1,0:T(8,128)(2,1)S(1)}, bf16[256,512]{1,0:T(8,128)(2,1)S(1)}) custom-call(s32[512,1]{1,0:T(8,128)S(1)} %get-tuple-element.67.place_ref, bf16[256,512]{1,0:T(8,128)(2,1)S(1)} %collective-permute-done.refs_0_, bf16[256,512]{1,0:T(8,128)(2,1)S(1)} %collective-permute-done.8.refs_1_, ...), custom_call_target="tpu_custom_call" | custom-call | tf_op jit(solution)/shard_map/pallas_call | solution.py:238
  31.4 1.7 %shard_map.75 = (bf16[128,512]{1,0:T(8,128)(2,1)S(1)}, bf16[128,512]{1,0:T(8,128)(2,1)S(1)}, bf16[128,512]{1,0:T(8,128)(2,1)S(1)}, bf16[128,512]{1,0:T(8,128)(2,1)S(1)}) custom-call(f32[512,512]{1,0:T(8,128)S(1)} %get-tuple-element.61.hidden_ref, f32[512,1]{1,0:T(8,128)S(1)} %get-tuple-element.62.rscale_ref, ...), custom_call_target="tpu_custom_call" | custom-call | flops 2147483648 | bytes 1048576 | tf_op jit(solution)/shard_map/pallas_call | solution.py:238
  33.1 0.5 shard_map.77
  33.8 1.5 %collective-permute-done.13.refs_1_ = bf16[16,16,512]{2,1,0:T(8,128)(2,1)S(1)} collective-permute-done((bf16[16,16,512]{2,1,0:T(8,128)(2,1)S(1)}, bf16[16,16,512]{2,1,0:T(8,128)(2,1)S(1)}, u32[]{:S(2)}, u32[]{:S(2)}) %collective-permute-start.13) | collective-permute-done | bytes 262176 | tf_op jit(solution)/shard_map/ppermute | solution.py:249
  35.4 1.5 %collective-permute-start.14 = (bf16[8,16,512]{2,1,0:T(8,128)(2,1)S(1)}, bf16[8,16,512]{2,1,0:T(8,128)(2,1)S(1)}, u32[]{:S(2)}, u32[]{:S(2)}) collective-permute-start(bf16[8,16,512]{2,1,0:T(8,128)(2,1)S(1)} %get-tuple-element.80), channel_id=1, source_target_pairs={{0,16},{1,17},{2,18},{3,19},{4,20},{5,21},{6,22},{7,23},{8,24},{9,... | collective-permute-start | bytes 393224 | tf_op jit(solution)/shard_map/ppermute | solution.py:249
  36.9 0.6 %collective-permute-start.10 = (bf16[128,512]{1,0:T(8,128)(2,1)S(1)}, bf16[128,512]{1,0:T(8,128)(2,1)S(1)}, u32[]{:S(2)}, u32[]{:S(2)}) collective-permute-start(bf16[128,512]{1,0:T(8,128)(2,1)S(1)} %get-tuple-element.74.refs_5_), channel_id=1, source_target_pairs={{0,1},{1,0},{2,3},{3,2},{4,5},{5,4},{6,7},{7,6},{8,9},{9,8},{10,11... | collective-permute-start | bytes 393224 | tf_op jit(solution)/shard_map/ppermute | solution.py:249
  37.5 1.2 %collective-permute-start.11 = (bf16[128,512]{1,0:T(8,128)(2,1)S(1)}, bf16[128,512]{1,0:T(8,128)(2,1)S(1)}, u32[]{:S(2)}, u32[]{:S(2)}) collective-permute-start(bf16[128,512]{1,0:T(8,128)(2,1)S(1)} %get-tuple-element.75.refs_6_), channel_id=1, source_target_pairs={{0,2},{1,3},{2,0},{3,1},{4,6},{5,7},{6,4},{7,5},{8,10},{9,11},{10,... | collective-permute-start | bytes 393224 | tf_op jit(solution)/shard_map/ppermute | solution.py:249
  38.7 1.7 %collective-permute-start.12 = (bf16[128,512]{1,0:T(8,128)(2,1)S(1)}, bf16[128,512]{1,0:T(8,128)(2,1)S(1)}, u32[]{:S(2)}, u32[]{:S(2)}) collective-permute-start(bf16[128,512]{1,0:T(8,128)(2,1)S(1)} %get-tuple-element.76.refs_7_), channel_id=1, source_target_pairs={{0,3},{1,2},{2,1},{3,0},{4,7},{5,6},{6,5},{7,4},{8,11},{9,10},{10,... | collective-permute-start | bytes 393224 | tf_op jit(solution)/shard_map/ppermute | solution.py:249
  40.4 0.6 %collective-permute-done.14.refs_1_ = bf16[8,16,512]{2,1,0:T(8,128)(2,1)S(1)} collective-permute-done((bf16[8,16,512]{2,1,0:T(8,128)(2,1)S(1)}, bf16[8,16,512]{2,1,0:T(8,128)(2,1)S(1)}, u32[]{:S(2)}, u32[]{:S(2)}) %collective-permute-start.14) | collective-permute-done | bytes 131104 | tf_op jit(solution)/shard_map/ppermute | solution.py:249
  41.0 3.3 %collective-permute-start.15 = (bf16[4,16,512]{2,1,0:T(8,128)(2,1)S(1)}, bf16[4,16,512]{2,1,0:T(8,128)(2,1)S(1)}, u32[]{:S(2)}, u32[]{:S(2)}) collective-permute-start(bf16[4,16,512]{2,1,0:T(8,128)(2,1)S(1)} %get-tuple-element.82), channel_id=1, source_target_pairs={{0,4},{1,5},{2,6},{3,7},{4,0},{5,1},{6,2},{7,3},{8,12},{9,13},{10,... | collective-permute-start | bytes 196616 | tf_op jit(solution)/shard_map/ppermute | solution.py:249
  44.4 2.3 %collective-permute-done.15.refs_1_ = bf16[4,16,512]{2,1,0:T(8,128)(2,1)S(1)} collective-permute-done((bf16[4,16,512]{2,1,0:T(8,128)(2,1)S(1)}, bf16[4,16,512]{2,1,0:T(8,128)(2,1)S(1)}, u32[]{:S(2)}, u32[]{:S(2)}) %collective-permute-start.15) | collective-permute-done | bytes 65568 | tf_op jit(solution)/shard_map/ppermute | solution.py:249
  46.7 3.2 %collective-permute-start.16 = (f32[1,16,512]{2,1,0:T(8,128)S(1)}, f32[1,16,512]{2,1,0:T(8,128)S(1)}, u32[]{:S(2)}, u32[]{:S(2)}) collective-permute-start(f32[1,16,512]{2,1,0:T(8,128)S(1)} %get-tuple-element.84), channel_id=1, source_target_pairs={{0,2},{1,3},{2,0},{3,1},{4,6},{5,7},{6,4},{7,5},{8,10},{9,11},{10,... | collective-permute-start | bytes 98312 | tf_op jit(solution)/shard_map/ppermute | solution.py:249
  50.0 1.4 %collective-permute-start.17 = (f32[1,16,512]{2,1,0:T(8,128)S(1)}, f32[1,16,512]{2,1,0:T(8,128)S(1)}, u32[]{:S(2)}, u32[]{:S(2)}) collective-permute-start(f32[1,16,512]{2,1,0:T(8,128)S(1)} %get-tuple-element.85), channel_id=1, source_target_pairs={{0,1},{1,0},{2,3},{3,2},{4,5},{5,4},{6,7},{7,6},{8,9},{9,8},{10,11... | collective-permute-start | bytes 98312 | tf_op jit(solution)/shard_map/ppermute | solution.py:249
  51.5 3.6 %shard_map.76 = bf16[4096,512]{1,0:T(8,128)(2,1)} custom-call(bf16[256,512]{1,0:T(8,128)(2,1)S(1)} %get-tuple-element.55.low_hot_ref, bf16[256,512]{1,0:T(8,128)(2,1)S(1)} %get-tuple-element.56.block_ref, bf16[512,512]{1,0:T(8,128)(2,1)S(1)} %copy-done.2, bf16[128,512]{1,0:T(8,128)(2,1)S(1)} %get-tuple-element.73.refs_0_.refs_4_, ...), custom_call_target="tpu_custom_call" | custom-call | flops 2147483648 | bytes 4194304 | tf_op jit(solution)/shard_map/pallas_call | solution.py:387
  55.1 1.1 %collective-permute-done.18.refs_3_ = f32[1,16,512]{2,1,0:T(8,128)S(1)} collective-permute-done((f32[1,16,512]{2,1,0:T(8,128)S(1)}, f32[1,16,512]{2,1,0:T(8,128)S(1)}, u32[]{:S(2)}, u32[]{:S(2)}) %collective-permute-start.18) | collective-permute-done | bytes 32800 | tf_op jit(solution)/shard_map/ppermute | solution.py:249
  56.2 0.6 %shard_map.81 = f32[16,512]{1,0:T(8,128)} custom-call(f32[1,16,512]{2,1,0:T(8,128)S(1)} %get-tuple-element.88.refs_0_, f32[1,16,512]{2,1,0:T(8,128)S(1)} %collective-permute-done.16.refs_1_, f32[1,16,512]{2,1,0:T(8,128)S(1)} %collective-permute-done.17.refs_2_, f32[1,16,512]{2,1,0:T(8,128)S(1)} %collective-permute-done.18.refs_3_), custom_call_target="tpu_custom_call" | custom-call | bytes 1048576 | tf_op jit(solution)/shard_map/pallas_call | solution.py:238
  (28 shorter events, 1.0 us)
Async XLA Ops:
  0.6 18.4 %collective-permute-start = (bf16[256,512]{1,0:T(8,128)(2,1)}, bf16[256,512]{1,0:T(8,128)(2,1)S(1)}, u32[]{:S(2)}, u32[]{:S(2)}) collective-permute-start(bf16[256,512]{1,0:T(8,128)(2,1)} %refs_0_), channel_id=1, source_target_pairs={{0,4},{1,5},{2,6},{3,7},{4,0},{5,1},{6,2},{7,3},{8,12},{9,13},{10,... | collective-permute-start | bytes 786440 | tf_op jit(solution)/shard_map/ppermute | solution.py:249
  4.7 14.4 %collective-permute-start.1 = (bf16[256,512]{1,0:T(8,128)(2,1)}, bf16[256,512]{1,0:T(8,128)(2,1)S(1)}, u32[]{:S(2)}, u32[]{:S(2)}) collective-permute-start(bf16[256,512]{1,0:T(8,128)(2,1)} %refs_0_), channel_id=1, source_target_pairs={{0,16},{1,17},{2,18},{3,19},{4,20},{5,21},{6,22},{7,23},{8,24},{9,... | collective-permute-start | bytes 786440 | tf_op jit(solution)/shard_map/ppermute | solution.py:249
  6.9 12.2 %copy-start.1 = (bf16[256,512]{1,0:T(8,128)(2,1)S(1)}, bf16[256,512]{1,0:T(8,128)(2,1)}, u32[]{:S(2)}) copy-start(bf16[256,512]{1,0:T(8,128)(2,1)} %refs_0_) | copy-start | bytes 786436
  6.9 13.3 %copy-start = (bf16[4096,512]{1,0:T(8,128)(2,1)S(1)}, bf16[4096,512]{1,0:T(8,128)(2,1)}, u32[]{:S(2)}) copy-start(bf16[4096,512]{1,0:T(8,128)(2,1)} %table_ref.5) | copy-start | bytes 12582916
  19.1 5.8 %collective-permute-start.2 = (bf16[256,512]{1,0:T(8,128)(2,1)S(1)}, bf16[256,512]{1,0:T(8,128)(2,1)S(1)}, u32[]{:S(2)}, u32[]{:S(2)}) collective-permute-start(bf16[256,512]{1,0:T(8,128)(2,1)S(1)} %copy-done.1), channel_id=1, source_target_pairs={{0,8},{1,9},{2,10},{3,11},{4,12},{5,13},{6,14},{7,15},{8,0},{9,1},... | collective-permute-start | bytes 786440 | tf_op jit(solution)/shard_map/ppermute | solution.py:249
  19.2 8.1 %collective-permute-start.3 = (bf16[256,512]{1,0:T(8,128)(2,1)S(1)}, bf16[256,512]{1,0:T(8,128)(2,1)S(1)}, u32[]{:S(2)}, u32[]{:S(2)}) collective-permute-start(bf16[256,512]{1,0:T(8,128)(2,1)S(1)} %collective-permute-done.1.refs_2_), channel_id=1, source_target_pairs={{0,8},{1,9},{2,10},{3,11},{4,12},{5,13},{6,14},{7,15},{8,0},{9,1},... | collective-permute-start | bytes 786440 | tf_op jit(solution)/shard_map/ppermute | solution.py:249
  19.7 8.7 %collective-permute-start.7 = (bf16[256,512]{1,0:T(8,128)(2,1)S(1)}, bf16[256,512]{1,0:T(8,128)(2,1)S(1)}, u32[]{:S(2)}, u32[]{:S(2)}) collective-permute-start(bf16[256,512]{1,0:T(8,128)(2,1)S(1)} %collective-permute-done.refs_0_), channel_id=1, source_target_pairs={{0,16},{1,17},{2,18},{3,19},{4,20},{5,21},{6,22},{7,23},{8,24},{9,... | collective-permute-start | bytes 786440 | tf_op jit(solution)/shard_map/ppermute | solution.py:249
  21.2 9.0 %copy-start.2 = (bf16[512,512]{1,0:T(8,128)(2,1)S(1)}, bf16[512,512]{1,0:T(8,128)(2,1)}, u32[]{:S(2)}) copy-start(bf16[512,512]{1,0:T(8,128)(2,1)} %weight_ref.3) | copy-start | bytes 1572868
  21.2 7.7 %collective-permute-start.6 = (bf16[128,512]{1,0:T(8,128)(2,1)S(1)}, bf16[128,512]{1,0:T(8,128)(2,1)S(1)}, u32[]{:S(2)}, u32[]{:S(2)}) collective-permute-start(bf16[128,512]{1,0:T(8,128)(2,1)S(1)} %shard_map.69), channel_id=1, source_target_pairs={{0,3},{1,2},{2,1},{3,0},{4,7},{5,6},{6,5},{7,4},{8,11},{9,10},{10,... | collective-permute-start | bytes 393224 | tf_op jit(solution)/shard_map/ppermute | solution.py:249
  23.6 6.6 %collective-permute-start.4 = (bf16[128,512]{1,0:T(8,128)(2,1)S(1)}, bf16[128,512]{1,0:T(8,128)(2,1)S(1)}, u32[]{:S(2)}, u32[]{:S(2)}) collective-permute-start(bf16[128,512]{1,0:T(8,128)(2,1)S(1)} %get-tuple-element.58), channel_id=1, source_target_pairs={{0,1},{1,0},{2,3},{3,2},{4,5},{5,4},{6,7},{7,6},{8,9},{9,8},{10,11... | collective-permute-start | bytes 393224 | tf_op jit(solution)/shard_map/ppermute | solution.py:249
  24.9 5.2 %collective-permute-start.5 = (bf16[128,512]{1,0:T(8,128)(2,1)S(1)}, bf16[128,512]{1,0:T(8,128)(2,1)S(1)}, u32[]{:S(2)}, u32[]{:S(2)}) collective-permute-start(bf16[128,512]{1,0:T(8,128)(2,1)S(1)} %get-tuple-element.59), channel_id=1, source_target_pairs={{0,2},{1,3},{2,0},{3,1},{4,6},{5,7},{6,4},{7,5},{8,10},{9,11},{10,... | collective-permute-start | bytes 393224 | tf_op jit(solution)/shard_map/ppermute | solution.py:249
  28.3 2.3 %collective-permute-start.8 = (bf16[256,512]{1,0:T(8,128)(2,1)S(1)}, bf16[256,512]{1,0:T(8,128)(2,1)S(1)}, u32[]{:S(2)}, u32[]{:S(2)}) collective-permute-start(bf16[256,512]{1,0:T(8,128)(2,1)S(1)} %collective-permute-done.refs_0_), channel_id=1, source_target_pairs={{0,8},{1,9},{2,10},{3,11},{4,12},{5,13},{6,14},{7,15},{8,0},{9,1},... | collective-permute-start | bytes 786440 | tf_op jit(solution)/shard_map/ppermute | solution.py:249
  28.4 2.3 %collective-permute-start.9 = (bf16[256,512]{1,0:T(8,128)(2,1)S(1)}, bf16[256,512]{1,0:T(8,128)(2,1)S(1)}, u32[]{:S(2)}, u32[]{:S(2)}) collective-permute-start(bf16[256,512]{1,0:T(8,128)(2,1)S(1)} %collective-permute-done.7.refs_2_), channel_id=1, source_target_pairs={{0,8},{1,9},{2,10},{3,11},{4,12},{5,13},{6,14},{7,15},{8,0},{9,1},... | collective-permute-start | bytes 786440 | tf_op jit(solution)/shard_map/ppermute | solution.py:249
  33.7 1.6 %collective-permute-start.13 = (bf16[16,16,512]{2,1,0:T(8,128)(2,1)S(1)}, bf16[16,16,512]{2,1,0:T(8,128)(2,1)S(1)}, u32[]{:S(2)}, u32[]{:S(2)}) collective-permute-start(bf16[16,16,512]{2,1,0:T(8,128)(2,1)S(1)} %get-tuple-element.78), channel_id=1, source_target_pairs={{0,8},{1,9},{2,10},{3,11},{4,12},{5,13},{6,14},{7,15},{8,0},{9,1},... | collective-permute-start | bytes 786440 | tf_op jit(solution)/shard_map/ppermute | solution.py:249
  35.4 5.6 %collective-permute-start.14 = (bf16[8,16,512]{2,1,0:T(8,128)(2,1)S(1)}, bf16[8,16,512]{2,1,0:T(8,128)(2,1)S(1)}, u32[]{:S(2)}, u32[]{:S(2)}) collective-permute-start(bf16[8,16,512]{2,1,0:T(8,128)(2,1)S(1)} %get-tuple-element.80), channel_id=1, source_target_pairs={{0,16},{1,17},{2,18},{3,19},{4,20},{5,21},{6,22},{7,23},{8,24},{9,... | collective-permute-start | bytes 393224 | tf_op jit(solution)/shard_map/ppermute | solution.py:249
  36.9 14.5 %collective-permute-start.10 = (bf16[128,512]{1,0:T(8,128)(2,1)S(1)}, bf16[128,512]{1,0:T(8,128)(2,1)S(1)}, u32[]{:S(2)}, u32[]{:S(2)}) collective-permute-start(bf16[128,512]{1,0:T(8,128)(2,1)S(1)} %get-tuple-element.74.refs_5_), channel_id=1, source_target_pairs={{0,1},{1,0},{2,3},{3,2},{4,5},{5,4},{6,7},{7,6},{8,9},{9,8},{10,11... | collective-permute-start | bytes 393224 | tf_op jit(solution)/shard_map/ppermute | solution.py:249
  37.5 14.0 %collective-permute-start.11 = (bf16[128,512]{1,0:T(8,128)(2,1)S(1)}, bf16[128,512]{1,0:T(8,128)(2,1)S(1)}, u32[]{:S(2)}, u32[]{:S(2)}) collective-permute-start(bf16[128,512]{1,0:T(8,128)(2,1)S(1)} %get-tuple-element.75.refs_6_), channel_id=1, source_target_pairs={{0,2},{1,3},{2,0},{3,1},{4,6},{5,7},{6,4},{7,5},{8,10},{9,11},{10,... | collective-permute-start | bytes 393224 | tf_op jit(solution)/shard_map/ppermute | solution.py:249
  38.7 12.8 %collective-permute-start.12 = (bf16[128,512]{1,0:T(8,128)(2,1)S(1)}, bf16[128,512]{1,0:T(8,128)(2,1)S(1)}, u32[]{:S(2)}, u32[]{:S(2)}) collective-permute-start(bf16[128,512]{1,0:T(8,128)(2,1)S(1)} %get-tuple-element.76.refs_7_), channel_id=1, source_target_pairs={{0,3},{1,2},{2,1},{3,0},{4,7},{5,6},{6,5},{7,4},{8,11},{9,10},{10,... | collective-permute-start | bytes 393224 | tf_op jit(solution)/shard_map/ppermute | solution.py:249
  41.0 5.7 %collective-permute-start.15 = (bf16[4,16,512]{2,1,0:T(8,128)(2,1)S(1)}, bf16[4,16,512]{2,1,0:T(8,128)(2,1)S(1)}, u32[]{:S(2)}, u32[]{:S(2)}) collective-permute-start(bf16[4,16,512]{2,1,0:T(8,128)(2,1)S(1)} %get-tuple-element.82), channel_id=1, source_target_pairs={{0,4},{1,5},{2,6},{3,7},{4,0},{5,1},{6,2},{7,3},{8,12},{9,13},{10,... | collective-permute-start | bytes 196616 | tf_op jit(solution)/shard_map/ppermute | solution.py:249
  46.7 8.4 %collective-permute-start.16 = (f32[1,16,512]{2,1,0:T(8,128)S(1)}, f32[1,16,512]{2,1,0:T(8,128)S(1)}, u32[]{:S(2)}, u32[]{:S(2)}) collective-permute-start(f32[1,16,512]{2,1,0:T(8,128)S(1)} %get-tuple-element.84), channel_id=1, source_target_pairs={{0,2},{1,3},{2,0},{3,1},{4,6},{5,7},{6,4},{7,5},{8,10},{9,11},{10,... | collective-permute-start | bytes 98312 | tf_op jit(solution)/shard_map/ppermute | solution.py:249
  50.0 5.2 %collective-permute-start.17 = (f32[1,16,512]{2,1,0:T(8,128)S(1)}, f32[1,16,512]{2,1,0:T(8,128)S(1)}, u32[]{:S(2)}, u32[]{:S(2)}) collective-permute-start(f32[1,16,512]{2,1,0:T(8,128)S(1)} %get-tuple-element.85), channel_id=1, source_target_pairs={{0,1},{1,0},{2,3},{3,2},{4,5},{5,4},{6,7},{7,6},{8,9},{9,8},{10,11... | collective-permute-start | bytes 98312 | tf_op jit(solution)/shard_map/ppermute | solution.py:249
  51.4 4.8 %collective-permute-start.18 = (f32[1,16,512]{2,1,0:T(8,128)S(1)}, f32[1,16,512]{2,1,0:T(8,128)S(1)}, u32[]{:S(2)}, u32[]{:S(2)}) collective-permute-start(f32[1,16,512]{2,1,0:T(8,128)S(1)} %get-tuple-element.86), channel_id=1, source_target_pairs={{0,3},{1,2},{2,1},{3,0},{4,7},{5,6},{6,5},{7,4},{8,11},{9,10},{10,... | collective-permute-start | bytes 98312 | tf_op jit(solution)/shard_map/ppermute | solution.py:249

commit v18 on v15

--- a/solution.py
+++ b/solution.py
@@ -205,23 +205,24 @@
     total_ref[...] = sum(ref[...].astype(f32) for ref in came)[0]
 
 
-def table_kernel(low_hot_ref, block_ref, weight_ref, *refs):
-    *incoming, table_grad_hbm, ready, sems = refs
-    dhidden = jnp.concatenate([ref[...] for ref in incoming], axis=0)
-    drow = dot(dhidden, weight_ref[...], 1, 1).astype(bf16)
-    groups = sems.shape[0]
-    size = ready.shape[0] // groups
-    copies = []
-    for g in range(groups):
-        here = pl.ds(g * size, size)
+def row_kernel(weight_ref, *refs):
+    *incoming, drow_ref = refs
+    drow_ref[...] = dot(jnp.concatenate([ref[...] for ref in incoming], axis=0), weight_ref[...], 1, 1).astype(bf16)
+
+
+def table_kernel(sizes, low_hot_ref, block_ref, drow_ref, table_grad_hbm, ready, sems):
+    copies, start = [], 0
+    for g, size in enumerate(sizes):
+        here = pl.ds(start, size)
         picks = [
             jnp.where(block_ref[...] == jnp.bfloat16(k), low_hot_ref[...], jnp.bfloat16(0))
-            for k in range(g * size // BLOCK, (g + 1) * size // BLOCK)
+            for k in range(start // BLOCK, (start + size) // BLOCK)
         ]
-        ready[here] = dot(jnp.concatenate(picks, axis=0), drow).astype(bf16)
+        ready[here] = dot(jnp.concatenate(picks, axis=0), drow_ref[...]).astype(bf16)
         copy = pltpu.make_async_copy(ready.at[here], table_grad_hbm.at[here], sems.at[g])
         copy.start()
         copies.append(copy)
+        start += size
     for copy in copies:
         copy.wait()
 
@@ -257,7 +258,7 @@
     return sum((lax.axis_size("item") if axis == "batch" else 1) << level for axis, level in bits)
 
 
-def reduce_scatter(fetched, dhidden, incoming):
+def reduce_scatter(fetched, dhidden, drow):
     width = dhidden[0].shape[1]
     n_item, devices = lax.axis_size("item"), lax.axis_size("batch") * lax.axis_size("item")
     part = width // devices
@@ -289,8 +290,8 @@
         )
         values = [kept] + [swap(value, mask) for mask, value in zip(masks, sends)]
         if k == 2:
-            values, incoming = lax.optimization_barrier((values, incoming))
-    return values, incoming
+            values, drow = lax.optimization_barrier((values, drow))
+    return values, drow
 
 
 def local(user_vectors, item_table, tower_weight, item_owner, item_row):
@@ -303,7 +304,7 @@
     slots = 2 * n // devices
     total = devices * slots
     size = total // near
-    groups = rows // min(512, rows)
+    sizes = [rows // 2, rows // 4, rows // 8, rows // 8]
 
     far = [batch * n_item for batch in range(2, n_batch, 2)]
     users = {0: user_vectors}
@@ -339,7 +340,9 @@
 
     fetched = {}
     for parts in [[near - 1], list(range(1, near - 1)), [0]]:
-        asked, *values = lax.optimization_barrier((asked, *fetch(parts)))
+        close = {mask: users[mask] for mask in [0, *far]}
+        (asked, close), *values = lax.optimization_barrier(((asked, close), *fetch(parts)))
+        users |= close if 0 not in parts else {}
         for part, value in zip(parts, values):
             fetched[part] = swap(value, part) if part else value
     fetched = [fetched[part] for part in range(near)]
@@ -385,15 +388,16 @@
         mib=40,
     )
     incoming = [swap(dhidden[part], part) for part in range(1, near)]
-    terms, incoming = reduce_scatter(fetched, dhidden, incoming)
+    (drow,) = call(row_kernel, [((total, width), bf16)], tower_weight, dhidden[0], *incoming, free=True)
+    terms, drow = reduce_scatter(fetched, dhidden, drow)
     table_grad = pl.pallas_call(
-        table_kernel,
+        functools.partial(table_kernel, sizes),
         out_specs=pl.BlockSpec(memory_space=pl.ANY),
         out_shape=jax.ShapeDtypeStruct((rows, width), bf16),
-        scratch_shapes=[pltpu.VMEM((rows, width), bf16), pltpu.SemaphoreType.DMA((groups,))],
+        scratch_shapes=[pltpu.VMEM((rows, width), bf16), pltpu.SemaphoreType.DMA((len(sizes),))],
         compiler_params=params(16),
         cost_estimate=cost(2 * total * rows * width, 2 * rows * width),
-    )(low_hot, block, tower_weight, dhidden[0], *incoming)
+    )(low_hot, block, drow)
     table_grad, *terms = lax.optimization_barrier((table_grad, *terms))
     (weight_grad,) = call(last_kernel, [((width // devices, width), f32)], *terms)
     return (table_grad, weight_grad)

time: 55.2 us -> 56.5 us (1.024)
  waiting for transfers between devices: 6.57 us -> 7.89 us
    ppermute x19, waiting for transfers between devices: 6.57 us -> 7.89 us  [swap(): lax.ppermute(value, ('batch', 'item'), [(k, k ^ mask) for k in range(devi...]
    pallas_call x13 -> x14, Pallas kernels: 9.08 us -> 9.55 us  [call(): pl.pallas_call(kernel, out_shape=[jax.ShapeDtypeStruct(shape, dtype) for...]
  transfers between devices with their start and end apart: 19 -> 19, of which waited for: 6 -> 8; matrix products, arithmetic and copies ran while one was open for 1% -> 1% of each run, Pallas kernels for 16% -> 12%
where the time goes in v18:
time: 56.5 us; the launch traced here: 56.3 us
  starting transfers between devices  22.3 us (39%)
  Pallas kernels  12.8 us (23%)
  blocking collectives  11.7 us (21%)
  waiting for transfers between devices  7.89 us (14%)
  between operations  0.81 us (1%)
  other arithmetic  0.7 us (1%)
    ppermute x19, starting transfers between devices, swap(): lax.ppermute(value, ('batch', 'item'), [(k, k ^ mask) for k in range(devi...  22.3 us
    all_to_all x1, blocking collectives, local(): lax.all_to_all(request, ('batch', 'item'), split_axis=0, concat_axis=0, t...  11.7 us
    pallas_call x14, Pallas kernels, call(): pl.pallas_call(kernel, out_shape=[jax.ShapeDtypeStruct(shape, dtype) for...  9.55 us
    ppermute x19, waiting for transfers between devices, swap(): lax.ppermute(value, ('batch', 'item'), [(k, k ^ mask) for k in range(devi...  7.89 us
    pallas_call x1, Pallas kernels, local(): pl.pallas_call(functools.partial(table_kernel, sizes), out_specs=pl.Block...  3.29 us
  transfers between devices with their start and end apart: 19, of which 8 were waited for; matrix products, arithmetic and copies ran while one was open for 1% of the time, Pallas kernels for 12%

profile of v18, /device:TPU:0, one launch (start us, length us, event | category | flops | bytes accessed | tf_op | source)
XLA Modules:
  0.0 56.3 jit_solution(12889840696993867269)
XLA Ops:
  0.6 4.1 %collective-permute-start = (bf16[256,512]{1,0:T(8,128)(2,1)}, bf16[256,512]{1,0:T(8,128)(2,1)S(1)}, u32[]{:S(2)}, u32[]{:S(2)}) collective-permute-start(bf16[256,512]{1,0:T(8,128)(2,1)} %refs_0_), channel_id=1, source_target_pairs={{0,4},{1,5},{2,6},{3,7},{4,0},{5,1},{6,2},{7,3},{8,12},{9,13},{10,... | collective-permute-start | bytes 786440 | tf_op jit(solution)/shard_map/ppermute | solution.py:250
  4.7 1.5 %collective-permute-start.1 = (bf16[256,512]{1,0:T(8,128)(2,1)}, bf16[256,512]{1,0:T(8,128)(2,1)S(1)}, u32[]{:S(2)}, u32[]{:S(2)}) collective-permute-start(bf16[256,512]{1,0:T(8,128)(2,1)} %refs_0_), channel_id=1, source_target_pairs={{0,16},{1,17},{2,18},{3,19},{4,20},{5,21},{6,22},{7,23},{8,24},{9,... | collective-permute-start | bytes 786440 | tf_op jit(solution)/shard_map/ppermute | solution.py:250
  6.2 0.7 %pad_add_fusion.named_ref = s32[2,256]{1,0:T(2,128)S(1)} fusion(s32[1,256]{1,0:T(1,128)} %bitcast.11, s32[1,256]{1,0:T(1,128)} %bitcast.12), kind=kLoop, calls=%fused_computation | loop fusion | flops 512 | bytes 4096 | tf_op jit(solution)/shard_map/stack | solution.py:317
  7.4 11.7 %all_to_all.12 = s32[32,1,80]{2,1,0:T(1,128)S(1)} all-to-all(s32[32,1,80]{2,1,0:T(1,128)S(1)} %bitcast.10), channel_id=1, replica_groups=mesh['batch'=4,'item'=8] {'batch','item'}, dimensions={0} | all-to-all | bytes 20480 | tf_op jit(solution)/shard_map/all_to_all | solution.py:320
  19.1 0.9 %shard_map.69 = bf16[128,512]{1,0:T(8,128)(2,1)S(1)} custom-call(s32[32,80]{1,0:T(8,128)S(1)} %bitcast.6, bf16[4096,512]{1,0:T(8,128)(2,1)S(1)} %copy-done), custom_call_target="tpu_custom_call" | custom-call | flops 536870912 | bytes 1048576 | tf_op jit(solution)/shard_map/pallas_call | solution.py:239
  20.0 1.6 %shard_map.70 = (bf16[128,512]{1,0:T(8,128)(2,1)S(1)}, bf16[128,512]{1,0:T(8,128)(2,1)S(1)}) custom-call(s32[32,80]{1,0:T(8,128)S(1)} %bitcast.7, bf16[4096,512]{1,0:T(8,128)(2,1)S(1)} %copy-done), custom_call_target="tpu_custom_call" | custom-call | flops 1073741824 | bytes 1048576 | tf_op jit(solution)/shard_map/pallas_call | solution.py:239
  21.7 0.5 collective-permute-start.3
  22.2 0.6 %collective-permute-start.7 = (bf16[256,512]{1,0:T(8,128)(2,1)S(1)}, bf16[256,512]{1,0:T(8,128)(2,1)S(1)}, u32[]{:S(2)}, u32[]{:S(2)}) collective-permute-start(bf16[256,512]{1,0:T(8,128)(2,1)S(1)} %collective-permute-done.refs_0_), channel_id=1, source_target_pairs={{0,16},{1,17},{2,18},{3,19},{4,20},{5,21},{6,22},{7,23},{8,24},{9,... | collective-permute-start | bytes 786440 | tf_op jit(solution)/shard_map/ppermute | solution.py:250
  22.8 0.8 %collective-permute-start.6 = (bf16[128,512]{1,0:T(8,128)(2,1)S(1)}, bf16[128,512]{1,0:T(8,128)(2,1)S(1)}, u32[]{:S(2)}, u32[]{:S(2)}) collective-permute-start(bf16[128,512]{1,0:T(8,128)(2,1)S(1)} %shard_map.69), channel_id=1, source_target_pairs={{0,3},{1,2},{2,1},{3,0},{4,7},{5,6},{6,5},{7,4},{8,11},{9,10},{10,... | collective-permute-start | bytes 393224 | tf_op jit(solution)/shard_map/ppermute | solution.py:250
  23.5 1.3 %collective-permute-start.4 = (bf16[128,512]{1,0:T(8,128)(2,1)S(1)}, bf16[128,512]{1,0:T(8,128)(2,1)S(1)}, u32[]{:S(2)}, u32[]{:S(2)}) collective-permute-start(bf16[128,512]{1,0:T(8,128)(2,1)S(1)} %get-tuple-element.69), channel_id=1, source_target_pairs={{0,1},{1,0},{2,3},{3,2},{4,5},{5,4},{6,7},{7,6},{8,9},{9,8},{10,11... | collective-permute-start | bytes 393224 | tf_op jit(solution)/shard_map/ppermute | solution.py:250
  24.8 1.5 %collective-permute-start.5 = (bf16[128,512]{1,0:T(8,128)(2,1)S(1)}, bf16[128,512]{1,0:T(8,128)(2,1)S(1)}, u32[]{:S(2)}, u32[]{:S(2)}) collective-permute-start(bf16[128,512]{1,0:T(8,128)(2,1)S(1)} %get-tuple-element.70), channel_id=1, source_target_pairs={{0,2},{1,3},{2,0},{3,1},{4,6},{5,7},{6,4},{7,5},{8,10},{9,11},{10,... | collective-permute-start | bytes 393224 | tf_op jit(solution)/shard_map/ppermute | solution.py:250
  26.3 0.9 %shard_map.71.refs_0_ = bf16[128,512]{1,0:T(8,128)(2,1)S(1)} custom-call(s32[32,80]{1,0:T(8,128)S(1)} %bitcast.8, bf16[4096,512]{1,0:T(8,128)(2,1)S(1)} %copy-done), custom_call_target="tpu_custom_call" | custom-call | flops 536870912 | bytes 1048576 | tf_op jit(solution)/shard_map/pallas_call | solution.py:239
  27.2 1.0 %shard_map.72 = (s32[512,1]{1,0:T(8,128)S(1)}, bf16[256,512]{1,0:T(8,128)(2,1)S(1)}, bf16[256,512]{1,0:T(8,128)(2,1)S(1)}, bf16[1024,512]{1,0:T(8,128)(2,1)S(1)}, bf16[256,512]{1,0:T(8,128)(2,1)S(1)}) custom-call(s32[32,80]{1,0:T(8,128)S(1)} %bitcast.9, bf16[256,512]{1,0:T(8,128)(2,1)S(1)} %copy-done.2, bf16[256,512]{1,0:T(8,128)(2,1)S(1)} %collective-permute-done.2.refs_1_, ...), custom_call_target="tpu_custom_call" | custom-call | tf_op jit(solution)/shard_map/pallas_call | solution.py:239
  28.2 2.3 %collective-permute-done.7.refs_2_ = bf16[256,512]{1,0:T(8,128)(2,1)S(1)} collective-permute-done((bf16[256,512]{1,0:T(8,128)(2,1)S(1)}, bf16[256,512]{1,0:T(8,128)(2,1)S(1)}, u32[]{:S(2)}, u32[]{:S(2)}) %collective-permute-start.7) | collective-permute-done | bytes 262176 | tf_op jit(solution)/shard_map/ppermute | solution.py:250
  30.5 0.5 collective-permute-start.9
  31.3 0.5 shard_map.73
  32.4 0.7 %shard_map.74 = (bf16[1024,512]{1,0:T(8,128)(2,1)S(1)}, bf16[256,512]{1,0:T(8,128)(2,1)S(1)}) custom-call(s32[512,1]{1,0:T(8,128)S(1)} %get-tuple-element.78.place_ref, bf16[256,512]{1,0:T(8,128)(2,1)S(1)} %collective-permute-done.refs_0_, bf16[256,512]{1,0:T(8,128)(2,1)S(1)} %collective-permute-done.8.refs_1_, ...), custom_call_target="tpu_custom_call" | custom-call | tf_op jit(solution)/shard_map/pallas_call | solution.py:239
  33.1 1.7 %shard_map.75 = (bf16[128,512]{1,0:T(8,128)(2,1)S(1)}, bf16[128,512]{1,0:T(8,128)(2,1)S(1)}, bf16[128,512]{1,0:T(8,128)(2,1)S(1)}, bf16[128,512]{1,0:T(8,128)(2,1)S(1)}) custom-call(f32[512,512]{1,0:T(8,128)S(1)} %get-tuple-element.72.hidden_ref, f32[512,1]{1,0:T(8,128)S(1)} %get-tuple-element.73.rscale_ref, ...), custom_call_target="tpu_custom_call" | custom-call | flops 2147483648 | bytes 1048576 | tf_op jit(solution)/shard_map/pallas_call | solution.py:239
  34.8 0.5 shard_map.76
  35.6 1.4 %collective-permute-done.10.refs_1_ = bf16[16,16,512]{2,1,0:T(8,128)(2,1)S(1)} collective-permute-done((bf16[16,16,512]{2,1,0:T(8,128)(2,1)S(1)}, bf16[16,16,512]{2,1,0:T(8,128)(2,1)S(1)}, u32[]{:S(2)}, u32[]{:S(2)}) %collective-permute-start.10) | collective-permute-done | bytes 262176 | tf_op jit(solution)/shard_map/ppermute | solution.py:250
  37.1 0.8 %collective-permute-start.11 = (bf16[8,16,512]{2,1,0:T(8,128)(2,1)S(1)}, bf16[8,16,512]{2,1,0:T(8,128)(2,1)S(1)}, u32[]{:S(2)}, u32[]{:S(2)}) collective-permute-start(bf16[8,16,512]{2,1,0:T(8,128)(2,1)S(1)} %get-tuple-element.91), channel_id=1, source_target_pairs={{0,16},{1,17},{2,18},{3,19},{4,20},{5,21},{6,22},{7,23},{8,24},{9,... | collective-permute-start | bytes 393224 | tf_op jit(solution)/shard_map/ppermute | solution.py:250
  37.8 1.2 %collective-permute-start.15 = (bf16[128,512]{1,0:T(8,128)(2,1)S(1)}, bf16[128,512]{1,0:T(8,128)(2,1)S(1)}, u32[]{:S(2)}, u32[]{:S(2)}) collective-permute-start(bf16[128,512]{1,0:T(8,128)(2,1)S(1)} %get-tuple-element.85.refs_5_), channel_id=1, source_target_pairs={{0,1},{1,0},{2,3},{3,2},{4,5},{5,4},{6,7},{7,6},{8,9},{9,8},{10,11... | collective-permute-start | bytes 393224 | tf_op jit(solution)/shard_map/ppermute | solution.py:250
  39.0 0.6 %collective-permute-start.16 = (bf16[128,512]{1,0:T(8,128)(2,1)S(1)}, bf16[128,512]{1,0:T(8,128)(2,1)S(1)}, u32[]{:S(2)}, u32[]{:S(2)}) collective-permute-start(bf16[128,512]{1,0:T(8,128)(2,1)S(1)} %get-tuple-element.86.refs_6_), channel_id=1, source_target_pairs={{0,2},{1,3},{2,0},{3,1},{4,6},{5,7},{6,4},{7,5},{8,10},{9,11},{10,... | collective-permute-start | bytes 393224 | tf_op jit(solution)/shard_map/ppermute | solution.py:250
  39.6 1.7 %collective-permute-start.17 = (bf16[128,512]{1,0:T(8,128)(2,1)S(1)}, bf16[128,512]{1,0:T(8,128)(2,1)S(1)}, u32[]{:S(2)}, u32[]{:S(2)}) collective-permute-start(bf16[128,512]{1,0:T(8,128)(2,1)S(1)} %get-tuple-element.87.refs_7_), channel_id=1, source_target_pairs={{0,3},{1,2},{2,1},{3,0},{4,7},{5,6},{6,5},{7,4},{8,11},{9,10},{10,... | collective-permute-start | bytes 393224 | tf_op jit(solution)/shard_map/ppermute | solution.py:250
  41.3 1.4 %collective-permute-done.11.refs_1_ = bf16[8,16,512]{2,1,0:T(8,128)(2,1)S(1)} collective-permute-done((bf16[8,16,512]{2,1,0:T(8,128)(2,1)S(1)}, bf16[8,16,512]{2,1,0:T(8,128)(2,1)S(1)}, u32[]{:S(2)}, u32[]{:S(2)}) %collective-permute-start.11) | collective-permute-done | bytes 131104 | tf_op jit(solution)/shard_map/ppermute | solution.py:250
  42.7 0.7 %collective-permute-start.12 = (bf16[2,16,512]{2,1,0:T(8,128)(2,1)S(1)}, bf16[2,16,512]{2,1,0:T(8,128)(2,1)S(1)}, u32[]{:S(2)}, u32[]{:S(2)}) collective-permute-start(bf16[2,16,512]{2,1,0:T(8,128)(2,1)S(1)} %get-tuple-element.93), channel_id=1, source_target_pairs={{0,2},{1,3},{2,0},{3,1},{4,6},{5,7},{6,4},{7,5},{8,10},{9,11},{10,... | collective-permute-start | bytes 98312 | tf_op jit(solution)/shard_map/ppermute | solution.py:250
  43.4 0.5 collective-permute-start.13
  44.0 2.3 %collective-permute-start.14 = (bf16[2,16,512]{2,1,0:T(8,128)(2,1)S(1)}, bf16[2,16,512]{2,1,0:T(8,128)(2,1)S(1)}, u32[]{:S(2)}, u32[]{:S(2)}) collective-permute-start(bf16[2,16,512]{2,1,0:T(8,128)(2,1)S(1)} %get-tuple-element.95), channel_id=1, source_target_pairs={{0,3},{1,2},{2,1},{3,0},{4,7},{5,6},{6,5},{7,4},{8,11},{9,10},{10,... | collective-permute-start | bytes 98312 | tf_op jit(solution)/shard_map/ppermute | solution.py:250
  46.3 1.5 %collective-permute-done.17.refs_3_ = bf16[128,512]{1,0:T(8,128)(2,1)S(1)} collective-permute-done((bf16[128,512]{1,0:T(8,128)(2,1)S(1)}, bf16[128,512]{1,0:T(8,128)(2,1)S(1)}, u32[]{:S(2)}, u32[]{:S(2)}) %collective-permute-start.17) | collective-permute-done | bytes 131104 | tf_op jit(solution)/shard_map/ppermute | solution.py:250
  48.8 3.5 %collective-permute-start.18 = (f32[1,16,512]{2,1,0:T(8,128)S(1)}, f32[1,16,512]{2,1,0:T(8,128)S(1)}, u32[]{:S(2)}, u32[]{:S(2)}) collective-permute-start(f32[1,16,512]{2,1,0:T(8,128)S(1)} %get-tuple-element.102), channel_id=1, source_target_pairs={{0,4},{1,5},{2,6},{3,7},{4,0},{5,1},{6,2},{7,3},{8,12},{9,13},{10,... | collective-permute-start | bytes 98312 | tf_op jit(solution)/shard_map/ppermute | solution.py:250
  52.3 3.3 %shard_map.80 = bf16[4096,512]{1,0:T(8,128)(2,1)} custom-call(bf16[256,512]{1,0:T(8,128)(2,1)S(1)} %get-tuple-element.66.low_hot_ref, bf16[256,512]{1,0:T(8,128)(2,1)S(1)} %get-tuple-element.67.block_ref, bf16[512,512]{1,0:T(8,128)(2,1)S(1)} %shard_map.79.drow_ref), custom_call_target="tpu_custom_call" | custom-call | flops 2147483648 | bytes 4194304 | tf_op jit(solution)/shard_map/pallas_call | solution.py:393
  55.7 0.6 %shard_map.82 = f32[16,512]{1,0:T(8,128)} custom-call(f32[1,16,512]{2,1,0:T(8,128)S(1)} %get-tuple-element.104.refs_0_, f32[1,16,512]{2,1,0:T(8,128)S(1)} %collective-permute-done.18.refs_1_), custom_call_target="tpu_custom_call" | custom-call | bytes 1048576 | tf_op jit(solution)/shard_map/pallas_call | solution.py:239
  (29 shorter events, 2.7 us)
Async XLA Ops:
  0.6 18.4 %collective-permute-start = (bf16[256,512]{1,0:T(8,128)(2,1)}, bf16[256,512]{1,0:T(8,128)(2,1)S(1)}, u32[]{:S(2)}, u32[]{:S(2)}) collective-permute-start(bf16[256,512]{1,0:T(8,128)(2,1)} %refs_0_), channel_id=1, source_target_pairs={{0,4},{1,5},{2,6},{3,7},{4,0},{5,1},{6,2},{7,3},{8,12},{9,13},{10,... | collective-permute-start | bytes 786440 | tf_op jit(solution)/shard_map/ppermute | solution.py:250
  4.7 14.4 %collective-permute-start.1 = (bf16[256,512]{1,0:T(8,128)(2,1)}, bf16[256,512]{1,0:T(8,128)(2,1)S(1)}, u32[]{:S(2)}, u32[]{:S(2)}) collective-permute-start(bf16[256,512]{1,0:T(8,128)(2,1)} %refs_0_), channel_id=1, source_target_pairs={{0,16},{1,17},{2,18},{3,19},{4,20},{5,21},{6,22},{7,23},{8,24},{9,... | collective-permute-start | bytes 786440 | tf_op jit(solution)/shard_map/ppermute | solution.py:250
  6.9 12.2 %copy-start = (bf16[4096,512]{1,0:T(8,128)(2,1)S(1)}, bf16[4096,512]{1,0:T(8,128)(2,1)}, u32[]{:S(2)}) copy-start(bf16[4096,512]{1,0:T(8,128)(2,1)} %table_ref.5) | copy-start | bytes 12582916
  19.1 2.5 %copy-start.2 = (bf16[256,512]{1,0:T(8,128)(2,1)S(1)}, bf16[256,512]{1,0:T(8,128)(2,1)}, u32[]{:S(2)}) copy-start(bf16[256,512]{1,0:T(8,128)(2,1)} %refs_0_) | copy-start | bytes 786436
  20.0 11.3 %copy-start.1 = (bf16[512,512]{1,0:T(8,128)(2,1)S(1)}, bf16[512,512]{1,0:T(8,128)(2,1)}, u32[]{:S(2)}) copy-start(bf16[512,512]{1,0:T(8,128)(2,1)} %weight_ref.3) | copy-start | bytes 1572868
  21.6 3.2 %collective-permute-start.2 = (bf16[256,512]{1,0:T(8,128)(2,1)S(1)}, bf16[256,512]{1,0:T(8,128)(2,1)S(1)}, u32[]{:S(2)}, u32[]{:S(2)}) collective-permute-start(bf16[256,512]{1,0:T(8,128)(2,1)S(1)} %copy-done.2), channel_id=1, source_target_pairs={{0,8},{1,9},{2,10},{3,11},{4,12},{5,13},{6,14},{7,15},{8,0},{9,1},... | collective-permute-start | bytes 786440 | tf_op jit(solution)/shard_map/ppermute | solution.py:250
  21.7 5.5 %collective-permute-start.3 = (bf16[256,512]{1,0:T(8,128)(2,1)S(1)}, bf16[256,512]{1,0:T(8,128)(2,1)S(1)}, u32[]{:S(2)}, u32[]{:S(2)}) collective-permute-start(bf16[256,512]{1,0:T(8,128)(2,1)S(1)} %collective-permute-done.1.refs_2_), channel_id=1, source_target_pairs={{0,8},{1,9},{2,10},{3,11},{4,12},{5,13},{6,14},{7,15},{8,0},{9,1},... | collective-permute-start | bytes 786440 | tf_op jit(solution)/shard_map/ppermute | solution.py:250
  22.2 8.3 %collective-permute-start.7 = (bf16[256,512]{1,0:T(8,128)(2,1)S(1)}, bf16[256,512]{1,0:T(8,128)(2,1)S(1)}, u32[]{:S(2)}, u32[]{:S(2)}) collective-permute-start(bf16[256,512]{1,0:T(8,128)(2,1)S(1)} %collective-permute-done.refs_0_), channel_id=1, source_target_pairs={{0,16},{1,17},{2,18},{3,19},{4,20},{5,21},{6,22},{7,23},{8,24},{9,... | collective-permute-start | bytes 786440 | tf_op jit(solution)/shard_map/ppermute | solution.py:250
  22.8 8.2 %collective-permute-start.6 = (bf16[128,512]{1,0:T(8,128)(2,1)S(1)}, bf16[128,512]{1,0:T(8,128)(2,1)S(1)}, u32[]{:S(2)}, u32[]{:S(2)}) collective-permute-start(bf16[128,512]{1,0:T(8,128)(2,1)S(1)} %shard_map.69), channel_id=1, source_target_pairs={{0,3},{1,2},{2,1},{3,0},{4,7},{5,6},{6,5},{7,4},{8,11},{9,10},{10,... | collective-permute-start | bytes 393224 | tf_op jit(solution)/shard_map/ppermute | solution.py:250
  23.5 7.7 %collective-permute-start.4 = (bf16[128,512]{1,0:T(8,128)(2,1)S(1)}, bf16[128,512]{1,0:T(8,128)(2,1)S(1)}, u32[]{:S(2)}, u32[]{:S(2)}) collective-permute-start(bf16[128,512]{1,0:T(8,128)(2,1)S(1)} %get-tuple-element.69), channel_id=1, source_target_pairs={{0,1},{1,0},{2,3},{3,2},{4,5},{5,4},{6,7},{7,6},{8,9},{9,8},{10,11... | collective-permute-start | bytes 393224 | tf_op jit(solution)/shard_map/ppermute | solution.py:250
  24.8 6.5 %collective-permute-start.5 = (bf16[128,512]{1,0:T(8,128)(2,1)S(1)}, bf16[128,512]{1,0:T(8,128)(2,1)S(1)}, u32[]{:S(2)}, u32[]{:S(2)}) collective-permute-start(bf16[128,512]{1,0:T(8,128)(2,1)S(1)} %get-tuple-element.70), channel_id=1, source_target_pairs={{0,2},{1,3},{2,0},{3,1},{4,6},{5,7},{6,4},{7,5},{8,10},{9,11},{10,... | collective-permute-start | bytes 393224 | tf_op jit(solution)/shard_map/ppermute | solution.py:250
  30.5 1.5 %collective-permute-start.8 = (bf16[256,512]{1,0:T(8,128)(2,1)S(1)}, bf16[256,512]{1,0:T(8,128)(2,1)S(1)}, u32[]{:S(2)}, u32[]{:S(2)}) collective-permute-start(bf16[256,512]{1,0:T(8,128)(2,1)S(1)} %collective-permute-done.refs_0_), channel_id=1, source_target_pairs={{0,8},{1,9},{2,10},{3,11},{4,12},{5,13},{6,14},{7,15},{8,0},{9,1},... | collective-permute-start | bytes 786440 | tf_op jit(solution)/shard_map/ppermute | solution.py:250
  30.5 1.9 %collective-permute-start.9 = (bf16[256,512]{1,0:T(8,128)(2,1)S(1)}, bf16[256,512]{1,0:T(8,128)(2,1)S(1)}, u32[]{:S(2)}, u32[]{:S(2)}) collective-permute-start(bf16[256,512]{1,0:T(8,128)(2,1)S(1)} %collective-permute-done.7.refs_2_), channel_id=1, source_target_pairs={{0,8},{1,9},{2,10},{3,11},{4,12},{5,13},{6,14},{7,15},{8,0},{9,1},... | collective-permute-start | bytes 786440 | tf_op jit(solution)/shard_map/ppermute | solution.py:250
  35.4 1.6 %collective-permute-start.10 = (bf16[16,16,512]{2,1,0:T(8,128)(2,1)S(1)}, bf16[16,16,512]{2,1,0:T(8,128)(2,1)S(1)}, u32[]{:S(2)}, u32[]{:S(2)}) collective-permute-start(bf16[16,16,512]{2,1,0:T(8,128)(2,1)S(1)} %get-tuple-element.89), channel_id=1, source_target_pairs={{0,8},{1,9},{2,10},{3,11},{4,12},{5,13},{6,14},{7,15},{8,0},{9,1},... | collective-permute-start | bytes 786440 | tf_op jit(solution)/shard_map/ppermute | solution.py:250
  37.1 5.6 %collective-permute-start.11 = (bf16[8,16,512]{2,1,0:T(8,128)(2,1)S(1)}, bf16[8,16,512]{2,1,0:T(8,128)(2,1)S(1)}, u32[]{:S(2)}, u32[]{:S(2)}) collective-permute-start(bf16[8,16,512]{2,1,0:T(8,128)(2,1)S(1)} %get-tuple-element.91), channel_id=1, source_target_pairs={{0,16},{1,17},{2,18},{3,19},{4,20},{5,21},{6,22},{7,23},{8,24},{9,... | collective-permute-start | bytes 393224 | tf_op jit(solution)/shard_map/ppermute | solution.py:250
  37.8 6.2 %collective-permute-start.15 = (bf16[128,512]{1,0:T(8,128)(2,1)S(1)}, bf16[128,512]{1,0:T(8,128)(2,1)S(1)}, u32[]{:S(2)}, u32[]{:S(2)}) collective-permute-start(bf16[128,512]{1,0:T(8,128)(2,1)S(1)} %get-tuple-element.85.refs_5_), channel_id=1, source_target_pairs={{0,1},{1,0},{2,3},{3,2},{4,5},{5,4},{6,7},{7,6},{8,9},{9,8},{10,11... | collective-permute-start | bytes 393224 | tf_op jit(solution)/shard_map/ppermute | solution.py:250
  39.0 7.3 %collective-permute-start.16 = (bf16[128,512]{1,0:T(8,128)(2,1)S(1)}, bf16[128,512]{1,0:T(8,128)(2,1)S(1)}, u32[]{:S(2)}, u32[]{:S(2)}) collective-permute-start(bf16[128,512]{1,0:T(8,128)(2,1)S(1)} %get-tuple-element.86.refs_6_), channel_id=1, source_target_pairs={{0,2},{1,3},{2,0},{3,1},{4,6},{5,7},{6,4},{7,5},{8,10},{9,11},{10,... | collective-permute-start | bytes 393224 | tf_op jit(solution)/shard_map/ppermute | solution.py:250
  39.6 8.2 %collective-permute-start.17 = (bf16[128,512]{1,0:T(8,128)(2,1)S(1)}, bf16[128,512]{1,0:T(8,128)(2,1)S(1)}, u32[]{:S(2)}, u32[]{:S(2)}) collective-permute-start(bf16[128,512]{1,0:T(8,128)(2,1)S(1)} %get-tuple-element.87.refs_7_), channel_id=1, source_target_pairs={{0,3},{1,2},{2,1},{3,0},{4,7},{5,6},{6,5},{7,4},{8,11},{9,10},{10,... | collective-permute-start | bytes 393224 | tf_op jit(solution)/shard_map/ppermute | solution.py:250
  42.7 5.6 %collective-permute-start.12 = (bf16[2,16,512]{2,1,0:T(8,128)(2,1)S(1)}, bf16[2,16,512]{2,1,0:T(8,128)(2,1)S(1)}, u32[]{:S(2)}, u32[]{:S(2)}) collective-permute-start(bf16[2,16,512]{2,1,0:T(8,128)(2,1)S(1)} %get-tuple-element.93), channel_id=1, source_target_pairs={{0,2},{1,3},{2,0},{3,1},{4,6},{5,7},{6,4},{7,5},{8,10},{9,11},{10,... | collective-permute-start | bytes 98312 | tf_op jit(solution)/shard_map/ppermute | solution.py:250
  43.4 4.9 %collective-permute-start.13 = (bf16[2,16,512]{2,1,0:T(8,128)(2,1)S(1)}, bf16[2,16,512]{2,1,0:T(8,128)(2,1)S(1)}, u32[]{:S(2)}, u32[]{:S(2)}) collective-permute-start(bf16[2,16,512]{2,1,0:T(8,128)(2,1)S(1)} %get-tuple-element.94), channel_id=1, source_target_pairs={{0,1},{1,0},{2,3},{3,2},{4,5},{5,4},{6,7},{7,6},{8,9},{9,8},{10,11... | collective-permute-start | bytes 98312 | tf_op jit(solution)/shard_map/ppermute | solution.py:250
  44.0 4.8 %collective-permute-start.14 = (bf16[2,16,512]{2,1,0:T(8,128)(2,1)S(1)}, bf16[2,16,512]{2,1,0:T(8,128)(2,1)S(1)}, u32[]{:S(2)}, u32[]{:S(2)}) collective-permute-start(bf16[2,16,512]{2,1,0:T(8,128)(2,1)S(1)} %get-tuple-element.95), channel_id=1, source_target_pairs={{0,3},{1,2},{2,1},{3,0},{4,7},{5,6},{6,5},{7,4},{8,11},{9,10},{10,... | collective-permute-start | bytes 98312 | tf_op jit(solution)/shard_map/ppermute | solution.py:250
  48.8 6.8 %collective-permute-start.18 = (f32[1,16,512]{2,1,0:T(8,128)S(1)}, f32[1,16,512]{2,1,0:T(8,128)S(1)}, u32[]{:S(2)}, u32[]{:S(2)}) collective-permute-start(f32[1,16,512]{2,1,0:T(8,128)S(1)} %get-tuple-element.102), channel_id=1, source_target_pairs={{0,4},{1,5},{2,6},{3,7},{4,0},{5,1},{6,2},{7,3},{8,12},{9,13},{10,... | collective-permute-start | bytes 98312 | tf_op jit(solution)/shard_map/ppermute | solution.py:250

commit v19 on v18

--- a/solution.py
+++ b/solution.py
@@ -304,7 +304,7 @@
     slots = 2 * n // devices
     total = devices * slots
     size = total // near
-    sizes = [rows // 2, rows // 4, rows // 8, rows // 8]
+    sizes = [rows // 8] + [rows // 4] * 3 + [rows // 8]
 
     far = [batch * n_item for batch in range(2, n_batch, 2)]
     users = {0: user_vectors}
@@ -340,9 +340,7 @@
 
     fetched = {}
     for parts in [[near - 1], list(range(1, near - 1)), [0]]:
-        close = {mask: users[mask] for mask in [0, *far]}
-        (asked, close), *values = lax.optimization_barrier(((asked, close), *fetch(parts)))
-        users |= close if 0 not in parts else {}
+        asked, *values = lax.optimization_barrier((asked, *fetch(parts)))
         for part, value in zip(parts, values):
             fetched[part] = swap(value, part) if part else value
     fetched = [fetched[part] for part in range(near)]

time: 56.5 us -> 54.9 us (0.972)
  waiting for transfers between devices: 7.89 us -> 6.08 us
    ppermute x19, waiting for transfers between devices: 7.89 us -> 6.08 us  [swap(): lax.ppermute(value, ('batch', 'item'), [(k, k ^ mask) for k in range(devi...]
  transfers between devices with their start and end apart: 19 -> 19, of which waited for: 8 -> 5; matrix products, arithmetic and copies ran while one was open for 1% -> 1% of each run, Pallas kernels for 12% -> 17%
where the time goes in v19:
time: 54.9 us; the launch traced here: 54.7 us
  starting transfers between devices  22.6 us (41%)
  Pallas kernels  12.8 us (23%)
  blocking collectives  11.7 us (21%)
  waiting for transfers between devices  6.08 us (11%)
  between operations  0.82 us (1%)
  other arithmetic  0.7 us (1%)
    ppermute x19, starting transfers between devices, swap(): lax.ppermute(value, ('batch', 'item'), [(k, k ^ mask) for k in range(devi...  22.6 us
    all_to_all x1, blocking collectives, local(): lax.all_to_all(request, ('batch', 'item'), split_axis=0, concat_axis=0, t...  11.7 us
    pallas_call x14, Pallas kernels, call(): pl.pallas_call(kernel, out_shape=[jax.ShapeDtypeStruct(shape, dtype) for...  9.55 us
    ppermute x19, waiting for transfers between devices, swap(): lax.ppermute(value, ('batch', 'item'), [(k, k ^ mask) for k in range(devi...  6.08 us
    pallas_call x1, Pallas kernels, local(): pl.pallas_call(functools.partial(table_kernel, sizes), out_specs=pl.Block...  3.25 us
  transfers between devices with their start and end apart: 19, of which 5 were waited for; matrix products, arithmetic and copies ran while one was open for 1% of the time, Pallas kernels for 17%

profile of v19, /device:TPU:0, one launch (start us, length us, event | category | flops | bytes accessed | tf_op | source)
XLA Modules:
  0.0 54.7 jit_solution(5547028401935446097)
XLA Ops:
  0.6 4.1 %collective-permute-start = (bf16[256,512]{1,0:T(8,128)(2,1)}, bf16[256,512]{1,0:T(8,128)(2,1)S(1)}, u32[]{:S(2)}, u32[]{:S(2)}) collective-permute-start(bf16[256,512]{1,0:T(8,128)(2,1)} %refs_0_), channel_id=1, source_target_pairs={{0,4},{1,5},{2,6},{3,7},{4,0},{5,1},{6,2},{7,3},{8,12},{9,13},{10,... | collective-permute-start | bytes 786440 | tf_op jit(solution)/shard_map/ppermute | solution.py:250
  4.7 1.5 %collective-permute-start.1 = (bf16[256,512]{1,0:T(8,128)(2,1)}, bf16[256,512]{1,0:T(8,128)(2,1)S(1)}, u32[]{:S(2)}, u32[]{:S(2)}) collective-permute-start(bf16[256,512]{1,0:T(8,128)(2,1)} %refs_0_), channel_id=1, source_target_pairs={{0,16},{1,17},{2,18},{3,19},{4,20},{5,21},{6,22},{7,23},{8,24},{9,... | collective-permute-start | bytes 786440 | tf_op jit(solution)/shard_map/ppermute | solution.py:250
  6.2 0.7 %pad_add_fusion.named_ref = s32[2,256]{1,0:T(2,128)S(1)} fusion(s32[1,256]{1,0:T(1,128)} %bitcast.11, s32[1,256]{1,0:T(1,128)} %bitcast.12), kind=kLoop, calls=%fused_computation | loop fusion | flops 512 | bytes 4096 | tf_op jit(solution)/shard_map/stack | solution.py:317
  7.4 11.7 %all_to_all.12 = s32[32,1,80]{2,1,0:T(1,128)S(1)} all-to-all(s32[32,1,80]{2,1,0:T(1,128)S(1)} %bitcast.10), channel_id=1, replica_groups=mesh['batch'=4,'item'=8] {'batch','item'}, dimensions={0} | all-to-all | bytes 20480 | tf_op jit(solution)/shard_map/all_to_all | solution.py:320
  19.2 0.5 collective-permute-start.3
  19.7 0.6 %collective-permute-start.7 = (bf16[256,512]{1,0:T(8,128)(2,1)S(1)}, bf16[256,512]{1,0:T(8,128)(2,1)S(1)}, u32[]{:S(2)}, u32[]{:S(2)}) collective-permute-start(bf16[256,512]{1,0:T(8,128)(2,1)S(1)} %collective-permute-done.refs_0_), channel_id=1, source_target_pairs={{0,16},{1,17},{2,18},{3,19},{4,20},{5,21},{6,22},{7,23},{8,24},{9,... | collective-permute-start | bytes 786440 | tf_op jit(solution)/shard_map/ppermute | solution.py:250
  20.3 0.9 %shard_map.69 = bf16[128,512]{1,0:T(8,128)(2,1)S(1)} custom-call(s32[32,80]{1,0:T(8,128)S(1)} %bitcast.6, bf16[4096,512]{1,0:T(8,128)(2,1)S(1)} %copy-done), custom_call_target="tpu_custom_call" | custom-call | flops 536870912 | bytes 1048576 | tf_op jit(solution)/shard_map/pallas_call | solution.py:239
  21.2 0.8 %collective-permute-start.6 = (bf16[128,512]{1,0:T(8,128)(2,1)S(1)}, bf16[128,512]{1,0:T(8,128)(2,1)S(1)}, u32[]{:S(2)}, u32[]{:S(2)}) collective-permute-start(bf16[128,512]{1,0:T(8,128)(2,1)S(1)} %shard_map.69), channel_id=1, source_target_pairs={{0,3},{1,2},{2,1},{3,0},{4,7},{5,6},{6,5},{7,4},{8,11},{9,10},{10,... | collective-permute-start | bytes 393224 | tf_op jit(solution)/shard_map/ppermute | solution.py:250
  22.0 1.6 %shard_map.70 = (bf16[128,512]{1,0:T(8,128)(2,1)S(1)}, bf16[128,512]{1,0:T(8,128)(2,1)S(1)}) custom-call(s32[32,80]{1,0:T(8,128)S(1)} %bitcast.7, bf16[4096,512]{1,0:T(8,128)(2,1)S(1)} %copy-done), custom_call_target="tpu_custom_call" | custom-call | flops 1073741824 | bytes 1048576 | tf_op jit(solution)/shard_map/pallas_call | solution.py:239
  23.6 1.3 %collective-permute-start.4 = (bf16[128,512]{1,0:T(8,128)(2,1)S(1)}, bf16[128,512]{1,0:T(8,128)(2,1)S(1)}, u32[]{:S(2)}, u32[]{:S(2)}) collective-permute-start(bf16[128,512]{1,0:T(8,128)(2,1)S(1)} %get-tuple-element.61), channel_id=1, source_target_pairs={{0,1},{1,0},{2,3},{3,2},{4,5},{5,4},{6,7},{7,6},{8,9},{9,8},{10,11... | collective-permute-start | bytes 393224 | tf_op jit(solution)/shard_map/ppermute | solution.py:250
  24.9 1.5 %collective-permute-start.5 = (bf16[128,512]{1,0:T(8,128)(2,1)S(1)}, bf16[128,512]{1,0:T(8,128)(2,1)S(1)}, u32[]{:S(2)}, u32[]{:S(2)}) collective-permute-start(bf16[128,512]{1,0:T(8,128)(2,1)S(1)} %get-tuple-element.62), channel_id=1, source_target_pairs={{0,2},{1,3},{2,0},{3,1},{4,6},{5,7},{6,4},{7,5},{8,10},{9,11},{10,... | collective-permute-start | bytes 393224 | tf_op jit(solution)/shard_map/ppermute | solution.py:250
  26.4 0.9 %shard_map.71.refs_0_ = bf16[128,512]{1,0:T(8,128)(2,1)S(1)} custom-call(s32[32,80]{1,0:T(8,128)S(1)} %bitcast.8, bf16[4096,512]{1,0:T(8,128)(2,1)S(1)} %copy-done), custom_call_target="tpu_custom_call" | custom-call | flops 536870912 | bytes 1048576 | tf_op jit(solution)/shard_map/pallas_call | solution.py:239
  27.3 1.0 %shard_map.72 = (s32[512,1]{1,0:T(8,128)S(1)}, bf16[256,512]{1,0:T(8,128)(2,1)S(1)}, bf16[256,512]{1,0:T(8,128)(2,1)S(1)}, bf16[1024,512]{1,0:T(8,128)(2,1)S(1)}, bf16[256,512]{1,0:T(8,128)(2,1)S(1)}) custom-call(s32[32,80]{1,0:T(8,128)S(1)} %bitcast.9, bf16[256,512]{1,0:T(8,128)(2,1)S(1)} %copy-done.2, bf16[256,512]{1,0:T(8,128)(2,1)S(1)} %collective-permute-done.2.refs_1_, ...), custom_call_target="tpu_custom_call" | custom-call | tf_op jit(solution)/shard_map/pallas_call | solution.py:239
  28.4 0.5 collective-permute-start.9
  28.9 1.2 %collective-permute-done.4.refs_1_ = bf16[128,512]{1,0:T(8,128)(2,1)S(1)} collective-permute-done((bf16[128,512]{1,0:T(8,128)(2,1)S(1)}, bf16[128,512]{1,0:T(8,128)(2,1)S(1)}, u32[]{:S(2)}, u32[]{:S(2)}) %collective-permute-start.4) | collective-permute-done | bytes 131104 | tf_op jit(solution)/shard_map/ppermute | solution.py:250
  30.2 0.5 shard_map.73
  30.7 0.7 %shard_map.74 = (bf16[1024,512]{1,0:T(8,128)(2,1)S(1)}, bf16[256,512]{1,0:T(8,128)(2,1)S(1)}) custom-call(s32[512,1]{1,0:T(8,128)S(1)} %get-tuple-element.70.place_ref, bf16[256,512]{1,0:T(8,128)(2,1)S(1)} %collective-permute-done.refs_0_, bf16[256,512]{1,0:T(8,128)(2,1)S(1)} %collective-permute-done.8.refs_1_, ...), custom_call_target="tpu_custom_call" | custom-call | tf_op jit(solution)/shard_map/pallas_call | solution.py:239
  31.4 1.7 %shard_map.75 = (bf16[128,512]{1,0:T(8,128)(2,1)S(1)}, bf16[128,512]{1,0:T(8,128)(2,1)S(1)}, bf16[128,512]{1,0:T(8,128)(2,1)S(1)}, bf16[128,512]{1,0:T(8,128)(2,1)S(1)}) custom-call(f32[512,512]{1,0:T(8,128)S(1)} %get-tuple-element.64.hidden_ref, f32[512,1]{1,0:T(8,128)S(1)} %get-tuple-element.65.rscale_ref, ...), custom_call_target="tpu_custom_call" | custom-call | flops 2147483648 | bytes 1048576 | tf_op jit(solution)/shard_map/pallas_call | solution.py:239
  33.1 0.5 shard_map.76
  33.8 1.5 %collective-permute-done.10.refs_1_ = bf16[16,16,512]{2,1,0:T(8,128)(2,1)S(1)} collective-permute-done((bf16[16,16,512]{2,1,0:T(8,128)(2,1)S(1)}, bf16[16,16,512]{2,1,0:T(8,128)(2,1)S(1)}, u32[]{:S(2)}, u32[]{:S(2)}) %collective-permute-start.10) | collective-permute-done | bytes 262176 | tf_op jit(solution)/shard_map/ppermute | solution.py:250
  35.4 1.5 %collective-permute-start.11 = (bf16[8,16,512]{2,1,0:T(8,128)(2,1)S(1)}, bf16[8,16,512]{2,1,0:T(8,128)(2,1)S(1)}, u32[]{:S(2)}, u32[]{:S(2)}) collective-permute-start(bf16[8,16,512]{2,1,0:T(8,128)(2,1)S(1)} %get-tuple-element.83), channel_id=1, source_target_pairs={{0,16},{1,17},{2,18},{3,19},{4,20},{5,21},{6,22},{7,23},{8,24},{9,... | collective-permute-start | bytes 393224 | tf_op jit(solution)/shard_map/ppermute | solution.py:250
  36.9 0.6 %collective-permute-start.15 = (bf16[128,512]{1,0:T(8,128)(2,1)S(1)}, bf16[128,512]{1,0:T(8,128)(2,1)S(1)}, u32[]{:S(2)}, u32[]{:S(2)}) collective-permute-start(bf16[128,512]{1,0:T(8,128)(2,1)S(1)} %get-tuple-element.77.refs_5_), channel_id=1, source_target_pairs={{0,1},{1,0},{2,3},{3,2},{4,5},{5,4},{6,7},{7,6},{8,9},{9,8},{10,11... | collective-permute-start | bytes 393224 | tf_op jit(solution)/shard_map/ppermute | solution.py:250
  37.5 1.2 %collective-permute-start.16 = (bf16[128,512]{1,0:T(8,128)(2,1)S(1)}, bf16[128,512]{1,0:T(8,128)(2,1)S(1)}, u32[]{:S(2)}, u32[]{:S(2)}) collective-permute-start(bf16[128,512]{1,0:T(8,128)(2,1)S(1)} %get-tuple-element.78.refs_6_), channel_id=1, source_target_pairs={{0,2},{1,3},{2,0},{3,1},{4,6},{5,7},{6,4},{7,5},{8,10},{9,11},{10,... | collective-permute-start | bytes 393224 | tf_op jit(solution)/shard_map/ppermute | solution.py:250
  38.7 1.7 %collective-permute-start.17 = (bf16[128,512]{1,0:T(8,128)(2,1)S(1)}, bf16[128,512]{1,0:T(8,128)(2,1)S(1)}, u32[]{:S(2)}, u32[]{:S(2)}) collective-permute-start(bf16[128,512]{1,0:T(8,128)(2,1)S(1)} %get-tuple-element.79.refs_7_), channel_id=1, source_target_pairs={{0,3},{1,2},{2,1},{3,0},{4,7},{5,6},{6,5},{7,4},{8,11},{9,10},{10,... | collective-permute-start | bytes 393224 | tf_op jit(solution)/shard_map/ppermute | solution.py:250
  40.4 0.6 %collective-permute-done.11.refs_1_ = bf16[8,16,512]{2,1,0:T(8,128)(2,1)S(1)} collective-permute-done((bf16[8,16,512]{2,1,0:T(8,128)(2,1)S(1)}, bf16[8,16,512]{2,1,0:T(8,128)(2,1)S(1)}, u32[]{:S(2)}, u32[]{:S(2)}) %collective-permute-start.11) | collective-permute-done | bytes 131104 | tf_op jit(solution)/shard_map/ppermute | solution.py:250
  41.0 1.3 %collective-permute-start.12 = (bf16[2,16,512]{2,1,0:T(8,128)(2,1)S(1)}, bf16[2,16,512]{2,1,0:T(8,128)(2,1)S(1)}, u32[]{:S(2)}, u32[]{:S(2)}) collective-permute-start(bf16[2,16,512]{2,1,0:T(8,128)(2,1)S(1)} %get-tuple-element.85), channel_id=1, source_target_pairs={{0,2},{1,3},{2,0},{3,1},{4,6},{5,7},{6,4},{7,5},{8,10},{9,11},{10,... | collective-permute-start | bytes 98312 | tf_op jit(solution)/shard_map/ppermute | solution.py:250
  42.3 0.7 %collective-permute-start.13 = (bf16[2,16,512]{2,1,0:T(8,128)(2,1)S(1)}, bf16[2,16,512]{2,1,0:T(8,128)(2,1)S(1)}, u32[]{:S(2)}, u32[]{:S(2)}) collective-permute-start(bf16[2,16,512]{2,1,0:T(8,128)(2,1)S(1)} %get-tuple-element.86), channel_id=1, source_target_pairs={{0,1},{1,0},{2,3},{3,2},{4,5},{5,4},{6,7},{7,6},{8,9},{9,8},{10,11... | collective-permute-start | bytes 98312 | tf_op jit(solution)/shard_map/ppermute | solution.py:250
  43.0 1.6 %collective-permute-start.14 = (bf16[2,16,512]{2,1,0:T(8,128)(2,1)S(1)}, bf16[2,16,512]{2,1,0:T(8,128)(2,1)S(1)}, u32[]{:S(2)}, u32[]{:S(2)}) collective-permute-start(bf16[2,16,512]{2,1,0:T(8,128)(2,1)S(1)} %get-tuple-element.87), channel_id=1, source_target_pairs={{0,3},{1,2},{2,1},{3,0},{4,7},{5,6},{6,5},{7,4},{8,11},{9,10},{10,... | collective-permute-start | bytes 98312 | tf_op jit(solution)/shard_map/ppermute | solution.py:250
  44.6 2.3 %collective-permute-done.17.refs_3_ = bf16[128,512]{1,0:T(8,128)(2,1)S(1)} collective-permute-done((bf16[128,512]{1,0:T(8,128)(2,1)S(1)}, bf16[128,512]{1,0:T(8,128)(2,1)S(1)}, u32[]{:S(2)}, u32[]{:S(2)}) %collective-permute-start.17) | collective-permute-done | bytes 131104 | tf_op jit(solution)/shard_map/ppermute | solution.py:250
  47.8 3.0 %collective-permute-start.18 = (f32[1,16,512]{2,1,0:T(8,128)S(1)}, f32[1,16,512]{2,1,0:T(8,128)S(1)}, u32[]{:S(2)}, u32[]{:S(2)}) collective-permute-start(f32[1,16,512]{2,1,0:T(8,128)S(1)} %get-tuple-element.94), channel_id=1, source_target_pairs={{0,4},{1,5},{2,6},{3,7},{4,0},{5,1},{6,2},{7,3},{8,12},{9,13},{10,... | collective-permute-start | bytes 98312 | tf_op jit(solution)/shard_map/ppermute | solution.py:250
  50.8 3.2 %shard_map.80 = bf16[4096,512]{1,0:T(8,128)(2,1)} custom-call(bf16[256,512]{1,0:T(8,128)(2,1)S(1)} %get-tuple-element.58.low_hot_ref, bf16[256,512]{1,0:T(8,128)(2,1)S(1)} %get-tuple-element.59.block_ref, bf16[512,512]{1,0:T(8,128)(2,1)S(1)} %shard_map.79.drow_ref), custom_call_target="tpu_custom_call" | custom-call | flops 2147483648 | bytes 4194304 | tf_op jit(solution)/shard_map/pallas_call | solution.py:391
  54.1 0.6 %shard_map.82 = f32[16,512]{1,0:T(8,128)} custom-call(f32[1,16,512]{2,1,0:T(8,128)S(1)} %get-tuple-element.96.refs_0_, f32[1,16,512]{2,1,0:T(8,128)S(1)} %collective-permute-done.18.refs_1_), custom_call_target="tpu_custom_call" | custom-call | bytes 1048576 | tf_op jit(solution)/shard_map/pallas_call | solution.py:239
  (29 shorter events, 1.7 us)
Async XLA Ops:
  0.6 18.4 %collective-permute-start = (bf16[256,512]{1,0:T(8,128)(2,1)}, bf16[256,512]{1,0:T(8,128)(2,1)S(1)}, u32[]{:S(2)}, u32[]{:S(2)}) collective-permute-start(bf16[256,512]{1,0:T(8,128)(2,1)} %refs_0_), channel_id=1, source_target_pairs={{0,4},{1,5},{2,6},{3,7},{4,0},{5,1},{6,2},{7,3},{8,12},{9,13},{10,... | collective-permute-start | bytes 786440 | tf_op jit(solution)/shard_map/ppermute | solution.py:250
  4.7 14.4 %collective-permute-start.1 = (bf16[256,512]{1,0:T(8,128)(2,1)}, bf16[256,512]{1,0:T(8,128)(2,1)S(1)}, u32[]{:S(2)}, u32[]{:S(2)}) collective-permute-start(bf16[256,512]{1,0:T(8,128)(2,1)} %refs_0_), channel_id=1, source_target_pairs={{0,16},{1,17},{2,18},{3,19},{4,20},{5,21},{6,22},{7,23},{8,24},{9,... | collective-permute-start | bytes 786440 | tf_op jit(solution)/shard_map/ppermute | solution.py:250
  6.9 12.2 %copy-start.2 = (bf16[256,512]{1,0:T(8,128)(2,1)S(1)}, bf16[256,512]{1,0:T(8,128)(2,1)}, u32[]{:S(2)}) copy-start(bf16[256,512]{1,0:T(8,128)(2,1)} %refs_0_) | copy-start | bytes 786436
  6.9 13.3 %copy-start = (bf16[4096,512]{1,0:T(8,128)(2,1)S(1)}, bf16[4096,512]{1,0:T(8,128)(2,1)}, u32[]{:S(2)}) copy-start(bf16[4096,512]{1,0:T(8,128)(2,1)} %table_ref.5) | copy-start | bytes 12582916
  19.1 5.8 %collective-permute-start.2 = (bf16[256,512]{1,0:T(8,128)(2,1)S(1)}, bf16[256,512]{1,0:T(8,128)(2,1)S(1)}, u32[]{:S(2)}, u32[]{:S(2)}) collective-permute-start(bf16[256,512]{1,0:T(8,128)(2,1)S(1)} %copy-done.2), channel_id=1, source_target_pairs={{0,8},{1,9},{2,10},{3,11},{4,12},{5,13},{6,14},{7,15},{8,0},{9,1},... | collective-permute-start | bytes 786440 | tf_op jit(solution)/shard_map/ppermute | solution.py:250
  19.2 8.1 %collective-permute-start.3 = (bf16[256,512]{1,0:T(8,128)(2,1)S(1)}, bf16[256,512]{1,0:T(8,128)(2,1)S(1)}, u32[]{:S(2)}, u32[]{:S(2)}) collective-permute-start(bf16[256,512]{1,0:T(8,128)(2,1)S(1)} %collective-permute-done.1.refs_2_), channel_id=1, source_target_pairs={{0,8},{1,9},{2,10},{3,11},{4,12},{5,13},{6,14},{7,15},{8,0},{9,1},... | collective-permute-start | bytes 786440 | tf_op jit(solution)/shard_map/ppermute | solution.py:250
  19.7 8.7 %collective-permute-start.7 = (bf16[256,512]{1,0:T(8,128)(2,1)S(1)}, bf16[256,512]{1,0:T(8,128)(2,1)S(1)}, u32[]{:S(2)}, u32[]{:S(2)}) collective-permute-start(bf16[256,512]{1,0:T(8,128)(2,1)S(1)} %collective-permute-done.refs_0_), channel_id=1, source_target_pairs={{0,16},{1,17},{2,18},{3,19},{4,20},{5,21},{6,22},{7,23},{8,24},{9,... | collective-permute-start | bytes 786440 | tf_op jit(solution)/shard_map/ppermute | solution.py:250
  21.2 9.0 %copy-start.1 = (bf16[512,512]{1,0:T(8,128)(2,1)S(1)}, bf16[512,512]{1,0:T(8,128)(2,1)}, u32[]{:S(2)}) copy-start(bf16[512,512]{1,0:T(8,128)(2,1)} %weight_ref.3) | copy-start | bytes 1572868
  21.2 7.7 %collective-permute-start.6 = (bf16[128,512]{1,0:T(8,128)(2,1)S(1)}, bf16[128,512]{1,0:T(8,128)(2,1)S(1)}, u32[]{:S(2)}, u32[]{:S(2)}) collective-permute-start(bf16[128,512]{1,0:T(8,128)(2,1)S(1)} %shard_map.69), channel_id=1, source_target_pairs={{0,3},{1,2},{2,1},{3,0},{4,7},{5,6},{6,5},{7,4},{8,11},{9,10},{10,... | collective-permute-start | bytes 393224 | tf_op jit(solution)/shard_map/ppermute | solution.py:250
  23.6 6.6 %collective-permute-start.4 = (bf16[128,512]{1,0:T(8,128)(2,1)S(1)}, bf16[128,512]{1,0:T(8,128)(2,1)S(1)}, u32[]{:S(2)}, u32[]{:S(2)}) collective-permute-start(bf16[128,512]{1,0:T(8,128)(2,1)S(1)} %get-tuple-element.61), channel_id=1, source_target_pairs={{0,1},{1,0},{2,3},{3,2},{4,5},{5,4},{6,7},{7,6},{8,9},{9,8},{10,11... | collective-permute-start | bytes 393224 | tf_op jit(solution)/shard_map/ppermute | solution.py:250
  24.9 5.2 %collective-permute-start.5 = (bf16[128,512]{1,0:T(8,128)(2,1)S(1)}, bf16[128,512]{1,0:T(8,128)(2,1)S(1)}, u32[]{:S(2)}, u32[]{:S(2)}) collective-permute-start(bf16[128,512]{1,0:T(8,128)(2,1)S(1)} %get-tuple-element.62), channel_id=1, source_target_pairs={{0,2},{1,3},{2,0},{3,1},{4,6},{5,7},{6,4},{7,5},{8,10},{9,11},{10,... | collective-permute-start | bytes 393224 | tf_op jit(solution)/shard_map/ppermute | solution.py:250
  28.3 2.3 %collective-permute-start.8 = (bf16[256,512]{1,0:T(8,128)(2,1)S(1)}, bf16[256,512]{1,0:T(8,128)(2,1)S(1)}, u32[]{:S(2)}, u32[]{:S(2)}) collective-permute-start(bf16[256,512]{1,0:T(8,128)(2,1)S(1)} %collective-permute-done.refs_0_), channel_id=1, source_target_pairs={{0,8},{1,9},{2,10},{3,11},{4,12},{5,13},{6,14},{7,15},{8,0},{9,1},... | collective-permute-start | bytes 786440 | tf_op jit(solution)/shard_map/ppermute | solution.py:250
  28.4 2.3 %collective-permute-start.9 = (bf16[256,512]{1,0:T(8,128)(2,1)S(1)}, bf16[256,512]{1,0:T(8,128)(2,1)S(1)}, u32[]{:S(2)}, u32[]{:S(2)}) collective-permute-start(bf16[256,512]{1,0:T(8,128)(2,1)S(1)} %collective-permute-done.7.refs_2_), channel_id=1, source_target_pairs={{0,8},{1,9},{2,10},{3,11},{4,12},{5,13},{6,14},{7,15},{8,0},{9,1},... | collective-permute-start | bytes 786440 | tf_op jit(solution)/shard_map/ppermute | solution.py:250
  33.7 1.6 %collective-permute-start.10 = (bf16[16,16,512]{2,1,0:T(8,128)(2,1)S(1)}, bf16[16,16,512]{2,1,0:T(8,128)(2,1)S(1)}, u32[]{:S(2)}, u32[]{:S(2)}) collective-permute-start(bf16[16,16,512]{2,1,0:T(8,128)(2,1)S(1)} %get-tuple-element.81), channel_id=1, source_target_pairs={{0,8},{1,9},{2,10},{3,11},{4,12},{5,13},{6,14},{7,15},{8,0},{9,1},... | collective-permute-start | bytes 786440 | tf_op jit(solution)/shard_map/ppermute | solution.py:250
  35.4 5.6 %collective-permute-start.11 = (bf16[8,16,512]{2,1,0:T(8,128)(2,1)S(1)}, bf16[8,16,512]{2,1,0:T(8,128)(2,1)S(1)}, u32[]{:S(2)}, u32[]{:S(2)}) collective-permute-start(bf16[8,16,512]{2,1,0:T(8,128)(2,1)S(1)} %get-tuple-element.83), channel_id=1, source_target_pairs={{0,16},{1,17},{2,18},{3,19},{4,20},{5,21},{6,22},{7,23},{8,24},{9,... | collective-permute-start | bytes 393224 | tf_op jit(solution)/shard_map/ppermute | solution.py:250
  36.9 6.1 %collective-permute-start.15 = (bf16[128,512]{1,0:T(8,128)(2,1)S(1)}, bf16[128,512]{1,0:T(8,128)(2,1)S(1)}, u32[]{:S(2)}, u32[]{:S(2)}) collective-permute-start(bf16[128,512]{1,0:T(8,128)(2,1)S(1)} %get-tuple-element.77.refs_5_), channel_id=1, source_target_pairs={{0,1},{1,0},{2,3},{3,2},{4,5},{5,4},{6,7},{7,6},{8,9},{9,8},{10,11... | collective-permute-start | bytes 393224 | tf_op jit(solution)/shard_map/ppermute | solution.py:250
  37.5 7.1 %collective-permute-start.16 = (bf16[128,512]{1,0:T(8,128)(2,1)S(1)}, bf16[128,512]{1,0:T(8,128)(2,1)S(1)}, u32[]{:S(2)}, u32[]{:S(2)}) collective-permute-start(bf16[128,512]{1,0:T(8,128)(2,1)S(1)} %get-tuple-element.78.refs_6_), channel_id=1, source_target_pairs={{0,2},{1,3},{2,0},{3,1},{4,6},{5,7},{6,4},{7,5},{8,10},{9,11},{10,... | collective-permute-start | bytes 393224 | tf_op jit(solution)/shard_map/ppermute | solution.py:250
  38.7 8.2 %collective-permute-start.17 = (bf16[128,512]{1,0:T(8,128)(2,1)S(1)}, bf16[128,512]{1,0:T(8,128)(2,1)S(1)}, u32[]{:S(2)}, u32[]{:S(2)}) collective-permute-start(bf16[128,512]{1,0:T(8,128)(2,1)S(1)} %get-tuple-element.79.refs_7_), channel_id=1, source_target_pairs={{0,3},{1,2},{2,1},{3,0},{4,7},{5,6},{6,5},{7,4},{8,11},{9,10},{10,... | collective-permute-start | bytes 393224 | tf_op jit(solution)/shard_map/ppermute | solution.py:250
  41.0 6.3 %collective-permute-start.12 = (bf16[2,16,512]{2,1,0:T(8,128)(2,1)S(1)}, bf16[2,16,512]{2,1,0:T(8,128)(2,1)S(1)}, u32[]{:S(2)}, u32[]{:S(2)}) collective-permute-start(bf16[2,16,512]{2,1,0:T(8,128)(2,1)S(1)} %get-tuple-element.85), channel_id=1, source_target_pairs={{0,2},{1,3},{2,0},{3,1},{4,6},{5,7},{6,4},{7,5},{8,10},{9,11},{10,... | collective-permute-start | bytes 98312 | tf_op jit(solution)/shard_map/ppermute | solution.py:250
  42.3 5.1 %collective-permute-start.13 = (bf16[2,16,512]{2,1,0:T(8,128)(2,1)S(1)}, bf16[2,16,512]{2,1,0:T(8,128)(2,1)S(1)}, u32[]{:S(2)}, u32[]{:S(2)}) collective-permute-start(bf16[2,16,512]{2,1,0:T(8,128)(2,1)S(1)} %get-tuple-element.86), channel_id=1, source_target_pairs={{0,1},{1,0},{2,3},{3,2},{4,5},{5,4},{6,7},{7,6},{8,9},{9,8},{10,11... | collective-permute-start | bytes 98312 | tf_op jit(solution)/shard_map/ppermute | solution.py:250
  43.0 4.8 %collective-permute-start.14 = (bf16[2,16,512]{2,1,0:T(8,128)(2,1)S(1)}, bf16[2,16,512]{2,1,0:T(8,128)(2,1)S(1)}, u32[]{:S(2)}, u32[]{:S(2)}) collective-permute-start(bf16[2,16,512]{2,1,0:T(8,128)(2,1)S(1)} %get-tuple-element.87), channel_id=1, source_target_pairs={{0,3},{1,2},{2,1},{3,0},{4,7},{5,6},{6,5},{7,4},{8,11},{9,10},{10,... | collective-permute-start | bytes 98312 | tf_op jit(solution)/shard_map/ppermute | solution.py:250
  47.8 6.3 %collective-permute-start.18 = (f32[1,16,512]{2,1,0:T(8,128)S(1)}, f32[1,16,512]{2,1,0:T(8,128)S(1)}, u32[]{:S(2)}, u32[]{:S(2)}) collective-permute-start(f32[1,16,512]{2,1,0:T(8,128)S(1)} %get-tuple-element.94), channel_id=1, source_target_pairs={{0,4},{1,5},{2,6},{3,7},{4,0},{5,1},{6,2},{7,3},{8,12},{9,13},{10,... | collective-permute-start | bytes 98312 | tf_op jit(solution)/shard_map/ppermute | solution.py:250

commit v20 on v19

--- a/solution.py
+++ b/solution.py
@@ -40,12 +40,16 @@
     return value.bit_length() - 1
 
 
-def request_kernel(near, named_ref, request_ref):
-    devices, lanes = request_ref.shape
+def request_kernel(near, named_ref, stay_ref, cross_ref):
+    half, lanes = stay_ref.shape
+    devices, n_half = 2 * half, lax.axis_size("item") // 2
+    mine = lax.axis_index("item") & n_half
     slots = lanes // (1 + near)
     n = named_ref.shape[1]
     owner, row = named_ref[0:1], named_ref[1:2]
-    device = iota((devices, n), 0)
+    spot = iota((devices, n), 0)
+    place = spot & (half - 1)
+    device = (((place >> log2(n_half)) << log2(2 * n_half)) | (place & (n_half - 1)) | mine) ^ ((spot >> log2(half)) * n_half)
     named = owner == device
     count = dot(hot(named), hot(iota((n, n), 0) <= iota((n, n), 1)))
     rank = jnp.sum(jnp.where(named, count, 0.0), axis=0, keepdims=True).astype(i32) - 1
@@ -56,13 +60,25 @@
         here = (owner ^ mask) == device
         high = dot(jnp.where(here, high, 0.0).astype(bf16), in_slot, 1, 1)
         low = dot(jnp.where(here, low, 0.0).astype(bf16), in_slot, 1, 1)
-        request_ref[:, k * slots : (k + 1) * slots] = (high * 256.0 + low).astype(i32) - 1
+        value = (high * 256.0 + low).astype(i32) - 1
+        stay_ref[:, k * slots : (k + 1) * slots] = value[:half]
+        cross_ref[:, k * slots : (k + 1) * slots] = value[half:]
+
+
+def pair_kernel(stay_ref, came_ref, pair_ref):
+    for k in range(pair_ref.shape[0]):
+        pair_ref[k, 0:1] = stay_ref[k : k + 1]
+        pair_ref[k, 1:2] = came_ref[k : k + 1]
 
 
 def asker_of(spot, part, near, n_batch, slots):
     batch = (spot >> log2(slots)) & (n_batch - 1)
     level = spot >> log2(slots * n_batch)
-    return position() ^ (batch * lax.axis_size("item") + level * near + part)
+    n_item = lax.axis_size("item")
+    asker = position() ^ (batch * n_item + level * near + part)
+    low = asker & (n_item // 2 - 1)
+    cross = ((asker ^ lax.axis_index("item")) >> log2(n_item // 2)) & 1
+    return ((((asker >> log2(n_item)) << log2(n_item // 2)) | low) << 1) | cross
 
 
 def slot_column(asked, part, near, n_batch):
@@ -307,27 +323,24 @@
     sizes = [rows // 8] + [rows // 4] * 3 + [rows // 8]
 
     far = [batch * n_item for batch in range(2, n_batch, 2)]
-    users = {0: user_vectors}
-    for mask in [near << k for k in range(log2(levels))] + far:
-        users[mask] = swap(user_vectors, mask)
-
-    (request,) = call(
+    steps = [near << k for k in range(log2(levels))]
+    users = {mask: swap(user_vectors, mask) for mask in far}
+    stay, cross = call(
         functools.partial(request_kernel, near),
-        [((devices, (1 + near) * slots), i32)],
+        [((devices // 2, (1 + near) * slots), i32)] * 2,
         jnp.stack([item_owner.reshape(n), item_row]),
         flops=1 << 34,
     )
-    asked = lax.all_to_all(request, ("batch", "item"), split_axis=0, concat_axis=0, tiled=True)
-    early = list(users)
-    asked, *values = lax.optimization_barrier((asked, *users.values()))
-    users = dict(zip(early, values))
-
-    for level in range(1, levels):
-        if near * level not in users:
-            top = 1 << log2(level)
-            users[near * level] = swap(users[near * (level - top)], near * top)
-        for mask in far:
-            users[mask + near * level] = swap(users[near * level], mask)
+    came = swap(cross, n_item // 2)
+    came, mine = lax.optimization_barrier((came, user_vectors))
+    users |= {mask: swap(mine, mask) for mask in steps}
+    (pair,) = call(pair_kernel, [((devices // 2, 2, (1 + near) * slots), i32)], stay, came, free=True)
+    halves_of = [[k for k in range(devices) if bool(k & (n_item // 2)) == side] for side in (False, True)]
+    asked = lax.all_to_all(
+        pair, ("batch", "item"), split_axis=0, concat_axis=0, axis_index_groups=halves_of, tiled=True
+    ).reshape(devices, (1 + near) * slots)
+    asked, mine, *values = lax.optimization_barrier((asked, mine, *[users[mask] for mask in far]))
+    users |= dict(zip(far, values)) | {0: mine}
 
     def fetch(parts):
         return call(
@@ -341,8 +354,17 @@
     fetched = {}
     for parts in [[near - 1], list(range(1, near - 1)), [0]]:
         asked, *values = lax.optimization_barrier((asked, *fetch(parts)))
+        if 1 in parts:
+            _, across = lax.optimization_barrier((values, [users[mask] for mask in steps]))
+            users |= dict(zip(steps, across))
         for part, value in zip(parts, values):
             fetched[part] = swap(value, part) if part else value
+    for level in range(1, levels):
+        if near * level not in users:
+            top = 1 << log2(level)
+            users[near * level] = swap(users[near * (level - top)], near * top)
+        for mask in far:
+            users[mask + near * level] = swap(users[near * level], mask)
     fetched = [fetched[part] for part in range(near)]
 
     for mask in [0, *far]:

time: 54.9 us -> 59.8 us (1.089)
  waiting for transfers between devices: 6.08 us -> 11.5 us
    ppermute x19 -> x20, waiting for transfers between devices: 6.08 us -> 11.5 us  [swap(): lax.ppermute(value, ('batch', 'item'), [(k, k ^ mask) for k in range(devi...]
    ppermute x19 -> x20, starting transfers between devices: 22.6 us -> 22.1 us  [swap(): lax.ppermute(value, ('batch', 'item'), [(k, k ^ mask) for k in range(devi...]
    pallas_call x14 -> x15, Pallas kernels: 9.55 us -> 9.59 us  [call(): pl.pallas_call(kernel, out_shape=[jax.ShapeDtypeStruct(shape, dtype) for...]
  transfers between devices with their start and end apart: 19 -> 20, of which waited for: 5 -> 10; matrix products, arithmetic and copies ran while one was open for 1% -> 1% of each run, Pallas kernels for 17% -> 15%
where the time goes in v20:
time: 59.8 us; the launch traced here: 59.6 us
  starting transfers between devices  22.1 us (37%)
  Pallas kernels  12.8 us (21%)
  blocking collectives  11.6 us (19%)
  waiting for transfers between devices  11.5 us (19%)
  between operations  0.82 us (1%)
  other arithmetic  0.7 us (1%)
    ppermute x20, starting transfers between devices, swap(): lax.ppermute(value, ('batch', 'item'), [(k, k ^ mask) for k in range(devi...  22.1 us
    all_to_all x1, blocking collectives, local(): lax.all_to_all(pair, ('batch', 'item'), split_axis=0, concat_axis=0, axis...  11.6 us
    ppermute x20, waiting for transfers between devices, swap(): lax.ppermute(value, ('batch', 'item'), [(k, k ^ mask) for k in range(devi...  11.5 us
    pallas_call x15, Pallas kernels, call(): pl.pallas_call(kernel, out_shape=[jax.ShapeDtypeStruct(shape, dtype) for...  9.59 us
    pallas_call x1, Pallas kernels, local(): pl.pallas_call(functools.partial(table_kernel, sizes), out_specs=pl.Block...  3.25 us
  transfers between devices with their start and end apart: 20, of which 10 were waited for; matrix products, arithmetic and copies ran while one was open for 1% of the time, Pallas kernels for 15%

profile of v20, /device:TPU:0, one launch (start us, length us, event | category | flops | bytes accessed | tf_op | source)
XLA Modules:
  0.0 59.6 jit_solution(4835205262199768392)
XLA Ops:
  0.6 3.0 %collective-permute-start.1 = (bf16[256,512]{1,0:T(8,128)(2,1)}, bf16[256,512]{1,0:T(8,128)(2,1)S(1)}, u32[]{:S(2)}, u32[]{:S(2)}) collective-permute-start(bf16[256,512]{1,0:T(8,128)(2,1)} %refs_0_), channel_id=1, source_target_pairs={{0,16},{1,17},{2,18},{3,19},{4,20},{5,21},{6,22},{7,23},{8,24},{9,... | collective-permute-start | bytes 786440 | tf_op jit(solution)/shard_map/ppermute | solution.py:266
  3.6 0.7 %pad_add_fusion.named_ref = s32[2,256]{1,0:T(2,128)S(1)} fusion(s32[1,256]{1,0:T(1,128)} %bitcast.7, s32[1,256]{1,0:T(1,128)} %bitcast.8), kind=kLoop, calls=%fused_computation | loop fusion | flops 512 | bytes 4096 | tf_op jit(solution)/shard_map/stack | solution.py:331
  4.8 2.7 %collective-permute-start = (s32[16,80]{1,0:T(8,128)S(1)}, s32[16,80]{1,0:T(8,128)S(1)}, u32[]{:S(2)}, u32[]{:S(2)}) collective-permute-start(s32[16,80]{1,0:T(8,128)S(1)} %get-tuple-element.55), channel_id=1, source_target_pairs={{0,4},{1,5},{2,6},{3,7},{4,0},{5,1},{6,2},{7,3},{8,12},{9,13},{10,... | collective-permute-start | bytes 15368 | tf_op jit(solution)/shard_map/ppermute | solution.py:266
  7.4 2.0 %collective-permute-done.came_ref = s32[16,80]{1,0:T(8,128)S(1)} collective-permute-done((s32[16,80]{1,0:T(8,128)S(1)}, s32[16,80]{1,0:T(8,128)S(1)}, u32[]{:S(2)}, u32[]{:S(2)}) %collective-permute-start) | collective-permute-done | bytes 5152 | tf_op jit(solution)/shard_map/ppermute | solution.py:266
  9.4 2.6 %collective-permute-start.7 = (bf16[256,512]{1,0:T(8,128)(2,1)S(1)}, bf16[256,512]{1,0:T(8,128)(2,1)S(1)}, u32[]{:S(2)}, u32[]{:S(2)}) collective-permute-start(bf16[256,512]{1,0:T(8,128)(2,1)S(1)} %copy-done.2), channel_id=1, source_target_pairs={{0,4},{1,5},{2,6},{3,7},{4,0},{5,1},{6,2},{7,3},{8,12},{9,13},{10,... | collective-permute-start | bytes 786440 | tf_op jit(solution)/shard_map/ppermute | solution.py:266
  12.0 11.6 %all_to_all.5 = s32[16,2,80]{2,1,0:T(2,128)S(1)} all-to-all(s32[16,2,80]{2,1,0:T(2,128)S(1)} %shard_map.69), channel_id=1, replica_groups={{0,1,2,3,8,9,10,11,16,17,18,19,24,25,26,27},{4,5,6,7,12,13,14,15,20,21,..., dimensions={0} | all-to-all | bytes 20480 | tf_op jit(solution)/shard_map/all_to_all | solution.py:339
  23.7 0.9 %shard_map.70 = bf16[128,512]{1,0:T(8,128)(2,1)S(1)} custom-call(s32[32,80]{1,0:T(8,128)S(1)} %bitcast.3, bf16[4096,512]{1,0:T(8,128)(2,1)S(1)} %copy-done), custom_call_target="tpu_custom_call" | custom-call | flops 536870912 | bytes 1048576 | tf_op jit(solution)/shard_map/pallas_call | solution.py:255
  24.6 1.6 %shard_map.71 = (bf16[128,512]{1,0:T(8,128)(2,1)S(1)}, bf16[128,512]{1,0:T(8,128)(2,1)S(1)}) custom-call(s32[32,80]{1,0:T(8,128)S(1)} %bitcast.4, bf16[4096,512]{1,0:T(8,128)(2,1)S(1)} %copy-done), custom_call_target="tpu_custom_call" | custom-call | flops 1073741824 | bytes 1048576 | tf_op jit(solution)/shard_map/pallas_call | solution.py:255
  26.2 0.5 collective-permute-start.3
  26.7 1.4 %collective-permute-start.8 = (bf16[256,512]{1,0:T(8,128)(2,1)S(1)}, bf16[256,512]{1,0:T(8,128)(2,1)S(1)}, u32[]{:S(2)}, u32[]{:S(2)}) collective-permute-start(bf16[256,512]{1,0:T(8,128)(2,1)S(1)} %collective-permute-done.7.refs_0_), channel_id=1, source_target_pairs={{0,16},{1,17},{2,18},{3,19},{4,20},{5,21},{6,22},{7,23},{8,24},{9,... | collective-permute-start | bytes 786440 | tf_op jit(solution)/shard_map/ppermute | solution.py:266
  28.2 0.5 collective-permute-start.4
  28.7 2.9 %collective-permute-start.5 = (bf16[128,512]{1,0:T(8,128)(2,1)S(1)}, bf16[128,512]{1,0:T(8,128)(2,1)S(1)}, u32[]{:S(2)}, u32[]{:S(2)}) collective-permute-start(bf16[128,512]{1,0:T(8,128)(2,1)S(1)} %get-tuple-element.70), channel_id=1, source_target_pairs={{0,2},{1,3},{2,0},{3,1},{4,6},{5,7},{6,4},{7,5},{8,10},{9,11},{10,... | collective-permute-start | bytes 393224 | tf_op jit(solution)/shard_map/ppermute | solution.py:266
  31.7 0.9 %shard_map.72.refs_0_ = bf16[128,512]{1,0:T(8,128)(2,1)S(1)} custom-call(s32[32,80]{1,0:T(8,128)S(1)} %bitcast.5, bf16[4096,512]{1,0:T(8,128)(2,1)S(1)} %copy-done), custom_call_target="tpu_custom_call" | custom-call | flops 536870912 | bytes 1048576 | tf_op jit(solution)/shard_map/pallas_call | solution.py:255
  32.6 1.0 %shard_map.73 = (s32[512,1]{1,0:T(8,128)S(1)}, bf16[256,512]{1,0:T(8,128)(2,1)S(1)}, bf16[256,512]{1,0:T(8,128)(2,1)S(1)}, bf16[1024,512]{1,0:T(8,128)(2,1)S(1)}, bf16[256,512]{1,0:T(8,128)(2,1)S(1)}) custom-call(s32[32,80]{1,0:T(8,128)S(1)} %bitcast.6, bf16[256,512]{1,0:T(8,128)(2,1)S(1)} %copy-done.2, bf16[256,512]{1,0:T(8,128)(2,1)S(1)} %collective-permute-done.2.refs_1_, ...), custom_call_target="tpu_custom_call" | custom-call | tf_op jit(solution)/shard_map/pallas_call | solution.py:255
  33.6 1.4 %collective-permute-done.8.refs_2_ = bf16[256,512]{1,0:T(8,128)(2,1)S(1)} collective-permute-done((bf16[256,512]{1,0:T(8,128)(2,1)S(1)}, bf16[256,512]{1,0:T(8,128)(2,1)S(1)}, u32[]{:S(2)}, u32[]{:S(2)}) %collective-permute-start.8) | collective-permute-done | bytes 262176 | tf_op jit(solution)/shard_map/ppermute | solution.py:266
  35.0 0.5 collective-permute-start.10
  36.2 1.2 %collective-permute-done.5.refs_2_ = bf16[128,512]{1,0:T(8,128)(2,1)S(1)} collective-permute-done((bf16[128,512]{1,0:T(8,128)(2,1)S(1)}, bf16[128,512]{1,0:T(8,128)(2,1)S(1)}, u32[]{:S(2)}, u32[]{:S(2)}) %collective-permute-start.5) | collective-permute-done | bytes 131104 | tf_op jit(solution)/shard_map/ppermute | solution.py:266
  37.5 0.5 shard_map.74
  38.0 0.7 %shard_map.75 = (bf16[1024,512]{1,0:T(8,128)(2,1)S(1)}, bf16[256,512]{1,0:T(8,128)(2,1)S(1)}) custom-call(s32[512,1]{1,0:T(8,128)S(1)} %get-tuple-element.78.place_ref, bf16[256,512]{1,0:T(8,128)(2,1)S(1)} %collective-permute-done.7.refs_0_, bf16[256,512]{1,0:T(8,128)(2,1)S(1)} %collective-permute-done.9.refs_1_, ...), custom_call_target="tpu_custom_call" | custom-call | tf_op jit(solution)/shard_map/pallas_call | solution.py:255
  38.7 1.7 %shard_map.76 = (bf16[128,512]{1,0:T(8,128)(2,1)S(1)}, bf16[128,512]{1,0:T(8,128)(2,1)S(1)}, bf16[128,512]{1,0:T(8,128)(2,1)S(1)}, bf16[128,512]{1,0:T(8,128)(2,1)S(1)}) custom-call(f32[512,512]{1,0:T(8,128)S(1)} %get-tuple-element.72.hidden_ref, f32[512,1]{1,0:T(8,128)S(1)} %get-tuple-element.73.rscale_ref, ...), custom_call_target="tpu_custom_call" | custom-call | flops 2147483648 | bytes 1048576 | tf_op jit(solution)/shard_map/pallas_call | solution.py:255
  40.4 0.5 shard_map.77
  41.1 1.5 %collective-permute-done.11.refs_1_ = bf16[16,16,512]{2,1,0:T(8,128)(2,1)S(1)} collective-permute-done((bf16[16,16,512]{2,1,0:T(8,128)(2,1)S(1)}, bf16[16,16,512]{2,1,0:T(8,128)(2,1)S(1)}, u32[]{:S(2)}, u32[]{:S(2)}) %collective-permute-start.11) | collective-permute-done | bytes 262176 | tf_op jit(solution)/shard_map/ppermute | solution.py:266
  42.7 0.6 %collective-permute-start.12 = (bf16[8,16,512]{2,1,0:T(8,128)(2,1)S(1)}, bf16[8,16,512]{2,1,0:T(8,128)(2,1)S(1)}, u32[]{:S(2)}, u32[]{:S(2)}) collective-permute-start(bf16[8,16,512]{2,1,0:T(8,128)(2,1)S(1)} %get-tuple-element.91), channel_id=1, source_target_pairs={{0,16},{1,17},{2,18},{3,19},{4,20},{5,21},{6,22},{7,23},{8,24},{9,... | collective-permute-start | bytes 393224 | tf_op jit(solution)/shard_map/ppermute | solution.py:266
  43.3 0.5 collective-permute-start.16
  44.1 2.7 %collective-permute-start.18 = (bf16[128,512]{1,0:T(8,128)(2,1)S(1)}, bf16[128,512]{1,0:T(8,128)(2,1)S(1)}, u32[]{:S(2)}, u32[]{:S(2)}) collective-permute-start(bf16[128,512]{1,0:T(8,128)(2,1)S(1)} %get-tuple-element.87.refs_7_), channel_id=1, source_target_pairs={{0,3},{1,2},{2,1},{3,0},{4,7},{5,6},{6,5},{7,4},{8,11},{9,10},{10,... | collective-permute-start | bytes 393224 | tf_op jit(solution)/shard_map/ppermute | solution.py:266
  46.8 1.5 %collective-permute-done.12.refs_1_ = bf16[8,16,512]{2,1,0:T(8,128)(2,1)S(1)} collective-permute-done((bf16[8,16,512]{2,1,0:T(8,128)(2,1)S(1)}, bf16[8,16,512]{2,1,0:T(8,128)(2,1)S(1)}, u32[]{:S(2)}, u32[]{:S(2)}) %collective-permute-start.12) | collective-permute-done | bytes 131104 | tf_op jit(solution)/shard_map/ppermute | solution.py:266
  48.4 0.8 %collective-permute-start.14 = (bf16[2,16,512]{2,1,0:T(8,128)(2,1)S(1)}, bf16[2,16,512]{2,1,0:T(8,128)(2,1)S(1)}, u32[]{:S(2)}, u32[]{:S(2)}) collective-permute-start(bf16[2,16,512]{2,1,0:T(8,128)(2,1)S(1)} %get-tuple-element.94), channel_id=1, source_target_pairs={{0,1},{1,0},{2,3},{3,2},{4,5},{5,4},{6,7},{7,6},{8,9},{9,8},{10,11... | collective-permute-start | bytes 98312 | tf_op jit(solution)/shard_map/ppermute | solution.py:266
  49.2 2.7 %collective-permute-start.15 = (bf16[2,16,512]{2,1,0:T(8,128)(2,1)S(1)}, bf16[2,16,512]{2,1,0:T(8,128)(2,1)S(1)}, u32[]{:S(2)}, u32[]{:S(2)}) collective-permute-start(bf16[2,16,512]{2,1,0:T(8,128)(2,1)S(1)} %get-tuple-element.95), channel_id=1, source_target_pairs={{0,3},{1,2},{2,1},{3,0},{4,7},{5,6},{6,5},{7,4},{8,11},{9,10},{10,... | collective-permute-start | bytes 98312 | tf_op jit(solution)/shard_map/ppermute | solution.py:266
  51.9 1.4 %collective-permute-done.18.refs_3_ = bf16[128,512]{1,0:T(8,128)(2,1)S(1)} collective-permute-done((bf16[128,512]{1,0:T(8,128)(2,1)S(1)}, bf16[128,512]{1,0:T(8,128)(2,1)S(1)}, u32[]{:S(2)}, u32[]{:S(2)}) %collective-permute-start.18) | collective-permute-done | bytes 131104 | tf_op jit(solution)/shard_map/ppermute | solution.py:266
  54.1 3.2 %shard_map.81 = bf16[4096,512]{1,0:T(8,128)(2,1)} custom-call(bf16[256,512]{1,0:T(8,128)(2,1)S(1)} %get-tuple-element.66.low_hot_ref, bf16[256,512]{1,0:T(8,128)(2,1)S(1)} %get-tuple-element.67.block_ref, bf16[512,512]{1,0:T(8,128)(2,1)S(1)} %shard_map.80.drow_ref), custom_call_target="tpu_custom_call" | custom-call | flops 2147483648 | bytes 4194304 | tf_op jit(solution)/shard_map/pallas_call | solution.py:413
  57.4 1.5 %collective-permute-done.19.refs_1_ = f32[1,16,512]{2,1,0:T(8,128)S(1)} collective-permute-done((f32[1,16,512]{2,1,0:T(8,128)S(1)}, f32[1,16,512]{2,1,0:T(8,128)S(1)}, u32[]{:S(2)}, u32[]{:S(2)}) %collective-permute-start.19) | collective-permute-done | bytes 32800 | tf_op jit(solution)/shard_map/ppermute | solution.py:266
  58.9 0.6 %shard_map.83 = f32[16,512]{1,0:T(8,128)} custom-call(f32[1,16,512]{2,1,0:T(8,128)S(1)} %get-tuple-element.104.refs_0_, f32[1,16,512]{2,1,0:T(8,128)S(1)} %collective-permute-done.19.refs_1_), custom_call_target="tpu_custom_call" | custom-call | bytes 1048576 | tf_op jit(solution)/shard_map/pallas_call | solution.py:255
  (32 shorter events, 2.5 us)
Async XLA Ops:
  0.6 23.0 %collective-permute-start.1 = (bf16[256,512]{1,0:T(8,128)(2,1)}, bf16[256,512]{1,0:T(8,128)(2,1)S(1)}, u32[]{:S(2)}, u32[]{:S(2)}) collective-permute-start(bf16[256,512]{1,0:T(8,128)(2,1)} %refs_0_), channel_id=1, source_target_pairs={{0,16},{1,17},{2,18},{3,19},{4,20},{5,21},{6,22},{7,23},{8,24},{9,... | collective-permute-start | bytes 786440 | tf_op jit(solution)/shard_map/ppermute | solution.py:266
  4.3 5.1 %copy-start.2 = (bf16[256,512]{1,0:T(8,128)(2,1)S(1)}, bf16[256,512]{1,0:T(8,128)(2,1)}, u32[]{:S(2)}) copy-start(bf16[256,512]{1,0:T(8,128)(2,1)} %refs_0_) | copy-start | bytes 786436
  4.3 19.4 %copy-start = (bf16[4096,512]{1,0:T(8,128)(2,1)S(1)}, bf16[4096,512]{1,0:T(8,128)(2,1)}, u32[]{:S(2)}) copy-start(bf16[4096,512]{1,0:T(8,128)(2,1)} %table_ref.5) | copy-start | bytes 12582916
  4.8 4.6 %collective-permute-start = (s32[16,80]{1,0:T(8,128)S(1)}, s32[16,80]{1,0:T(8,128)S(1)}, u32[]{:S(2)}, u32[]{:S(2)}) collective-permute-start(s32[16,80]{1,0:T(8,128)S(1)} %get-tuple-element.55), channel_id=1, source_target_pairs={{0,4},{1,5},{2,6},{3,7},{4,0},{5,1},{6,2},{7,3},{8,12},{9,13},{10,... | collective-permute-start | bytes 15368 | tf_op jit(solution)/shard_map/ppermute | solution.py:266
  9.4 17.3 %collective-permute-start.7 = (bf16[256,512]{1,0:T(8,128)(2,1)S(1)}, bf16[256,512]{1,0:T(8,128)(2,1)S(1)}, u32[]{:S(2)}, u32[]{:S(2)}) collective-permute-start(bf16[256,512]{1,0:T(8,128)(2,1)S(1)} %copy-done.2), channel_id=1, source_target_pairs={{0,4},{1,5},{2,6},{3,7},{4,0},{5,1},{6,2},{7,3},{8,12},{9,13},{10,... | collective-permute-start | bytes 786440 | tf_op jit(solution)/shard_map/ppermute | solution.py:266
  23.6 5.1 %collective-permute-start.2 = (bf16[256,512]{1,0:T(8,128)(2,1)S(1)}, bf16[256,512]{1,0:T(8,128)(2,1)S(1)}, u32[]{:S(2)}, u32[]{:S(2)}) collective-permute-start(bf16[256,512]{1,0:T(8,128)(2,1)S(1)} %copy-done.2), channel_id=1, source_target_pairs={{0,8},{1,9},{2,10},{3,11},{4,12},{5,13},{6,14},{7,15},{8,0},{9,1},... | collective-permute-start | bytes 786440 | tf_op jit(solution)/shard_map/ppermute | solution.py:266
  24.6 12.8 %copy-start.1 = (bf16[512,512]{1,0:T(8,128)(2,1)S(1)}, bf16[512,512]{1,0:T(8,128)(2,1)}, u32[]{:S(2)}) copy-start(bf16[512,512]{1,0:T(8,128)(2,1)} %weight_ref.3) | copy-start | bytes 1572868
  26.2 6.4 %collective-permute-start.3 = (bf16[256,512]{1,0:T(8,128)(2,1)S(1)}, bf16[256,512]{1,0:T(8,128)(2,1)S(1)}, u32[]{:S(2)}, u32[]{:S(2)}) collective-permute-start(bf16[256,512]{1,0:T(8,128)(2,1)S(1)} %collective-permute-done.1.refs_2_), channel_id=1, source_target_pairs={{0,8},{1,9},{2,10},{3,11},{4,12},{5,13},{6,14},{7,15},{8,0},{9,1},... | collective-permute-start | bytes 786440 | tf_op jit(solution)/shard_map/ppermute | solution.py:266
  26.7 8.3 %collective-permute-start.8 = (bf16[256,512]{1,0:T(8,128)(2,1)S(1)}, bf16[256,512]{1,0:T(8,128)(2,1)S(1)}, u32[]{:S(2)}, u32[]{:S(2)}) collective-permute-start(bf16[256,512]{1,0:T(8,128)(2,1)S(1)} %collective-permute-done.7.refs_0_), channel_id=1, source_target_pairs={{0,16},{1,17},{2,18},{3,19},{4,20},{5,21},{6,22},{7,23},{8,24},{9,... | collective-permute-start | bytes 786440 | tf_op jit(solution)/shard_map/ppermute | solution.py:266
  28.2 8.0 %collective-permute-start.4 = (bf16[128,512]{1,0:T(8,128)(2,1)S(1)}, bf16[128,512]{1,0:T(8,128)(2,1)S(1)}, u32[]{:S(2)}, u32[]{:S(2)}) collective-permute-start(bf16[128,512]{1,0:T(8,128)(2,1)S(1)} %get-tuple-element.69), channel_id=1, source_target_pairs={{0,1},{1,0},{2,3},{3,2},{4,5},{5,4},{6,7},{7,6},{8,9},{9,8},{10,11... | collective-permute-start | bytes 393224 | tf_op jit(solution)/shard_map/ppermute | solution.py:266
  28.7 7.3 %collective-permute-start.6 = (bf16[128,512]{1,0:T(8,128)(2,1)S(1)}, bf16[128,512]{1,0:T(8,128)(2,1)S(1)}, u32[]{:S(2)}, u32[]{:S(2)}) collective-permute-start(bf16[128,512]{1,0:T(8,128)(2,1)S(1)} %shard_map.70), channel_id=1, source_target_pairs={{0,3},{1,2},{2,1},{3,0},{4,7},{5,6},{6,5},{7,4},{8,11},{9,10},{10,... | collective-permute-start | bytes 393224 | tf_op jit(solution)/shard_map/ppermute | solution.py:266
  28.7 8.7 %collective-permute-start.5 = (bf16[128,512]{1,0:T(8,128)(2,1)S(1)}, bf16[128,512]{1,0:T(8,128)(2,1)S(1)}, u32[]{:S(2)}, u32[]{:S(2)}) collective-permute-start(bf16[128,512]{1,0:T(8,128)(2,1)S(1)} %get-tuple-element.70), channel_id=1, source_target_pairs={{0,2},{1,3},{2,0},{3,1},{4,6},{5,7},{6,4},{7,5},{8,10},{9,11},{10,... | collective-permute-start | bytes 393224 | tf_op jit(solution)/shard_map/ppermute | solution.py:266
  35.0 3.0 %collective-permute-start.9 = (bf16[256,512]{1,0:T(8,128)(2,1)S(1)}, bf16[256,512]{1,0:T(8,128)(2,1)S(1)}, u32[]{:S(2)}, u32[]{:S(2)}) collective-permute-start(bf16[256,512]{1,0:T(8,128)(2,1)S(1)} %collective-permute-done.7.refs_0_), channel_id=1, source_target_pairs={{0,8},{1,9},{2,10},{3,11},{4,12},{5,13},{6,14},{7,15},{8,0},{9,1},... | collective-permute-start | bytes 786440 | tf_op jit(solution)/shard_map/ppermute | solution.py:266
  35.0 3.0 %collective-permute-start.10 = (bf16[256,512]{1,0:T(8,128)(2,1)S(1)}, bf16[256,512]{1,0:T(8,128)(2,1)S(1)}, u32[]{:S(2)}, u32[]{:S(2)}) collective-permute-start(bf16[256,512]{1,0:T(8,128)(2,1)S(1)} %collective-permute-done.8.refs_2_), channel_id=1, source_target_pairs={{0,8},{1,9},{2,10},{3,11},{4,12},{5,13},{6,14},{7,15},{8,0},{9,1},... | collective-permute-start | bytes 786440 | tf_op jit(solution)/shard_map/ppermute | solution.py:266
  41.0 1.6 %collective-permute-start.11 = (bf16[16,16,512]{2,1,0:T(8,128)(2,1)S(1)}, bf16[16,16,512]{2,1,0:T(8,128)(2,1)S(1)}, u32[]{:S(2)}, u32[]{:S(2)}) collective-permute-start(bf16[16,16,512]{2,1,0:T(8,128)(2,1)S(1)} %get-tuple-element.89), channel_id=1, source_target_pairs={{0,8},{1,9},{2,10},{3,11},{4,12},{5,13},{6,14},{7,15},{8,0},{9,1},... | collective-permute-start | bytes 786440 | tf_op jit(solution)/shard_map/ppermute | solution.py:266
  42.7 5.6 %collective-permute-start.12 = (bf16[8,16,512]{2,1,0:T(8,128)(2,1)S(1)}, bf16[8,16,512]{2,1,0:T(8,128)(2,1)S(1)}, u32[]{:S(2)}, u32[]{:S(2)}) collective-permute-start(bf16[8,16,512]{2,1,0:T(8,128)(2,1)S(1)} %get-tuple-element.91), channel_id=1, source_target_pairs={{0,16},{1,17},{2,18},{3,19},{4,20},{5,21},{6,22},{7,23},{8,24},{9,... | collective-permute-start | bytes 393224 | tf_op jit(solution)/shard_map/ppermute | solution.py:266
  43.3 5.9 %collective-permute-start.16 = (bf16[128,512]{1,0:T(8,128)(2,1)S(1)}, bf16[128,512]{1,0:T(8,128)(2,1)S(1)}, u32[]{:S(2)}, u32[]{:S(2)}) collective-permute-start(bf16[128,512]{1,0:T(8,128)(2,1)S(1)} %get-tuple-element.85.refs_5_), channel_id=1, source_target_pairs={{0,1},{1,0},{2,3},{3,2},{4,5},{5,4},{6,7},{7,6},{8,9},{9,8},{10,11... | collective-permute-start | bytes 393224 | tf_op jit(solution)/shard_map/ppermute | solution.py:266
  43.8 8.1 %collective-permute-start.17 = (bf16[128,512]{1,0:T(8,128)(2,1)S(1)}, bf16[128,512]{1,0:T(8,128)(2,1)S(1)}, u32[]{:S(2)}, u32[]{:S(2)}) collective-permute-start(bf16[128,512]{1,0:T(8,128)(2,1)S(1)} %get-tuple-element.86.refs_6_), channel_id=1, source_target_pairs={{0,2},{1,3},{2,0},{3,1},{4,6},{5,7},{6,4},{7,5},{8,10},{9,11},{10,... | collective-permute-start | bytes 393224 | tf_op jit(solution)/shard_map/ppermute | solution.py:266
  44.1 9.2 %collective-permute-start.18 = (bf16[128,512]{1,0:T(8,128)(2,1)S(1)}, bf16[128,512]{1,0:T(8,128)(2,1)S(1)}, u32[]{:S(2)}, u32[]{:S(2)}) collective-permute-start(bf16[128,512]{1,0:T(8,128)(2,1)S(1)} %get-tuple-element.87.refs_7_), channel_id=1, source_target_pairs={{0,3},{1,2},{2,1},{3,0},{4,7},{5,6},{6,5},{7,4},{8,11},{9,10},{10,... | collective-permute-start | bytes 393224 | tf_op jit(solution)/shard_map/ppermute | solution.py:266
  48.3 5.5 %collective-permute-start.13 = (bf16[2,16,512]{2,1,0:T(8,128)(2,1)S(1)}, bf16[2,16,512]{2,1,0:T(8,128)(2,1)S(1)}, u32[]{:S(2)}, u32[]{:S(2)}) collective-permute-start(bf16[2,16,512]{2,1,0:T(8,128)(2,1)S(1)} %get-tuple-element.93), channel_id=1, source_target_pairs={{0,2},{1,3},{2,0},{3,1},{4,6},{5,7},{6,4},{7,5},{8,10},{9,11},{10,... | collective-permute-start | bytes 98312 | tf_op jit(solution)/shard_map/ppermute | solution.py:266
  48.4 5.4 %collective-permute-start.14 = (bf16[2,16,512]{2,1,0:T(8,128)(2,1)S(1)}, bf16[2,16,512]{2,1,0:T(8,128)(2,1)S(1)}, u32[]{:S(2)}, u32[]{:S(2)}) collective-permute-start(bf16[2,16,512]{2,1,0:T(8,128)(2,1)S(1)} %get-tuple-element.94), channel_id=1, source_target_pairs={{0,1},{1,0},{2,3},{3,2},{4,5},{5,4},{6,7},{7,6},{8,9},{9,8},{10,11... | collective-permute-start | bytes 98312 | tf_op jit(solution)/shard_map/ppermute | solution.py:266
  49.2 4.8 %collective-permute-start.15 = (bf16[2,16,512]{2,1,0:T(8,128)(2,1)S(1)}, bf16[2,16,512]{2,1,0:T(8,128)(2,1)S(1)}, u32[]{:S(2)}, u32[]{:S(2)}) collective-permute-start(bf16[2,16,512]{2,1,0:T(8,128)(2,1)S(1)} %get-tuple-element.95), channel_id=1, source_target_pairs={{0,3},{1,2},{2,1},{3,0},{4,7},{5,6},{6,5},{7,4},{8,11},{9,10},{10,... | collective-permute-start | bytes 98312 | tf_op jit(solution)/shard_map/ppermute | solution.py:266
  54.1 4.9 %collective-permute-start.19 = (f32[1,16,512]{2,1,0:T(8,128)S(1)}, f32[1,16,512]{2,1,0:T(8,128)S(1)}, u32[]{:S(2)}, u32[]{:S(2)}) collective-permute-start(f32[1,16,512]{2,1,0:T(8,128)S(1)} %get-tuple-element.102), channel_id=1, source_target_pairs={{0,4},{1,5},{2,6},{3,7},{4,0},{5,1},{6,2},{7,3},{8,12},{9,13},{10,... | collective-permute-start | bytes 98312 | tf_op jit(solution)/shard_map/ppermute | solution.py:266

commit v21 on v19

--- a/solution.py
+++ b/solution.py
@@ -170,7 +170,8 @@
         dvec = (cweight * score_scale) * (mixed * (1.0 / sums) - own)
         inner = jnp.sum(hidden * dvec, axis=1, keepdims=True)
         dhidden = (rscale * root * (dvec - hidden * (rscale * rscale * inner * (1.0 / width)))).astype(bf16)
-        for part, ref in enumerate(outs):
+        for spot, ref in enumerate(outs):
+            part = -spot % len(outs)
             ref[pl.ds(level * size, size)] = dhidden[part * size : (part + 1) * size]
 
 
@@ -339,7 +340,7 @@
         )
 
     fetched = {}
-    for parts in [[near - 1], list(range(1, near - 1)), [0]]:
+    for parts in [list(reversed(range(1, near))), [0]]:
         asked, *values = lax.optimization_barrier((asked, *fetch(parts)))
         for part, value in zip(parts, values):
             fetched[part] = swap(value, part) if part else value
@@ -385,6 +386,7 @@
         flops=1 << 31,
         mib=40,
     )
+    dhidden = [dhidden[-part % near] for part in range(near)]
     incoming = [swap(dhidden[part], part) for part in range(1, near)]
     (drow,) = call(row_kernel, [((total, width), bf16)], tower_weight, dhidden[0], *incoming, free=True)
     terms, drow = reduce_scatter(fetched, dhidden, drow)

time: 54.9 us -> 56.2 us (1.024)
  waiting for transfers between devices: 6.08 us -> 7.82 us
    ppermute x19, waiting for transfers between devices: 6.08 us -> 7.82 us  [swap(): lax.ppermute(value, ('batch', 'item'), [(k, k ^ mask) for k in range(devi...]
    pallas_call x14 -> x13, Pallas kernels: 9.55 us -> 9.19 us  [call(): pl.pallas_call(kernel, out_shape=[jax.ShapeDtypeStruct(shape, dtype) for...]
  transfers between devices with their start and end apart: 19 -> 19, of which waited for: 5 -> 7; matrix products, arithmetic and copies ran while one was open for 1% -> 1% of each run, Pallas kernels for 17% -> 16%
where the time goes in v21:
time: 56.2 us; the launch traced here: 56 us
  starting transfers between devices  22.5 us (40%)
  Pallas kernels  12.4 us (22%)
  blocking collectives  11.7 us (21%)
  waiting for transfers between devices  7.82 us (14%)
  between operations  0.82 us (1%)
  other arithmetic  0.7 us (1%)
    ppermute x19, starting transfers between devices, swap(): lax.ppermute(value, ('batch', 'item'), [(k, k ^ mask) for k in range(devi...  22.5 us
    all_to_all x1, blocking collectives, local(): lax.all_to_all(request, ('batch', 'item'), split_axis=0, concat_axis=0, t...  11.7 us
    pallas_call x13, Pallas kernels, call(): pl.pallas_call(kernel, out_shape=[jax.ShapeDtypeStruct(shape, dtype) for...  9.19 us
    ppermute x19, waiting for transfers between devices, swap(): lax.ppermute(value, ('batch', 'item'), [(k, k ^ mask) for k in range(devi...  7.82 us
    pallas_call x1, Pallas kernels, local(): pl.pallas_call(functools.partial(table_kernel, sizes), out_specs=pl.Block...  3.25 us
  transfers between devices with their start and end apart: 19, of which 7 were waited for; matrix products, arithmetic and copies ran while one was open for 1% of the time, Pallas kernels for 16%

profile of v21, /device:TPU:0, one launch (start us, length us, event | category | flops | bytes accessed | tf_op | source)
XLA Modules:
  0.0 56.0 jit_solution(12886975298345000603)
XLA Ops:
  0.6 4.1 %collective-permute-start = (bf16[256,512]{1,0:T(8,128)(2,1)}, bf16[256,512]{1,0:T(8,128)(2,1)S(1)}, u32[]{:S(2)}, u32[]{:S(2)}) collective-permute-start(bf16[256,512]{1,0:T(8,128)(2,1)} %refs_0_), channel_id=1, source_target_pairs={{0,4},{1,5},{2,6},{3,7},{4,0},{5,1},{6,2},{7,3},{8,12},{9,13},{10,... | collective-permute-start | bytes 786440 | tf_op jit(solution)/shard_map/ppermute | solution.py:251
  4.7 1.5 %collective-permute-start.1 = (bf16[256,512]{1,0:T(8,128)(2,1)}, bf16[256,512]{1,0:T(8,128)(2,1)S(1)}, u32[]{:S(2)}, u32[]{:S(2)}) collective-permute-start(bf16[256,512]{1,0:T(8,128)(2,1)} %refs_0_), channel_id=1, source_target_pairs={{0,16},{1,17},{2,18},{3,19},{4,20},{5,21},{6,22},{7,23},{8,24},{9,... | collective-permute-start | bytes 786440 | tf_op jit(solution)/shard_map/ppermute | solution.py:251
  6.2 0.7 %pad_add_fusion.named_ref = s32[2,256]{1,0:T(2,128)S(1)} fusion(s32[1,256]{1,0:T(1,128)} %bitcast.10, s32[1,256]{1,0:T(1,128)} %bitcast.11), kind=kLoop, calls=%fused_computation | loop fusion | flops 512 | bytes 4096 | tf_op jit(solution)/shard_map/stack | solution.py:318
  7.4 11.7 %all_to_all.12 = s32[32,1,80]{2,1,0:T(1,128)S(1)} all-to-all(s32[32,1,80]{2,1,0:T(1,128)S(1)} %bitcast.9), channel_id=1, replica_groups=mesh['batch'=4,'item'=8] {'batch','item'}, dimensions={0} | all-to-all | bytes 20480 | tf_op jit(solution)/shard_map/all_to_all | solution.py:321
  19.2 0.5 collective-permute-start.3
  19.7 0.6 %collective-permute-start.7 = (bf16[256,512]{1,0:T(8,128)(2,1)S(1)}, bf16[256,512]{1,0:T(8,128)(2,1)S(1)}, u32[]{:S(2)}, u32[]{:S(2)}) collective-permute-start(bf16[256,512]{1,0:T(8,128)(2,1)S(1)} %collective-permute-done.refs_0_), channel_id=1, source_target_pairs={{0,16},{1,17},{2,18},{3,19},{4,20},{5,21},{6,22},{7,23},{8,24},{9,... | collective-permute-start | bytes 786440 | tf_op jit(solution)/shard_map/ppermute | solution.py:251
  20.3 2.1 %shard_map.69 = (bf16[128,512]{1,0:T(8,128)(2,1)S(1)}, bf16[128,512]{1,0:T(8,128)(2,1)S(1)}, bf16[128,512]{1,0:T(8,128)(2,1)S(1)}) custom-call(s32[32,80]{1,0:T(8,128)S(1)} %bitcast.6, bf16[4096,512]{1,0:T(8,128)(2,1)S(1)} %copy-done), custom_call_target="tpu_custom_call" | custom-call | flops 1610612736 | bytes 1048576 | tf_op jit(solution)/shard_map/pallas_call | solution.py:240
  22.4 0.7 %collective-permute-start.4 = (bf16[128,512]{1,0:T(8,128)(2,1)S(1)}, bf16[128,512]{1,0:T(8,128)(2,1)S(1)}, u32[]{:S(2)}, u32[]{:S(2)}) collective-permute-start(bf16[128,512]{1,0:T(8,128)(2,1)S(1)} %get-tuple-element.61), channel_id=1, source_target_pairs={{0,1},{1,0},{2,3},{3,2},{4,5},{5,4},{6,7},{7,6},{8,9},{9,8},{10,11... | collective-permute-start | bytes 393224 | tf_op jit(solution)/shard_map/ppermute | solution.py:251
  23.1 0.6 %collective-permute-start.5 = (bf16[128,512]{1,0:T(8,128)(2,1)S(1)}, bf16[128,512]{1,0:T(8,128)(2,1)S(1)}, u32[]{:S(2)}, u32[]{:S(2)}) collective-permute-start(bf16[128,512]{1,0:T(8,128)(2,1)S(1)} %get-tuple-element.62), channel_id=1, source_target_pairs={{0,2},{1,3},{2,0},{3,1},{4,6},{5,7},{6,4},{7,5},{8,10},{9,11},{10,... | collective-permute-start | bytes 393224 | tf_op jit(solution)/shard_map/ppermute | solution.py:251
  23.8 2.2 %collective-permute-start.6 = (bf16[128,512]{1,0:T(8,128)(2,1)S(1)}, bf16[128,512]{1,0:T(8,128)(2,1)S(1)}, u32[]{:S(2)}, u32[]{:S(2)}) collective-permute-start(bf16[128,512]{1,0:T(8,128)(2,1)S(1)} %get-tuple-element.63), channel_id=1, source_target_pairs={{0,3},{1,2},{2,1},{3,0},{4,7},{5,6},{6,5},{7,4},{8,11},{9,10},{10,... | collective-permute-start | bytes 393224 | tf_op jit(solution)/shard_map/ppermute | solution.py:251
  25.9 0.9 %shard_map.70.refs_0_ = bf16[128,512]{1,0:T(8,128)(2,1)S(1)} custom-call(s32[32,80]{1,0:T(8,128)S(1)} %bitcast.7, bf16[4096,512]{1,0:T(8,128)(2,1)S(1)} %copy-done), custom_call_target="tpu_custom_call" | custom-call | flops 536870912 | bytes 1048576 | tf_op jit(solution)/shard_map/pallas_call | solution.py:240
  26.9 1.0 %shard_map.71 = (s32[512,1]{1,0:T(8,128)S(1)}, bf16[256,512]{1,0:T(8,128)(2,1)S(1)}, bf16[256,512]{1,0:T(8,128)(2,1)S(1)}, bf16[1024,512]{1,0:T(8,128)(2,1)S(1)}, bf16[256,512]{1,0:T(8,128)(2,1)S(1)}) custom-call(s32[32,80]{1,0:T(8,128)S(1)} %bitcast.8, bf16[256,512]{1,0:T(8,128)(2,1)S(1)} %copy-done.2, bf16[256,512]{1,0:T(8,128)(2,1)S(1)} %collective-permute-done.2.refs_1_, ...), custom_call_target="tpu_custom_call" | custom-call | tf_op jit(solution)/shard_map/pallas_call | solution.py:240
  28.0 0.5 collective-permute-start.9
  28.5 1.0 %collective-permute-done.5.refs_2_ = bf16[128,512]{1,0:T(8,128)(2,1)S(1)} collective-permute-done((bf16[128,512]{1,0:T(8,128)(2,1)S(1)}, bf16[128,512]{1,0:T(8,128)(2,1)S(1)}, u32[]{:S(2)}, u32[]{:S(2)}) %collective-permute-start.5) | collective-permute-done | bytes 131104 | tf_op jit(solution)/shard_map/ppermute | solution.py:251
  29.4 2.2 %collective-permute-done.6.refs_3_ = bf16[128,512]{1,0:T(8,128)(2,1)S(1)} collective-permute-done((bf16[128,512]{1,0:T(8,128)(2,1)S(1)}, bf16[128,512]{1,0:T(8,128)(2,1)S(1)}, u32[]{:S(2)}, u32[]{:S(2)}) %collective-permute-start.6) | collective-permute-done | bytes 131104 | tf_op jit(solution)/shard_map/ppermute | solution.py:251
  31.6 0.5 shard_map.72
  32.2 0.7 %shard_map.73 = (bf16[1024,512]{1,0:T(8,128)(2,1)S(1)}, bf16[256,512]{1,0:T(8,128)(2,1)S(1)}) custom-call(s32[512,1]{1,0:T(8,128)S(1)} %get-tuple-element.70.place_ref, bf16[256,512]{1,0:T(8,128)(2,1)S(1)} %collective-permute-done.refs_0_, bf16[256,512]{1,0:T(8,128)(2,1)S(1)} %collective-permute-done.8.refs_1_, ...), custom_call_target="tpu_custom_call" | custom-call | tf_op jit(solution)/shard_map/pallas_call | solution.py:240
  32.9 1.7 %shard_map.74 = (bf16[128,512]{1,0:T(8,128)(2,1)S(1)}, bf16[128,512]{1,0:T(8,128)(2,1)S(1)}, bf16[128,512]{1,0:T(8,128)(2,1)S(1)}, bf16[128,512]{1,0:T(8,128)(2,1)S(1)}) custom-call(f32[512,512]{1,0:T(8,128)S(1)} %get-tuple-element.64.hidden_ref, f32[512,1]{1,0:T(8,128)S(1)} %get-tuple-element.65.rscale_ref, ...), custom_call_target="tpu_custom_call" | custom-call | flops 2147483648 | bytes 1048576 | tf_op jit(solution)/shard_map/pallas_call | solution.py:240
  34.6 0.5 shard_map.75
  35.2 1.5 %collective-permute-done.10.refs_1_ = bf16[16,16,512]{2,1,0:T(8,128)(2,1)S(1)} collective-permute-done((bf16[16,16,512]{2,1,0:T(8,128)(2,1)S(1)}, bf16[16,16,512]{2,1,0:T(8,128)(2,1)S(1)}, u32[]{:S(2)}, u32[]{:S(2)}) %collective-permute-start.10) | collective-permute-done | bytes 262176 | tf_op jit(solution)/shard_map/ppermute | solution.py:251
  36.9 1.5 %collective-permute-start.11 = (bf16[8,16,512]{2,1,0:T(8,128)(2,1)S(1)}, bf16[8,16,512]{2,1,0:T(8,128)(2,1)S(1)}, u32[]{:S(2)}, u32[]{:S(2)}) collective-permute-start(bf16[8,16,512]{2,1,0:T(8,128)(2,1)S(1)} %get-tuple-element.83), channel_id=1, source_target_pairs={{0,16},{1,17},{2,18},{3,19},{4,20},{5,21},{6,22},{7,23},{8,24},{9,... | collective-permute-start | bytes 393224 | tf_op jit(solution)/shard_map/ppermute | solution.py:251
  38.4 0.6 %collective-permute-start.15 = (bf16[128,512]{1,0:T(8,128)(2,1)S(1)}, bf16[128,512]{1,0:T(8,128)(2,1)S(1)}, u32[]{:S(2)}, u32[]{:S(2)}) collective-permute-start(bf16[128,512]{1,0:T(8,128)(2,1)S(1)} %get-tuple-element.77.refs_5_), channel_id=1, source_target_pairs={{0,1},{1,0},{2,3},{3,2},{4,5},{5,4},{6,7},{7,6},{8,9},{9,8},{10,11... | collective-permute-start | bytes 393224 | tf_op jit(solution)/shard_map/ppermute | solution.py:251
  39.0 0.6 %collective-permute-start.16 = (bf16[128,512]{1,0:T(8,128)(2,1)S(1)}, bf16[128,512]{1,0:T(8,128)(2,1)S(1)}, u32[]{:S(2)}, u32[]{:S(2)}) collective-permute-start(bf16[128,512]{1,0:T(8,128)(2,1)S(1)} %get-tuple-element.78.refs_6_), channel_id=1, source_target_pairs={{0,2},{1,3},{2,0},{3,1},{4,6},{5,7},{6,4},{7,5},{8,10},{9,11},{10,... | collective-permute-start | bytes 393224 | tf_op jit(solution)/shard_map/ppermute | solution.py:251
  39.6 2.3 %collective-permute-start.17 = (bf16[128,512]{1,0:T(8,128)(2,1)S(1)}, bf16[128,512]{1,0:T(8,128)(2,1)S(1)}, u32[]{:S(2)}, u32[]{:S(2)}) collective-permute-start(bf16[128,512]{1,0:T(8,128)(2,1)S(1)} %get-tuple-element.79.refs_7_), channel_id=1, source_target_pairs={{0,3},{1,2},{2,1},{3,0},{4,7},{5,6},{6,5},{7,4},{8,11},{9,10},{10,... | collective-permute-start | bytes 393224 | tf_op jit(solution)/shard_map/ppermute | solution.py:251
  41.9 0.6 %collective-permute-done.11.refs_1_ = bf16[8,16,512]{2,1,0:T(8,128)(2,1)S(1)} collective-permute-done((bf16[8,16,512]{2,1,0:T(8,128)(2,1)S(1)}, bf16[8,16,512]{2,1,0:T(8,128)(2,1)S(1)}, u32[]{:S(2)}, u32[]{:S(2)}) %collective-permute-start.11) | collective-permute-done | bytes 131104 | tf_op jit(solution)/shard_map/ppermute | solution.py:251
  42.5 0.7 %collective-permute-start.12 = (bf16[2,16,512]{2,1,0:T(8,128)(2,1)S(1)}, bf16[2,16,512]{2,1,0:T(8,128)(2,1)S(1)}, u32[]{:S(2)}, u32[]{:S(2)}) collective-permute-start(bf16[2,16,512]{2,1,0:T(8,128)(2,1)S(1)} %get-tuple-element.85), channel_id=1, source_target_pairs={{0,2},{1,3},{2,0},{3,1},{4,6},{5,7},{6,4},{7,5},{8,10},{9,11},{10,... | collective-permute-start | bytes 98312 | tf_op jit(solution)/shard_map/ppermute | solution.py:251
  43.2 0.8 %collective-permute-start.13 = (bf16[2,16,512]{2,1,0:T(8,128)(2,1)S(1)}, bf16[2,16,512]{2,1,0:T(8,128)(2,1)S(1)}, u32[]{:S(2)}, u32[]{:S(2)}) collective-permute-start(bf16[2,16,512]{2,1,0:T(8,128)(2,1)S(1)} %get-tuple-element.86), channel_id=1, source_target_pairs={{0,1},{1,0},{2,3},{3,2},{4,5},{5,4},{6,7},{7,6},{8,9},{9,8},{10,11... | collective-permute-start | bytes 98312 | tf_op jit(solution)/shard_map/ppermute | solution.py:251
  44.0 2.1 %collective-permute-start.14 = (bf16[2,16,512]{2,1,0:T(8,128)(2,1)S(1)}, bf16[2,16,512]{2,1,0:T(8,128)(2,1)S(1)}, u32[]{:S(2)}, u32[]{:S(2)}) collective-permute-start(bf16[2,16,512]{2,1,0:T(8,128)(2,1)S(1)} %get-tuple-element.87), channel_id=1, source_target_pairs={{0,3},{1,2},{2,1},{3,0},{4,7},{5,6},{6,5},{7,4},{8,11},{9,10},{10,... | collective-permute-start | bytes 98312 | tf_op jit(solution)/shard_map/ppermute | solution.py:251
  46.1 2.3 %collective-permute-done.17.refs_3_ = bf16[128,512]{1,0:T(8,128)(2,1)S(1)} collective-permute-done((bf16[128,512]{1,0:T(8,128)(2,1)S(1)}, bf16[128,512]{1,0:T(8,128)(2,1)S(1)}, u32[]{:S(2)}, u32[]{:S(2)}) %collective-permute-start.17) | collective-permute-done | bytes 131104 | tf_op jit(solution)/shard_map/ppermute | solution.py:251
  49.1 3.1 %collective-permute-start.18 = (f32[1,16,512]{2,1,0:T(8,128)S(1)}, f32[1,16,512]{2,1,0:T(8,128)S(1)}, u32[]{:S(2)}, u32[]{:S(2)}) collective-permute-start(f32[1,16,512]{2,1,0:T(8,128)S(1)} %get-tuple-element.94), channel_id=1, source_target_pairs={{0,4},{1,5},{2,6},{3,7},{4,0},{5,1},{6,2},{7,3},{8,12},{9,13},{10,... | collective-permute-start | bytes 98312 | tf_op jit(solution)/shard_map/ppermute | solution.py:251
  52.2 3.2 %shard_map.79 = bf16[4096,512]{1,0:T(8,128)(2,1)} custom-call(bf16[256,512]{1,0:T(8,128)(2,1)S(1)} %get-tuple-element.58.low_hot_ref, bf16[256,512]{1,0:T(8,128)(2,1)S(1)} %get-tuple-element.59.block_ref, bf16[512,512]{1,0:T(8,128)(2,1)S(1)} %shard_map.78.drow_ref), custom_call_target="tpu_custom_call" | custom-call | flops 2147483648 | bytes 4194304 | tf_op jit(solution)/shard_map/pallas_call | solution.py:393
  55.4 0.6 %shard_map.81 = f32[16,512]{1,0:T(8,128)} custom-call(f32[1,16,512]{2,1,0:T(8,128)S(1)} %get-tuple-element.96.refs_0_, f32[1,16,512]{2,1,0:T(8,128)S(1)} %collective-permute-done.18.refs_1_), custom_call_target="tpu_custom_call" | custom-call | bytes 1048576 | tf_op jit(solution)/shard_map/pallas_call | solution.py:240
  (28 shorter events, 1.5 us)
Async XLA Ops:
  0.6 18.4 %collective-permute-start = (bf16[256,512]{1,0:T(8,128)(2,1)}, bf16[256,512]{1,0:T(8,128)(2,1)S(1)}, u32[]{:S(2)}, u32[]{:S(2)}) collective-permute-start(bf16[256,512]{1,0:T(8,128)(2,1)} %refs_0_), channel_id=1, source_target_pairs={{0,4},{1,5},{2,6},{3,7},{4,0},{5,1},{6,2},{7,3},{8,12},{9,13},{10,... | collective-permute-start | bytes 786440 | tf_op jit(solution)/shard_map/ppermute | solution.py:251
  4.7 14.4 %collective-permute-start.1 = (bf16[256,512]{1,0:T(8,128)(2,1)}, bf16[256,512]{1,0:T(8,128)(2,1)S(1)}, u32[]{:S(2)}, u32[]{:S(2)}) collective-permute-start(bf16[256,512]{1,0:T(8,128)(2,1)} %refs_0_), channel_id=1, source_target_pairs={{0,16},{1,17},{2,18},{3,19},{4,20},{5,21},{6,22},{7,23},{8,24},{9,... | collective-permute-start | bytes 786440 | tf_op jit(solution)/shard_map/ppermute | solution.py:251
  6.9 12.2 %copy-start.2 = (bf16[256,512]{1,0:T(8,128)(2,1)S(1)}, bf16[256,512]{1,0:T(8,128)(2,1)}, u32[]{:S(2)}) copy-start(bf16[256,512]{1,0:T(8,128)(2,1)} %refs_0_) | copy-start | bytes 786436
  6.9 13.3 %copy-start = (bf16[4096,512]{1,0:T(8,128)(2,1)S(1)}, bf16[4096,512]{1,0:T(8,128)(2,1)}, u32[]{:S(2)}) copy-start(bf16[4096,512]{1,0:T(8,128)(2,1)} %table_ref.3) | copy-start | bytes 12582916
  19.1 4.7 %collective-permute-start.2 = (bf16[256,512]{1,0:T(8,128)(2,1)S(1)}, bf16[256,512]{1,0:T(8,128)(2,1)S(1)}, u32[]{:S(2)}, u32[]{:S(2)}) collective-permute-start(bf16[256,512]{1,0:T(8,128)(2,1)S(1)} %copy-done.2), channel_id=1, source_target_pairs={{0,8},{1,9},{2,10},{3,11},{4,12},{5,13},{6,14},{7,15},{8,0},{9,1},... | collective-permute-start | bytes 786440 | tf_op jit(solution)/shard_map/ppermute | solution.py:251
  19.2 7.7 %collective-permute-start.3 = (bf16[256,512]{1,0:T(8,128)(2,1)S(1)}, bf16[256,512]{1,0:T(8,128)(2,1)S(1)}, u32[]{:S(2)}, u32[]{:S(2)}) collective-permute-start(bf16[256,512]{1,0:T(8,128)(2,1)S(1)} %collective-permute-done.1.refs_2_), channel_id=1, source_target_pairs={{0,8},{1,9},{2,10},{3,11},{4,12},{5,13},{6,14},{7,15},{8,0},{9,1},... | collective-permute-start | bytes 786440 | tf_op jit(solution)/shard_map/ppermute | solution.py:251
  19.7 8.3 %collective-permute-start.7 = (bf16[256,512]{1,0:T(8,128)(2,1)S(1)}, bf16[256,512]{1,0:T(8,128)(2,1)S(1)}, u32[]{:S(2)}, u32[]{:S(2)}) collective-permute-start(bf16[256,512]{1,0:T(8,128)(2,1)S(1)} %collective-permute-done.refs_0_), channel_id=1, source_target_pairs={{0,16},{1,17},{2,18},{3,19},{4,20},{5,21},{6,22},{7,23},{8,24},{9,... | collective-permute-start | bytes 786440 | tf_op jit(solution)/shard_map/ppermute | solution.py:251
  22.4 9.3 %copy-start.1 = (bf16[512,512]{1,0:T(8,128)(2,1)S(1)}, bf16[512,512]{1,0:T(8,128)(2,1)}, u32[]{:S(2)}) copy-start(bf16[512,512]{1,0:T(8,128)(2,1)} %weight_ref.3) | copy-start | bytes 1572868
  22.4 6.1 %collective-permute-start.4 = (bf16[128,512]{1,0:T(8,128)(2,1)S(1)}, bf16[128,512]{1,0:T(8,128)(2,1)S(1)}, u32[]{:S(2)}, u32[]{:S(2)}) collective-permute-start(bf16[128,512]{1,0:T(8,128)(2,1)S(1)} %get-tuple-element.61), channel_id=1, source_target_pairs={{0,1},{1,0},{2,3},{3,2},{4,5},{5,4},{6,7},{7,6},{8,9},{9,8},{10,11... | collective-permute-start | bytes 393224 | tf_op jit(solution)/shard_map/ppermute | solution.py:251
  23.1 6.3 %collective-permute-start.5 = (bf16[128,512]{1,0:T(8,128)(2,1)S(1)}, bf16[128,512]{1,0:T(8,128)(2,1)S(1)}, u32[]{:S(2)}, u32[]{:S(2)}) collective-permute-start(bf16[128,512]{1,0:T(8,128)(2,1)S(1)} %get-tuple-element.62), channel_id=1, source_target_pairs={{0,2},{1,3},{2,0},{3,1},{4,6},{5,7},{6,4},{7,5},{8,10},{9,11},{10,... | collective-permute-start | bytes 393224 | tf_op jit(solution)/shard_map/ppermute | solution.py:251
  23.8 7.9 %collective-permute-start.6 = (bf16[128,512]{1,0:T(8,128)(2,1)S(1)}, bf16[128,512]{1,0:T(8,128)(2,1)S(1)}, u32[]{:S(2)}, u32[]{:S(2)}) collective-permute-start(bf16[128,512]{1,0:T(8,128)(2,1)S(1)} %get-tuple-element.63), channel_id=1, source_target_pairs={{0,3},{1,2},{2,1},{3,0},{4,7},{5,6},{6,5},{7,4},{8,11},{9,10},{10,... | collective-permute-start | bytes 393224 | tf_op jit(solution)/shard_map/ppermute | solution.py:251
  28.0 4.2 %collective-permute-start.8 = (bf16[256,512]{1,0:T(8,128)(2,1)S(1)}, bf16[256,512]{1,0:T(8,128)(2,1)S(1)}, u32[]{:S(2)}, u32[]{:S(2)}) collective-permute-start(bf16[256,512]{1,0:T(8,128)(2,1)S(1)} %collective-permute-done.refs_0_), channel_id=1, source_target_pairs={{0,8},{1,9},{2,10},{3,11},{4,12},{5,13},{6,14},{7,15},{8,0},{9,1},... | collective-permute-start | bytes 786440 | tf_op jit(solution)/shard_map/ppermute | solution.py:251
  28.0 4.2 %collective-permute-start.9 = (bf16[256,512]{1,0:T(8,128)(2,1)S(1)}, bf16[256,512]{1,0:T(8,128)(2,1)S(1)}, u32[]{:S(2)}, u32[]{:S(2)}) collective-permute-start(bf16[256,512]{1,0:T(8,128)(2,1)S(1)} %collective-permute-done.7.refs_2_), channel_id=1, source_target_pairs={{0,8},{1,9},{2,10},{3,11},{4,12},{5,13},{6,14},{7,15},{8,0},{9,1},... | collective-permute-start | bytes 786440 | tf_op jit(solution)/shard_map/ppermute | solution.py:251
  35.2 1.6 %collective-permute-start.10 = (bf16[16,16,512]{2,1,0:T(8,128)(2,1)S(1)}, bf16[16,16,512]{2,1,0:T(8,128)(2,1)S(1)}, u32[]{:S(2)}, u32[]{:S(2)}) collective-permute-start(bf16[16,16,512]{2,1,0:T(8,128)(2,1)S(1)} %get-tuple-element.81), channel_id=1, source_target_pairs={{0,8},{1,9},{2,10},{3,11},{4,12},{5,13},{6,14},{7,15},{8,0},{9,1},... | collective-permute-start | bytes 786440 | tf_op jit(solution)/shard_map/ppermute | solution.py:251
  36.9 5.6 %collective-permute-start.11 = (bf16[8,16,512]{2,1,0:T(8,128)(2,1)S(1)}, bf16[8,16,512]{2,1,0:T(8,128)(2,1)S(1)}, u32[]{:S(2)}, u32[]{:S(2)}) collective-permute-start(bf16[8,16,512]{2,1,0:T(8,128)(2,1)S(1)} %get-tuple-element.83), channel_id=1, source_target_pairs={{0,16},{1,17},{2,18},{3,19},{4,20},{5,21},{6,22},{7,23},{8,24},{9,... | collective-permute-start | bytes 393224 | tf_op jit(solution)/shard_map/ppermute | solution.py:251
  38.4 5.6 %collective-permute-start.15 = (bf16[128,512]{1,0:T(8,128)(2,1)S(1)}, bf16[128,512]{1,0:T(8,128)(2,1)S(1)}, u32[]{:S(2)}, u32[]{:S(2)}) collective-permute-start(bf16[128,512]{1,0:T(8,128)(2,1)S(1)} %get-tuple-element.77.refs_5_), channel_id=1, source_target_pairs={{0,1},{1,0},{2,3},{3,2},{4,5},{5,4},{6,7},{7,6},{8,9},{9,8},{10,11... | collective-permute-start | bytes 393224 | tf_op jit(solution)/shard_map/ppermute | solution.py:251
  39.0 7.1 %collective-permute-start.16 = (bf16[128,512]{1,0:T(8,128)(2,1)S(1)}, bf16[128,512]{1,0:T(8,128)(2,1)S(1)}, u32[]{:S(2)}, u32[]{:S(2)}) collective-permute-start(bf16[128,512]{1,0:T(8,128)(2,1)S(1)} %get-tuple-element.78.refs_6_), channel_id=1, source_target_pairs={{0,2},{1,3},{2,0},{3,1},{4,6},{5,7},{6,4},{7,5},{8,10},{9,11},{10,... | collective-permute-start | bytes 393224 | tf_op jit(solution)/shard_map/ppermute | solution.py:251
  39.6 8.8 %collective-permute-start.17 = (bf16[128,512]{1,0:T(8,128)(2,1)S(1)}, bf16[128,512]{1,0:T(8,128)(2,1)S(1)}, u32[]{:S(2)}, u32[]{:S(2)}) collective-permute-start(bf16[128,512]{1,0:T(8,128)(2,1)S(1)} %get-tuple-element.79.refs_7_), channel_id=1, source_target_pairs={{0,3},{1,2},{2,1},{3,0},{4,7},{5,6},{6,5},{7,4},{8,11},{9,10},{10,... | collective-permute-start | bytes 393224 | tf_op jit(solution)/shard_map/ppermute | solution.py:251
  42.5 6.3 %collective-permute-start.12 = (bf16[2,16,512]{2,1,0:T(8,128)(2,1)S(1)}, bf16[2,16,512]{2,1,0:T(8,128)(2,1)S(1)}, u32[]{:S(2)}, u32[]{:S(2)}) collective-permute-start(bf16[2,16,512]{2,1,0:T(8,128)(2,1)S(1)} %get-tuple-element.85), channel_id=1, source_target_pairs={{0,2},{1,3},{2,0},{3,1},{4,6},{5,7},{6,4},{7,5},{8,10},{9,11},{10,... | collective-permute-start | bytes 98312 | tf_op jit(solution)/shard_map/ppermute | solution.py:251
  43.2 5.7 %collective-permute-start.13 = (bf16[2,16,512]{2,1,0:T(8,128)(2,1)S(1)}, bf16[2,16,512]{2,1,0:T(8,128)(2,1)S(1)}, u32[]{:S(2)}, u32[]{:S(2)}) collective-permute-start(bf16[2,16,512]{2,1,0:T(8,128)(2,1)S(1)} %get-tuple-element.86), channel_id=1, source_target_pairs={{0,1},{1,0},{2,3},{3,2},{4,5},{5,4},{6,7},{7,6},{8,9},{9,8},{10,11... | collective-permute-start | bytes 98312 | tf_op jit(solution)/shard_map/ppermute | solution.py:251
  44.0 5.1 %collective-permute-start.14 = (bf16[2,16,512]{2,1,0:T(8,128)(2,1)S(1)}, bf16[2,16,512]{2,1,0:T(8,128)(2,1)S(1)}, u32[]{:S(2)}, u32[]{:S(2)}) collective-permute-start(bf16[2,16,512]{2,1,0:T(8,128)(2,1)S(1)} %get-tuple-element.87), channel_id=1, source_target_pairs={{0,3},{1,2},{2,1},{3,0},{4,7},{5,6},{6,5},{7,4},{8,11},{9,10},{10,... | collective-permute-start | bytes 98312 | tf_op jit(solution)/shard_map/ppermute | solution.py:251
  49.1 6.4 %collective-permute-start.18 = (f32[1,16,512]{2,1,0:T(8,128)S(1)}, f32[1,16,512]{2,1,0:T(8,128)S(1)}, u32[]{:S(2)}, u32[]{:S(2)}) collective-permute-start(f32[1,16,512]{2,1,0:T(8,128)S(1)} %get-tuple-element.94), channel_id=1, source_target_pairs={{0,4},{1,5},{2,6},{3,7},{4,0},{5,1},{6,2},{7,3},{8,12},{9,13},{10,... | collective-permute-start | bytes 98312 | tf_op jit(solution)/shard_map/ppermute | solution.py:251

commit v22 on v19

--- a/solution.py
+++ b/solution.py
@@ -178,9 +178,13 @@
     return sum(((lax.axis_index(axis) >> level) & 1) << k for k, (axis, level) in enumerate(reversed(bits)))
 
 
+def steps_of(bits):
+    return sorted(range(1 << len(bits)), key=lambda step: -step.bit_count() if step else -len(bits) - 1)
+
+
 def cut(blocks, bits, refs):
     size = refs[0].shape[0]
-    for step, ref in enumerate(refs):
+    for step, ref in zip(steps_of(bits), refs):
         ref[...] = blocks[pl.ds((coordinate(bits) ^ step) * size, size)].astype(ref.dtype)
 
 
@@ -207,7 +211,8 @@
 
 def row_kernel(weight_ref, *refs):
     *incoming, drow_ref = refs
-    drow_ref[...] = dot(jnp.concatenate([ref[...] for ref in incoming], axis=0), weight_ref[...], 1, 1).astype(bf16)
+    dhidden = jnp.concatenate([ref[...] for ref in reversed(incoming)], axis=0)
+    drow_ref[...] = dot(dhidden, weight_ref[...], 1, 1).astype(bf16)
 
 
 def table_kernel(sizes, low_hot_ref, block_ref, drow_ref, table_grad_hbm, ready, sems):
@@ -276,7 +281,7 @@
     for k, stage in enumerate(stages):
         whole, left = left, left >> len(stage)
         masks = [
-            mask_of([bit for j, bit in enumerate(reversed(stage)) if step >> j & 1]) for step in range(1, 1 << len(stage))
+            mask_of([bit for j, bit in enumerate(reversed(stage)) if step >> j & 1]) for step in steps_of(stage)[1:]
         ]
         sent = f32 if k == len(stages) - 1 else bf16
         count = len(values)
@@ -386,8 +391,9 @@
         mib=40,
     )
     incoming = [swap(dhidden[part], part) for part in range(1, near)]
-    (drow,) = call(row_kernel, [((total, width), bf16)], tower_weight, dhidden[0], *incoming, free=True)
-    terms, drow = reduce_scatter(fetched, dhidden, drow)
+    (drow,) = call(row_kernel, [((total, width), bf16)], tower_weight, *reversed(incoming), dhidden[0], free=True)
+    order = [-part % near for part in range(near)]
+    terms, drow = reduce_scatter([fetched[part] for part in order], [dhidden[part] for part in order], drow)
     table_grad = pl.pallas_call(
         functools.partial(table_kernel, sizes),
         out_specs=pl.BlockSpec(memory_space=pl.ANY),

time: 54.9 us -> 54.9 us (level)
  starting transfers between devices: 22.6 us -> 22 us
    ppermute x19, starting transfers between devices: 22.6 us -> 22 us  [swap(): lax.ppermute(value, ('batch', 'item'), [(k, k ^ mask) for k in range(devi...]
  transfers between devices with their start and end apart: 19 -> 19, of which waited for: 5 -> 8; matrix products, arithmetic and copies ran while one was open for 1% -> 1% of each run, Pallas kernels for 17% -> 17%
where the time goes in v22:
time: 54.9 us; the launch traced here: 54.7 us
  starting transfers between devices  22 us (40%)
  Pallas kernels  12.8 us (23%)
  blocking collectives  11.7 us (21%)
  waiting for transfers between devices  6.6 us (12%)
  between operations  0.83 us (2%)
  other arithmetic  0.7 us (1%)
    ppermute x19, starting transfers between devices, swap(): lax.ppermute(value, ('batch', 'item'), [(k, k ^ mask) for k in range(devi...  22 us
    all_to_all x1, blocking collectives, local(): lax.all_to_all(request, ('batch', 'item'), split_axis=0, concat_axis=0, t...  11.7 us
    pallas_call x14, Pallas kernels, call(): pl.pallas_call(kernel, out_shape=[jax.ShapeDtypeStruct(shape, dtype) for...  9.56 us
    ppermute x19, waiting for transfers between devices, swap(): lax.ppermute(value, ('batch', 'item'), [(k, k ^ mask) for k in range(devi...  6.6 us
    pallas_call x1, Pallas kernels, local(): pl.pallas_call(functools.partial(table_kernel, sizes), out_specs=pl.Block...  3.25 us
  transfers between devices with their start and end apart: 19, of which 8 were waited for; matrix products, arithmetic and copies ran while one was open for 1% of the time, Pallas kernels for 17%

profile of v22, /device:TPU:0, one launch (start us, length us, event | category | flops | bytes accessed | tf_op | source)
XLA Modules:
  0.0 54.7 jit_solution(11666792789812424440)
XLA Ops:
  0.6 4.1 %collective-permute-start = (bf16[256,512]{1,0:T(8,128)(2,1)}, bf16[256,512]{1,0:T(8,128)(2,1)S(1)}, u32[]{:S(2)}, u32[]{:S(2)}) collective-permute-start(bf16[256,512]{1,0:T(8,128)(2,1)} %refs_0_), channel_id=1, source_target_pairs={{0,4},{1,5},{2,6},{3,7},{4,0},{5,1},{6,2},{7,3},{8,12},{9,13},{10,... | collective-permute-start | bytes 786440 | tf_op jit(solution)/shard_map/ppermute | solution.py:255
  4.7 1.5 %collective-permute-start.1 = (bf16[256,512]{1,0:T(8,128)(2,1)}, bf16[256,512]{1,0:T(8,128)(2,1)S(1)}, u32[]{:S(2)}, u32[]{:S(2)}) collective-permute-start(bf16[256,512]{1,0:T(8,128)(2,1)} %refs_0_), channel_id=1, source_target_pairs={{0,16},{1,17},{2,18},{3,19},{4,20},{5,21},{6,22},{7,23},{8,24},{9,... | collective-permute-start | bytes 786440 | tf_op jit(solution)/shard_map/ppermute | solution.py:255
  6.2 0.7 %pad_add_fusion.named_ref = s32[2,256]{1,0:T(2,128)S(1)} fusion(s32[1,256]{1,0:T(1,128)} %bitcast.11, s32[1,256]{1,0:T(1,128)} %bitcast.12), kind=kLoop, calls=%fused_computation | loop fusion | flops 512 | bytes 4096 | tf_op jit(solution)/shard_map/stack | solution.py:322
  7.4 11.7 %all_to_all.12 = s32[32,1,80]{2,1,0:T(1,128)S(1)} all-to-all(s32[32,1,80]{2,1,0:T(1,128)S(1)} %bitcast.10), channel_id=1, replica_groups=mesh['batch'=4,'item'=8] {'batch','item'}, dimensions={0} | all-to-all | bytes 20480 | tf_op jit(solution)/shard_map/all_to_all | solution.py:325
  19.7 0.6 %collective-permute-start.7 = (bf16[256,512]{1,0:T(8,128)(2,1)S(1)}, bf16[256,512]{1,0:T(8,128)(2,1)S(1)}, u32[]{:S(2)}, u32[]{:S(2)}) collective-permute-start(bf16[256,512]{1,0:T(8,128)(2,1)S(1)} %collective-permute-done.refs_0_), channel_id=1, source_target_pairs={{0,16},{1,17},{2,18},{3,19},{4,20},{5,21},{6,22},{7,23},{8,24},{9,... | collective-permute-start | bytes 786440 | tf_op jit(solution)/shard_map/ppermute | solution.py:255
  20.3 0.9 %shard_map.69 = bf16[128,512]{1,0:T(8,128)(2,1)S(1)} custom-call(s32[32,80]{1,0:T(8,128)S(1)} %bitcast.6, bf16[4096,512]{1,0:T(8,128)(2,1)S(1)} %copy-done), custom_call_target="tpu_custom_call" | custom-call | flops 536870912 | bytes 1048576 | tf_op jit(solution)/shard_map/pallas_call | solution.py:244
  21.2 0.8 %collective-permute-start.4 = (bf16[128,512]{1,0:T(8,128)(2,1)S(1)}, bf16[128,512]{1,0:T(8,128)(2,1)S(1)}, u32[]{:S(2)}, u32[]{:S(2)}) collective-permute-start(bf16[128,512]{1,0:T(8,128)(2,1)S(1)} %shard_map.69), channel_id=1, source_target_pairs={{0,3},{1,2},{2,1},{3,0},{4,7},{5,6},{6,5},{7,4},{8,11},{9,10},{10,... | collective-permute-start | bytes 393224 | tf_op jit(solution)/shard_map/ppermute | solution.py:255
  22.0 1.6 %shard_map.70 = (bf16[128,512]{1,0:T(8,128)(2,1)S(1)}, bf16[128,512]{1,0:T(8,128)(2,1)S(1)}) custom-call(s32[32,80]{1,0:T(8,128)S(1)} %bitcast.7, bf16[4096,512]{1,0:T(8,128)(2,1)S(1)} %copy-done), custom_call_target="tpu_custom_call" | custom-call | flops 1073741824 | bytes 1048576 | tf_op jit(solution)/shard_map/pallas_call | solution.py:244
  23.6 1.4 %collective-permute-start.5 = (bf16[128,512]{1,0:T(8,128)(2,1)S(1)}, bf16[128,512]{1,0:T(8,128)(2,1)S(1)}, u32[]{:S(2)}, u32[]{:S(2)}) collective-permute-start(bf16[128,512]{1,0:T(8,128)(2,1)S(1)} %get-tuple-element.62), channel_id=1, source_target_pairs={{0,2},{1,3},{2,0},{3,1},{4,6},{5,7},{6,4},{7,5},{8,10},{9,11},{10,... | collective-permute-start | bytes 393224 | tf_op jit(solution)/shard_map/ppermute | solution.py:255
  25.0 1.4 %collective-permute-start.6 = (bf16[128,512]{1,0:T(8,128)(2,1)S(1)}, bf16[128,512]{1,0:T(8,128)(2,1)S(1)}, u32[]{:S(2)}, u32[]{:S(2)}) collective-permute-start(bf16[128,512]{1,0:T(8,128)(2,1)S(1)} %get-tuple-element.63), channel_id=1, source_target_pairs={{0,1},{1,0},{2,3},{3,2},{4,5},{5,4},{6,7},{7,6},{8,9},{9,8},{10,11... | collective-permute-start | bytes 393224 | tf_op jit(solution)/shard_map/ppermute | solution.py:255
  26.4 0.9 %shard_map.71.refs_0_ = bf16[128,512]{1,0:T(8,128)(2,1)S(1)} custom-call(s32[32,80]{1,0:T(8,128)S(1)} %bitcast.8, bf16[4096,512]{1,0:T(8,128)(2,1)S(1)} %copy-done), custom_call_target="tpu_custom_call" | custom-call | flops 536870912 | bytes 1048576 | tf_op jit(solution)/shard_map/pallas_call | solution.py:244
  27.3 1.0 %shard_map.72 = (s32[512,1]{1,0:T(8,128)S(1)}, bf16[256,512]{1,0:T(8,128)(2,1)S(1)}, bf16[256,512]{1,0:T(8,128)(2,1)S(1)}, bf16[1024,512]{1,0:T(8,128)(2,1)S(1)}, bf16[256,512]{1,0:T(8,128)(2,1)S(1)}) custom-call(s32[32,80]{1,0:T(8,128)S(1)} %bitcast.9, bf16[256,512]{1,0:T(8,128)(2,1)S(1)} %copy-done.2, bf16[256,512]{1,0:T(8,128)(2,1)S(1)} %collective-permute-done.2.refs_1_, ...), custom_call_target="tpu_custom_call" | custom-call | tf_op jit(solution)/shard_map/pallas_call | solution.py:244
  29.4 1.0 %collective-permute-done.6.refs_1_.refs_3_ = bf16[128,512]{1,0:T(8,128)(2,1)S(1)} collective-permute-done((bf16[128,512]{1,0:T(8,128)(2,1)S(1)}, bf16[128,512]{1,0:T(8,128)(2,1)S(1)}, u32[]{:S(2)}, u32[]{:S(2)}) %collective-permute-start.6) | collective-permute-done | bytes 131104 | tf_op jit(solution)/shard_map/ppermute | solution.py:255
  30.4 0.5 shard_map.73
  30.9 0.7 %shard_map.74 = (bf16[1024,512]{1,0:T(8,128)(2,1)S(1)}, bf16[256,512]{1,0:T(8,128)(2,1)S(1)}) custom-call(s32[512,1]{1,0:T(8,128)S(1)} %get-tuple-element.70.place_ref, bf16[256,512]{1,0:T(8,128)(2,1)S(1)} %collective-permute-done.refs_0_, bf16[256,512]{1,0:T(8,128)(2,1)S(1)} %collective-permute-done.8.refs_1_, ...), custom_call_target="tpu_custom_call" | custom-call | tf_op jit(solution)/shard_map/pallas_call | solution.py:244
  31.6 1.7 %shard_map.75 = (bf16[128,512]{1,0:T(8,128)(2,1)S(1)}, bf16[128,512]{1,0:T(8,128)(2,1)S(1)}, bf16[128,512]{1,0:T(8,128)(2,1)S(1)}, bf16[128,512]{1,0:T(8,128)(2,1)S(1)}) custom-call(f32[512,512]{1,0:T(8,128)S(1)} %get-tuple-element.64.hidden_ref, f32[512,1]{1,0:T(8,128)S(1)} %get-tuple-element.65.rscale_ref, ...), custom_call_target="tpu_custom_call" | custom-call | flops 2147483648 | bytes 1048576 | tf_op jit(solution)/shard_map/pallas_call | solution.py:244
  33.4 0.5 shard_map.76
  34.0 1.5 %collective-permute-done.10.refs_1_ = bf16[16,16,512]{2,1,0:T(8,128)(2,1)S(1)} collective-permute-done((bf16[16,16,512]{2,1,0:T(8,128)(2,1)S(1)}, bf16[16,16,512]{2,1,0:T(8,128)(2,1)S(1)}, u32[]{:S(2)}, u32[]{:S(2)}) %collective-permute-start.10) | collective-permute-done | bytes 262176 | tf_op jit(solution)/shard_map/ppermute | solution.py:255
  35.6 1.4 %collective-permute-start.11 = (bf16[8,16,512]{2,1,0:T(8,128)(2,1)S(1)}, bf16[8,16,512]{2,1,0:T(8,128)(2,1)S(1)}, u32[]{:S(2)}, u32[]{:S(2)}) collective-permute-start(bf16[8,16,512]{2,1,0:T(8,128)(2,1)S(1)} %get-tuple-element.83), channel_id=1, source_target_pairs={{0,16},{1,17},{2,18},{3,19},{4,20},{5,21},{6,22},{7,23},{8,24},{9,... | collective-permute-start | bytes 393224 | tf_op jit(solution)/shard_map/ppermute | solution.py:255
  37.0 1.1 %collective-permute-start.15 = (bf16[128,512]{1,0:T(8,128)(2,1)S(1)}, bf16[128,512]{1,0:T(8,128)(2,1)S(1)}, u32[]{:S(2)}, u32[]{:S(2)}) collective-permute-start(bf16[128,512]{1,0:T(8,128)(2,1)S(1)} %get-tuple-element.77.refs_5_), channel_id=1, source_target_pairs={{0,3},{1,2},{2,1},{3,0},{4,7},{5,6},{6,5},{7,4},{8,11},{9,10},{10,... | collective-permute-start | bytes 393224 | tf_op jit(solution)/shard_map/ppermute | solution.py:255
  38.1 1.4 %collective-permute-start.16 = (bf16[128,512]{1,0:T(8,128)(2,1)S(1)}, bf16[128,512]{1,0:T(8,128)(2,1)S(1)}, u32[]{:S(2)}, u32[]{:S(2)}) collective-permute-start(bf16[128,512]{1,0:T(8,128)(2,1)S(1)} %get-tuple-element.78.refs_6_), channel_id=1, source_target_pairs={{0,2},{1,3},{2,0},{3,1},{4,6},{5,7},{6,4},{7,5},{8,10},{9,11},{10,... | collective-permute-start | bytes 393224 | tf_op jit(solution)/shard_map/ppermute | solution.py:255
  39.6 1.0 %collective-permute-start.17 = (bf16[128,512]{1,0:T(8,128)(2,1)S(1)}, bf16[128,512]{1,0:T(8,128)(2,1)S(1)}, u32[]{:S(2)}, u32[]{:S(2)}) collective-permute-start(bf16[128,512]{1,0:T(8,128)(2,1)S(1)} %get-tuple-element.79.refs_7_), channel_id=1, source_target_pairs={{0,1},{1,0},{2,3},{3,2},{4,5},{5,4},{6,7},{7,6},{8,9},{9,8},{10,11... | collective-permute-start | bytes 393224 | tf_op jit(solution)/shard_map/ppermute | solution.py:255
  40.5 0.7 %collective-permute-done.11.refs_1_ = bf16[8,16,512]{2,1,0:T(8,128)(2,1)S(1)} collective-permute-done((bf16[8,16,512]{2,1,0:T(8,128)(2,1)S(1)}, bf16[8,16,512]{2,1,0:T(8,128)(2,1)S(1)}, u32[]{:S(2)}, u32[]{:S(2)}) %collective-permute-start.11) | collective-permute-done | bytes 131104 | tf_op jit(solution)/shard_map/ppermute | solution.py:255
  41.3 1.1 %collective-permute-start.12 = (bf16[2,16,512]{2,1,0:T(8,128)(2,1)S(1)}, bf16[2,16,512]{2,1,0:T(8,128)(2,1)S(1)}, u32[]{:S(2)}, u32[]{:S(2)}) collective-permute-start(bf16[2,16,512]{2,1,0:T(8,128)(2,1)S(1)} %get-tuple-element.85), channel_id=1, source_target_pairs={{0,3},{1,2},{2,1},{3,0},{4,7},{5,6},{6,5},{7,4},{8,11},{9,10},{10,... | collective-permute-start | bytes 98312 | tf_op jit(solution)/shard_map/ppermute | solution.py:255
  42.3 1.4 %collective-permute-start.13 = (bf16[2,16,512]{2,1,0:T(8,128)(2,1)S(1)}, bf16[2,16,512]{2,1,0:T(8,128)(2,1)S(1)}, u32[]{:S(2)}, u32[]{:S(2)}) collective-permute-start(bf16[2,16,512]{2,1,0:T(8,128)(2,1)S(1)} %get-tuple-element.86), channel_id=1, source_target_pairs={{0,2},{1,3},{2,0},{3,1},{4,6},{5,7},{6,4},{7,5},{8,10},{9,11},{10,... | collective-permute-start | bytes 98312 | tf_op jit(solution)/shard_map/ppermute | solution.py:255
  43.8 0.6 %collective-permute-done.15.refs_0_ = bf16[128,512]{1,0:T(8,128)(2,1)S(1)} collective-permute-done((bf16[128,512]{1,0:T(8,128)(2,1)S(1)}, bf16[128,512]{1,0:T(8,128)(2,1)S(1)}, u32[]{:S(2)}, u32[]{:S(2)}) %collective-permute-start.15) | collective-permute-done | bytes 131104 | tf_op jit(solution)/shard_map/ppermute | solution.py:255
  44.3 1.1 %collective-permute-start.14 = (bf16[2,16,512]{2,1,0:T(8,128)(2,1)S(1)}, bf16[2,16,512]{2,1,0:T(8,128)(2,1)S(1)}, u32[]{:S(2)}, u32[]{:S(2)}) collective-permute-start(bf16[2,16,512]{2,1,0:T(8,128)(2,1)S(1)} %get-tuple-element.87), channel_id=1, source_target_pairs={{0,1},{1,0},{2,3},{3,2},{4,5},{5,4},{6,7},{7,6},{8,9},{9,8},{10,11... | collective-permute-start | bytes 98312 | tf_op jit(solution)/shard_map/ppermute | solution.py:255
  45.4 0.9 %collective-permute-done.16.refs_1_ = bf16[128,512]{1,0:T(8,128)(2,1)S(1)} collective-permute-done((bf16[128,512]{1,0:T(8,128)(2,1)S(1)}, bf16[128,512]{1,0:T(8,128)(2,1)S(1)}, u32[]{:S(2)}, u32[]{:S(2)}) %collective-permute-start.16) | collective-permute-done | bytes 131104 | tf_op jit(solution)/shard_map/ppermute | solution.py:255
  47.2 1.0 %collective-permute-done.14.refs_3_ = bf16[2,16,512]{2,1,0:T(8,128)(2,1)S(1)} collective-permute-done((bf16[2,16,512]{2,1,0:T(8,128)(2,1)S(1)}, bf16[2,16,512]{2,1,0:T(8,128)(2,1)S(1)}, u32[]{:S(2)}, u32[]{:S(2)}) %collective-permute-start.14) | collective-permute-done | bytes 32800 | tf_op jit(solution)/shard_map/ppermute | solution.py:255
  48.3 2.5 %collective-permute-start.18 = (f32[1,16,512]{2,1,0:T(8,128)S(1)}, f32[1,16,512]{2,1,0:T(8,128)S(1)}, u32[]{:S(2)}, u32[]{:S(2)}) collective-permute-start(f32[1,16,512]{2,1,0:T(8,128)S(1)} %get-tuple-element.94), channel_id=1, source_target_pairs={{0,4},{1,5},{2,6},{3,7},{4,0},{5,1},{6,2},{7,3},{8,12},{9,13},{10,... | collective-permute-start | bytes 98312 | tf_op jit(solution)/shard_map/ppermute | solution.py:255
  50.8 3.2 %shard_map.80 = bf16[4096,512]{1,0:T(8,128)(2,1)} custom-call(bf16[256,512]{1,0:T(8,128)(2,1)S(1)} %get-tuple-element.58.low_hot_ref, bf16[256,512]{1,0:T(8,128)(2,1)S(1)} %get-tuple-element.59.block_ref, bf16[512,512]{1,0:T(8,128)(2,1)S(1)} %shard_map.79.drow_ref), custom_call_target="tpu_custom_call" | custom-call | flops 2147483648 | bytes 4194304 | tf_op jit(solution)/shard_map/pallas_call | solution.py:397
  54.0 0.6 %shard_map.82 = f32[16,512]{1,0:T(8,128)} custom-call(f32[1,16,512]{2,1,0:T(8,128)S(1)} %get-tuple-element.96.refs_0_, f32[1,16,512]{2,1,0:T(8,128)S(1)} %collective-permute-done.18.refs_1_), custom_call_target="tpu_custom_call" | custom-call | bytes 1048576 | tf_op jit(solution)/shard_map/pallas_call | solution.py:244
  (29 shorter events, 3.2 us)
Async XLA Ops:
  0.6 18.4 %collective-permute-start = (bf16[256,512]{1,0:T(8,128)(2,1)}, bf16[256,512]{1,0:T(8,128)(2,1)S(1)}, u32[]{:S(2)}, u32[]{:S(2)}) collective-permute-start(bf16[256,512]{1,0:T(8,128)(2,1)} %refs_0_), channel_id=1, source_target_pairs={{0,4},{1,5},{2,6},{3,7},{4,0},{5,1},{6,2},{7,3},{8,12},{9,13},{10,... | collective-permute-start | bytes 786440 | tf_op jit(solution)/shard_map/ppermute | solution.py:255
  4.7 14.4 %collective-permute-start.1 = (bf16[256,512]{1,0:T(8,128)(2,1)}, bf16[256,512]{1,0:T(8,128)(2,1)S(1)}, u32[]{:S(2)}, u32[]{:S(2)}) collective-permute-start(bf16[256,512]{1,0:T(8,128)(2,1)} %refs_0_), channel_id=1, source_target_pairs={{0,16},{1,17},{2,18},{3,19},{4,20},{5,21},{6,22},{7,23},{8,24},{9,... | collective-permute-start | bytes 786440 | tf_op jit(solution)/shard_map/ppermute | solution.py:255
  6.9 12.2 %copy-start.2 = (bf16[256,512]{1,0:T(8,128)(2,1)S(1)}, bf16[256,512]{1,0:T(8,128)(2,1)}, u32[]{:S(2)}) copy-start(bf16[256,512]{1,0:T(8,128)(2,1)} %refs_0_) | copy-start | bytes 786436
  6.9 13.3 %copy-start = (bf16[4096,512]{1,0:T(8,128)(2,1)S(1)}, bf16[4096,512]{1,0:T(8,128)(2,1)}, u32[]{:S(2)}) copy-start(bf16[4096,512]{1,0:T(8,128)(2,1)} %table_ref.5) | copy-start | bytes 12582916
  19.1 5.9 %collective-permute-start.2 = (bf16[256,512]{1,0:T(8,128)(2,1)S(1)}, bf16[256,512]{1,0:T(8,128)(2,1)S(1)}, u32[]{:S(2)}, u32[]{:S(2)}) collective-permute-start(bf16[256,512]{1,0:T(8,128)(2,1)S(1)} %copy-done.2), channel_id=1, source_target_pairs={{0,8},{1,9},{2,10},{3,11},{4,12},{5,13},{6,14},{7,15},{8,0},{9,1},... | collective-permute-start | bytes 786440 | tf_op jit(solution)/shard_map/ppermute | solution.py:255
  19.2 8.1 %collective-permute-start.3 = (bf16[256,512]{1,0:T(8,128)(2,1)S(1)}, bf16[256,512]{1,0:T(8,128)(2,1)S(1)}, u32[]{:S(2)}, u32[]{:S(2)}) collective-permute-start(bf16[256,512]{1,0:T(8,128)(2,1)S(1)} %collective-permute-done.1.refs_2_), channel_id=1, source_target_pairs={{0,8},{1,9},{2,10},{3,11},{4,12},{5,13},{6,14},{7,15},{8,0},{9,1},... | collective-permute-start | bytes 786440 | tf_op jit(solution)/shard_map/ppermute | solution.py:255
  19.7 8.7 %collective-permute-start.7 = (bf16[256,512]{1,0:T(8,128)(2,1)S(1)}, bf16[256,512]{1,0:T(8,128)(2,1)S(1)}, u32[]{:S(2)}, u32[]{:S(2)}) collective-permute-start(bf16[256,512]{1,0:T(8,128)(2,1)S(1)} %collective-permute-done.refs_0_), channel_id=1, source_target_pairs={{0,16},{1,17},{2,18},{3,19},{4,20},{5,21},{6,22},{7,23},{8,24},{9,... | collective-permute-start | bytes 786440 | tf_op jit(solution)/shard_map/ppermute | solution.py:255
  21.2 9.2 %copy-start.1 = (bf16[512,512]{1,0:T(8,128)(2,1)S(1)}, bf16[512,512]{1,0:T(8,128)(2,1)}, u32[]{:S(2)}) copy-start(bf16[512,512]{1,0:T(8,128)(2,1)} %weight_ref.3) | copy-start | bytes 1572868
  21.2 7.7 %collective-permute-start.4 = (bf16[128,512]{1,0:T(8,128)(2,1)S(1)}, bf16[128,512]{1,0:T(8,128)(2,1)S(1)}, u32[]{:S(2)}, u32[]{:S(2)}) collective-permute-start(bf16[128,512]{1,0:T(8,128)(2,1)S(1)} %shard_map.69), channel_id=1, source_target_pairs={{0,3},{1,2},{2,1},{3,0},{4,7},{5,6},{6,5},{7,4},{8,11},{9,10},{10,... | collective-permute-start | bytes 393224 | tf_op jit(solution)/shard_map/ppermute | solution.py:255
  23.6 5.8 %collective-permute-start.5 = (bf16[128,512]{1,0:T(8,128)(2,1)S(1)}, bf16[128,512]{1,0:T(8,128)(2,1)S(1)}, u32[]{:S(2)}, u32[]{:S(2)}) collective-permute-start(bf16[128,512]{1,0:T(8,128)(2,1)S(1)} %get-tuple-element.62), channel_id=1, source_target_pairs={{0,2},{1,3},{2,0},{3,1},{4,6},{5,7},{6,4},{7,5},{8,10},{9,11},{10,... | collective-permute-start | bytes 393224 | tf_op jit(solution)/shard_map/ppermute | solution.py:255
  25.0 5.3 %collective-permute-start.6 = (bf16[128,512]{1,0:T(8,128)(2,1)S(1)}, bf16[128,512]{1,0:T(8,128)(2,1)S(1)}, u32[]{:S(2)}, u32[]{:S(2)}) collective-permute-start(bf16[128,512]{1,0:T(8,128)(2,1)S(1)} %get-tuple-element.63), channel_id=1, source_target_pairs={{0,1},{1,0},{2,3},{3,2},{4,5},{5,4},{6,7},{7,6},{8,9},{9,8},{10,11... | collective-permute-start | bytes 393224 | tf_op jit(solution)/shard_map/ppermute | solution.py:255
  28.3 2.6 %collective-permute-start.8 = (bf16[256,512]{1,0:T(8,128)(2,1)S(1)}, bf16[256,512]{1,0:T(8,128)(2,1)S(1)}, u32[]{:S(2)}, u32[]{:S(2)}) collective-permute-start(bf16[256,512]{1,0:T(8,128)(2,1)S(1)} %collective-permute-done.refs_0_), channel_id=1, source_target_pairs={{0,8},{1,9},{2,10},{3,11},{4,12},{5,13},{6,14},{7,15},{8,0},{9,1},... | collective-permute-start | bytes 786440 | tf_op jit(solution)/shard_map/ppermute | solution.py:255
  28.4 2.5 %collective-permute-start.9 = (bf16[256,512]{1,0:T(8,128)(2,1)S(1)}, bf16[256,512]{1,0:T(8,128)(2,1)S(1)}, u32[]{:S(2)}, u32[]{:S(2)}) collective-permute-start(bf16[256,512]{1,0:T(8,128)(2,1)S(1)} %collective-permute-done.7.refs_2_), channel_id=1, source_target_pairs={{0,8},{1,9},{2,10},{3,11},{4,12},{5,13},{6,14},{7,15},{8,0},{9,1},... | collective-permute-start | bytes 786440 | tf_op jit(solution)/shard_map/ppermute | solution.py:255
  33.9 1.6 %collective-permute-start.10 = (bf16[16,16,512]{2,1,0:T(8,128)(2,1)S(1)}, bf16[16,16,512]{2,1,0:T(8,128)(2,1)S(1)}, u32[]{:S(2)}, u32[]{:S(2)}) collective-permute-start(bf16[16,16,512]{2,1,0:T(8,128)(2,1)S(1)} %get-tuple-element.81), channel_id=1, source_target_pairs={{0,8},{1,9},{2,10},{3,11},{4,12},{5,13},{6,14},{7,15},{8,0},{9,1},... | collective-permute-start | bytes 786440 | tf_op jit(solution)/shard_map/ppermute | solution.py:255
  35.6 5.6 %collective-permute-start.11 = (bf16[8,16,512]{2,1,0:T(8,128)(2,1)S(1)}, bf16[8,16,512]{2,1,0:T(8,128)(2,1)S(1)}, u32[]{:S(2)}, u32[]{:S(2)}) collective-permute-start(bf16[8,16,512]{2,1,0:T(8,128)(2,1)S(1)} %get-tuple-element.83), channel_id=1, source_target_pairs={{0,16},{1,17},{2,18},{3,19},{4,20},{5,21},{6,22},{7,23},{8,24},{9,... | collective-permute-start | bytes 393224 | tf_op jit(solution)/shard_map/ppermute | solution.py:255
  37.0 7.3 %collective-permute-start.15 = (bf16[128,512]{1,0:T(8,128)(2,1)S(1)}, bf16[128,512]{1,0:T(8,128)(2,1)S(1)}, u32[]{:S(2)}, u32[]{:S(2)}) collective-permute-start(bf16[128,512]{1,0:T(8,128)(2,1)S(1)} %get-tuple-element.77.refs_5_), channel_id=1, source_target_pairs={{0,3},{1,2},{2,1},{3,0},{4,7},{5,6},{6,5},{7,4},{8,11},{9,10},{10,... | collective-permute-start | bytes 393224 | tf_op jit(solution)/shard_map/ppermute | solution.py:255
  38.1 8.2 %collective-permute-start.16 = (bf16[128,512]{1,0:T(8,128)(2,1)S(1)}, bf16[128,512]{1,0:T(8,128)(2,1)S(1)}, u32[]{:S(2)}, u32[]{:S(2)}) collective-permute-start(bf16[128,512]{1,0:T(8,128)(2,1)S(1)} %get-tuple-element.78.refs_6_), channel_id=1, source_target_pairs={{0,2},{1,3},{2,0},{3,1},{4,6},{5,7},{6,4},{7,5},{8,10},{9,11},{10,... | collective-permute-start | bytes 393224 | tf_op jit(solution)/shard_map/ppermute | solution.py:255
  39.6 7.2 %collective-permute-start.17 = (bf16[128,512]{1,0:T(8,128)(2,1)S(1)}, bf16[128,512]{1,0:T(8,128)(2,1)S(1)}, u32[]{:S(2)}, u32[]{:S(2)}) collective-permute-start(bf16[128,512]{1,0:T(8,128)(2,1)S(1)} %get-tuple-element.79.refs_7_), channel_id=1, source_target_pairs={{0,1},{1,0},{2,3},{3,2},{4,5},{5,4},{6,7},{7,6},{8,9},{9,8},{10,11... | collective-permute-start | bytes 393224 | tf_op jit(solution)/shard_map/ppermute | solution.py:255
  41.3 5.9 %collective-permute-start.12 = (bf16[2,16,512]{2,1,0:T(8,128)(2,1)S(1)}, bf16[2,16,512]{2,1,0:T(8,128)(2,1)S(1)}, u32[]{:S(2)}, u32[]{:S(2)}) collective-permute-start(bf16[2,16,512]{2,1,0:T(8,128)(2,1)S(1)} %get-tuple-element.85), channel_id=1, source_target_pairs={{0,3},{1,2},{2,1},{3,0},{4,7},{5,6},{6,5},{7,4},{8,11},{9,10},{10,... | collective-permute-start | bytes 98312 | tf_op jit(solution)/shard_map/ppermute | solution.py:255
  42.3 4.9 %collective-permute-start.13 = (bf16[2,16,512]{2,1,0:T(8,128)(2,1)S(1)}, bf16[2,16,512]{2,1,0:T(8,128)(2,1)S(1)}, u32[]{:S(2)}, u32[]{:S(2)}) collective-permute-start(bf16[2,16,512]{2,1,0:T(8,128)(2,1)S(1)} %get-tuple-element.86), channel_id=1, source_target_pairs={{0,2},{1,3},{2,0},{3,1},{4,6},{5,7},{6,4},{7,5},{8,10},{9,11},{10,... | collective-permute-start | bytes 98312 | tf_op jit(solution)/shard_map/ppermute | solution.py:255
  44.3 3.9 %collective-permute-start.14 = (bf16[2,16,512]{2,1,0:T(8,128)(2,1)S(1)}, bf16[2,16,512]{2,1,0:T(8,128)(2,1)S(1)}, u32[]{:S(2)}, u32[]{:S(2)}) collective-permute-start(bf16[2,16,512]{2,1,0:T(8,128)(2,1)S(1)} %get-tuple-element.87), channel_id=1, source_target_pairs={{0,1},{1,0},{2,3},{3,2},{4,5},{5,4},{6,7},{7,6},{8,9},{9,8},{10,11... | collective-permute-start | bytes 98312 | tf_op jit(solution)/shard_map/ppermute | solution.py:255
  48.3 5.8 %collective-permute-start.18 = (f32[1,16,512]{2,1,0:T(8,128)S(1)}, f32[1,16,512]{2,1,0:T(8,128)S(1)}, u32[]{:S(2)}, u32[]{:S(2)}) collective-permute-start(f32[1,16,512]{2,1,0:T(8,128)S(1)} %get-tuple-element.94), channel_id=1, source_target_pairs={{0,4},{1,5},{2,6},{3,7},{4,0},{5,1},{6,2},{7,3},{8,12},{9,13},{10,... | collective-permute-start | bytes 98312 | tf_op jit(solution)/shard_map/ppermute | solution.py:255

commit v23 on v22

--- a/solution.py
+++ b/solution.py
@@ -215,16 +215,17 @@
     drow_ref[...] = dot(dhidden, weight_ref[...], 1, 1).astype(bf16)
 
 
-def table_kernel(sizes, low_hot_ref, block_ref, drow_ref, table_grad_hbm, ready, sems):
-    copies, start = [], 0
+def table_kernel(first, sizes, low_hot_ref, block_ref, drow_ref, *refs):
+    *_, table_grad_hbm, ready, sems = refs
+    copies, start = [], first
     for g, size in enumerate(sizes):
-        here = pl.ds(start, size)
+        here = pl.ds(start - first, size)
         picks = [
             jnp.where(block_ref[...] == jnp.bfloat16(k), low_hot_ref[...], jnp.bfloat16(0))
             for k in range(start // BLOCK, (start + size) // BLOCK)
         ]
         ready[here] = dot(jnp.concatenate(picks, axis=0), drow_ref[...]).astype(bf16)
-        copy = pltpu.make_async_copy(ready.at[here], table_grad_hbm.at[here], sems.at[g])
+        copy = pltpu.make_async_copy(ready.at[here], table_grad_hbm.at[pl.ds(start, size)], sems.at[g])
         copy.start()
         copies.append(copy)
         start += size
@@ -261,6 +262,20 @@
 
 def mask_of(bits):
     return sum((lax.axis_size("item") if axis == "batch" else 1) << level for axis, level in bits)
+
+
+def table_call(rows, first, sizes, masks, drow, *before, flops=0):
+    total, width = drow.shape
+    return pl.pallas_call(
+        functools.partial(table_kernel, first, sizes),
+        in_specs=[pl.BlockSpec(memory_space=pltpu.VMEM)] * 3 + [pl.BlockSpec(memory_space=pl.ANY)] * len(before),
+        out_specs=pl.BlockSpec(memory_space=pl.ANY),
+        out_shape=jax.ShapeDtypeStruct((rows, width), bf16),
+        scratch_shapes=[pltpu.VMEM((sum(sizes), width), bf16), pltpu.SemaphoreType.DMA((len(sizes),))],
+        input_output_aliases={3: 0} if before else {},
+        compiler_params=params(16),
+        cost_estimate=cost(flops, 2 * sum(sizes) * width if flops else 0),
+    )(*masks, drow, *before)
 
 
 def reduce_scatter(fetched, dhidden, drow):
@@ -309,7 +324,7 @@
     slots = 2 * n // devices
     total = devices * slots
     size = total // near
-    sizes = [rows // 8] + [rows // 4] * 3 + [rows // 8]
+    sizes = [rows // 8] * 3 + [rows // 4] * 2 + [rows // 8]
 
     far = [batch * n_item for batch in range(2, n_batch, 2)]
     users = {0: user_vectors}
@@ -393,15 +408,12 @@
     incoming = [swap(dhidden[part], part) for part in range(1, near)]
     (drow,) = call(row_kernel, [((total, width), bf16)], tower_weight, *reversed(incoming), dhidden[0], free=True)
     order = [-part % near for part in range(near)]
-    terms, drow = reduce_scatter([fetched[part] for part in order], [dhidden[part] for part in order], drow)
-    table_grad = pl.pallas_call(
-        functools.partial(table_kernel, sizes),
-        out_specs=pl.BlockSpec(memory_space=pl.ANY),
-        out_shape=jax.ShapeDtypeStruct((rows, width), bf16),
-        scratch_shapes=[pltpu.VMEM((rows, width), bf16), pltpu.SemaphoreType.DMA((len(sizes),))],
-        compiler_params=params(16),
-        cost_estimate=cost(2 * total * rows * width, 2 * rows * width),
-    )(low_hot, block, drow)
+    table_grad = table_call(rows, 0, sizes[:2], (low_hot, block), drow)
+    terms, (drow, table_grad) = reduce_scatter(
+        [fetched[part] for part in order], [dhidden[part] for part in order], (drow, table_grad)
+    )
+    flops = 2 * total * rows * width
+    table_grad = table_call(rows, sum(sizes[:2]), sizes[2:], (low_hot, block), drow, table_grad, flops=flops)
     table_grad, *terms = lax.optimization_barrier((table_grad, *terms))
     (weight_grad,) = call(last_kernel, [((width // devices, width), f32)], *terms)
     return (table_grad, weight_grad)

time: 54.9 us -> 56.6 us (1.031)
  starting transfers between devices: 22 us -> 23.1 us
  Pallas kernels: 12.8 us -> 13.8 us
    ppermute x19, starting transfers between devices: 22 us -> 23.1 us  [swap(): lax.ppermute(value, ('batch', 'item'), [(k, k ^ mask) for k in range(devi...]
    pallas_call x1 -> x2, Pallas kernels: 3.25 us -> 4.22 us  [table_call(): pl.pallas_call(functools.partial(table_kernel, first, sizes), in_specs=[p...]
  transfers between devices with their start and end apart: 19 -> 19, of which waited for: 8 -> 7; matrix products, arithmetic and copies ran while one was open for 1% -> 1% of each run, Pallas kernels for 17% -> 18%
where the time goes in v23:
time: 56.6 us; the launch traced here: 56.4 us
  starting transfers between devices  23.1 us (41%)
  Pallas kernels  13.8 us (24%)
  blocking collectives  11.7 us (21%)
  waiting for transfers between devices  6.26 us (11%)
  between operations  0.85 us (2%)
  other arithmetic  0.7 us (1%)
    ppermute x19, starting transfers between devices, swap(): lax.ppermute(value, ('batch', 'item'), [(k, k ^ mask) for k in range(devi...  23.1 us
    all_to_all x1, blocking collectives, local(): lax.all_to_all(request, ('batch', 'item'), split_axis=0, concat_axis=0, t...  11.7 us
    pallas_call x14, Pallas kernels, call(): pl.pallas_call(kernel, out_shape=[jax.ShapeDtypeStruct(shape, dtype) for...  9.56 us
    ppermute x19, waiting for transfers between devices, swap(): lax.ppermute(value, ('batch', 'item'), [(k, k ^ mask) for k in range(devi...  6.26 us
    pallas_call x2, Pallas kernels, table_call(): pl.pallas_call(functools.partial(table_kernel, first, sizes), in_specs=[p...  4.22 us
  transfers between devices with their start and end apart: 19, of which 7 were waited for; matrix products, arithmetic and copies ran while one was open for 1% of the time, Pallas kernels for 18%

profile of v23, /device:TPU:0, one launch (start us, length us, event | category | flops | bytes accessed | tf_op | source)
XLA Modules:
  0.0 56.4 jit_solution(15842611803287271807)
XLA Ops:
  0.6 4.1 %collective-permute-start = (bf16[256,512]{1,0:T(8,128)(2,1)}, bf16[256,512]{1,0:T(8,128)(2,1)S(1)}, u32[]{:S(2)}, u32[]{:S(2)}) collective-permute-start(bf16[256,512]{1,0:T(8,128)(2,1)} %refs_0_), channel_id=1, source_target_pairs={{0,4},{1,5},{2,6},{3,7},{4,0},{5,1},{6,2},{7,3},{8,12},{9,13},{10,... | collective-permute-start | bytes 786440 | tf_op jit(solution)/shard_map/ppermute | solution.py:256
  4.7 1.5 %collective-permute-start.1 = (bf16[256,512]{1,0:T(8,128)(2,1)}, bf16[256,512]{1,0:T(8,128)(2,1)S(1)}, u32[]{:S(2)}, u32[]{:S(2)}) collective-permute-start(bf16[256,512]{1,0:T(8,128)(2,1)} %refs_0_), channel_id=1, source_target_pairs={{0,16},{1,17},{2,18},{3,19},{4,20},{5,21},{6,22},{7,23},{8,24},{9,... | collective-permute-start | bytes 786440 | tf_op jit(solution)/shard_map/ppermute | solution.py:256
  6.2 0.7 %pad_add_fusion.named_ref = s32[2,256]{1,0:T(2,128)S(1)} fusion(s32[1,256]{1,0:T(1,128)} %bitcast.11, s32[1,256]{1,0:T(1,128)} %bitcast.12), kind=kLoop, calls=%fused_computation | loop fusion | flops 512 | bytes 4096 | tf_op jit(solution)/shard_map/stack | solution.py:337
  7.4 11.7 %all_to_all.12 = s32[32,1,80]{2,1,0:T(1,128)S(1)} all-to-all(s32[32,1,80]{2,1,0:T(1,128)S(1)} %bitcast.10), channel_id=1, replica_groups=mesh['batch'=4,'item'=8] {'batch','item'}, dimensions={0} | all-to-all | bytes 20480 | tf_op jit(solution)/shard_map/all_to_all | solution.py:340
  19.7 0.6 %collective-permute-start.7 = (bf16[256,512]{1,0:T(8,128)(2,1)S(1)}, bf16[256,512]{1,0:T(8,128)(2,1)S(1)}, u32[]{:S(2)}, u32[]{:S(2)}) collective-permute-start(bf16[256,512]{1,0:T(8,128)(2,1)S(1)} %collective-permute-done.refs_0_), channel_id=1, source_target_pairs={{0,16},{1,17},{2,18},{3,19},{4,20},{5,21},{6,22},{7,23},{8,24},{9,... | collective-permute-start | bytes 786440 | tf_op jit(solution)/shard_map/ppermute | solution.py:256
  20.3 0.9 %shard_map.69 = bf16[128,512]{1,0:T(8,128)(2,1)S(1)} custom-call(s32[32,80]{1,0:T(8,128)S(1)} %bitcast.6, bf16[4096,512]{1,0:T(8,128)(2,1)S(1)} %copy-done), custom_call_target="tpu_custom_call" | custom-call | flops 536870912 | bytes 1048576 | tf_op jit(solution)/shard_map/pallas_call | solution.py:245
  21.2 1.6 %shard_map.70 = (bf16[128,512]{1,0:T(8,128)(2,1)S(1)}, bf16[128,512]{1,0:T(8,128)(2,1)S(1)}) custom-call(s32[32,80]{1,0:T(8,128)S(1)} %bitcast.7, bf16[4096,512]{1,0:T(8,128)(2,1)S(1)} %copy-done), custom_call_target="tpu_custom_call" | custom-call | flops 1073741824 | bytes 1048576 | tf_op jit(solution)/shard_map/pallas_call | solution.py:245
  22.8 0.6 %collective-permute-start.5 = (bf16[128,512]{1,0:T(8,128)(2,1)S(1)}, bf16[128,512]{1,0:T(8,128)(2,1)S(1)}, u32[]{:S(2)}, u32[]{:S(2)}) collective-permute-start(bf16[128,512]{1,0:T(8,128)(2,1)S(1)} %get-tuple-element.63), channel_id=1, source_target_pairs={{0,2},{1,3},{2,0},{3,1},{4,6},{5,7},{6,4},{7,5},{8,10},{9,11},{10,... | collective-permute-start | bytes 393224 | tf_op jit(solution)/shard_map/ppermute | solution.py:256
  23.4 0.7 %collective-permute-start.6 = (bf16[128,512]{1,0:T(8,128)(2,1)S(1)}, bf16[128,512]{1,0:T(8,128)(2,1)S(1)}, u32[]{:S(2)}, u32[]{:S(2)}) collective-permute-start(bf16[128,512]{1,0:T(8,128)(2,1)S(1)} %get-tuple-element.64), channel_id=1, source_target_pairs={{0,1},{1,0},{2,3},{3,2},{4,5},{5,4},{6,7},{7,6},{8,9},{9,8},{10,11... | collective-permute-start | bytes 393224 | tf_op jit(solution)/shard_map/ppermute | solution.py:256
  24.1 2.2 %collective-permute-start.4 = (bf16[128,512]{1,0:T(8,128)(2,1)S(1)}, bf16[128,512]{1,0:T(8,128)(2,1)S(1)}, u32[]{:S(2)}, u32[]{:S(2)}) collective-permute-start(bf16[128,512]{1,0:T(8,128)(2,1)S(1)} %shard_map.69), channel_id=1, source_target_pairs={{0,3},{1,2},{2,1},{3,0},{4,7},{5,6},{6,5},{7,4},{8,11},{9,10},{10,... | collective-permute-start | bytes 393224 | tf_op jit(solution)/shard_map/ppermute | solution.py:256
  26.3 0.9 %shard_map.71.refs_0_ = bf16[128,512]{1,0:T(8,128)(2,1)S(1)} custom-call(s32[32,80]{1,0:T(8,128)S(1)} %bitcast.8, bf16[4096,512]{1,0:T(8,128)(2,1)S(1)} %copy-done), custom_call_target="tpu_custom_call" | custom-call | flops 536870912 | bytes 1048576 | tf_op jit(solution)/shard_map/pallas_call | solution.py:245
  27.2 1.0 %shard_map.72 = (s32[512,1]{1,0:T(8,128)S(1)}, bf16[256,512]{1,0:T(8,128)(2,1)S(1)}, bf16[256,512]{1,0:T(8,128)(2,1)S(1)}, bf16[1024,512]{1,0:T(8,128)(2,1)S(1)}, bf16[256,512]{1,0:T(8,128)(2,1)S(1)}) custom-call(s32[32,80]{1,0:T(8,128)S(1)} %bitcast.9, bf16[256,512]{1,0:T(8,128)(2,1)S(1)} %copy-done.2, bf16[256,512]{1,0:T(8,128)(2,1)S(1)} %collective-permute-done.2.refs_1_, ...), custom_call_target="tpu_custom_call" | custom-call | tf_op jit(solution)/shard_map/pallas_call | solution.py:245
  29.2 2.0 %collective-permute-done.6.refs_1_.refs_3_ = bf16[128,512]{1,0:T(8,128)(2,1)S(1)} collective-permute-done((bf16[128,512]{1,0:T(8,128)(2,1)S(1)}, bf16[128,512]{1,0:T(8,128)(2,1)S(1)}, u32[]{:S(2)}, u32[]{:S(2)}) %collective-permute-start.6) | collective-permute-done | bytes 131104 | tf_op jit(solution)/shard_map/ppermute | solution.py:256
  31.2 0.5 shard_map.73
  31.7 0.7 %shard_map.74 = (bf16[1024,512]{1,0:T(8,128)(2,1)S(1)}, bf16[256,512]{1,0:T(8,128)(2,1)S(1)}) custom-call(s32[512,1]{1,0:T(8,128)S(1)} %get-tuple-element.71.place_ref, bf16[256,512]{1,0:T(8,128)(2,1)S(1)} %collective-permute-done.refs_0_, bf16[256,512]{1,0:T(8,128)(2,1)S(1)} %collective-permute-done.8.refs_1_, ...), custom_call_target="tpu_custom_call" | custom-call | tf_op jit(solution)/shard_map/pallas_call | solution.py:245
  32.5 1.7 %shard_map.75 = (bf16[128,512]{1,0:T(8,128)(2,1)S(1)}, bf16[128,512]{1,0:T(8,128)(2,1)S(1)}, bf16[128,512]{1,0:T(8,128)(2,1)S(1)}, bf16[128,512]{1,0:T(8,128)(2,1)S(1)}) custom-call(f32[512,512]{1,0:T(8,128)S(1)} %get-tuple-element.65.hidden_ref, f32[512,1]{1,0:T(8,128)S(1)} %get-tuple-element.66.rscale_ref, ...), custom_call_target="tpu_custom_call" | custom-call | flops 2147483648 | bytes 1048576 | tf_op jit(solution)/shard_map/pallas_call | solution.py:245
  34.2 0.5 shard_map.76
  34.8 1.5 %collective-permute-done.10.refs_1_ = bf16[16,16,512]{2,1,0:T(8,128)(2,1)S(1)} collective-permute-done((bf16[16,16,512]{2,1,0:T(8,128)(2,1)S(1)}, bf16[16,16,512]{2,1,0:T(8,128)(2,1)S(1)}, u32[]{:S(2)}, u32[]{:S(2)}) %collective-permute-start.10) | collective-permute-done | bytes 262176 | tf_op jit(solution)/shard_map/ppermute | solution.py:256
  36.4 1.5 %collective-permute-start.11 = (bf16[8,16,512]{2,1,0:T(8,128)(2,1)S(1)}, bf16[8,16,512]{2,1,0:T(8,128)(2,1)S(1)}, u32[]{:S(2)}, u32[]{:S(2)}) collective-permute-start(bf16[8,16,512]{2,1,0:T(8,128)(2,1)S(1)} %get-tuple-element.84), channel_id=1, source_target_pairs={{0,16},{1,17},{2,18},{3,19},{4,20},{5,21},{6,22},{7,23},{8,24},{9,... | collective-permute-start | bytes 393224 | tf_op jit(solution)/shard_map/ppermute | solution.py:256
  37.9 1.5 %collective-permute-start.15 = (bf16[128,512]{1,0:T(8,128)(2,1)S(1)}, bf16[128,512]{1,0:T(8,128)(2,1)S(1)}, u32[]{:S(2)}, u32[]{:S(2)}) collective-permute-start(bf16[128,512]{1,0:T(8,128)(2,1)S(1)} %get-tuple-element.78.refs_5_), channel_id=1, source_target_pairs={{0,3},{1,2},{2,1},{3,0},{4,7},{5,6},{6,5},{7,4},{8,11},{9,10},{10,... | collective-permute-start | bytes 393224 | tf_op jit(solution)/shard_map/ppermute | solution.py:256
  39.4 1.1 %collective-permute-start.16 = (bf16[128,512]{1,0:T(8,128)(2,1)S(1)}, bf16[128,512]{1,0:T(8,128)(2,1)S(1)}, u32[]{:S(2)}, u32[]{:S(2)}) collective-permute-start(bf16[128,512]{1,0:T(8,128)(2,1)S(1)} %get-tuple-element.79.refs_6_), channel_id=1, source_target_pairs={{0,2},{1,3},{2,0},{3,1},{4,6},{5,7},{6,4},{7,5},{8,10},{9,11},{10,... | collective-permute-start | bytes 393224 | tf_op jit(solution)/shard_map/ppermute | solution.py:256
  40.5 0.9 %collective-permute-start.17 = (bf16[128,512]{1,0:T(8,128)(2,1)S(1)}, bf16[128,512]{1,0:T(8,128)(2,1)S(1)}, u32[]{:S(2)}, u32[]{:S(2)}) collective-permute-start(bf16[128,512]{1,0:T(8,128)(2,1)S(1)} %get-tuple-element.80.refs_7_), channel_id=1, source_target_pairs={{0,1},{1,0},{2,3},{3,2},{4,5},{5,4},{6,7},{7,6},{8,9},{9,8},{10,11... | collective-permute-start | bytes 393224 | tf_op jit(solution)/shard_map/ppermute | solution.py:256
  41.4 0.6 %collective-permute-done.11.refs_1_ = bf16[8,16,512]{2,1,0:T(8,128)(2,1)S(1)} collective-permute-done((bf16[8,16,512]{2,1,0:T(8,128)(2,1)S(1)}, bf16[8,16,512]{2,1,0:T(8,128)(2,1)S(1)}, u32[]{:S(2)}, u32[]{:S(2)}) %collective-permute-start.11) | collective-permute-done | bytes 131104 | tf_op jit(solution)/shard_map/ppermute | solution.py:256
  42.1 1.6 %collective-permute-start.12 = (bf16[2,16,512]{2,1,0:T(8,128)(2,1)S(1)}, bf16[2,16,512]{2,1,0:T(8,128)(2,1)S(1)}, u32[]{:S(2)}, u32[]{:S(2)}) collective-permute-start(bf16[2,16,512]{2,1,0:T(8,128)(2,1)S(1)} %get-tuple-element.86), channel_id=1, source_target_pairs={{0,3},{1,2},{2,1},{3,0},{4,7},{5,6},{6,5},{7,4},{8,11},{9,10},{10,... | collective-permute-start | bytes 98312 | tf_op jit(solution)/shard_map/ppermute | solution.py:256
  43.7 1.0 %collective-permute-start.13 = (bf16[2,16,512]{2,1,0:T(8,128)(2,1)S(1)}, bf16[2,16,512]{2,1,0:T(8,128)(2,1)S(1)}, u32[]{:S(2)}, u32[]{:S(2)}) collective-permute-start(bf16[2,16,512]{2,1,0:T(8,128)(2,1)S(1)} %get-tuple-element.87), channel_id=1, source_target_pairs={{0,2},{1,3},{2,0},{3,1},{4,6},{5,7},{6,4},{7,5},{8,10},{9,11},{10,... | collective-permute-start | bytes 98312 | tf_op jit(solution)/shard_map/ppermute | solution.py:256
  44.7 0.5 collective-permute-done.15.refs_0_
  45.2 1.1 %collective-permute-start.14 = (bf16[2,16,512]{2,1,0:T(8,128)(2,1)S(1)}, bf16[2,16,512]{2,1,0:T(8,128)(2,1)S(1)}, u32[]{:S(2)}, u32[]{:S(2)}) collective-permute-start(bf16[2,16,512]{2,1,0:T(8,128)(2,1)S(1)} %get-tuple-element.88), channel_id=1, source_target_pairs={{0,1},{1,0},{2,3},{3,2},{4,5},{5,4},{6,7},{7,6},{8,9},{9,8},{10,11... | collective-permute-start | bytes 98312 | tf_op jit(solution)/shard_map/ppermute | solution.py:256
  46.3 0.9 %collective-permute-done.16.refs_1_ = bf16[128,512]{1,0:T(8,128)(2,1)S(1)} collective-permute-done((bf16[128,512]{1,0:T(8,128)(2,1)S(1)}, bf16[128,512]{1,0:T(8,128)(2,1)S(1)}, u32[]{:S(2)}, u32[]{:S(2)}) %collective-permute-start.16) | collective-permute-done | bytes 131104 | tf_op jit(solution)/shard_map/ppermute | solution.py:256
  48.1 1.5 %shard_map.80.refs_0_ = bf16[4096,512]{1,0:T(8,128)(2,1)} custom-call(bf16[256,512]{1,0:T(8,128)(2,1)S(1)} %get-tuple-element.59.low_hot_ref, bf16[256,512]{1,0:T(8,128)(2,1)S(1)} %get-tuple-element.60.block_ref, bf16[512,512]{1,0:T(8,128)(2,1)S(1)} %shard_map.79.drow_ref), custom_call_target="tpu_custom_call" | custom-call | tf_op jit(solution)/shard_map/pallas_call | solution.py:269
  49.7 3.4 %collective-permute-start.18 = (f32[1,16,512]{2,1,0:T(8,128)S(1)}, f32[1,16,512]{2,1,0:T(8,128)S(1)}, u32[]{:S(2)}, u32[]{:S(2)}) collective-permute-start(f32[1,16,512]{2,1,0:T(8,128)S(1)} %get-tuple-element.96), channel_id=1, source_target_pairs={{0,4},{1,5},{2,6},{3,7},{4,0},{5,1},{6,2},{7,3},{8,12},{9,13},{10,... | collective-permute-start | bytes 98312 | tf_op jit(solution)/shard_map/ppermute | solution.py:256
  53.1 2.7 %shard_map.81 = bf16[4096,512]{1,0:T(8,128)(2,1)} custom-call(bf16[256,512]{1,0:T(8,128)(2,1)S(1)} %get-tuple-element.59.low_hot_ref, bf16[256,512]{1,0:T(8,128)(2,1)S(1)} %get-tuple-element.60.block_ref, bf16[512,512]{1,0:T(8,128)(2,1)S(1)} %shard_map.79.drow_ref, bf16[4096,512]{1,0:T(8,128)(2,1)} %shard_map.80.refs_0_), custom_call_target="tpu_custom_call", output_to_operand_aliasing={{}: (3, {})} | custom-call | flops 2147483648 | bytes 3145728 | tf_op jit(solution)/shard_map/pallas_call | solution.py:269
  55.8 0.6 %shard_map.83 = f32[16,512]{1,0:T(8,128)} custom-call(f32[1,16,512]{2,1,0:T(8,128)S(1)} %get-tuple-element.98.refs_0_, f32[1,16,512]{2,1,0:T(8,128)S(1)} %collective-permute-done.18.refs_1_), custom_call_target="tpu_custom_call" | custom-call | bytes 1048576 | tf_op jit(solution)/shard_map/pallas_call | solution.py:245
  (30 shorter events, 3.0 us)
Async XLA Ops:
  0.6 18.4 %collective-permute-start = (bf16[256,512]{1,0:T(8,128)(2,1)}, bf16[256,512]{1,0:T(8,128)(2,1)S(1)}, u32[]{:S(2)}, u32[]{:S(2)}) collective-permute-start(bf16[256,512]{1,0:T(8,128)(2,1)} %refs_0_), channel_id=1, source_target_pairs={{0,4},{1,5},{2,6},{3,7},{4,0},{5,1},{6,2},{7,3},{8,12},{9,13},{10,... | collective-permute-start | bytes 786440 | tf_op jit(solution)/shard_map/ppermute | solution.py:256
  4.7 14.4 %collective-permute-start.1 = (bf16[256,512]{1,0:T(8,128)(2,1)}, bf16[256,512]{1,0:T(8,128)(2,1)S(1)}, u32[]{:S(2)}, u32[]{:S(2)}) collective-permute-start(bf16[256,512]{1,0:T(8,128)(2,1)} %refs_0_), channel_id=1, source_target_pairs={{0,16},{1,17},{2,18},{3,19},{4,20},{5,21},{6,22},{7,23},{8,24},{9,... | collective-permute-start | bytes 786440 | tf_op jit(solution)/shard_map/ppermute | solution.py:256
  6.9 12.2 %copy-start.2 = (bf16[256,512]{1,0:T(8,128)(2,1)S(1)}, bf16[256,512]{1,0:T(8,128)(2,1)}, u32[]{:S(2)}) copy-start(bf16[256,512]{1,0:T(8,128)(2,1)} %refs_0_) | copy-start | bytes 786436
  6.9 13.3 %copy-start = (bf16[4096,512]{1,0:T(8,128)(2,1)S(1)}, bf16[4096,512]{1,0:T(8,128)(2,1)}, u32[]{:S(2)}) copy-start(bf16[4096,512]{1,0:T(8,128)(2,1)} %table_ref.5) | copy-start | bytes 12582916
  19.1 5.1 %collective-permute-start.2 = (bf16[256,512]{1,0:T(8,128)(2,1)S(1)}, bf16[256,512]{1,0:T(8,128)(2,1)S(1)}, u32[]{:S(2)}, u32[]{:S(2)}) collective-permute-start(bf16[256,512]{1,0:T(8,128)(2,1)S(1)} %copy-done.2), channel_id=1, source_target_pairs={{0,8},{1,9},{2,10},{3,11},{4,12},{5,13},{6,14},{7,15},{8,0},{9,1},... | collective-permute-start | bytes 786440 | tf_op jit(solution)/shard_map/ppermute | solution.py:256
  19.2 8.1 %collective-permute-start.3 = (bf16[256,512]{1,0:T(8,128)(2,1)S(1)}, bf16[256,512]{1,0:T(8,128)(2,1)S(1)}, u32[]{:S(2)}, u32[]{:S(2)}) collective-permute-start(bf16[256,512]{1,0:T(8,128)(2,1)S(1)} %collective-permute-done.1.refs_2_), channel_id=1, source_target_pairs={{0,8},{1,9},{2,10},{3,11},{4,12},{5,13},{6,14},{7,15},{8,0},{9,1},... | collective-permute-start | bytes 786440 | tf_op jit(solution)/shard_map/ppermute | solution.py:256
  19.7 8.6 %collective-permute-start.7 = (bf16[256,512]{1,0:T(8,128)(2,1)S(1)}, bf16[256,512]{1,0:T(8,128)(2,1)S(1)}, u32[]{:S(2)}, u32[]{:S(2)}) collective-permute-start(bf16[256,512]{1,0:T(8,128)(2,1)S(1)} %collective-permute-done.refs_0_), channel_id=1, source_target_pairs={{0,16},{1,17},{2,18},{3,19},{4,20},{5,21},{6,22},{7,23},{8,24},{9,... | collective-permute-start | bytes 786440 | tf_op jit(solution)/shard_map/ppermute | solution.py:256
  21.2 10.0 %copy-start.1 = (bf16[512,512]{1,0:T(8,128)(2,1)S(1)}, bf16[512,512]{1,0:T(8,128)(2,1)}, u32[]{:S(2)}) copy-start(bf16[512,512]{1,0:T(8,128)(2,1)} %weight_ref.3) | copy-start | bytes 1572868
  22.8 6.5 %collective-permute-start.5 = (bf16[128,512]{1,0:T(8,128)(2,1)S(1)}, bf16[128,512]{1,0:T(8,128)(2,1)S(1)}, u32[]{:S(2)}, u32[]{:S(2)}) collective-permute-start(bf16[128,512]{1,0:T(8,128)(2,1)S(1)} %get-tuple-element.63), channel_id=1, source_target_pairs={{0,2},{1,3},{2,0},{3,1},{4,6},{5,7},{6,4},{7,5},{8,10},{9,11},{10,... | collective-permute-start | bytes 393224 | tf_op jit(solution)/shard_map/ppermute | solution.py:256
  23.4 7.8 %collective-permute-start.6 = (bf16[128,512]{1,0:T(8,128)(2,1)S(1)}, bf16[128,512]{1,0:T(8,128)(2,1)S(1)}, u32[]{:S(2)}, u32[]{:S(2)}) collective-permute-start(bf16[128,512]{1,0:T(8,128)(2,1)S(1)} %get-tuple-element.64), channel_id=1, source_target_pairs={{0,1},{1,0},{2,3},{3,2},{4,5},{5,4},{6,7},{7,6},{8,9},{9,8},{10,11... | collective-permute-start | bytes 393224 | tf_op jit(solution)/shard_map/ppermute | solution.py:256
  24.1 7.0 %collective-permute-start.4 = (bf16[128,512]{1,0:T(8,128)(2,1)S(1)}, bf16[128,512]{1,0:T(8,128)(2,1)S(1)}, u32[]{:S(2)}, u32[]{:S(2)}) collective-permute-start(bf16[128,512]{1,0:T(8,128)(2,1)S(1)} %shard_map.69), channel_id=1, source_target_pairs={{0,3},{1,2},{2,1},{3,0},{4,7},{5,6},{6,5},{7,4},{8,11},{9,10},{10,... | collective-permute-start | bytes 393224 | tf_op jit(solution)/shard_map/ppermute | solution.py:256
  28.3 3.4 %collective-permute-start.8 = (bf16[256,512]{1,0:T(8,128)(2,1)S(1)}, bf16[256,512]{1,0:T(8,128)(2,1)S(1)}, u32[]{:S(2)}, u32[]{:S(2)}) collective-permute-start(bf16[256,512]{1,0:T(8,128)(2,1)S(1)} %collective-permute-done.refs_0_), channel_id=1, source_target_pairs={{0,8},{1,9},{2,10},{3,11},{4,12},{5,13},{6,14},{7,15},{8,0},{9,1},... | collective-permute-start | bytes 786440 | tf_op jit(solution)/shard_map/ppermute | solution.py:256
  28.4 3.4 %collective-permute-start.9 = (bf16[256,512]{1,0:T(8,128)(2,1)S(1)}, bf16[256,512]{1,0:T(8,128)(2,1)S(1)}, u32[]{:S(2)}, u32[]{:S(2)}) collective-permute-start(bf16[256,512]{1,0:T(8,128)(2,1)S(1)} %collective-permute-done.7.refs_2_), channel_id=1, source_target_pairs={{0,8},{1,9},{2,10},{3,11},{4,12},{5,13},{6,14},{7,15},{8,0},{9,1},... | collective-permute-start | bytes 786440 | tf_op jit(solution)/shard_map/ppermute | solution.py:256
  34.7 1.6 %collective-permute-start.10 = (bf16[16,16,512]{2,1,0:T(8,128)(2,1)S(1)}, bf16[16,16,512]{2,1,0:T(8,128)(2,1)S(1)}, u32[]{:S(2)}, u32[]{:S(2)}) collective-permute-start(bf16[16,16,512]{2,1,0:T(8,128)(2,1)S(1)} %get-tuple-element.82), channel_id=1, source_target_pairs={{0,8},{1,9},{2,10},{3,11},{4,12},{5,13},{6,14},{7,15},{8,0},{9,1},... | collective-permute-start | bytes 786440 | tf_op jit(solution)/shard_map/ppermute | solution.py:256
  36.4 5.6 %collective-permute-start.11 = (bf16[8,16,512]{2,1,0:T(8,128)(2,1)S(1)}, bf16[8,16,512]{2,1,0:T(8,128)(2,1)S(1)}, u32[]{:S(2)}, u32[]{:S(2)}) collective-permute-start(bf16[8,16,512]{2,1,0:T(8,128)(2,1)S(1)} %get-tuple-element.84), channel_id=1, source_target_pairs={{0,16},{1,17},{2,18},{3,19},{4,20},{5,21},{6,22},{7,23},{8,24},{9,... | collective-permute-start | bytes 393224 | tf_op jit(solution)/shard_map/ppermute | solution.py:256
  37.9 7.3 %collective-permute-start.15 = (bf16[128,512]{1,0:T(8,128)(2,1)S(1)}, bf16[128,512]{1,0:T(8,128)(2,1)S(1)}, u32[]{:S(2)}, u32[]{:S(2)}) collective-permute-start(bf16[128,512]{1,0:T(8,128)(2,1)S(1)} %get-tuple-element.78.refs_5_), channel_id=1, source_target_pairs={{0,3},{1,2},{2,1},{3,0},{4,7},{5,6},{6,5},{7,4},{8,11},{9,10},{10,... | collective-permute-start | bytes 393224 | tf_op jit(solution)/shard_map/ppermute | solution.py:256
  39.4 7.8 %collective-permute-start.16 = (bf16[128,512]{1,0:T(8,128)(2,1)S(1)}, bf16[128,512]{1,0:T(8,128)(2,1)S(1)}, u32[]{:S(2)}, u32[]{:S(2)}) collective-permute-start(bf16[128,512]{1,0:T(8,128)(2,1)S(1)} %get-tuple-element.79.refs_6_), channel_id=1, source_target_pairs={{0,2},{1,3},{2,0},{3,1},{4,6},{5,7},{6,4},{7,5},{8,10},{9,11},{10,... | collective-permute-start | bytes 393224 | tf_op jit(solution)/shard_map/ppermute | solution.py:256
  40.5 7.1 %collective-permute-start.17 = (bf16[128,512]{1,0:T(8,128)(2,1)S(1)}, bf16[128,512]{1,0:T(8,128)(2,1)S(1)}, u32[]{:S(2)}, u32[]{:S(2)}) collective-permute-start(bf16[128,512]{1,0:T(8,128)(2,1)S(1)} %get-tuple-element.80.refs_7_), channel_id=1, source_target_pairs={{0,1},{1,0},{2,3},{3,2},{4,5},{5,4},{6,7},{7,6},{8,9},{9,8},{10,11... | collective-permute-start | bytes 393224 | tf_op jit(solution)/shard_map/ppermute | solution.py:256
  42.1 7.5 %collective-permute-start.12 = (bf16[2,16,512]{2,1,0:T(8,128)(2,1)S(1)}, bf16[2,16,512]{2,1,0:T(8,128)(2,1)S(1)}, u32[]{:S(2)}, u32[]{:S(2)}) collective-permute-start(bf16[2,16,512]{2,1,0:T(8,128)(2,1)S(1)} %get-tuple-element.86), channel_id=1, source_target_pairs={{0,3},{1,2},{2,1},{3,0},{4,7},{5,6},{6,5},{7,4},{8,11},{9,10},{10,... | collective-permute-start | bytes 98312 | tf_op jit(solution)/shard_map/ppermute | solution.py:256
  43.7 5.9 %collective-permute-start.13 = (bf16[2,16,512]{2,1,0:T(8,128)(2,1)S(1)}, bf16[2,16,512]{2,1,0:T(8,128)(2,1)S(1)}, u32[]{:S(2)}, u32[]{:S(2)}) collective-permute-start(bf16[2,16,512]{2,1,0:T(8,128)(2,1)S(1)} %get-tuple-element.87), channel_id=1, source_target_pairs={{0,2},{1,3},{2,0},{3,1},{4,6},{5,7},{6,4},{7,5},{8,10},{9,11},{10,... | collective-permute-start | bytes 98312 | tf_op jit(solution)/shard_map/ppermute | solution.py:256
  45.2 4.4 %collective-permute-start.14 = (bf16[2,16,512]{2,1,0:T(8,128)(2,1)S(1)}, bf16[2,16,512]{2,1,0:T(8,128)(2,1)S(1)}, u32[]{:S(2)}, u32[]{:S(2)}) collective-permute-start(bf16[2,16,512]{2,1,0:T(8,128)(2,1)S(1)} %get-tuple-element.88), channel_id=1, source_target_pairs={{0,1},{1,0},{2,3},{3,2},{4,5},{5,4},{6,7},{7,6},{8,9},{9,8},{10,11... | collective-permute-start | bytes 98312 | tf_op jit(solution)/shard_map/ppermute | solution.py:256
  49.7 6.1 %collective-permute-start.18 = (f32[1,16,512]{2,1,0:T(8,128)S(1)}, f32[1,16,512]{2,1,0:T(8,128)S(1)}, u32[]{:S(2)}, u32[]{:S(2)}) collective-permute-start(f32[1,16,512]{2,1,0:T(8,128)S(1)} %get-tuple-element.96), channel_id=1, source_target_pairs={{0,4},{1,5},{2,6},{3,7},{4,0},{5,1},{6,2},{7,3},{8,12},{9,13},{10,... | collective-permute-start | bytes 98312 | tf_op jit(solution)/shard_map/ppermute | solution.py:256

commit v24 on v22

--- a/solution.py
+++ b/solution.py
@@ -151,8 +151,13 @@
         item_ref[here] = (hidden * (rscale * (1.0 / width**0.5))).astype(bf16)
 
 
-def main_kernel(levels, hidden_ref, rscale_ref, item_ref, *refs):
-    units, owns, outs = refs[:levels], refs[levels : 2 * levels], refs[2 * levels :]
+def main_kernel(levels, near, place_ref, hidden_ref, rscale_ref, item_ref, *refs):
+    later = levels - 1
+    units, owns = refs[0:1] + refs[len(refs) - 2 * later : len(refs) - later], refs[1:2] + refs[len(refs) - later :]
+    users, outs = refs[2 : len(refs) - 2 * later - near], refs[len(refs) - 2 * later - near : len(refs) - 2 * later]
+    for level in range(1, levels):
+        few = len(users) // later
+        users_kernel(level, near, place_ref, *users[(level - 1) * few : level * few], units[level], owns[level])
     total, width = hidden_ref.shape
     size = outs[0].shape[0] // levels
     root = 1.0 / width**0.5
@@ -367,13 +372,6 @@
     late = {mask: users[mask] for mask in users if mask & (n_item - near)}
     place, late = lax.optimization_barrier((place, late))
     users |= late | {mask + n_item: swap(late[mask], n_item) for mask in late}
-    units, owns = zip(
-        first,
-        *[
-            call(functools.partial(users_kernel, level, near), group_outs, place, *group(level), free=True)
-            for level in range(1, levels)
-        ],
-    )
     hidden = call(
         functools.partial(hidden_kernel, levels),
         [((total, width), f32), ((total, 1), f32), ((total, width), bf16)],
@@ -382,13 +380,15 @@
         flops=1 << 34,
     )
     dhidden = call(
-        functools.partial(main_kernel, levels),
+        functools.partial(main_kernel, levels, near),
         [((size, width), bf16)] * near,
+        place,
         *hidden,
-        *units,
-        *owns,
+        *first,
+        *[value for level in range(1, levels) for value in group(level)],
         flops=1 << 31,
         mib=40,
+        scratch=[pltpu.VMEM(shape, kind) for shape, kind in group_outs[:1] * (levels - 1) + group_outs[1:] * (levels - 1)],
     )
     incoming = [swap(dhidden[part], part) for part in range(1, near)]
     (drow,) = call(row_kernel, [((total, width), bf16)], tower_weight, *reversed(incoming), dhidden[0], free=True)

time: 54.9 us -> 54.6 us (level)
    pallas_call x14 -> x13, Pallas kernels: 9.56 us -> 9.34 us  [call(): pl.pallas_call(kernel, out_shape=[jax.ShapeDtypeStruct(shape, dtype) for...]
where the time goes in v24:
time: 54.6 us; the launch traced here: 54.4 us
  starting transfers between devices  22 us (40%)
  Pallas kernels  12.6 us (23%)
  blocking collectives  11.7 us (21%)
  waiting for transfers between devices  6.57 us (12%)
  between operations  0.82 us (2%)
  other arithmetic  0.7 us (1%)
    ppermute x19, starting transfers between devices, swap(): lax.ppermute(value, ('batch', 'item'), [(k, k ^ mask) for k in range(devi...  22 us
    all_to_all x1, blocking collectives, local(): lax.all_to_all(request, ('batch', 'item'), split_axis=0, concat_axis=0, t...  11.7 us
    pallas_call x13, Pallas kernels, call(): pl.pallas_call(kernel, out_shape=[jax.ShapeDtypeStruct(shape, dtype) for...  9.34 us
    ppermute x19, waiting for transfers between devices, swap(): lax.ppermute(value, ('batch', 'item'), [(k, k ^ mask) for k in range(devi...  6.57 us
    pallas_call x1, Pallas kernels, local(): pl.pallas_call(functools.partial(table_kernel, sizes), out_specs=pl.Block...  3.25 us
  transfers between devices with their start and end apart: 19, of which 8 were waited for; matrix products, arithmetic and copies ran while one was open for 1% of the time, Pallas kernels for 17%

profile of v24, /device:TPU:0, one launch (start us, length us, event | category | flops | bytes accessed | tf_op | source)
XLA Modules:
  0.0 54.4 jit_solution(1140252528339313304)
XLA Ops:
  0.6 4.1 %collective-permute-start = (bf16[256,512]{1,0:T(8,128)(2,1)}, bf16[256,512]{1,0:T(8,128)(2,1)S(1)}, u32[]{:S(2)}, u32[]{:S(2)}) collective-permute-start(bf16[256,512]{1,0:T(8,128)(2,1)} %refs_0_), channel_id=1, source_target_pairs={{0,4},{1,5},{2,6},{3,7},{4,0},{5,1},{6,2},{7,3},{8,12},{9,13},{10,... | collective-permute-start | bytes 786440 | tf_op jit(solution)/shard_map/ppermute | solution.py:260
  4.7 1.5 %collective-permute-start.1 = (bf16[256,512]{1,0:T(8,128)(2,1)}, bf16[256,512]{1,0:T(8,128)(2,1)S(1)}, u32[]{:S(2)}, u32[]{:S(2)}) collective-permute-start(bf16[256,512]{1,0:T(8,128)(2,1)} %refs_0_), channel_id=1, source_target_pairs={{0,16},{1,17},{2,18},{3,19},{4,20},{5,21},{6,22},{7,23},{8,24},{9,... | collective-permute-start | bytes 786440 | tf_op jit(solution)/shard_map/ppermute | solution.py:260
  6.2 0.7 %pad_add_fusion.named_ref = s32[2,256]{1,0:T(2,128)S(1)} fusion(s32[1,256]{1,0:T(1,128)} %bitcast.11, s32[1,256]{1,0:T(1,128)} %bitcast.12), kind=kLoop, calls=%fused_computation | loop fusion | flops 512 | bytes 4096 | tf_op jit(solution)/shard_map/stack | solution.py:327
  7.4 11.7 %all_to_all.12 = s32[32,1,80]{2,1,0:T(1,128)S(1)} all-to-all(s32[32,1,80]{2,1,0:T(1,128)S(1)} %bitcast.10), channel_id=1, replica_groups=mesh['batch'=4,'item'=8] {'batch','item'}, dimensions={0} | all-to-all | bytes 20480 | tf_op jit(solution)/shard_map/all_to_all | solution.py:330
  19.7 0.6 %collective-permute-start.7 = (bf16[256,512]{1,0:T(8,128)(2,1)S(1)}, bf16[256,512]{1,0:T(8,128)(2,1)S(1)}, u32[]{:S(2)}, u32[]{:S(2)}) collective-permute-start(bf16[256,512]{1,0:T(8,128)(2,1)S(1)} %collective-permute-done.refs_2_), channel_id=1, source_target_pairs={{0,16},{1,17},{2,18},{3,19},{4,20},{5,21},{6,22},{7,23},{8,24},{9,... | collective-permute-start | bytes 786440 | tf_op jit(solution)/shard_map/ppermute | solution.py:260
  20.3 0.9 %shard_map.69 = bf16[128,512]{1,0:T(8,128)(2,1)S(1)} custom-call(s32[32,80]{1,0:T(8,128)S(1)} %bitcast.6, bf16[4096,512]{1,0:T(8,128)(2,1)S(1)} %copy-done), custom_call_target="tpu_custom_call" | custom-call | flops 536870912 | bytes 1048576 | tf_op jit(solution)/shard_map/pallas_call | solution.py:249
  21.2 0.8 %collective-permute-start.4 = (bf16[128,512]{1,0:T(8,128)(2,1)S(1)}, bf16[128,512]{1,0:T(8,128)(2,1)S(1)}, u32[]{:S(2)}, u32[]{:S(2)}) collective-permute-start(bf16[128,512]{1,0:T(8,128)(2,1)S(1)} %shard_map.69), channel_id=1, source_target_pairs={{0,3},{1,2},{2,1},{3,0},{4,7},{5,6},{6,5},{7,4},{8,11},{9,10},{10,... | collective-permute-start | bytes 393224 | tf_op jit(solution)/shard_map/ppermute | solution.py:260
  22.0 1.6 %shard_map.70 = (bf16[128,512]{1,0:T(8,128)(2,1)S(1)}, bf16[128,512]{1,0:T(8,128)(2,1)S(1)}) custom-call(s32[32,80]{1,0:T(8,128)S(1)} %bitcast.7, bf16[4096,512]{1,0:T(8,128)(2,1)S(1)} %copy-done), custom_call_target="tpu_custom_call" | custom-call | flops 1073741824 | bytes 1048576 | tf_op jit(solution)/shard_map/pallas_call | solution.py:249
  23.6 1.4 %collective-permute-start.5 = (bf16[128,512]{1,0:T(8,128)(2,1)S(1)}, bf16[128,512]{1,0:T(8,128)(2,1)S(1)}, u32[]{:S(2)}, u32[]{:S(2)}) collective-permute-start(bf16[128,512]{1,0:T(8,128)(2,1)S(1)} %get-tuple-element.60), channel_id=1, source_target_pairs={{0,2},{1,3},{2,0},{3,1},{4,6},{5,7},{6,4},{7,5},{8,10},{9,11},{10,... | collective-permute-start | bytes 393224 | tf_op jit(solution)/shard_map/ppermute | solution.py:260
  25.0 1.4 %collective-permute-start.6 = (bf16[128,512]{1,0:T(8,128)(2,1)S(1)}, bf16[128,512]{1,0:T(8,128)(2,1)S(1)}, u32[]{:S(2)}, u32[]{:S(2)}) collective-permute-start(bf16[128,512]{1,0:T(8,128)(2,1)S(1)} %get-tuple-element.61), channel_id=1, source_target_pairs={{0,1},{1,0},{2,3},{3,2},{4,5},{5,4},{6,7},{7,6},{8,9},{9,8},{10,11... | collective-permute-start | bytes 393224 | tf_op jit(solution)/shard_map/ppermute | solution.py:260
  26.4 0.9 %shard_map.71.refs_0_ = bf16[128,512]{1,0:T(8,128)(2,1)S(1)} custom-call(s32[32,80]{1,0:T(8,128)S(1)} %bitcast.8, bf16[4096,512]{1,0:T(8,128)(2,1)S(1)} %copy-done), custom_call_target="tpu_custom_call" | custom-call | flops 536870912 | bytes 1048576 | tf_op jit(solution)/shard_map/pallas_call | solution.py:249
  27.3 1.0 %shard_map.72 = (s32[512,1]{1,0:T(8,128)S(1)}, bf16[256,512]{1,0:T(8,128)(2,1)S(1)}, bf16[256,512]{1,0:T(8,128)(2,1)S(1)}, bf16[1024,512]{1,0:T(8,128)(2,1)S(1)}, bf16[256,512]{1,0:T(8,128)(2,1)S(1)}) custom-call(s32[32,80]{1,0:T(8,128)S(1)} %bitcast.9, bf16[256,512]{1,0:T(8,128)(2,1)S(1)} %copy-done.2, bf16[256,512]{1,0:T(8,128)(2,1)S(1)} %collective-permute-done.2.refs_1_, ...), custom_call_target="tpu_custom_call" | custom-call | tf_op jit(solution)/shard_map/pallas_call | solution.py:249
  28.4 0.5 collective-permute-start.9
  29.4 1.0 %collective-permute-done.6.refs_1_.refs_3_ = bf16[128,512]{1,0:T(8,128)(2,1)S(1)} collective-permute-done((bf16[128,512]{1,0:T(8,128)(2,1)S(1)}, bf16[128,512]{1,0:T(8,128)(2,1)S(1)}, u32[]{:S(2)}, u32[]{:S(2)}) %collective-permute-start.6) | collective-permute-done | bytes 131104 | tf_op jit(solution)/shard_map/ppermute | solution.py:260
  30.4 0.5 shard_map.73
  30.9 2.2 %shard_map.74 = (bf16[128,512]{1,0:T(8,128)(2,1)S(1)}, bf16[128,512]{1,0:T(8,128)(2,1)S(1)}, bf16[128,512]{1,0:T(8,128)(2,1)S(1)}, bf16[128,512]{1,0:T(8,128)(2,1)S(1)}) custom-call(s32[512,1]{1,0:T(8,128)S(1)} %get-tuple-element.64.place_ref, f32[512,512]{1,0:T(8,128)S(1)} %get-tuple-element.65.hidden_ref, f32[512,1]{1,0:T(8,128)S(1)} %get-tuple-element.66.rscale_ref, ...), custom_call_target="tpu_custom_call" | custom-call | flops 2147483648 | bytes 1048576 | tf_op jit(solution)/shard_map/pallas_call | solution.py:249
  33.1 0.5 shard_map.75
  33.7 1.5 %collective-permute-done.10.refs_1_ = bf16[16,16,512]{2,1,0:T(8,128)(2,1)S(1)} collective-permute-done((bf16[16,16,512]{2,1,0:T(8,128)(2,1)S(1)}, bf16[16,16,512]{2,1,0:T(8,128)(2,1)S(1)}, u32[]{:S(2)}, u32[]{:S(2)}) %collective-permute-start.10) | collective-permute-done | bytes 262176 | tf_op jit(solution)/shard_map/ppermute | solution.py:260
  35.4 1.4 %collective-permute-start.11 = (bf16[8,16,512]{2,1,0:T(8,128)(2,1)S(1)}, bf16[8,16,512]{2,1,0:T(8,128)(2,1)S(1)}, u32[]{:S(2)}, u32[]{:S(2)}) collective-permute-start(bf16[8,16,512]{2,1,0:T(8,128)(2,1)S(1)} %get-tuple-element.79), channel_id=1, source_target_pairs={{0,16},{1,17},{2,18},{3,19},{4,20},{5,21},{6,22},{7,23},{8,24},{9,... | collective-permute-start | bytes 393224 | tf_op jit(solution)/shard_map/ppermute | solution.py:260
  36.8 1.1 %collective-permute-start.15 = (bf16[128,512]{1,0:T(8,128)(2,1)S(1)}, bf16[128,512]{1,0:T(8,128)(2,1)S(1)}, u32[]{:S(2)}, u32[]{:S(2)}) collective-permute-start(bf16[128,512]{1,0:T(8,128)(2,1)S(1)} %get-tuple-element.73.refs_5_), channel_id=1, source_target_pairs={{0,3},{1,2},{2,1},{3,0},{4,7},{5,6},{6,5},{7,4},{8,11},{9,10},{10,... | collective-permute-start | bytes 393224 | tf_op jit(solution)/shard_map/ppermute | solution.py:260
  37.9 1.4 %collective-permute-start.16 = (bf16[128,512]{1,0:T(8,128)(2,1)S(1)}, bf16[128,512]{1,0:T(8,128)(2,1)S(1)}, u32[]{:S(2)}, u32[]{:S(2)}) collective-permute-start(bf16[128,512]{1,0:T(8,128)(2,1)S(1)} %get-tuple-element.74.refs_6_), channel_id=1, source_target_pairs={{0,2},{1,3},{2,0},{3,1},{4,6},{5,7},{6,4},{7,5},{8,10},{9,11},{10,... | collective-permute-start | bytes 393224 | tf_op jit(solution)/shard_map/ppermute | solution.py:260
  39.3 1.0 %collective-permute-start.17 = (bf16[128,512]{1,0:T(8,128)(2,1)S(1)}, bf16[128,512]{1,0:T(8,128)(2,1)S(1)}, u32[]{:S(2)}, u32[]{:S(2)}) collective-permute-start(bf16[128,512]{1,0:T(8,128)(2,1)S(1)} %get-tuple-element.75.refs_7_), channel_id=1, source_target_pairs={{0,1},{1,0},{2,3},{3,2},{4,5},{5,4},{6,7},{7,6},{8,9},{9,8},{10,11... | collective-permute-start | bytes 393224 | tf_op jit(solution)/shard_map/ppermute | solution.py:260
  40.3 0.7 %collective-permute-done.11.refs_1_ = bf16[8,16,512]{2,1,0:T(8,128)(2,1)S(1)} collective-permute-done((bf16[8,16,512]{2,1,0:T(8,128)(2,1)S(1)}, bf16[8,16,512]{2,1,0:T(8,128)(2,1)S(1)}, u32[]{:S(2)}, u32[]{:S(2)}) %collective-permute-start.11) | collective-permute-done | bytes 131104 | tf_op jit(solution)/shard_map/ppermute | solution.py:260
  41.0 1.1 %collective-permute-start.12 = (bf16[2,16,512]{2,1,0:T(8,128)(2,1)S(1)}, bf16[2,16,512]{2,1,0:T(8,128)(2,1)S(1)}, u32[]{:S(2)}, u32[]{:S(2)}) collective-permute-start(bf16[2,16,512]{2,1,0:T(8,128)(2,1)S(1)} %get-tuple-element.81), channel_id=1, source_target_pairs={{0,3},{1,2},{2,1},{3,0},{4,7},{5,6},{6,5},{7,4},{8,11},{9,10},{10,... | collective-permute-start | bytes 98312 | tf_op jit(solution)/shard_map/ppermute | solution.py:260
  42.1 1.4 %collective-permute-start.13 = (bf16[2,16,512]{2,1,0:T(8,128)(2,1)S(1)}, bf16[2,16,512]{2,1,0:T(8,128)(2,1)S(1)}, u32[]{:S(2)}, u32[]{:S(2)}) collective-permute-start(bf16[2,16,512]{2,1,0:T(8,128)(2,1)S(1)} %get-tuple-element.82), channel_id=1, source_target_pairs={{0,2},{1,3},{2,0},{3,1},{4,6},{5,7},{6,4},{7,5},{8,10},{9,11},{10,... | collective-permute-start | bytes 98312 | tf_op jit(solution)/shard_map/ppermute | solution.py:260
  43.5 0.5 %collective-permute-done.15.refs_0_ = bf16[128,512]{1,0:T(8,128)(2,1)S(1)} collective-permute-done((bf16[128,512]{1,0:T(8,128)(2,1)S(1)}, bf16[128,512]{1,0:T(8,128)(2,1)S(1)}, u32[]{:S(2)}, u32[]{:S(2)}) %collective-permute-start.15) | collective-permute-done | bytes 131104 | tf_op jit(solution)/shard_map/ppermute | solution.py:260
  44.1 1.1 %collective-permute-start.14 = (bf16[2,16,512]{2,1,0:T(8,128)(2,1)S(1)}, bf16[2,16,512]{2,1,0:T(8,128)(2,1)S(1)}, u32[]{:S(2)}, u32[]{:S(2)}) collective-permute-start(bf16[2,16,512]{2,1,0:T(8,128)(2,1)S(1)} %get-tuple-element.83), channel_id=1, source_target_pairs={{0,1},{1,0},{2,3},{3,2},{4,5},{5,4},{6,7},{7,6},{8,9},{9,8},{10,11... | collective-permute-start | bytes 98312 | tf_op jit(solution)/shard_map/ppermute | solution.py:260
  45.2 0.9 %collective-permute-done.16.refs_1_ = bf16[128,512]{1,0:T(8,128)(2,1)S(1)} collective-permute-done((bf16[128,512]{1,0:T(8,128)(2,1)S(1)}, bf16[128,512]{1,0:T(8,128)(2,1)S(1)}, u32[]{:S(2)}, u32[]{:S(2)}) %collective-permute-start.16) | collective-permute-done | bytes 131104 | tf_op jit(solution)/shard_map/ppermute | solution.py:260
  47.0 1.0 %collective-permute-done.14.refs_3_ = bf16[2,16,512]{2,1,0:T(8,128)(2,1)S(1)} collective-permute-done((bf16[2,16,512]{2,1,0:T(8,128)(2,1)S(1)}, bf16[2,16,512]{2,1,0:T(8,128)(2,1)S(1)}, u32[]{:S(2)}, u32[]{:S(2)}) %collective-permute-start.14) | collective-permute-done | bytes 32800 | tf_op jit(solution)/shard_map/ppermute | solution.py:260
  48.0 2.5 %collective-permute-start.18 = (f32[1,16,512]{2,1,0:T(8,128)S(1)}, f32[1,16,512]{2,1,0:T(8,128)S(1)}, u32[]{:S(2)}, u32[]{:S(2)}) collective-permute-start(f32[1,16,512]{2,1,0:T(8,128)S(1)} %get-tuple-element.90), channel_id=1, source_target_pairs={{0,4},{1,5},{2,6},{3,7},{4,0},{5,1},{6,2},{7,3},{8,12},{9,13},{10,... | collective-permute-start | bytes 98312 | tf_op jit(solution)/shard_map/ppermute | solution.py:260
  50.5 3.3 %shard_map.79 = bf16[4096,512]{1,0:T(8,128)(2,1)} custom-call(bf16[256,512]{1,0:T(8,128)(2,1)S(1)} %get-tuple-element.56.low_hot_ref, bf16[256,512]{1,0:T(8,128)(2,1)S(1)} %get-tuple-element.57.block_ref, bf16[512,512]{1,0:T(8,128)(2,1)S(1)} %shard_map.78.drow_ref), custom_call_target="tpu_custom_call" | custom-call | flops 2147483648 | bytes 4194304 | tf_op jit(solution)/shard_map/pallas_call | solution.py:397
  53.8 0.6 %shard_map.81 = f32[16,512]{1,0:T(8,128)} custom-call(f32[1,16,512]{2,1,0:T(8,128)S(1)} %get-tuple-element.92.refs_0_, f32[1,16,512]{2,1,0:T(8,128)S(1)} %collective-permute-done.18.refs_1_), custom_call_target="tpu_custom_call" | custom-call | bytes 1048576 | tf_op jit(solution)/shard_map/pallas_call | solution.py:249
  (28 shorter events, 2.7 us)
Async XLA Ops:
  0.6 18.4 %collective-permute-start = (bf16[256,512]{1,0:T(8,128)(2,1)}, bf16[256,512]{1,0:T(8,128)(2,1)S(1)}, u32[]{:S(2)}, u32[]{:S(2)}) collective-permute-start(bf16[256,512]{1,0:T(8,128)(2,1)} %refs_0_), channel_id=1, source_target_pairs={{0,4},{1,5},{2,6},{3,7},{4,0},{5,1},{6,2},{7,3},{8,12},{9,13},{10,... | collective-permute-start | bytes 786440 | tf_op jit(solution)/shard_map/ppermute | solution.py:260
  4.7 14.4 %collective-permute-start.1 = (bf16[256,512]{1,0:T(8,128)(2,1)}, bf16[256,512]{1,0:T(8,128)(2,1)S(1)}, u32[]{:S(2)}, u32[]{:S(2)}) collective-permute-start(bf16[256,512]{1,0:T(8,128)(2,1)} %refs_0_), channel_id=1, source_target_pairs={{0,16},{1,17},{2,18},{3,19},{4,20},{5,21},{6,22},{7,23},{8,24},{9,... | collective-permute-start | bytes 786440 | tf_op jit(solution)/shard_map/ppermute | solution.py:260
  6.9 12.2 %copy-start.2 = (bf16[256,512]{1,0:T(8,128)(2,1)S(1)}, bf16[256,512]{1,0:T(8,128)(2,1)}, u32[]{:S(2)}) copy-start(bf16[256,512]{1,0:T(8,128)(2,1)} %refs_0_) | copy-start | bytes 786436
  6.9 13.3 %copy-start = (bf16[4096,512]{1,0:T(8,128)(2,1)S(1)}, bf16[4096,512]{1,0:T(8,128)(2,1)}, u32[]{:S(2)}) copy-start(bf16[4096,512]{1,0:T(8,128)(2,1)} %table_ref.5) | copy-start | bytes 12582916
  19.1 5.9 %collective-permute-start.2 = (bf16[256,512]{1,0:T(8,128)(2,1)S(1)}, bf16[256,512]{1,0:T(8,128)(2,1)S(1)}, u32[]{:S(2)}, u32[]{:S(2)}) collective-permute-start(bf16[256,512]{1,0:T(8,128)(2,1)S(1)} %copy-done.2), channel_id=1, source_target_pairs={{0,8},{1,9},{2,10},{3,11},{4,12},{5,13},{6,14},{7,15},{8,0},{9,1},... | collective-permute-start | bytes 786440 | tf_op jit(solution)/shard_map/ppermute | solution.py:260
  19.2 8.1 %collective-permute-start.3 = (bf16[256,512]{1,0:T(8,128)(2,1)S(1)}, bf16[256,512]{1,0:T(8,128)(2,1)S(1)}, u32[]{:S(2)}, u32[]{:S(2)}) collective-permute-start(bf16[256,512]{1,0:T(8,128)(2,1)S(1)} %collective-permute-done.1.refs_2_), channel_id=1, source_target_pairs={{0,8},{1,9},{2,10},{3,11},{4,12},{5,13},{6,14},{7,15},{8,0},{9,1},... | collective-permute-start | bytes 786440 | tf_op jit(solution)/shard_map/ppermute | solution.py:260
  19.7 8.7 %collective-permute-start.7 = (bf16[256,512]{1,0:T(8,128)(2,1)S(1)}, bf16[256,512]{1,0:T(8,128)(2,1)S(1)}, u32[]{:S(2)}, u32[]{:S(2)}) collective-permute-start(bf16[256,512]{1,0:T(8,128)(2,1)S(1)} %collective-permute-done.refs_2_), channel_id=1, source_target_pairs={{0,16},{1,17},{2,18},{3,19},{4,20},{5,21},{6,22},{7,23},{8,24},{9,... | collective-permute-start | bytes 786440 | tf_op jit(solution)/shard_map/ppermute | solution.py:260
  21.2 9.2 %copy-start.1 = (bf16[512,512]{1,0:T(8,128)(2,1)S(1)}, bf16[512,512]{1,0:T(8,128)(2,1)}, u32[]{:S(2)}) copy-start(bf16[512,512]{1,0:T(8,128)(2,1)} %weight_ref.3) | copy-start | bytes 1572868
  21.2 7.7 %collective-permute-start.4 = (bf16[128,512]{1,0:T(8,128)(2,1)S(1)}, bf16[128,512]{1,0:T(8,128)(2,1)S(1)}, u32[]{:S(2)}, u32[]{:S(2)}) collective-permute-start(bf16[128,512]{1,0:T(8,128)(2,1)S(1)} %shard_map.69), channel_id=1, source_target_pairs={{0,3},{1,2},{2,1},{3,0},{4,7},{5,6},{6,5},{7,4},{8,11},{9,10},{10,... | collective-permute-start | bytes 393224 | tf_op jit(solution)/shard_map/ppermute | solution.py:260
  23.6 5.8 %collective-permute-start.5 = (bf16[128,512]{1,0:T(8,128)(2,1)S(1)}, bf16[128,512]{1,0:T(8,128)(2,1)S(1)}, u32[]{:S(2)}, u32[]{:S(2)}) collective-permute-start(bf16[128,512]{1,0:T(8,128)(2,1)S(1)} %get-tuple-element.60), channel_id=1, source_target_pairs={{0,2},{1,3},{2,0},{3,1},{4,6},{5,7},{6,4},{7,5},{8,10},{9,11},{10,... | collective-permute-start | bytes 393224 | tf_op jit(solution)/shard_map/ppermute | solution.py:260
  25.0 5.3 %collective-permute-start.6 = (bf16[128,512]{1,0:T(8,128)(2,1)S(1)}, bf16[128,512]{1,0:T(8,128)(2,1)S(1)}, u32[]{:S(2)}, u32[]{:S(2)}) collective-permute-start(bf16[128,512]{1,0:T(8,128)(2,1)S(1)} %get-tuple-element.61), channel_id=1, source_target_pairs={{0,1},{1,0},{2,3},{3,2},{4,5},{5,4},{6,7},{7,6},{8,9},{9,8},{10,11... | collective-permute-start | bytes 393224 | tf_op jit(solution)/shard_map/ppermute | solution.py:260
  28.3 2.6 %collective-permute-start.8 = (bf16[256,512]{1,0:T(8,128)(2,1)S(1)}, bf16[256,512]{1,0:T(8,128)(2,1)S(1)}, u32[]{:S(2)}, u32[]{:S(2)}) collective-permute-start(bf16[256,512]{1,0:T(8,128)(2,1)S(1)} %collective-permute-done.refs_2_), channel_id=1, source_target_pairs={{0,8},{1,9},{2,10},{3,11},{4,12},{5,13},{6,14},{7,15},{8,0},{9,1},... | collective-permute-start | bytes 786440 | tf_op jit(solution)/shard_map/ppermute | solution.py:260
  28.4 2.5 %collective-permute-start.9 = (bf16[256,512]{1,0:T(8,128)(2,1)S(1)}, bf16[256,512]{1,0:T(8,128)(2,1)S(1)}, u32[]{:S(2)}, u32[]{:S(2)}) collective-permute-start(bf16[256,512]{1,0:T(8,128)(2,1)S(1)} %collective-permute-done.7.refs_4_), channel_id=1, source_target_pairs={{0,8},{1,9},{2,10},{3,11},{4,12},{5,13},{6,14},{7,15},{8,0},{9,1},... | collective-permute-start | bytes 786440 | tf_op jit(solution)/shard_map/ppermute | solution.py:260
  33.7 1.6 %collective-permute-start.10 = (bf16[16,16,512]{2,1,0:T(8,128)(2,1)S(1)}, bf16[16,16,512]{2,1,0:T(8,128)(2,1)S(1)}, u32[]{:S(2)}, u32[]{:S(2)}) collective-permute-start(bf16[16,16,512]{2,1,0:T(8,128)(2,1)S(1)} %get-tuple-element.77), channel_id=1, source_target_pairs={{0,8},{1,9},{2,10},{3,11},{4,12},{5,13},{6,14},{7,15},{8,0},{9,1},... | collective-permute-start | bytes 786440 | tf_op jit(solution)/shard_map/ppermute | solution.py:260
  35.4 5.6 %collective-permute-start.11 = (bf16[8,16,512]{2,1,0:T(8,128)(2,1)S(1)}, bf16[8,16,512]{2,1,0:T(8,128)(2,1)S(1)}, u32[]{:S(2)}, u32[]{:S(2)}) collective-permute-start(bf16[8,16,512]{2,1,0:T(8,128)(2,1)S(1)} %get-tuple-element.79), channel_id=1, source_target_pairs={{0,16},{1,17},{2,18},{3,19},{4,20},{5,21},{6,22},{7,23},{8,24},{9,... | collective-permute-start | bytes 393224 | tf_op jit(solution)/shard_map/ppermute | solution.py:260
  36.8 7.3 %collective-permute-start.15 = (bf16[128,512]{1,0:T(8,128)(2,1)S(1)}, bf16[128,512]{1,0:T(8,128)(2,1)S(1)}, u32[]{:S(2)}, u32[]{:S(2)}) collective-permute-start(bf16[128,512]{1,0:T(8,128)(2,1)S(1)} %get-tuple-element.73.refs_5_), channel_id=1, source_target_pairs={{0,3},{1,2},{2,1},{3,0},{4,7},{5,6},{6,5},{7,4},{8,11},{9,10},{10,... | collective-permute-start | bytes 393224 | tf_op jit(solution)/shard_map/ppermute | solution.py:260
  37.9 8.2 %collective-permute-start.16 = (bf16[128,512]{1,0:T(8,128)(2,1)S(1)}, bf16[128,512]{1,0:T(8,128)(2,1)S(1)}, u32[]{:S(2)}, u32[]{:S(2)}) collective-permute-start(bf16[128,512]{1,0:T(8,128)(2,1)S(1)} %get-tuple-element.74.refs_6_), channel_id=1, source_target_pairs={{0,2},{1,3},{2,0},{3,1},{4,6},{5,7},{6,4},{7,5},{8,10},{9,11},{10,... | collective-permute-start | bytes 393224 | tf_op jit(solution)/shard_map/ppermute | solution.py:260
  39.3 7.1 %collective-permute-start.17 = (bf16[128,512]{1,0:T(8,128)(2,1)S(1)}, bf16[128,512]{1,0:T(8,128)(2,1)S(1)}, u32[]{:S(2)}, u32[]{:S(2)}) collective-permute-start(bf16[128,512]{1,0:T(8,128)(2,1)S(1)} %get-tuple-element.75.refs_7_), channel_id=1, source_target_pairs={{0,1},{1,0},{2,3},{3,2},{4,5},{5,4},{6,7},{7,6},{8,9},{9,8},{10,11... | collective-permute-start | bytes 393224 | tf_op jit(solution)/shard_map/ppermute | solution.py:260
  41.0 5.9 %collective-permute-start.12 = (bf16[2,16,512]{2,1,0:T(8,128)(2,1)S(1)}, bf16[2,16,512]{2,1,0:T(8,128)(2,1)S(1)}, u32[]{:S(2)}, u32[]{:S(2)}) collective-permute-start(bf16[2,16,512]{2,1,0:T(8,128)(2,1)S(1)} %get-tuple-element.81), channel_id=1, source_target_pairs={{0,3},{1,2},{2,1},{3,0},{4,7},{5,6},{6,5},{7,4},{8,11},{9,10},{10,... | collective-permute-start | bytes 98312 | tf_op jit(solution)/shard_map/ppermute | solution.py:260
  42.1 4.9 %collective-permute-start.13 = (bf16[2,16,512]{2,1,0:T(8,128)(2,1)S(1)}, bf16[2,16,512]{2,1,0:T(8,128)(2,1)S(1)}, u32[]{:S(2)}, u32[]{:S(2)}) collective-permute-start(bf16[2,16,512]{2,1,0:T(8,128)(2,1)S(1)} %get-tuple-element.82), channel_id=1, source_target_pairs={{0,2},{1,3},{2,0},{3,1},{4,6},{5,7},{6,4},{7,5},{8,10},{9,11},{10,... | collective-permute-start | bytes 98312 | tf_op jit(solution)/shard_map/ppermute | solution.py:260
  44.1 3.9 %collective-permute-start.14 = (bf16[2,16,512]{2,1,0:T(8,128)(2,1)S(1)}, bf16[2,16,512]{2,1,0:T(8,128)(2,1)S(1)}, u32[]{:S(2)}, u32[]{:S(2)}) collective-permute-start(bf16[2,16,512]{2,1,0:T(8,128)(2,1)S(1)} %get-tuple-element.83), channel_id=1, source_target_pairs={{0,1},{1,0},{2,3},{3,2},{4,5},{5,4},{6,7},{7,6},{8,9},{9,8},{10,11... | collective-permute-start | bytes 98312 | tf_op jit(solution)/shard_map/ppermute | solution.py:260
  48.0 5.8 %collective-permute-start.18 = (f32[1,16,512]{2,1,0:T(8,128)S(1)}, f32[1,16,512]{2,1,0:T(8,128)S(1)}, u32[]{:S(2)}, u32[]{:S(2)}) collective-permute-start(f32[1,16,512]{2,1,0:T(8,128)S(1)} %get-tuple-element.90), channel_id=1, source_target_pairs={{0,4},{1,5},{2,6},{3,7},{4,0},{5,1},{6,2},{7,3},{8,12},{9,13},{10,... | collective-permute-start | bytes 98312 | tf_op jit(solution)/shard_map/ppermute | solution.py:260

commit v25 on v24

--- a/solution.py
+++ b/solution.py
@@ -151,9 +151,13 @@
         item_ref[here] = (hidden * (rscale * (1.0 / width**0.5))).astype(bf16)
 
 
-def main_kernel(levels, near, place_ref, hidden_ref, rscale_ref, item_ref, *refs):
+def main_kernel(levels, near, order, bits, place_ref, hidden_ref, rscale_ref, item_ref, *refs):
+    fetched, *refs = refs[:near], *refs[near:-1], refs[-1]
+    *refs, blocks = refs
+    scratch = 2 * (levels - 1)
+    shares, refs = refs[len(refs) - scratch - 2 : len(refs) - scratch], refs[: len(refs) - scratch - 2] + refs[len(refs) - scratch :]
     later = levels - 1
-    units, owns = refs[0:1] + refs[len(refs) - 2 * later : len(refs) - later], refs[1:2] + refs[len(refs) - later :]
+    units, owns = [refs[0], *refs[len(refs) - 2 * later : len(refs) - later]], [refs[1], *refs[len(refs) - later :]]
     users, outs = refs[2 : len(refs) - 2 * later - near], refs[len(refs) - 2 * later - near : len(refs) - 2 * later]
     for level in range(1, levels):
         few = len(users) // later
@@ -177,6 +181,7 @@
         dhidden = (rscale * root * (dvec - hidden * (rscale * rscale * inner * (1.0 / width)))).astype(bf16)
         for part, ref in enumerate(outs):
             ref[pl.ds(level * size, size)] = dhidden[part * size : (part + 1) * size]
+    share_kernel(order, bits, 2 * near, *fetched, *outs, *shares, blocks)
 
 
 def coordinate(bits):
@@ -268,11 +273,9 @@
     return sum((lax.axis_size("item") if axis == "batch" else 1) << level for axis, level in bits)
 
 
-def reduce_scatter(fetched, dhidden, drow):
-    width = dhidden[0].shape[1]
+def stages_of(near):
     n_item, devices = lax.axis_size("item"), lax.axis_size("batch") * lax.axis_size("item")
-    part = width // devices
-    close = log2(len(dhidden))
+    close = log2(near)
     batch_bits, item_bits = bits_of("batch"), bits_of("item")
     stages = [batch_bits[:1], batch_bits[1:], item_bits[:close], item_bits[close:]]
     bits = sum(stages, [])
@@ -282,17 +285,20 @@
         for k, (axis, level) in enumerate(bits):
             at[axis] |= (spot >> (len(bits) - 1 - k) & 1) << level
         order.append(at["batch"] * n_item + at["item"])
-    left, values = devices, [*fetched, *dhidden]
+    return stages, order
+
+
+def reduce_scatter(stages, first, width, drow):
+    devices = lax.axis_size("batch") * lax.axis_size("item")
+    left, part, values = devices, width // devices, None
     for k, stage in enumerate(stages):
         whole, left = left, left >> len(stage)
         masks = [
             mask_of([bit for j, bit in enumerate(reversed(stage)) if step >> j & 1]) for step in steps_of(stage)[1:]
         ]
         sent = f32 if k == len(stages) - 1 else bf16
-        count = len(values)
-        kernel = functools.partial(stage_kernel, stage, count) if k else functools.partial(share_kernel, order, stage, count)
-        kept, *sends = call(
-            kernel,
+        kept, *sends = first if k == 0 else call(
+            functools.partial(stage_kernel, stage, len(values)),
             [((left, part, width), f32)] + [((left, part, width), sent)] * len(masks),
             *values,
             scratch=[pltpu.VMEM((whole, part, width), f32)],
@@ -379,21 +385,24 @@
         *fetched,
         flops=1 << 34,
     )
-    dhidden = call(
-        functools.partial(main_kernel, levels, near),
-        [((size, width), bf16)] * near,
+    stages, order = stages_of(near)
+    half, part = devices // 2, width // devices
+    *dhidden, kept, sent = call(
+        functools.partial(main_kernel, levels, near, order, stages[0]),
+        [((size, width), bf16)] * near + [((half, part, width), f32), ((half, part, width), bf16)],
         place,
         *hidden,
+        *fetched,
         *first,
         *[value for level in range(1, levels) for value in group(level)],
         flops=1 << 31,
         mib=40,
-        scratch=[pltpu.VMEM(shape, kind) for shape, kind in group_outs[:1] * (levels - 1) + group_outs[1:] * (levels - 1)],
+        scratch=[pltpu.VMEM(shape, kind) for shape, kind in group_outs[:1] * (levels - 1) + group_outs[1:] * (levels - 1)]
+        + [pltpu.VMEM((devices, part, width), f32)],
     )
     incoming = [swap(dhidden[part], part) for part in range(1, near)]
     (drow,) = call(row_kernel, [((total, width), bf16)], tower_weight, *reversed(incoming), dhidden[0], free=True)
-    order = [-part % near for part in range(near)]
-    terms, drow = reduce_scatter([fetched[part] for part in order], [dhidden[part] for part in order], drow)
+    terms, drow = reduce_scatter(stages, (kept, sent), width, drow)
     table_grad = pl.pallas_call(
         functools.partial(table_kernel, sizes),
         out_specs=pl.BlockSpec(memory_space=pl.ANY),

time: 54.6 us -> 55.1 us (level)
    pallas_call x13 -> x12, Pallas kernels: 9.34 us -> 9.24 us  [call(): pl.pallas_call(kernel, out_shape=[jax.ShapeDtypeStruct(shape, dtype) for...]
  transfers between devices with their start and end apart: 19 -> 19, of which waited for: 8 -> 7; matrix products, arithmetic and copies ran while one was open for 1% -> 1% of each run, Pallas kernels for 17% -> 17%
where the time goes in v25:
time: 55.1 us; the launch traced here: 54.9 us
  starting transfers between devices  22.1 us (40%)
  Pallas kernels  12.5 us (23%)
  blocking collectives  11.7 us (21%)
  waiting for transfers between devices  7.12 us (13%)
  between operations  0.82 us (1%)
  other arithmetic  0.7 us (1%)
    ppermute x19, starting transfers between devices, swap(): lax.ppermute(value, ('batch', 'item'), [(k, k ^ mask) for k in range(devi...  22.1 us
    all_to_all x1, blocking collectives, local(): lax.all_to_all(request, ('batch', 'item'), split_axis=0, concat_axis=0, t...  11.7 us
    pallas_call x12, Pallas kernels, call(): pl.pallas_call(kernel, out_shape=[jax.ShapeDtypeStruct(shape, dtype) for...  9.24 us
    ppermute x19, waiting for transfers between devices, swap(): lax.ppermute(value, ('batch', 'item'), [(k, k ^ mask) for k in range(devi...  7.12 us
    pallas_call x1, Pallas kernels, local(): pl.pallas_call(functools.partial(table_kernel, sizes), out_specs=pl.Block...  3.25 us
  transfers between devices with their start and end apart: 19, of which 7 were waited for; matrix products, arithmetic and copies ran while one was open for 1% of the time, Pallas kernels for 17%

profile of v25, /device:TPU:0, one launch (start us, length us, event | category | flops | bytes accessed | tf_op | source)
XLA Modules:
  0.0 54.9 jit_solution(5553687014073130970)
XLA Ops:
  0.6 4.1 %collective-permute-start = (bf16[256,512]{1,0:T(8,128)(2,1)}, bf16[256,512]{1,0:T(8,128)(2,1)S(1)}, u32[]{:S(2)}, u32[]{:S(2)}) collective-permute-start(bf16[256,512]{1,0:T(8,128)(2,1)} %refs_0_), channel_id=1, source_target_pairs={{0,4},{1,5},{2,6},{3,7},{4,0},{5,1},{6,2},{7,3},{8,12},{9,13},{10,... | collective-permute-start | bytes 786440 | tf_op jit(solution)/shard_map/ppermute | solution.py:265
  4.7 1.5 %collective-permute-start.1 = (bf16[256,512]{1,0:T(8,128)(2,1)}, bf16[256,512]{1,0:T(8,128)(2,1)S(1)}, u32[]{:S(2)}, u32[]{:S(2)}) collective-permute-start(bf16[256,512]{1,0:T(8,128)(2,1)} %refs_0_), channel_id=1, source_target_pairs={{0,16},{1,17},{2,18},{3,19},{4,20},{5,21},{6,22},{7,23},{8,24},{9,... | collective-permute-start | bytes 786440 | tf_op jit(solution)/shard_map/ppermute | solution.py:265
  6.2 0.7 %pad_add_fusion.named_ref = s32[2,256]{1,0:T(2,128)S(1)} fusion(s32[1,256]{1,0:T(1,128)} %bitcast.11, s32[1,256]{1,0:T(1,128)} %bitcast.12), kind=kLoop, calls=%fused_computation | loop fusion | flops 512 | bytes 4096 | tf_op jit(solution)/shard_map/stack | solution.py:333
  7.4 11.7 %all_to_all.12 = s32[32,1,80]{2,1,0:T(1,128)S(1)} all-to-all(s32[32,1,80]{2,1,0:T(1,128)S(1)} %bitcast.10), channel_id=1, replica_groups=mesh['batch'=4,'item'=8] {'batch','item'}, dimensions={0} | all-to-all | bytes 20480 | tf_op jit(solution)/shard_map/all_to_all | solution.py:336
  19.2 0.5 collective-permute-start.3
  19.7 0.6 %collective-permute-start.4 = (bf16[256,512]{1,0:T(8,128)(2,1)S(1)}, bf16[256,512]{1,0:T(8,128)(2,1)S(1)}, u32[]{:S(2)}, u32[]{:S(2)}) collective-permute-start(bf16[256,512]{1,0:T(8,128)(2,1)S(1)} %collective-permute-done.refs_6_), channel_id=1, source_target_pairs={{0,16},{1,17},{2,18},{3,19},{4,20},{5,21},{6,22},{7,23},{8,24},{9,... | collective-permute-start | bytes 786440 | tf_op jit(solution)/shard_map/ppermute | solution.py:265
  20.3 0.9 %shard_map.69 = bf16[128,512]{1,0:T(8,128)(2,1)S(1)} custom-call(s32[32,80]{1,0:T(8,128)S(1)} %bitcast.6, bf16[4096,512]{1,0:T(8,128)(2,1)S(1)} %copy-done), custom_call_target="tpu_custom_call" | custom-call | flops 536870912 | bytes 1048576 | tf_op jit(solution)/shard_map/pallas_call | solution.py:254
  21.2 0.8 %collective-permute-start.7 = (bf16[128,512]{1,0:T(8,128)(2,1)S(1)}, bf16[128,512]{1,0:T(8,128)(2,1)S(1)}, u32[]{:S(2)}, u32[]{:S(2)}) collective-permute-start(bf16[128,512]{1,0:T(8,128)(2,1)S(1)} %shard_map.69), channel_id=1, source_target_pairs={{0,3},{1,2},{2,1},{3,0},{4,7},{5,6},{6,5},{7,4},{8,11},{9,10},{10,... | collective-permute-start | bytes 393224 | tf_op jit(solution)/shard_map/ppermute | solution.py:265
  22.0 1.6 %shard_map.70 = (bf16[128,512]{1,0:T(8,128)(2,1)S(1)}, bf16[128,512]{1,0:T(8,128)(2,1)S(1)}) custom-call(s32[32,80]{1,0:T(8,128)S(1)} %bitcast.7, bf16[4096,512]{1,0:T(8,128)(2,1)S(1)} %copy-done), custom_call_target="tpu_custom_call" | custom-call | flops 1073741824 | bytes 1048576 | tf_op jit(solution)/shard_map/pallas_call | solution.py:254
  23.6 1.3 %collective-permute-start.5 = (bf16[128,512]{1,0:T(8,128)(2,1)S(1)}, bf16[128,512]{1,0:T(8,128)(2,1)S(1)}, u32[]{:S(2)}, u32[]{:S(2)}) collective-permute-start(bf16[128,512]{1,0:T(8,128)(2,1)S(1)} %get-tuple-element.62), channel_id=1, source_target_pairs={{0,1},{1,0},{2,3},{3,2},{4,5},{5,4},{6,7},{7,6},{8,9},{9,8},{10,11... | collective-permute-start | bytes 393224 | tf_op jit(solution)/shard_map/ppermute | solution.py:265
  24.9 1.5 %collective-permute-start.6 = (bf16[128,512]{1,0:T(8,128)(2,1)S(1)}, bf16[128,512]{1,0:T(8,128)(2,1)S(1)}, u32[]{:S(2)}, u32[]{:S(2)}) collective-permute-start(bf16[128,512]{1,0:T(8,128)(2,1)S(1)} %get-tuple-element.63), channel_id=1, source_target_pairs={{0,2},{1,3},{2,0},{3,1},{4,6},{5,7},{6,4},{7,5},{8,10},{9,11},{10,... | collective-permute-start | bytes 393224 | tf_op jit(solution)/shard_map/ppermute | solution.py:265
  26.4 0.9 %shard_map.71.refs_0_ = bf16[128,512]{1,0:T(8,128)(2,1)S(1)} custom-call(s32[32,80]{1,0:T(8,128)S(1)} %bitcast.8, bf16[4096,512]{1,0:T(8,128)(2,1)S(1)} %copy-done), custom_call_target="tpu_custom_call" | custom-call | flops 536870912 | bytes 1048576 | tf_op jit(solution)/shard_map/pallas_call | solution.py:254
  27.3 1.0 %shard_map.72 = (s32[512,1]{1,0:T(8,128)S(1)}, bf16[256,512]{1,0:T(8,128)(2,1)S(1)}, bf16[256,512]{1,0:T(8,128)(2,1)S(1)}, bf16[1024,512]{1,0:T(8,128)(2,1)S(1)}, bf16[256,512]{1,0:T(8,128)(2,1)S(1)}) custom-call(s32[32,80]{1,0:T(8,128)S(1)} %bitcast.9, bf16[256,512]{1,0:T(8,128)(2,1)S(1)} %copy-done.2, bf16[256,512]{1,0:T(8,128)(2,1)S(1)} %collective-permute-done.2.refs_1_, ...), custom_call_target="tpu_custom_call" | custom-call | tf_op jit(solution)/shard_map/pallas_call | solution.py:254
  28.9 1.2 %collective-permute-done.5.refs_1_ = bf16[128,512]{1,0:T(8,128)(2,1)S(1)} collective-permute-done((bf16[128,512]{1,0:T(8,128)(2,1)S(1)}, bf16[128,512]{1,0:T(8,128)(2,1)S(1)}, u32[]{:S(2)}, u32[]{:S(2)}) %collective-permute-start.5) | collective-permute-done | bytes 131104 | tf_op jit(solution)/shard_map/ppermute | solution.py:265
  30.2 0.5 shard_map.73
  30.7 2.6 %shard_map.74 = (bf16[128,512]{1,0:T(8,128)(2,1)S(1)}, bf16[128,512]{1,0:T(8,128)(2,1)S(1)}, bf16[128,512]{1,0:T(8,128)(2,1)S(1)}, bf16[128,512]{1,0:T(8,128)(2,...) custom-call(s32[512,1]{1,0:T(8,128)S(1)} %get-tuple-element.60.place_ref, ...), custom_call_target="tpu_custom_call" | custom-call | flops 2147483648 | bytes 1048576 | tf_op jit(solution)/shard_map/pallas_call | solution.py:254
  33.4 1.5 %collective-permute-done.10.refs_1_ = bf16[16,16,512]{2,1,0:T(8,128)(2,1)S(1)} collective-permute-done((bf16[16,16,512]{2,1,0:T(8,128)(2,1)S(1)}, bf16[16,16,512]{2,1,0:T(8,128)(2,1)S(1)}, u32[]{:S(2)}, u32[]{:S(2)}) %collective-permute-start.10) | collective-permute-done | bytes 262176 | tf_op jit(solution)/shard_map/ppermute | solution.py:265
  35.1 1.5 %collective-permute-start.11 = (bf16[8,16,512]{2,1,0:T(8,128)(2,1)S(1)}, bf16[8,16,512]{2,1,0:T(8,128)(2,1)S(1)}, u32[]{:S(2)}, u32[]{:S(2)}) collective-permute-start(bf16[8,16,512]{2,1,0:T(8,128)(2,1)S(1)} %get-tuple-element.75), channel_id=1, source_target_pairs={{0,16},{1,17},{2,18},{3,19},{4,20},{5,21},{6,22},{7,23},{8,24},{9,... | collective-permute-start | bytes 393224 | tf_op jit(solution)/shard_map/ppermute | solution.py:265
  36.6 1.2 %collective-permute-start.15 = (bf16[128,512]{1,0:T(8,128)(2,1)S(1)}, bf16[128,512]{1,0:T(8,128)(2,1)S(1)}, u32[]{:S(2)}, u32[]{:S(2)}) collective-permute-start(bf16[128,512]{1,0:T(8,128)(2,1)S(1)} %get-tuple-element.80), channel_id=1, source_target_pairs={{0,3},{1,2},{2,1},{3,0},{4,7},{5,6},{6,5},{7,4},{8,11},{9,10},{10,... | collective-permute-start | bytes 393224 | tf_op jit(solution)/shard_map/ppermute | solution.py:265
  37.8 0.8 %collective-permute-start.16 = (bf16[128,512]{1,0:T(8,128)(2,1)S(1)}, bf16[128,512]{1,0:T(8,128)(2,1)S(1)}, u32[]{:S(2)}, u32[]{:S(2)}) collective-permute-start(bf16[128,512]{1,0:T(8,128)(2,1)S(1)} %get-tuple-element.81), channel_id=1, source_target_pairs={{0,2},{1,3},{2,0},{3,1},{4,6},{5,7},{6,4},{7,5},{8,10},{9,11},{10,... | collective-permute-start | bytes 393224 | tf_op jit(solution)/shard_map/ppermute | solution.py:265
  38.6 1.4 %collective-permute-start.17 = (bf16[128,512]{1,0:T(8,128)(2,1)S(1)}, bf16[128,512]{1,0:T(8,128)(2,1)S(1)}, u32[]{:S(2)}, u32[]{:S(2)}) collective-permute-start(bf16[128,512]{1,0:T(8,128)(2,1)S(1)} %get-tuple-element.82), channel_id=1, source_target_pairs={{0,1},{1,0},{2,3},{3,2},{4,5},{5,4},{6,7},{7,6},{8,9},{9,8},{10,11... | collective-permute-start | bytes 393224 | tf_op jit(solution)/shard_map/ppermute | solution.py:265
  40.1 0.6 %collective-permute-done.11.refs_1_ = bf16[8,16,512]{2,1,0:T(8,128)(2,1)S(1)} collective-permute-done((bf16[8,16,512]{2,1,0:T(8,128)(2,1)S(1)}, bf16[8,16,512]{2,1,0:T(8,128)(2,1)S(1)}, u32[]{:S(2)}, u32[]{:S(2)}) %collective-permute-start.11) | collective-permute-done | bytes 131104 | tf_op jit(solution)/shard_map/ppermute | solution.py:265
  40.7 1.4 %collective-permute-start.12 = (bf16[2,16,512]{2,1,0:T(8,128)(2,1)S(1)}, bf16[2,16,512]{2,1,0:T(8,128)(2,1)S(1)}, u32[]{:S(2)}, u32[]{:S(2)}) collective-permute-start(bf16[2,16,512]{2,1,0:T(8,128)(2,1)S(1)} %get-tuple-element.77), channel_id=1, source_target_pairs={{0,3},{1,2},{2,1},{3,0},{4,7},{5,6},{6,5},{7,4},{8,11},{9,10},{10,... | collective-permute-start | bytes 98312 | tf_op jit(solution)/shard_map/ppermute | solution.py:265
  42.1 0.8 %collective-permute-start.13 = (bf16[2,16,512]{2,1,0:T(8,128)(2,1)S(1)}, bf16[2,16,512]{2,1,0:T(8,128)(2,1)S(1)}, u32[]{:S(2)}, u32[]{:S(2)}) collective-permute-start(bf16[2,16,512]{2,1,0:T(8,128)(2,1)S(1)} %get-tuple-element.78), channel_id=1, source_target_pairs={{0,2},{1,3},{2,0},{3,1},{4,6},{5,7},{6,4},{7,5},{8,10},{9,11},{10,... | collective-permute-start | bytes 98312 | tf_op jit(solution)/shard_map/ppermute | solution.py:265
  42.9 0.9 %collective-permute-done.15.refs_0_ = bf16[128,512]{1,0:T(8,128)(2,1)S(1)} collective-permute-done((bf16[128,512]{1,0:T(8,128)(2,1)S(1)}, bf16[128,512]{1,0:T(8,128)(2,1)S(1)}, u32[]{:S(2)}, u32[]{:S(2)}) %collective-permute-start.15) | collective-permute-done | bytes 131104 | tf_op jit(solution)/shard_map/ppermute | solution.py:265
  43.8 0.6 %collective-permute-start.14 = (bf16[2,16,512]{2,1,0:T(8,128)(2,1)S(1)}, bf16[2,16,512]{2,1,0:T(8,128)(2,1)S(1)}, u32[]{:S(2)}, u32[]{:S(2)}) collective-permute-start(bf16[2,16,512]{2,1,0:T(8,128)(2,1)S(1)} %get-tuple-element.79), channel_id=1, source_target_pairs={{0,1},{1,0},{2,3},{3,2},{4,5},{5,4},{6,7},{7,6},{8,9},{9,8},{10,11... | collective-permute-start | bytes 98312 | tf_op jit(solution)/shard_map/ppermute | solution.py:265
  44.5 0.9 %collective-permute-done.16.refs_1_ = bf16[128,512]{1,0:T(8,128)(2,1)S(1)} collective-permute-done((bf16[128,512]{1,0:T(8,128)(2,1)S(1)}, bf16[128,512]{1,0:T(8,128)(2,1)S(1)}, u32[]{:S(2)}, u32[]{:S(2)}) %collective-permute-start.16) | collective-permute-done | bytes 131104 | tf_op jit(solution)/shard_map/ppermute | solution.py:265
  45.4 0.8 %collective-permute-done.17.refs_2_ = bf16[128,512]{1,0:T(8,128)(2,1)S(1)} collective-permute-done((bf16[128,512]{1,0:T(8,128)(2,1)S(1)}, bf16[128,512]{1,0:T(8,128)(2,1)S(1)}, u32[]{:S(2)}, u32[]{:S(2)}) %collective-permute-start.17) | collective-permute-done | bytes 131104 | tf_op jit(solution)/shard_map/ppermute | solution.py:265
  46.7 1.1 %collective-permute-done.14.refs_3_ = bf16[2,16,512]{2,1,0:T(8,128)(2,1)S(1)} collective-permute-done((bf16[2,16,512]{2,1,0:T(8,128)(2,1)S(1)}, bf16[2,16,512]{2,1,0:T(8,128)(2,1)S(1)}, u32[]{:S(2)}, u32[]{:S(2)}) %collective-permute-start.14) | collective-permute-done | bytes 32800 | tf_op jit(solution)/shard_map/ppermute | solution.py:265
  47.8 3.3 %collective-permute-start.18 = (f32[1,16,512]{2,1,0:T(8,128)S(1)}, f32[1,16,512]{2,1,0:T(8,128)S(1)}, u32[]{:S(2)}, u32[]{:S(2)}) collective-permute-start(f32[1,16,512]{2,1,0:T(8,128)S(1)} %get-tuple-element.90), channel_id=1, source_target_pairs={{0,4},{1,5},{2,6},{3,7},{4,0},{5,1},{6,2},{7,3},{8,12},{9,13},{10,... | collective-permute-start | bytes 98312 | tf_op jit(solution)/shard_map/ppermute | solution.py:265
  51.0 3.2 %shard_map.78 = bf16[4096,512]{1,0:T(8,128)(2,1)} custom-call(bf16[256,512]{1,0:T(8,128)(2,1)S(1)} %get-tuple-element.56.low_hot_ref, bf16[256,512]{1,0:T(8,128)(2,1)S(1)} %get-tuple-element.57.block_ref, bf16[512,512]{1,0:T(8,128)(2,1)S(1)} %shard_map.77.drow_ref), custom_call_target="tpu_custom_call" | custom-call | flops 2147483648 | bytes 4194304 | tf_op jit(solution)/shard_map/pallas_call | solution.py:406
  54.3 0.6 %shard_map.80 = f32[16,512]{1,0:T(8,128)} custom-call(f32[1,16,512]{2,1,0:T(8,128)S(1)} %get-tuple-element.92.refs_0_, f32[1,16,512]{2,1,0:T(8,128)S(1)} %collective-permute-done.18.refs_1_), custom_call_target="tpu_custom_call" | custom-call | bytes 1048576 | tf_op jit(solution)/shard_map/pallas_call | solution.py:254
  (27 shorter events, 1.8 us)
Async XLA Ops:
  0.6 18.4 %collective-permute-start = (bf16[256,512]{1,0:T(8,128)(2,1)}, bf16[256,512]{1,0:T(8,128)(2,1)S(1)}, u32[]{:S(2)}, u32[]{:S(2)}) collective-permute-start(bf16[256,512]{1,0:T(8,128)(2,1)} %refs_0_), channel_id=1, source_target_pairs={{0,4},{1,5},{2,6},{3,7},{4,0},{5,1},{6,2},{7,3},{8,12},{9,13},{10,... | collective-permute-start | bytes 786440 | tf_op jit(solution)/shard_map/ppermute | solution.py:265
  4.7 14.4 %collective-permute-start.1 = (bf16[256,512]{1,0:T(8,128)(2,1)}, bf16[256,512]{1,0:T(8,128)(2,1)S(1)}, u32[]{:S(2)}, u32[]{:S(2)}) collective-permute-start(bf16[256,512]{1,0:T(8,128)(2,1)} %refs_0_), channel_id=1, source_target_pairs={{0,16},{1,17},{2,18},{3,19},{4,20},{5,21},{6,22},{7,23},{8,24},{9,... | collective-permute-start | bytes 786440 | tf_op jit(solution)/shard_map/ppermute | solution.py:265
  6.9 12.2 %copy-start.2 = (bf16[256,512]{1,0:T(8,128)(2,1)S(1)}, bf16[256,512]{1,0:T(8,128)(2,1)}, u32[]{:S(2)}) copy-start(bf16[256,512]{1,0:T(8,128)(2,1)} %refs_0_) | copy-start | bytes 786436
  6.9 13.3 %copy-start = (bf16[4096,512]{1,0:T(8,128)(2,1)S(1)}, bf16[4096,512]{1,0:T(8,128)(2,1)}, u32[]{:S(2)}) copy-start(bf16[4096,512]{1,0:T(8,128)(2,1)} %table_ref.5) | copy-start | bytes 12582916
  19.1 5.8 %collective-permute-start.2 = (bf16[256,512]{1,0:T(8,128)(2,1)S(1)}, bf16[256,512]{1,0:T(8,128)(2,1)S(1)}, u32[]{:S(2)}, u32[]{:S(2)}) collective-permute-start(bf16[256,512]{1,0:T(8,128)(2,1)S(1)} %copy-done.2), channel_id=1, source_target_pairs={{0,8},{1,9},{2,10},{3,11},{4,12},{5,13},{6,14},{7,15},{8,0},{9,1},... | collective-permute-start | bytes 786440 | tf_op jit(solution)/shard_map/ppermute | solution.py:265
  19.2 8.1 %collective-permute-start.3 = (bf16[256,512]{1,0:T(8,128)(2,1)S(1)}, bf16[256,512]{1,0:T(8,128)(2,1)S(1)}, u32[]{:S(2)}, u32[]{:S(2)}) collective-permute-start(bf16[256,512]{1,0:T(8,128)(2,1)S(1)} %collective-permute-done.1.refs_2_), channel_id=1, source_target_pairs={{0,8},{1,9},{2,10},{3,11},{4,12},{5,13},{6,14},{7,15},{8,0},{9,1},... | collective-permute-start | bytes 786440 | tf_op jit(solution)/shard_map/ppermute | solution.py:265
  19.7 8.7 %collective-permute-start.4 = (bf16[256,512]{1,0:T(8,128)(2,1)S(1)}, bf16[256,512]{1,0:T(8,128)(2,1)S(1)}, u32[]{:S(2)}, u32[]{:S(2)}) collective-permute-start(bf16[256,512]{1,0:T(8,128)(2,1)S(1)} %collective-permute-done.refs_6_), channel_id=1, source_target_pairs={{0,16},{1,17},{2,18},{3,19},{4,20},{5,21},{6,22},{7,23},{8,24},{9,... | collective-permute-start | bytes 786440 | tf_op jit(solution)/shard_map/ppermute | solution.py:265
  21.2 9.0 %copy-start.1 = (bf16[512,512]{1,0:T(8,128)(2,1)S(1)}, bf16[512,512]{1,0:T(8,128)(2,1)}, u32[]{:S(2)}) copy-start(bf16[512,512]{1,0:T(8,128)(2,1)} %weight_ref.3) | copy-start | bytes 1572868
  21.2 7.7 %collective-permute-start.7 = (bf16[128,512]{1,0:T(8,128)(2,1)S(1)}, bf16[128,512]{1,0:T(8,128)(2,1)S(1)}, u32[]{:S(2)}, u32[]{:S(2)}) collective-permute-start(bf16[128,512]{1,0:T(8,128)(2,1)S(1)} %shard_map.69), channel_id=1, source_target_pairs={{0,3},{1,2},{2,1},{3,0},{4,7},{5,6},{6,5},{7,4},{8,11},{9,10},{10,... | collective-permute-start | bytes 393224 | tf_op jit(solution)/shard_map/ppermute | solution.py:265
  23.6 6.6 %collective-permute-start.5 = (bf16[128,512]{1,0:T(8,128)(2,1)S(1)}, bf16[128,512]{1,0:T(8,128)(2,1)S(1)}, u32[]{:S(2)}, u32[]{:S(2)}) collective-permute-start(bf16[128,512]{1,0:T(8,128)(2,1)S(1)} %get-tuple-element.62), channel_id=1, source_target_pairs={{0,1},{1,0},{2,3},{3,2},{4,5},{5,4},{6,7},{7,6},{8,9},{9,8},{10,11... | collective-permute-start | bytes 393224 | tf_op jit(solution)/shard_map/ppermute | solution.py:265
  24.9 5.2 %collective-permute-start.6 = (bf16[128,512]{1,0:T(8,128)(2,1)S(1)}, bf16[128,512]{1,0:T(8,128)(2,1)S(1)}, u32[]{:S(2)}, u32[]{:S(2)}) collective-permute-start(bf16[128,512]{1,0:T(8,128)(2,1)S(1)} %get-tuple-element.63), channel_id=1, source_target_pairs={{0,2},{1,3},{2,0},{3,1},{4,6},{5,7},{6,4},{7,5},{8,10},{9,11},{10,... | collective-permute-start | bytes 393224 | tf_op jit(solution)/shard_map/ppermute | solution.py:265
  28.3 2.3 %collective-permute-start.8 = (bf16[256,512]{1,0:T(8,128)(2,1)S(1)}, bf16[256,512]{1,0:T(8,128)(2,1)S(1)}, u32[]{:S(2)}, u32[]{:S(2)}) collective-permute-start(bf16[256,512]{1,0:T(8,128)(2,1)S(1)} %collective-permute-done.refs_6_), channel_id=1, source_target_pairs={{0,8},{1,9},{2,10},{3,11},{4,12},{5,13},{6,14},{7,15},{8,0},{9,1},... | collective-permute-start | bytes 786440 | tf_op jit(solution)/shard_map/ppermute | solution.py:265
  28.4 2.3 %collective-permute-start.9 = (bf16[256,512]{1,0:T(8,128)(2,1)S(1)}, bf16[256,512]{1,0:T(8,128)(2,1)S(1)}, u32[]{:S(2)}, u32[]{:S(2)}) collective-permute-start(bf16[256,512]{1,0:T(8,128)(2,1)S(1)} %collective-permute-done.4.refs_8_), channel_id=1, source_target_pairs={{0,8},{1,9},{2,10},{3,11},{4,12},{5,13},{6,14},{7,15},{8,0},{9,1},... | collective-permute-start | bytes 786440 | tf_op jit(solution)/shard_map/ppermute | solution.py:265
  33.4 1.6 %collective-permute-start.10 = (bf16[16,16,512]{2,1,0:T(8,128)(2,1)S(1)}, bf16[16,16,512]{2,1,0:T(8,128)(2,1)S(1)}, u32[]{:S(2)}, u32[]{:S(2)}) collective-permute-start(bf16[16,16,512]{2,1,0:T(8,128)(2,1)S(1)} %get-tuple-element.73), channel_id=1, source_target_pairs={{0,8},{1,9},{2,10},{3,11},{4,12},{5,13},{6,14},{7,15},{8,0},{9,1},... | collective-permute-start | bytes 786440 | tf_op jit(solution)/shard_map/ppermute | solution.py:265
  35.1 5.6 %collective-permute-start.11 = (bf16[8,16,512]{2,1,0:T(8,128)(2,1)S(1)}, bf16[8,16,512]{2,1,0:T(8,128)(2,1)S(1)}, u32[]{:S(2)}, u32[]{:S(2)}) collective-permute-start(bf16[8,16,512]{2,1,0:T(8,128)(2,1)S(1)} %get-tuple-element.75), channel_id=1, source_target_pairs={{0,16},{1,17},{2,18},{3,19},{4,20},{5,21},{6,22},{7,23},{8,24},{9,... | collective-permute-start | bytes 393224 | tf_op jit(solution)/shard_map/ppermute | solution.py:265
  36.6 7.3 %collective-permute-start.15 = (bf16[128,512]{1,0:T(8,128)(2,1)S(1)}, bf16[128,512]{1,0:T(8,128)(2,1)S(1)}, u32[]{:S(2)}, u32[]{:S(2)}) collective-permute-start(bf16[128,512]{1,0:T(8,128)(2,1)S(1)} %get-tuple-element.80), channel_id=1, source_target_pairs={{0,3},{1,2},{2,1},{3,0},{4,7},{5,6},{6,5},{7,4},{8,11},{9,10},{10,... | collective-permute-start | bytes 393224 | tf_op jit(solution)/shard_map/ppermute | solution.py:265
  37.8 7.6 %collective-permute-start.16 = (bf16[128,512]{1,0:T(8,128)(2,1)S(1)}, bf16[128,512]{1,0:T(8,128)(2,1)S(1)}, u32[]{:S(2)}, u32[]{:S(2)}) collective-permute-start(bf16[128,512]{1,0:T(8,128)(2,1)S(1)} %get-tuple-element.81), channel_id=1, source_target_pairs={{0,2},{1,3},{2,0},{3,1},{4,6},{5,7},{6,4},{7,5},{8,10},{9,11},{10,... | collective-permute-start | bytes 393224 | tf_op jit(solution)/shard_map/ppermute | solution.py:265
  38.6 7.5 %collective-permute-start.17 = (bf16[128,512]{1,0:T(8,128)(2,1)S(1)}, bf16[128,512]{1,0:T(8,128)(2,1)S(1)}, u32[]{:S(2)}, u32[]{:S(2)}) collective-permute-start(bf16[128,512]{1,0:T(8,128)(2,1)S(1)} %get-tuple-element.82), channel_id=1, source_target_pairs={{0,1},{1,0},{2,3},{3,2},{4,5},{5,4},{6,7},{7,6},{8,9},{9,8},{10,11... | collective-permute-start | bytes 393224 | tf_op jit(solution)/shard_map/ppermute | solution.py:265
  40.7 5.9 %collective-permute-start.12 = (bf16[2,16,512]{2,1,0:T(8,128)(2,1)S(1)}, bf16[2,16,512]{2,1,0:T(8,128)(2,1)S(1)}, u32[]{:S(2)}, u32[]{:S(2)}) collective-permute-start(bf16[2,16,512]{2,1,0:T(8,128)(2,1)S(1)} %get-tuple-element.77), channel_id=1, source_target_pairs={{0,3},{1,2},{2,1},{3,0},{4,7},{5,6},{6,5},{7,4},{8,11},{9,10},{10,... | collective-permute-start | bytes 98312 | tf_op jit(solution)/shard_map/ppermute | solution.py:265
  42.1 4.6 %collective-permute-start.13 = (bf16[2,16,512]{2,1,0:T(8,128)(2,1)S(1)}, bf16[2,16,512]{2,1,0:T(8,128)(2,1)S(1)}, u32[]{:S(2)}, u32[]{:S(2)}) collective-permute-start(bf16[2,16,512]{2,1,0:T(8,128)(2,1)S(1)} %get-tuple-element.78), channel_id=1, source_target_pairs={{0,2},{1,3},{2,0},{3,1},{4,6},{5,7},{6,4},{7,5},{8,10},{9,11},{10,... | collective-permute-start | bytes 98312 | tf_op jit(solution)/shard_map/ppermute | solution.py:265
  43.8 3.9 %collective-permute-start.14 = (bf16[2,16,512]{2,1,0:T(8,128)(2,1)S(1)}, bf16[2,16,512]{2,1,0:T(8,128)(2,1)S(1)}, u32[]{:S(2)}, u32[]{:S(2)}) collective-permute-start(bf16[2,16,512]{2,1,0:T(8,128)(2,1)S(1)} %get-tuple-element.79), channel_id=1, source_target_pairs={{0,1},{1,0},{2,3},{3,2},{4,5},{5,4},{6,7},{7,6},{8,9},{9,8},{10,11... | collective-permute-start | bytes 98312 | tf_op jit(solution)/shard_map/ppermute | solution.py:265
  47.8 6.5 %collective-permute-start.18 = (f32[1,16,512]{2,1,0:T(8,128)S(1)}, f32[1,16,512]{2,1,0:T(8,128)S(1)}, u32[]{:S(2)}, u32[]{:S(2)}) collective-permute-start(f32[1,16,512]{2,1,0:T(8,128)S(1)} %get-tuple-element.90), channel_id=1, source_target_pairs={{0,4},{1,5},{2,6},{3,7},{4,0},{5,1},{6,2},{7,3},{8,12},{9,13},{10,... | collective-permute-start | bytes 98312 | tf_op jit(solution)/shard_map/ppermute | solution.py:265

commit v26 on v24

--- a/solution.py
+++ b/solution.py
@@ -314,7 +314,7 @@
     slots = 2 * n // devices
     total = devices * slots
     size = total // near
-    sizes = [rows // 8] + [rows // 4] * 3 + [rows // 8]
+    sizes = [rows // 16 * k for k in (1, 2, 4, 4, 3, 2)]
 
     far = [batch * n_item for batch in range(2, n_batch, 2)]
     users = {0: user_vectors}

time: 54.6 us -> 54.6 us (level)
  no operation moved by 1% of the time
where the time goes in v26:
time: 54.6 us; the launch traced here: 54.4 us
  starting transfers between devices  22 us (40%)
  Pallas kernels  12.5 us (23%)
  blocking collectives  11.7 us (21%)
  waiting for transfers between devices  6.57 us (12%)
  between operations  0.82 us (2%)
  other arithmetic  0.7 us (1%)
    ppermute x19, starting transfers between devices, swap(): lax.ppermute(value, ('batch', 'item'), [(k, k ^ mask) for k in range(devi...  22 us
    all_to_all x1, blocking collectives, local(): lax.all_to_all(request, ('batch', 'item'), split_axis=0, concat_axis=0, t...  11.7 us
    pallas_call x13, Pallas kernels, call(): pl.pallas_call(kernel, out_shape=[jax.ShapeDtypeStruct(shape, dtype) for...  9.34 us
    ppermute x19, waiting for transfers between devices, swap(): lax.ppermute(value, ('batch', 'item'), [(k, k ^ mask) for k in range(devi...  6.57 us
    pallas_call x1, Pallas kernels, local(): pl.pallas_call(functools.partial(table_kernel, sizes), out_specs=pl.Block...  3.19 us
  transfers between devices with their start and end apart: 19, of which 8 were waited for; matrix products, arithmetic and copies ran while one was open for 1% of the time, Pallas kernels for 17%

profile of v26, /device:TPU:0, one launch (start us, length us, event | category | flops | bytes accessed | tf_op | source)
XLA Modules:
  0.0 54.4 jit_solution(3635671640389001367)
XLA Ops:
  0.6 4.1 %collective-permute-start = (bf16[256,512]{1,0:T(8,128)(2,1)}, bf16[256,512]{1,0:T(8,128)(2,1)S(1)}, u32[]{:S(2)}, u32[]{:S(2)}) collective-permute-start(bf16[256,512]{1,0:T(8,128)(2,1)} %refs_0_), channel_id=1, source_target_pairs={{0,4},{1,5},{2,6},{3,7},{4,0},{5,1},{6,2},{7,3},{8,12},{9,13},{10,... | collective-permute-start | bytes 786440 | tf_op jit(solution)/shard_map/ppermute | solution.py:260
  4.7 1.5 %collective-permute-start.1 = (bf16[256,512]{1,0:T(8,128)(2,1)}, bf16[256,512]{1,0:T(8,128)(2,1)S(1)}, u32[]{:S(2)}, u32[]{:S(2)}) collective-permute-start(bf16[256,512]{1,0:T(8,128)(2,1)} %refs_0_), channel_id=1, source_target_pairs={{0,16},{1,17},{2,18},{3,19},{4,20},{5,21},{6,22},{7,23},{8,24},{9,... | collective-permute-start | bytes 786440 | tf_op jit(solution)/shard_map/ppermute | solution.py:260
  6.2 0.7 %pad_add_fusion.named_ref = s32[2,256]{1,0:T(2,128)S(1)} fusion(s32[1,256]{1,0:T(1,128)} %bitcast.11, s32[1,256]{1,0:T(1,128)} %bitcast.12), kind=kLoop, calls=%fused_computation | loop fusion | flops 512 | bytes 4096 | tf_op jit(solution)/shard_map/stack | solution.py:327
  7.4 11.7 %all_to_all.12 = s32[32,1,80]{2,1,0:T(1,128)S(1)} all-to-all(s32[32,1,80]{2,1,0:T(1,128)S(1)} %bitcast.10), channel_id=1, replica_groups=mesh['batch'=4,'item'=8] {'batch','item'}, dimensions={0} | all-to-all | bytes 20480 | tf_op jit(solution)/shard_map/all_to_all | solution.py:330
  19.2 0.5 collective-permute-start.3
  19.7 0.6 %collective-permute-start.7 = (bf16[256,512]{1,0:T(8,128)(2,1)S(1)}, bf16[256,512]{1,0:T(8,128)(2,1)S(1)}, u32[]{:S(2)}, u32[]{:S(2)}) collective-permute-start(bf16[256,512]{1,0:T(8,128)(2,1)S(1)} %collective-permute-done.refs_2_), channel_id=1, source_target_pairs={{0,16},{1,17},{2,18},{3,19},{4,20},{5,21},{6,22},{7,23},{8,24},{9,... | collective-permute-start | bytes 786440 | tf_op jit(solution)/shard_map/ppermute | solution.py:260
  20.3 0.9 %shard_map.69 = bf16[128,512]{1,0:T(8,128)(2,1)S(1)} custom-call(s32[32,80]{1,0:T(8,128)S(1)} %bitcast.6, bf16[4096,512]{1,0:T(8,128)(2,1)S(1)} %copy-done), custom_call_target="tpu_custom_call" | custom-call | flops 536870912 | bytes 1048576 | tf_op jit(solution)/shard_map/pallas_call | solution.py:249
  21.2 0.8 %collective-permute-start.4 = (bf16[128,512]{1,0:T(8,128)(2,1)S(1)}, bf16[128,512]{1,0:T(8,128)(2,1)S(1)}, u32[]{:S(2)}, u32[]{:S(2)}) collective-permute-start(bf16[128,512]{1,0:T(8,128)(2,1)S(1)} %shard_map.69), channel_id=1, source_target_pairs={{0,3},{1,2},{2,1},{3,0},{4,7},{5,6},{6,5},{7,4},{8,11},{9,10},{10,... | collective-permute-start | bytes 393224 | tf_op jit(solution)/shard_map/ppermute | solution.py:260
  22.0 1.6 %shard_map.70 = (bf16[128,512]{1,0:T(8,128)(2,1)S(1)}, bf16[128,512]{1,0:T(8,128)(2,1)S(1)}) custom-call(s32[32,80]{1,0:T(8,128)S(1)} %bitcast.7, bf16[4096,512]{1,0:T(8,128)(2,1)S(1)} %copy-done), custom_call_target="tpu_custom_call" | custom-call | flops 1073741824 | bytes 1048576 | tf_op jit(solution)/shard_map/pallas_call | solution.py:249
  23.6 1.4 %collective-permute-start.5 = (bf16[128,512]{1,0:T(8,128)(2,1)S(1)}, bf16[128,512]{1,0:T(8,128)(2,1)S(1)}, u32[]{:S(2)}, u32[]{:S(2)}) collective-permute-start(bf16[128,512]{1,0:T(8,128)(2,1)S(1)} %get-tuple-element.60), channel_id=1, source_target_pairs={{0,2},{1,3},{2,0},{3,1},{4,6},{5,7},{6,4},{7,5},{8,10},{9,11},{10,... | collective-permute-start | bytes 393224 | tf_op jit(solution)/shard_map/ppermute | solution.py:260
  25.0 1.4 %collective-permute-start.6 = (bf16[128,512]{1,0:T(8,128)(2,1)S(1)}, bf16[128,512]{1,0:T(8,128)(2,1)S(1)}, u32[]{:S(2)}, u32[]{:S(2)}) collective-permute-start(bf16[128,512]{1,0:T(8,128)(2,1)S(1)} %get-tuple-element.61), channel_id=1, source_target_pairs={{0,1},{1,0},{2,3},{3,2},{4,5},{5,4},{6,7},{7,6},{8,9},{9,8},{10,11... | collective-permute-start | bytes 393224 | tf_op jit(solution)/shard_map/ppermute | solution.py:260
  26.4 0.9 %shard_map.71.refs_0_ = bf16[128,512]{1,0:T(8,128)(2,1)S(1)} custom-call(s32[32,80]{1,0:T(8,128)S(1)} %bitcast.8, bf16[4096,512]{1,0:T(8,128)(2,1)S(1)} %copy-done), custom_call_target="tpu_custom_call" | custom-call | flops 536870912 | bytes 1048576 | tf_op jit(solution)/shard_map/pallas_call | solution.py:249
  27.3 1.0 %shard_map.72 = (s32[512,1]{1,0:T(8,128)S(1)}, bf16[256,512]{1,0:T(8,128)(2,1)S(1)}, bf16[256,512]{1,0:T(8,128)(2,1)S(1)}, bf16[1024,512]{1,0:T(8,128)(2,1)S(1)}, bf16[256,512]{1,0:T(8,128)(2,1)S(1)}) custom-call(s32[32,80]{1,0:T(8,128)S(1)} %bitcast.9, bf16[256,512]{1,0:T(8,128)(2,1)S(1)} %copy-done.2, bf16[256,512]{1,0:T(8,128)(2,1)S(1)} %collective-permute-done.2.refs_1_, ...), custom_call_target="tpu_custom_call" | custom-call | tf_op jit(solution)/shard_map/pallas_call | solution.py:249
  29.4 1.0 %collective-permute-done.6.refs_1_.refs_3_ = bf16[128,512]{1,0:T(8,128)(2,1)S(1)} collective-permute-done((bf16[128,512]{1,0:T(8,128)(2,1)S(1)}, bf16[128,512]{1,0:T(8,128)(2,1)S(1)}, u32[]{:S(2)}, u32[]{:S(2)}) %collective-permute-start.6) | collective-permute-done | bytes 131104 | tf_op jit(solution)/shard_map/ppermute | solution.py:260
  30.4 0.5 shard_map.73
  30.9 2.2 %shard_map.74 = (bf16[128,512]{1,0:T(8,128)(2,1)S(1)}, bf16[128,512]{1,0:T(8,128)(2,1)S(1)}, bf16[128,512]{1,0:T(8,128)(2,1)S(1)}, bf16[128,512]{1,0:T(8,128)(2,1)S(1)}) custom-call(s32[512,1]{1,0:T(8,128)S(1)} %get-tuple-element.64.place_ref, f32[512,512]{1,0:T(8,128)S(1)} %get-tuple-element.65.hidden_ref, f32[512,1]{1,0:T(8,128)S(1)} %get-tuple-element.66.rscale_ref, ...), custom_call_target="tpu_custom_call" | custom-call | flops 2147483648 | bytes 1048576 | tf_op jit(solution)/shard_map/pallas_call | solution.py:249
  33.1 0.5 shard_map.75
  33.7 1.5 %collective-permute-done.10.refs_1_ = bf16[16,16,512]{2,1,0:T(8,128)(2,1)S(1)} collective-permute-done((bf16[16,16,512]{2,1,0:T(8,128)(2,1)S(1)}, bf16[16,16,512]{2,1,0:T(8,128)(2,1)S(1)}, u32[]{:S(2)}, u32[]{:S(2)}) %collective-permute-start.10) | collective-permute-done | bytes 262176 | tf_op jit(solution)/shard_map/ppermute | solution.py:260
  35.4 1.4 %collective-permute-start.11 = (bf16[8,16,512]{2,1,0:T(8,128)(2,1)S(1)}, bf16[8,16,512]{2,1,0:T(8,128)(2,1)S(1)}, u32[]{:S(2)}, u32[]{:S(2)}) collective-permute-start(bf16[8,16,512]{2,1,0:T(8,128)(2,1)S(1)} %get-tuple-element.79), channel_id=1, source_target_pairs={{0,16},{1,17},{2,18},{3,19},{4,20},{5,21},{6,22},{7,23},{8,24},{9,... | collective-permute-start | bytes 393224 | tf_op jit(solution)/shard_map/ppermute | solution.py:260
  36.8 1.1 %collective-permute-start.15 = (bf16[128,512]{1,0:T(8,128)(2,1)S(1)}, bf16[128,512]{1,0:T(8,128)(2,1)S(1)}, u32[]{:S(2)}, u32[]{:S(2)}) collective-permute-start(bf16[128,512]{1,0:T(8,128)(2,1)S(1)} %get-tuple-element.73.refs_5_), channel_id=1, source_target_pairs={{0,3},{1,2},{2,1},{3,0},{4,7},{5,6},{6,5},{7,4},{8,11},{9,10},{10,... | collective-permute-start | bytes 393224 | tf_op jit(solution)/shard_map/ppermute | solution.py:260
  37.9 1.4 %collective-permute-start.16 = (bf16[128,512]{1,0:T(8,128)(2,1)S(1)}, bf16[128,512]{1,0:T(8,128)(2,1)S(1)}, u32[]{:S(2)}, u32[]{:S(2)}) collective-permute-start(bf16[128,512]{1,0:T(8,128)(2,1)S(1)} %get-tuple-element.74.refs_6_), channel_id=1, source_target_pairs={{0,2},{1,3},{2,0},{3,1},{4,6},{5,7},{6,4},{7,5},{8,10},{9,11},{10,... | collective-permute-start | bytes 393224 | tf_op jit(solution)/shard_map/ppermute | solution.py:260
  39.3 1.0 %collective-permute-start.17 = (bf16[128,512]{1,0:T(8,128)(2,1)S(1)}, bf16[128,512]{1,0:T(8,128)(2,1)S(1)}, u32[]{:S(2)}, u32[]{:S(2)}) collective-permute-start(bf16[128,512]{1,0:T(8,128)(2,1)S(1)} %get-tuple-element.75.refs_7_), channel_id=1, source_target_pairs={{0,1},{1,0},{2,3},{3,2},{4,5},{5,4},{6,7},{7,6},{8,9},{9,8},{10,11... | collective-permute-start | bytes 393224 | tf_op jit(solution)/shard_map/ppermute | solution.py:260
  40.3 0.7 %collective-permute-done.11.refs_1_ = bf16[8,16,512]{2,1,0:T(8,128)(2,1)S(1)} collective-permute-done((bf16[8,16,512]{2,1,0:T(8,128)(2,1)S(1)}, bf16[8,16,512]{2,1,0:T(8,128)(2,1)S(1)}, u32[]{:S(2)}, u32[]{:S(2)}) %collective-permute-start.11) | collective-permute-done | bytes 131104 | tf_op jit(solution)/shard_map/ppermute | solution.py:260
  41.0 1.1 %collective-permute-start.12 = (bf16[2,16,512]{2,1,0:T(8,128)(2,1)S(1)}, bf16[2,16,512]{2,1,0:T(8,128)(2,1)S(1)}, u32[]{:S(2)}, u32[]{:S(2)}) collective-permute-start(bf16[2,16,512]{2,1,0:T(8,128)(2,1)S(1)} %get-tuple-element.81), channel_id=1, source_target_pairs={{0,3},{1,2},{2,1},{3,0},{4,7},{5,6},{6,5},{7,4},{8,11},{9,10},{10,... | collective-permute-start | bytes 98312 | tf_op jit(solution)/shard_map/ppermute | solution.py:260
  42.1 1.4 %collective-permute-start.13 = (bf16[2,16,512]{2,1,0:T(8,128)(2,1)S(1)}, bf16[2,16,512]{2,1,0:T(8,128)(2,1)S(1)}, u32[]{:S(2)}, u32[]{:S(2)}) collective-permute-start(bf16[2,16,512]{2,1,0:T(8,128)(2,1)S(1)} %get-tuple-element.82), channel_id=1, source_target_pairs={{0,2},{1,3},{2,0},{3,1},{4,6},{5,7},{6,4},{7,5},{8,10},{9,11},{10,... | collective-permute-start | bytes 98312 | tf_op jit(solution)/shard_map/ppermute | solution.py:260
  43.5 0.5 %collective-permute-done.15.refs_0_ = bf16[128,512]{1,0:T(8,128)(2,1)S(1)} collective-permute-done((bf16[128,512]{1,0:T(8,128)(2,1)S(1)}, bf16[128,512]{1,0:T(8,128)(2,1)S(1)}, u32[]{:S(2)}, u32[]{:S(2)}) %collective-permute-start.15) | collective-permute-done | bytes 131104 | tf_op jit(solution)/shard_map/ppermute | solution.py:260
  44.1 1.1 %collective-permute-start.14 = (bf16[2,16,512]{2,1,0:T(8,128)(2,1)S(1)}, bf16[2,16,512]{2,1,0:T(8,128)(2,1)S(1)}, u32[]{:S(2)}, u32[]{:S(2)}) collective-permute-start(bf16[2,16,512]{2,1,0:T(8,128)(2,1)S(1)} %get-tuple-element.83), channel_id=1, source_target_pairs={{0,1},{1,0},{2,3},{3,2},{4,5},{5,4},{6,7},{7,6},{8,9},{9,8},{10,11... | collective-permute-start | bytes 98312 | tf_op jit(solution)/shard_map/ppermute | solution.py:260
  45.2 0.9 %collective-permute-done.16.refs_1_ = bf16[128,512]{1,0:T(8,128)(2,1)S(1)} collective-permute-done((bf16[128,512]{1,0:T(8,128)(2,1)S(1)}, bf16[128,512]{1,0:T(8,128)(2,1)S(1)}, u32[]{:S(2)}, u32[]{:S(2)}) %collective-permute-start.16) | collective-permute-done | bytes 131104 | tf_op jit(solution)/shard_map/ppermute | solution.py:260
  47.0 1.0 %collective-permute-done.14.refs_3_ = bf16[2,16,512]{2,1,0:T(8,128)(2,1)S(1)} collective-permute-done((bf16[2,16,512]{2,1,0:T(8,128)(2,1)S(1)}, bf16[2,16,512]{2,1,0:T(8,128)(2,1)S(1)}, u32[]{:S(2)}, u32[]{:S(2)}) %collective-permute-start.14) | collective-permute-done | bytes 32800 | tf_op jit(solution)/shard_map/ppermute | solution.py:260
  48.0 2.5 %collective-permute-start.18 = (f32[1,16,512]{2,1,0:T(8,128)S(1)}, f32[1,16,512]{2,1,0:T(8,128)S(1)}, u32[]{:S(2)}, u32[]{:S(2)}) collective-permute-start(f32[1,16,512]{2,1,0:T(8,128)S(1)} %get-tuple-element.90), channel_id=1, source_target_pairs={{0,4},{1,5},{2,6},{3,7},{4,0},{5,1},{6,2},{7,3},{8,12},{9,13},{10,... | collective-permute-start | bytes 98312 | tf_op jit(solution)/shard_map/ppermute | solution.py:260
  50.5 3.2 %shard_map.79 = bf16[4096,512]{1,0:T(8,128)(2,1)} custom-call(bf16[256,512]{1,0:T(8,128)(2,1)S(1)} %get-tuple-element.56.low_hot_ref, bf16[256,512]{1,0:T(8,128)(2,1)S(1)} %get-tuple-element.57.block_ref, bf16[512,512]{1,0:T(8,128)(2,1)S(1)} %shard_map.78.drow_ref), custom_call_target="tpu_custom_call" | custom-call | flops 2147483648 | bytes 4194304 | tf_op jit(solution)/shard_map/pallas_call | solution.py:397
  53.8 0.6 %shard_map.81 = f32[16,512]{1,0:T(8,128)} custom-call(f32[1,16,512]{2,1,0:T(8,128)S(1)} %get-tuple-element.92.refs_0_, f32[1,16,512]{2,1,0:T(8,128)S(1)} %collective-permute-done.18.refs_1_), custom_call_target="tpu_custom_call" | custom-call | bytes 1048576 | tf_op jit(solution)/shard_map/pallas_call | solution.py:249
  (28 shorter events, 2.7 us)
Async XLA Ops:
  0.6 18.4 %collective-permute-start = (bf16[256,512]{1,0:T(8,128)(2,1)}, bf16[256,512]{1,0:T(8,128)(2,1)S(1)}, u32[]{:S(2)}, u32[]{:S(2)}) collective-permute-start(bf16[256,512]{1,0:T(8,128)(2,1)} %refs_0_), channel_id=1, source_target_pairs={{0,4},{1,5},{2,6},{3,7},{4,0},{5,1},{6,2},{7,3},{8,12},{9,13},{10,... | collective-permute-start | bytes 786440 | tf_op jit(solution)/shard_map/ppermute | solution.py:260
  4.7 14.4 %collective-permute-start.1 = (bf16[256,512]{1,0:T(8,128)(2,1)}, bf16[256,512]{1,0:T(8,128)(2,1)S(1)}, u32[]{:S(2)}, u32[]{:S(2)}) collective-permute-start(bf16[256,512]{1,0:T(8,128)(2,1)} %refs_0_), channel_id=1, source_target_pairs={{0,16},{1,17},{2,18},{3,19},{4,20},{5,21},{6,22},{7,23},{8,24},{9,... | collective-permute-start | bytes 786440 | tf_op jit(solution)/shard_map/ppermute | solution.py:260
  6.9 12.2 %copy-start.2 = (bf16[256,512]{1,0:T(8,128)(2,1)S(1)}, bf16[256,512]{1,0:T(8,128)(2,1)}, u32[]{:S(2)}) copy-start(bf16[256,512]{1,0:T(8,128)(2,1)} %refs_0_) | copy-start | bytes 786436
  6.9 13.3 %copy-start = (bf16[4096,512]{1,0:T(8,128)(2,1)S(1)}, bf16[4096,512]{1,0:T(8,128)(2,1)}, u32[]{:S(2)}) copy-start(bf16[4096,512]{1,0:T(8,128)(2,1)} %table_ref.5) | copy-start | bytes 12582916
  19.1 5.9 %collective-permute-start.2 = (bf16[256,512]{1,0:T(8,128)(2,1)S(1)}, bf16[256,512]{1,0:T(8,128)(2,1)S(1)}, u32[]{:S(2)}, u32[]{:S(2)}) collective-permute-start(bf16[256,512]{1,0:T(8,128)(2,1)S(1)} %copy-done.2), channel_id=1, source_target_pairs={{0,8},{1,9},{2,10},{3,11},{4,12},{5,13},{6,14},{7,15},{8,0},{9,1},... | collective-permute-start | bytes 786440 | tf_op jit(solution)/shard_map/ppermute | solution.py:260
  19.2 8.1 %collective-permute-start.3 = (bf16[256,512]{1,0:T(8,128)(2,1)S(1)}, bf16[256,512]{1,0:T(8,128)(2,1)S(1)}, u32[]{:S(2)}, u32[]{:S(2)}) collective-permute-start(bf16[256,512]{1,0:T(8,128)(2,1)S(1)} %collective-permute-done.1.refs_2_), channel_id=1, source_target_pairs={{0,8},{1,9},{2,10},{3,11},{4,12},{5,13},{6,14},{7,15},{8,0},{9,1},... | collective-permute-start | bytes 786440 | tf_op jit(solution)/shard_map/ppermute | solution.py:260
  19.7 8.7 %collective-permute-start.7 = (bf16[256,512]{1,0:T(8,128)(2,1)S(1)}, bf16[256,512]{1,0:T(8,128)(2,1)S(1)}, u32[]{:S(2)}, u32[]{:S(2)}) collective-permute-start(bf16[256,512]{1,0:T(8,128)(2,1)S(1)} %collective-permute-done.refs_2_), channel_id=1, source_target_pairs={{0,16},{1,17},{2,18},{3,19},{4,20},{5,21},{6,22},{7,23},{8,24},{9,... | collective-permute-start | bytes 786440 | tf_op jit(solution)/shard_map/ppermute | solution.py:260
  21.2 9.2 %copy-start.1 = (bf16[512,512]{1,0:T(8,128)(2,1)S(1)}, bf16[512,512]{1,0:T(8,128)(2,1)}, u32[]{:S(2)}) copy-start(bf16[512,512]{1,0:T(8,128)(2,1)} %weight_ref.3) | copy-start | bytes 1572868
  21.2 7.7 %collective-permute-start.4 = (bf16[128,512]{1,0:T(8,128)(2,1)S(1)}, bf16[128,512]{1,0:T(8,128)(2,1)S(1)}, u32[]{:S(2)}, u32[]{:S(2)}) collective-permute-start(bf16[128,512]{1,0:T(8,128)(2,1)S(1)} %shard_map.69), channel_id=1, source_target_pairs={{0,3},{1,2},{2,1},{3,0},{4,7},{5,6},{6,5},{7,4},{8,11},{9,10},{10,... | collective-permute-start | bytes 393224 | tf_op jit(solution)/shard_map/ppermute | solution.py:260
  23.6 5.8 %collective-permute-start.5 = (bf16[128,512]{1,0:T(8,128)(2,1)S(1)}, bf16[128,512]{1,0:T(8,128)(2,1)S(1)}, u32[]{:S(2)}, u32[]{:S(2)}) collective-permute-start(bf16[128,512]{1,0:T(8,128)(2,1)S(1)} %get-tuple-element.60), channel_id=1, source_target_pairs={{0,2},{1,3},{2,0},{3,1},{4,6},{5,7},{6,4},{7,5},{8,10},{9,11},{10,... | collective-permute-start | bytes 393224 | tf_op jit(solution)/shard_map/ppermute | solution.py:260
  25.0 5.3 %collective-permute-start.6 = (bf16[128,512]{1,0:T(8,128)(2,1)S(1)}, bf16[128,512]{1,0:T(8,128)(2,1)S(1)}, u32[]{:S(2)}, u32[]{:S(2)}) collective-permute-start(bf16[128,512]{1,0:T(8,128)(2,1)S(1)} %get-tuple-element.61), channel_id=1, source_target_pairs={{0,1},{1,0},{2,3},{3,2},{4,5},{5,4},{6,7},{7,6},{8,9},{9,8},{10,11... | collective-permute-start | bytes 393224 | tf_op jit(solution)/shard_map/ppermute | solution.py:260
  28.3 2.6 %collective-permute-start.8 = (bf16[256,512]{1,0:T(8,128)(2,1)S(1)}, bf16[256,512]{1,0:T(8,128)(2,1)S(1)}, u32[]{:S(2)}, u32[]{:S(2)}) collective-permute-start(bf16[256,512]{1,0:T(8,128)(2,1)S(1)} %collective-permute-done.refs_2_), channel_id=1, source_target_pairs={{0,8},{1,9},{2,10},{3,11},{4,12},{5,13},{6,14},{7,15},{8,0},{9,1},... | collective-permute-start | bytes 786440 | tf_op jit(solution)/shard_map/ppermute | solution.py:260
  28.4 2.5 %collective-permute-start.9 = (bf16[256,512]{1,0:T(8,128)(2,1)S(1)}, bf16[256,512]{1,0:T(8,128)(2,1)S(1)}, u32[]{:S(2)}, u32[]{:S(2)}) collective-permute-start(bf16[256,512]{1,0:T(8,128)(2,1)S(1)} %collective-permute-done.7.refs_4_), channel_id=1, source_target_pairs={{0,8},{1,9},{2,10},{3,11},{4,12},{5,13},{6,14},{7,15},{8,0},{9,1},... | collective-permute-start | bytes 786440 | tf_op jit(solution)/shard_map/ppermute | solution.py:260
  33.7 1.6 %collective-permute-start.10 = (bf16[16,16,512]{2,1,0:T(8,128)(2,1)S(1)}, bf16[16,16,512]{2,1,0:T(8,128)(2,1)S(1)}, u32[]{:S(2)}, u32[]{:S(2)}) collective-permute-start(bf16[16,16,512]{2,1,0:T(8,128)(2,1)S(1)} %get-tuple-element.77), channel_id=1, source_target_pairs={{0,8},{1,9},{2,10},{3,11},{4,12},{5,13},{6,14},{7,15},{8,0},{9,1},... | collective-permute-start | bytes 786440 | tf_op jit(solution)/shard_map/ppermute | solution.py:260
  35.4 5.6 %collective-permute-start.11 = (bf16[8,16,512]{2,1,0:T(8,128)(2,1)S(1)}, bf16[8,16,512]{2,1,0:T(8,128)(2,1)S(1)}, u32[]{:S(2)}, u32[]{:S(2)}) collective-permute-start(bf16[8,16,512]{2,1,0:T(8,128)(2,1)S(1)} %get-tuple-element.79), channel_id=1, source_target_pairs={{0,16},{1,17},{2,18},{3,19},{4,20},{5,21},{6,22},{7,23},{8,24},{9,... | collective-permute-start | bytes 393224 | tf_op jit(solution)/shard_map/ppermute | solution.py:260
  36.8 7.3 %collective-permute-start.15 = (bf16[128,512]{1,0:T(8,128)(2,1)S(1)}, bf16[128,512]{1,0:T(8,128)(2,1)S(1)}, u32[]{:S(2)}, u32[]{:S(2)}) collective-permute-start(bf16[128,512]{1,0:T(8,128)(2,1)S(1)} %get-tuple-element.73.refs_5_), channel_id=1, source_target_pairs={{0,3},{1,2},{2,1},{3,0},{4,7},{5,6},{6,5},{7,4},{8,11},{9,10},{10,... | collective-permute-start | bytes 393224 | tf_op jit(solution)/shard_map/ppermute | solution.py:260
  37.9 8.2 %collective-permute-start.16 = (bf16[128,512]{1,0:T(8,128)(2,1)S(1)}, bf16[128,512]{1,0:T(8,128)(2,1)S(1)}, u32[]{:S(2)}, u32[]{:S(2)}) collective-permute-start(bf16[128,512]{1,0:T(8,128)(2,1)S(1)} %get-tuple-element.74.refs_6_), channel_id=1, source_target_pairs={{0,2},{1,3},{2,0},{3,1},{4,6},{5,7},{6,4},{7,5},{8,10},{9,11},{10,... | collective-permute-start | bytes 393224 | tf_op jit(solution)/shard_map/ppermute | solution.py:260
  39.3 7.1 %collective-permute-start.17 = (bf16[128,512]{1,0:T(8,128)(2,1)S(1)}, bf16[128,512]{1,0:T(8,128)(2,1)S(1)}, u32[]{:S(2)}, u32[]{:S(2)}) collective-permute-start(bf16[128,512]{1,0:T(8,128)(2,1)S(1)} %get-tuple-element.75.refs_7_), channel_id=1, source_target_pairs={{0,1},{1,0},{2,3},{3,2},{4,5},{5,4},{6,7},{7,6},{8,9},{9,8},{10,11... | collective-permute-start | bytes 393224 | tf_op jit(solution)/shard_map/ppermute | solution.py:260
  41.0 5.9 %collective-permute-start.12 = (bf16[2,16,512]{2,1,0:T(8,128)(2,1)S(1)}, bf16[2,16,512]{2,1,0:T(8,128)(2,1)S(1)}, u32[]{:S(2)}, u32[]{:S(2)}) collective-permute-start(bf16[2,16,512]{2,1,0:T(8,128)(2,1)S(1)} %get-tuple-element.81), channel_id=1, source_target_pairs={{0,3},{1,2},{2,1},{3,0},{4,7},{5,6},{6,5},{7,4},{8,11},{9,10},{10,... | collective-permute-start | bytes 98312 | tf_op jit(solution)/shard_map/ppermute | solution.py:260
  42.1 4.9 %collective-permute-start.13 = (bf16[2,16,512]{2,1,0:T(8,128)(2,1)S(1)}, bf16[2,16,512]{2,1,0:T(8,128)(2,1)S(1)}, u32[]{:S(2)}, u32[]{:S(2)}) collective-permute-start(bf16[2,16,512]{2,1,0:T(8,128)(2,1)S(1)} %get-tuple-element.82), channel_id=1, source_target_pairs={{0,2},{1,3},{2,0},{3,1},{4,6},{5,7},{6,4},{7,5},{8,10},{9,11},{10,... | collective-permute-start | bytes 98312 | tf_op jit(solution)/shard_map/ppermute | solution.py:260
  44.1 3.9 %collective-permute-start.14 = (bf16[2,16,512]{2,1,0:T(8,128)(2,1)S(1)}, bf16[2,16,512]{2,1,0:T(8,128)(2,1)S(1)}, u32[]{:S(2)}, u32[]{:S(2)}) collective-permute-start(bf16[2,16,512]{2,1,0:T(8,128)(2,1)S(1)} %get-tuple-element.83), channel_id=1, source_target_pairs={{0,1},{1,0},{2,3},{3,2},{4,5},{5,4},{6,7},{7,6},{8,9},{9,8},{10,11... | collective-permute-start | bytes 98312 | tf_op jit(solution)/shard_map/ppermute | solution.py:260
  48.0 5.7 %collective-permute-start.18 = (f32[1,16,512]{2,1,0:T(8,128)S(1)}, f32[1,16,512]{2,1,0:T(8,128)S(1)}, u32[]{:S(2)}, u32[]{:S(2)}) collective-permute-start(f32[1,16,512]{2,1,0:T(8,128)S(1)} %get-tuple-element.90), channel_id=1, source_target_pairs={{0,4},{1,5},{2,6},{3,7},{4,0},{5,1},{6,2},{7,3},{8,12},{9,13},{10,... | collective-permute-start | bytes 98312 | tf_op jit(solution)/shard_map/ppermute | solution.py:260

commit v27 on v26

--- a/solution.py
+++ b/solution.py
@@ -288,7 +288,7 @@
         masks = [
             mask_of([bit for j, bit in enumerate(reversed(stage)) if step >> j & 1]) for step in steps_of(stage)[1:]
         ]
-        sent = f32 if k == len(stages) - 1 else bf16
+        sent = bf16
         count = len(values)
         kernel = functools.partial(stage_kernel, stage, count) if k else functools.partial(share_kernel, order, stage, count)
         kept, *sends = call(

time: 54.6 us -> 54.6 us (level)
  no operation moved by 1% of the time
where the time goes in v27:
time: 54.6 us; the launch traced here: 54.4 us
  starting transfers between devices  22 us (40%)
  Pallas kernels  12.5 us (23%)
  blocking collectives  11.7 us (21%)
  waiting for transfers between devices  6.57 us (12%)
  between operations  0.82 us (2%)
  other arithmetic  0.7 us (1%)
    ppermute x19, starting transfers between devices, swap(): lax.ppermute(value, ('batch', 'item'), [(k, k ^ mask) for k in range(devi...  22 us
    all_to_all x1, blocking collectives, local(): lax.all_to_all(request, ('batch', 'item'), split_axis=0, concat_axis=0, t...  11.7 us
    pallas_call x13, Pallas kernels, call(): pl.pallas_call(kernel, out_shape=[jax.ShapeDtypeStruct(shape, dtype) for...  9.34 us
    ppermute x19, waiting for transfers between devices, swap(): lax.ppermute(value, ('batch', 'item'), [(k, k ^ mask) for k in range(devi...  6.57 us
    pallas_call x1, Pallas kernels, local(): pl.pallas_call(functools.partial(table_kernel, sizes), out_specs=pl.Block...  3.19 us
  transfers between devices with their start and end apart: 19, of which 8 were waited for; matrix products, arithmetic and copies ran while one was open for 1% of the time, Pallas kernels for 17%

profile of v27, /device:TPU:0, one launch (start us, length us, event | category | flops | bytes accessed | tf_op | source)
XLA Modules:
  0.0 54.4 jit_solution(7572649569800330621)
XLA Ops:
  0.6 4.1 %collective-permute-start = (bf16[256,512]{1,0:T(8,128)(2,1)}, bf16[256,512]{1,0:T(8,128)(2,1)S(1)}, u32[]{:S(2)}, u32[]{:S(2)}) collective-permute-start(bf16[256,512]{1,0:T(8,128)(2,1)} %refs_0_), channel_id=1, source_target_pairs={{0,4},{1,5},{2,6},{3,7},{4,0},{5,1},{6,2},{7,3},{8,12},{9,13},{10,... | collective-permute-start | bytes 786440 | tf_op jit(solution)/shard_map/ppermute | solution.py:260
  4.7 1.5 %collective-permute-start.1 = (bf16[256,512]{1,0:T(8,128)(2,1)}, bf16[256,512]{1,0:T(8,128)(2,1)S(1)}, u32[]{:S(2)}, u32[]{:S(2)}) collective-permute-start(bf16[256,512]{1,0:T(8,128)(2,1)} %refs_0_), channel_id=1, source_target_pairs={{0,16},{1,17},{2,18},{3,19},{4,20},{5,21},{6,22},{7,23},{8,24},{9,... | collective-permute-start | bytes 786440 | tf_op jit(solution)/shard_map/ppermute | solution.py:260
  6.2 0.7 %pad_add_fusion.named_ref = s32[2,256]{1,0:T(2,128)S(1)} fusion(s32[1,256]{1,0:T(1,128)} %bitcast.11, s32[1,256]{1,0:T(1,128)} %bitcast.12), kind=kLoop, calls=%fused_computation | loop fusion | flops 512 | bytes 4096 | tf_op jit(solution)/shard_map/stack | solution.py:327
  7.4 11.7 %all_to_all.12 = s32[32,1,80]{2,1,0:T(1,128)S(1)} all-to-all(s32[32,1,80]{2,1,0:T(1,128)S(1)} %bitcast.10), channel_id=1, replica_groups=mesh['batch'=4,'item'=8] {'batch','item'}, dimensions={0} | all-to-all | bytes 20480 | tf_op jit(solution)/shard_map/all_to_all | solution.py:330
  19.2 0.5 collective-permute-start.3
  19.7 0.6 %collective-permute-start.7 = (bf16[256,512]{1,0:T(8,128)(2,1)S(1)}, bf16[256,512]{1,0:T(8,128)(2,1)S(1)}, u32[]{:S(2)}, u32[]{:S(2)}) collective-permute-start(bf16[256,512]{1,0:T(8,128)(2,1)S(1)} %collective-permute-done.refs_2_), channel_id=1, source_target_pairs={{0,16},{1,17},{2,18},{3,19},{4,20},{5,21},{6,22},{7,23},{8,24},{9,... | collective-permute-start | bytes 786440 | tf_op jit(solution)/shard_map/ppermute | solution.py:260
  20.3 0.9 %shard_map.69 = bf16[128,512]{1,0:T(8,128)(2,1)S(1)} custom-call(s32[32,80]{1,0:T(8,128)S(1)} %bitcast.6, bf16[4096,512]{1,0:T(8,128)(2,1)S(1)} %copy-done), custom_call_target="tpu_custom_call" | custom-call | flops 536870912 | bytes 1048576 | tf_op jit(solution)/shard_map/pallas_call | solution.py:249
  21.2 0.8 %collective-permute-start.4 = (bf16[128,512]{1,0:T(8,128)(2,1)S(1)}, bf16[128,512]{1,0:T(8,128)(2,1)S(1)}, u32[]{:S(2)}, u32[]{:S(2)}) collective-permute-start(bf16[128,512]{1,0:T(8,128)(2,1)S(1)} %shard_map.69), channel_id=1, source_target_pairs={{0,3},{1,2},{2,1},{3,0},{4,7},{5,6},{6,5},{7,4},{8,11},{9,10},{10,... | collective-permute-start | bytes 393224 | tf_op jit(solution)/shard_map/ppermute | solution.py:260
  22.0 1.6 %shard_map.70 = (bf16[128,512]{1,0:T(8,128)(2,1)S(1)}, bf16[128,512]{1,0:T(8,128)(2,1)S(1)}) custom-call(s32[32,80]{1,0:T(8,128)S(1)} %bitcast.7, bf16[4096,512]{1,0:T(8,128)(2,1)S(1)} %copy-done), custom_call_target="tpu_custom_call" | custom-call | flops 1073741824 | bytes 1048576 | tf_op jit(solution)/shard_map/pallas_call | solution.py:249
  23.6 1.4 %collective-permute-start.5 = (bf16[128,512]{1,0:T(8,128)(2,1)S(1)}, bf16[128,512]{1,0:T(8,128)(2,1)S(1)}, u32[]{:S(2)}, u32[]{:S(2)}) collective-permute-start(bf16[128,512]{1,0:T(8,128)(2,1)S(1)} %get-tuple-element.60), channel_id=1, source_target_pairs={{0,2},{1,3},{2,0},{3,1},{4,6},{5,7},{6,4},{7,5},{8,10},{9,11},{10,... | collective-permute-start | bytes 393224 | tf_op jit(solution)/shard_map/ppermute | solution.py:260
  25.0 1.4 %collective-permute-start.6 = (bf16[128,512]{1,0:T(8,128)(2,1)S(1)}, bf16[128,512]{1,0:T(8,128)(2,1)S(1)}, u32[]{:S(2)}, u32[]{:S(2)}) collective-permute-start(bf16[128,512]{1,0:T(8,128)(2,1)S(1)} %get-tuple-element.61), channel_id=1, source_target_pairs={{0,1},{1,0},{2,3},{3,2},{4,5},{5,4},{6,7},{7,6},{8,9},{9,8},{10,11... | collective-permute-start | bytes 393224 | tf_op jit(solution)/shard_map/ppermute | solution.py:260
  26.4 0.9 %shard_map.71.refs_0_ = bf16[128,512]{1,0:T(8,128)(2,1)S(1)} custom-call(s32[32,80]{1,0:T(8,128)S(1)} %bitcast.8, bf16[4096,512]{1,0:T(8,128)(2,1)S(1)} %copy-done), custom_call_target="tpu_custom_call" | custom-call | flops 536870912 | bytes 1048576 | tf_op jit(solution)/shard_map/pallas_call | solution.py:249
  27.3 1.0 %shard_map.72 = (s32[512,1]{1,0:T(8,128)S(1)}, bf16[256,512]{1,0:T(8,128)(2,1)S(1)}, bf16[256,512]{1,0:T(8,128)(2,1)S(1)}, bf16[1024,512]{1,0:T(8,128)(2,1)S(1)}, bf16[256,512]{1,0:T(8,128)(2,1)S(1)}) custom-call(s32[32,80]{1,0:T(8,128)S(1)} %bitcast.9, bf16[256,512]{1,0:T(8,128)(2,1)S(1)} %copy-done.2, bf16[256,512]{1,0:T(8,128)(2,1)S(1)} %collective-permute-done.2.refs_1_, ...), custom_call_target="tpu_custom_call" | custom-call | tf_op jit(solution)/shard_map/pallas_call | solution.py:249
  29.4 1.0 %collective-permute-done.6.refs_1_.refs_3_ = bf16[128,512]{1,0:T(8,128)(2,1)S(1)} collective-permute-done((bf16[128,512]{1,0:T(8,128)(2,1)S(1)}, bf16[128,512]{1,0:T(8,128)(2,1)S(1)}, u32[]{:S(2)}, u32[]{:S(2)}) %collective-permute-start.6) | collective-permute-done | bytes 131104 | tf_op jit(solution)/shard_map/ppermute | solution.py:260
  30.4 0.5 shard_map.73
  30.9 2.2 %shard_map.74 = (bf16[128,512]{1,0:T(8,128)(2,1)S(1)}, bf16[128,512]{1,0:T(8,128)(2,1)S(1)}, bf16[128,512]{1,0:T(8,128)(2,1)S(1)}, bf16[128,512]{1,0:T(8,128)(2,1)S(1)}) custom-call(s32[512,1]{1,0:T(8,128)S(1)} %get-tuple-element.64.place_ref, f32[512,512]{1,0:T(8,128)S(1)} %get-tuple-element.65.hidden_ref, f32[512,1]{1,0:T(8,128)S(1)} %get-tuple-element.66.rscale_ref, ...), custom_call_target="tpu_custom_call" | custom-call | flops 2147483648 | bytes 1048576 | tf_op jit(solution)/shard_map/pallas_call | solution.py:249
  33.1 0.5 shard_map.75
  33.7 1.5 %collective-permute-done.10.refs_1_ = bf16[16,16,512]{2,1,0:T(8,128)(2,1)S(1)} collective-permute-done((bf16[16,16,512]{2,1,0:T(8,128)(2,1)S(1)}, bf16[16,16,512]{2,1,0:T(8,128)(2,1)S(1)}, u32[]{:S(2)}, u32[]{:S(2)}) %collective-permute-start.10) | collective-permute-done | bytes 262176 | tf_op jit(solution)/shard_map/ppermute | solution.py:260
  35.4 1.4 %collective-permute-start.11 = (bf16[8,16,512]{2,1,0:T(8,128)(2,1)S(1)}, bf16[8,16,512]{2,1,0:T(8,128)(2,1)S(1)}, u32[]{:S(2)}, u32[]{:S(2)}) collective-permute-start(bf16[8,16,512]{2,1,0:T(8,128)(2,1)S(1)} %get-tuple-element.79), channel_id=1, source_target_pairs={{0,16},{1,17},{2,18},{3,19},{4,20},{5,21},{6,22},{7,23},{8,24},{9,... | collective-permute-start | bytes 393224 | tf_op jit(solution)/shard_map/ppermute | solution.py:260
  36.8 1.1 %collective-permute-start.15 = (bf16[128,512]{1,0:T(8,128)(2,1)S(1)}, bf16[128,512]{1,0:T(8,128)(2,1)S(1)}, u32[]{:S(2)}, u32[]{:S(2)}) collective-permute-start(bf16[128,512]{1,0:T(8,128)(2,1)S(1)} %get-tuple-element.73.refs_5_), channel_id=1, source_target_pairs={{0,3},{1,2},{2,1},{3,0},{4,7},{5,6},{6,5},{7,4},{8,11},{9,10},{10,... | collective-permute-start | bytes 393224 | tf_op jit(solution)/shard_map/ppermute | solution.py:260
  37.9 1.4 %collective-permute-start.16 = (bf16[128,512]{1,0:T(8,128)(2,1)S(1)}, bf16[128,512]{1,0:T(8,128)(2,1)S(1)}, u32[]{:S(2)}, u32[]{:S(2)}) collective-permute-start(bf16[128,512]{1,0:T(8,128)(2,1)S(1)} %get-tuple-element.74.refs_6_), channel_id=1, source_target_pairs={{0,2},{1,3},{2,0},{3,1},{4,6},{5,7},{6,4},{7,5},{8,10},{9,11},{10,... | collective-permute-start | bytes 393224 | tf_op jit(solution)/shard_map/ppermute | solution.py:260
  39.3 1.0 %collective-permute-start.17 = (bf16[128,512]{1,0:T(8,128)(2,1)S(1)}, bf16[128,512]{1,0:T(8,128)(2,1)S(1)}, u32[]{:S(2)}, u32[]{:S(2)}) collective-permute-start(bf16[128,512]{1,0:T(8,128)(2,1)S(1)} %get-tuple-element.75.refs_7_), channel_id=1, source_target_pairs={{0,1},{1,0},{2,3},{3,2},{4,5},{5,4},{6,7},{7,6},{8,9},{9,8},{10,11... | collective-permute-start | bytes 393224 | tf_op jit(solution)/shard_map/ppermute | solution.py:260
  40.3 0.7 %collective-permute-done.11.refs_1_ = bf16[8,16,512]{2,1,0:T(8,128)(2,1)S(1)} collective-permute-done((bf16[8,16,512]{2,1,0:T(8,128)(2,1)S(1)}, bf16[8,16,512]{2,1,0:T(8,128)(2,1)S(1)}, u32[]{:S(2)}, u32[]{:S(2)}) %collective-permute-start.11) | collective-permute-done | bytes 131104 | tf_op jit(solution)/shard_map/ppermute | solution.py:260
  41.0 1.1 %collective-permute-start.12 = (bf16[2,16,512]{2,1,0:T(8,128)(2,1)S(1)}, bf16[2,16,512]{2,1,0:T(8,128)(2,1)S(1)}, u32[]{:S(2)}, u32[]{:S(2)}) collective-permute-start(bf16[2,16,512]{2,1,0:T(8,128)(2,1)S(1)} %get-tuple-element.81), channel_id=1, source_target_pairs={{0,3},{1,2},{2,1},{3,0},{4,7},{5,6},{6,5},{7,4},{8,11},{9,10},{10,... | collective-permute-start | bytes 98312 | tf_op jit(solution)/shard_map/ppermute | solution.py:260
  42.1 1.4 %collective-permute-start.13 = (bf16[2,16,512]{2,1,0:T(8,128)(2,1)S(1)}, bf16[2,16,512]{2,1,0:T(8,128)(2,1)S(1)}, u32[]{:S(2)}, u32[]{:S(2)}) collective-permute-start(bf16[2,16,512]{2,1,0:T(8,128)(2,1)S(1)} %get-tuple-element.82), channel_id=1, source_target_pairs={{0,2},{1,3},{2,0},{3,1},{4,6},{5,7},{6,4},{7,5},{8,10},{9,11},{10,... | collective-permute-start | bytes 98312 | tf_op jit(solution)/shard_map/ppermute | solution.py:260
  43.5 0.5 %collective-permute-done.15.refs_0_ = bf16[128,512]{1,0:T(8,128)(2,1)S(1)} collective-permute-done((bf16[128,512]{1,0:T(8,128)(2,1)S(1)}, bf16[128,512]{1,0:T(8,128)(2,1)S(1)}, u32[]{:S(2)}, u32[]{:S(2)}) %collective-permute-start.15) | collective-permute-done | bytes 131104 | tf_op jit(solution)/shard_map/ppermute | solution.py:260
  44.1 1.1 %collective-permute-start.14 = (bf16[2,16,512]{2,1,0:T(8,128)(2,1)S(1)}, bf16[2,16,512]{2,1,0:T(8,128)(2,1)S(1)}, u32[]{:S(2)}, u32[]{:S(2)}) collective-permute-start(bf16[2,16,512]{2,1,0:T(8,128)(2,1)S(1)} %get-tuple-element.83), channel_id=1, source_target_pairs={{0,1},{1,0},{2,3},{3,2},{4,5},{5,4},{6,7},{7,6},{8,9},{9,8},{10,11... | collective-permute-start | bytes 98312 | tf_op jit(solution)/shard_map/ppermute | solution.py:260
  45.2 0.9 %collective-permute-done.16.refs_1_ = bf16[128,512]{1,0:T(8,128)(2,1)S(1)} collective-permute-done((bf16[128,512]{1,0:T(8,128)(2,1)S(1)}, bf16[128,512]{1,0:T(8,128)(2,1)S(1)}, u32[]{:S(2)}, u32[]{:S(2)}) %collective-permute-start.16) | collective-permute-done | bytes 131104 | tf_op jit(solution)/shard_map/ppermute | solution.py:260
  47.0 1.0 %collective-permute-done.14.refs_3_ = bf16[2,16,512]{2,1,0:T(8,128)(2,1)S(1)} collective-permute-done((bf16[2,16,512]{2,1,0:T(8,128)(2,1)S(1)}, bf16[2,16,512]{2,1,0:T(8,128)(2,1)S(1)}, u32[]{:S(2)}, u32[]{:S(2)}) %collective-permute-start.14) | collective-permute-done | bytes 32800 | tf_op jit(solution)/shard_map/ppermute | solution.py:260
  48.0 2.5 %collective-permute-start.18 = (bf16[1,16,512]{2,1,0:T(8,128)(2,1)S(1)}, bf16[1,16,512]{2,1,0:T(8,128)(2,1)S(1)}, u32[]{:S(2)}, u32[]{:S(2)}) collective-permute-start(bf16[1,16,512]{2,1,0:T(8,128)(2,1)S(1)} %get-tuple-element.90), channel_id=1, source_target_pairs={{0,4},{1,5},{2,6},{3,7},{4,0},{5,1},{6,2},{7,3},{8,12},{9,13},{10,... | collective-permute-start | bytes 49160 | tf_op jit(solution)/shard_map/ppermute | solution.py:260
  50.5 3.2 %shard_map.79 = bf16[4096,512]{1,0:T(8,128)(2,1)} custom-call(bf16[256,512]{1,0:T(8,128)(2,1)S(1)} %get-tuple-element.56.low_hot_ref, bf16[256,512]{1,0:T(8,128)(2,1)S(1)} %get-tuple-element.57.block_ref, bf16[512,512]{1,0:T(8,128)(2,1)S(1)} %shard_map.78.drow_ref), custom_call_target="tpu_custom_call" | custom-call | flops 2147483648 | bytes 4194304 | tf_op jit(solution)/shard_map/pallas_call | solution.py:397
  53.8 0.6 %shard_map.81 = f32[16,512]{1,0:T(8,128)} custom-call(f32[1,16,512]{2,1,0:T(8,128)S(1)} %get-tuple-element.92.refs_0_, bf16[1,16,512]{2,1,0:T(8,128)(2,1)S(1)} %collective-permute-done.18.refs_1_), custom_call_target="tpu_custom_call" | custom-call | bytes 1048576 | tf_op jit(solution)/shard_map/pallas_call | solution.py:249
  (28 shorter events, 2.7 us)
Async XLA Ops:
  0.6 18.4 %collective-permute-start = (bf16[256,512]{1,0:T(8,128)(2,1)}, bf16[256,512]{1,0:T(8,128)(2,1)S(1)}, u32[]{:S(2)}, u32[]{:S(2)}) collective-permute-start(bf16[256,512]{1,0:T(8,128)(2,1)} %refs_0_), channel_id=1, source_target_pairs={{0,4},{1,5},{2,6},{3,7},{4,0},{5,1},{6,2},{7,3},{8,12},{9,13},{10,... | collective-permute-start | bytes 786440 | tf_op jit(solution)/shard_map/ppermute | solution.py:260
  4.7 14.4 %collective-permute-start.1 = (bf16[256,512]{1,0:T(8,128)(2,1)}, bf16[256,512]{1,0:T(8,128)(2,1)S(1)}, u32[]{:S(2)}, u32[]{:S(2)}) collective-permute-start(bf16[256,512]{1,0:T(8,128)(2,1)} %refs_0_), channel_id=1, source_target_pairs={{0,16},{1,17},{2,18},{3,19},{4,20},{5,21},{6,22},{7,23},{8,24},{9,... | collective-permute-start | bytes 786440 | tf_op jit(solution)/shard_map/ppermute | solution.py:260
  6.9 12.2 %copy-start.2 = (bf16[256,512]{1,0:T(8,128)(2,1)S(1)}, bf16[256,512]{1,0:T(8,128)(2,1)}, u32[]{:S(2)}) copy-start(bf16[256,512]{1,0:T(8,128)(2,1)} %refs_0_) | copy-start | bytes 786436
  6.9 13.3 %copy-start = (bf16[4096,512]{1,0:T(8,128)(2,1)S(1)}, bf16[4096,512]{1,0:T(8,128)(2,1)}, u32[]{:S(2)}) copy-start(bf16[4096,512]{1,0:T(8,128)(2,1)} %table_ref.5) | copy-start | bytes 12582916
  19.1 5.9 %collective-permute-start.2 = (bf16[256,512]{1,0:T(8,128)(2,1)S(1)}, bf16[256,512]{1,0:T(8,128)(2,1)S(1)}, u32[]{:S(2)}, u32[]{:S(2)}) collective-permute-start(bf16[256,512]{1,0:T(8,128)(2,1)S(1)} %copy-done.2), channel_id=1, source_target_pairs={{0,8},{1,9},{2,10},{3,11},{4,12},{5,13},{6,14},{7,15},{8,0},{9,1},... | collective-permute-start | bytes 786440 | tf_op jit(solution)/shard_map/ppermute | solution.py:260
  19.2 8.1 %collective-permute-start.3 = (bf16[256,512]{1,0:T(8,128)(2,1)S(1)}, bf16[256,512]{1,0:T(8,128)(2,1)S(1)}, u32[]{:S(2)}, u32[]{:S(2)}) collective-permute-start(bf16[256,512]{1,0:T(8,128)(2,1)S(1)} %collective-permute-done.1.refs_2_), channel_id=1, source_target_pairs={{0,8},{1,9},{2,10},{3,11},{4,12},{5,13},{6,14},{7,15},{8,0},{9,1},... | collective-permute-start | bytes 786440 | tf_op jit(solution)/shard_map/ppermute | solution.py:260
  19.7 8.7 %collective-permute-start.7 = (bf16[256,512]{1,0:T(8,128)(2,1)S(1)}, bf16[256,512]{1,0:T(8,128)(2,1)S(1)}, u32[]{:S(2)}, u32[]{:S(2)}) collective-permute-start(bf16[256,512]{1,0:T(8,128)(2,1)S(1)} %collective-permute-done.refs_2_), channel_id=1, source_target_pairs={{0,16},{1,17},{2,18},{3,19},{4,20},{5,21},{6,22},{7,23},{8,24},{9,... | collective-permute-start | bytes 786440 | tf_op jit(solution)/shard_map/ppermute | solution.py:260
  21.2 9.2 %copy-start.1 = (bf16[512,512]{1,0:T(8,128)(2,1)S(1)}, bf16[512,512]{1,0:T(8,128)(2,1)}, u32[]{:S(2)}) copy-start(bf16[512,512]{1,0:T(8,128)(2,1)} %weight_ref.3) | copy-start | bytes 1572868
  21.2 7.7 %collective-permute-start.4 = (bf16[128,512]{1,0:T(8,128)(2,1)S(1)}, bf16[128,512]{1,0:T(8,128)(2,1)S(1)}, u32[]{:S(2)}, u32[]{:S(2)}) collective-permute-start(bf16[128,512]{1,0:T(8,128)(2,1)S(1)} %shard_map.69), channel_id=1, source_target_pairs={{0,3},{1,2},{2,1},{3,0},{4,7},{5,6},{6,5},{7,4},{8,11},{9,10},{10,... | collective-permute-start | bytes 393224 | tf_op jit(solution)/shard_map/ppermute | solution.py:260
  23.6 5.8 %collective-permute-start.5 = (bf16[128,512]{1,0:T(8,128)(2,1)S(1)}, bf16[128,512]{1,0:T(8,128)(2,1)S(1)}, u32[]{:S(2)}, u32[]{:S(2)}) collective-permute-start(bf16[128,512]{1,0:T(8,128)(2,1)S(1)} %get-tuple-element.60), channel_id=1, source_target_pairs={{0,2},{1,3},{2,0},{3,1},{4,6},{5,7},{6,4},{7,5},{8,10},{9,11},{10,... | collective-permute-start | bytes 393224 | tf_op jit(solution)/shard_map/ppermute | solution.py:260
  25.0 5.3 %collective-permute-start.6 = (bf16[128,512]{1,0:T(8,128)(2,1)S(1)}, bf16[128,512]{1,0:T(8,128)(2,1)S(1)}, u32[]{:S(2)}, u32[]{:S(2)}) collective-permute-start(bf16[128,512]{1,0:T(8,128)(2,1)S(1)} %get-tuple-element.61), channel_id=1, source_target_pairs={{0,1},{1,0},{2,3},{3,2},{4,5},{5,4},{6,7},{7,6},{8,9},{9,8},{10,11... | collective-permute-start | bytes 393224 | tf_op jit(solution)/shard_map/ppermute | solution.py:260
  28.3 2.6 %collective-permute-start.8 = (bf16[256,512]{1,0:T(8,128)(2,1)S(1)}, bf16[256,512]{1,0:T(8,128)(2,1)S(1)}, u32[]{:S(2)}, u32[]{:S(2)}) collective-permute-start(bf16[256,512]{1,0:T(8,128)(2,1)S(1)} %collective-permute-done.refs_2_), channel_id=1, source_target_pairs={{0,8},{1,9},{2,10},{3,11},{4,12},{5,13},{6,14},{7,15},{8,0},{9,1},... | collective-permute-start | bytes 786440 | tf_op jit(solution)/shard_map/ppermute | solution.py:260
  28.4 2.5 %collective-permute-start.9 = (bf16[256,512]{1,0:T(8,128)(2,1)S(1)}, bf16[256,512]{1,0:T(8,128)(2,1)S(1)}, u32[]{:S(2)}, u32[]{:S(2)}) collective-permute-start(bf16[256,512]{1,0:T(8,128)(2,1)S(1)} %collective-permute-done.7.refs_4_), channel_id=1, source_target_pairs={{0,8},{1,9},{2,10},{3,11},{4,12},{5,13},{6,14},{7,15},{8,0},{9,1},... | collective-permute-start | bytes 786440 | tf_op jit(solution)/shard_map/ppermute | solution.py:260
  33.7 1.6 %collective-permute-start.10 = (bf16[16,16,512]{2,1,0:T(8,128)(2,1)S(1)}, bf16[16,16,512]{2,1,0:T(8,128)(2,1)S(1)}, u32[]{:S(2)}, u32[]{:S(2)}) collective-permute-start(bf16[16,16,512]{2,1,0:T(8,128)(2,1)S(1)} %get-tuple-element.77), channel_id=1, source_target_pairs={{0,8},{1,9},{2,10},{3,11},{4,12},{5,13},{6,14},{7,15},{8,0},{9,1},... | collective-permute-start | bytes 786440 | tf_op jit(solution)/shard_map/ppermute | solution.py:260
  35.4 5.6 %collective-permute-start.11 = (bf16[8,16,512]{2,1,0:T(8,128)(2,1)S(1)}, bf16[8,16,512]{2,1,0:T(8,128)(2,1)S(1)}, u32[]{:S(2)}, u32[]{:S(2)}) collective-permute-start(bf16[8,16,512]{2,1,0:T(8,128)(2,1)S(1)} %get-tuple-element.79), channel_id=1, source_target_pairs={{0,16},{1,17},{2,18},{3,19},{4,20},{5,21},{6,22},{7,23},{8,24},{9,... | collective-permute-start | bytes 393224 | tf_op jit(solution)/shard_map/ppermute | solution.py:260
  36.8 7.3 %collective-permute-start.15 = (bf16[128,512]{1,0:T(8,128)(2,1)S(1)}, bf16[128,512]{1,0:T(8,128)(2,1)S(1)}, u32[]{:S(2)}, u32[]{:S(2)}) collective-permute-start(bf16[128,512]{1,0:T(8,128)(2,1)S(1)} %get-tuple-element.73.refs_5_), channel_id=1, source_target_pairs={{0,3},{1,2},{2,1},{3,0},{4,7},{5,6},{6,5},{7,4},{8,11},{9,10},{10,... | collective-permute-start | bytes 393224 | tf_op jit(solution)/shard_map/ppermute | solution.py:260
  37.9 8.2 %collective-permute-start.16 = (bf16[128,512]{1,0:T(8,128)(2,1)S(1)}, bf16[128,512]{1,0:T(8,128)(2,1)S(1)}, u32[]{:S(2)}, u32[]{:S(2)}) collective-permute-start(bf16[128,512]{1,0:T(8,128)(2,1)S(1)} %get-tuple-element.74.refs_6_), channel_id=1, source_target_pairs={{0,2},{1,3},{2,0},{3,1},{4,6},{5,7},{6,4},{7,5},{8,10},{9,11},{10,... | collective-permute-start | bytes 393224 | tf_op jit(solution)/shard_map/ppermute | solution.py:260
  39.3 7.1 %collective-permute-start.17 = (bf16[128,512]{1,0:T(8,128)(2,1)S(1)}, bf16[128,512]{1,0:T(8,128)(2,1)S(1)}, u32[]{:S(2)}, u32[]{:S(2)}) collective-permute-start(bf16[128,512]{1,0:T(8,128)(2,1)S(1)} %get-tuple-element.75.refs_7_), channel_id=1, source_target_pairs={{0,1},{1,0},{2,3},{3,2},{4,5},{5,4},{6,7},{7,6},{8,9},{9,8},{10,11... | collective-permute-start | bytes 393224 | tf_op jit(solution)/shard_map/ppermute | solution.py:260
  41.0 5.9 %collective-permute-start.12 = (bf16[2,16,512]{2,1,0:T(8,128)(2,1)S(1)}, bf16[2,16,512]{2,1,0:T(8,128)(2,1)S(1)}, u32[]{:S(2)}, u32[]{:S(2)}) collective-permute-start(bf16[2,16,512]{2,1,0:T(8,128)(2,1)S(1)} %get-tuple-element.81), channel_id=1, source_target_pairs={{0,3},{1,2},{2,1},{3,0},{4,7},{5,6},{6,5},{7,4},{8,11},{9,10},{10,... | collective-permute-start | bytes 98312 | tf_op jit(solution)/shard_map/ppermute | solution.py:260
  42.1 4.9 %collective-permute-start.13 = (bf16[2,16,512]{2,1,0:T(8,128)(2,1)S(1)}, bf16[2,16,512]{2,1,0:T(8,128)(2,1)S(1)}, u32[]{:S(2)}, u32[]{:S(2)}) collective-permute-start(bf16[2,16,512]{2,1,0:T(8,128)(2,1)S(1)} %get-tuple-element.82), channel_id=1, source_target_pairs={{0,2},{1,3},{2,0},{3,1},{4,6},{5,7},{6,4},{7,5},{8,10},{9,11},{10,... | collective-permute-start | bytes 98312 | tf_op jit(solution)/shard_map/ppermute | solution.py:260
  44.1 3.9 %collective-permute-start.14 = (bf16[2,16,512]{2,1,0:T(8,128)(2,1)S(1)}, bf16[2,16,512]{2,1,0:T(8,128)(2,1)S(1)}, u32[]{:S(2)}, u32[]{:S(2)}) collective-permute-start(bf16[2,16,512]{2,1,0:T(8,128)(2,1)S(1)} %get-tuple-element.83), channel_id=1, source_target_pairs={{0,1},{1,0},{2,3},{3,2},{4,5},{5,4},{6,7},{7,6},{8,9},{9,8},{10,11... | collective-permute-start | bytes 98312 | tf_op jit(solution)/shard_map/ppermute | solution.py:260
  48.0 5.7 %collective-permute-start.18 = (bf16[1,16,512]{2,1,0:T(8,128)(2,1)S(1)}, bf16[1,16,512]{2,1,0:T(8,128)(2,1)S(1)}, u32[]{:S(2)}, u32[]{:S(2)}) collective-permute-start(bf16[1,16,512]{2,1,0:T(8,128)(2,1)S(1)} %get-tuple-element.90), channel_id=1, source_target_pairs={{0,4},{1,5},{2,6},{3,7},{4,0},{5,1},{6,2},{7,3},{8,12},{9,13},{10,... | collective-permute-start | bytes 49160 | tf_op jit(solution)/shard_map/ppermute | solution.py:260
